TPU v7x, 32 devices: a whole 2x2x4 slice. The times are simulated.
32 devices in a mesh: dp: 2 (over y), station: 16 (over z, x, core).
Axes of the slice: x: 2, y: 2, z: 4, core: 2. Of those that a mesh axis runs over, the one named last changes fastest.
Arguments:
- query_states: bfloat16 [2, 16, 128, 768], P('dp', 'station'), may hold values from -6 to 6
- key_states: bfloat16 [2, 16, 128, 768], P('dp', 'station'), may hold values from -6 to 6
- value_states: bfloat16 [2, 16, 128, 768], P('dp', 'station'), may hold values from -15 to 15
- grad_output: bfloat16 [2, 16, 128, 768], P('dp', 'station'), may hold values from -6 to 6
- out_weight: bfloat16 [768, 768], replicated, may hold values from -0.21875 to 0.21875
- partner_ids: int32 [16, 6], replicated, may hold values from 0 to 15, as said below
- partner_count: int32 [16], replicated, may hold values from 1 to 6, as said below
Outputs:
- layer_output: bfloat16 [2, 16, 128, 768], P('dp', 'station')
- grad_query: bfloat16 [2, 16, 128, 768], P('dp', 'station')
- grad_key: bfloat16 [2, 16, 128, 768], P('dp', 'station')
- grad_value: bfloat16 [2, 16, 128, 768], P('dp', 'station')
- grad_weight: float32 [768, 768], P('dp')
Inputs may be any that keep to these rules, and one draw needn't show every extreme that they name: `partner_ids`: row s lists 6 different stations other than s, all held by devices within 3 places of the device of s along the station axis, taken as a loop (station s lies on device s); only the first partner_count[s] entries are partners. `partner_count`: some station has exactly 6 partners.
All inputs are finite; a program needn't handle non-finite values.
Results may differ from a plain program's by a relative error of at most 0.025.
Values may be sent and summed in bfloat16 or wider, within the bound.
No kernel may reach another device: no remote copies, remote signals or barrier semaphores. Data moves between devices by JAX's collectives and lax.ppermute only.
A program may use at most 64 MiB of HBM per device.

v0:
```python
import math

import jax
import jax.numpy as jnp
from jax import lax
from jax.sharding import PartitionSpec as P

HEADS = 12
PMAX = 6
HOPS = 3


neg_big = -1e30


def from_behind(value, axis, steps):
    count = lax.axis_size(axis)
    pairs = [(source, (source + steps) % count) for source in range(count)]
    return lax.ppermute(value, axis, pairs)


def split_heads(rows_in, head_count):
    return rows_in.reshape(rows_in.shape[:-1] + (head_count, rows_in.shape[-1] // head_count))


def local(
    query_states, key_states, value_states, grad_output, out_weight, partner_ids, partner_count
):
    window_count, per_device, span_rows, model_width = query_states.shape
    head_count = HEADS
    head_width = model_width // head_count
    score_scale = 1.0 / math.sqrt(head_width)
    slot_count = PMAX + 1
    device_count = lax.axis_size("station")
    station_count = per_device * device_count
    device_no = lax.axis_index("station")
    candidates = (2 * HOPS + 1) * per_device
    first_station = (device_no - HOPS) * per_device
    key_value = jnp.stack([key_states, value_states], 0)
    pieces = []
    for offset in range(-HOPS, HOPS + 1):
        if offset == 0:
            pieces.append(key_value)
        else:
            pieces.append(from_behind(key_value, "station", -offset))
    window = jnp.concatenate(pieces, 2)
    my_partners = lax.dynamic_slice_in_dim(partner_ids, device_no * per_device, per_device, 0)
    my_counts = lax.dynamic_slice_in_dim(partner_count, device_no * per_device, per_device, 0)
    partner_pos = jnp.mod(my_partners - first_station, station_count)
    self_pos = HOPS * per_device + jnp.arange(per_device, dtype=jnp.int32)
    slot_station = jnp.concatenate([self_pos[:, None], partner_pos], 1)
    slot_live = jnp.arange(slot_count, dtype=jnp.int32)[None, :] <= my_counts[:, None]
    row_count = window_count * per_device * span_rows
    flat_grad = grad_output.reshape(row_count, model_width)
    grad_mixed = lax.dot_general(
        flat_grad, out_weight, (((1,), (1,)), ((), ())), preferred_element_type=jnp.float32
    ).astype(jnp.bfloat16)
    grad_mixed = grad_mixed.reshape(query_states.shape)

    def one_station(number):
        window_no = number // per_device
        station_no = number % per_device
        query_rows = split_heads(query_states[window_no, station_no], head_count)
        grad_rows = split_heads(grad_mixed[window_no, station_no], head_count)
        picked = jnp.take(window[:, window_no], slot_station[station_no], axis=1)
        key_rows = picked[0].reshape(slot_count * span_rows, head_count, head_width)
        value_rows = picked[1].reshape(slot_count * span_rows, head_count, head_width)
        allowed = jnp.repeat(slot_live[station_no].astype(jnp.float32), span_rows)
        scores = (
            jnp.einsum("qhd,khd->hqk", query_rows, key_rows, preferred_element_type=jnp.float32)
            * score_scale
        )
        masked = jnp.where(allowed[None, None, :] > 0, scores, neg_big)
        row_max = jnp.max(masked, -1)
        weights_raw = jnp.exp(masked - row_max[..., None])
        row_sum = jnp.sum(weights_raw, -1)
        attn_probs = weights_raw / row_sum[..., None]
        probs_half = attn_probs.astype(jnp.bfloat16)
        mixed_rows = jnp.einsum(
            "hqk,khd->qhd", probs_half, value_rows, preferred_element_type=jnp.float32
        ).astype(jnp.bfloat16)
        row_delta = jnp.sum(grad_rows.astype(jnp.float32) * mixed_rows.astype(jnp.float32), -1).T
        grad_probs = jnp.einsum(
            "qhd,khd->hqk", grad_rows, value_rows, preferred_element_type=jnp.float32
        )
        grad_scores = (attn_probs * (grad_probs - row_delta[..., None])).astype(jnp.bfloat16)
        query_grad = (
            score_scale
            * jnp.einsum("hqk,khd->qhd", grad_scores, key_rows, preferred_element_type=jnp.float32)
        ).astype(jnp.bfloat16)
        result = (
            mixed_rows.reshape(span_rows, model_width),
            query_grad.reshape(span_rows, model_width),
        )
        key_part = score_scale * jnp.einsum(
            "hqk,qhd->khd", grad_scores, query_rows, preferred_element_type=jnp.float32
        )
        value_part = jnp.einsum(
            "hqk,qhd->khd", probs_half, grad_rows, preferred_element_type=jnp.float32
        )
        result = result + (
            jnp.stack([key_part, value_part], 0).reshape(2, -1, span_rows, model_width),
        )
        return result

    outputs = lax.map(one_station, jnp.arange(window_count * per_device, dtype=jnp.int32))
    mixed_all = outputs[0].reshape(query_states.shape)
    grad_query = outputs[1].reshape(query_states.shape)
    contribution = outputs[2].reshape(window_count, per_device, 2, -1, span_rows, model_width)
    moved = jnp.moveaxis(contribution, 2, 0).reshape(
        2, window_count, per_device * slot_count, span_rows, model_width
    )
    flat_slots = slot_station.reshape(-1)
    spread = (
        jnp.zeros((2, window_count, candidates, span_rows, model_width), jnp.float32)
        .at[:, :, flat_slots]
        .add(moved)
    )
    own_grads = spread[:, :, HOPS * per_device : (HOPS + 1) * per_device]
    for offset in range(-HOPS, HOPS + 1):
        if offset != 0:
            lower = (offset + HOPS) * per_device
            own_grads = own_grads + from_behind(
                spread[:, :, lower : lower + per_device].astype(jnp.bfloat16), "station", offset
            ).astype(jnp.float32)
    mixed_flat = mixed_all.reshape(row_count, model_width)
    layer_output = jnp.dot(mixed_flat, out_weight, preferred_element_type=jnp.float32).astype(
        jnp.bfloat16
    )
    grad_weight = lax.psum_scatter(
        lax.dot_general(
            mixed_flat, flat_grad, (((0,), (0,)), ((), ())), preferred_element_type=jnp.float32
        ).astype(jnp.bfloat16),
        "dp",
        scatter_dimension=0,
        tiled=True,
    ).astype(jnp.float32)
    grad_weight = lax.psum(grad_weight, "station")
    grad_weight = grad_weight / math.sqrt(row_count * lax.axis_size("dp") * device_count)
    return (
        layer_output.reshape(query_states.shape),
        grad_query,
        own_grads[0].astype(jnp.bfloat16),
        own_grads[1].astype(jnp.bfloat16),
        grad_weight,
    )


def solution(mesh):
    return jax.shard_map(
        local,
        mesh=mesh,
        in_specs=(
            P("dp", "station", None, None),
            P("dp", "station", None, None),
            P("dp", "station", None, None),
            P("dp", "station", None, None),
            P(),
            P(),
            P(),
        ),
        out_specs=(
            P("dp", "station", None, None),
            P("dp", "station", None, None),
            P("dp", "station", None, None),
            P("dp", "station", None, None),
            P("dp", None),
        ),
        check_vma=False,
    )
```

profile of v0, /device:TPU:0, one launch (start us, length us, event | category | flops | bytes accessed | tf_op | source)
XLA Modules:
  0.0 252.8 jit_solution(14811113623083308035)
XLA Ops:
  7.3 1.2 pad_maximum_fusion
  8.4 2.4 collective-permute-start
  10.9 1.5 collective-permute-start.1
  12.8 4.0 %collective-permute-start.3 = (bf16[2,1,1,128,768]{4,3,2,1,0:T(8,128)(2,1)S(1)}, bf16[2,1,1,128,768]{4,3,2,1,0:T(8,128)(2,1)S(1)}, u32[]{:S(2)}, u32[]{:S(2)}) collective-permute-start(bf16[2,1,1,128,768]{4,3,2,1,0:T(8,128)(2,1)S(1)} %pad_maximum_fusion), channel_id=1, source_target_pairs={{0,15},{1,0},{2,1},{3,2},{4,3},{5,4},{6,5},{7,6},{8,7},{9,8},{10,9... | collective-permute-start | bytes 1179656 | tf_op jit(solution)/shard_map/ppermute | solution.py:19
  17.3 1.2 dynamic_slice.20
  19.3 1.5 convolution_convert_fusion.2
  22.0 13.9 %collective-permute-done = bf16[2,1,1,128,768]{4,3,2,1,0:T(8,128)(2,1)} collective-permute-done((bf16[2,1,1,128,768]{4,3,2,1,0:T(8,128)(2,1)S(1)}, bf16[2,1,1,128,768]{4,3,2,1,0:T(8,128)(2,1)}, u32[]{:S(2)}, u32[]{:S(2)}) %collective-permute-start) | collective-permute-done | bytes 393248 | tf_op jit(solution)/shard_map/ppermute | solution.py:19
  35.9 1.8 constant_dynamic-update-slice_fusion.6
  37.7 6.7 %collective-permute-done.1 = bf16[2,1,1,128,768]{4,3,2,1,0:T(8,128)(2,1)} collective-permute-done((bf16[2,1,1,128,768]{4,3,2,1,0:T(8,128)(2,1)S(1)}, bf16[2,1,1,128,768]{4,3,2,1,0:T(8,128)(2,1)}, u32[]{:S(2)}, u32[]{:S(2)}) %collective-permute-start.1) | collective-permute-done | bytes 393248 | tf_op jit(solution)/shard_map/ppermute | solution.py:19
  44.3 1.8 constant_dynamic-update-slice_fusion.5
  46.1 1.8 constant_dynamic-update-slice_fusion.4
  47.9 0.8 constant_dynamic-update-slice_fusion.3
  50.0 0.8 constant_dynamic-update-slice_fusion.1
  50.8 0.8 constant_dynamic-update-slice_fusion
  51.5 4.1 %gather_fusion = bf16[7,2,128,768]{3,2,1,0:T(8,128)(2,1)} fusion(bf16[2,7,128,768]{3,2,1,0:T(8,128)(2,1)} %bitcast.2, s32[1024]{0:T(1024)S(1)} %pad_clamp_fusion), kind=kCustom, calls=%fused_computation | custom fusion | bytes 5505052 | tf_op jit(solution)/shard_map/while/body/eval_jaxpr/jit(_take)/gather | solution.py:65
  55.7 2.1 select_bitcast_fusion
  57.8 1.7 fusion.27
  59.5 2.1 copy.35
  61.6 2.5 squeeze.36
  64.1 2.1 copy.36
  66.2 2.5 squeeze.37
  68.7 5.9 %fusion.28 = (f32[12,128]{1,0:T(8,128)S(1)}, f32[12,128,896]{1,2,0:T(8,128)}) fusion(pred[896]{0:T(1024)(128)(4,1)S(1)} %broadcast_bitcast_fusion, bf16[896,12,64]{0,2,1:T(8,128)(2,1)} %squeeze.37, bf16[128,12,64]{0,2,1:T(8,128)(2,1)S(1)} %bitcast.88), kind=kOutput, calls=%fused_computation.65 | convolution fusion | flops 181666688 | bytes 7084928 | tf_op jit(solution)/shard_map/while/body/eval_jaxpr/sub | solution.py:75
  74.6 3.3 %fusion.8 = bf16[12,128,896]{1,2,0:T(8,128)(2,1)S(1)} fusion(f32[12,128,896]{1,2,0:T(8,128)} %get-tuple-element.58, f32[12,128]{1,0:T(8,128)S(1)} %get-tuple-element.57), kind=kLoop, calls=%fused_computation.16 | loop fusion | flops 2752512 | bytes 8263680 | tf_op jit(solution)/shard_map/while/body/eval_jaxpr/convert_element_type | solution.py:78
  77.9 2.7 %convolution_bitcast_fusion = f32[896,12,64]{0,2,1:T(8,128)} fusion(bf16[128,12,64]{0,2,1:T(8,128)(2,1)S(1)} %bitcast.83, bf16[12,128,896]{1,2,0:T(8,128)(2,1)S(1)} %fusion.8), kind=kOutput, calls=%fused_computation.17 | convolution fusion | flops 176160768 | bytes 5701632 | tf_op jit(solution)/shard_map/while/body/eval_jaxpr/hqk,qhd->khd/dot_general | solution.py:98
  81.4 2.9 %multiply_convert_fusion = bf16[12,128,896]{1,2,0:T(8,128)(2,1)} fusion(f32[12,128]{1,0:T(8,128)S(1)} %bitcast.95, bf16[128,12,64]{0,2,1:T(8,128)(2,1)S(1)} %bitcast.85, bf16[896,12,64]{0,2,1:T(8,128)(2,1)S(1)} %copy-done.3, f32[12,128,896]{1,2,0:T(8,128)S(1)} %bitcast.82, f32[12,128]{1,0:T(8,128)S(1)} %get-tuple-element.57), kind=kOutput, calls=%fused_computation.8 | convolution fusion | flops 181665792 | bytes 9842688 | tf_op jit(solution)/shard_map/while/body/eval_jaxpr/qhd,khd->hqk/dot_general | solution.py:83
  84.3 4.2 %stack.25 = f32[1,1,7,128,768]{3,2,4,1,0:T(8,128)} reshape(f32[896,12,64]{0,2,1:T(8,128)} %convolution_bitcast_fusion) | data formatting | bytes 5505024 | tf_op jit(solution)/shard_map/while/body/eval_jaxpr/stack | solution.py:102
  88.4 4.5 %multiply_bitcast_fusion = f32[896,12,64]{0,2,1:T(8,128)} fusion(bf16[12,128,896]{1,2,0:T(8,128)(2,1)} %multiply_convert_fusion, bf16[128,12,64]{0,2,1:T(8,128)(2,1)S(1)} %bitcast.89), kind=kOutput, calls=%fused_computation.11 | convolution fusion | flops 176848896 | bytes 5701632 | tf_op jit(solution)/shard_map/while/body/eval_jaxpr/hqk,qhd->khd/dot_general | solution.py:95
  92.9 4.2 %stack.24 = f32[1,1,7,128,768]{3,2,4,1,0:T(8,128)} reshape(f32[896,12,64]{0,2,1:T(8,128)} %multiply_bitcast_fusion) | data formatting | bytes 5505024 | tf_op jit(solution)/shard_map/while/body/eval_jaxpr/stack | solution.py:102
  97.1 1.5 convolution_convert_fusion
  98.6 6.1 %maximum_bitcast_fusion = f32[7,2,128,768]{2,0,3,1:T(8,128)} fusion(f32[1,1,7,128,768]{3,2,4,1,0:T(8,128)} %stack.25, f32[1,1,7,128,768]{3,2,4,1,0:T(8,128)} %stack.24), kind=kLoop, calls=%fused_computation.3 | loop fusion | flops 1376256 | bytes 11010048 | tf_op jit(solution)/shard_map/while/body/eval_jaxpr/stack | solution.py:102
  104.7 6.4 %copy.44 = f32[7,2,128,768]{3,2,1,0:T(8,128)} copy(f32[7,2,128,768]{2,0,3,1:T(8,128)} %maximum_bitcast_fusion) | data formatting | bytes 11010048 | tf_op jit(solution)/shard_map/while/body/eval_jaxpr/stack | solution.py:102
  111.1 3.0 %broadcast.96 = f32[2,7,128,768]{3,2,1,0:T(8,128)} broadcast(f32[]{:T(128)} %constant.87.clone.1), dimensions={} | broadcast | bytes 5505028 | tf_op jit(solution)/shard_map/broadcast_in_dim | solution.py:115
  114.1 14.1 %scatter_fusion = f32[2,7,128,768]{3,2,1,0:T(8,128)} fusion(f32[2,7,128,768]{3,2,1,0:T(8,128)} %broadcast.96, s32[7]{0:T(128)S(1)} %fusion.23, f32[7,2,128,768]{3,2,1,0:T(8,128)} %copy.44), kind=kCustom, calls=%fused_computation.1 | custom fusion | flops 1376256 | bytes 16515100 | tf_op jit(solution)/shard_map/scatter-add | solution.py:117
  128.2 2.9 %bitcast_convert_fusion = bf16[2,1,7,128,768]{4,3,2,0,1:T(8,128)(2,1)S(1)} fusion(f32[2,7,128,768]{3,2,1,0:T(8,128)} %scatter_fusion), kind=kLoop, calls=%fused_computation.60 | loop fusion | flops 1376256 | bytes 8257536 | tf_op jit(solution)/shard_map/convert.7
  131.1 1.1 fusion.26
  132.1 2.1 collective-permute-start.10
  134.2 1.4 collective-permute-start.9
  135.6 3.0 %collective-permute-start.8 = (bf16[2,1,1,128,768]{4,3,2,0,1:T(8,128)(2,1)}, bf16[2,1,1,128,768]{4,3,2,0,1:T(8,128)(2,1)}, u32[]{:S(2)}, u32[]{:S(2)}) collective-permute-start(bf16[2,1,1,128,768]{4,3,2,0,1:T(8,128)(2,1)} %get-tuple-element.51), channel_id=1, source_target_pairs={{0,15},{1,0},{2,1},{3,2},{4,3},{5,4},{6,5},{7,6},{8,7},{9,8},{10,9... | collective-permute-start | bytes 1179656 | tf_op jit(solution)/shard_map/ppermute | solution.py:19
  138.6 1.7 collective-permute-start.7
  140.3 0.9 collective-permute-done.11
  141.2 3.5 %collective-permute-start.6 = (bf16[2,1,1,128,768]{4,3,2,0,1:T(8,128)(2,1)S(1)}, bf16[2,1,1,128,768]{4,3,2,0,1:T(8,128)(2,1)}, u32[]{:S(2)}, u32[]{:S(2)}) collective-permute-start(bf16[2,1,1,128,768]{4,3,2,0,1:T(8,128)(2,1)S(1)} %get-tuple-element.47), channel_id=1, source_target_pairs={{0,13},{1,14},{2,15},{3,0},{4,1},{5,2},{6,3},{7,4},{8,5},{9,6},{10... | collective-permute-start | bytes 1179656 | tf_op jit(solution)/shard_map/ppermute | solution.py:19
  145.4 0.8 copy.45
  146.2 1.0 fusion.10
  147.2 16.7 %collective-permute-done.10 = bf16[2,1,1,128,768]{4,3,2,0,1:T(8,128)(2,1)S(1)} collective-permute-done((bf16[2,1,1,128,768]{4,3,2,0,1:T(8,128)(2,1)}, bf16[2,1,1,128,768]{4,3,2,0,1:T(8,128)(2,1)S(1)}, u32[]{:S(2)}, u32[]{:S(2)}) %collective-permute-start.10) | collective-permute-done | bytes 393248 | tf_op jit(solution)/shard_map/ppermute | solution.py:19
  163.9 8.6 %collective-permute-done.7 = bf16[2,1,1,128,768]{4,3,2,0,1:T(8,128)(2,1)} collective-permute-done((bf16[2,1,1,128,768]{4,3,2,0,1:T(8,128)(2,1)S(1)}, bf16[2,1,1,128,768]{4,3,2,0,1:T(8,128)(2,1)}, u32[]{:S(2)}, u32[]{:S(2)}) %collective-permute-start.7) | collective-permute-done | bytes 393248 | tf_op jit(solution)/shard_map/ppermute | solution.py:19
  172.5 1.8 fusion.16
  175.1 69.7 %all-reduce.1 = f32[384,768]{1,0:T(8,128)S(1)} all-reduce(bf16[384,768]{1,0:T(8,128)(2,1)} %reduce-scatter.2.cloned.1.call-done), channel_id=1, replica_groups=mesh['dp'=2,'station'=16] {'station'}, use_global_device_ids=true, to_apply=%region_5.6 | all-reduce | flops 294912 | bytes 1769472 | tf_op jit(solution)/shard_map/psum | solution.py:138
  244.9 1.1 broadcast_multiply_fusion
  (48 shorter events, 6.5 us)
Async XLA Ops:
  7.2 12.1 %copy-start = (bf16[768,768]{1,0:T(8,128)(2,1)S(1)}, bf16[768,768]{1,0:T(8,128)(2,1)}, u32[]{:S(2)}) copy-start(bf16[768,768]{1,0:T(8,128)(2,1)} %param.11) | copy-start | bytes 3538948
  7.2 14.7 %copy-start.7 = (bf16[1,1,128,768]{3,2,1,0:T(8,128)(2,1)S(1)}, bf16[1,1,128,768]{3,2,1,0:T(8,128)(2,1)}, u32[]{:S(2)}) copy-start(bf16[1,1,128,768]{3,2,1,0:T(8,128)(2,1)} %param.7) | copy-start | bytes 589828
  7.2 167.9 %reduce-scatter.2.cloned.1.call-start = ((), (), s32[]{:S(2)}) async-start(), calls=%async_computation.1 | async-start | bytes 1769472 | tf_op jit(solution)/shard_map/reduce_scatter | solution.py:130
  7.2 40.6 %copy-start.5 = (bf16[1,1,128,768]{3,2,1,0:T(8,128)(2,1)S(1)}, bf16[1,1,128,768]{3,2,1,0:T(8,128)(2,1)}, u32[]{:S(2)}) copy-start(bf16[1,1,128,768]{3,2,1,0:T(8,128)(2,1)} %param.9) | copy-start | bytes 589828
  7.2 40.6 %copy-start.6 = (bf16[1,1,128,768]{3,2,1,0:T(8,128)(2,1)S(1)}, bf16[1,1,128,768]{3,2,1,0:T(8,128)(2,1)}, u32[]{:S(2)}) copy-start(bf16[1,1,128,768]{3,2,1,0:T(8,128)(2,1)} %param.8) | copy-start | bytes 589828
  8.4 27.5 %collective-permute-start = (bf16[2,1,1,128,768]{4,3,2,1,0:T(8,128)(2,1)S(1)}, bf16[2,1,1,128,768]{4,3,2,1,0:T(8,128)(2,1)}, u32[]{:S(2)}, u32[]{:S(2)}) collective-permute-start(bf16[2,1,1,128,768]{4,3,2,1,0:T(8,128)(2,1)S(1)} %pad_maximum_fusion), channel_id=1, source_target_pairs={{0,3},{1,4},{2,5},{3,6},{4,7},{5,8},{6,9},{7,10},{8,11},{9,12},{10... | collective-permute-start | bytes 1179656 | tf_op jit(solution)/shard_map/ppermute | solution.py:19
  10.9 33.5 %collective-permute-start.1 = (bf16[2,1,1,128,768]{4,3,2,1,0:T(8,128)(2,1)S(1)}, bf16[2,1,1,128,768]{4,3,2,1,0:T(8,128)(2,1)}, u32[]{:S(2)}, u32[]{:S(2)}) collective-permute-start(bf16[2,1,1,128,768]{4,3,2,1,0:T(8,128)(2,1)S(1)} %pad_maximum_fusion), channel_id=1, source_target_pairs={{0,2},{1,3},{2,4},{3,5},{4,6},{5,7},{6,8},{7,9},{8,10},{9,11},{10,... | collective-permute-start | bytes 1179656 | tf_op jit(solution)/shard_map/ppermute | solution.py:19
  12.4 33.7 %collective-permute-start.2 = (bf16[2,1,1,128,768]{4,3,2,1,0:T(8,128)(2,1)S(1)}, bf16[2,1,1,128,768]{4,3,2,1,0:T(8,128)(2,1)}, u32[]{:S(2)}, u32[]{:S(2)}) collective-permute-start(bf16[2,1,1,128,768]{4,3,2,1,0:T(8,128)(2,1)S(1)} %pad_maximum_fusion), channel_id=1, source_target_pairs={{0,1},{1,2},{2,3},{3,4},{4,5},{5,6},{6,7},{7,8},{8,9},{9,10},{10,1... | collective-permute-start | bytes 1179656 | tf_op jit(solution)/shard_map/ppermute | solution.py:19
  12.8 35.8 %collective-permute-start.3 = (bf16[2,1,1,128,768]{4,3,2,1,0:T(8,128)(2,1)S(1)}, bf16[2,1,1,128,768]{4,3,2,1,0:T(8,128)(2,1)S(1)}, u32[]{:S(2)}, u32[]{:S(2)}) collective-permute-start(bf16[2,1,1,128,768]{4,3,2,1,0:T(8,128)(2,1)S(1)} %pad_maximum_fusion), channel_id=1, source_target_pairs={{0,15},{1,0},{2,1},{3,2},{4,3},{5,4},{6,5},{7,6},{8,7},{9,8},{10,9... | collective-permute-start | bytes 1179656 | tf_op jit(solution)/shard_map/ppermute | solution.py:19
  16.9 33.1 %collective-permute-start.4 = (bf16[2,1,1,128,768]{4,3,2,1,0:T(8,128)(2,1)S(1)}, bf16[2,1,1,128,768]{4,3,2,1,0:T(8,128)(2,1)S(1)}, u32[]{:S(2)}, u32[]{:S(2)}) collective-permute-start(bf16[2,1,1,128,768]{4,3,2,1,0:T(8,128)(2,1)S(1)} %pad_maximum_fusion), channel_id=1, source_target_pairs={{0,14},{1,15},{2,0},{3,1},{4,2},{5,3},{6,4},{7,5},{8,6},{9,7},{10,... | collective-permute-start | bytes 1179656 | tf_op jit(solution)/shard_map/ppermute | solution.py:19
  35.9 14.9 %collective-permute-start.5 = (bf16[2,1,1,128,768]{4,3,2,1,0:T(8,128)(2,1)S(1)}, bf16[2,1,1,128,768]{4,3,2,1,0:T(8,128)(2,1)S(1)}, u32[]{:S(2)}, u32[]{:S(2)}) collective-permute-start(bf16[2,1,1,128,768]{4,3,2,1,0:T(8,128)(2,1)S(1)} %pad_maximum_fusion), channel_id=1, source_target_pairs={{0,13},{1,14},{2,15},{3,0},{4,1},{5,2},{6,3},{7,4},{8,5},{9,6},{10... | collective-permute-start | bytes 1179656 | tf_op jit(solution)/shard_map/ppermute | solution.py:19
  74.6 6.7 %slice-start = ((s8[5505024]{0:T(1024)(128)(4,1)}), s8[4194304]{0:T(1024)(128)(4,1)S(1)}, s32[]{:S(2)}) async-start(s8[5505024]{0:T(1024)(128)(4,1)} %bitcast.81), calls=%async_computation.2 | async-start | bytes 8388608
  77.9 2.7 %copy-start.3 = (bf16[896,12,64]{0,2,1:T(8,128)(2,1)S(1)}, bf16[896,12,64]{0,2,1:T(8,128)(2,1)}, u32[]{:S(2)}) copy-start(bf16[896,12,64]{0,2,1:T(8,128)(2,1)} %squeeze.36) | copy-start | bytes 4128772
  77.9 3.4 %slice-start.1 = ((s8[5505024]{0:T(1024)(128)(4,1)}), s8[1310720]{0:T(1024)(128)(4,1)S(1)}, s32[]{:S(2)}) async-start(s8[5505024]{0:T(1024)(128)(4,1)} %bitcast.81), calls=%async_computation.3 | async-start | bytes 2621440
  92.9 4.2 %copy-start.4 = (bf16[1,1,128,768]{3,2,1,0:T(8,128)(2,1)S(1)}, bf16[1,1,128,768]{3,2,1,0:T(8,128)(2,1)}, u32[]{:S(2)}) copy-start(bf16[1,1,128,768]{3,2,1,0:T(8,128)(2,1)} %param.10) | copy-start | bytes 589828
  131.1 13.7 %copy-start.1 = (bf16[12,128,896]{1,2,0:T(8,128)(2,1)S(1)}, bf16[12,128,896]{1,2,0:T(8,128)(2,1)}, u32[]{:S(2)}) copy-start(bf16[12,128,896]{1,2,0:T(8,128)(2,1)} %multiply_convert_fusion) | copy-start | bytes 8257540
  131.1 13.6 %copy-start.2 = (bf16[896,12,64]{0,2,1:T(8,128)(2,1)S(1)}, bf16[896,12,64]{0,2,1:T(8,128)(2,1)}, u32[]{:S(2)}) copy-start(bf16[896,12,64]{0,2,1:T(8,128)(2,1)} %squeeze.37) | copy-start | bytes 4128772
  132.1 9.1 %collective-permute-start.11 = (bf16[2,1,1,128,768]{4,3,2,0,1:T(8,128)(2,1)S(1)}, bf16[2,1,1,128,768]{4,3,2,0,1:T(8,128)(2,1)S(1)}, u32[]{:S(2)}, u32[]{:S(2)}) collective-permute-start(bf16[2,1,1,128,768]{4,3,2,0,1:T(8,128)(2,1)S(1)} %get-tuple-element.48), channel_id=1, source_target_pairs={{0,3},{1,4},{2,5},{3,6},{4,7},{5,8},{6,9},{7,10},{8,11},{9,12},{10... | collective-permute-start | bytes 1179656 | tf_op jit(solution)/shard_map/ppermute | solution.py:19
  132.1 31.8 %collective-permute-start.10 = (bf16[2,1,1,128,768]{4,3,2,0,1:T(8,128)(2,1)}, bf16[2,1,1,128,768]{4,3,2,0,1:T(8,128)(2,1)S(1)}, u32[]{:S(2)}, u32[]{:S(2)}) collective-permute-start(bf16[2,1,1,128,768]{4,3,2,0,1:T(8,128)(2,1)} %get-tuple-element.49), channel_id=1, source_target_pairs={{0,2},{1,3},{2,4},{3,5},{4,6},{5,7},{6,8},{7,9},{8,10},{9,11},{10,... | collective-permute-start | bytes 1179656 | tf_op jit(solution)/shard_map/ppermute | solution.py:19
  134.2 29.8 %collective-permute-start.9 = (bf16[2,1,1,128,768]{4,3,2,0,1:T(8,128)(2,1)}, bf16[2,1,1,128,768]{4,3,2,0,1:T(8,128)(2,1)S(1)}, u32[]{:S(2)}, u32[]{:S(2)}) collective-permute-start(bf16[2,1,1,128,768]{4,3,2,0,1:T(8,128)(2,1)} %get-tuple-element.50), channel_id=1, source_target_pairs={{0,1},{1,2},{2,3},{3,4},{4,5},{5,6},{6,7},{7,8},{8,9},{9,10},{10,1... | collective-permute-start | bytes 1179656 | tf_op jit(solution)/shard_map/ppermute | solution.py:19
  135.6 28.3 %collective-permute-start.8 = (bf16[2,1,1,128,768]{4,3,2,0,1:T(8,128)(2,1)}, bf16[2,1,1,128,768]{4,3,2,0,1:T(8,128)(2,1)}, u32[]{:S(2)}, u32[]{:S(2)}) collective-permute-start(bf16[2,1,1,128,768]{4,3,2,0,1:T(8,128)(2,1)} %get-tuple-element.51), channel_id=1, source_target_pairs={{0,15},{1,0},{2,1},{3,2},{4,3},{5,4},{6,5},{7,6},{8,7},{9,8},{10,9... | collective-permute-start | bytes 1179656 | tf_op jit(solution)/shard_map/ppermute | solution.py:19
  138.6 33.9 %collective-permute-start.7 = (bf16[2,1,1,128,768]{4,3,2,0,1:T(8,128)(2,1)S(1)}, bf16[2,1,1,128,768]{4,3,2,0,1:T(8,128)(2,1)}, u32[]{:S(2)}, u32[]{:S(2)}) collective-permute-start(bf16[2,1,1,128,768]{4,3,2,0,1:T(8,128)(2,1)S(1)} %get-tuple-element.52), channel_id=1, source_target_pairs={{0,14},{1,15},{2,0},{3,1},{4,2},{5,3},{6,4},{7,5},{8,6},{9,7},{10,... | collective-permute-start | bytes 1179656 | tf_op jit(solution)/shard_map/ppermute | solution.py:19
  141.2 31.3 %collective-permute-start.6 = (bf16[2,1,1,128,768]{4,3,2,0,1:T(8,128)(2,1)S(1)}, bf16[2,1,1,128,768]{4,3,2,0,1:T(8,128)(2,1)}, u32[]{:S(2)}, u32[]{:S(2)}) collective-permute-start(bf16[2,1,1,128,768]{4,3,2,0,1:T(8,128)(2,1)S(1)} %get-tuple-element.47), channel_id=1, source_target_pairs={{0,13},{1,14},{2,15},{3,0},{4,1},{5,2},{6,3},{7,4},{8,5},{9,6},{10... | collective-permute-start | bytes 1179656 | tf_op jit(solution)/shard_map/ppermute | solution.py:19
Sparse Core Ops, SparseCore 0:
  98.7 24.7 reduce-scatter.1
where the time goes:
time: 254 us; the launch traced here: 253 us
  blocking collectives  69.7 us (27%)
  waiting for transfers between devices  47.3 us (19%)
  local copies, waits for them, and re-layouts  44.7 us (18%)
  other arithmetic  34.9 us (14%)
  matrix products  21.3 us (8%)
  starting transfers between devices  20.6 us (8%)
  between operations  14.2 us (6%)
    psum x1, blocking collectives, local(): grad_weight = lax.psum(grad_weight, 'station')  69.7 us
    ppermute x12, waiting for transfers between devices, from_behind(): return lax.ppermute(value, axis, pairs)  47.3 us
    ppermute x12, starting transfers between devices, from_behind(): return lax.ppermute(value, axis, pairs)  20.6 us
    another operation x3, local copies, waits for them, and re-layouts, one_station(): jnp.stack([key_part, value_part], 0).reshape(2, -1, span_rows, model_width)  14.7 us
    scatter-add x1, other arithmetic, local(): spread = jnp.zeros((2, window_count, candidates, span_rows, model_width),...  14.1 us
    unnamed x27, local copies, waits for them, and re-layouts  7.86 us
    another operation x1, other arithmetic, one_station(): jnp.stack([key_part, value_part], 0).reshape(2, -1, span_rows, model_width)  6.11 us
    sub x1, matrix products, one_station(): weights_raw = jnp.exp(masked - row_max[..., None])  5.93 us
  transfers between devices with their start and end apart: 13, of which 6 were waited for; matrix products, arithmetic and copies ran while one was open for 20% of the time, Pallas kernels for 0%

commit v1 on v0

v1 whole, which is shorter than its diff:
```python
import functools
import math

import jax
import jax.numpy as jnp
from jax import lax
from jax.experimental import pallas as pl
from jax.experimental.pallas import tpu as pltpu
from jax.sharding import PartitionSpec as P

HEADS = 12
PMAX = 6
GROUP = 4

neg_big = -1e30


def attend(
    my_ref, ids_ref, count_ref, q_ref, g_ref, k_ref, v_ref, a_ref, b_ref, c_ref, s_ref, sa_ref, sb_ref,
    mixed_ref, dq_ref, own_ref, sib_ref, oa_ref, ob_ref, oc_ref,
    keys, values, q_wide, g_wide, probs, probs_half, grads, grads_half,
    *, station_count,
):
    span, width = q_ref.shape
    head_width = width // HEADS
    lanes = GROUP * head_width
    slots = PMAX + 1
    me = my_ref[0]
    side = 2 * lax.rem(me, 2) - 1
    offsets = (0, side, 2 * side, 3 * side, -side, -2 * side, -3 * side)
    live = []
    for offset in offsets:
        station = lax.rem(me + offset + station_count, station_count)
        hit = jnp.int32(1) if not live else jnp.int32(0)
        for j in range(PMAX):
            here = jnp.logical_and(ids_ref[me, j] == station, j < count_ref[me])
            hit = jnp.maximum(hit, here.astype(jnp.int32))
        live.append(hit)
    keys[0:span] = k_ref[...]
    values[0:span] = v_ref[...]
    for j, ref in enumerate((a_ref, b_ref, c_ref, s_ref, sa_ref, sb_ref)):
        keys[(j + 1) * span : (j + 2) * span] = ref[0]
        values[(j + 1) * span : (j + 2) * span] = ref[1]
    head_of = lax.broadcasted_iota(jnp.int32, (span, lanes), 1) // head_width
    nt = (((1,), (1,)), ((), ()))
    tn = (((0,), (0,)), ((), ()))
    nn = (((1,), (0,)), ((), ()))
    f32 = jnp.float32

    def dot(x, y, dims):
        return lax.dot_general(x, y, dims, preferred_element_type=f32)

    def pick(wide):
        blocks = [
            wide[h * head_width : (h + 1) * head_width, h * span : (h + 1) * span] for h in range(GROUP)
        ]
        return jnp.concatenate(blocks, 0).T

    for group in range(HEADS // GROUP):
        at = slice(group * lanes, (group + 1) * lanes)
        q_now = q_ref[:, at] * jnp.bfloat16(1.0 / math.sqrt(head_width))
        g_now = g_ref[:, at]
        zero = jnp.zeros_like(q_now)
        for h in range(GROUP):
            q_wide[h * span : (h + 1) * span] = jnp.where(head_of == h, q_now, zero)
            g_wide[h * span : (h + 1) * span] = jnp.where(head_of == h, g_now, zero)
        top = None
        for j in range(slots):
            rows = slice(j * span, (j + 1) * span)
            scores = dot(keys[rows, at], q_wide[...], nt)
            scores = jnp.where(live[j] > 0, scores, neg_big)
            probs[rows] = scores
            here = jnp.max(scores, 0, keepdims=True)
            top = here if top is None else jnp.maximum(top, here)
        total = jnp.zeros_like(top)
        for j in range(slots):
            rows = slice(j * span, (j + 1) * span)
            raw = jnp.exp(probs[rows] - top)
            probs[rows] = raw
            total = total + jnp.sum(raw, 0, keepdims=True)
        inverse = 1.0 / total
        delta = jnp.zeros_like(top)
        for j in range(slots):
            rows = slice(j * span, (j + 1) * span)
            prob = probs[rows] * inverse
            probs[rows] = prob
            probs_half[rows] = prob.astype(jnp.bfloat16)
            back = dot(values[rows, at], g_wide[...], nt)
            grads[rows] = back
            delta = delta + jnp.sum(back * prob, 0, keepdims=True)
        for j in range(slots):
            rows = slice(j * span, (j + 1) * span)
            grads_half[rows] = (probs[rows] * (grads[rows] - delta)).astype(jnp.bfloat16)
        mixed_ref[:, at] = pick(dot(values[:, at], probs_half[...], tn)).astype(jnp.bfloat16)
        query_grad = pick(dot(keys[:, at], grads_half[...], tn))
        dq_ref[:, at] = (query_grad * (1.0 / math.sqrt(head_width))).astype(jnp.bfloat16)
        for part, left, right in ((0, grads_half, q_wide), (1, probs_half, g_wide)):
            for j in range(slots):
                rows = slice(j * span, (j + 1) * span)
                piece = dot(left[rows], right[...], nn)
                if j == 0:
                    own_ref[part, :, at] = piece
                elif j <= 3:
                    (oa_ref, ob_ref, oc_ref)[j - 1][part, :, at] = piece.astype(jnp.bfloat16)
                else:
                    sib_ref[j - 4, part, :, at] = piece.astype(jnp.bfloat16)


def local(
    query_states, key_states, value_states, grad_output, out_weight, partner_ids, partner_count
):
    span, width = query_states.shape[2:]
    bf16, f32 = jnp.bfloat16, jnp.float32
    stations = lax.axis_size("station")
    windows = lax.axis_size("dp")
    me = lax.axis_index("station")
    side = [1 if s % 2 else -1 for s in range(stations)]

    def routes(steps):
        return [((s + steps * side[s]) % stations, s) for s in range(stations)]

    def back(pairs):
        return [(d, s) for s, d in pairs]

    def swap(value, stride):
        return lax.ppermute(value, "station", [(s ^ stride, s) for s in range(stations)])

    def flat(x):
        return x.reshape(span, width)

    q, k, v, g = flat(query_states), flat(key_states), flat(value_states), flat(grad_output)
    own = jnp.stack([k, v], 0)
    near = lax.ppermute(own, "station", routes(1))
    middle = lax.ppermute(own, "station", routes(2))
    far = lax.ppermute(own, "station", routes(3))
    sib = swap(own, 1)
    sib_near = swap(near, 1)
    sib_middle = swap(middle, 1)
    if windows == 2:
        g_peer = lax.ppermute(g, "dp", [(0, 1), (1, 0)])
    grad_mixed = lax.dot_general(
        g, out_weight, (((1,), (1,)), ((), ())), preferred_element_type=f32
    ).astype(bf16)

    slots = PMAX + 1
    lanes = width // HEADS * GROUP
    pair = jax.ShapeDtypeStruct((2, span, width), bf16)
    flat_shape = jax.ShapeDtypeStruct((span, width), bf16)
    smem = pl.BlockSpec(memory_space=pltpu.SMEM)
    vmem = pl.BlockSpec(memory_space=pltpu.VMEM)
    mixed, grad_query, own_grad, sib_grad, near_grad, middle_grad, far_grad = pl.pallas_call(
        functools.partial(attend, station_count=stations),
        in_specs=[smem] * 3 + [vmem] * 10,
        out_specs=[vmem] * 7,
        out_shape=[
            flat_shape,
            flat_shape,
            jax.ShapeDtypeStruct((2, span, width), f32),
            jax.ShapeDtypeStruct((3, 2, span, width), bf16),
            pair,
            pair,
            pair,
        ],
        scratch_shapes=[
            pltpu.VMEM((slots * span, width), bf16),
            pltpu.VMEM((slots * span, width), bf16),
            pltpu.VMEM((GROUP * span, lanes), bf16),
            pltpu.VMEM((GROUP * span, lanes), bf16),
            pltpu.VMEM((slots * span, GROUP * span), f32),
            pltpu.VMEM((slots * span, GROUP * span), bf16),
            pltpu.VMEM((slots * span, GROUP * span), f32),
            pltpu.VMEM((slots * span, GROUP * span), bf16),
        ],
        compiler_params=pltpu.CompilerParams(vmem_limit_bytes=40 * 1024 * 1024),
        cost_estimate=pl.CostEstimate(
            flops=2 * 5 * slots * span * span * width * 4,
            bytes_accessed=30 * span * width * 2,
            transcendentals=HEADS * slots * span * span,
        ),
        name="attend",
    )(
        me.reshape(1).astype(jnp.int32), partner_ids, partner_count,
        q, grad_mixed, k, v, near, middle, far, sib, sib_near, sib_middle,
    )

    far_home = lax.ppermute(far_grad, "station", back(routes(3)))
    from_sib = swap(sib_grad, 1)
    near_sum = (near_grad.astype(f32) + from_sib[1].astype(f32)).astype(bf16)
    middle_sum = (middle_grad.astype(f32) + from_sib[2].astype(f32)).astype(bf16)
    near_home = lax.ppermute(near_sum, "station", back(routes(1)))
    middle_home = lax.ppermute(middle_sum, "station", back(routes(2)))

    layer_output = jnp.dot(mixed, out_weight, preferred_element_type=f32).astype(bf16)

    dims = (((0,), (0,)), ((), ()))
    rows = width // windows
    if windows == 2:
        w_no = lax.axis_index("dp")
        mine = lax.dynamic_slice_in_dim(mixed, w_no * rows, rows, 1)
        other = lax.dynamic_slice_in_dim(mixed, (1 - w_no) * rows, rows, 1)
        peer = lax.ppermute(other, "dp", [(0, 1), (1, 0)])
        part = lax.dot_general(
            jnp.concatenate([mine, peer], 0), jnp.concatenate([g, g_peer], 0), dims,
            preferred_element_type=f32,
        )
    else:
        whole = lax.dot_general(mixed, g, dims, preferred_element_type=f32).astype(bf16)
        part = lax.psum_scatter(whole, "dp", scatter_dimension=0, tiled=True).astype(f32)
    stride = 1
    halved = []
    while stride < stations:
        if rows % 32 == 0 and rows >= 96:
            rows //= 2
            bit = (me // stride) % 2
            keep = lax.dynamic_slice_in_dim(part, bit * rows, rows, 0)
            send = lax.dynamic_slice_in_dim(part, (1 - bit) * rows, rows, 0).astype(bf16)
            part = keep + swap(send, stride).astype(f32)
            halved.append((stride, bit))
        else:
            half = part.astype(bf16)
            part = half.astype(f32) + swap(half, stride).astype(f32)
        stride *= 2
    result = part.astype(bf16)
    for stride, bit in reversed(halved):
        got = swap(result, stride)
        result = jnp.where(
            bit == 0, jnp.concatenate([result, got], 0), jnp.concatenate([got, result], 0)
        )
    token_count = span * windows * stations
    grad_weight = result.astype(f32) / math.sqrt(token_count)

    home = (
        own_grad + from_sib[0].astype(f32) + far_home.astype(f32) + near_home.astype(f32)
        + middle_home.astype(f32)
    ).astype(bf16)
    shape = query_states.shape
    return (
        layer_output.reshape(shape),
        grad_query.reshape(shape),
        home[0].reshape(shape),
        home[1].reshape(shape),
        grad_weight,
    )


def solution(mesh):
    split = P("dp", "station", None, None)
    return jax.shard_map(
        local,
        mesh=mesh,
        in_specs=(split, split, split, split, P(), P(), P()),
        out_specs=(split, split, split, split, P("dp", None)),
        check_vma=False,
    )
```

time: 254 us -> 113 us (0.44)
  the two profiles are of different devices: /device:TPU:0 before, /device:TPU:1 now
where the time goes in v1:
time: 113 us; the launch traced here: 112 us
  waiting for transfers between devices  42.3 us (37%)
  starting transfers between devices  29.6 us (26%)
  other arithmetic  13.8 us (12%)
  local copies, waits for them, and re-layouts  12.1 us (11%)
  Pallas kernels  9.55 us (8%)
  matrix products  3.85 us (3%)
    ppermute x11, starting transfers between devices, swap(): lax.ppermute(value, 'station', [(s ^ stride, s) for s in range(stations)])  15.5 us
    ppermute x1, waiting for transfers between devices, local(): near = lax.ppermute(own, 'station', routes(1))  12.5 us
    unnamed x41, local copies, waits for them, and re-layouts  10.6 us
    ppermute x11, waiting for transfers between devices, swap(): lax.ppermute(value, 'station', [(s ^ stride, s) for s in range(stations)])  10.3 us
    ppermute x1, waiting for transfers between devices, local(): middle_home = lax.ppermute(middle_sum, 'station', back(routes(2)))  9.76 us
    pallas_call x1, Pallas kernels, local(): pl.pallas_call(functools.partial(attend, station_count=stations), in_spec...  9.55 us
    ppermute x1, starting transfers between devices, local(): far_home = lax.ppermute(far_grad, 'station', back(routes(3)))  5.82 us
    ppermute x1, waiting for transfers between devices, local(): near_home = lax.ppermute(near_sum, 'station', back(routes(1)))  5.22 us
  transfers between devices with their start and end apart: 19, of which 10 were waited for; matrix products, arithmetic and copies ran while one was open for 11% of the time, Pallas kernels for 9%

profile of v1, /device:TPU:1, one launch (start us, length us, event | category | flops | bytes accessed | tf_op | source)
XLA Modules:
  0.0 112.0 jit_solution(15975941609687586229)
XLA Ops:
  0.7 1.9 %pad_maximum_fusion = bf16[2,128,768]{2,1,0:T(8,128)(2,1)} fusion(bf16[1,128,768]{2,1,0:T(8,128)(2,1)} %bitcast.36, bf16[1,128,768]{2,1,0:T(8,128)(2,1)} %bitcast.34), kind=kLoop, calls=%fused_computation.19 | loop fusion | flops 196608 | bytes 786432 | tf_op jit(solution)/shard_map/stack | solution.py:132
  2.6 2.6 %collective-permute-start = (bf16[2,128,768]{2,1,0:T(8,128)(2,1)}, bf16[2,128,768]{2,1,0:T(8,128)(2,1)S(1)}, u32[]{:S(2)}, u32[]{:S(2)}) collective-permute-start(bf16[2,128,768]{2,1,0:T(8,128)(2,1)} %pad_maximum_fusion), channel_id=1, source_target_pairs={{15,0},{2,1},{1,2},{4,3},{3,4},{6,5},{5,6},{8,7},{7,8},{10,9},{9,1... | collective-permute-start | bytes 1179656 | tf_op jit(solution)/shard_map/ppermute | solution.py:133
  5.2 2.5 %collective-permute-start.1 = (bf16[2,128,768]{2,1,0:T(8,128)(2,1)}, bf16[2,128,768]{2,1,0:T(8,128)(2,1)S(1)}, u32[]{:S(2)}, u32[]{:S(2)}) collective-permute-start(bf16[2,128,768]{2,1,0:T(8,128)(2,1)} %pad_maximum_fusion), channel_id=1, source_target_pairs={{14,0},{3,1},{0,2},{5,3},{2,4},{7,5},{4,6},{9,7},{6,8},{11,9},{8,1... | collective-permute-start | bytes 1179656 | tf_op jit(solution)/shard_map/ppermute | solution.py:134
  7.7 2.4 %collective-permute-start.3 = (bf16[2,128,768]{2,1,0:T(8,128)(2,1)}, bf16[2,128,768]{2,1,0:T(8,128)(2,1)S(1)}, u32[]{:S(2)}, u32[]{:S(2)}) collective-permute-start(bf16[2,128,768]{2,1,0:T(8,128)(2,1)} %pad_maximum_fusion), channel_id=1, source_target_pairs={{1,0},{0,1},{3,2},{2,3},{5,4},{4,5},{7,6},{6,7},{9,8},{8,9},{11,10... | collective-permute-start | bytes 1179656 | tf_op jit(solution)/shard_map/ppermute | solution.py:126
  10.1 12.5 %collective-permute-done.a_ref = bf16[2,128,768]{2,1,0:T(8,128)(2,1)S(1)} collective-permute-done((bf16[2,128,768]{2,1,0:T(8,128)(2,1)}, bf16[2,128,768]{2,1,0:T(8,128)(2,1)S(1)}, u32[]{:S(2)}, u32[]{:S(2)}) %collective-permute-start) | collective-permute-done | bytes 393248 | tf_op jit(solution)/shard_map/ppermute | solution.py:133
  22.6 1.2 %collective-permute-done.1.b_ref = bf16[2,128,768]{2,1,0:T(8,128)(2,1)S(1)} collective-permute-done((bf16[2,128,768]{2,1,0:T(8,128)(2,1)}, bf16[2,128,768]{2,1,0:T(8,128)(2,1)S(1)}, u32[]{:S(2)}, u32[]{:S(2)}) %collective-permute-start.1) | collective-permute-done | bytes 393248 | tf_op jit(solution)/shard_map/ppermute | solution.py:134
  23.8 1.2 %collective-permute-start.11 = (bf16[128,768]{1,0:T(8,128)(2,1)}, bf16[128,768]{1,0:T(8,128)(2,1)}, u32[]{:S(2)}, u32[]{:S(2)}) collective-permute-start(bf16[128,768]{1,0:T(8,128)(2,1)} %bitcast.39), channel_id=1, source_target_pairs={{0,16},{16,0},{1,17},{17,1},{2,18},{18,2},{3,19},{19,3},{4,20},{20... | collective-permute-start | bytes 589832 | tf_op jit(solution)/shard_map/ppermute | solution.py:140
  25.1 0.8 copy.12.ids_ref
  25.8 1.5 %convolution_convert_fusion.1.g_ref = bf16[128,768]{1,0:T(8,128)(2,1)S(1)} fusion(bf16[768,768]{1,0:T(8,128)(2,1)S(1)} %copy-done, bf16[1,1,128,768]{3,2,1,0:T(8,128)(2,1)} %param.10), kind=kOutput, calls=%fused_computation.2 | convolution fusion | flops 151093248 | bytes 1572864 | tf_op jit(solution)/shard_map/dot_general | solution.py:141
  27.3 0.7 copy-done.10
  28.1 0.7 copy-done.12
  28.9 1.0 copy-done.7
  29.9 1.0 copy-done.9
  30.9 1.0 copy-done.11
  31.9 1.0 copy-done.13
  32.9 9.6 %attend.1 = (bf16[128,768]{1,0:T(8,128)(2,1)S(1)}, bf16[128,768]{1,0:T(8,128)(2,1)}, f32[2,128,768]{2,1,0:T(8,128)S(1)}, bf16[3,2,128,768]{3,2,1,0:T(8,128)(2,1)...) custom-call(s32[1]{0:T(128)} %bitcast.my_ref, ...), custom_call_target="tpu_custom_call" | custom-call | flops 3523215360 | bytes 5898240 | tf_op jit(solution)/shard_map/attend/pallas_call | solution.py:151
  42.4 1.0 copy-done.3
  43.4 0.7 copy-done.4
  44.5 3.2 %collective-permute-done.10 = bf16[128,384]{1,0:T(8,128)(2,1)S(1)} collective-permute-done((bf16[128,384]{1,0:T(8,128)(2,1)S(1)}, bf16[128,384]{1,0:T(8,128)(2,1)S(1)}, u32[]{:S(2)}, u32[]{:S(2)}) %collective-permute-start.10) | collective-permute-done | bytes 98336 | tf_op jit(solution)/shard_map/ppermute | solution.py:201
  47.7 1.4 %fusion.7 = f32[384,768]{1,0:T(8,128)S(1)} fusion(bf16[128,768]{1,0:T(8,128)(2,1)} %collective-permute-done.11, bf16[128,768]{1,0:T(8,128)(2,1)} %bitcast.40, bf16[128,384]{1,0:T(8,128)(2,1)S(1)} %collective-permute-done.10, bf16[128,384]{1,0:T(8,128)(2,1)S(1)} %get-tuple-element.23), kind=kOutput, calls=%fused_computation.20 | convolution fusion | flops 152174592 | bytes 1769472 | tf_op jit(solution)/shard_map/dot_general | solution.py:202
  49.1 1.0 copy-done.16
  50.2 2.0 %collective-permute-start.12 = (bf16[192,768]{1,0:T(8,128)(2,1)S(1)}, bf16[192,768]{1,0:T(8,128)(2,1)S(1)}, u32[]{:S(2)}, u32[]{:S(2)}) collective-permute-start(bf16[192,768]{1,0:T(8,128)(2,1)S(1)} %dynamic-slice_convert_fusion), channel_id=1, source_target_pairs={{1,0},{0,1},{3,2},{2,3},{5,4},{4,5},{7,6},{6,7},{9,8},{8,9},{11,10... | collective-permute-start | bytes 884744 | tf_op jit(solution)/shard_map/ppermute | solution.py:126
  52.2 1.2 %collective-permute-done.12 = bf16[192,768]{1,0:T(8,128)(2,1)S(1)} collective-permute-done((bf16[192,768]{1,0:T(8,128)(2,1)S(1)}, bf16[192,768]{1,0:T(8,128)(2,1)S(1)}, u32[]{:S(2)}, u32[]{:S(2)}) %collective-permute-start.12) | collective-permute-done | bytes 294944 | tf_op jit(solution)/shard_map/ppermute | solution.py:126
  53.4 1.1 convert_add_fusion.3
  54.5 0.8 copy-done.17
  56.0 1.4 %collective-permute-start.13 = (bf16[96,768]{1,0:T(8,128)(2,1)}, bf16[96,768]{1,0:T(8,128)(2,1)S(1)}, u32[]{:S(2)}, u32[]{:S(2)}) collective-permute-start(bf16[96,768]{1,0:T(8,128)(2,1)} %dynamic-slice_convert_fusion.1), channel_id=1, source_target_pairs={{2,0},{3,1},{0,2},{1,3},{6,4},{7,5},{4,6},{5,7},{10,8},{11,9},{8,1... | collective-permute-start | bytes 442376 | tf_op jit(solution)/shard_map/ppermute | solution.py:126
  58.1 3.3 %collective-permute-done.13 = bf16[96,768]{1,0:T(8,128)(2,1)S(1)} collective-permute-done((bf16[96,768]{1,0:T(8,128)(2,1)}, bf16[96,768]{1,0:T(8,128)(2,1)S(1)}, u32[]{:S(2)}, u32[]{:S(2)}) %collective-permute-start.13) | collective-permute-done | bytes 147488 | tf_op jit(solution)/shard_map/ppermute | solution.py:126
  61.3 1.0 convert_add_fusion.4
  63.0 1.4 %collective-permute-start.14 = (bf16[48,768]{1,0:T(8,128)(2,1)S(1)}, bf16[48,768]{1,0:T(8,128)(2,1)S(1)}, u32[]{:S(2)}, u32[]{:S(2)}) collective-permute-start(bf16[48,768]{1,0:T(8,128)(2,1)S(1)} %dynamic-slice_convert_fusion.2), channel_id=1, source_target_pairs={{4,0},{5,1},{6,2},{7,3},{0,4},{1,5},{2,6},{3,7},{12,8},{13,9},{14,... | collective-permute-start | bytes 221192 | tf_op jit(solution)/shard_map/ppermute | solution.py:126
  64.4 1.9 %collective-permute-done.14 = bf16[48,768]{1,0:T(8,128)(2,1)S(1)} collective-permute-done((bf16[48,768]{1,0:T(8,128)(2,1)S(1)}, bf16[48,768]{1,0:T(8,128)(2,1)S(1)}, u32[]{:S(2)}, u32[]{:S(2)}) %collective-permute-start.14) | collective-permute-done | bytes 73760 | tf_op jit(solution)/shard_map/ppermute | solution.py:126
  66.3 0.9 add_convert_fusion.1
  67.2 2.4 %collective-permute-start.15 = (bf16[48,768]{1,0:T(8,128)(2,1)S(1)}, bf16[48,768]{1,0:T(8,128)(2,1)S(1)}, u32[]{:S(2)}, u32[]{:S(2)}) collective-permute-start(bf16[48,768]{1,0:T(8,128)(2,1)S(1)} %add_convert_fusion.1), channel_id=1, source_target_pairs={{8,0},{9,1},{10,2},{11,3},{12,4},{13,5},{14,6},{15,7},{0,8},{1,9},... | collective-permute-start | bytes 221192 | tf_op jit(solution)/shard_map/ppermute | solution.py:126
  69.6 1.8 %collective-permute-done.15 = bf16[48,768]{1,0:T(8,128)(2,1)S(1)} collective-permute-done((bf16[48,768]{1,0:T(8,128)(2,1)S(1)}, bf16[48,768]{1,0:T(8,128)(2,1)S(1)}, u32[]{:S(2)}, u32[]{:S(2)}) %collective-permute-start.15) | collective-permute-done | bytes 73760 | tf_op jit(solution)/shard_map/ppermute | solution.py:126
  71.4 1.5 %collective-permute-start.16 = (bf16[48,768]{1,0:T(8,128)(2,1)S(1)}, bf16[48,768]{1,0:T(8,128)(2,1)}, u32[]{:S(2)}, u32[]{:S(2)}) collective-permute-start(bf16[48,768]{1,0:T(8,128)(2,1)S(1)} %add_convert_fusion), channel_id=1, source_target_pairs={{4,0},{5,1},{6,2},{7,3},{0,4},{1,5},{2,6},{3,7},{12,8},{13,9},{14,... | collective-permute-start | bytes 221192 | tf_op jit(solution)/shard_map/ppermute | solution.py:126
  73.0 2.1 %collective-permute-done.16 = bf16[48,768]{1,0:T(8,128)(2,1)} collective-permute-done((bf16[48,768]{1,0:T(8,128)(2,1)S(1)}, bf16[48,768]{1,0:T(8,128)(2,1)}, u32[]{:S(2)}, u32[]{:S(2)}) %collective-permute-start.16) | collective-permute-done | bytes 73760 | tf_op jit(solution)/shard_map/ppermute | solution.py:126
  75.1 1.0 maximum_select_fusion.2
  76.1 1.4 %collective-permute-start.17 = (bf16[96,768]{1,0:T(8,128)(2,1)S(1)}, bf16[96,768]{1,0:T(8,128)(2,1)}, u32[]{:S(2)}, u32[]{:S(2)}) collective-permute-start(bf16[96,768]{1,0:T(8,128)(2,1)S(1)} %maximum_select_fusion.2), channel_id=1, source_target_pairs={{2,0},{3,1},{0,2},{1,3},{6,4},{7,5},{4,6},{5,7},{10,8},{11,9},{8,1... | collective-permute-start | bytes 442376 | tf_op jit(solution)/shard_map/ppermute | solution.py:126
  77.6 5.8 %collective-permute-start.7 = (bf16[2,128,768]{2,1,0:T(8,128)(2,1)S(1)}, bf16[2,128,768]{2,1,0:T(8,128)(2,1)}, u32[]{:S(2)}, u32[]{:S(2)}) collective-permute-start(bf16[2,128,768]{2,1,0:T(8,128)(2,1)S(1)} %copy-done.5), channel_id=1, source_target_pairs={{0,13},{1,4},{2,15},{3,6},{4,1},{5,8},{6,3},{7,10},{8,5},{9,12},{1... | collective-permute-start | bytes 1179656 | tf_op jit(solution)/shard_map/ppermute | solution.py:186
  83.4 1.8 %maximum_select_fusion.1 = bf16[192,768]{1,0:T(8,128)(2,1)} fusion(bf16[96,768]{1,0:T(8,128)(2,1)} %collective-permute-done.17, bf16[96,768]{1,0:T(8,128)(2,1)S(1)} %maximum_select_fusion.2, pred[]{:T(512)S(6)} %eq.14), kind=kLoop, calls=%fused_computation.24 | loop fusion | flops 1327104 | bytes 589825 | tf_op jit(solution)/shard_map/jit(_where)/select_n | solution.py:226
  85.1 2.4 %collective-permute-start.18 = (bf16[192,768]{1,0:T(8,128)(2,1)}, bf16[192,768]{1,0:T(8,128)(2,1)}, u32[]{:S(2)}, u32[]{:S(2)}) collective-permute-start(bf16[192,768]{1,0:T(8,128)(2,1)} %maximum_select_fusion.1), channel_id=1, source_target_pairs={{1,0},{0,1},{3,2},{2,3},{5,4},{4,5},{7,6},{6,7},{9,8},{8,9},{11,10... | collective-permute-start | bytes 884744 | tf_op jit(solution)/shard_map/ppermute | solution.py:126
  87.6 2.2 %fusion.2 = (bf16[2,128,768]{2,1,0:T(8,128)(2,1)}, bf16[2,128,768]{2,1,0:T(8,128)(2,1)}) fusion(bf16[2,128,768]{2,1,0:T(8,128)(2,1)S(1)} %get-tuple-element.17, bf16[3,2,128,768]{3,2,1,0:T(8,128)(2,1)} %collective-permute-done.6, bf16[2,128,768]{2,1,0:T(8,128)(2,1)S(1)} %get-tuple-element.18), kind=kLoop, calls=%fused_computation.7 | loop fusion | flops 1572864 | bytes 2359296 | tf_op jit(solution)/shard_map/convert_element_type | solution.py:188
  89.8 1.4 %collective-permute-start.9 = (bf16[2,128,768]{2,1,0:T(8,128)(2,1)}, bf16[2,128,768]{2,1,0:T(8,128)(2,1)S(1)}, u32[]{:S(2)}, u32[]{:S(2)}) collective-permute-start(bf16[2,128,768]{2,1,0:T(8,128)(2,1)} %get-tuple-element.20), channel_id=1, source_target_pairs={{0,14},{1,3},{2,0},{3,5},{4,2},{5,7},{6,4},{7,9},{8,6},{9,11},{10,... | collective-permute-start | bytes 1179656 | tf_op jit(solution)/shard_map/ppermute | solution.py:191
  91.4 1.0 fusion
  92.4 2.4 %convert_multiply_fusion = f32[384,768]{1,0:T(8,128)} fusion(bf16[192,768]{1,0:T(8,128)(2,1)} %collective-permute-done.18, bf16[192,768]{1,0:T(8,128)(2,1)} %maximum_select_fusion.1, pred[]{:T(512)S(6)} %eq.13), kind=kLoop, calls=%fused_computation | loop fusion | flops 3244032 | bytes 1769473 | tf_op jit(solution)/shard_map/div | solution.py:230
  94.8 9.8 %collective-permute-done.9 = bf16[2,128,768]{2,1,0:T(8,128)(2,1)S(1)} collective-permute-done((bf16[2,128,768]{2,1,0:T(8,128)(2,1)}, bf16[2,128,768]{2,1,0:T(8,128)(2,1)S(1)}, u32[]{:S(2)}, u32[]{:S(2)}) %collective-permute-start.9) | collective-permute-done | bytes 393248 | tf_op jit(solution)/shard_map/ppermute | solution.py:191
  104.6 5.2 %collective-permute-done.8 = bf16[2,128,768]{2,1,0:T(8,128)(2,1)} collective-permute-done((bf16[2,128,768]{2,1,0:T(8,128)(2,1)}, bf16[2,128,768]{2,1,0:T(8,128)(2,1)}, u32[]{:S(2)}, u32[]{:S(2)}) %collective-permute-start.8) | collective-permute-done | bytes 393248 | tf_op jit(solution)/shard_map/ppermute | solution.py:190
  109.8 1.5 %fusion.6 = bf16[2,128,768]{2,1,0:T(8,128)(2,1)S(1)} fusion(f32[2,128,768]{2,1,0:T(8,128)S(1)} %get-tuple-element.14, bf16[2,128,768]{2,1,0:T(8,128)(2,1)S(1)} %collective-permute-done.9, bf16[2,128,768]{2,1,0:T(8,128)(2,1)} %collective-permute-done.8, bf16[2,128,768]{2,1,0:T(8,128)(2,1)} %collective-permute-done.7, ...), kind=kLoop, calls=%fused_computation.12 | loop fusion | flops 1769472 | bytes 2752512 | tf_op jit(solution)/shard_map/convert_element_type | solution.py:235
  111.3 0.8 slice_bitcast_fusion.3
  (50 shorter events, 2.8 us)
Async XLA Ops:
  0.6 25.2 %copy-start = (bf16[768,768]{1,0:T(8,128)(2,1)S(1)}, bf16[768,768]{1,0:T(8,128)(2,1)}, u32[]{:S(2)}) copy-start(bf16[768,768]{1,0:T(8,128)(2,1)} %param.11) | copy-start | bytes 3538948
  0.6 28.2 %copy-start.1 = (bf16[1,1,128,768]{3,2,1,0:T(8,128)(2,1)S(1)}, bf16[1,1,128,768]{3,2,1,0:T(8,128)(2,1)}, u32[]{:S(2)}) copy-start(bf16[1,1,128,768]{3,2,1,0:T(8,128)(2,1)} %param.8) | copy-start | bytes 589828
  0.7 28.2 %copy-start.2 = (bf16[1,1,128,768]{3,2,1,0:T(8,128)(2,1)S(1)}, bf16[1,1,128,768]{3,2,1,0:T(8,128)(2,1)}, u32[]{:S(2)}) copy-start(bf16[1,1,128,768]{3,2,1,0:T(8,128)(2,1)} %param.9) | copy-start | bytes 589828
  0.7 28.2 %copy-start.14 = (bf16[1,1,128,768]{3,2,1,0:T(8,128)(2,1)S(1)}, bf16[1,1,128,768]{3,2,1,0:T(8,128)(2,1)}, u32[]{:S(2)}) copy-start(bf16[1,1,128,768]{3,2,1,0:T(8,128)(2,1)} %param.7) | copy-start | bytes 589828
  0.7 28.2 %copy-start.15 = (s32[16]{0:T(128)S(1)}, s32[16]{0:T(128)}, u32[]{:S(2)}) copy-start(s32[16]{0:T(128)} %count_ref.1) | copy-start | bytes 196
  2.6 20.0 %collective-permute-start = (bf16[2,128,768]{2,1,0:T(8,128)(2,1)}, bf16[2,128,768]{2,1,0:T(8,128)(2,1)S(1)}, u32[]{:S(2)}, u32[]{:S(2)}) collective-permute-start(bf16[2,128,768]{2,1,0:T(8,128)(2,1)} %pad_maximum_fusion), channel_id=1, source_target_pairs={{15,0},{2,1},{1,2},{4,3},{3,4},{6,5},{5,6},{8,7},{7,8},{10,9},{9,1... | collective-permute-start | bytes 1179656 | tf_op jit(solution)/shard_map/ppermute | solution.py:133
  5.2 18.6 %collective-permute-start.1 = (bf16[2,128,768]{2,1,0:T(8,128)(2,1)}, bf16[2,128,768]{2,1,0:T(8,128)(2,1)S(1)}, u32[]{:S(2)}, u32[]{:S(2)}) collective-permute-start(bf16[2,128,768]{2,1,0:T(8,128)(2,1)} %pad_maximum_fusion), channel_id=1, source_target_pairs={{14,0},{3,1},{0,2},{5,3},{2,4},{7,5},{4,6},{9,7},{6,8},{11,9},{8,1... | collective-permute-start | bytes 1179656 | tf_op jit(solution)/shard_map/ppermute | solution.py:134
  7.7 19.6 %collective-permute-start.2 = (bf16[2,128,768]{2,1,0:T(8,128)(2,1)}, bf16[2,128,768]{2,1,0:T(8,128)(2,1)S(1)}, u32[]{:S(2)}, u32[]{:S(2)}) collective-permute-start(bf16[2,128,768]{2,1,0:T(8,128)(2,1)} %pad_maximum_fusion), channel_id=1, source_target_pairs={{13,0},{4,1},{15,2},{6,3},{1,4},{8,5},{3,6},{10,7},{5,8},{12,9},{7... | collective-permute-start | bytes 1179656 | tf_op jit(solution)/shard_map/ppermute | solution.py:135
  7.7 20.3 %collective-permute-start.3 = (bf16[2,128,768]{2,1,0:T(8,128)(2,1)}, bf16[2,128,768]{2,1,0:T(8,128)(2,1)S(1)}, u32[]{:S(2)}, u32[]{:S(2)}) collective-permute-start(bf16[2,128,768]{2,1,0:T(8,128)(2,1)} %pad_maximum_fusion), channel_id=1, source_target_pairs={{1,0},{0,1},{3,2},{2,3},{5,4},{4,5},{7,6},{6,7},{9,8},{8,9},{11,10... | collective-permute-start | bytes 1179656 | tf_op jit(solution)/shard_map/ppermute | solution.py:126
  22.6 6.2 %copy-start.6 = (bf16[2,128,768]{2,1,0:T(8,128)(2,1)}, bf16[2,128,768]{2,1,0:T(8,128)(2,1)S(1)}, u32[]{:S(2)}) copy-start(bf16[2,128,768]{2,1,0:T(8,128)(2,1)S(1)} %collective-permute-done.a_ref) | copy-start | bytes 1179652
  22.6 6.2 %collective-permute-start.4 = (bf16[2,128,768]{2,1,0:T(8,128)(2,1)S(1)}, bf16[2,128,768]{2,1,0:T(8,128)(2,1)}, u32[]{:S(2)}, u32[]{:S(2)}) collective-permute-start(bf16[2,128,768]{2,1,0:T(8,128)(2,1)S(1)} %collective-permute-done.a_ref), channel_id=1, source_target_pairs={{1,0},{0,1},{3,2},{2,3},{5,4},{4,5},{7,6},{6,7},{9,8},{8,9},{11,10... | collective-permute-start | bytes 1179656 | tf_op jit(solution)/shard_map/ppermute | solution.py:126
  23.8 5.0 %copy-start.8 = (bf16[2,128,768]{2,1,0:T(8,128)(2,1)}, bf16[2,128,768]{2,1,0:T(8,128)(2,1)S(1)}, u32[]{:S(2)}) copy-start(bf16[2,128,768]{2,1,0:T(8,128)(2,1)S(1)} %collective-permute-done.1.b_ref) | copy-start | bytes 1179652
  23.8 5.0 %collective-permute-start.5 = (bf16[2,128,768]{2,1,0:T(8,128)(2,1)S(1)}, bf16[2,128,768]{2,1,0:T(8,128)(2,1)}, u32[]{:S(2)}, u32[]{:S(2)}) collective-permute-start(bf16[2,128,768]{2,1,0:T(8,128)(2,1)S(1)} %collective-permute-done.1.b_ref), channel_id=1, source_target_pairs={{1,0},{0,1},{3,2},{2,3},{5,4},{4,5},{7,6},{6,7},{9,8},{8,9},{11,10... | collective-permute-start | bytes 1179656 | tf_op jit(solution)/shard_map/ppermute | solution.py:126
  23.8 20.7 %collective-permute-start.11 = (bf16[128,768]{1,0:T(8,128)(2,1)}, bf16[128,768]{1,0:T(8,128)(2,1)}, u32[]{:S(2)}, u32[]{:S(2)}) collective-permute-start(bf16[128,768]{1,0:T(8,128)(2,1)} %bitcast.39), channel_id=1, source_target_pairs={{0,16},{16,0},{1,17},{17,1},{2,18},{18,2},{3,19},{19,3},{4,20},{20... | collective-permute-start | bytes 589832 | tf_op jit(solution)/shard_map/ppermute | solution.py:140
  27.3 0.8 copy-start.10
  28.1 0.7 copy-start.12
  28.9 1.0 copy-start.7
  29.9 1.0 copy-start.9
  30.9 1.0 copy-start.11
  31.9 1.0 copy-start.13
  42.4 1.0 copy-start.3
  43.4 0.7 copy-start.4
  44.2 3.5 %collective-permute-start.10 = (bf16[128,384]{1,0:T(8,128)(2,1)S(1)}, bf16[128,384]{1,0:T(8,128)(2,1)S(1)}, u32[]{:S(2)}, u32[]{:S(2)}) collective-permute-start(bf16[128,384]{1,0:T(8,128)(2,1)S(1)} %get-tuple-element.24), channel_id=1, source_target_pairs={{0,16},{16,0},{1,17},{17,1},{2,18},{18,2},{3,19},{19,3},{4,20},{20... | collective-permute-start | bytes 294920 | tf_op jit(solution)/shard_map/ppermute | solution.py:201
  49.1 1.0 copy-start.16
  50.2 3.2 %collective-permute-start.12 = (bf16[192,768]{1,0:T(8,128)(2,1)S(1)}, bf16[192,768]{1,0:T(8,128)(2,1)S(1)}, u32[]{:S(2)}, u32[]{:S(2)}) collective-permute-start(bf16[192,768]{1,0:T(8,128)(2,1)S(1)} %dynamic-slice_convert_fusion), channel_id=1, source_target_pairs={{1,0},{0,1},{3,2},{2,3},{5,4},{4,5},{7,6},{6,7},{9,8},{8,9},{11,10... | collective-permute-start | bytes 884744 | tf_op jit(solution)/shard_map/ppermute | solution.py:126
  54.5 0.8 copy-start.17
  55.4 22.2 %copy-start.5 = (bf16[2,128,768]{2,1,0:T(8,128)(2,1)S(1)}, bf16[2,128,768]{2,1,0:T(8,128)(2,1)}, u32[]{:S(2)}) copy-start(bf16[2,128,768]{2,1,0:T(8,128)(2,1)} %copy-done.4) | copy-start | bytes 1179652
  56.0 5.3 %collective-permute-start.13 = (bf16[96,768]{1,0:T(8,128)(2,1)}, bf16[96,768]{1,0:T(8,128)(2,1)S(1)}, u32[]{:S(2)}, u32[]{:S(2)}) collective-permute-start(bf16[96,768]{1,0:T(8,128)(2,1)} %dynamic-slice_convert_fusion.1), channel_id=1, source_target_pairs={{2,0},{3,1},{0,2},{1,3},{6,4},{7,5},{4,6},{5,7},{10,8},{11,9},{8,1... | collective-permute-start | bytes 442376 | tf_op jit(solution)/shard_map/ppermute | solution.py:126
  57.4 30.2 %collective-permute-start.6 = (bf16[3,2,128,768]{3,2,1,0:T(8,128)(2,1)}, bf16[3,2,128,768]{3,2,1,0:T(8,128)(2,1)}, u32[]{:S(2)}, u32[]{:S(2)}) collective-permute-start(bf16[3,2,128,768]{3,2,1,0:T(8,128)(2,1)} %copy-done.3), channel_id=1, source_target_pairs={{1,0},{0,1},{3,2},{2,3},{5,4},{4,5},{7,6},{6,7},{9,8},{8,9},{11,10... | collective-permute-start | bytes 3538952 | tf_op jit(solution)/shard_map/ppermute | solution.py:126
  62.3 0.7 copy-start.18
  63.0 3.3 %collective-permute-start.14 = (bf16[48,768]{1,0:T(8,128)(2,1)S(1)}, bf16[48,768]{1,0:T(8,128)(2,1)S(1)}, u32[]{:S(2)}, u32[]{:S(2)}) collective-permute-start(bf16[48,768]{1,0:T(8,128)(2,1)S(1)} %dynamic-slice_convert_fusion.2), channel_id=1, source_target_pairs={{4,0},{5,1},{6,2},{7,3},{0,4},{1,5},{2,6},{3,7},{12,8},{13,9},{14,... | collective-permute-start | bytes 221192 | tf_op jit(solution)/shard_map/ppermute | solution.py:126
  67.2 4.2 %collective-permute-start.15 = (bf16[48,768]{1,0:T(8,128)(2,1)S(1)}, bf16[48,768]{1,0:T(8,128)(2,1)S(1)}, u32[]{:S(2)}, u32[]{:S(2)}) collective-permute-start(bf16[48,768]{1,0:T(8,128)(2,1)S(1)} %add_convert_fusion.1), channel_id=1, source_target_pairs={{8,0},{9,1},{10,2},{11,3},{12,4},{13,5},{14,6},{15,7},{0,8},{1,9},... | collective-permute-start | bytes 221192 | tf_op jit(solution)/shard_map/ppermute | solution.py:126
  71.4 1.6 %copy-start.19 = (bf16[48,768]{1,0:T(8,128)(2,1)}, bf16[48,768]{1,0:T(8,128)(2,1)S(1)}, u32[]{:S(2)}) copy-start(bf16[48,768]{1,0:T(8,128)(2,1)S(1)} %add_convert_fusion) | copy-start | bytes 221188
  71.4 3.7 %collective-permute-start.16 = (bf16[48,768]{1,0:T(8,128)(2,1)S(1)}, bf16[48,768]{1,0:T(8,128)(2,1)}, u32[]{:S(2)}, u32[]{:S(2)}) collective-permute-start(bf16[48,768]{1,0:T(8,128)(2,1)S(1)} %add_convert_fusion), channel_id=1, source_target_pairs={{4,0},{5,1},{6,2},{7,3},{0,4},{1,5},{2,6},{3,7},{12,8},{13,9},{14,... | collective-permute-start | bytes 221192 | tf_op jit(solution)/shard_map/ppermute | solution.py:126
  76.1 7.2 %collective-permute-start.17 = (bf16[96,768]{1,0:T(8,128)(2,1)S(1)}, bf16[96,768]{1,0:T(8,128)(2,1)}, u32[]{:S(2)}, u32[]{:S(2)}) collective-permute-start(bf16[96,768]{1,0:T(8,128)(2,1)S(1)} %maximum_select_fusion.2), channel_id=1, source_target_pairs={{2,0},{3,1},{0,2},{1,3},{6,4},{7,5},{4,6},{5,7},{10,8},{11,9},{8,1... | collective-permute-start | bytes 442376 | tf_op jit(solution)/shard_map/ppermute | solution.py:126
  77.6 17.3 %collective-permute-start.7 = (bf16[2,128,768]{2,1,0:T(8,128)(2,1)S(1)}, bf16[2,128,768]{2,1,0:T(8,128)(2,1)}, u32[]{:S(2)}, u32[]{:S(2)}) collective-permute-start(bf16[2,128,768]{2,1,0:T(8,128)(2,1)S(1)} %copy-done.5), channel_id=1, source_target_pairs={{0,13},{1,4},{2,15},{3,6},{4,1},{5,8},{6,3},{7,10},{8,5},{9,12},{1... | collective-permute-start | bytes 1179656 | tf_op jit(solution)/shard_map/ppermute | solution.py:186
  85.1 7.3 %collective-permute-start.18 = (bf16[192,768]{1,0:T(8,128)(2,1)}, bf16[192,768]{1,0:T(8,128)(2,1)}, u32[]{:S(2)}, u32[]{:S(2)}) collective-permute-start(bf16[192,768]{1,0:T(8,128)(2,1)} %maximum_select_fusion.1), channel_id=1, source_target_pairs={{1,0},{0,1},{3,2},{2,3},{5,4},{4,5},{7,6},{6,7},{9,8},{8,9},{11,10... | collective-permute-start | bytes 884744 | tf_op jit(solution)/shard_map/ppermute | solution.py:126
  89.8 14.8 %collective-permute-start.9 = (bf16[2,128,768]{2,1,0:T(8,128)(2,1)}, bf16[2,128,768]{2,1,0:T(8,128)(2,1)S(1)}, u32[]{:S(2)}, u32[]{:S(2)}) collective-permute-start(bf16[2,128,768]{2,1,0:T(8,128)(2,1)} %get-tuple-element.20), channel_id=1, source_target_pairs={{0,14},{1,3},{2,0},{3,5},{4,2},{5,7},{6,4},{7,9},{8,6},{9,11},{10,... | collective-permute-start | bytes 1179656 | tf_op jit(solution)/shard_map/ppermute | solution.py:191
  91.1 18.7 %collective-permute-start.8 = (bf16[2,128,768]{2,1,0:T(8,128)(2,1)}, bf16[2,128,768]{2,1,0:T(8,128)(2,1)}, u32[]{:S(2)}, u32[]{:S(2)}) collective-permute-start(bf16[2,128,768]{2,1,0:T(8,128)(2,1)} %get-tuple-element.19), channel_id=1, source_target_pairs={{0,15},{1,2},{2,1},{3,4},{4,3},{5,6},{6,5},{7,8},{8,7},{9,10},{10,... | collective-permute-start | bytes 1179656 | tf_op jit(solution)/shard_map/ppermute | solution.py:190

commit v2 on v1

v2 whole, which is shorter than its diff:
```python
import functools
import math

import jax
import jax.numpy as jnp
from jax import lax
from jax.experimental import pallas as pl
from jax.experimental.pallas import tpu as pltpu
from jax.sharding import PartitionSpec as P

HEADS = 12
PMAX = 6
GROUP = 4
SLOTS = PMAX + 1
MIB = 1024 * 1024

neg_big = -1e30
bf16, f32 = jnp.bfloat16, jnp.float32
SMEM = pl.BlockSpec(memory_space=pltpu.SMEM)
VMEM = pl.BlockSpec(memory_space=pltpu.VMEM)
ANY = pl.BlockSpec(memory_space=pl.ANY)
NN = (((1,), (0,)), ((), ()))
NT = (((1,), (1,)), ((), ()))
TN = (((0,), (0,)), ((), ()))


def dot(x, y, dims):
    return lax.dot_general(x, y, dims, preferred_element_type=f32)


def shape_of(*dims, dtype=bf16):
    return jax.ShapeDtypeStruct(dims, dtype)


def call(kernel, ins, outs, args, scratch=(), limit=8, flops=1000, name=None):
    moved = sum(x.size * x.dtype.itemsize for x in outs)
    return pl.pallas_call(
        kernel,
        in_specs=ins,
        out_specs=[VMEM] * len(outs),
        out_shape=outs,
        scratch_shapes=list(scratch),
        compiler_params=pltpu.CompilerParams(vmem_limit_bytes=limit * MIB),
        cost_estimate=pl.CostEstimate(flops=flops, bytes_accessed=2 * moved, transcendentals=0),
        name=name,
    )(*args)


def fetch(pairs, sems):
    copies = [pltpu.make_async_copy(a, b, sems.at[n]) for n, (a, b) in enumerate(pairs)]
    for copy in copies:
        copy.start()
    return copies


def pack_kernel(k_ref, v_ref, out_ref, sems):
    for copy in fetch([(k_ref, out_ref.at[0]), (v_ref, out_ref.at[1])], sems):
        copy.wait()


def widen(x, wide_ref, head_of):
    span = x.shape[0]
    zero = jnp.zeros_like(x)
    for h in range(GROUP):
        wide_ref[h * span : (h + 1) * span] = jnp.where(head_of == h, x, zero)


def pick(wide, span, head_width):
    blocks = [
        wide[h * head_width : (h + 1) * head_width, h * span : (h + 1) * span] for h in range(GROUP)
    ]
    return jnp.concatenate(blocks, 0)


def forward_kernel(
    at_ref, ids_ref, count_ref, q_ref, own_ref, near_ref, middle_ref, far_ref, sib_ref, sib_near_ref,
    sib_middle_ref, g_win_ref, g_sib_ref, g_both_ref,
    mixed_ref, mine_ref, to_win_ref, to_sib_ref, to_both_ref, probs_ref, keys, values,
    q_all, q_wide, raw, sems,
    *, station_count,
):
    span, width = q_all.shape
    head_width = width // HEADS
    lanes = GROUP * head_width
    parts = (own_ref, near_ref, middle_ref, far_ref, sib_ref, sib_near_ref, sib_middle_ref)
    pairs = [(q_ref, q_all)]
    for j, ref in enumerate(parts):
        pairs.append((ref.at[0], keys.at[j * span : (j + 1) * span]))
    for j, ref in enumerate(parts):
        pairs.append((ref.at[1], values.at[j * span : (j + 1) * span]))
    copies = fetch(pairs, sems)
    me = at_ref[0]
    side = 2 * lax.rem(me, 2) - 1
    live = [None]
    for offset in (side, 2 * side, 3 * side, -side, -2 * side, -3 * side):
        station = lax.rem(me + offset + station_count, station_count)
        hit = jnp.int32(0)
        for j in range(PMAX):
            here = jnp.logical_and(ids_ref[me, j] == station, j < count_ref[me])
            hit = jnp.maximum(hit, here.astype(jnp.int32))
        live.append(hit)
    head_of = lax.broadcasted_iota(jnp.int32, (span, lanes), 1) // head_width
    copies[0].wait()
    for group in range(HEADS // GROUP):
        cols = slice(group * lanes, (group + 1) * lanes)
        widen(q_all[:, cols] * bf16(1.0 / math.sqrt(head_width)), q_wide, head_of)
        top = None
        for j in range(SLOTS):
            rows = slice(j * span, (j + 1) * span)
            if group == 0:
                copies[1 + j].wait()
            scores = dot(keys[rows, cols], q_wide[...], NT)
            if j:
                scores = jnp.where(live[j] > 0, scores, neg_big)
            raw[rows] = scores
            here = jnp.max(scores, 0, keepdims=True)
            top = here if top is None else jnp.maximum(top, here)
        total = jnp.zeros_like(top)
        for j in range(SLOTS):
            rows = slice(j * span, (j + 1) * span)
            weight = jnp.exp(raw[rows] - top)
            raw[rows] = weight
            total = total + jnp.sum(weight, 0, keepdims=True)
        inverse = 1.0 / total
        for j in range(SLOTS):
            rows = slice(j * span, (j + 1) * span)
            probs_ref[group, rows] = (raw[rows] * inverse).astype(bf16)
            if group == 0:
                copies[1 + SLOTS + j].wait()
        wide = dot(values[:, cols], probs_ref[group], TN)
        mixed_ref[cols] = pick(wide, span, head_width).astype(bf16)
    quarter = mine_ref.shape[0]
    core, window = lax.rem(me, 2), at_ref[1]
    for ref, w, c in (
        (mine_ref, window, core),
        (to_win_ref, 1 - window, core),
        (to_sib_ref, window, 1 - core),
        (to_both_ref, 1 - window, 1 - core),
    ):
        start = pl.multiple_of(lax.rem(2 * w + c, width // quarter) * quarter, quarter)
        ref[...] = mixed_ref[pl.ds(start, quarter)]


def backward_kernel(
    q_ref, g_ref, keys, values, probs_ref,
    dq_ref, own_ref, near_ref, middle_ref, far_ref, sib_ref,
    q_all, g_all, q_wide, g_wide, grads, grads_half, sems,
):
    span, width = q_all.shape
    head_width = width // HEADS
    lanes = GROUP * head_width
    scale = 1.0 / math.sqrt(head_width)
    for copy in fetch([(q_ref, q_all), (g_ref, g_all)], sems):
        copy.wait()
    head_of = lax.broadcasted_iota(jnp.int32, (span, lanes), 1) // head_width
    for group in range(HEADS // GROUP):
        cols = slice(group * lanes, (group + 1) * lanes)
        widen(q_all[:, cols] * bf16(scale), q_wide, head_of)
        widen(g_all[:, cols], g_wide, head_of)
        delta = None
        for j in range(SLOTS):
            rows = slice(j * span, (j + 1) * span)
            back = dot(values[rows, cols], g_wide[...], NT)
            grads[rows] = back
            here = jnp.sum(back * probs_ref[group, rows].astype(f32), 0, keepdims=True)
            delta = here if delta is None else delta + here
        for j in range(SLOTS):
            rows = slice(j * span, (j + 1) * span)
            grad = probs_ref[group, rows].astype(f32) * (grads[rows] - delta)
            grads_half[rows] = grad.astype(bf16)
        wide = dot(keys[:, cols], grads_half[...], TN)
        dq_ref[:, cols] = (pick(wide, span, head_width).T * scale).astype(bf16)
        for part, left, right in ((0, grads_half, q_wide), (1, probs_ref.at[group], g_wide)):
            for j in range(SLOTS):
                rows = slice(j * span, (j + 1) * span)
                piece = dot(left[rows], right[...], NN)
                if j == 0:
                    own_ref[part, :, cols] = piece
                elif j <= 3:
                    (near_ref, middle_ref, far_ref)[j - 1][part, :, cols] = piece.astype(bf16)
                else:
                    sib_ref[j - 4, part, :, cols] = piece.astype(bf16)


def sums_kernel(own_ref, near_ref, middle_ref, got_ref, own_out, near_out, middle_out, got, sems):
    copies = fetch([(got_ref.at[j], got.at[j]) for j in range(3)], sems)
    copies[1].wait()
    near_out[...] = (near_ref[...].astype(f32) + got[1].astype(f32)).astype(bf16)
    copies[2].wait()
    middle_out[...] = (middle_ref[...].astype(f32) + got[2].astype(f32)).astype(bf16)
    copies[0].wait()
    own_out[...] = own_ref[...] + got[0].astype(f32)


def home_kernel(own_ref, near_ref, middle_ref, far_ref, dk_ref, dv_ref, got, sems):
    refs = (near_ref, middle_ref, far_ref)
    copies = fetch([(ref, got.at[j]) for j, ref in enumerate(refs)], sems)
    for copy in copies:
        copy.wait()
    for part, out in ((0, dk_ref), (1, dv_ref)):
        total = own_ref[part]
        for j in range(3):
            total = total + got[j, part].astype(f32)
        out[...] = total.astype(bf16)


def weight_kernel(
    stride, at_ref, mine_ref, win_ref, sib_ref, both_ref, g_ref, g_win_ref, g_sib_ref, g_both_ref,
    after_ref, send_ref, keep_ref, left, right, sems,
):
    span = mine_ref.shape[1]
    half = send_ref.shape[0]
    pairs = []
    for j, (a, b) in enumerate(
        ((mine_ref, g_ref), (win_ref, g_win_ref), (sib_ref, g_sib_ref), (both_ref, g_both_ref))
    ):
        pairs.append((a, left.at[:, j * span : (j + 1) * span]))
        pairs.append((b, right.at[j * span : (j + 1) * span]))
    for copy in fetch(pairs, sems):
        copy.wait()
    bit = lax.rem(at_ref[0] // stride, 2)
    send = pl.ds(pl.multiple_of((1 - bit) * half, half), half)
    keep = pl.ds(pl.multiple_of(bit * half, half), half)
    send_ref[...] = dot(left[send], right[...], NN).astype(bf16)
    keep_ref[...] = dot(left[keep], right[...], NN)


def split_kernel(stride, at_ref, part_ref, got_ref, after_ref, send_ref, keep_ref, got, sems):
    half = send_ref.shape[0]
    for copy in fetch([(got_ref, got)], sems):
        copy.wait()
    bit = lax.rem(at_ref[0] // stride, 2)
    send = pl.ds(pl.multiple_of((1 - bit) * half, half), half)
    keep = pl.ds(pl.multiple_of(bit * half, half), half)
    send_ref[...] = (part_ref[send] + got[send].astype(f32)).astype(bf16)
    keep_ref[...] = part_ref[keep] + got[keep].astype(f32)


def round_kernel(part_ref, got_ref, after_ref, out_ref, got, sems):
    for copy in fetch([(got_ref, got)], sems):
        copy.wait()
    out_ref[...] = (part_ref[...].astype(f32) + got[...].astype(f32)).astype(bf16)


def join_kernel(stride, scale, at_ref, mine_ref, got_ref, after_a, after_b, after_c, out_ref, got, sems):
    half = mine_ref.shape[0]
    copies = fetch([(got_ref, got)], sems)
    bit = lax.rem(at_ref[0] // stride, 2)

    def put(place, value):
        if scale is not None:
            value = value.astype(f32) * scale
        out_ref[pl.ds(pl.multiple_of(place * half, half), half)] = value

    put(bit, mine_ref[...])
    copies[0].wait()
    put(1 - bit, got[...])


def local(
    query_states, key_states, value_states, grad_output, out_weight, partner_ids, partner_count
):
    span, width = query_states.shape[2:]
    stations = lax.axis_size("station")
    windows = lax.axis_size("dp")
    me = lax.axis_index("station").astype(jnp.int32)
    window = lax.axis_index("dp").astype(jnp.int32)
    at = jnp.stack([me, window])
    side = [1 if s % 2 else -1 for s in range(stations)]

    def routes(steps):
        return [((s + steps * side[s]) % stations, s) for s in range(stations)]

    def back(pairs):
        return [(d, s) for s, d in pairs]

    def swap(value, stride):
        return lax.ppermute(value, "station", [(s ^ stride, s) for s in range(stations)])

    def other_window(value):
        return lax.ppermute(value, "dp", [(0, 1), (1, 0)])

    def other_both(value):
        count = 2 * stations
        pairs = [(s, (s + stations) % count ^ 1) for s in range(count)]
        return lax.ppermute(value, ("dp", "station"), pairs)

    def flat(x):
        return x.reshape(span, width)

    q, k, v, g = flat(query_states), flat(key_states), flat(value_states), flat(grad_output)
    dma = pltpu.SemaphoreType.DMA
    (own,) = call(
        pack_kernel, [ANY, ANY], [shape_of(2, span, width)], (k, v), [dma((2,))], name="pack"
    )
    near = lax.ppermute(own, "station", routes(1))
    middle = lax.ppermute(own, "station", routes(2))
    far = lax.ppermute(own, "station", routes(3))
    sib = swap(own, 1)
    sib_near = swap(near, 1)
    sib_middle = swap(middle, 1)
    grad_mixed = dot(g, out_weight, NT).astype(bf16)

    if windows == 2:
        g_late, near = lax.optimization_barrier((g, near))
        peers = (other_window(g_late), swap(g_late, 1), other_both(g_late))
    else:
        peers = (g, g, g)

    lanes = width // HEADS * GROUP
    groups = HEADS // GROUP
    quarter = width // 4
    attend_flops = 2 * SLOTS * span * span * width * 8
    small = shape_of(quarter, span)
    mixed, mine, to_win, to_sib, to_both, probs, keys, values = call(
        functools.partial(forward_kernel, station_count=stations),
        [SMEM] * 3 + [ANY] * 11,
        [
            shape_of(width, span), small, small, small, small,
            shape_of(groups, SLOTS * span, GROUP * span),
            shape_of(SLOTS * span, width),
            shape_of(SLOTS * span, width),
        ],
        (at, partner_ids, partner_count, q, own, near, middle, far, sib, sib_near, sib_middle)
        + peers,
        [
            pltpu.VMEM((span, width), bf16),
            pltpu.VMEM((GROUP * span, lanes), bf16),
            pltpu.VMEM((SLOTS * span, GROUP * span), f32),
            dma((1 + 2 * SLOTS,)),
        ],
        limit=24, flops=attend_flops, name="forward",
    )
    pair = shape_of(2, span, width)
    grad_query, own_grad, near_grad, middle_grad, far_grad, sib_grad = call(
        backward_kernel,
        [ANY, ANY, VMEM, VMEM, VMEM],
        [
            shape_of(span, width), shape_of(2, span, width, dtype=f32), pair, pair, pair,
            shape_of(3, 2, span, width),
        ],
        (q, grad_mixed, keys, values, probs),
        [
            pltpu.VMEM((span, width), bf16),
            pltpu.VMEM((span, width), bf16),
            pltpu.VMEM((GROUP * span, lanes), bf16),
            pltpu.VMEM((GROUP * span, lanes), bf16),
            pltpu.VMEM((SLOTS * span, GROUP * span), f32),
            pltpu.VMEM((SLOTS * span, GROUP * span), bf16),
            dma((2,)),
        ],
        limit=24, flops=2 * attend_flops, name="backward",
    )

    if windows == 2:
        quarters = (other_window(to_win), swap(to_sib, 1), other_both(to_both))
        far_grad, sib_grad, own_grad, *quarters = lax.optimization_barrier(
            (far_grad, sib_grad, own_grad, *quarters)
        )

    far_home = lax.ppermute(far_grad, "station", back(routes(3)))
    from_sib = swap(sib_grad, 1)
    own_sum, near_sum, middle_sum = call(
        sums_kernel,
        [VMEM, VMEM, VMEM, ANY],
        [shape_of(2, span, width, dtype=f32), pair, pair],
        (own_grad, near_grad, middle_grad, from_sib),
        [pltpu.VMEM((3, 2, span, width), bf16), dma((3,))],
        name="sums",
    )
    near_home = lax.ppermute(near_sum, "station", back(routes(1)))
    middle_home = lax.ppermute(middle_sum, "station", back(routes(2)))

    if windows == 2:
        stride, rows = 2, quarter // 2
        send, part = call(
            functools.partial(weight_kernel, stride),
            [SMEM] + [ANY] * 9,
            [shape_of(rows, width), shape_of(rows, width, dtype=f32)],
            (
                at, mine, *quarters,
                g, *peers, own_grad,
            ),
            [pltpu.VMEM((quarter, 4 * span), bf16), pltpu.VMEM((4 * span, width), bf16), dma((8,))],
            flops=2 * quarter * 4 * span * width, name="weight",
        )
    else:
        stride = 1
        whole = lax.dot_general(mixed, g, NN, preferred_element_type=f32).astype(bf16)
        whole = lax.psum_scatter(whole, "dp", scatter_dimension=0, tiled=True).astype(f32)
        rows = whole.shape[0] // 2
        bit = me % 2
        part = lax.dynamic_slice_in_dim(whole, bit * rows, rows, 0)
        send = lax.dynamic_slice_in_dim(whole, (1 - bit) * rows, rows, 0).astype(bf16)
    first = stride
    got = swap(send, stride)
    halved = [stride]
    stride *= 2
    after = near_sum
    while rows >= 96 and stride < stations:
        rows //= 2
        send, part = call(
            functools.partial(split_kernel, stride),
            [SMEM, VMEM, ANY, ANY],
            [shape_of(rows, width), shape_of(rows, width, dtype=f32)],
            (at, part, got, after),
            [pltpu.VMEM((2 * rows, width), bf16), dma((1,))],
            name="split",
        )
        got = swap(send, stride)
        halved.append(stride)
        stride *= 2

    def add_round(part, got):
        (total,) = call(
            round_kernel,
            [VMEM, ANY, ANY],
            [shape_of(rows, width)],
            (part, got, after),
            [pltpu.VMEM((rows, width), bf16), dma((1,))],
            name="add",
        )
        return total

    total = add_round(part, got)
    while stride < stations:
        total = add_round(total, swap(total, stride))
        stride *= 2
    if first == 2:
        halved.insert(0, 1)
    scale = 1.0 / math.sqrt(span * windows * stations)
    for stride in reversed(halved):
        last = stride == 1
        got = swap(total, stride)
        half = total.shape[0]
        (total,) = call(
            functools.partial(join_kernel, stride, scale if last else None),
            [SMEM, VMEM, ANY, ANY, ANY, ANY],
            [shape_of(2 * half, width, dtype=f32 if last else bf16)],
            (at, total, got, *((near_home, middle_home, far_home) if stride == 2 else (after,) * 3)),
            [pltpu.VMEM((half, width), bf16), dma((1,))],
            name="join",
        )

    layer_output = lax.dot_general(mixed, out_weight, TN, preferred_element_type=f32).astype(bf16)
    grad_key, grad_value = call(
        home_kernel,
        [VMEM, ANY, ANY, ANY],
        [shape_of(span, width)] * 2,
        (own_sum, near_home, middle_home, far_home),
        [pltpu.VMEM((3, 2, span, width), bf16), dma((3,))],
        name="home",
    )
    shape = query_states.shape
    return (
        layer_output.reshape(shape),
        grad_query.reshape(shape),
        grad_key.reshape(shape),
        grad_value.reshape(shape),
        total,
    )


def solution(mesh):
    split = P("dp", "station", None, None)
    return jax.shard_map(
        local,
        mesh=mesh,
        in_specs=(split, split, split, split, P(), P(), P()),
        out_specs=(split, split, split, split, P("dp", None)),
        check_vma=False,
    )
```

time: 113 us -> 104 us (0.920)
  Pallas kernels: 9.55 us -> 25.1 us
  other arithmetic: 13.8 us -> 0.07 us
  starting transfers between devices: 29.6 us -> 42.6 us
  waiting for transfers between devices: 42.3 us -> 29.7 us
  local copies, waits for them, and re-layouts: 12.1 us -> 2.72 us
  matrix products: 3.85 us -> 2.52 us
    pallas_call x1 -> x12, Pallas kernels: 9.55 us -> 25.1 us  [call(): pl.pallas_call(kernel, in_specs=ins, out_specs=[VMEM] * len(outs), out_sh...]
    ppermute x11 -> x12, starting transfers between devices: 15.5 us -> 28.8 us  [swap(): lax.ppermute(value, 'station', [(s ^ stride, s) for s in range(stations)])]
    ppermute x1, waiting for transfers between devices: 12.5 us -> 0.01 us  [local(): near = lax.ppermute(own, 'station', routes(1))]
    ppermute x1, waiting for transfers between devices: 9.76 us -> 0.01 us  [local(): middle_home = lax.ppermute(middle_sum, 'station', back(routes(2)))]
    ppermute x1, waiting for transfers between devices: 1.19 us -> 9.55 us  [local(): middle = lax.ppermute(own, 'station', routes(2))]
    unnamed x41 -> x13, local copies, waits for them, and re-layouts: 10.6 us -> 2.72 us
    ppermute x1, waiting for transfers between devices: 5.22 us -> 0.01 us  [local(): near_home = lax.ppermute(near_sum, 'station', back(routes(1)))]
    ppermute x2 -> x4, waiting for transfers between devices: 3.23 us -> 8.12 us  [the longest x2 4.14 us: other_window(): return lax.ppermute(value, 'dp', [(0, 1), (1, 0)])]
  transfers between devices with their start and end apart: 19 -> 22, of which waited for: 10 -> 7; matrix products, arithmetic and copies ran while one was open for 11% -> 3% of each run, Pallas kernels for 9% -> 12%
where the time goes in v2:
time: 104 us
  starting transfers between devices  42.6 us (41%)
  waiting for transfers between devices  29.7 us (29%)
  Pallas kernels  25.1 us (24%)
  local copies, waits for them, and re-layouts  2.72 us (3%)
  matrix products  2.52 us (2%)
    ppermute x12, starting transfers between devices, swap(): lax.ppermute(value, 'station', [(s ^ stride, s) for s in range(stations)])  28.8 us
    pallas_call x12, Pallas kernels, call(): pl.pallas_call(kernel, in_specs=ins, out_specs=[VMEM] * len(outs), out_sh...  25.1 us
    ppermute x12, waiting for transfers between devices, swap(): lax.ppermute(value, 'station', [(s ^ stride, s) for s in range(stations)])  12.1 us
    ppermute x1, waiting for transfers between devices, local(): middle = lax.ppermute(own, 'station', routes(2))  9.55 us
    ppermute x1, starting transfers between devices, local(): middle = lax.ppermute(own, 'station', routes(2))  5.13 us
    ppermute x2, waiting for transfers between devices, other_window(): return lax.ppermute(value, 'dp', [(0, 1), (1, 0)])  4.14 us
    ppermute x2, waiting for transfers between devices, other_both(): return lax.ppermute(value, ('dp', 'station'), pairs)  3.98 us
    ppermute x1, starting transfers between devices, local(): near_home = lax.ppermute(near_sum, 'station', back(routes(1)))  3.69 us
  transfers between devices with their start and end apart: 22, of which 7 were waited for; matrix products, arithmetic and copies ran while one was open for 3% of the time, Pallas kernels for 12%

profile of v2, /device:TPU:1, one launch (start us, length us, event | category | flops | bytes accessed | tf_op | source)
XLA Modules:
  0.0 103.6 jit_solution(3854032579694645425)
XLA Ops:
  0.6 0.0 copy-start
  0.7 1.0 copy-done.2
  1.7 0.9 copy-done.3
  2.6 0.5 pack.1.own_ref
  3.1 5.1 %collective-permute-start.1 = (bf16[2,128,768]{2,1,0:T(8,128)(2,1)S(1)}, bf16[2,128,768]{2,1,0:T(8,128)(2,1)S(1)}, u32[]{:S(2)}, u32[]{:S(2)}) collective-permute-start(bf16[2,128,768]{2,1,0:T(8,128)(2,1)S(1)} %pack.1.own_ref), channel_id=1, source_target_pairs={{14,0},{3,1},{0,2},{5,3},{2,4},{7,5},{4,6},{9,7},{6,8},{11,9},{8,1... | collective-permute-start | bytes 1179656 | tf_op jit(solution)/shard_map/ppermute | solution.py:297
  8.2 0.6 collective-permute-start.3
  8.9 0.1 collective-permute-start.2
  9.0 9.5 %collective-permute-done.1.middle_ref = bf16[2,128,768]{2,1,0:T(8,128)(2,1)S(1)} collective-permute-done((bf16[2,128,768]{2,1,0:T(8,128)(2,1)S(1)}, bf16[2,128,768]{2,1,0:T(8,128)(2,1)S(1)}, u32[]{:S(2)}, u32[]{:S(2)}) %collective-permute-start.1) | collective-permute-done | bytes 393248 | tf_op jit(solution)/shard_map/ppermute | solution.py:297
  18.6 5.2 %collective-permute-start.5 = (bf16[2,128,768]{2,1,0:T(8,128)(2,1)S(1)}, bf16[2,128,768]{2,1,0:T(8,128)(2,1)S(1)}, u32[]{:S(2)}, u32[]{:S(2)}) collective-permute-start(bf16[2,128,768]{2,1,0:T(8,128)(2,1)S(1)} %collective-permute-done.1.middle_ref), channel_id=1, source_target_pairs={{1,0},{0,1},{3,2},{2,3},{5,4},{4,5},{7,6},{6,7},{9,8},{8,9},{11,10... | collective-permute-start | bytes 1179656 | tf_op jit(solution)/shard_map/ppermute | solution.py:278
  23.8 0.0 collective-permute-done.near_ref
  23.8 0.0 collective-permute-start.4
  23.8 0.8 copy.12.ids_ref
  24.5 0.1 pad_add_fusion.at_ref
  24.6 1.6 %collective-permute-start.8 = (bf16[128,768]{1,0:T(8,128)(2,1)}, bf16[128,768]{1,0:T(8,128)(2,1)S(1)}, u32[]{:S(2)}, u32[]{:S(2)}) collective-permute-start(bf16[128,768]{1,0:T(8,128)(2,1)} %bitcast.16), channel_id=1, source_target_pairs={{0,17},{1,16},{2,19},{3,18},{4,21},{5,20},{6,23},{7,22},{8,25},{9,... | collective-permute-start | bytes 589832 | tf_op jit(solution)/shard_map/ppermute | solution.py:286
  26.2 0.0 collective-permute-start.7
  26.3 0.3 collective-permute-start.6
  26.5 1.5 %convolution_convert_fusion.g_ref = bf16[128,768]{1,0:T(8,128)(2,1)S(1)} fusion(bf16[768,768]{1,0:T(8,128)(2,1)S(1)} %copy-done, bf16[1,1,128,768]{3,2,1,0:T(8,128)(2,1)} %param.10), kind=kOutput, calls=%fused_computation | convolution fusion | flops 151093248 | bytes 1572864 | tf_op jit(solution)/shard_map/dot_general | solution.py:28
  28.0 4.0 %collective-permute-done.8.g_both_ref = bf16[128,768]{1,0:T(8,128)(2,1)S(1)} collective-permute-done((bf16[128,768]{1,0:T(8,128)(2,1)}, bf16[128,768]{1,0:T(8,128)(2,1)S(1)}, u32[]{:S(2)}, u32[]{:S(2)}) %collective-permute-start.8) | collective-permute-done | bytes 196640 | tf_op jit(solution)/shard_map/ppermute | solution.py:286
  32.0 4.1 %collective-permute-done.6.g_win_ref = bf16[128,768]{1,0:T(8,128)(2,1)S(1)} collective-permute-done((bf16[128,768]{1,0:T(8,128)(2,1)}, bf16[128,768]{1,0:T(8,128)(2,1)S(1)}, u32[]{:S(2)}, u32[]{:S(2)}) %collective-permute-start.6) | collective-permute-done | bytes 196640 | tf_op jit(solution)/shard_map/ppermute | solution.py:281
  36.2 9.8 %forward.1 = (bf16[768,128]{1,0:T(8,128)(2,1)S(1)}, bf16[192,128]{1,0:T(8,128)(2,1)S(1)}, bf16[192,128]{1,0:T(8,128)(2,1)S(1)}, bf16[192,128]{1,0:T(8,128)(2,1)S...) custom-call(s32[2]{0:T(128)S(1)} %pad_add_fusion.at_ref, ...), custom_call_target="tpu_custom_call" | custom-call | flops 1409286144 | bytes 11796480 | tf_op jit(solution)/shard_map/forward/pallas_call | solution.py:37
  46.0 1.3 %collective-permute-start.9 = (bf16[192,128]{1,0:T(8,128)(2,1)S(1)}, bf16[192,128]{1,0:T(8,128)(2,1)S(1)}, u32[]{:S(2)}, u32[]{:S(2)}) collective-permute-start(bf16[192,128]{1,0:T(8,128)(2,1)S(1)} %get-tuple-element.46), channel_id=1, source_target_pairs={{0,16},{16,0},{1,17},{17,1},{2,18},{18,2},{3,19},{19,3},{4,20},{20... | collective-permute-start | bytes 147464 | tf_op jit(solution)/shard_map/ppermute | solution.py:281
  47.3 0.9 collective-permute-start.10
  48.2 0.1 collective-permute-start.11
  48.3 6.3 %backward.1 = (bf16[128,768]{1,0:T(8,128)(2,1)}, f32[2,128,768]{2,1,0:T(8,128)S(1)}, bf16[2,128,768]{2,1,0:T(8,128)(2,1)S(1)}, bf16[2,128,768]{2,1,0:T(8,128)(2,...) custom-call(bf16[128,768]{1,0:T(8,128)(2,1)S(1)} %bitcast.23, ...), custom_call_target="tpu_custom_call" | custom-call | flops 2818572288 | bytes 6684672 | tf_op jit(solution)/shard_map/backward/pallas_call | solution.py:37
  54.6 0.6 collective-permute-start.12
  55.2 2.1 %weight.1 = (bf16[96,768]{1,0:T(8,128)(2,1)S(1)}, f32[96,768]{1,0:T(8,128)S(1)}) custom-call(s32[2]{0:T(128)S(1)} %pad_add_fusion.at_ref, bf16[192,128]{1,0:T(8,128)(2,1)S(1)} %get-tuple-element.59.mine_ref, bf16[192,128]{1,0:T(8,128)(2,1)S(1)} %collective-permute-done.9.win_ref, bf16[192,128]{1,0:T(8,128)(2,1)S(1)} %collective-permute-done.10.sib_ref, ...), custom_call_target="tpu_custom_call" | custom-call | flops 150994944 | bytes 884736 | tf_op jit(solution)/shard_map/weight/pallas_call | solution.py:37
  57.3 2.3 %collective-permute-start.16 = (bf16[96,768]{1,0:T(8,128)(2,1)S(1)}, bf16[96,768]{1,0:T(8,128)(2,1)S(1)}, u32[]{:S(2)}, u32[]{:S(2)}) collective-permute-start(bf16[96,768]{1,0:T(8,128)(2,1)S(1)} %get-tuple-element.64), channel_id=1, source_target_pairs={{2,0},{3,1},{0,2},{1,3},{6,4},{7,5},{4,6},{5,7},{10,8},{11,9},{8,1... | collective-permute-start | bytes 442376 | tf_op jit(solution)/shard_map/ppermute | solution.py:278
  59.5 1.5 %collective-permute-start.15 = (bf16[2,128,768]{2,1,0:T(8,128)(2,1)S(1)}, bf16[2,128,768]{2,1,0:T(8,128)(2,1)S(1)}, u32[]{:S(2)}, u32[]{:S(2)}) collective-permute-start(bf16[2,128,768]{2,1,0:T(8,128)(2,1)S(1)} %get-tuple-element.56), channel_id=1, source_target_pairs={{0,13},{1,4},{2,15},{3,6},{4,1},{5,8},{6,3},{7,10},{8,5},{9,12},{1... | collective-permute-start | bytes 1179656 | tf_op jit(solution)/shard_map/ppermute | solution.py:361
  61.0 0.8 sums.1
  61.9 0.1 collective-permute-start.14
  61.9 3.7 %collective-permute-start.13 = (bf16[2,128,768]{2,1,0:T(8,128)(2,1)S(1)}, bf16[2,128,768]{2,1,0:T(8,128)(2,1)S(1)}, u32[]{:S(2)}, u32[]{:S(2)}) collective-permute-start(bf16[2,128,768]{2,1,0:T(8,128)(2,1)S(1)} %get-tuple-element.54.after_ref.after_a.after_b.after_c), channel_id=1, source_target_pairs={{0,15},{1,2},{2,1},{3,4},{4,3},{5,6},{6,5},{7,8},{8,7},{9,10},{10,... | collective-permute-start | bytes 1179656 | tf_op jit(solution)/shard_map/ppermute | solution.py:371
  65.6 0.8 split.1
  66.4 0.1 collective-permute-start.17
  66.5 5.6 %collective-permute-done.17.got_ref = bf16[48,768]{1,0:T(8,128)(2,1)S(1)} collective-permute-done((bf16[48,768]{1,0:T(8,128)(2,1)S(1)}, bf16[48,768]{1,0:T(8,128)(2,1)S(1)}, u32[]{:S(2)}, u32[]{:S(2)}) %collective-permute-start.17) | collective-permute-done | bytes 73760 | tf_op jit(solution)/shard_map/ppermute | solution.py:278
  72.1 0.1 add.4.part_ref
  72.2 10.0 %collective-permute-start.18 = (bf16[48,768]{1,0:T(8,128)(2,1)S(1)}, bf16[48,768]{1,0:T(8,128)(2,1)S(1)}, u32[]{:S(2)}, u32[]{:S(2)}) collective-permute-start(bf16[48,768]{1,0:T(8,128)(2,1)S(1)} %add.4.part_ref), channel_id=1, source_target_pairs={{8,0},{9,1},{10,2},{11,3},{12,4},{13,5},{14,6},{15,7},{0,8},{1,9},... | collective-permute-start | bytes 221192 | tf_op jit(solution)/shard_map/ppermute | solution.py:278
  82.2 1.7 %collective-permute-done.18.got_ref = bf16[48,768]{1,0:T(8,128)(2,1)S(1)} collective-permute-done((bf16[48,768]{1,0:T(8,128)(2,1)S(1)}, bf16[48,768]{1,0:T(8,128)(2,1)S(1)}, u32[]{:S(2)}, u32[]{:S(2)}) %collective-permute-start.18) | collective-permute-done | bytes 73760 | tf_op jit(solution)/shard_map/ppermute | solution.py:278
  83.9 0.1 add.5.mine_ref
  84.0 2.3 %collective-permute-start.19 = (bf16[48,768]{1,0:T(8,128)(2,1)S(1)}, bf16[48,768]{1,0:T(8,128)(2,1)S(1)}, u32[]{:S(2)}, u32[]{:S(2)}) collective-permute-start(bf16[48,768]{1,0:T(8,128)(2,1)S(1)} %add.5.mine_ref), channel_id=1, source_target_pairs={{4,0},{5,1},{6,2},{7,3},{0,4},{1,5},{2,6},{3,7},{12,8},{13,9},{14,... | collective-permute-start | bytes 221192 | tf_op jit(solution)/shard_map/ppermute | solution.py:278
  86.4 1.9 %collective-permute-done.19.got_ref = bf16[48,768]{1,0:T(8,128)(2,1)S(1)} collective-permute-done((bf16[48,768]{1,0:T(8,128)(2,1)S(1)}, bf16[48,768]{1,0:T(8,128)(2,1)S(1)}, u32[]{:S(2)}, u32[]{:S(2)}) %collective-permute-start.19) | collective-permute-done | bytes 73760 | tf_op jit(solution)/shard_map/ppermute | solution.py:278
  88.3 0.7 join.3.mine_ref
  88.9 1.3 %collective-permute-start.20 = (bf16[96,768]{1,0:T(8,128)(2,1)S(1)}, bf16[96,768]{1,0:T(8,128)(2,1)S(1)}, u32[]{:S(2)}, u32[]{:S(2)}) collective-permute-start(bf16[96,768]{1,0:T(8,128)(2,1)S(1)} %join.3.mine_ref), channel_id=1, source_target_pairs={{2,0},{3,1},{0,2},{1,3},{6,4},{7,5},{4,6},{5,7},{10,8},{11,9},{8,1... | collective-permute-start | bytes 442376 | tf_op jit(solution)/shard_map/ppermute | solution.py:278
  90.2 2.8 %collective-permute-done.20.got_ref = bf16[96,768]{1,0:T(8,128)(2,1)S(1)} collective-permute-done((bf16[96,768]{1,0:T(8,128)(2,1)S(1)}, bf16[96,768]{1,0:T(8,128)(2,1)S(1)}, u32[]{:S(2)}, u32[]{:S(2)}) %collective-permute-start.20) | collective-permute-done | bytes 147488 | tf_op jit(solution)/shard_map/ppermute | solution.py:278
  93.0 0.8 join.4.mine_ref
  93.8 5.6 %collective-permute-start.21 = (bf16[192,768]{1,0:T(8,128)(2,1)S(1)}, bf16[192,768]{1,0:T(8,128)(2,1)S(1)}, u32[]{:S(2)}, u32[]{:S(2)}) collective-permute-start(bf16[192,768]{1,0:T(8,128)(2,1)S(1)} %join.4.mine_ref), channel_id=1, source_target_pairs={{1,0},{0,1},{3,2},{2,3},{5,4},{4,5},{7,6},{6,7},{9,8},{8,9},{11,10... | collective-permute-start | bytes 884744 | tf_op jit(solution)/shard_map/ppermute | solution.py:278
  99.4 1.0 fusion
  100.5 1.4 %home.1 = (bf16[128,768]{1,0:T(8,128)(2,1)}, bf16[128,768]{1,0:T(8,128)(2,1)}) custom-call(f32[2,128,768]{2,1,0:T(8,128)S(1)} %get-tuple-element.53.own_ref, bf16[2,128,768]{2,1,0:T(8,128)(2,1)S(1)} %collective-permute-done.13.near_ref.after_a, bf16[2,128,768]{2,1,0:T(8,128)(2,1)S(1)} %collective-permute-done.14.middle_ref.after_b, ...), custom_call_target="tpu_custom_call" | custom-call | flops 1000 | bytes 786432 | tf_op jit(solution)/shard_map/home/pallas_call | solution.py:37
  101.9 1.7 %join.5 = f32[384,768]{1,0:T(8,128)} custom-call(s32[2]{0:T(128)S(1)} %pad_add_fusion.at_ref, bf16[192,768]{1,0:T(8,128)(2,1)S(1)} %join.4.mine_ref, bf16[192,768]{1,0:T(8,128)(2,1)S(1)} %collective-permute-done.21.got_ref, bf16[2,128,768]{2,1,0:T(8,128)(2,1)S(1)} %get-tuple-element.54.after_ref.after_a.after_b.after_c, ...), custom_call_target="tpu_custom_call" | custom-call | flops 1000 | bytes 2359296 | tf_op jit(solution)/shard_map/join/pallas_call | solution.py:37
  (24 shorter events, 0.1 us)
Async XLA Ops:
  0.6 25.9 %copy-start = (bf16[768,768]{1,0:T(8,128)(2,1)S(1)}, bf16[768,768]{1,0:T(8,128)(2,1)}, u32[]{:S(2)}) copy-start(bf16[768,768]{1,0:T(8,128)(2,1)} %param.11) | copy-start | bytes 3538948
  0.6 1.0 copy-start.2
  1.7 0.9 copy-start.3
  2.6 33.6 %copy-start.5 = (s32[16]{0:T(128)S(1)}, s32[16]{0:T(128)}, u32[]{:S(2)}) copy-start(s32[16]{0:T(128)} %count_ref.1) | copy-start | bytes 196
  3.1 15.4 %collective-permute-start.1 = (bf16[2,128,768]{2,1,0:T(8,128)(2,1)S(1)}, bf16[2,128,768]{2,1,0:T(8,128)(2,1)S(1)}, u32[]{:S(2)}, u32[]{:S(2)}) collective-permute-start(bf16[2,128,768]{2,1,0:T(8,128)(2,1)S(1)} %pack.1.own_ref), channel_id=1, source_target_pairs={{14,0},{3,1},{0,2},{5,3},{2,4},{7,5},{4,6},{9,7},{6,8},{11,9},{8,1... | collective-permute-start | bytes 1179656 | tf_op jit(solution)/shard_map/ppermute | solution.py:297
  8.2 15.5 %collective-permute-start = (bf16[2,128,768]{2,1,0:T(8,128)(2,1)S(1)}, bf16[2,128,768]{2,1,0:T(8,128)(2,1)S(1)}, u32[]{:S(2)}, u32[]{:S(2)}) collective-permute-start(bf16[2,128,768]{2,1,0:T(8,128)(2,1)S(1)} %pack.1.own_ref), channel_id=1, source_target_pairs={{15,0},{2,1},{1,2},{4,3},{3,4},{6,5},{5,6},{8,7},{7,8},{10,9},{9,1... | collective-permute-start | bytes 1179656 | tf_op jit(solution)/shard_map/ppermute | solution.py:296
  8.2 18.0 %collective-permute-start.3 = (bf16[2,128,768]{2,1,0:T(8,128)(2,1)S(1)}, bf16[2,128,768]{2,1,0:T(8,128)(2,1)S(1)}, u32[]{:S(2)}, u32[]{:S(2)}) collective-permute-start(bf16[2,128,768]{2,1,0:T(8,128)(2,1)S(1)} %pack.1.own_ref), channel_id=1, source_target_pairs={{1,0},{0,1},{3,2},{2,3},{5,4},{4,5},{7,6},{6,7},{9,8},{8,9},{11,10... | collective-permute-start | bytes 1179656 | tf_op jit(solution)/shard_map/ppermute | solution.py:278
  8.9 17.4 %collective-permute-start.2 = (bf16[2,128,768]{2,1,0:T(8,128)(2,1)S(1)}, bf16[2,128,768]{2,1,0:T(8,128)(2,1)S(1)}, u32[]{:S(2)}, u32[]{:S(2)}) collective-permute-start(bf16[2,128,768]{2,1,0:T(8,128)(2,1)S(1)} %pack.1.own_ref), channel_id=1, source_target_pairs={{13,0},{4,1},{15,2},{6,3},{1,4},{8,5},{3,6},{10,7},{5,8},{12,9},{7... | collective-permute-start | bytes 1179656 | tf_op jit(solution)/shard_map/ppermute | solution.py:298
  18.6 17.6 %collective-permute-start.5 = (bf16[2,128,768]{2,1,0:T(8,128)(2,1)S(1)}, bf16[2,128,768]{2,1,0:T(8,128)(2,1)S(1)}, u32[]{:S(2)}, u32[]{:S(2)}) collective-permute-start(bf16[2,128,768]{2,1,0:T(8,128)(2,1)S(1)} %collective-permute-done.1.middle_ref), channel_id=1, source_target_pairs={{1,0},{0,1},{3,2},{2,3},{5,4},{4,5},{7,6},{6,7},{9,8},{8,9},{11,10... | collective-permute-start | bytes 1179656 | tf_op jit(solution)/shard_map/ppermute | solution.py:278
  23.8 12.4 %collective-permute-start.4 = (bf16[2,128,768]{2,1,0:T(8,128)(2,1)S(1)}, bf16[2,128,768]{2,1,0:T(8,128)(2,1)}, u32[]{:S(2)}, u32[]{:S(2)}) collective-permute-start(bf16[2,128,768]{2,1,0:T(8,128)(2,1)S(1)} %collective-permute-done.near_ref), channel_id=1, source_target_pairs={{1,0},{0,1},{3,2},{2,3},{5,4},{4,5},{7,6},{6,7},{9,8},{8,9},{11,10... | collective-permute-start | bytes 1179656 | tf_op jit(solution)/shard_map/ppermute | solution.py:278
  24.5 11.6 %copy-start.4 = (bf16[1,1,128,768]{3,2,1,0:T(8,128)(2,1)S(1)}, bf16[1,1,128,768]{3,2,1,0:T(8,128)(2,1)}, u32[]{:S(2)}) copy-start(bf16[1,1,128,768]{3,2,1,0:T(8,128)(2,1)} %param.7) | copy-start | bytes 589828
  24.6 7.4 %collective-permute-start.8 = (bf16[128,768]{1,0:T(8,128)(2,1)}, bf16[128,768]{1,0:T(8,128)(2,1)S(1)}, u32[]{:S(2)}, u32[]{:S(2)}) collective-permute-start(bf16[128,768]{1,0:T(8,128)(2,1)} %bitcast.16), channel_id=1, source_target_pairs={{0,17},{1,16},{2,19},{3,18},{4,21},{5,20},{6,23},{7,22},{8,25},{9,... | collective-permute-start | bytes 589832 | tf_op jit(solution)/shard_map/ppermute | solution.py:286
  26.2 5.8 %collective-permute-start.7 = (bf16[128,768]{1,0:T(8,128)(2,1)}, bf16[128,768]{1,0:T(8,128)(2,1)S(1)}, u32[]{:S(2)}, u32[]{:S(2)}) collective-permute-start(bf16[128,768]{1,0:T(8,128)(2,1)} %bitcast.17), channel_id=1, source_target_pairs={{1,0},{0,1},{3,2},{2,3},{5,4},{4,5},{7,6},{6,7},{9,8},{8,9},{11,10... | collective-permute-start | bytes 589832 | tf_op jit(solution)/shard_map/ppermute | solution.py:278
  26.3 9.9 %collective-permute-start.6 = (bf16[128,768]{1,0:T(8,128)(2,1)}, bf16[128,768]{1,0:T(8,128)(2,1)S(1)}, u32[]{:S(2)}, u32[]{:S(2)}) collective-permute-start(bf16[128,768]{1,0:T(8,128)(2,1)} %bitcast.18), channel_id=1, source_target_pairs={{0,16},{16,0},{1,17},{17,1},{2,18},{18,2},{3,19},{19,3},{4,20},{20... | collective-permute-start | bytes 589832 | tf_op jit(solution)/shard_map/ppermute | solution.py:281
  46.0 8.6 %collective-permute-start.9 = (bf16[192,128]{1,0:T(8,128)(2,1)S(1)}, bf16[192,128]{1,0:T(8,128)(2,1)S(1)}, u32[]{:S(2)}, u32[]{:S(2)}) collective-permute-start(bf16[192,128]{1,0:T(8,128)(2,1)S(1)} %get-tuple-element.46), channel_id=1, source_target_pairs={{0,16},{16,0},{1,17},{17,1},{2,18},{18,2},{3,19},{19,3},{4,20},{20... | collective-permute-start | bytes 147464 | tf_op jit(solution)/shard_map/ppermute | solution.py:281
  47.3 7.3 %collective-permute-start.10 = (bf16[192,128]{1,0:T(8,128)(2,1)S(1)}, bf16[192,128]{1,0:T(8,128)(2,1)S(1)}, u32[]{:S(2)}, u32[]{:S(2)}) collective-permute-start(bf16[192,128]{1,0:T(8,128)(2,1)S(1)} %get-tuple-element.47), channel_id=1, source_target_pairs={{1,0},{0,1},{3,2},{2,3},{5,4},{4,5},{7,6},{6,7},{9,8},{8,9},{11,10... | collective-permute-start | bytes 147464 | tf_op jit(solution)/shard_map/ppermute | solution.py:278
  48.2 6.5 %collective-permute-start.11 = (bf16[192,128]{1,0:T(8,128)(2,1)S(1)}, bf16[192,128]{1,0:T(8,128)(2,1)S(1)}, u32[]{:S(2)}, u32[]{:S(2)}) collective-permute-start(bf16[192,128]{1,0:T(8,128)(2,1)S(1)} %get-tuple-element.48), channel_id=1, source_target_pairs={{0,17},{1,16},{2,19},{3,18},{4,21},{5,20},{6,23},{7,22},{8,25},{9,... | collective-permute-start | bytes 147464 | tf_op jit(solution)/shard_map/ppermute | solution.py:286
  48.3 6.9 %copy-start.1 = (bf16[1,1,128,768]{3,2,1,0:T(8,128)(2,1)S(1)}, bf16[1,1,128,768]{3,2,1,0:T(8,128)(2,1)}, u32[]{:S(2)}) copy-start(bf16[1,1,128,768]{3,2,1,0:T(8,128)(2,1)} %param.10) | copy-start | bytes 589828
  54.6 6.4 %collective-permute-start.12 = (bf16[3,2,128,768]{3,2,1,0:T(8,128)(2,1)S(1)}, bf16[3,2,128,768]{3,2,1,0:T(8,128)(2,1)S(1)}, u32[]{:S(2)}, u32[]{:S(2)}) collective-permute-start(bf16[3,2,128,768]{3,2,1,0:T(8,128)(2,1)S(1)} %get-tuple-element.52), channel_id=1, source_target_pairs={{1,0},{0,1},{3,2},{2,3},{5,4},{4,5},{7,6},{6,7},{9,8},{8,9},{11,10... | collective-permute-start | bytes 3538952 | tf_op jit(solution)/shard_map/ppermute | solution.py:278
  57.3 8.4 %collective-permute-start.16 = (bf16[96,768]{1,0:T(8,128)(2,1)S(1)}, bf16[96,768]{1,0:T(8,128)(2,1)S(1)}, u32[]{:S(2)}, u32[]{:S(2)}) collective-permute-start(bf16[96,768]{1,0:T(8,128)(2,1)S(1)} %get-tuple-element.64), channel_id=1, source_target_pairs={{2,0},{3,1},{0,2},{1,3},{6,4},{7,5},{4,6},{5,7},{10,8},{11,9},{8,1... | collective-permute-start | bytes 442376 | tf_op jit(solution)/shard_map/ppermute | solution.py:278
  59.5 30.7 %collective-permute-start.15 = (bf16[2,128,768]{2,1,0:T(8,128)(2,1)S(1)}, bf16[2,128,768]{2,1,0:T(8,128)(2,1)S(1)}, u32[]{:S(2)}, u32[]{:S(2)}) collective-permute-start(bf16[2,128,768]{2,1,0:T(8,128)(2,1)S(1)} %get-tuple-element.56), channel_id=1, source_target_pairs={{0,13},{1,4},{2,15},{3,6},{4,1},{5,8},{6,3},{7,10},{8,5},{9,12},{1... | collective-permute-start | bytes 1179656 | tf_op jit(solution)/shard_map/ppermute | solution.py:361
  61.9 31.1 %collective-permute-start.14 = (bf16[2,128,768]{2,1,0:T(8,128)(2,1)S(1)}, bf16[2,128,768]{2,1,0:T(8,128)(2,1)S(1)}, u32[]{:S(2)}, u32[]{:S(2)}) collective-permute-start(bf16[2,128,768]{2,1,0:T(8,128)(2,1)S(1)} %get-tuple-element.55), channel_id=1, source_target_pairs={{0,14},{1,3},{2,0},{3,5},{4,2},{5,7},{6,4},{7,9},{8,6},{9,11},{10,... | collective-permute-start | bytes 1179656 | tf_op jit(solution)/shard_map/ppermute | solution.py:372
  61.9 31.1 %collective-permute-start.13 = (bf16[2,128,768]{2,1,0:T(8,128)(2,1)S(1)}, bf16[2,128,768]{2,1,0:T(8,128)(2,1)S(1)}, u32[]{:S(2)}, u32[]{:S(2)}) collective-permute-start(bf16[2,128,768]{2,1,0:T(8,128)(2,1)S(1)} %get-tuple-element.54.after_ref.after_a.after_b.after_c), channel_id=1, source_target_pairs={{0,15},{1,2},{2,1},{3,4},{4,3},{5,6},{6,5},{7,8},{8,7},{9,10},{10,... | collective-permute-start | bytes 1179656 | tf_op jit(solution)/shard_map/ppermute | solution.py:371
  66.4 5.7 %collective-permute-start.17 = (bf16[48,768]{1,0:T(8,128)(2,1)S(1)}, bf16[48,768]{1,0:T(8,128)(2,1)S(1)}, u32[]{:S(2)}, u32[]{:S(2)}) collective-permute-start(bf16[48,768]{1,0:T(8,128)(2,1)S(1)} %get-tuple-element.66), channel_id=1, source_target_pairs={{4,0},{5,1},{6,2},{7,3},{0,4},{1,5},{2,6},{3,7},{12,8},{13,9},{14,... | collective-permute-start | bytes 221192 | tf_op jit(solution)/shard_map/ppermute | solution.py:278
  72.2 11.7 %collective-permute-start.18 = (bf16[48,768]{1,0:T(8,128)(2,1)S(1)}, bf16[48,768]{1,0:T(8,128)(2,1)S(1)}, u32[]{:S(2)}, u32[]{:S(2)}) collective-permute-start(bf16[48,768]{1,0:T(8,128)(2,1)S(1)} %add.4.part_ref), channel_id=1, source_target_pairs={{8,0},{9,1},{10,2},{11,3},{12,4},{13,5},{14,6},{15,7},{0,8},{1,9},... | collective-permute-start | bytes 221192 | tf_op jit(solution)/shard_map/ppermute | solution.py:278
  84.0 4.2 %collective-permute-start.19 = (bf16[48,768]{1,0:T(8,128)(2,1)S(1)}, bf16[48,768]{1,0:T(8,128)(2,1)S(1)}, u32[]{:S(2)}, u32[]{:S(2)}) collective-permute-start(bf16[48,768]{1,0:T(8,128)(2,1)S(1)} %add.5.mine_ref), channel_id=1, source_target_pairs={{4,0},{5,1},{6,2},{7,3},{0,4},{1,5},{2,6},{3,7},{12,8},{13,9},{14,... | collective-permute-start | bytes 221192 | tf_op jit(solution)/shard_map/ppermute | solution.py:278
  88.9 4.1 %collective-permute-start.20 = (bf16[96,768]{1,0:T(8,128)(2,1)S(1)}, bf16[96,768]{1,0:T(8,128)(2,1)S(1)}, u32[]{:S(2)}, u32[]{:S(2)}) collective-permute-start(bf16[96,768]{1,0:T(8,128)(2,1)S(1)} %join.3.mine_ref), channel_id=1, source_target_pairs={{2,0},{3,1},{0,2},{1,3},{6,4},{7,5},{4,6},{5,7},{10,8},{11,9},{8,1... | collective-permute-start | bytes 442376 | tf_op jit(solution)/shard_map/ppermute | solution.py:278
  93.8 8.1 %collective-permute-start.21 = (bf16[192,768]{1,0:T(8,128)(2,1)S(1)}, bf16[192,768]{1,0:T(8,128)(2,1)S(1)}, u32[]{:S(2)}, u32[]{:S(2)}) collective-permute-start(bf16[192,768]{1,0:T(8,128)(2,1)S(1)} %join.4.mine_ref), channel_id=1, source_target_pairs={{1,0},{0,1},{3,2},{2,3},{5,4},{4,5},{7,6},{6,7},{9,8},{8,9},{11,10... | collective-permute-start | bytes 884744 | tf_op jit(solution)/shard_map/ppermute | solution.py:278

commit v3 on v2

v3 whole, which is shorter than its diff:
```python
import functools
import math

import jax
import jax.numpy as jnp
from jax import lax
from jax.experimental import pallas as pl
from jax.experimental.pallas import tpu as pltpu
from jax.sharding import PartitionSpec as P

HEADS = 12
PMAX = 6
GROUP = 4
SLOTS = PMAX + 1
MIB = 1024 * 1024

neg_big = -1e30
bf16, f32 = jnp.bfloat16, jnp.float32
SMEM = pl.BlockSpec(memory_space=pltpu.SMEM)
VMEM = pl.BlockSpec(memory_space=pltpu.VMEM)
ANY = pl.BlockSpec(memory_space=pl.ANY)
NN = (((1,), (0,)), ((), ()))
NT = (((1,), (1,)), ((), ()))
TN = (((0,), (0,)), ((), ()))


def dot(x, y, dims):
    return lax.dot_general(x, y, dims, preferred_element_type=f32)


def shape_of(*dims, dtype=bf16):
    return jax.ShapeDtypeStruct(dims, dtype)


def skip_refs(kernel, first, count, *refs):
    kernel(*refs[:first], *refs[first + count :])


def call(kernel, ins, outs, args, scratch=(), limit=8, name=None, after=()):
    ins, args = [*ins, *[ANY] * len(after)], (*args, *after)
    if after:
        kernel = functools.partial(skip_refs, kernel, len(args) - len(after), len(after))
    return pl.pallas_call(
        kernel,
        in_specs=ins,
        out_specs=[VMEM] * len(outs),
        out_shape=outs,
        scratch_shapes=list(scratch),
        compiler_params=pltpu.CompilerParams(vmem_limit_bytes=limit * MIB),
        cost_estimate=pl.CostEstimate(flops=1, bytes_accessed=1, transcendentals=0),
        name=name,
    )(*args)


def pack_kernel(k_ref, v_ref, out_ref, sems):
    copies = [
        pltpu.make_async_copy(ref, out_ref.at[n], sems.at[n]) for n, ref in enumerate((k_ref, v_ref))
    ]
    for copy in copies:
        copy.start()
    for copy in copies:
        copy.wait()


def query_kernel(q_ref, g_ref, weight_ref, out_ref):
    out_ref[0] = q_ref[...]
    out_ref[1] = dot(g_ref[...], weight_ref[...], NT).astype(bf16)


def widen(x, wide_ref):
    span, lanes = x.shape
    head_of = lax.broadcasted_iota(jnp.int32, (span, lanes), 1) // (lanes // GROUP)
    zero = jnp.zeros_like(x)
    for h in range(GROUP):
        wide_ref[h * span : (h + 1) * span] = jnp.where(head_of == h, x, zero)


def pick(wide, span, head_width):
    blocks = [
        wide[h * head_width : (h + 1) * head_width, h * span : (h + 1) * span] for h in range(GROUP)
    ]
    return jnp.concatenate(blocks, 0)


def offsets_of(me):
    side = 2 * lax.rem(me, 2) - 1
    return (0, side, 2 * side, 3 * side, -side, -2 * side, -3 * side)


def listed(ids_ref, count_ref, reader, block):
    hit = jnp.int32(0)
    for j in range(PMAX):
        here = jnp.logical_and(ids_ref[reader, j] == block, j < count_ref[reader])
        hit = jnp.maximum(hit, here.astype(jnp.int32))
    return hit


def forward_kernel(
    ids_ref, count_ref, query_ref, own_ref, near_ref, middle_ref, far_ref, sib_ref, sib_near_ref,
    sib_middle_ref,
    mixed_ref, mine_ref, to_win_ref, stats_ref, probs_ref, keys, values,
    q_wide, raw,
    *, station_count,
):
    span, width = query_ref.shape[1:]
    head_width = width // HEADS
    lanes = GROUP * head_width
    me = lax.axis_index("station")
    window = lax.axis_index("dp")
    parts = (own_ref, near_ref, middle_ref, far_ref, sib_ref, sib_near_ref, sib_middle_ref)
    live = []
    for j, offset in enumerate(offsets_of(me)):
        station = lax.rem(me + offset + station_count, station_count)
        live.append(listed(ids_ref, count_ref, me, station) if j else None)
        keys[j * span : (j + 1) * span] = parts[j][0]
        values[j * span : (j + 1) * span] = parts[j][1]
    for group in range(HEADS // GROUP):
        cols = slice(group * lanes, (group + 1) * lanes)
        widen(query_ref[0, :, cols] * bf16(1.0 / math.sqrt(head_width)), q_wide)
        top = None
        for j in range(SLOTS):
            rows = slice(j * span, (j + 1) * span)
            scores = dot(keys[rows, cols], q_wide[...], NT)
            if j:
                scores = jnp.where(live[j] > 0, scores, neg_big)
            raw[rows] = scores
            here = jnp.max(scores, 0, keepdims=True)
            top = here if top is None else jnp.maximum(top, here)
        total = jnp.zeros_like(top)
        for j in range(SLOTS):
            rows = slice(j * span, (j + 1) * span)
            weight = jnp.exp(raw[rows] - top)
            raw[rows] = weight
            total = total + jnp.sum(weight, 0, keepdims=True)
        inverse = 1.0 / total
        for j in range(SLOTS):
            rows = slice(j * span, (j + 1) * span)
            probs_ref[group, rows] = (raw[rows] * inverse).astype(bf16)
        mixed = pick(dot(values[:, cols], probs_ref[group], TN), span, head_width).astype(bf16)
        mixed_ref[cols] = mixed
        product = query_ref[1, :, cols].astype(f32).T * mixed.astype(f32)
        log_sum = top + jnp.log(total)
        for h in range(GROUP):
            head = group * GROUP + h
            stats_ref[head : head + 1] = log_sum[:, h * span : (h + 1) * span]
            stats_ref[HEADS + head : HEADS + head + 1] = jnp.sum(
                product[h * head_width : (h + 1) * head_width], 0, keepdims=True
            )
    half = mine_ref.shape[0]
    for ref, w in ((mine_ref, window), (to_win_ref, 1 - window)):
        start = pl.multiple_of(lax.rem(w, 2) * half, half)
        ref[...] = mixed_ref[pl.ds(start, half)]


def query_grad_kernel(query_ref, stats_ref, keys, values, probs_ref, dq_ref, g_wide, grads_half):
    span, width = query_ref.shape[1:]
    head_width = width // HEADS
    lanes = GROUP * head_width
    scale = 1.0 / math.sqrt(head_width)
    for group in range(HEADS // GROUP):
        cols = slice(group * lanes, (group + 1) * lanes)
        widen(query_ref[1, :, cols], g_wide)
        first = HEADS + group * GROUP
        delta = jnp.concatenate([stats_ref[first + h : first + h + 1] for h in range(GROUP)], 1)
        for j in range(SLOTS):
            rows = slice(j * span, (j + 1) * span)
            back = dot(values[rows, cols], g_wide[...], NT)
            grads_half[rows] = (probs_ref[group, rows].astype(f32) * (back - delta)).astype(bf16)
        wide = dot(keys[:, cols], grads_half[...], TN)
        dq_ref[:, cols] = (pick(wide, span, head_width).T * scale).astype(bf16)


def key_grad_kernel(
    ids_ref, count_ref, stats_ref, kv_ref, own_ref, near_ref, middle_ref, far_ref, sib_ref,
    sib_near_ref, sib_middle_ref,
    dk_ref, dv_ref,
    queries, grads, k_wide, v_wide, stats, probs_half, grads_half,
    *, station_count,
):
    span, width = kv_ref.shape[1:]
    head_width = width // HEADS
    lanes = GROUP * head_width
    scale = 1.0 / math.sqrt(head_width)
    me = lax.axis_index("station")
    parts = (own_ref, near_ref, middle_ref, far_ref, sib_ref, sib_near_ref, sib_middle_ref)
    live = []
    for j, offset in enumerate(offsets_of(me)):
        station = lax.rem(me + offset + station_count, station_count)
        live.append(listed(ids_ref, count_ref, station, me) if j else None)
        queries[j * span : (j + 1) * span] = parts[j][0]
        grads[j * span : (j + 1) * span] = parts[j][1]
        stats[j] = stats_ref[station].T
    for group in range(HEADS // GROUP):
        cols = slice(group * lanes, (group + 1) * lanes)
        widen(kv_ref[0, :, cols] * bf16(scale), k_wide)
        widen(kv_ref[1, :, cols], v_wide)
        for j in range(SLOTS):
            rows = slice(j * span, (j + 1) * span)
            scores = dot(queries[rows, cols], k_wide[...], NT)
            back = dot(grads[rows, cols], v_wide[...], NT)
            for h in range(GROUP):
                head = group * GROUP + h
                at = slice(h * span, (h + 1) * span)
                prob = jnp.exp(scores[:, at] - stats[j, :, head : head + 1])
                if j:
                    prob = jnp.where(live[j] > 0, prob, 0.0)
                probs_half[rows, at] = prob.astype(bf16)
                delta = stats[j, :, HEADS + head : HEADS + head + 1]
                grads_half[rows, at] = (prob * (back[:, at] - delta)).astype(bf16)
        wide = dot(queries[:, cols], grads_half[...], TN)
        dk_ref[:, cols] = (pick(wide, span, head_width).T * scale).astype(bf16)
        wide = dot(grads[:, cols], probs_half[...], TN)
        dv_ref[:, cols] = pick(wide, span, head_width).T.astype(bf16)


def sides(stride, half):
    bit = lax.rem(lax.axis_index("station") // stride, 2)
    send = pl.ds(pl.multiple_of((1 - bit) * half, half), half)
    keep = pl.ds(pl.multiple_of(bit * half, half), half)
    return send, keep


def weight_kernel(stride, mine_ref, win_ref, g_ref, g_win_ref, send_ref, keep_ref, left, right):
    span = mine_ref.shape[1]
    send, keep = sides(stride, send_ref.shape[0])
    left[:, :span] = mine_ref[...]
    left[:, span:] = win_ref[...]
    right[:span] = g_ref[...]
    right[span:] = g_win_ref[...]
    send_ref[...] = dot(left[send], right[...], NN).astype(bf16)
    keep_ref[...] = dot(left[keep], right[...], NN)


def split_kernel(stride, part_ref, got_ref, send_ref, keep_ref):
    send, keep = sides(stride, send_ref.shape[0])
    send_ref[...] = (part_ref[send] + got_ref[send].astype(f32)).astype(bf16)
    keep_ref[...] = part_ref[keep] + got_ref[keep].astype(f32)


def round_kernel(part_ref, got_ref, out_ref):
    out_ref[...] = (part_ref[...].astype(f32) + got_ref[...].astype(f32)).astype(bf16)


def join_kernel(stride, scale, mine_ref, got_ref, out_ref):
    other, here = sides(stride, mine_ref.shape[0])
    for place, ref in ((here, mine_ref), (other, got_ref)):
        value = ref[...]
        if scale is not None:
            value = value.astype(f32) * scale
        out_ref[place] = value


def local(
    query_states, key_states, value_states, grad_output, out_weight, partner_ids, partner_count
):
    span, width = query_states.shape[2:]
    stations = lax.axis_size("station")
    windows = lax.axis_size("dp")
    me = lax.axis_index("station").astype(jnp.int32)
    side = [1 if s % 2 else -1 for s in range(stations)]

    def routes(steps):
        return [((s + steps * side[s]) % stations, s) for s in range(stations)]

    def swap(value, stride):
        return lax.ppermute(value, "station", [(s ^ stride, s) for s in range(stations)])

    def other_window(value):
        return lax.ppermute(value, "dp", [(0, 1), (1, 0)])

    def flat(x):
        return x.reshape(span, width)

    q, k, v, g = flat(query_states), flat(key_states), flat(value_states), flat(grad_output)
    dma = pltpu.SemaphoreType.DMA
    pair = shape_of(2, span, width)
    (kv,) = call(pack_kernel, [ANY, ANY], [pair], (k, v), [dma((2,))], limit=56, name="pack")

    def spread(value):
        near, middle, far = (lax.ppermute(value, "station", routes(n)) for n in (1, 2, 3))
        return value, near, middle, far, swap(value, 1), swap(near, 1), swap(middle, 1)

    kv_all = spread(kv)
    g_win = other_window(g) if windows == 2 else g
    (qg,) = call(query_kernel, [VMEM] * 3, [pair], (q, g, out_weight), name="queries")
    qg_all = spread(qg)

    lanes = width // HEADS * GROUP
    groups = HEADS // GROUP
    half = width // 2
    half_shape = shape_of(half, span)
    mixed, mine, to_win, stats, probs, keys, values = call(
        functools.partial(forward_kernel, station_count=stations),
        [SMEM] * 2 + [VMEM] * 8,
        [
            shape_of(width, span), half_shape, half_shape,
            shape_of(2 * HEADS, span, dtype=f32),
            shape_of(groups, SLOTS * span, GROUP * span),
            shape_of(SLOTS * span, width),
            shape_of(SLOTS * span, width),
        ],
        (partner_ids, partner_count, qg, *kv_all),
        [pltpu.VMEM((GROUP * span, lanes), bf16), pltpu.VMEM((SLOTS * span, GROUP * span), f32)],
        limit=20, name="forward",
    )
    all_stats = lax.all_gather(stats, "station", axis=0)
    (grad_query,) = call(
        query_grad_kernel,
        [VMEM] * 5,
        [shape_of(span, width)],
        (qg, stats, keys, values, probs),
        [pltpu.VMEM((GROUP * span, lanes), bf16), pltpu.VMEM((SLOTS * span, GROUP * span), bf16)],
        limit=20, name="query_grad",
    )

    grad_key, grad_value = call(
        functools.partial(key_grad_kernel, station_count=stations),
        [SMEM] * 2 + [VMEM] * 9,
        [shape_of(span, width)] * 2,
        (partner_ids, partner_count, all_stats, kv, *qg_all),
        [
            pltpu.VMEM((SLOTS * span, width), bf16),
            pltpu.VMEM((SLOTS * span, width), bf16),
            pltpu.VMEM((GROUP * span, lanes), bf16),
            pltpu.VMEM((GROUP * span, lanes), bf16),
            pltpu.VMEM((SLOTS, span, 2 * HEADS), f32),
            pltpu.VMEM((SLOTS * span, GROUP * span), bf16),
            pltpu.VMEM((SLOTS * span, GROUP * span), bf16),
        ],
        limit=20, name="key_grad",
    )

    if windows == 2:
        rows = half // 2
        send, part = call(
            functools.partial(weight_kernel, 1),
            [VMEM] * 4,
            [shape_of(rows, width), shape_of(rows, width, dtype=f32)],
            (mine, other_window(to_win), g, g_win),
            [pltpu.VMEM((half, 2 * span), bf16), pltpu.VMEM((2 * span, width), bf16)],
            name="weight", after=(grad_query, *qg_all[1:3]),
        )
    else:
        whole = lax.dot_general(mixed, g, NN, preferred_element_type=f32).astype(bf16)
        whole = lax.psum_scatter(whole, "dp", scatter_dimension=0, tiled=True).astype(f32)
        rows = whole.shape[0] // 2
        bit = me % 2
        part = lax.dynamic_slice_in_dim(whole, bit * rows, rows, 0)
        send = lax.dynamic_slice_in_dim(whole, (1 - bit) * rows, rows, 0).astype(bf16)
    got = swap(send, 1)
    halved = [1]
    stride = 2
    while rows >= 96 and stride < stations:
        rows //= 2
        send, part = call(
            functools.partial(split_kernel, stride),
            [VMEM, VMEM],
            [shape_of(rows, width), shape_of(rows, width, dtype=f32)],
            (part, got),
            name="split", after=qg_all[3:4] if stride == 4 else (),
        )
        got = swap(send, stride)
        halved.append(stride)
        stride *= 2

    def add_round(part, got, after=()):
        out = [shape_of(rows, width)]
        return call(round_kernel, [VMEM, VMEM], out, (part, got), name="add", after=after)[0]

    total = add_round(part, got, (all_stats,))
    while stride < stations:
        total = add_round(total, swap(total, stride))
        stride *= 2
    scale = 1.0 / math.sqrt(span * windows * stations)
    for stride in reversed(halved):
        last = stride == 1
        (total,) = call(
            functools.partial(join_kernel, stride, scale if last else None),
            [VMEM, VMEM],
            [shape_of(2 * total.shape[0], width, dtype=f32 if last else bf16)],
            (total, swap(total, stride)),
            name="join", after=(grad_key,) if stride == 2 else (),
        )

    layer_output = lax.dot_general(mixed, out_weight, TN, preferred_element_type=f32).astype(bf16)
    shape = query_states.shape
    return (
        layer_output.reshape(shape),
        grad_query.reshape(shape),
        grad_key.reshape(shape),
        grad_value.reshape(shape),
        total,
    )


def solution(mesh):
    split = P("dp", "station", None, None)
    return jax.shard_map(
        local,
        mesh=mesh,
        in_specs=(split, split, split, split, P(), P(), P()),
        out_specs=(split, split, split, split, P("dp", None)),
        check_vma=False,
    )
```

time: 104 us -> 106 us (1.019)
  the two profiles are of different devices: /device:TPU:1 before, /device:TPU:3 now
where the time goes in v3:
time: 106 us; the launch traced here: 105 us
  starting transfers between devices  31.7 us (30%)
  waiting for transfers between devices  26.6 us (25%)
  Pallas kernels  22.4 us (21%)
  blocking collectives  18.4 us (17%)
  local copies, waits for them, and re-layouts  4.15 us (4%)
    ppermute x13, starting transfers between devices, swap(): lax.ppermute(value, 'station', [(s ^ stride, s) for s in range(stations)])  23.2 us
    pallas_call x13, Pallas kernels, call(): pl.pallas_call(kernel, in_specs=ins, out_specs=[VMEM] * len(outs), out_sh...  22.4 us
    all_gather x1, blocking collectives, local(): all_stats = lax.all_gather(stats, 'station', axis=0)  18.4 us
    ppermute x6, waiting for transfers between devices, spread(): lax.ppermute(value, 'station', routes(n))  18.3 us
    ppermute x13, waiting for transfers between devices, swap(): lax.ppermute(value, 'station', [(s ^ stride, s) for s in range(stations)])  8.28 us
    ppermute x6, starting transfers between devices, spread(): lax.ppermute(value, 'station', routes(n))  6.96 us
    unnamed x17, local copies, waits for them, and re-layouts  4.15 us
  transfers between devices with their start and end apart: 21, of which 6 were waited for; matrix products, arithmetic and copies ran while one was open for 1% of the time, Pallas kernels for 17%

profile of v3, /device:TPU:3, one launch (start us, length us, event | category | flops | bytes accessed | tf_op | source)
XLA Modules:
  0.0 105.1 jit_solution(3867573342076154508)
XLA Ops:
  0.6 1.8 %pack.1.own_ref.kv_ref = bf16[2,128,768]{2,1,0:T(8,128)(2,1)} custom-call(bf16[128,768]{1,0:T(8,128)(2,1)} %bitcast.17, bf16[128,768]{1,0:T(8,128)(2,1)} %bitcast.18), custom_call_target="tpu_custom_call" | custom-call | flops 1 | bytes 1 | tf_op jit(solution)/shard_map/pack/pallas_call | solution.py:43
  2.4 0.0 copy-start.6
  2.5 1.9 %collective-permute-start = (bf16[2,128,768]{2,1,0:T(8,128)(2,1)}, bf16[2,128,768]{2,1,0:T(8,128)(2,1)S(1)}, u32[]{:S(2)}, u32[]{:S(2)}) collective-permute-start(bf16[2,128,768]{2,1,0:T(8,128)(2,1)} %pack.1.own_ref.kv_ref), channel_id=1, source_target_pairs={{15,0},{2,1},{1,2},{4,3},{3,4},{6,5},{5,6},{8,7},{7,8},{10,9},{9,1... | collective-permute-start | bytes 1179656 | tf_op jit(solution)/shard_map/ppermute | solution.py:280
  4.3 0.2 collective-permute-start.1
  4.5 2.2 %collective-permute-start.2 = (bf16[2,128,768]{2,1,0:T(8,128)(2,1)}, bf16[2,128,768]{2,1,0:T(8,128)(2,1)S(1)}, u32[]{:S(2)}, u32[]{:S(2)}) collective-permute-start(bf16[2,128,768]{2,1,0:T(8,128)(2,1)} %pack.1.own_ref.kv_ref), channel_id=1, source_target_pairs={{13,0},{4,1},{15,2},{6,3},{1,4},{8,5},{3,6},{10,7},{5,8},{12,9},{7... | collective-permute-start | bytes 1179656 | tf_op jit(solution)/shard_map/ppermute | solution.py:280
  6.7 1.5 %collective-permute-start.3 = (bf16[2,128,768]{2,1,0:T(8,128)(2,1)}, bf16[2,128,768]{2,1,0:T(8,128)(2,1)S(1)}, u32[]{:S(2)}, u32[]{:S(2)}) collective-permute-start(bf16[2,128,768]{2,1,0:T(8,128)(2,1)} %pack.1.own_ref.kv_ref), channel_id=1, source_target_pairs={{1,0},{0,1},{3,2},{2,3},{5,4},{4,5},{7,6},{6,7},{9,8},{8,9},{11,10... | collective-permute-start | bytes 1179656 | tf_op jit(solution)/shard_map/ppermute | solution.py:266
  8.3 5.9 %collective-permute-done.near_ref = bf16[2,128,768]{2,1,0:T(8,128)(2,1)S(1)} collective-permute-done((bf16[2,128,768]{2,1,0:T(8,128)(2,1)}, bf16[2,128,768]{2,1,0:T(8,128)(2,1)S(1)}, u32[]{:S(2)}, u32[]{:S(2)}) %collective-permute-start) | collective-permute-done | bytes 393248 | tf_op jit(solution)/shard_map/ppermute | solution.py:280
  14.1 8.0 %collective-permute-start.4 = (bf16[2,128,768]{2,1,0:T(8,128)(2,1)S(1)}, bf16[2,128,768]{2,1,0:T(8,128)(2,1)S(1)}, u32[]{:S(2)}, u32[]{:S(2)}) collective-permute-start(bf16[2,128,768]{2,1,0:T(8,128)(2,1)S(1)} %collective-permute-done.near_ref), channel_id=1, source_target_pairs={{1,0},{0,1},{3,2},{2,3},{5,4},{4,5},{7,6},{6,7},{9,8},{8,9},{11,10... | collective-permute-start | bytes 1179656 | tf_op jit(solution)/shard_map/ppermute | solution.py:266
  22.2 0.0 collective-permute-done.1.middle_ref
  22.2 1.1 %collective-permute-start.5 = (bf16[2,128,768]{2,1,0:T(8,128)(2,1)S(1)}, bf16[2,128,768]{2,1,0:T(8,128)(2,1)}, u32[]{:S(2)}, u32[]{:S(2)}) collective-permute-start(bf16[2,128,768]{2,1,0:T(8,128)(2,1)S(1)} %collective-permute-done.1.middle_ref), channel_id=1, source_target_pairs={{1,0},{0,1},{3,2},{2,3},{5,4},{4,5},{7,6},{6,7},{9,8},{8,9},{11,10... | collective-permute-start | bytes 1179656 | tf_op jit(solution)/shard_map/ppermute | solution.py:266
  23.2 1.3 %copy-done = bf16[768,768]{1,0:T(8,128)(2,1)S(1)} copy-done((bf16[768,768]{1,0:T(8,128)(2,1)S(1)}, bf16[768,768]{1,0:T(8,128)(2,1)}, u32[]{:S(2)}) %copy-start) | copy-done | bytes 1179672
  24.5 0.9 copy-done.5
  25.4 1.5 %queries.1.query_ref.own_ref = bf16[2,128,768]{2,1,0:T(8,128)(2,1)S(1)} custom-call(bf16[128,768]{1,0:T(8,128)(2,1)S(1)} %bitcast.16, bf16[128,768]{1,0:T(8,128)(2,1)} %bitcast.1.g_ref.refs_2_, bf16[768,768]{1,0:T(8,128)(2,1)S(1)} %copy-done), custom_call_target="tpu_custom_call" | custom-call | flops 1 | bytes 1 | tf_op jit(solution)/shard_map/queries/pallas_call | solution.py:43
  27.0 1.4 %collective-permute-start.6 = (bf16[2,128,768]{2,1,0:T(8,128)(2,1)S(1)}, bf16[2,128,768]{2,1,0:T(8,128)(2,1)S(1)}, u32[]{:S(2)}, u32[]{:S(2)}) collective-permute-start(bf16[2,128,768]{2,1,0:T(8,128)(2,1)S(1)} %queries.1.query_ref.own_ref), channel_id=1, source_target_pairs={{15,0},{2,1},{1,2},{4,3},{3,4},{6,5},{5,6},{8,7},{7,8},{10,9},{9,1... | collective-permute-start | bytes 1179656 | tf_op jit(solution)/shard_map/ppermute | solution.py:280
  28.3 0.0 collective-permute-done.2.far_ref
  28.3 0.0 collective-permute-start.7
  28.4 1.3 %collective-permute-start.13 = (bf16[128,768]{1,0:T(8,128)(2,1)}, bf16[128,768]{1,0:T(8,128)(2,1)}, u32[]{:S(2)}, u32[]{:S(2)}) collective-permute-start(bf16[128,768]{1,0:T(8,128)(2,1)} %bitcast.1.g_ref.refs_2_), channel_id=1, source_target_pairs={{0,16},{16,0},{1,17},{17,1},{2,18},{18,2},{3,19},{19,3},{4,20},{20... | collective-permute-start | bytes 589832 | tf_op jit(solution)/shard_map/ppermute | solution.py:269
  29.7 0.1 copy.12.ids_ref
  29.8 0.0 collective-permute-done.5.sib_middle_ref
  29.8 5.5 %forward.1 = (bf16[768,128]{1,0:T(8,128)(2,1)S(1)}, bf16[384,128]{1,0:T(8,128)(2,1)S(1)}, bf16[384,128]{1,0:T(8,128)(2,1)S(1)}, f32[24,128]{1,0:T(8,128)S(1)}, b...) custom-call(s32[16,6]{1,0:T(8,128)S(1)} %copy.12.ids_ref, ...), custom_call_target="tpu_custom_call" | custom-call | flops 1 | bytes 1 | tf_op jit(solution)/shard_map/forward/pallas_call | solution.py:43
  35.2 0.3 collective-permute-start.12
  35.5 3.5 %query_grad.1.refs_4_ = bf16[128,768]{1,0:T(8,128)(2,1)} custom-call(bf16[2,128,768]{2,1,0:T(8,128)(2,1)S(1)} %queries.1.query_ref.own_ref, f32[24,128]{1,0:T(8,128)S(1)} %get-tuple-element.21.stats_ref, bf16[896,768]{1,0:T(8,128)(2,1)S(1)} %get-tuple-element.22.keys, bf16[896,768]{1,0:T(8,128)(2,1)S(1)} %get-tuple-element.23.values, ...), custom_call_target="tpu_custom_call" | custom-call | flops 1 | bytes 1 | tf_op jit(solution)/shard_map/query_grad/pallas_call | solution.py:43
  39.0 0.0 collective-permute-done.6.near_ref.refs_5_
  39.0 5.9 %collective-permute-done.7.middle_ref.refs_6_ = bf16[2,128,768]{2,1,0:T(8,128)(2,1)S(1)} collective-permute-done((bf16[2,128,768]{2,1,0:T(8,128)(2,1)S(1)}, bf16[2,128,768]{2,1,0:T(8,128)(2,1)S(1)}, u32[]{:S(2)}, u32[]{:S(2)}) %collective-permute-start.7) | collective-permute-done | bytes 393248 | tf_op jit(solution)/shard_map/ppermute | solution.py:280
  44.9 0.0 collective-permute-done.12.refs_1_
  44.9 0.9 copy-done.3
  45.8 1.3 %weight.1 = (bf16[192,768]{1,0:T(8,128)(2,1)S(1)}, f32[192,768]{1,0:T(8,128)S(1)}) custom-call(bf16[384,128]{1,0:T(8,128)(2,1)S(1)} %get-tuple-element.27.refs_0_, bf16[384,128]{1,0:T(8,128)(2,1)S(1)} %collective-permute-done.12.refs_1_, bf16[128,768]{1,0:T(8,128)(2,1)} %bitcast.1.g_ref.refs_2_, bf16[128,768]{1,0:T(8,128)(2,1)} %collective-permute-done.13.refs_3_, ...), custom_call_target="tpu_custom_call" | custom-call | flops 1 | bytes 1 | tf_op jit(solution)/shard_map/weight/pallas_call | solution.py:43
  47.2 2.1 %collective-permute-start.14 = (bf16[192,768]{1,0:T(8,128)(2,1)S(1)}, bf16[192,768]{1,0:T(8,128)(2,1)S(1)}, u32[]{:S(2)}, u32[]{:S(2)}) collective-permute-start(bf16[192,768]{1,0:T(8,128)(2,1)S(1)} %get-tuple-element.30), channel_id=1, source_target_pairs={{1,0},{0,1},{3,2},{2,3},{5,4},{4,5},{7,6},{6,7},{9,8},{8,9},{11,10... | collective-permute-start | bytes 884744 | tf_op jit(solution)/shard_map/ppermute | solution.py:266
  49.2 1.3 %collective-permute-start.8 = (bf16[2,128,768]{2,1,0:T(8,128)(2,1)S(1)}, bf16[2,128,768]{2,1,0:T(8,128)(2,1)S(1)}, u32[]{:S(2)}, u32[]{:S(2)}) collective-permute-start(bf16[2,128,768]{2,1,0:T(8,128)(2,1)S(1)} %queries.1.query_ref.own_ref), channel_id=1, source_target_pairs={{13,0},{4,1},{15,2},{6,3},{1,4},{8,5},{3,6},{10,7},{5,8},{12,9},{7... | collective-permute-start | bytes 1179656 | tf_op jit(solution)/shard_map/ppermute | solution.py:280
  50.5 0.0 collective-permute-done.14.got_ref
  50.5 0.4 collective-permute-start.15
  50.9 2.4 %collective-permute-start.9 = (bf16[2,128,768]{2,1,0:T(8,128)(2,1)S(1)}, bf16[2,128,768]{2,1,0:T(8,128)(2,1)S(1)}, u32[]{:S(2)}, u32[]{:S(2)}) collective-permute-start(bf16[2,128,768]{2,1,0:T(8,128)(2,1)S(1)} %queries.1.query_ref.own_ref), channel_id=1, source_target_pairs={{1,0},{0,1},{3,2},{2,3},{5,4},{4,5},{7,6},{6,7},{9,8},{8,9},{11,10... | collective-permute-start | bytes 1179656 | tf_op jit(solution)/shard_map/ppermute | solution.py:266
  53.3 0.5 collective-permute-start.11
  53.8 6.5 %collective-permute-done.8.far_ref.refs_2_ = bf16[2,128,768]{2,1,0:T(8,128)(2,1)S(1)} collective-permute-done((bf16[2,128,768]{2,1,0:T(8,128)(2,1)S(1)}, bf16[2,128,768]{2,1,0:T(8,128)(2,1)S(1)}, u32[]{:S(2)}, u32[]{:S(2)}) %collective-permute-start.8) | collective-permute-done | bytes 393248 | tf_op jit(solution)/shard_map/ppermute | solution.py:280
  60.4 1.7 %collective-permute-start.16 = (bf16[48,768]{1,0:T(8,128)(2,1)S(1)}, bf16[48,768]{1,0:T(8,128)(2,1)S(1)}, u32[]{:S(2)}, u32[]{:S(2)}) collective-permute-start(bf16[48,768]{1,0:T(8,128)(2,1)S(1)} %get-tuple-element.34), channel_id=1, source_target_pairs={{4,0},{5,1},{6,2},{7,3},{0,4},{1,5},{2,6},{3,7},{12,8},{13,9},{14,... | collective-permute-start | bytes 221192 | tf_op jit(solution)/shard_map/ppermute | solution.py:266
  62.0 18.4 %all-gather = f32[384,128]{1,0:T(8,128)S(1)} all-gather(f32[24,128]{1,0:T(8,128)S(1)} %get-tuple-element.21.stats_ref), channel_id=2, replica_groups=mesh['dp'=2,'station'=16] {'station'}, dimensions={0}, use_global_device_ids=true | all-gather | bytes 208896 | tf_op jit(solution)/shard_map/all_gather | solution.py:306
  80.5 0.1 collective-permute-start.17
  80.6 4.9 %collective-permute-done.17.got_ref = bf16[48,768]{1,0:T(8,128)(2,1)S(1)} collective-permute-done((bf16[48,768]{1,0:T(8,128)(2,1)S(1)}, bf16[48,768]{1,0:T(8,128)(2,1)S(1)}, u32[]{:S(2)}, u32[]{:S(2)}) %collective-permute-start.17) | collective-permute-done | bytes 73760 | tf_op jit(solution)/shard_map/ppermute | solution.py:266
  85.5 0.1 collective-permute-start.18
  85.6 3.2 %collective-permute-done.18.got_ref = bf16[48,768]{1,0:T(8,128)(2,1)S(1)} collective-permute-done((bf16[48,768]{1,0:T(8,128)(2,1)S(1)}, bf16[48,768]{1,0:T(8,128)(2,1)S(1)}, u32[]{:S(2)}, u32[]{:S(2)}) %collective-permute-start.18) | collective-permute-done | bytes 73760 | tf_op jit(solution)/shard_map/ppermute | solution.py:266
  88.8 0.0 copy-start.1
  88.8 3.0 %collective-permute-start.19 = (bf16[96,768]{1,0:T(8,128)(2,1)S(1)}, bf16[96,768]{1,0:T(8,128)(2,1)S(1)}, u32[]{:S(2)}, u32[]{:S(2)}) collective-permute-start(bf16[96,768]{1,0:T(8,128)(2,1)S(1)} %join.3.refs_0_), channel_id=1, source_target_pairs={{2,0},{3,1},{0,2},{1,3},{6,4},{7,5},{4,6},{5,7},{10,8},{11,9},{8,1... | collective-permute-start | bytes 442376 | tf_op jit(solution)/shard_map/ppermute | solution.py:266
  91.8 7.5 %key_grad.1 = (bf16[128,768]{1,0:T(8,128)(2,1)}, bf16[128,768]{1,0:T(8,128)(2,1)}) custom-call(s32[16,6]{1,0:T(8,128)S(1)} %copy.12.ids_ref, s32[16]{0:T(128)S(1)} %copy-done.6, f32[16,24,128]{2,1,0:T(8,128)S(1)} %bitcast.13, bf16[2,128,768]{2,1,0:T(8,128)(2,1)S(1)} %copy-done.2, bf16[2,128,768]{2,1,0:T(8,128)(2,1)S(1)} %queries.1.query_ref.own_ref, ...), custom_call_target="tpu_custom_call" | custom-call | flops 1 | bytes 1 | tf_op jit(solution)/shard_map/key_grad/pallas_call | solution.py:43
  99.3 0.9 copy-done.4
  100.3 2.5 %collective-permute-start.20 = (bf16[192,768]{1,0:T(8,128)(2,1)S(1)}, bf16[192,768]{1,0:T(8,128)(2,1)S(1)}, u32[]{:S(2)}, u32[]{:S(2)}) collective-permute-start(bf16[192,768]{1,0:T(8,128)(2,1)S(1)} %join.4.mine_ref), channel_id=1, source_target_pairs={{1,0},{0,1},{3,2},{2,3},{5,4},{4,5},{7,6},{6,7},{9,8},{8,9},{11,10... | collective-permute-start | bytes 884744 | tf_op jit(solution)/shard_map/ppermute | solution.py:266
  102.7 1.0 fusion
  103.8 0.2 collective-permute-done.20.got_ref
  104.0 1.1 %join.5 = f32[384,768]{1,0:T(8,128)} custom-call(bf16[192,768]{1,0:T(8,128)(2,1)S(1)} %join.4.mine_ref, bf16[192,768]{1,0:T(8,128)(2,1)S(1)} %collective-permute-done.20.got_ref), custom_call_target="tpu_custom_call" | custom-call | flops 1 | bytes 1 | tf_op jit(solution)/shard_map/join/pallas_call | solution.py:43
  (26 shorter events, 0.2 us)
Async XLA Ops:
  0.6 29.0 %copy-start.7 = (s32[16,6]{0,1:T(8,128)S(1)}, s32[16,6]{0,1:T(8,128)}, u32[]{:S(2)}) copy-start(s32[16,6]{0,1:T(8,128)} %param.12) | copy-start | bytes 1156
  2.4 27.3 %copy-start.6 = (s32[16]{0:T(128)S(1)}, s32[16]{0:T(128)}, u32[]{:S(2)}) copy-start(s32[16]{0:T(128)} %count_ref.3) | copy-start | bytes 196
  2.5 11.7 %collective-permute-start = (bf16[2,128,768]{2,1,0:T(8,128)(2,1)}, bf16[2,128,768]{2,1,0:T(8,128)(2,1)S(1)}, u32[]{:S(2)}, u32[]{:S(2)}) collective-permute-start(bf16[2,128,768]{2,1,0:T(8,128)(2,1)} %pack.1.own_ref.kv_ref), channel_id=1, source_target_pairs={{15,0},{2,1},{1,2},{4,3},{3,4},{6,5},{5,6},{8,7},{7,8},{10,9},{9,1... | collective-permute-start | bytes 1179656 | tf_op jit(solution)/shard_map/ppermute | solution.py:280
  4.3 17.8 %collective-permute-start.1 = (bf16[2,128,768]{2,1,0:T(8,128)(2,1)}, bf16[2,128,768]{2,1,0:T(8,128)(2,1)S(1)}, u32[]{:S(2)}, u32[]{:S(2)}) collective-permute-start(bf16[2,128,768]{2,1,0:T(8,128)(2,1)} %pack.1.own_ref.kv_ref), channel_id=1, source_target_pairs={{14,0},{3,1},{0,2},{5,3},{2,4},{7,5},{4,6},{9,7},{6,8},{11,9},{8,1... | collective-permute-start | bytes 1179656 | tf_op jit(solution)/shard_map/ppermute | solution.py:280
  4.5 23.8 %collective-permute-start.2 = (bf16[2,128,768]{2,1,0:T(8,128)(2,1)}, bf16[2,128,768]{2,1,0:T(8,128)(2,1)S(1)}, u32[]{:S(2)}, u32[]{:S(2)}) collective-permute-start(bf16[2,128,768]{2,1,0:T(8,128)(2,1)} %pack.1.own_ref.kv_ref), channel_id=1, source_target_pairs={{13,0},{4,1},{15,2},{6,3},{1,4},{8,5},{3,6},{10,7},{5,8},{12,9},{7... | collective-permute-start | bytes 1179656 | tf_op jit(solution)/shard_map/ppermute | solution.py:280
  6.7 21.7 %collective-permute-start.3 = (bf16[2,128,768]{2,1,0:T(8,128)(2,1)}, bf16[2,128,768]{2,1,0:T(8,128)(2,1)S(1)}, u32[]{:S(2)}, u32[]{:S(2)}) collective-permute-start(bf16[2,128,768]{2,1,0:T(8,128)(2,1)} %pack.1.own_ref.kv_ref), channel_id=1, source_target_pairs={{1,0},{0,1},{3,2},{2,3},{5,4},{4,5},{7,6},{6,7},{9,8},{8,9},{11,10... | collective-permute-start | bytes 1179656 | tf_op jit(solution)/shard_map/ppermute | solution.py:266
  14.1 15.6 %collective-permute-start.4 = (bf16[2,128,768]{2,1,0:T(8,128)(2,1)S(1)}, bf16[2,128,768]{2,1,0:T(8,128)(2,1)S(1)}, u32[]{:S(2)}, u32[]{:S(2)}) collective-permute-start(bf16[2,128,768]{2,1,0:T(8,128)(2,1)S(1)} %collective-permute-done.near_ref), channel_id=1, source_target_pairs={{1,0},{0,1},{3,2},{2,3},{5,4},{4,5},{7,6},{6,7},{9,8},{8,9},{11,10... | collective-permute-start | bytes 1179656 | tf_op jit(solution)/shard_map/ppermute | solution.py:266
  22.2 7.6 %collective-permute-start.5 = (bf16[2,128,768]{2,1,0:T(8,128)(2,1)S(1)}, bf16[2,128,768]{2,1,0:T(8,128)(2,1)}, u32[]{:S(2)}, u32[]{:S(2)}) collective-permute-start(bf16[2,128,768]{2,1,0:T(8,128)(2,1)S(1)} %collective-permute-done.1.middle_ref), channel_id=1, source_target_pairs={{1,0},{0,1},{3,2},{2,3},{5,4},{4,5},{7,6},{6,7},{9,8},{8,9},{11,10... | collective-permute-start | bytes 1179656 | tf_op jit(solution)/shard_map/ppermute | solution.py:266
  23.2 1.3 %copy-start = (bf16[768,768]{1,0:T(8,128)(2,1)S(1)}, bf16[768,768]{1,0:T(8,128)(2,1)}, u32[]{:S(2)}) copy-start(bf16[768,768]{1,0:T(8,128)(2,1)} %weight_ref.1) | copy-start | bytes 3538948
  24.5 0.9 copy-start.5
  25.4 4.3 %copy-start.2 = (bf16[2,128,768]{2,1,0:T(8,128)(2,1)S(1)}, bf16[2,128,768]{2,1,0:T(8,128)(2,1)}, u32[]{:S(2)}) copy-start(bf16[2,128,768]{2,1,0:T(8,128)(2,1)} %pack.1.own_ref.kv_ref) | copy-start | bytes 1179652
  27.0 12.0 %collective-permute-start.6 = (bf16[2,128,768]{2,1,0:T(8,128)(2,1)S(1)}, bf16[2,128,768]{2,1,0:T(8,128)(2,1)S(1)}, u32[]{:S(2)}, u32[]{:S(2)}) collective-permute-start(bf16[2,128,768]{2,1,0:T(8,128)(2,1)S(1)} %queries.1.query_ref.own_ref), channel_id=1, source_target_pairs={{15,0},{2,1},{1,2},{4,3},{3,4},{6,5},{5,6},{8,7},{7,8},{10,9},{9,1... | collective-permute-start | bytes 1179656 | tf_op jit(solution)/shard_map/ppermute | solution.py:280
  28.3 16.5 %collective-permute-start.7 = (bf16[2,128,768]{2,1,0:T(8,128)(2,1)S(1)}, bf16[2,128,768]{2,1,0:T(8,128)(2,1)S(1)}, u32[]{:S(2)}, u32[]{:S(2)}) collective-permute-start(bf16[2,128,768]{2,1,0:T(8,128)(2,1)S(1)} %queries.1.query_ref.own_ref), channel_id=1, source_target_pairs={{14,0},{3,1},{0,2},{5,3},{2,4},{7,5},{4,6},{9,7},{6,8},{11,9},{8,1... | collective-permute-start | bytes 1179656 | tf_op jit(solution)/shard_map/ppermute | solution.py:280
  28.4 10.6 %collective-permute-start.13 = (bf16[128,768]{1,0:T(8,128)(2,1)}, bf16[128,768]{1,0:T(8,128)(2,1)}, u32[]{:S(2)}, u32[]{:S(2)}) collective-permute-start(bf16[128,768]{1,0:T(8,128)(2,1)} %bitcast.1.g_ref.refs_2_), channel_id=1, source_target_pairs={{0,16},{16,0},{1,17},{17,1},{2,18},{18,2},{3,19},{19,3},{4,20},{20... | collective-permute-start | bytes 589832 | tf_op jit(solution)/shard_map/ppermute | solution.py:269
  35.2 9.6 %collective-permute-start.12 = (bf16[384,128]{1,0:T(8,128)(2,1)S(1)}, bf16[384,128]{1,0:T(8,128)(2,1)S(1)}, u32[]{:S(2)}, u32[]{:S(2)}) collective-permute-start(bf16[384,128]{1,0:T(8,128)(2,1)S(1)} %get-tuple-element.28), channel_id=1, source_target_pairs={{0,16},{16,0},{1,17},{17,1},{2,18},{18,2},{3,19},{19,3},{4,20},{20... | collective-permute-start | bytes 294920 | tf_op jit(solution)/shard_map/ppermute | solution.py:269
  44.9 0.9 copy-start.3
  47.2 3.3 %collective-permute-start.14 = (bf16[192,768]{1,0:T(8,128)(2,1)S(1)}, bf16[192,768]{1,0:T(8,128)(2,1)S(1)}, u32[]{:S(2)}, u32[]{:S(2)}) collective-permute-start(bf16[192,768]{1,0:T(8,128)(2,1)S(1)} %get-tuple-element.30), channel_id=1, source_target_pairs={{1,0},{0,1},{3,2},{2,3},{5,4},{4,5},{7,6},{6,7},{9,8},{8,9},{11,10... | collective-permute-start | bytes 884744 | tf_op jit(solution)/shard_map/ppermute | solution.py:266
  49.2 11.1 %collective-permute-start.8 = (bf16[2,128,768]{2,1,0:T(8,128)(2,1)S(1)}, bf16[2,128,768]{2,1,0:T(8,128)(2,1)S(1)}, u32[]{:S(2)}, u32[]{:S(2)}) collective-permute-start(bf16[2,128,768]{2,1,0:T(8,128)(2,1)S(1)} %queries.1.query_ref.own_ref), channel_id=1, source_target_pairs={{13,0},{4,1},{15,2},{6,3},{1,4},{8,5},{3,6},{10,7},{5,8},{12,9},{7... | collective-permute-start | bytes 1179656 | tf_op jit(solution)/shard_map/ppermute | solution.py:280
  50.5 9.8 %collective-permute-start.15 = (bf16[96,768]{1,0:T(8,128)(2,1)S(1)}, bf16[96,768]{1,0:T(8,128)(2,1)S(1)}, u32[]{:S(2)}, u32[]{:S(2)}) collective-permute-start(bf16[96,768]{1,0:T(8,128)(2,1)S(1)} %get-tuple-element.32), channel_id=1, source_target_pairs={{2,0},{3,1},{0,2},{1,3},{6,4},{7,5},{4,6},{5,7},{10,8},{11,9},{8,1... | collective-permute-start | bytes 442376 | tf_op jit(solution)/shard_map/ppermute | solution.py:266
  50.9 40.8 %collective-permute-start.9 = (bf16[2,128,768]{2,1,0:T(8,128)(2,1)S(1)}, bf16[2,128,768]{2,1,0:T(8,128)(2,1)S(1)}, u32[]{:S(2)}, u32[]{:S(2)}) collective-permute-start(bf16[2,128,768]{2,1,0:T(8,128)(2,1)S(1)} %queries.1.query_ref.own_ref), channel_id=1, source_target_pairs={{1,0},{0,1},{3,2},{2,3},{5,4},{4,5},{7,6},{6,7},{9,8},{8,9},{11,10... | collective-permute-start | bytes 1179656 | tf_op jit(solution)/shard_map/ppermute | solution.py:266
  53.3 38.4 %collective-permute-start.10 = (bf16[2,128,768]{2,1,0:T(8,128)(2,1)S(1)}, bf16[2,128,768]{2,1,0:T(8,128)(2,1)S(1)}, u32[]{:S(2)}, u32[]{:S(2)}) collective-permute-start(bf16[2,128,768]{2,1,0:T(8,128)(2,1)S(1)} %collective-permute-done.6.near_ref.refs_5_), channel_id=1, source_target_pairs={{1,0},{0,1},{3,2},{2,3},{5,4},{4,5},{7,6},{6,7},{9,8},{8,9},{11,10... | collective-permute-start | bytes 1179656 | tf_op jit(solution)/shard_map/ppermute | solution.py:266
  53.3 38.4 %collective-permute-start.11 = (bf16[2,128,768]{2,1,0:T(8,128)(2,1)S(1)}, bf16[2,128,768]{2,1,0:T(8,128)(2,1)S(1)}, u32[]{:S(2)}, u32[]{:S(2)}) collective-permute-start(bf16[2,128,768]{2,1,0:T(8,128)(2,1)S(1)} %collective-permute-done.7.middle_ref.refs_6_), channel_id=1, source_target_pairs={{1,0},{0,1},{3,2},{2,3},{5,4},{4,5},{7,6},{6,7},{9,8},{8,9},{11,10... | collective-permute-start | bytes 1179656 | tf_op jit(solution)/shard_map/ppermute | solution.py:266
  60.4 20.1 %collective-permute-start.16 = (bf16[48,768]{1,0:T(8,128)(2,1)S(1)}, bf16[48,768]{1,0:T(8,128)(2,1)S(1)}, u32[]{:S(2)}, u32[]{:S(2)}) collective-permute-start(bf16[48,768]{1,0:T(8,128)(2,1)S(1)} %get-tuple-element.34), channel_id=1, source_target_pairs={{4,0},{5,1},{6,2},{7,3},{0,4},{1,5},{2,6},{3,7},{12,8},{13,9},{14,... | collective-permute-start | bytes 221192 | tf_op jit(solution)/shard_map/ppermute | solution.py:266
  80.5 5.0 %collective-permute-start.17 = (bf16[48,768]{1,0:T(8,128)(2,1)S(1)}, bf16[48,768]{1,0:T(8,128)(2,1)S(1)}, u32[]{:S(2)}, u32[]{:S(2)}) collective-permute-start(bf16[48,768]{1,0:T(8,128)(2,1)S(1)} %add.2.part_ref), channel_id=1, source_target_pairs={{8,0},{9,1},{10,2},{11,3},{12,4},{13,5},{14,6},{15,7},{0,8},{1,9},... | collective-permute-start | bytes 221192 | tf_op jit(solution)/shard_map/ppermute | solution.py:266
  85.5 3.3 %collective-permute-start.18 = (bf16[48,768]{1,0:T(8,128)(2,1)S(1)}, bf16[48,768]{1,0:T(8,128)(2,1)S(1)}, u32[]{:S(2)}, u32[]{:S(2)}) collective-permute-start(bf16[48,768]{1,0:T(8,128)(2,1)S(1)} %add.3.mine_ref), channel_id=1, source_target_pairs={{4,0},{5,1},{6,2},{7,3},{0,4},{1,5},{2,6},{3,7},{12,8},{13,9},{14,... | collective-permute-start | bytes 221192 | tf_op jit(solution)/shard_map/ppermute | solution.py:266
  88.8 14.0 %copy-start.1 = (bf16[768,768]{1,0:T(8,128)(2,1)S(1)}, bf16[768,768]{1,0:T(8,128)(2,1)}, u32[]{:S(2)}) copy-start(bf16[768,768]{1,0:T(8,128)(2,1)} %weight_ref.1) | copy-start | bytes 3538948
  88.8 10.5 %collective-permute-start.19 = (bf16[96,768]{1,0:T(8,128)(2,1)S(1)}, bf16[96,768]{1,0:T(8,128)(2,1)S(1)}, u32[]{:S(2)}, u32[]{:S(2)}) collective-permute-start(bf16[96,768]{1,0:T(8,128)(2,1)S(1)} %join.3.refs_0_), channel_id=1, source_target_pairs={{2,0},{3,1},{0,2},{1,3},{6,4},{7,5},{4,6},{5,7},{10,8},{11,9},{8,1... | collective-permute-start | bytes 442376 | tf_op jit(solution)/shard_map/ppermute | solution.py:266
  99.3 0.9 copy-start.4
  100.3 3.7 %collective-permute-start.20 = (bf16[192,768]{1,0:T(8,128)(2,1)S(1)}, bf16[192,768]{1,0:T(8,128)(2,1)S(1)}, u32[]{:S(2)}, u32[]{:S(2)}) collective-permute-start(bf16[192,768]{1,0:T(8,128)(2,1)S(1)} %join.4.mine_ref), channel_id=1, source_target_pairs={{1,0},{0,1},{3,2},{2,3},{5,4},{4,5},{7,6},{6,7},{9,8},{8,9},{11,10... | collective-permute-start | bytes 884744 | tf_op jit(solution)/shard_map/ppermute | solution.py:266

commit v4 on v3

--- a/solution.py
+++ b/solution.py
@@ -36,14 +36,15 @@
     kernel(*refs[:first], *refs[first + count :])
 
 
-def call(kernel, ins, outs, args, scratch=(), limit=8, name=None, after=()):
+def call(kernel, ins, outs, args, scratch=(), limit=8, name=None, after=(), place=None, alias={}):
     ins, args = [*ins, *[ANY] * len(after)], (*args, *after)
     if after:
         kernel = functools.partial(skip_refs, kernel, len(args) - len(after), len(after))
     return pl.pallas_call(
         kernel,
         in_specs=ins,
-        out_specs=[VMEM] * len(outs),
+        out_specs=place or [VMEM] * len(outs),
+        input_output_aliases=alias,
         out_shape=outs,
         scratch_shapes=list(scratch),
         compiler_params=pltpu.CompilerParams(vmem_limit_bytes=limit * MIB),
@@ -62,7 +63,8 @@
         copy.wait()
 
 
-def query_kernel(q_ref, g_ref, weight_ref, out_ref):
+def query_kernel(q_ref, g_ref, weight_ref, out_ref, copy_ref):
+    copy_ref[...] = g_ref[...]
     out_ref[0] = q_ref[...]
     out_ref[1] = dot(g_ref[...], weight_ref[...], NT).astype(bf16)
 
@@ -98,7 +100,7 @@
 def forward_kernel(
     ids_ref, count_ref, query_ref, own_ref, near_ref, middle_ref, far_ref, sib_ref, sib_near_ref,
     sib_middle_ref,
-    mixed_ref, mine_ref, to_win_ref, stats_ref, probs_ref, keys, values,
+    mixed_ref, mine_ref, to_win_ref, stats_ref, dead_ref, probs_ref, keys, values,
     q_wide, raw,
     *, station_count,
 ):
@@ -112,6 +114,8 @@
     for j, offset in enumerate(offsets_of(me)):
         station = lax.rem(me + offset + station_count, station_count)
         live.append(listed(ids_ref, count_ref, me, station) if j else None)
+        reads = listed(ids_ref, count_ref, station, me) if j else jnp.int32(1)
+        dead_ref[j : j + 1] = jnp.where(reads > 0, 0.0, -neg_big) * jnp.ones((1, span), f32)
         keys[j * span : (j + 1) * span] = parts[j][0]
         values[j * span : (j + 1) * span] = parts[j][1]
     for group in range(HEADS // GROUP):
@@ -152,7 +156,10 @@
         ref[...] = mixed_ref[pl.ds(start, half)]
 
 
-def query_grad_kernel(query_ref, stats_ref, keys, values, probs_ref, dq_ref, g_wide, grads_half):
+def query_grad_kernel(
+    query_ref, stats_ref, keys, values, probs_ref, dq_ref, token_ref, g_wide, grads_half
+):
+    token_ref[...] = jnp.zeros_like(token_ref)
     span, width = query_ref.shape[1:]
     head_width = width // HEADS
     lanes = GROUP * head_width
@@ -170,47 +177,47 @@
         dq_ref[:, cols] = (pick(wide, span, head_width).T * scale).astype(bf16)
 
 
-def key_grad_kernel(
-    ids_ref, count_ref, stats_ref, kv_ref, own_ref, near_ref, middle_ref, far_ref, sib_ref,
-    sib_near_ref, sib_middle_ref,
-    dk_ref, dv_ref,
-    queries, grads, k_wide, v_wide, stats, probs_half, grads_half,
-    *, station_count,
-):
+def key_grad_kernel(group, kv_ref, dead_ref, *refs):
+    queries_in, stats_in, refs = refs[:SLOTS], refs[SLOTS : 2 * SLOTS], refs[2 * SLOTS :]
+    if group:
+        refs = refs[2:]
+    dk_ref, dv_ref, token_ref, queries, grads, k_wide, v_wide, stats, probs_half, grads_half, out, sems = refs
     span, width = kv_ref.shape[1:]
     head_width = width // HEADS
     lanes = GROUP * head_width
     scale = 1.0 / math.sqrt(head_width)
-    me = lax.axis_index("station")
-    parts = (own_ref, near_ref, middle_ref, far_ref, sib_ref, sib_near_ref, sib_middle_ref)
-    live = []
-    for j, offset in enumerate(offsets_of(me)):
-        station = lax.rem(me + offset + station_count, station_count)
-        live.append(listed(ids_ref, count_ref, station, me) if j else None)
-        queries[j * span : (j + 1) * span] = parts[j][0]
-        grads[j * span : (j + 1) * span] = parts[j][1]
-        stats[j] = stats_ref[station].T
-    for group in range(HEADS // GROUP):
-        cols = slice(group * lanes, (group + 1) * lanes)
-        widen(kv_ref[0, :, cols] * bf16(scale), k_wide)
-        widen(kv_ref[1, :, cols], v_wide)
-        for j in range(SLOTS):
-            rows = slice(j * span, (j + 1) * span)
-            scores = dot(queries[rows, cols], k_wide[...], NT)
-            back = dot(grads[rows, cols], v_wide[...], NT)
-            for h in range(GROUP):
-                head = group * GROUP + h
-                at = slice(h * span, (h + 1) * span)
-                prob = jnp.exp(scores[:, at] - stats[j, :, head : head + 1])
-                if j:
-                    prob = jnp.where(live[j] > 0, prob, 0.0)
-                probs_half[rows, at] = prob.astype(bf16)
-                delta = stats[j, :, HEADS + head : HEADS + head + 1]
-                grads_half[rows, at] = (prob * (back[:, at] - delta)).astype(bf16)
-        wide = dot(queries[:, cols], grads_half[...], TN)
-        dk_ref[:, cols] = (pick(wide, span, head_width).T * scale).astype(bf16)
-        wide = dot(grads[:, cols], probs_half[...], TN)
-        dv_ref[:, cols] = pick(wide, span, head_width).T.astype(bf16)
+    cols = slice(group * lanes, (group + 1) * lanes)
+    widen(kv_ref[0, :, cols] * bf16(scale), k_wide)
+    widen(kv_ref[1, :, cols], v_wide)
+    for j in range(SLOTS):
+        rows = slice(j * span, (j + 1) * span)
+        queries[rows] = queries_in[j][0, :, cols]
+        grads[rows] = queries_in[j][1, :, cols]
+        stats[j, :HEADS] = stats_in[j][:HEADS] + dead_ref[j : j + 1]
+        stats[j, HEADS:] = stats_in[j][HEADS:]
+        columns = stats[j].T
+        scores = dot(queries[rows], k_wide[...], NT)
+        back = dot(grads[rows], v_wide[...], NT)
+        for h in range(GROUP):
+            head = group * GROUP + h
+            at = slice(h * span, (h + 1) * span)
+            prob = jnp.exp(scores[:, at] - columns[:, head : head + 1])
+            probs_half[rows, at] = prob.astype(bf16)
+            delta = columns[:, HEADS + head : HEADS + head + 1]
+            grads_half[rows, at] = (prob * (back[:, at] - delta)).astype(bf16)
+    wide = dot(queries[...], grads_half[...], TN)
+    out[0] = (pick(wide, span, head_width).T * scale).astype(bf16)
+    wide = dot(grads[...], probs_half[...], TN)
+    out[1] = pick(wide, span, head_width).T.astype(bf16)
+    copies = [
+        pltpu.make_async_copy(out.at[n], ref.at[:, cols], sems.at[n])
+        for n, ref in enumerate((dk_ref, dv_ref))
+    ]
+    for copy in copies:
+        copy.start()
+    token_ref[...] = jnp.zeros_like(token_ref)
+    for copy in copies:
+        copy.wait()
 
 
 def sides(stride, half):
@@ -276,25 +283,35 @@
     pair = shape_of(2, span, width)
     (kv,) = call(pack_kernel, [ANY, ANY], [pair], (k, v), [dma((2,))], limit=56, name="pack")
 
+    def to_reach(value):
+        return [lax.ppermute(value, "station", routes(n)) for n in (1, 2, 3)]
+
     def spread(value):
-        near, middle, far = (lax.ppermute(value, "station", routes(n)) for n in (1, 2, 3))
+        near, middle, far = to_reach(value)
         return value, near, middle, far, swap(value, 1), swap(near, 1), swap(middle, 1)
 
-    kv_all = spread(kv)
+    near, middle, far = to_reach(kv)
+    sib = swap(kv, 1)
     g_win = other_window(g) if windows == 2 else g
-    (qg,) = call(query_kernel, [VMEM] * 3, [pair], (q, g, out_weight), name="queries")
-    qg_all = spread(qg)
+    qg, g_near = call(
+        query_kernel, [VMEM] * 3, [pair, shape_of(span, width)], (q, g, out_weight), name="queries"
+    )
+    near, qg_later = lax.optimization_barrier((near, qg))
+    kv_all = kv, near, middle, far, sib, swap(near, 1), swap(middle, 1)
+    qg_all = spread(qg_later)
 
     lanes = width // HEADS * GROUP
     groups = HEADS // GROUP
     half = width // 2
     half_shape = shape_of(half, span)
-    mixed, mine, to_win, stats, probs, keys, values = call(
+    token_shape = shape_of(8, 128, dtype=f32)
+    mixed, mine, to_win, stats, dead, probs, keys, values = call(
         functools.partial(forward_kernel, station_count=stations),
         [SMEM] * 2 + [VMEM] * 8,
         [
             shape_of(width, span), half_shape, half_shape,
             shape_of(2 * HEADS, span, dtype=f32),
+            shape_of(SLOTS, span, dtype=f32),
             shape_of(groups, SLOTS * span, GROUP * span),
             shape_of(SLOTS * span, width),
             shape_of(SLOTS * span, width),
@@ -303,32 +320,41 @@
         [pltpu.VMEM((GROUP * span, lanes), bf16), pltpu.VMEM((SLOTS * span, GROUP * span), f32)],
         limit=20, name="forward",
     )
-    all_stats = lax.all_gather(stats, "station", axis=0)
-    (grad_query,) = call(
+    stats_in = spread(stats)
+    grad_query, query_token = call(
         query_grad_kernel,
         [VMEM] * 5,
-        [shape_of(span, width)],
+        [shape_of(span, width), token_shape],
         (qg, stats, keys, values, probs),
         [pltpu.VMEM((GROUP * span, lanes), bf16), pltpu.VMEM((SLOTS * span, GROUP * span), bf16)],
         limit=20, name="query_grad",
     )
 
-    grad_key, grad_value = call(
-        functools.partial(key_grad_kernel, station_count=stations),
-        [SMEM] * 2 + [VMEM] * 9,
-        [shape_of(span, width)] * 2,
-        (partner_ids, partner_count, all_stats, kv, *qg_all),
-        [
-            pltpu.VMEM((SLOTS * span, width), bf16),
-            pltpu.VMEM((SLOTS * span, width), bf16),
-            pltpu.VMEM((GROUP * span, lanes), bf16),
-            pltpu.VMEM((GROUP * span, lanes), bf16),
-            pltpu.VMEM((SLOTS, span, 2 * HEADS), f32),
-            pltpu.VMEM((SLOTS * span, GROUP * span), bf16),
-            pltpu.VMEM((SLOTS * span, GROUP * span), bf16),
-        ],
-        limit=20, name="key_grad",
-    )
+    grads_out, key_grads = (), []
+    for group in range(groups):
+        *grads_out, token = call(
+            functools.partial(key_grad_kernel, group),
+            [VMEM] * (2 + 2 * SLOTS) + [ANY] * len(grads_out),
+            [shape_of(span, width)] * 2 + [token_shape],
+            (kv, dead, *qg_all, *stats_in, *grads_out),
+            [
+                pltpu.VMEM((SLOTS * span, lanes), bf16),
+                pltpu.VMEM((SLOTS * span, lanes), bf16),
+                pltpu.VMEM((GROUP * span, lanes), bf16),
+                pltpu.VMEM((GROUP * span, lanes), bf16),
+                pltpu.VMEM((SLOTS, 2 * HEADS, span), f32),
+                pltpu.VMEM((SLOTS * span, GROUP * span), bf16),
+                pltpu.VMEM((SLOTS * span, GROUP * span), bf16),
+                pltpu.VMEM((2, span, lanes), bf16),
+                dma((2,)),
+            ],
+            limit=20, name="key_grad", place=[ANY, ANY, VMEM],
+            alias={2 + 2 * SLOTS + n: n for n in range(len(grads_out))},
+        )
+        key_grads.append(token)
+    grad_key, grad_value = grads_out
+
+    layer_output = lax.dot_general(mixed, out_weight, TN, preferred_element_type=f32).astype(bf16)
 
     if windows == 2:
         rows = half // 2
@@ -336,9 +362,9 @@
             functools.partial(weight_kernel, 1),
             [VMEM] * 4,
             [shape_of(rows, width), shape_of(rows, width, dtype=f32)],
-            (mine, other_window(to_win), g, g_win),
+            (mine, other_window(to_win), g_near, g_win),
             [pltpu.VMEM((half, 2 * span), bf16), pltpu.VMEM((2 * span, width), bf16)],
-            name="weight", after=(grad_query, *qg_all[1:3]),
+            name="weight", after=(query_token, *qg_all[1:3]),
         )
     else:
         whole = lax.dot_general(mixed, g, NN, preferred_element_type=f32).astype(bf16)
@@ -357,7 +383,7 @@
             [VMEM, VMEM],
             [shape_of(rows, width), shape_of(rows, width, dtype=f32)],
             (part, got),
-            name="split", after=qg_all[3:4] if stride == 4 else (),
+            name="split", after={2: stats_in[1::3], 4: (stats_in[2], qg_all[3])}.get(stride, ()),
         )
         got = swap(send, stride)
         halved.append(stride)
@@ -367,9 +393,9 @@
         out = [shape_of(rows, width)]
         return call(round_kernel, [VMEM, VMEM], out, (part, got), name="add", after=after)[0]
 
-    total = add_round(part, got, (all_stats,))
+    total = add_round(part, got, stats_in[3:6:2])
     while stride < stations:
-        total = add_round(total, swap(total, stride))
+        total = add_round(total, swap(total, stride), key_grads[:1])
         stride *= 2
     scale = 1.0 / math.sqrt(span * windows * stations)
     for stride in reversed(halved):
@@ -379,10 +405,9 @@
             [VMEM, VMEM],
             [shape_of(2 * total.shape[0], width, dtype=f32 if last else bf16)],
             (total, swap(total, stride)),
-            name="join", after=(grad_key,) if stride == 2 else (),
+            name="join", after={4: key_grads[1:2], 2: key_grads[2:], 1: [layer_output]}.get(stride, ()),
         )
 
-    layer_output = lax.dot_general(mixed, out_weight, TN, preferred_element_type=f32).astype(bf16)
     shape = query_states.shape
     return (
         layer_output.reshape(shape),

time: 106 us -> 91.9 us (0.87)
  the two profiles are of different devices: /device:TPU:3 before, /device:TPU:0 now
where the time goes in v4:
time: 91.9 us; the launch traced here: 91.6 us
  waiting for transfers between devices  32.5 us (35%)
  starting transfers between devices  31.1 us (34%)
  Pallas kernels  23.8 us (26%)
  local copies, waits for them, and re-layouts  2.98 us (3%)
    ppermute x9, waiting for transfers between devices, to_reach(): return [lax.ppermute(value, 'station', routes(n)) for n in (1, 2, 3)]  23.9 us
    pallas_call x15, Pallas kernels, call(): pl.pallas_call(kernel, in_specs=ins, out_specs=place or [VMEM] * len(outs...  23.8 us
    ppermute x9, starting transfers between devices, to_reach(): return [lax.ppermute(value, 'station', routes(n)) for n in (1, 2, 3)]  19.2 us
    ppermute x16, starting transfers between devices, swap(): lax.ppermute(value, 'station', [(s ^ stride, s) for s in range(stations)])  9.76 us
    ppermute x16, waiting for transfers between devices, swap(): lax.ppermute(value, 'station', [(s ^ stride, s) for s in range(stations)])  8.58 us
    unnamed x19, local copies, waits for them, and re-layouts  2.98 us
    ppermute x2, starting transfers between devices, other_window(): return lax.ppermute(value, 'dp', [(0, 1), (1, 0)])  2.16 us
  transfers between devices with their start and end apart: 27, of which 12 were waited for; matrix products, arithmetic and copies ran while one was open for 0% of the time, Pallas kernels for 21%

profile of v4, /device:TPU:0, one launch (start us, length us, event | category | flops | bytes accessed | tf_op | source)
XLA Modules:
  0.0 91.6 jit_solution(18392654804385537885)
XLA Ops:
  0.7 1.8 %pack.1.own_ref.kv_ref = bf16[2,128,768]{2,1,0:T(8,128)(2,1)} custom-call(bf16[128,768]{1,0:T(8,128)(2,1)} %bitcast.14, bf16[128,768]{1,0:T(8,128)(2,1)} %bitcast.15), custom_call_target="tpu_custom_call" | custom-call | flops 1 | bytes 1 | tf_op jit(solution)/shard_map/pack/pallas_call | solution.py:43
  2.5 0.0 copy-start
  2.5 5.5 %collective-permute-start = (bf16[2,128,768]{2,1,0:T(8,128)(2,1)}, bf16[2,128,768]{2,1,0:T(8,128)(2,1)S(1)}, u32[]{:S(2)}, u32[]{:S(2)}) collective-permute-start(bf16[2,128,768]{2,1,0:T(8,128)(2,1)} %pack.1.own_ref.kv_ref), channel_id=1, source_target_pairs={{15,0},{2,1},{1,2},{4,3},{3,4},{6,5},{5,6},{8,7},{7,8},{10,9},{9,1... | collective-permute-start | bytes 1179656 | tf_op jit(solution)/shard_map/ppermute | solution.py:287
  8.0 2.0 %collective-permute-start.2 = (bf16[2,128,768]{2,1,0:T(8,128)(2,1)}, bf16[2,128,768]{2,1,0:T(8,128)(2,1)S(1)}, u32[]{:S(2)}, u32[]{:S(2)}) collective-permute-start(bf16[2,128,768]{2,1,0:T(8,128)(2,1)} %pack.1.own_ref.kv_ref), channel_id=1, source_target_pairs={{13,0},{4,1},{15,2},{6,3},{1,4},{8,5},{3,6},{10,7},{5,8},{12,9},{7... | collective-permute-start | bytes 1179656 | tf_op jit(solution)/shard_map/ppermute | solution.py:287
  10.0 1.3 %copy-done.1 = bf16[768,768]{1,0:T(8,128)(2,1)S(1)} copy-done((bf16[768,768]{1,0:T(8,128)(2,1)S(1)}, bf16[768,768]{1,0:T(8,128)(2,1)}, u32[]{:S(2)}) %copy-start.1) | copy-done | bytes 1179672
  11.2 0.9 %copy-done.4 = bf16[1,1,128,768]{3,2,1,0:T(8,128)(2,1)S(1)} copy-done((bf16[1,1,128,768]{3,2,1,0:T(8,128)(2,1)S(1)}, bf16[1,1,128,768]{3,2,1,0:T(8,128)(2,1)}, u32[]{:S(2)}) %copy-start.4) | copy-done | bytes 196632
  12.1 1.5 %queries.1 = (bf16[2,128,768]{2,1,0:T(8,128)(2,1)S(1)}, bf16[128,768]{1,0:T(8,128)(2,1)S(1)}) custom-call(bf16[128,768]{1,0:T(8,128)(2,1)S(1)} %bitcast.11, bf16[128,768]{1,0:T(8,128)(2,1)} %bitcast.1.g_ref, bf16[768,768]{1,0:T(8,128)(2,1)S(1)} %copy-done.1), custom_call_target="tpu_custom_call" | custom-call | flops 1 | bytes 1 | tf_op jit(solution)/shard_map/queries/pallas_call | solution.py:43
  13.7 0.7 copy-done.5
  14.3 3.4 %collective-permute-done.near_ref = bf16[2,128,768]{2,1,0:T(8,128)(2,1)S(1)} collective-permute-done((bf16[2,128,768]{2,1,0:T(8,128)(2,1)}, bf16[2,128,768]{2,1,0:T(8,128)(2,1)S(1)}, u32[]{:S(2)}, u32[]{:S(2)}) %collective-permute-start) | collective-permute-done | bytes 393248 | tf_op jit(solution)/shard_map/ppermute | solution.py:287
  17.7 5.3 %collective-permute-start.4 = (bf16[2,128,768]{2,1,0:T(8,128)(2,1)S(1)}, bf16[2,128,768]{2,1,0:T(8,128)(2,1)S(1)}, u32[]{:S(2)}, u32[]{:S(2)}) collective-permute-start(bf16[2,128,768]{2,1,0:T(8,128)(2,1)S(1)} %collective-permute-done.near_ref), channel_id=1, source_target_pairs={{1,0},{0,1},{3,2},{2,3},{5,4},{4,5},{7,6},{6,7},{9,8},{8,9},{11,10... | collective-permute-start | bytes 1179656 | tf_op jit(solution)/shard_map/ppermute | solution.py:273
  23.0 0.1 collective-permute-done.1.middle_ref
  23.1 1.0 %collective-permute-start.5 = (bf16[2,128,768]{2,1,0:T(8,128)(2,1)S(1)}, bf16[2,128,768]{2,1,0:T(8,128)(2,1)}, u32[]{:S(2)}, u32[]{:S(2)}) collective-permute-start(bf16[2,128,768]{2,1,0:T(8,128)(2,1)S(1)} %collective-permute-done.1.middle_ref), channel_id=1, source_target_pairs={{1,0},{0,1},{3,2},{2,3},{5,4},{4,5},{7,6},{6,7},{9,8},{8,9},{11,10... | collective-permute-start | bytes 1179656 | tf_op jit(solution)/shard_map/ppermute | solution.py:273
  24.2 4.5 %collective-permute-start.6 = (bf16[2,128,768]{2,1,0:T(8,128)(2,1)S(1)}, bf16[2,128,768]{2,1,0:T(8,128)(2,1)S(1)}, u32[]{:S(2)}, u32[]{:S(2)}) collective-permute-start(bf16[2,128,768]{2,1,0:T(8,128)(2,1)S(1)} %get-tuple-element.43.query_ref.refs_0_), channel_id=1, source_target_pairs={{15,0},{2,1},{1,2},{4,3},{3,4},{6,5},{5,6},{8,7},{7,8},{10,9},{9,1... | collective-permute-start | bytes 1179656 | tf_op jit(solution)/shard_map/ppermute | solution.py:287
  28.7 1.6 %collective-permute-start.19 = (bf16[128,768]{1,0:T(8,128)(2,1)}, bf16[128,768]{1,0:T(8,128)(2,1)}, u32[]{:S(2)}, u32[]{:S(2)}) collective-permute-start(bf16[128,768]{1,0:T(8,128)(2,1)} %bitcast.1.g_ref), channel_id=1, source_target_pairs={{0,16},{16,0},{1,17},{17,1},{2,18},{18,2},{3,19},{19,3},{4,20},{20... | collective-permute-start | bytes 589832 | tf_op jit(solution)/shard_map/ppermute | solution.py:276
  30.3 0.1 copy.16.ids_ref
  30.4 5.5 %forward.1 = (bf16[768,128]{1,0:T(8,128)(2,1)S(1)}, bf16[384,128]{1,0:T(8,128)(2,1)S(1)}, bf16[384,128]{1,0:T(8,128)(2,1)S(1)}, f32[24,128]{1,0:T(8,128)S(1)}, f...) custom-call(s32[16,6]{1,0:T(8,128)S(1)} %copy.16.ids_ref, ...), custom_call_target="tpu_custom_call" | custom-call | flops 1 | bytes 1 | tf_op jit(solution)/shard_map/forward/pallas_call | solution.py:43
  35.9 0.6 collective-permute-start.18
  36.5 3.5 %query_grad.1 = (bf16[128,768]{1,0:T(8,128)(2,1)}, f32[8,128]{1,0:T(8,128)S(1)}) custom-call(bf16[2,128,768]{2,1,0:T(8,128)(2,1)S(1)} %get-tuple-element.43.query_ref.refs_0_, f32[24,128]{1,0:T(8,128)S(1)} %get-tuple-element.37.stats_ref.refs_7_, bf16[896,768]{1,0:T(8,128)(2,1)S(1)} %get-tuple-element.38.keys, ...), custom_call_target="tpu_custom_call" | custom-call | flops 1 | bytes 1 | tf_op jit(solution)/shard_map/query_grad/pallas_call | solution.py:43
  40.0 2.9 %collective-permute-done.7.refs_2_.refs_6_ = bf16[2,128,768]{2,1,0:T(8,128)(2,1)S(1)} collective-permute-done((bf16[2,128,768]{2,1,0:T(8,128)(2,1)S(1)}, bf16[2,128,768]{2,1,0:T(8,128)(2,1)S(1)}, u32[]{:S(2)}, u32[]{:S(2)}) %collective-permute-start.7) | collective-permute-done | bytes 393248 | tf_op jit(solution)/shard_map/ppermute | solution.py:287
  42.9 1.3 %weight.1 = (bf16[192,768]{1,0:T(8,128)(2,1)S(1)}, f32[192,768]{1,0:T(8,128)S(1)}) custom-call(bf16[384,128]{1,0:T(8,128)(2,1)S(1)} %get-tuple-element.50.refs_0_, bf16[384,128]{1,0:T(8,128)(2,1)S(1)} %collective-permute-done.18.refs_1_, bf16[128,768]{1,0:T(8,128)(2,1)S(1)} %copy-done.6, bf16[128,768]{1,0:T(8,128)(2,1)} %collective-permute-done.19.refs_3_, ...), custom_call_target="tpu_custom_call" | custom-call | flops 1 | bytes 1 | tf_op jit(solution)/shard_map/weight/pallas_call | solution.py:43
  44.1 1.2 %collective-permute-start.20 = (bf16[192,768]{1,0:T(8,128)(2,1)S(1)}, bf16[192,768]{1,0:T(8,128)(2,1)S(1)}, u32[]{:S(2)}, u32[]{:S(2)}) collective-permute-start(bf16[192,768]{1,0:T(8,128)(2,1)S(1)} %get-tuple-element.55), channel_id=1, source_target_pairs={{1,0},{0,1},{3,2},{2,3},{5,4},{4,5},{7,6},{6,7},{9,8},{8,9},{11,10... | collective-permute-start | bytes 884744 | tf_op jit(solution)/shard_map/ppermute | solution.py:273
  45.4 3.3 %collective-permute-start.8 = (bf16[2,128,768]{2,1,0:T(8,128)(2,1)S(1)}, bf16[2,128,768]{2,1,0:T(8,128)(2,1)S(1)}, u32[]{:S(2)}, u32[]{:S(2)}) collective-permute-start(bf16[2,128,768]{2,1,0:T(8,128)(2,1)S(1)} %get-tuple-element.43.query_ref.refs_0_), channel_id=1, source_target_pairs={{13,0},{4,1},{15,2},{6,3},{1,4},{8,5},{3,6},{10,7},{5,8},{12,9},{7... | collective-permute-start | bytes 1179656 | tf_op jit(solution)/shard_map/ppermute | solution.py:287
  48.7 1.2 %collective-permute-start.12 = (f32[24,128]{1,0:T(8,128)S(1)}, f32[24,128]{1,0:T(8,128)S(1)}, u32[]{:S(2)}, u32[]{:S(2)}) collective-permute-start(f32[24,128]{1,0:T(8,128)S(1)} %get-tuple-element.37.stats_ref.refs_7_), channel_id=1, source_target_pairs={{15,0},{2,1},{1,2},{4,3},{3,4},{6,5},{5,6},{8,7},{7,8},{10,9},{9,1... | collective-permute-start | bytes 36872 | tf_op jit(solution)/shard_map/ppermute | solution.py:287
  49.9 0.7 collective-permute-start.15
  50.5 8.5 %collective-permute-done.12.refs_8_.refs_2_ = f32[24,128]{1,0:T(8,128)S(1)} collective-permute-done((f32[24,128]{1,0:T(8,128)S(1)}, f32[24,128]{1,0:T(8,128)S(1)}, u32[]{:S(2)}, u32[]{:S(2)}) %collective-permute-start.12) | collective-permute-done | bytes 12320 | tf_op jit(solution)/shard_map/ppermute | solution.py:287
  59.1 0.5 collective-permute-start.11
  59.6 0.1 collective-permute-start.21
  59.7 2.0 %collective-permute-start.13 = (f32[24,128]{1,0:T(8,128)S(1)}, f32[24,128]{1,0:T(8,128)S(1)}, u32[]{:S(2)}, u32[]{:S(2)}) collective-permute-start(f32[24,128]{1,0:T(8,128)S(1)} %get-tuple-element.37.stats_ref.refs_7_), channel_id=1, source_target_pairs={{14,0},{3,1},{0,2},{5,3},{2,4},{7,5},{4,6},{9,7},{6,8},{11,9},{8,1... | collective-permute-start | bytes 36872 | tf_op jit(solution)/shard_map/ppermute | solution.py:287
  61.7 4.6 %collective-permute-done.13.refs_9_.refs_2_ = f32[24,128]{1,0:T(8,128)S(1)} collective-permute-done((f32[24,128]{1,0:T(8,128)S(1)}, f32[24,128]{1,0:T(8,128)S(1)}, u32[]{:S(2)}, u32[]{:S(2)}) %collective-permute-start.13) | collective-permute-done | bytes 12320 | tf_op jit(solution)/shard_map/ppermute | solution.py:287
  66.4 0.1 collective-permute-start.22
  66.5 0.8 collective-permute-start.14
  67.2 4.2 %collective-permute-done.14.refs_10_.refs_2_ = f32[24,128]{1,0:T(8,128)S(1)} collective-permute-done((f32[24,128]{1,0:T(8,128)S(1)}, f32[24,128]{1,0:T(8,128)S(1)}, u32[]{:S(2)}, u32[]{:S(2)}) %collective-permute-start.14) | collective-permute-done | bytes 12320 | tf_op jit(solution)/shard_map/ppermute | solution.py:287
  71.5 1.2 %collective-permute-done.16.refs_12_.refs_3_ = f32[24,128]{1,0:T(8,128)S(1)} collective-permute-done((f32[24,128]{1,0:T(8,128)S(1)}, f32[24,128]{1,0:T(8,128)S(1)}, u32[]{:S(2)}, u32[]{:S(2)}) %collective-permute-start.16) | collective-permute-done | bytes 12320 | tf_op jit(solution)/shard_map/ppermute | solution.py:273
  72.7 0.4 collective-permute-start.23
  73.1 1.2 %collective-permute-done.17.refs_13_ = f32[24,128]{1,0:T(8,128)S(1)} collective-permute-done((f32[24,128]{1,0:T(8,128)S(1)}, f32[24,128]{1,0:T(8,128)S(1)}, u32[]{:S(2)}, u32[]{:S(2)}) %collective-permute-start.17) | collective-permute-done | bytes 12320 | tf_op jit(solution)/shard_map/ppermute | solution.py:273
  74.3 3.0 %key_grad.3 = (bf16[128,768]{1,0:T(8,128)(2,1)}, bf16[128,768]{1,0:T(8,128)(2,1)}, f32[8,128]{1,0:T(8,128)S(1)}) custom-call(bf16[2,128,768]{2,1,0:T(8,128)(2,1)S(1)} %copy-done, f32[7,128]{1,0:T(8,128)S(1)} %get-tuple-element.42.dead_ref, bf16[2,128,768]{2,1,0:T(8,128)(2,1)S(1)} %get-tuple-element.43.query_ref.refs_0_, ...), custom_call_target="tpu_custom_call" | custom-call | flops 1 | bytes 1 | tf_op jit(solution)/shard_map/key_grad/pallas_call | solution.py:43
  77.3 1.8 %collective-permute-done.23.refs_1_ = bf16[48,768]{1,0:T(8,128)(2,1)S(1)} collective-permute-done((bf16[48,768]{1,0:T(8,128)(2,1)S(1)}, bf16[48,768]{1,0:T(8,128)(2,1)S(1)}, u32[]{:S(2)}, u32[]{:S(2)}) %collective-permute-start.23) | collective-permute-done | bytes 73760 | tf_op jit(solution)/shard_map/ppermute | solution.py:273
  79.2 0.1 collective-permute-start.24
  79.2 3.0 %key_grad.4 = (bf16[128,768]{1,0:T(8,128)(2,1)}, bf16[128,768]{1,0:T(8,128)(2,1)}, f32[8,128]{1,0:T(8,128)S(1)}) custom-call(bf16[2,128,768]{2,1,0:T(8,128)(2,1)S(1)} %copy-done, f32[7,128]{1,0:T(8,128)S(1)} %get-tuple-element.42.dead_ref, ...), custom_call_target="tpu_custom_call", output_to_operand_aliasing={{0}: (16, {}), {1}: (17, {})} | custom-call | flops 1 | bytes 1 | tf_op jit(solution)/shard_map/key_grad/pallas_call | solution.py:43
  82.3 1.3 %collective-permute-done.24.refs_1_ = bf16[48,768]{1,0:T(8,128)(2,1)S(1)} collective-permute-done((bf16[48,768]{1,0:T(8,128)(2,1)S(1)}, bf16[48,768]{1,0:T(8,128)(2,1)S(1)}, u32[]{:S(2)}, u32[]{:S(2)}) %collective-permute-start.24) | collective-permute-done | bytes 73760 | tf_op jit(solution)/shard_map/ppermute | solution.py:273
  83.6 0.3 collective-permute-start.25
  83.9 3.0 %key_grad.5 = (bf16[128,768]{1,0:T(8,128)(2,1)}, bf16[128,768]{1,0:T(8,128)(2,1)}, f32[8,128]{1,0:T(8,128)S(1)}) custom-call(bf16[2,128,768]{2,1,0:T(8,128)(2,1)S(1)} %copy-done, f32[7,128]{1,0:T(8,128)S(1)} %get-tuple-element.42.dead_ref, ...), custom_call_target="tpu_custom_call", output_to_operand_aliasing={{0}: (16, {}), {1}: (17, {})} | custom-call | flops 1 | bytes 1 | tf_op jit(solution)/shard_map/key_grad/pallas_call | solution.py:43
  86.9 1.9 %collective-permute-done.25.refs_1_ = bf16[96,768]{1,0:T(8,128)(2,1)S(1)} collective-permute-done((bf16[96,768]{1,0:T(8,128)(2,1)S(1)}, bf16[96,768]{1,0:T(8,128)(2,1)S(1)}, u32[]{:S(2)}, u32[]{:S(2)}) %collective-permute-start.25) | collective-permute-done | bytes 147488 | tf_op jit(solution)/shard_map/ppermute | solution.py:273
  88.9 0.1 collective-permute-start.26
  88.9 0.3 convolution_convert_fusion.refs_2_
  89.3 0.0 copy-start.3
  89.3 1.2 %collective-permute-done.26.refs_1_ = bf16[192,768]{1,0:T(8,128)(2,1)S(1)} collective-permute-done((bf16[192,768]{1,0:T(8,128)(2,1)S(1)}, bf16[192,768]{1,0:T(8,128)(2,1)S(1)}, u32[]{:S(2)}, u32[]{:S(2)}) %collective-permute-start.26) | collective-permute-done | bytes 294944 | tf_op jit(solution)/shard_map/ppermute | solution.py:273
  90.5 1.1 %join.5 = f32[384,768]{1,0:T(8,128)} custom-call(bf16[192,768]{1,0:T(8,128)(2,1)S(1)} %join.4.refs_0_, bf16[192,768]{1,0:T(8,128)(2,1)S(1)} %collective-permute-done.26.refs_1_, bf16[128,768]{1,0:T(8,128)(2,1)S(1)} %convolution_convert_fusion.refs_2_), custom_call_target="tpu_custom_call" | custom-call | flops 1 | bytes 1 | tf_op jit(solution)/shard_map/join/pallas_call | solution.py:43
  (41 shorter events, 0.3 us)
Async XLA Ops:
  0.6 29.6 %copy-start.8 = (s32[16,6]{0,1:T(8,128)S(1)}, s32[16,6]{0,1:T(8,128)}, u32[]{:S(2)}) copy-start(s32[16,6]{0,1:T(8,128)} %param.12) | copy-start | bytes 1156
  0.6 29.7 %copy-start.7 = (s32[16]{0:T(128)S(1)}, s32[16]{0:T(128)}, u32[]{:S(2)}) copy-start(s32[16]{0:T(128)} %count_ref.1) | copy-start | bytes 196
  2.5 27.9 %copy-start = (bf16[2,128,768]{2,1,0:T(8,128)(2,1)S(1)}, bf16[2,128,768]{2,1,0:T(8,128)(2,1)}, u32[]{:S(2)}) copy-start(bf16[2,128,768]{2,1,0:T(8,128)(2,1)} %pack.1.own_ref.kv_ref) | copy-start | bytes 1179652
  2.5 15.3 %collective-permute-start = (bf16[2,128,768]{2,1,0:T(8,128)(2,1)}, bf16[2,128,768]{2,1,0:T(8,128)(2,1)S(1)}, u32[]{:S(2)}, u32[]{:S(2)}) collective-permute-start(bf16[2,128,768]{2,1,0:T(8,128)(2,1)} %pack.1.own_ref.kv_ref), channel_id=1, source_target_pairs={{15,0},{2,1},{1,2},{4,3},{3,4},{6,5},{5,6},{8,7},{7,8},{10,9},{9,1... | collective-permute-start | bytes 1179656 | tf_op jit(solution)/shard_map/ppermute | solution.py:287
  7.9 15.2 %collective-permute-start.1 = (bf16[2,128,768]{2,1,0:T(8,128)(2,1)}, bf16[2,128,768]{2,1,0:T(8,128)(2,1)S(1)}, u32[]{:S(2)}, u32[]{:S(2)}) collective-permute-start(bf16[2,128,768]{2,1,0:T(8,128)(2,1)} %pack.1.own_ref.kv_ref), channel_id=1, source_target_pairs={{14,0},{3,1},{0,2},{5,3},{2,4},{7,5},{4,6},{9,7},{6,8},{11,9},{8,1... | collective-permute-start | bytes 1179656 | tf_op jit(solution)/shard_map/ppermute | solution.py:287
  8.0 20.7 %collective-permute-start.2 = (bf16[2,128,768]{2,1,0:T(8,128)(2,1)}, bf16[2,128,768]{2,1,0:T(8,128)(2,1)S(1)}, u32[]{:S(2)}, u32[]{:S(2)}) collective-permute-start(bf16[2,128,768]{2,1,0:T(8,128)(2,1)} %pack.1.own_ref.kv_ref), channel_id=1, source_target_pairs={{13,0},{4,1},{15,2},{6,3},{1,4},{8,5},{3,6},{10,7},{5,8},{12,9},{7... | collective-permute-start | bytes 1179656 | tf_op jit(solution)/shard_map/ppermute | solution.py:287
  9.9 18.7 %collective-permute-start.3 = (bf16[2,128,768]{2,1,0:T(8,128)(2,1)}, bf16[2,128,768]{2,1,0:T(8,128)(2,1)S(1)}, u32[]{:S(2)}, u32[]{:S(2)}) collective-permute-start(bf16[2,128,768]{2,1,0:T(8,128)(2,1)} %pack.1.own_ref.kv_ref), channel_id=1, source_target_pairs={{1,0},{0,1},{3,2},{2,3},{5,4},{4,5},{7,6},{6,7},{9,8},{8,9},{11,10... | collective-permute-start | bytes 1179656 | tf_op jit(solution)/shard_map/ppermute | solution.py:273
  9.9 1.3 %copy-start.1 = (bf16[768,768]{1,0:T(8,128)(2,1)S(1)}, bf16[768,768]{1,0:T(8,128)(2,1)}, u32[]{:S(2)}) copy-start(bf16[768,768]{1,0:T(8,128)(2,1)} %weight_ref.1) | copy-start | bytes 3538948
  11.2 0.9 %copy-start.4 = (bf16[1,1,128,768]{3,2,1,0:T(8,128)(2,1)S(1)}, bf16[1,1,128,768]{3,2,1,0:T(8,128)(2,1)}, u32[]{:S(2)}) copy-start(bf16[1,1,128,768]{3,2,1,0:T(8,128)(2,1)} %param.7) | copy-start | bytes 589828
  13.6 0.7 copy-start.5
  17.7 12.6 %collective-permute-start.4 = (bf16[2,128,768]{2,1,0:T(8,128)(2,1)S(1)}, bf16[2,128,768]{2,1,0:T(8,128)(2,1)S(1)}, u32[]{:S(2)}, u32[]{:S(2)}) collective-permute-start(bf16[2,128,768]{2,1,0:T(8,128)(2,1)S(1)} %collective-permute-done.near_ref), channel_id=1, source_target_pairs={{1,0},{0,1},{3,2},{2,3},{5,4},{4,5},{7,6},{6,7},{9,8},{8,9},{11,10... | collective-permute-start | bytes 1179656 | tf_op jit(solution)/shard_map/ppermute | solution.py:273
  23.1 7.2 %collective-permute-start.5 = (bf16[2,128,768]{2,1,0:T(8,128)(2,1)S(1)}, bf16[2,128,768]{2,1,0:T(8,128)(2,1)}, u32[]{:S(2)}, u32[]{:S(2)}) collective-permute-start(bf16[2,128,768]{2,1,0:T(8,128)(2,1)S(1)} %collective-permute-done.1.middle_ref), channel_id=1, source_target_pairs={{1,0},{0,1},{3,2},{2,3},{5,4},{4,5},{7,6},{6,7},{9,8},{8,9},{11,10... | collective-permute-start | bytes 1179656 | tf_op jit(solution)/shard_map/ppermute | solution.py:273
  24.2 15.8 %collective-permute-start.6 = (bf16[2,128,768]{2,1,0:T(8,128)(2,1)S(1)}, bf16[2,128,768]{2,1,0:T(8,128)(2,1)S(1)}, u32[]{:S(2)}, u32[]{:S(2)}) collective-permute-start(bf16[2,128,768]{2,1,0:T(8,128)(2,1)S(1)} %get-tuple-element.43.query_ref.refs_0_), channel_id=1, source_target_pairs={{15,0},{2,1},{1,2},{4,3},{3,4},{6,5},{5,6},{8,7},{7,8},{10,9},{9,1... | collective-permute-start | bytes 1179656 | tf_op jit(solution)/shard_map/ppermute | solution.py:287
  28.7 14.2 %collective-permute-start.7 = (bf16[2,128,768]{2,1,0:T(8,128)(2,1)S(1)}, bf16[2,128,768]{2,1,0:T(8,128)(2,1)S(1)}, u32[]{:S(2)}, u32[]{:S(2)}) collective-permute-start(bf16[2,128,768]{2,1,0:T(8,128)(2,1)S(1)} %get-tuple-element.43.query_ref.refs_0_), channel_id=1, source_target_pairs={{14,0},{3,1},{0,2},{5,3},{2,4},{7,5},{4,6},{9,7},{6,8},{11,9},{8,1... | collective-permute-start | bytes 1179656 | tf_op jit(solution)/shard_map/ppermute | solution.py:287
  28.7 11.3 %collective-permute-start.19 = (bf16[128,768]{1,0:T(8,128)(2,1)}, bf16[128,768]{1,0:T(8,128)(2,1)}, u32[]{:S(2)}, u32[]{:S(2)}) collective-permute-start(bf16[128,768]{1,0:T(8,128)(2,1)} %bitcast.1.g_ref), channel_id=1, source_target_pairs={{0,16},{16,0},{1,17},{17,1},{2,18},{18,2},{3,19},{19,3},{4,20},{20... | collective-permute-start | bytes 589832 | tf_op jit(solution)/shard_map/ppermute | solution.py:276
  35.9 7.0 %collective-permute-start.18 = (bf16[384,128]{1,0:T(8,128)(2,1)S(1)}, bf16[384,128]{1,0:T(8,128)(2,1)S(1)}, u32[]{:S(2)}, u32[]{:S(2)}) collective-permute-start(bf16[384,128]{1,0:T(8,128)(2,1)S(1)} %get-tuple-element.51), channel_id=1, source_target_pairs={{0,16},{16,0},{1,17},{17,1},{2,18},{18,2},{3,19},{19,3},{4,20},{20... | collective-permute-start | bytes 294920 | tf_op jit(solution)/shard_map/ppermute | solution.py:276
  36.5 6.4 %copy-start.6 = (bf16[128,768]{1,0:T(8,128)(2,1)S(1)}, bf16[128,768]{1,0:T(8,128)(2,1)}, u32[]{:S(2)}) copy-start(bf16[128,768]{1,0:T(8,128)(2,1)} %copy-done.5) | copy-start | bytes 589828
  44.1 15.4 %collective-permute-start.20 = (bf16[192,768]{1,0:T(8,128)(2,1)S(1)}, bf16[192,768]{1,0:T(8,128)(2,1)S(1)}, u32[]{:S(2)}, u32[]{:S(2)}) collective-permute-start(bf16[192,768]{1,0:T(8,128)(2,1)S(1)} %get-tuple-element.55), channel_id=1, source_target_pairs={{1,0},{0,1},{3,2},{2,3},{5,4},{4,5},{7,6},{6,7},{9,8},{8,9},{11,10... | collective-permute-start | bytes 884744 | tf_op jit(solution)/shard_map/ppermute | solution.py:273
  45.4 14.4 %collective-permute-start.8 = (bf16[2,128,768]{2,1,0:T(8,128)(2,1)S(1)}, bf16[2,128,768]{2,1,0:T(8,128)(2,1)S(1)}, u32[]{:S(2)}, u32[]{:S(2)}) collective-permute-start(bf16[2,128,768]{2,1,0:T(8,128)(2,1)S(1)} %get-tuple-element.43.query_ref.refs_0_), channel_id=1, source_target_pairs={{13,0},{4,1},{15,2},{6,3},{1,4},{8,5},{3,6},{10,7},{5,8},{12,9},{7... | collective-permute-start | bytes 1179656 | tf_op jit(solution)/shard_map/ppermute | solution.py:287
  48.7 10.4 %collective-permute-start.12 = (f32[24,128]{1,0:T(8,128)S(1)}, f32[24,128]{1,0:T(8,128)S(1)}, u32[]{:S(2)}, u32[]{:S(2)}) collective-permute-start(f32[24,128]{1,0:T(8,128)S(1)} %get-tuple-element.37.stats_ref.refs_7_), channel_id=1, source_target_pairs={{15,0},{2,1},{1,2},{4,3},{3,4},{6,5},{5,6},{8,7},{7,8},{10,9},{9,1... | collective-permute-start | bytes 36872 | tf_op jit(solution)/shard_map/ppermute | solution.py:287
  49.9 9.2 %collective-permute-start.15 = (f32[24,128]{1,0:T(8,128)S(1)}, f32[24,128]{1,0:T(8,128)S(1)}, u32[]{:S(2)}, u32[]{:S(2)}) collective-permute-start(f32[24,128]{1,0:T(8,128)S(1)} %get-tuple-element.37.stats_ref.refs_7_), channel_id=1, source_target_pairs={{1,0},{0,1},{3,2},{2,3},{5,4},{4,5},{7,6},{6,7},{9,8},{8,9},{11,10... | collective-permute-start | bytes 36872 | tf_op jit(solution)/shard_map/ppermute | solution.py:273
  50.5 22.6 %collective-permute-start.9 = (bf16[2,128,768]{2,1,0:T(8,128)(2,1)S(1)}, bf16[2,128,768]{2,1,0:T(8,128)(2,1)S(1)}, u32[]{:S(2)}, u32[]{:S(2)}) collective-permute-start(bf16[2,128,768]{2,1,0:T(8,128)(2,1)S(1)} %get-tuple-element.43.query_ref.refs_0_), channel_id=1, source_target_pairs={{1,0},{0,1},{3,2},{2,3},{5,4},{4,5},{7,6},{6,7},{9,8},{8,9},{11,10... | collective-permute-start | bytes 1179656 | tf_op jit(solution)/shard_map/ppermute | solution.py:273
  59.1 15.2 %collective-permute-start.10 = (bf16[2,128,768]{2,1,0:T(8,128)(2,1)S(1)}, bf16[2,128,768]{2,1,0:T(8,128)(2,1)S(1)}, u32[]{:S(2)}, u32[]{:S(2)}) collective-permute-start(bf16[2,128,768]{2,1,0:T(8,128)(2,1)S(1)} %collective-permute-done.6.refs_1_.refs_5_), channel_id=1, source_target_pairs={{1,0},{0,1},{3,2},{2,3},{5,4},{4,5},{7,6},{6,7},{9,8},{8,9},{11,10... | collective-permute-start | bytes 1179656 | tf_op jit(solution)/shard_map/ppermute | solution.py:273
  59.1 15.2 %collective-permute-start.11 = (bf16[2,128,768]{2,1,0:T(8,128)(2,1)S(1)}, bf16[2,128,768]{2,1,0:T(8,128)(2,1)S(1)}, u32[]{:S(2)}, u32[]{:S(2)}) collective-permute-start(bf16[2,128,768]{2,1,0:T(8,128)(2,1)S(1)} %collective-permute-done.7.refs_2_.refs_6_), channel_id=1, source_target_pairs={{1,0},{0,1},{3,2},{2,3},{5,4},{4,5},{7,6},{6,7},{9,8},{8,9},{11,10... | collective-permute-start | bytes 1179656 | tf_op jit(solution)/shard_map/ppermute | solution.py:273
  59.6 6.7 %collective-permute-start.21 = (bf16[96,768]{1,0:T(8,128)(2,1)S(1)}, bf16[96,768]{1,0:T(8,128)(2,1)S(1)}, u32[]{:S(2)}, u32[]{:S(2)}) collective-permute-start(bf16[96,768]{1,0:T(8,128)(2,1)S(1)} %get-tuple-element.57), channel_id=1, source_target_pairs={{2,0},{3,1},{0,2},{1,3},{6,4},{7,5},{4,6},{5,7},{10,8},{11,9},{8,1... | collective-permute-start | bytes 442376 | tf_op jit(solution)/shard_map/ppermute | solution.py:273
  59.7 6.6 %collective-permute-start.13 = (f32[24,128]{1,0:T(8,128)S(1)}, f32[24,128]{1,0:T(8,128)S(1)}, u32[]{:S(2)}, u32[]{:S(2)}) collective-permute-start(f32[24,128]{1,0:T(8,128)S(1)} %get-tuple-element.37.stats_ref.refs_7_), channel_id=1, source_target_pairs={{14,0},{3,1},{0,2},{5,3},{2,4},{7,5},{4,6},{9,7},{6,8},{11,9},{8,1... | collective-permute-start | bytes 36872 | tf_op jit(solution)/shard_map/ppermute | solution.py:287
  66.4 6.2 %collective-permute-start.22 = (bf16[48,768]{1,0:T(8,128)(2,1)S(1)}, bf16[48,768]{1,0:T(8,128)(2,1)S(1)}, u32[]{:S(2)}, u32[]{:S(2)}) collective-permute-start(bf16[48,768]{1,0:T(8,128)(2,1)S(1)} %get-tuple-element.59), channel_id=1, source_target_pairs={{4,0},{5,1},{6,2},{7,3},{0,4},{1,5},{2,6},{3,7},{12,8},{13,9},{14,... | collective-permute-start | bytes 221192 | tf_op jit(solution)/shard_map/ppermute | solution.py:273
  66.5 5.0 %collective-permute-start.14 = (f32[24,128]{1,0:T(8,128)S(1)}, f32[24,128]{1,0:T(8,128)S(1)}, u32[]{:S(2)}, u32[]{:S(2)}) collective-permute-start(f32[24,128]{1,0:T(8,128)S(1)} %get-tuple-element.37.stats_ref.refs_7_), channel_id=1, source_target_pairs={{13,0},{4,1},{15,2},{6,3},{1,4},{8,5},{3,6},{10,7},{5,8},{12,9},{7... | collective-permute-start | bytes 36872 | tf_op jit(solution)/shard_map/ppermute | solution.py:287
  71.5 1.2 %collective-permute-start.16 = (f32[24,128]{1,0:T(8,128)S(1)}, f32[24,128]{1,0:T(8,128)S(1)}, u32[]{:S(2)}, u32[]{:S(2)}) collective-permute-start(f32[24,128]{1,0:T(8,128)S(1)} %collective-permute-done.12.refs_8_.refs_2_), channel_id=1, source_target_pairs={{1,0},{0,1},{3,2},{2,3},{5,4},{4,5},{7,6},{6,7},{9,8},{8,9},{11,10... | collective-permute-start | bytes 36872 | tf_op jit(solution)/shard_map/ppermute | solution.py:273
  72.7 6.5 %collective-permute-start.23 = (bf16[48,768]{1,0:T(8,128)(2,1)S(1)}, bf16[48,768]{1,0:T(8,128)(2,1)S(1)}, u32[]{:S(2)}, u32[]{:S(2)}) collective-permute-start(bf16[48,768]{1,0:T(8,128)(2,1)S(1)} %add.2.refs_0_), channel_id=1, source_target_pairs={{8,0},{9,1},{10,2},{11,3},{12,4},{13,5},{14,6},{15,7},{0,8},{1,9},... | collective-permute-start | bytes 221192 | tf_op jit(solution)/shard_map/ppermute | solution.py:273
  73.1 1.2 %collective-permute-start.17 = (f32[24,128]{1,0:T(8,128)S(1)}, f32[24,128]{1,0:T(8,128)S(1)}, u32[]{:S(2)}, u32[]{:S(2)}) collective-permute-start(f32[24,128]{1,0:T(8,128)S(1)} %collective-permute-done.13.refs_9_.refs_2_), channel_id=1, source_target_pairs={{1,0},{0,1},{3,2},{2,3},{5,4},{4,5},{7,6},{6,7},{9,8},{8,9},{11,10... | collective-permute-start | bytes 36872 | tf_op jit(solution)/shard_map/ppermute | solution.py:273
  79.2 4.4 %collective-permute-start.24 = (bf16[48,768]{1,0:T(8,128)(2,1)S(1)}, bf16[48,768]{1,0:T(8,128)(2,1)S(1)}, u32[]{:S(2)}, u32[]{:S(2)}) collective-permute-start(bf16[48,768]{1,0:T(8,128)(2,1)S(1)} %add.3.refs_0_), channel_id=1, source_target_pairs={{4,0},{5,1},{6,2},{7,3},{0,4},{1,5},{2,6},{3,7},{12,8},{13,9},{14,... | collective-permute-start | bytes 221192 | tf_op jit(solution)/shard_map/ppermute | solution.py:273
  83.6 5.2 %collective-permute-start.25 = (bf16[96,768]{1,0:T(8,128)(2,1)S(1)}, bf16[96,768]{1,0:T(8,128)(2,1)S(1)}, u32[]{:S(2)}, u32[]{:S(2)}) collective-permute-start(bf16[96,768]{1,0:T(8,128)(2,1)S(1)} %join.3.refs_0_), channel_id=1, source_target_pairs={{2,0},{3,1},{0,2},{1,3},{6,4},{7,5},{4,6},{5,7},{10,8},{11,9},{8,1... | collective-permute-start | bytes 442376 | tf_op jit(solution)/shard_map/ppermute | solution.py:273
  83.9 5.0 %copy-start.2 = (bf16[768,768]{1,0:T(8,128)(2,1)S(1)}, bf16[768,768]{1,0:T(8,128)(2,1)}, u32[]{:S(2)}) copy-start(bf16[768,768]{1,0:T(8,128)(2,1)} %weight_ref.1) | copy-start | bytes 3538948
  88.9 1.6 %collective-permute-start.26 = (bf16[192,768]{1,0:T(8,128)(2,1)S(1)}, bf16[192,768]{1,0:T(8,128)(2,1)S(1)}, u32[]{:S(2)}, u32[]{:S(2)}) collective-permute-start(bf16[192,768]{1,0:T(8,128)(2,1)S(1)} %join.4.refs_0_), channel_id=1, source_target_pairs={{1,0},{0,1},{3,2},{2,3},{5,4},{4,5},{7,6},{6,7},{9,8},{8,9},{11,10... | collective-permute-start | bytes 884744 | tf_op jit(solution)/shard_map/ppermute | solution.py:273
  89.3 2.3 %copy-start.3 = (bf16[128,768]{1,0:T(8,128)(2,1)}, bf16[128,768]{1,0:T(8,128)(2,1)S(1)}, u32[]{:S(2)}) copy-start(bf16[128,768]{1,0:T(8,128)(2,1)S(1)} %convolution_convert_fusion.refs_2_) | copy-start | bytes 589828

commit v5 on v0

v5 whole, which is shorter than its diff:
```python
import functools
import math

import jax
import jax.numpy as jnp
from jax import lax
from jax.experimental import pallas as pl
from jax.experimental.pallas import tpu as pltpu
from jax.sharding import PartitionSpec as P

HEADS = 12
PMAX = 6
HOPS = 3
LAYER = 4
LOCAL = HEADS // LAYER
BLOCKS = LAYER + 2 * HOPS
SLOTS = 2 * HOPS + 1
MIB = 1024 * 1024

neg_big = -1e30
bf16, f32 = jnp.bfloat16, jnp.float32
SMEM = pl.BlockSpec(memory_space=pltpu.SMEM)
VMEM = pl.BlockSpec(memory_space=pltpu.VMEM)
ANY = pl.BlockSpec(memory_space=pl.ANY)
HBM = pl.BlockSpec(memory_space=pltpu.HBM)
NN = (((1,), (0,)), ((), ()))
NT = (((1,), (1,)), ((), ()))
TN = (((0,), (0,)), ((), ()))


def dot(x, y, dims):
    return lax.dot_general(x, y, dims, preferred_element_type=f32)


def shape_of(*dims, dtype=bf16):
    return jax.ShapeDtypeStruct(dims, dtype)


TOKEN = shape_of(8, 128, dtype=f32)


def skip_refs(kernel, first, count, *refs):
    kernel(*refs[:first], *refs[first + count :])


def call(kernel, ins, outs, args, scratch=(), limit=8, name=None, after=()):
    ins, args = [*ins, *[ANY] * len(after)], (*args, *after)
    if after:
        kernel = functools.partial(skip_refs, kernel, len(args) - len(after), len(after))
    return pl.pallas_call(
        kernel,
        in_specs=ins,
        out_specs=[VMEM] * len(outs),
        out_shape=outs,
        scratch_shapes=list(scratch),
        compiler_params=pltpu.CompilerParams(vmem_limit_bytes=limit * MIB),
        cost_estimate=pl.CostEstimate(flops=1, bytes_accessed=1, transcendentals=0),
        name=name,
    )(*args)


def place(peer, size):
    position = jnp.bitwise_xor(lax.rem(lax.axis_index("station"), LAYER), peer)
    return pl.ds(pl.multiple_of(position * size, size), size)


def block(j, span):
    return slice(j * span, (j + 1) * span)


def readers(j):
    return max(0, j - 2 * HOPS), min(LAYER - 1, j)


def pack_kernel(k_ref, v_ref, q_ref, *refs):
    outs, (natural, flipped, sems) = refs[:LAYER], refs[LAYER:]
    rows = outs[0].shape[1]
    copies = [
        pltpu.make_async_copy(ref, natural.at[n], sems.at[n])
        for n, ref in enumerate((k_ref, v_ref, q_ref))
    ]
    for copy in copies:
        copy.start()
    scale = 1.0 / math.sqrt(flipped.shape[1] // HEADS)
    for n, copy in enumerate(copies):
        copy.wait()
        value = natural[n].T
        flipped[n] = value * bf16(scale) if n == 2 else value
    for peer, out in enumerate(outs):
        out[...] = flipped[:, place(peer, rows)]


def gather_kernel(*refs):
    ins, (up_ref, down_ref, pair_ref, query_ref) = refs[:LAYER], refs[LAYER:]
    span = ins[0].shape[2]
    for peer, ref in enumerate(ins):
        at = place(peer, span)
        pair_ref[0, :, at] = ref[0]
        pair_ref[1, :, at] = ref[1]
        query_ref[:, at] = ref[2]
    up_ref[...] = pair_ref[:, :, span:]
    down_ref[...] = pair_ref[:, :, : HOPS * span]


def project_kernel(
    station_count, ids_ref, count_ref, *refs
):
    ins, refs = refs[:LAYER], refs[LAYER:]
    weight_ref, query_ref, all_ref, grad_ref, up_ref, down_ref, bias_ref, dead_ref = refs
    span = ins[0].shape[0]
    rows = query_ref.shape[0]
    for peer, ref in enumerate(ins):
        all_ref[place(peer, span)] = ref[...]
    grad_ref[...] = dot(weight_ref[place(0, rows)], all_ref[...], NT).astype(bf16)
    for n, ref in enumerate((query_ref, grad_ref)):
        up_ref[n] = ref[:, span:]
        down_ref[n] = ref[:, : HOPS * span]
    first = lax.axis_index("station") // LAYER * LAYER
    ones = jnp.ones((1, span), f32)

    def listed(reader, other):
        hit = jnp.int32(0)
        for j in range(PMAX):
            here = jnp.logical_and(ids_ref[reader, j] == other, j < count_ref[reader])
            hit = jnp.maximum(hit, here.astype(jnp.int32))
        return hit > 0

    for j in range(BLOCKS):
        outer = lax.rem(first + (j - HOPS) + station_count, station_count)
        low, high = readers(j)
        for i in range(low, high + 1):
            inner = first + i
            slot = j - i
            if slot == HOPS:
                bias_ref[j : j + 1, block(i, span)] = 0.0 * ones
                dead_ref[i : i + 1, block(slot, span)] = 0.0 * ones
            else:
                reads = jnp.where(listed(inner, outer), 0.0, neg_big)
                bias_ref[j : j + 1, block(i, span)] = reads * ones
                read_by = jnp.where(listed(outer, inner), 0.0, -neg_big)
                dead_ref[i : i + 1, block(slot, span)] = read_by * ones


def clear(ref, span):
    for j in range(BLOCKS):
        low, high = readers(j)
        for i in range(LAYER):
            if not low <= i <= high:
                ref[block(j, span), block(i, span)] = jnp.zeros((span, span), bf16)


def forward_kernel(
    pair_ref, low_ref, high_ref, query_ref, grad_ref, bias_ref,
    mixed_ref, stats_ref, stats_up, stats_down, probs_ref, window_ref,
    raw,
):
    rows = query_ref.shape[0]
    span = query_ref.shape[1] // LAYER
    head_width = rows // LOCAL
    reach = HOPS * span
    window_ref[:, :, :reach] = low_ref[...]
    window_ref[:, :, reach : reach + LAYER * span] = pair_ref[...]
    window_ref[:, :, reach + LAYER * span :] = high_ref[...]
    for head in range(LOCAL):
        clear(probs_ref.at[head], span)
        at = block(head, head_width)
        query = query_ref[at]
        tops = [None] * LAYER
        for j in range(BLOCKS):
            low, high = readers(j)
            cols = slice(low * span, (high + 1) * span)
            scores = dot(window_ref[0, at, block(j, span)], query[:, cols], TN)
            scores = scores + bias_ref[j : j + 1, cols]
            raw[block(j, span), cols] = scores
            here = jnp.max(scores, 0, keepdims=True)
            for i in range(low, high + 1):
                mine = here[:, block(i - low, span)]
                tops[i] = mine if tops[i] is None else jnp.maximum(tops[i], mine)
        top = jnp.concatenate(tops, 1)
        totals = [jnp.zeros((1, span), f32)] * LAYER
        for j in range(BLOCKS):
            low, high = readers(j)
            cols = slice(low * span, (high + 1) * span)
            weight = jnp.exp(raw[block(j, span), cols] - top[:, cols])
            raw[block(j, span), cols] = weight
            here = jnp.sum(weight, 0, keepdims=True)
            for i in range(low, high + 1):
                totals[i] = totals[i] + here[:, block(i - low, span)]
        total = jnp.concatenate(totals, 1)
        inverse = 1.0 / total
        for j in range(BLOCKS):
            low, high = readers(j)
            cols = slice(low * span, (high + 1) * span)
            probs_ref[head, block(j, span), cols] = (
                raw[block(j, span), cols] * inverse[:, cols]
            ).astype(bf16)
        mixed = dot(window_ref[1, at], probs_ref[head], NN).astype(bf16)
        mixed_ref[at] = mixed
        product = grad_ref[at].astype(f32) * mixed.astype(f32)
        stats_ref[head : head + 1] = top + jnp.log(total)
        stats_ref[LOCAL + head : LOCAL + head + 1] = jnp.sum(product, 0, keepdims=True)
    stats_ref[2 * LOCAL :] = jnp.zeros((8 - 2 * LOCAL, LAYER * span), f32)
    stats_up[...] = stats_ref[:, span:]
    stats_down[...] = stats_ref[:, :reach]


def query_grad_kernel(window_ref, probs_ref, grad_ref, stats_ref, mixed_ref, *refs):
    outs, (token_ref, grads, flipped) = refs[:LAYER], refs[LAYER:]
    rows = grad_ref.shape[0]
    span = grad_ref.shape[1] // LAYER
    head_width = rows // LOCAL
    scale = 1.0 / math.sqrt(head_width)
    clear(grads, span)
    for head in range(LOCAL):
        at = block(head, head_width)
        grad = grad_ref[at]
        delta = stats_ref[LOCAL + head : LOCAL + head + 1]
        for j in range(BLOCKS):
            low, high = readers(j)
            cols = slice(low * span, (high + 1) * span)
            back = dot(window_ref[1, at, block(j, span)], grad[:, cols], TN)
            prob = probs_ref[head, block(j, span), cols].astype(f32)
            grads[block(j, span), cols] = (prob * (back - delta[:, cols])).astype(bf16)
        flipped[at] = (dot(window_ref[0, at], grads[...], NN) * scale).astype(bf16)
    for peer, out in enumerate(outs):
        out[0] = mixed_ref[:, place(peer, span)]
        out[1] = flipped[:, place(peer, span)]
    token_ref[...] = jnp.zeros_like(token_ref)


def key_grad_kernel(
    head, pair_ref, query_ref, grad_ref, low_ref, high_ref, stats_ref, stats_low, stats_high,
    dead_ref, *refs
):
    before, refs = refs[:head], refs[head:]
    out_ref, refs = refs[0], refs[1:]
    span = query_ref.shape[1] // LAYER
    head_width = query_ref.shape[0] // LOCAL
    at = block(head, head_width)

    def window(low, own, high):
        return jnp.concatenate([low, own, high], 1)

    query = window(low_ref[0, at], query_ref[at], high_ref[0, at])
    grad = window(low_ref[1, at], grad_ref[at], high_ref[1, at])
    row = slice(head, head + 1)
    log_sum = window(stats_low[row], stats_ref[row], stats_high[row])
    row = slice(LOCAL + head, LOCAL + head + 1)
    delta = window(stats_low[row], stats_ref[row], stats_high[row])
    for i in range(LAYER):
        cols = slice(i * span, (i + SLOTS) * span)
        own = block(i, span)
        scores = dot(pair_ref[0, at, own], query[:, cols], TN)
        prob = jnp.exp(scores - (log_sum[:, cols] + dead_ref[i : i + 1]))
        back = dot(pair_ref[1, at, own], grad[:, cols], TN)
        grads = (prob * (back - delta[:, cols])).astype(bf16)
        out_ref[0, :, own] = dot(query[:, cols], grads, NT).astype(bf16)
        out_ref[1, :, own] = dot(grad[:, cols], prob.astype(bf16), NT).astype(bf16)
    if head == LOCAL - 1:
        for peer, ref in enumerate(refs[:LAYER]):
            for h, source in enumerate((*before, out_ref)):
                ref[:, block(h, head_width)] = source[:, :, place(peer, span)]
    refs[-1][...] = jnp.zeros_like(refs[-1])


def output_kernel(*refs):
    ins, (weight_ref, out_ref, dq_ref, token_ref, flipped) = refs[:LAYER], refs[LAYER:]
    for peer, ref in enumerate(ins):
        flipped[:, place(peer, ref.shape[1])] = ref[...]
    out_ref[...] = dot(flipped[0], weight_ref[...], TN).astype(bf16)
    dq_ref[...] = flipped[1].T
    token_ref[...] = jnp.zeros_like(token_ref)


def key_output_kernel(*refs):
    ins, (dk_ref, dv_ref, flipped) = refs[:LAYER], refs[LAYER:]
    for peer, ref in enumerate(ins):
        flipped[:, place(peer, ref.shape[1])] = ref[...]
    dk_ref[...] = flipped[0].T
    dv_ref[...] = flipped[1].T


def halves(bit, half):
    send = pl.ds(pl.multiple_of((1 - bit) * half, half), half)
    keep = pl.ds(pl.multiple_of(bit * half, half), half)
    return send, keep


def bit_of(stride):
    return lax.rem(lax.axis_index("station") // stride, 2)


def weight_kernel(mixed_ref, all_ref, send_ref, keep_ref):
    send, keep = halves(lax.rem(lax.axis_index("dp"), 2), send_ref.shape[0])
    send_ref[...] = dot(mixed_ref[send], all_ref[...], NN).astype(bf16)
    keep_ref[...] = dot(mixed_ref[keep], all_ref[...], NN)


def split_kernel(stride, part_ref, got_ref, send_ref, keep_ref):
    send, keep = halves(bit_of(stride), send_ref.shape[0])
    send_ref[...] = (part_ref[send] + got_ref[send].astype(f32)).astype(bf16)
    keep_ref[...] = part_ref[keep] + got_ref[keep].astype(f32)


def round_kernel(part_ref, got_ref, out_ref):
    out_ref[...] = (part_ref[...].astype(f32) + got_ref[...].astype(f32)).astype(bf16)


def join_kernel(stride, scale, mine_ref, got_ref, out_ref):
    other, here = halves(bit_of(stride), mine_ref.shape[0])
    for at, ref in ((here, mine_ref), (other, got_ref)):
        value = ref[...]
        if scale is not None:
            value = value.astype(f32) * scale
        out_ref[at] = value


def cross_kernel(mine_ref, first_ref, second_ref, out_ref):
    window = lax.rem(lax.axis_index("dp"), 2)
    other, here = halves(window, mine_ref.shape[0])
    at_home = bit_of(2) == window
    mine, first, second = mine_ref[...], first_ref[...], second_ref[...]
    out_ref[here] = jnp.where(at_home, mine, first)
    out_ref[other] = jnp.where(at_home, first, second)


def local(
    query_states, key_states, value_states, grad_output, out_weight, partner_ids, partner_count
):
    span, width = query_states.shape[2:]
    stations = lax.axis_size("station")
    windows = lax.axis_size("dp")
    rows = width // LAYER
    dma = pltpu.SemaphoreType.DMA

    def swap(value, stride):
        return lax.ppermute(value, "station", [(s ^ stride, s) for s in range(stations)])

    def in_layer(values):
        return [swap(values[n], n + 1) for n in range(LAYER - 1)]

    def along(up, down):
        low = lax.ppermute(up, "station", [(s, (s + LAYER) % stations) for s in range(stations)])
        high = lax.ppermute(down, "station", [(s, (s - LAYER) % stations) for s in range(stations)])
        return low, high

    def other_window(value):
        return lax.ppermute(value, "dp", [(0, 1), (1, 0)])

    def flat(x):
        return x.reshape(span, width)

    q, k, v, g = flat(query_states), flat(key_states), flat(value_states), flat(grad_output)
    reach_shape = shape_of(2, rows, HOPS * span)
    layer_shape = shape_of(rows, LAYER * span)
    mine, *parts = call(
        pack_kernel, [HBM] * 3, [shape_of(3, rows, span)] * LAYER, (k, v, q),
        [pltpu.VMEM((3, span, width), bf16), pltpu.VMEM((3, width, span), bf16), dma((3,))],
        limit=58, name="pack",
    )
    parts = in_layer(parts)
    up, down, pair, query = call(
        gather_kernel, [VMEM] * LAYER,
        [reach_shape, reach_shape, shape_of(2, rows, LAYER * span), layer_shape],
        (mine, *parts), name="gather",
    )
    g_later, up, down = lax.optimization_barrier((g, up, down))
    kv_low, kv_high = along(up, down)
    g_parts = in_layer([g_later] * 3)
    all_grad, grad, up, down, bias, dead = call(
        functools.partial(project_kernel, stations),
        [SMEM] * 2 + [VMEM] * (LAYER + 2),
        [
            shape_of(LAYER * span, width), layer_shape, reach_shape, reach_shape,
            shape_of(16, LAYER * span, dtype=f32), shape_of(8, SLOTS * span, dtype=f32),
        ],
        (partner_ids, partner_count, g, *g_parts, out_weight, query),
        limit=16, name="project",
    )
    qg_low, qg_high = along(up, down)
    stats_shape = shape_of(8, HOPS * span, dtype=f32)
    mixed, stats, up, down, probs, window = call(
        forward_kernel, [VMEM] * 6,
        [
            layer_shape, shape_of(8, LAYER * span, dtype=f32), stats_shape, stats_shape,
            shape_of(LOCAL, BLOCKS * span, LAYER * span), shape_of(2, rows, BLOCKS * span),
        ],
        (pair, kv_low, kv_high, query, grad, bias),
        [pltpu.VMEM((BLOCKS * span, LAYER * span), f32)],
        limit=20, name="forward",
    )
    stats_low, stats_high = along(up, down)

    send, part = call(
        weight_kernel, [VMEM] * 2,
        [shape_of(rows // 2, width), shape_of(rows // 2, width, dtype=f32)],
        (mixed, all_grad), name="weight",
    )

    part_shape = shape_of(2, rows, span)
    mine, *parts, query_token = call(
        query_grad_kernel, [VMEM] * 5, [part_shape] * LAYER + [TOKEN],
        (window, probs, grad, stats, mixed),
        [pltpu.VMEM((BLOCKS * span, LAYER * span), bf16), pltpu.VMEM((rows, LAYER * span), bf16)],
        limit=20, name="query_grad",
    )
    parts = in_layer(parts)
    layer_output, grad_query, output_token = call(
        output_kernel, [VMEM] * (LAYER + 1), [shape_of(span, width)] * 2 + [TOKEN],
        (mine, *parts, out_weight), [pltpu.VMEM((2, width, span), bf16)], name="output",
    )

    before, key_tokens = [], []
    for head in range(LOCAL):
        last = head == LOCAL - 1
        out, *parts, token = call(
            functools.partial(key_grad_kernel, head),
            [VMEM] * (9 + len(before)),
            [shape_of(2, rows // LOCAL, LAYER * span)] + [part_shape] * (LAYER * last) + [TOKEN],
            (pair, query, grad, qg_low, qg_high, stats, stats_low, stats_high, dead, *before),
            limit=20, name="key_grad",
        )
        before.append(out)
        key_tokens.append(token)
    mine, *parts = parts
    grad_key, grad_value = call(
        key_output_kernel, [VMEM] * LAYER, [shape_of(span, width)] * 2,
        (mine, *in_layer(parts)), [pltpu.VMEM((2, width, span), bf16)], name="key_output",
    )

    scale = 1.0 / math.sqrt(span * windows * stations)
    if windows == 2:
        count = rows // 4
        got = other_window(send)
        send, part = call(
            functools.partial(split_kernel, LAYER), [VMEM] * 2,
            [shape_of(count, width), shape_of(count, width, dtype=f32)],
            (part, got), name="split", after=(query_token, qg_low, qg_high),
        )

        def add_round(part, got, after=()):
            out = [shape_of(count, width)]
            return call(round_kernel, [VMEM] * 2, out, (part, got), name="add", after=after)[0]

        total = add_round(part, swap(send, LAYER), key_tokens[:1])
        stride = 2 * LAYER
        while stride < stations:
            total = add_round(total, swap(total, stride), key_tokens[1:2])
            stride *= 2
        (total,) = call(
            functools.partial(join_kernel, LAYER, None), [VMEM] * 2, [shape_of(2 * count, width)],
            (total, swap(total, LAYER)), name="join", after=key_tokens[2:],
        )
        first, second = [], []
        for w in range(2):
            for s in range(stations):
                if s // 2 % 2 == w:
                    first.append((w * stations + s, w * stations + (s ^ 2)))
                else:
                    first.append((w * stations + s, (1 - w) * stations + s))
                    second.append((w * stations + s, (1 - w) * stations + (s ^ 2)))
        axes = ("dp", "station")
        (total,) = call(
            cross_kernel, [VMEM] * 3, [shape_of(4 * count, width)],
            (total, lax.ppermute(total, axes, first), lax.ppermute(total, axes, second)),
            name="cross", after=(output_token,),
        )
        (grad_weight,) = call(
            functools.partial(join_kernel, 1, scale), [VMEM] * 2,
            [shape_of(8 * count, width, dtype=f32)], (total, swap(total, 1)), name="last",
        )
    else:
        start = lax.axis_index("station") % LAYER * rows
        mine = dot(mixed, all_grad, NN).astype(bf16)
        whole = lax.dynamic_update_slice_in_dim(jnp.zeros((width, width), bf16), mine, start, 0)
        whole = lax.psum_scatter(whole, "dp", scatter_dimension=0, tiled=True)
        grad_weight = lax.psum(whole.astype(f32), "station") * scale
    shape = query_states.shape
    return (
        layer_output.reshape(shape),
        grad_query.reshape(shape),
        grad_key.reshape(shape),
        grad_value.reshape(shape),
        grad_weight,
    )


def solution(mesh):
    split = P("dp", "station", None, None)
    return jax.shard_map(
        local,
        mesh=mesh,
        in_specs=(split, split, split, split, P(), P(), P()),
        out_specs=(split, split, split, split, P("dp", None)),
        check_vma=False,
    )
```

time: 254 us -> 87.2 us (0.34)
  the two profiles are of different devices: /device:TPU:0 before, /device:TPU:3 now
where the time goes in v5:
time: 87.2 us; the launch traced here: 86.1 us
  waiting for transfers between devices  33.4 us (38%)
  starting transfers between devices  30.7 us (35%)
  Pallas kernels  18 us (21%)
  local copies, waits for them, and re-layouts  3.26 us (4%)
    ppermute x16, waiting for transfers between devices, swap(): lax.ppermute(value, 'station', [(s ^ stride, s) for s in range(stations)])  25.7 us
    pallas_call x17, Pallas kernels, call(): pl.pallas_call(kernel, in_specs=ins, out_specs=[VMEM] * len(outs), out_sh...  18 us
    ppermute x16, starting transfers between devices, swap(): lax.ppermute(value, 'station', [(s ^ stride, s) for s in range(stations)])  16.2 us
    ppermute x3, starting transfers between devices, along(): lax.ppermute(down, 'station', [(s, (s - LAYER) % stations) for s in range...  7.28 us
    ppermute x3, waiting for transfers between devices, along(): lax.ppermute(down, 'station', [(s, (s - LAYER) % stations) for s in range...  5.09 us
    unnamed x9, local copies, waits for them, and re-layouts  3.26 us
    ppermute x1, starting transfers between devices, local(): lax.ppermute(total, axes, second)  3.1 us
    ppermute x3, starting transfers between devices, along(): lax.ppermute(up, 'station', [(s, (s + LAYER) % stations) for s in range(s...  2.75 us
  transfers between devices with their start and end apart: 25, of which 13 were waited for; matrix products, arithmetic and copies ran while one was open for 1% of the time, Pallas kernels for 17%

profile of v5, /device:TPU:3, one launch (start us, length us, event | category | flops | bytes accessed | tf_op | source)
XLA Modules:
  0.0 86.1 jit_solution(8339449865477261312)
XLA Ops:
  0.6 2.2 %pack.1 = (bf16[3,192,128]{2,1,0:T(8,128)(2,1)}, bf16[3,192,128]{2,1,0:T(8,128)(2,1)}, bf16[3,192,128]{2,1,0:T(8,128)(2,1)}, bf16[3,192,128]{2,1,0:T(8,128)(2,1)}) custom-call(bf16[128,768]{1,0:T(8,128)(2,1)} %bitcast.12, bf16[128,768]{1,0:T(8,128)(2,1)} %bitcast.13, bf16[128,768]{1,0:T(8,128)(2,1)} %bitcast.14), custom_call_target="tpu_custom_call" | custom-call | flops 1 | bytes 1 | tf_op jit(solution)/shard_map/pack/pallas_call | solution.py:50
  2.8 0.7 collective-permute-start
  3.6 1.7 %collective-permute-start.2 = (bf16[3,192,128]{2,1,0:T(8,128)(2,1)}, bf16[3,192,128]{2,1,0:T(8,128)(2,1)S(1)}, u32[]{:S(2)}, u32[]{:S(2)}) collective-permute-start(bf16[3,192,128]{2,1,0:T(8,128)(2,1)} %get-tuple-element.54), channel_id=1, source_target_pairs={{3,0},{2,1},{1,2},{0,3},{7,4},{6,5},{5,6},{4,7},{11,8},{10,9},{9,1... | collective-permute-start | bytes 442376 | tf_op jit(solution)/shard_map/ppermute | solution.py:337
  5.3 3.9 %collective-permute-done.1.refs_2_ = bf16[3,192,128]{2,1,0:T(8,128)(2,1)S(1)} collective-permute-done((bf16[3,192,128]{2,1,0:T(8,128)(2,1)}, bf16[3,192,128]{2,1,0:T(8,128)(2,1)S(1)}, u32[]{:S(2)}, u32[]{:S(2)}) %collective-permute-start.1) | collective-permute-done | bytes 147488 | tf_op jit(solution)/shard_map/ppermute | solution.py:337
  9.2 3.3 %collective-permute-done.2.refs_3_ = bf16[3,192,128]{2,1,0:T(8,128)(2,1)S(1)} collective-permute-done((bf16[3,192,128]{2,1,0:T(8,128)(2,1)}, bf16[3,192,128]{2,1,0:T(8,128)(2,1)S(1)}, u32[]{:S(2)}, u32[]{:S(2)}) %collective-permute-start.2) | collective-permute-done | bytes 147488 | tf_op jit(solution)/shard_map/ppermute | solution.py:337
  12.5 0.9 %copy-done.2 = bf16[3,192,128]{2,1,0:T(8,128)(2,1)S(1)} copy-done((bf16[3,192,128]{2,1,0:T(8,128)(2,1)S(1)}, bf16[3,192,128]{2,1,0:T(8,128)(2,1)}, u32[]{:S(2)}) %copy-start.2) | copy-done | bytes 147480
  13.5 0.2 gather.1
  13.6 0.4 collective-permute-start.7
  14.0 1.3 %collective-permute-start.6 = (bf16[128,768]{1,0:T(8,128)(2,1)}, bf16[128,768]{1,0:T(8,128)(2,1)S(1)}, u32[]{:S(2)}, u32[]{:S(2)}) collective-permute-start(bf16[128,768]{1,0:T(8,128)(2,1)} %bitcast.9), channel_id=1, source_target_pairs={{2,0},{3,1},{0,2},{1,3},{6,4},{7,5},{4,6},{5,7},{10,8},{11,9},{8,1... | collective-permute-start | bytes 589832 | tf_op jit(solution)/shard_map/ppermute | solution.py:337
  15.3 0.6 collective-permute-start.5
  15.8 1.3 %collective-permute-start.3 = (bf16[2,192,384]{2,1,0:T(8,128)(2,1)S(1)}, bf16[2,192,384]{2,1,0:T(8,128)(2,1)S(1)}, u32[]{:S(2)}, u32[]{:S(2)}) collective-permute-start(bf16[2,192,384]{2,1,0:T(8,128)(2,1)S(1)} %get-tuple-element.58), channel_id=1, source_target_pairs={{0,4},{1,5},{2,6},{3,7},{4,8},{5,9},{6,10},{7,11},{8,12},{9,13},{1... | collective-permute-start | bytes 884744 | tf_op jit(solution)/shard_map/ppermute | solution.py:343
  17.1 2.0 %collective-permute-start.4 = (bf16[2,192,384]{2,1,0:T(8,128)(2,1)S(1)}, bf16[2,192,384]{2,1,0:T(8,128)(2,1)S(1)}, u32[]{:S(2)}, u32[]{:S(2)}) collective-permute-start(bf16[2,192,384]{2,1,0:T(8,128)(2,1)S(1)} %get-tuple-element.59), channel_id=1, source_target_pairs={{0,12},{1,13},{2,14},{3,15},{4,0},{5,1},{6,2},{7,3},{8,4},{9,5},{1... | collective-permute-start | bytes 884744 | tf_op jit(solution)/shard_map/ppermute | solution.py:344
  19.2 0.8 copy.12.ids_ref
  19.9 1.4 %collective-permute-done.7.refs_3_ = bf16[128,768]{1,0:T(8,128)(2,1)S(1)} collective-permute-done((bf16[128,768]{1,0:T(8,128)(2,1)}, bf16[128,768]{1,0:T(8,128)(2,1)S(1)}, u32[]{:S(2)}, u32[]{:S(2)}) %collective-permute-start.7) | collective-permute-done | bytes 196640 | tf_op jit(solution)/shard_map/ppermute | solution.py:337
  21.3 3.5 %collective-permute-done.6.refs_2_ = bf16[128,768]{1,0:T(8,128)(2,1)S(1)} collective-permute-done((bf16[128,768]{1,0:T(8,128)(2,1)}, bf16[128,768]{1,0:T(8,128)(2,1)S(1)}, u32[]{:S(2)}, u32[]{:S(2)}) %collective-permute-start.6) | collective-permute-done | bytes 196640 | tf_op jit(solution)/shard_map/ppermute | solution.py:337
  24.8 0.9 %copy-done.1 = bf16[1,1,128,768]{3,2,1,0:T(8,128)(2,1)S(1)} copy-done((bf16[1,1,128,768]{3,2,1,0:T(8,128)(2,1)S(1)}, bf16[1,1,128,768]{3,2,1,0:T(8,128)(2,1)}, u32[]{:S(2)}) %copy-start.1) | copy-done | bytes 196632
  25.7 0.7 copy-done.3
  26.4 1.5 %project.1 = (bf16[512,768]{1,0:T(8,128)(2,1)S(1)}, bf16[192,512]{1,0:T(8,128)(2,1)S(1)}, bf16[2,192,384]{2,1,0:T(8,128)(2,1)S(1)}, bf16[2,192,384]{2,1,0:T(8,12...) custom-call(s32[16,6]{1,0:T(8,128)S(1)} %copy.12.ids_ref, s32[16]{0:T(128)S(1)} %copy-done.3, ...), custom_call_target="tpu_custom_call" | custom-call | flops 1 | bytes 1 | tf_op jit(solution)/shard_map/project/pallas_call | solution.py:50
  27.9 1.3 %collective-permute-start.11 = (bf16[2,192,384]{2,1,0:T(8,128)(2,1)S(1)}, bf16[2,192,384]{2,1,0:T(8,128)(2,1)S(1)}, u32[]{:S(2)}, u32[]{:S(2)}) collective-permute-start(bf16[2,192,384]{2,1,0:T(8,128)(2,1)S(1)} %get-tuple-element.74), channel_id=1, source_target_pairs={{0,4},{1,5},{2,6},{3,7},{4,8},{5,9},{6,10},{7,11},{8,12},{9,13},{1... | collective-permute-start | bytes 884744 | tf_op jit(solution)/shard_map/ppermute | solution.py:343
  29.2 2.1 %collective-permute-start.12 = (bf16[2,192,384]{2,1,0:T(8,128)(2,1)S(1)}, bf16[2,192,384]{2,1,0:T(8,128)(2,1)S(1)}, u32[]{:S(2)}, u32[]{:S(2)}) collective-permute-start(bf16[2,192,384]{2,1,0:T(8,128)(2,1)S(1)} %get-tuple-element.75), channel_id=1, source_target_pairs={{0,12},{1,13},{2,14},{3,15},{4,0},{5,1},{6,2},{7,3},{8,4},{9,5},{1... | collective-permute-start | bytes 884744 | tf_op jit(solution)/shard_map/ppermute | solution.py:344
  31.3 0.5 collective-permute-done.4.high_ref
  31.9 3.2 %forward.1 = (bf16[192,512]{1,0:T(8,128)(2,1)S(1)}, f32[8,512]{1,0:T(8,128)S(1)}, f32[8,384]{1,0:T(8,128)S(1)}, f32[8,384]{1,0:T(8,128)S(1)}, bf16[3,1280,512]{2...) custom-call(bf16[2,192,512]{2,1,0:T(8,128)(2,1)S(1)} %get-tuple-element.55.pair_ref, ...), custom_call_target="tpu_custom_call" | custom-call | flops 1 | bytes 1 | tf_op jit(solution)/shard_map/forward/pallas_call | solution.py:50
  35.1 0.4 weight.1
  35.5 1.3 %collective-permute-start.18 = (bf16[96,768]{1,0:T(8,128)(2,1)S(1)}, bf16[96,768]{1,0:T(8,128)(2,1)S(1)}, u32[]{:S(2)}, u32[]{:S(2)}) collective-permute-start(bf16[96,768]{1,0:T(8,128)(2,1)S(1)} %get-tuple-element.89), channel_id=1, source_target_pairs={{0,16},{16,0},{1,17},{17,1},{2,18},{18,2},{3,19},{19,3},{4,20},{20... | collective-permute-start | bytes 442376 | tf_op jit(solution)/shard_map/ppermute | solution.py:348
  36.8 1.6 %query_grad.1 = (bf16[2,192,128]{2,1,0:T(8,128)(2,1)S(1)}, bf16[2,192,128]{2,1,0:T(8,128)(2,1)S(1)}, bf16[2,192,128]{2,1,0:T(8,128)(2,1)S(1)}, bf16[2,192,128]{2,1,0:T(8,128)(2,1)S(1)}, f32[8,128]{1,0:T(8,128)S(1)}) custom-call(bf16[2,192,1280]{2,1,0:T(8,128)(2,1)S(1)} %get-tuple-element.64.window_ref, ...), custom_call_target="tpu_custom_call" | custom-call | flops 1 | bytes 1 | tf_op jit(solution)/shard_map/query_grad/pallas_call | solution.py:50
  38.3 1.5 %collective-permute-done.18.refs_1_ = bf16[96,768]{1,0:T(8,128)(2,1)S(1)} collective-permute-done((bf16[96,768]{1,0:T(8,128)(2,1)S(1)}, bf16[96,768]{1,0:T(8,128)(2,1)S(1)}, u32[]{:S(2)}, u32[]{:S(2)}) %collective-permute-start.18) | collective-permute-done | bytes 147488 | tf_op jit(solution)/shard_map/ppermute | solution.py:348
  39.8 4.6 %collective-permute-done.12.high_ref.refs_4_ = bf16[2,192,384]{2,1,0:T(8,128)(2,1)S(1)} collective-permute-done((bf16[2,192,384]{2,1,0:T(8,128)(2,1)S(1)}, bf16[2,192,384]{2,1,0:T(8,128)(2,1)S(1)}, u32[]{:S(2)}, u32[]{:S(2)}) %collective-permute-start.12) | collective-permute-done | bytes 294944 | tf_op jit(solution)/shard_map/ppermute | solution.py:344
  44.4 1.4 %collective-permute-start.19 = (bf16[48,768]{1,0:T(8,128)(2,1)S(1)}, bf16[48,768]{1,0:T(8,128)(2,1)S(1)}, u32[]{:S(2)}, u32[]{:S(2)}) collective-permute-start(bf16[48,768]{1,0:T(8,128)(2,1)S(1)} %get-tuple-element.92), channel_id=1, source_target_pairs={{4,0},{5,1},{6,2},{7,3},{0,4},{1,5},{2,6},{3,7},{12,8},{13,9},{14,... | collective-permute-start | bytes 221192 | tf_op jit(solution)/shard_map/ppermute | solution.py:337
  46.0 3.2 %collective-permute-start.14 = (f32[8,384]{1,0:T(8,128)S(1)}, f32[8,384]{1,0:T(8,128)S(1)}, u32[]{:S(2)}, u32[]{:S(2)}) collective-permute-start(f32[8,384]{1,0:T(8,128)S(1)} %get-tuple-element.77), channel_id=1, source_target_pairs={{0,12},{1,13},{2,14},{3,15},{4,0},{5,1},{6,2},{7,3},{8,4},{9,5},{1... | collective-permute-start | bytes 36872 | tf_op jit(solution)/shard_map/ppermute | solution.py:344
  49.1 1.1 %collective-permute-done.13.stats_low = f32[8,384]{1,0:T(8,128)S(1)} collective-permute-done((f32[8,384]{1,0:T(8,128)S(1)}, f32[8,384]{1,0:T(8,128)S(1)}, u32[]{:S(2)}, u32[]{:S(2)}) %collective-permute-start.13) | collective-permute-done | bytes 12320 | tf_op jit(solution)/shard_map/ppermute | solution.py:343
  50.2 1.7 %key_grad.3 = (bf16[2,64,512]{2,1,0:T(8,128)(2,1)S(1)}, f32[8,128]{1,0:T(8,128)S(1)}) custom-call(bf16[2,192,512]{2,1,0:T(8,128)(2,1)S(1)} %get-tuple-element.55.pair_ref, bf16[192,512]{1,0:T(8,128)(2,1)S(1)} %get-tuple-element.60.refs_5_.query_ref, bf16[192,512]{1,0:T(8,128)(2,1)S(1)} %get-tuple-element.62.grad_ref, ...), custom_call_target="tpu_custom_call" | custom-call | flops 1 | bytes 1 | tf_op jit(solution)/shard_map/key_grad/pallas_call | solution.py:50
  51.9 0.5 collective-permute-start.20
  52.4 1.7 %key_grad.4 = (bf16[2,64,512]{2,1,0:T(8,128)(2,1)S(1)}, f32[8,128]{1,0:T(8,128)S(1)}) custom-call(bf16[2,192,512]{2,1,0:T(8,128)(2,1)S(1)} %get-tuple-element.55.pair_ref, bf16[192,512]{1,0:T(8,128)(2,1)S(1)} %get-tuple-element.60.refs_5_.query_ref, bf16[192,512]{1,0:T(8,128)(2,1)S(1)} %get-tuple-element.62.grad_ref, ...), custom_call_target="tpu_custom_call" | custom-call | flops 1 | bytes 1 | tf_op jit(solution)/shard_map/key_grad/pallas_call | solution.py:50
  54.1 2.0 %collective-permute-done.20.refs_1_ = bf16[48,768]{1,0:T(8,128)(2,1)S(1)} collective-permute-done((bf16[48,768]{1,0:T(8,128)(2,1)S(1)}, bf16[48,768]{1,0:T(8,128)(2,1)S(1)}, u32[]{:S(2)}, u32[]{:S(2)}) %collective-permute-start.20) | collective-permute-done | bytes 73760 | tf_op jit(solution)/shard_map/ppermute | solution.py:337
  56.1 1.2 %collective-permute-start.21 = (bf16[48,768]{1,0:T(8,128)(2,1)S(1)}, bf16[48,768]{1,0:T(8,128)(2,1)S(1)}, u32[]{:S(2)}, u32[]{:S(2)}) collective-permute-start(bf16[48,768]{1,0:T(8,128)(2,1)S(1)} %add.3.refs_0_), channel_id=1, source_target_pairs={{4,0},{5,1},{6,2},{7,3},{0,4},{1,5},{2,6},{3,7},{12,8},{13,9},{14,... | collective-permute-start | bytes 221192 | tf_op jit(solution)/shard_map/ppermute | solution.py:337
  57.4 2.4 %key_grad.5 = (bf16[2,64,512]{2,1,0:T(8,128)(2,1)}, bf16[2,192,128]{2,1,0:T(8,128)(2,1)S(1)}, bf16[2,192,128]{2,1,0:T(8,128)(2,1)S(1)}, bf16[2,192,128]{2,1,0:T(...) custom-call(bf16[2,192,512]{2,1,0:T(8,128)(2,1)S(1)} %get-tuple-element.55.pair_ref, ...), custom_call_target="tpu_custom_call" | custom-call | flops 1 | bytes 1 | tf_op jit(solution)/shard_map/key_grad/pallas_call | solution.py:50
  59.8 3.1 %collective-permute-start.23 = (bf16[96,768]{1,0:T(8,128)(2,1)S(1)}, bf16[96,768]{1,0:T(8,128)(2,1)S(1)}, u32[]{:S(2)}, u32[]{:S(2)}) collective-permute-start(bf16[96,768]{1,0:T(8,128)(2,1)S(1)} %join.1.refs_0_), channel_id=1, source_target_pairs={{2,16},{3,17},{6,20},{7,21},{10,24},{11,25},{14,28},{15,29},{16,2}... | collective-permute-start | bytes 442376 | tf_op jit(solution)/shard_map/ppermute | solution.py:465
  62.9 4.4 %collective-permute-start.8 = (bf16[2,192,128]{2,1,0:T(8,128)(2,1)S(1)}, bf16[2,192,128]{2,1,0:T(8,128)(2,1)S(1)}, u32[]{:S(2)}, u32[]{:S(2)}) collective-permute-start(bf16[2,192,128]{2,1,0:T(8,128)(2,1)S(1)} %get-tuple-element.69), channel_id=1, source_target_pairs={{1,0},{0,1},{3,2},{2,3},{5,4},{4,5},{7,6},{6,7},{9,8},{8,9},{11,10... | collective-permute-start | bytes 294920 | tf_op jit(solution)/shard_map/ppermute | solution.py:337
  67.4 1.7 %collective-permute-start.9 = (bf16[2,192,128]{2,1,0:T(8,128)(2,1)S(1)}, bf16[2,192,128]{2,1,0:T(8,128)(2,1)S(1)}, u32[]{:S(2)}, u32[]{:S(2)}) collective-permute-start(bf16[2,192,128]{2,1,0:T(8,128)(2,1)S(1)} %get-tuple-element.70), channel_id=1, source_target_pairs={{2,0},{3,1},{0,2},{1,3},{6,4},{7,5},{4,6},{5,7},{10,8},{11,9},{8,1... | collective-permute-start | bytes 294920 | tf_op jit(solution)/shard_map/ppermute | solution.py:337
  69.1 3.1 %collective-permute-done.9.refs_2_ = bf16[2,192,128]{2,1,0:T(8,128)(2,1)S(1)} collective-permute-done((bf16[2,192,128]{2,1,0:T(8,128)(2,1)S(1)}, bf16[2,192,128]{2,1,0:T(8,128)(2,1)S(1)}, u32[]{:S(2)}, u32[]{:S(2)}) %collective-permute-start.9) | collective-permute-done | bytes 98336 | tf_op jit(solution)/shard_map/ppermute | solution.py:337
  72.2 3.6 %collective-permute-done.10.refs_3_ = bf16[2,192,128]{2,1,0:T(8,128)(2,1)S(1)} collective-permute-done((bf16[2,192,128]{2,1,0:T(8,128)(2,1)S(1)}, bf16[2,192,128]{2,1,0:T(8,128)(2,1)S(1)}, u32[]{:S(2)}, u32[]{:S(2)}) %collective-permute-start.10) | collective-permute-done | bytes 98336 | tf_op jit(solution)/shard_map/ppermute | solution.py:337
  75.8 1.1 %output.1 = (bf16[128,768]{1,0:T(8,128)(2,1)}, bf16[128,768]{1,0:T(8,128)(2,1)}, f32[8,128]{1,0:T(8,128)S(1)}) custom-call(bf16[2,192,128]{2,1,0:T(8,128)(2,1)S(1)} %get-tuple-element.68.refs_0_, bf16[2,192,128]{2,1,0:T(8,128)(2,1)S(1)} %collective-permute-done.8.refs_1_, bf16[2,192,128]{2,1,0:T(8,128)(2,1)S(1)} %collective-permute-done.9.refs_2_, ...), custom_call_target="tpu_custom_call" | custom-call | flops 1 | bytes 1 | tf_op jit(solution)/shard_map/output/pallas_call | solution.py:50
  77.0 0.5 collective-permute-start.15
  77.5 1.7 %collective-permute-start.17 = (bf16[2,192,128]{2,1,0:T(8,128)(2,1)S(1)}, bf16[2,192,128]{2,1,0:T(8,128)(2,1)S(1)}, u32[]{:S(2)}, u32[]{:S(2)}) collective-permute-start(bf16[2,192,128]{2,1,0:T(8,128)(2,1)S(1)} %get-tuple-element.84), channel_id=1, source_target_pairs={{3,0},{2,1},{1,2},{0,3},{7,4},{6,5},{5,6},{4,7},{11,8},{10,9},{9,1... | collective-permute-start | bytes 294920 | tf_op jit(solution)/shard_map/ppermute | solution.py:337
  79.2 2.7 %collective-permute-done.16.refs_2_ = bf16[2,192,128]{2,1,0:T(8,128)(2,1)S(1)} collective-permute-done((bf16[2,192,128]{2,1,0:T(8,128)(2,1)S(1)}, bf16[2,192,128]{2,1,0:T(8,128)(2,1)S(1)}, u32[]{:S(2)}, u32[]{:S(2)}) %collective-permute-start.16) | collective-permute-done | bytes 98336 | tf_op jit(solution)/shard_map/ppermute | solution.py:337
  81.9 2.3 %collective-permute-done.17.refs_3_ = bf16[2,192,128]{2,1,0:T(8,128)(2,1)S(1)} collective-permute-done((bf16[2,192,128]{2,1,0:T(8,128)(2,1)S(1)}, bf16[2,192,128]{2,1,0:T(8,128)(2,1)S(1)}, u32[]{:S(2)}, u32[]{:S(2)}) %collective-permute-start.17) | collective-permute-done | bytes 98336 | tf_op jit(solution)/shard_map/ppermute | solution.py:337
  84.1 0.9 %key_output.1 = (bf16[128,768]{1,0:T(8,128)(2,1)}, bf16[128,768]{1,0:T(8,128)(2,1)}) custom-call(bf16[2,192,128]{2,1,0:T(8,128)(2,1)S(1)} %get-tuple-element.81.refs_0_, bf16[2,192,128]{2,1,0:T(8,128)(2,1)S(1)} %collective-permute-done.15.refs_1_, bf16[2,192,128]{2,1,0:T(8,128)(2,1)S(1)} %collective-permute-done.16.refs_2_, ...), custom_call_target="tpu_custom_call" | custom-call | flops 1 | bytes 1 | tf_op jit(solution)/shard_map/key_output/pallas_call | solution.py:50
  85.0 1.1 %last.1 = f32[384,768]{1,0:T(8,128)} custom-call(bf16[192,768]{1,0:T(8,128)(2,1)S(1)} %cross.1.mine_ref, bf16[192,768]{1,0:T(8,128)(2,1)S(1)} %collective-permute-done.24.got_ref), custom_call_target="tpu_custom_call" | custom-call | flops 1 | bytes 1 | tf_op jit(solution)/shard_map/last/pallas_call | solution.py:50
  (28 shorter events, 0.5 us)
Async XLA Ops:
  0.6 24.1 %copy-start = (bf16[768,768]{1,0:T(8,128)(2,1)S(1)}, bf16[768,768]{1,0:T(8,128)(2,1)}, u32[]{:S(2)}) copy-start(bf16[768,768]{1,0:T(8,128)(2,1)} %refs_4_.3) | copy-start | bytes 3538948
  2.8 2.4 %collective-permute-start = (bf16[3,192,128]{2,1,0:T(8,128)(2,1)}, bf16[3,192,128]{2,1,0:T(8,128)(2,1)S(1)}, u32[]{:S(2)}, u32[]{:S(2)}) collective-permute-start(bf16[3,192,128]{2,1,0:T(8,128)(2,1)} %get-tuple-element.52), channel_id=1, source_target_pairs={{1,0},{0,1},{3,2},{2,3},{5,4},{4,5},{7,6},{6,7},{9,8},{8,9},{11,10... | collective-permute-start | bytes 442376 | tf_op jit(solution)/shard_map/ppermute | solution.py:337
  3.6 5.6 %collective-permute-start.1 = (bf16[3,192,128]{2,1,0:T(8,128)(2,1)}, bf16[3,192,128]{2,1,0:T(8,128)(2,1)S(1)}, u32[]{:S(2)}, u32[]{:S(2)}) collective-permute-start(bf16[3,192,128]{2,1,0:T(8,128)(2,1)} %get-tuple-element.53), channel_id=1, source_target_pairs={{2,0},{3,1},{0,2},{1,3},{6,4},{7,5},{4,6},{5,7},{10,8},{11,9},{8,1... | collective-permute-start | bytes 442376 | tf_op jit(solution)/shard_map/ppermute | solution.py:337
  3.6 9.0 %collective-permute-start.2 = (bf16[3,192,128]{2,1,0:T(8,128)(2,1)}, bf16[3,192,128]{2,1,0:T(8,128)(2,1)S(1)}, u32[]{:S(2)}, u32[]{:S(2)}) collective-permute-start(bf16[3,192,128]{2,1,0:T(8,128)(2,1)} %get-tuple-element.54), channel_id=1, source_target_pairs={{3,0},{2,1},{1,2},{0,3},{7,4},{6,5},{5,6},{4,7},{11,8},{10,9},{9,1... | collective-permute-start | bytes 442376 | tf_op jit(solution)/shard_map/ppermute | solution.py:337
  12.5 0.9 %copy-start.2 = (bf16[3,192,128]{2,1,0:T(8,128)(2,1)S(1)}, bf16[3,192,128]{2,1,0:T(8,128)(2,1)}, u32[]{:S(2)}) copy-start(bf16[3,192,128]{2,1,0:T(8,128)(2,1)} %get-tuple-element.51.refs_0_) | copy-start | bytes 442372
  13.6 7.7 %collective-permute-start.7 = (bf16[128,768]{1,0:T(8,128)(2,1)}, bf16[128,768]{1,0:T(8,128)(2,1)S(1)}, u32[]{:S(2)}, u32[]{:S(2)}) collective-permute-start(bf16[128,768]{1,0:T(8,128)(2,1)} %bitcast.8), channel_id=1, source_target_pairs={{3,0},{2,1},{1,2},{0,3},{7,4},{6,5},{5,6},{4,7},{11,8},{10,9},{9,1... | collective-permute-start | bytes 589832 | tf_op jit(solution)/shard_map/ppermute | solution.py:337
  14.0 10.8 %collective-permute-start.6 = (bf16[128,768]{1,0:T(8,128)(2,1)}, bf16[128,768]{1,0:T(8,128)(2,1)S(1)}, u32[]{:S(2)}, u32[]{:S(2)}) collective-permute-start(bf16[128,768]{1,0:T(8,128)(2,1)} %bitcast.9), channel_id=1, source_target_pairs={{2,0},{3,1},{0,2},{1,3},{6,4},{7,5},{4,6},{5,7},{10,8},{11,9},{8,1... | collective-permute-start | bytes 589832 | tf_op jit(solution)/shard_map/ppermute | solution.py:337
  15.3 9.5 %collective-permute-start.5 = (bf16[128,768]{1,0:T(8,128)(2,1)}, bf16[128,768]{1,0:T(8,128)(2,1)S(1)}, u32[]{:S(2)}, u32[]{:S(2)}) collective-permute-start(bf16[128,768]{1,0:T(8,128)(2,1)} %bitcast.10), channel_id=1, source_target_pairs={{1,0},{0,1},{3,2},{2,3},{5,4},{4,5},{7,6},{6,7},{9,8},{8,9},{11,10... | collective-permute-start | bytes 589832 | tf_op jit(solution)/shard_map/ppermute | solution.py:337
  15.8 15.5 %collective-permute-start.3 = (bf16[2,192,384]{2,1,0:T(8,128)(2,1)S(1)}, bf16[2,192,384]{2,1,0:T(8,128)(2,1)S(1)}, u32[]{:S(2)}, u32[]{:S(2)}) collective-permute-start(bf16[2,192,384]{2,1,0:T(8,128)(2,1)S(1)} %get-tuple-element.58), channel_id=1, source_target_pairs={{0,4},{1,5},{2,6},{3,7},{4,8},{5,9},{6,10},{7,11},{8,12},{9,13},{1... | collective-permute-start | bytes 884744 | tf_op jit(solution)/shard_map/ppermute | solution.py:343
  17.1 14.7 %collective-permute-start.4 = (bf16[2,192,384]{2,1,0:T(8,128)(2,1)S(1)}, bf16[2,192,384]{2,1,0:T(8,128)(2,1)S(1)}, u32[]{:S(2)}, u32[]{:S(2)}) collective-permute-start(bf16[2,192,384]{2,1,0:T(8,128)(2,1)S(1)} %get-tuple-element.59), channel_id=1, source_target_pairs={{0,12},{1,13},{2,14},{3,15},{4,0},{5,1},{6,2},{7,3},{8,4},{9,5},{1... | collective-permute-start | bytes 884744 | tf_op jit(solution)/shard_map/ppermute | solution.py:344
  24.8 0.9 %copy-start.1 = (bf16[1,1,128,768]{3,2,1,0:T(8,128)(2,1)S(1)}, bf16[1,1,128,768]{3,2,1,0:T(8,128)(2,1)}, u32[]{:S(2)}) copy-start(bf16[1,1,128,768]{3,2,1,0:T(8,128)(2,1)} %param.10) | copy-start | bytes 589828
  25.7 0.7 copy-start.3
  27.9 11.9 %collective-permute-start.11 = (bf16[2,192,384]{2,1,0:T(8,128)(2,1)S(1)}, bf16[2,192,384]{2,1,0:T(8,128)(2,1)S(1)}, u32[]{:S(2)}, u32[]{:S(2)}) collective-permute-start(bf16[2,192,384]{2,1,0:T(8,128)(2,1)S(1)} %get-tuple-element.74), channel_id=1, source_target_pairs={{0,4},{1,5},{2,6},{3,7},{4,8},{5,9},{6,10},{7,11},{8,12},{9,13},{1... | collective-permute-start | bytes 884744 | tf_op jit(solution)/shard_map/ppermute | solution.py:343
  29.2 15.1 %collective-permute-start.12 = (bf16[2,192,384]{2,1,0:T(8,128)(2,1)S(1)}, bf16[2,192,384]{2,1,0:T(8,128)(2,1)S(1)}, u32[]{:S(2)}, u32[]{:S(2)}) collective-permute-start(bf16[2,192,384]{2,1,0:T(8,128)(2,1)S(1)} %get-tuple-element.75), channel_id=1, source_target_pairs={{0,12},{1,13},{2,14},{3,15},{4,0},{5,1},{6,2},{7,3},{8,4},{9,5},{1... | collective-permute-start | bytes 884744 | tf_op jit(solution)/shard_map/ppermute | solution.py:344
  35.5 4.4 %collective-permute-start.18 = (bf16[96,768]{1,0:T(8,128)(2,1)S(1)}, bf16[96,768]{1,0:T(8,128)(2,1)S(1)}, u32[]{:S(2)}, u32[]{:S(2)}) collective-permute-start(bf16[96,768]{1,0:T(8,128)(2,1)S(1)} %get-tuple-element.89), channel_id=1, source_target_pairs={{0,16},{16,0},{1,17},{17,1},{2,18},{18,2},{3,19},{19,3},{4,20},{20... | collective-permute-start | bytes 442376 | tf_op jit(solution)/shard_map/ppermute | solution.py:348
  44.4 7.5 %collective-permute-start.19 = (bf16[48,768]{1,0:T(8,128)(2,1)S(1)}, bf16[48,768]{1,0:T(8,128)(2,1)S(1)}, u32[]{:S(2)}, u32[]{:S(2)}) collective-permute-start(bf16[48,768]{1,0:T(8,128)(2,1)S(1)} %get-tuple-element.92), channel_id=1, source_target_pairs={{4,0},{5,1},{6,2},{7,3},{0,4},{1,5},{2,6},{3,7},{12,8},{13,9},{14,... | collective-permute-start | bytes 221192 | tf_op jit(solution)/shard_map/ppermute | solution.py:337
  45.9 4.3 %collective-permute-start.13 = (f32[8,384]{1,0:T(8,128)S(1)}, f32[8,384]{1,0:T(8,128)S(1)}, u32[]{:S(2)}, u32[]{:S(2)}) collective-permute-start(f32[8,384]{1,0:T(8,128)S(1)} %get-tuple-element.76), channel_id=1, source_target_pairs={{0,4},{1,5},{2,6},{3,7},{4,8},{5,9},{6,10},{7,11},{8,12},{9,13},{1... | collective-permute-start | bytes 36872 | tf_op jit(solution)/shard_map/ppermute | solution.py:343
  46.0 4.2 %collective-permute-start.14 = (f32[8,384]{1,0:T(8,128)S(1)}, f32[8,384]{1,0:T(8,128)S(1)}, u32[]{:S(2)}, u32[]{:S(2)}) collective-permute-start(f32[8,384]{1,0:T(8,128)S(1)} %get-tuple-element.77), channel_id=1, source_target_pairs={{0,12},{1,13},{2,14},{3,15},{4,0},{5,1},{6,2},{7,3},{8,4},{9,5},{1... | collective-permute-start | bytes 36872 | tf_op jit(solution)/shard_map/ppermute | solution.py:344
  51.9 4.2 %collective-permute-start.20 = (bf16[48,768]{1,0:T(8,128)(2,1)S(1)}, bf16[48,768]{1,0:T(8,128)(2,1)S(1)}, u32[]{:S(2)}, u32[]{:S(2)}) collective-permute-start(bf16[48,768]{1,0:T(8,128)(2,1)S(1)} %add.2.refs_0_), channel_id=1, source_target_pairs={{8,0},{9,1},{10,2},{11,3},{12,4},{13,5},{14,6},{15,7},{0,8},{1,9},... | collective-permute-start | bytes 221192 | tf_op jit(solution)/shard_map/ppermute | solution.py:337
  56.1 3.6 %collective-permute-start.21 = (bf16[48,768]{1,0:T(8,128)(2,1)S(1)}, bf16[48,768]{1,0:T(8,128)(2,1)S(1)}, u32[]{:S(2)}, u32[]{:S(2)}) collective-permute-start(bf16[48,768]{1,0:T(8,128)(2,1)S(1)} %add.3.refs_0_), channel_id=1, source_target_pairs={{4,0},{5,1},{6,2},{7,3},{0,4},{1,5},{2,6},{3,7},{12,8},{13,9},{14,... | collective-permute-start | bytes 221192 | tf_op jit(solution)/shard_map/ppermute | solution.py:337
  59.8 17.1 %collective-permute-start.23 = (bf16[96,768]{1,0:T(8,128)(2,1)S(1)}, bf16[96,768]{1,0:T(8,128)(2,1)S(1)}, u32[]{:S(2)}, u32[]{:S(2)}) collective-permute-start(bf16[96,768]{1,0:T(8,128)(2,1)S(1)} %join.1.refs_0_), channel_id=1, source_target_pairs={{2,16},{3,17},{6,20},{7,21},{10,24},{11,25},{14,28},{15,29},{16,2}... | collective-permute-start | bytes 442376 | tf_op jit(solution)/shard_map/ppermute | solution.py:465
  62.9 14.0 %collective-permute-start.22 = (bf16[96,768]{1,0:T(8,128)(2,1)S(1)}, bf16[96,768]{1,0:T(8,128)(2,1)S(1)}, u32[]{:S(2)}, u32[]{:S(2)}) collective-permute-start(bf16[96,768]{1,0:T(8,128)(2,1)S(1)} %join.1.refs_0_), channel_id=1, source_target_pairs={{0,2},{1,3},{2,18},{3,19},{4,6},{5,7},{6,22},{7,23},{8,10},{9,11},... | collective-permute-start | bytes 442376 | tf_op jit(solution)/shard_map/ppermute | solution.py:465
  62.9 6.2 %collective-permute-start.8 = (bf16[2,192,128]{2,1,0:T(8,128)(2,1)S(1)}, bf16[2,192,128]{2,1,0:T(8,128)(2,1)S(1)}, u32[]{:S(2)}, u32[]{:S(2)}) collective-permute-start(bf16[2,192,128]{2,1,0:T(8,128)(2,1)S(1)} %get-tuple-element.69), channel_id=1, source_target_pairs={{1,0},{0,1},{3,2},{2,3},{5,4},{4,5},{7,6},{6,7},{9,8},{8,9},{11,10... | collective-permute-start | bytes 294920 | tf_op jit(solution)/shard_map/ppermute | solution.py:337
  67.4 4.8 %collective-permute-start.9 = (bf16[2,192,128]{2,1,0:T(8,128)(2,1)S(1)}, bf16[2,192,128]{2,1,0:T(8,128)(2,1)S(1)}, u32[]{:S(2)}, u32[]{:S(2)}) collective-permute-start(bf16[2,192,128]{2,1,0:T(8,128)(2,1)S(1)} %get-tuple-element.70), channel_id=1, source_target_pairs={{2,0},{3,1},{0,2},{1,3},{6,4},{7,5},{4,6},{5,7},{10,8},{11,9},{8,1... | collective-permute-start | bytes 294920 | tf_op jit(solution)/shard_map/ppermute | solution.py:337
  69.0 6.7 %collective-permute-start.10 = (bf16[2,192,128]{2,1,0:T(8,128)(2,1)S(1)}, bf16[2,192,128]{2,1,0:T(8,128)(2,1)S(1)}, u32[]{:S(2)}, u32[]{:S(2)}) collective-permute-start(bf16[2,192,128]{2,1,0:T(8,128)(2,1)S(1)} %get-tuple-element.71), channel_id=1, source_target_pairs={{3,0},{2,1},{1,2},{0,3},{7,4},{6,5},{5,6},{4,7},{11,8},{10,9},{9,1... | collective-permute-start | bytes 294920 | tf_op jit(solution)/shard_map/ppermute | solution.py:337
  76.9 8.1 %collective-permute-start.24 = (bf16[192,768]{1,0:T(8,128)(2,1)S(1)}, bf16[192,768]{1,0:T(8,128)(2,1)S(1)}, u32[]{:S(2)}, u32[]{:S(2)}) collective-permute-start(bf16[192,768]{1,0:T(8,128)(2,1)S(1)} %cross.1.mine_ref), channel_id=1, source_target_pairs={{1,0},{0,1},{3,2},{2,3},{5,4},{4,5},{7,6},{6,7},{9,8},{8,9},{11,10... | collective-permute-start | bytes 884744 | tf_op jit(solution)/shard_map/ppermute | solution.py:337
  77.0 2.2 %collective-permute-start.15 = (bf16[2,192,128]{2,1,0:T(8,128)(2,1)S(1)}, bf16[2,192,128]{2,1,0:T(8,128)(2,1)S(1)}, u32[]{:S(2)}, u32[]{:S(2)}) collective-permute-start(bf16[2,192,128]{2,1,0:T(8,128)(2,1)S(1)} %get-tuple-element.82), channel_id=1, source_target_pairs={{1,0},{0,1},{3,2},{2,3},{5,4},{4,5},{7,6},{6,7},{9,8},{8,9},{11,10... | collective-permute-start | bytes 294920 | tf_op jit(solution)/shard_map/ppermute | solution.py:337
  77.5 4.4 %collective-permute-start.16 = (bf16[2,192,128]{2,1,0:T(8,128)(2,1)S(1)}, bf16[2,192,128]{2,1,0:T(8,128)(2,1)S(1)}, u32[]{:S(2)}, u32[]{:S(2)}) collective-permute-start(bf16[2,192,128]{2,1,0:T(8,128)(2,1)S(1)} %get-tuple-element.83), channel_id=1, source_target_pairs={{2,0},{3,1},{0,2},{1,3},{6,4},{7,5},{4,6},{5,7},{10,8},{11,9},{8,1... | collective-permute-start | bytes 294920 | tf_op jit(solution)/shard_map/ppermute | solution.py:337
  77.5 6.6 %collective-permute-start.17 = (bf16[2,192,128]{2,1,0:T(8,128)(2,1)S(1)}, bf16[2,192,128]{2,1,0:T(8,128)(2,1)S(1)}, u32[]{:S(2)}, u32[]{:S(2)}) collective-permute-start(bf16[2,192,128]{2,1,0:T(8,128)(2,1)S(1)} %get-tuple-element.84), channel_id=1, source_target_pairs={{3,0},{2,1},{1,2},{0,3},{7,4},{6,5},{5,6},{4,7},{11,8},{10,9},{9,1... | collective-permute-start | bytes 294920 | tf_op jit(solution)/shard_map/ppermute | solution.py:337

commit v6 on v5

--- a/solution.py
+++ b/solution.py
@@ -72,49 +72,47 @@
     return max(0, j - 2 * HOPS), min(LAYER - 1, j)
 
 
-def pack_kernel(k_ref, v_ref, q_ref, *refs):
+def pack_kernel(k_ref, v_ref, *refs):
     outs, (natural, flipped, sems) = refs[:LAYER], refs[LAYER:]
     rows = outs[0].shape[1]
     copies = [
-        pltpu.make_async_copy(ref, natural.at[n], sems.at[n])
-        for n, ref in enumerate((k_ref, v_ref, q_ref))
+        pltpu.make_async_copy(ref, natural.at[n], sems.at[n]) for n, ref in enumerate((k_ref, v_ref))
     ]
     for copy in copies:
         copy.start()
-    scale = 1.0 / math.sqrt(flipped.shape[1] // HEADS)
     for n, copy in enumerate(copies):
         copy.wait()
-        value = natural[n].T
-        flipped[n] = value * bf16(scale) if n == 2 else value
+        flipped[n] = natural[n].T
     for peer, out in enumerate(outs):
         out[...] = flipped[:, place(peer, rows)]
 
 
+def project_kernel(q_ref, g_ref, weight_ref, *refs):
+    outs, (copy_ref, flipped) = refs[:LAYER], refs[LAYER:]
+    rows = outs[0].shape[1]
+    copy_ref[...] = g_ref[...]
+    flipped[0] = q_ref[...].T * bf16(1.0 / math.sqrt(flipped.shape[1] // HEADS))
+    flipped[1] = dot(weight_ref[...], g_ref[...], NT).astype(bf16)
+    for peer, out in enumerate(outs):
+        out[...] = flipped[:, place(peer, rows)]
+
+
+def pair_kernel(first_ref, second_ref, out_ref):
+    out_ref[0] = first_ref[...]
+    out_ref[1] = second_ref[...]
+
+
 def gather_kernel(*refs):
-    ins, (up_ref, down_ref, pair_ref, query_ref) = refs[:LAYER], refs[LAYER:]
+    ins, (up_ref, down_ref, pair_ref) = refs[:LAYER], refs[LAYER:]
     span = ins[0].shape[2]
     for peer, ref in enumerate(ins):
-        at = place(peer, span)
-        pair_ref[0, :, at] = ref[0]
-        pair_ref[1, :, at] = ref[1]
-        query_ref[:, at] = ref[2]
+        pair_ref[:, :, place(peer, span)] = ref[...]
     up_ref[...] = pair_ref[:, :, span:]
     down_ref[...] = pair_ref[:, :, : HOPS * span]
 
 
-def project_kernel(
-    station_count, ids_ref, count_ref, *refs
-):
-    ins, refs = refs[:LAYER], refs[LAYER:]
-    weight_ref, query_ref, all_ref, grad_ref, up_ref, down_ref, bias_ref, dead_ref = refs
-    span = ins[0].shape[0]
-    rows = query_ref.shape[0]
-    for peer, ref in enumerate(ins):
-        all_ref[place(peer, span)] = ref[...]
-    grad_ref[...] = dot(weight_ref[place(0, rows)], all_ref[...], NT).astype(bf16)
-    for n, ref in enumerate((query_ref, grad_ref)):
-        up_ref[n] = ref[:, span:]
-        down_ref[n] = ref[:, : HOPS * span]
+def live_kernel(station_count, ids_ref, count_ref, bias_ref, dead_ref):
+    span = bias_ref.shape[1] // LAYER
     first = lax.axis_index("station") // LAYER * LAYER
     ones = jnp.ones((1, span), f32)
 
@@ -150,12 +148,12 @@
 
 
 def forward_kernel(
-    pair_ref, low_ref, high_ref, query_ref, grad_ref, bias_ref,
+    pair_ref, low_ref, high_ref, query_ref, bias_ref,
     mixed_ref, stats_ref, stats_up, stats_down, probs_ref, window_ref,
     raw,
 ):
-    rows = query_ref.shape[0]
-    span = query_ref.shape[1] // LAYER
+    rows = query_ref.shape[1]
+    span = query_ref.shape[2] // LAYER
     head_width = rows // LOCAL
     reach = HOPS * span
     window_ref[:, :, :reach] = low_ref[...]
@@ -164,7 +162,7 @@
     for head in range(LOCAL):
         clear(probs_ref.at[head], span)
         at = block(head, head_width)
-        query = query_ref[at]
+        query = query_ref[0, at]
         tops = [None] * LAYER
         for j in range(BLOCKS):
             low, high = readers(j)
@@ -196,7 +194,7 @@
             ).astype(bf16)
         mixed = dot(window_ref[1, at], probs_ref[head], NN).astype(bf16)
         mixed_ref[at] = mixed
-        product = grad_ref[at].astype(f32) * mixed.astype(f32)
+        product = query_ref[1, at].astype(f32) * mixed.astype(f32)
         stats_ref[head : head + 1] = top + jnp.log(total)
         stats_ref[LOCAL + head : LOCAL + head + 1] = jnp.sum(product, 0, keepdims=True)
     stats_ref[2 * LOCAL :] = jnp.zeros((8 - 2 * LOCAL, LAYER * span), f32)
@@ -204,16 +202,16 @@
     stats_down[...] = stats_ref[:, :reach]
 
 
-def query_grad_kernel(window_ref, probs_ref, grad_ref, stats_ref, mixed_ref, *refs):
+def query_grad_kernel(window_ref, probs_ref, query_ref, stats_ref, mixed_ref, *refs):
     outs, (token_ref, grads, flipped) = refs[:LAYER], refs[LAYER:]
-    rows = grad_ref.shape[0]
-    span = grad_ref.shape[1] // LAYER
+    rows = query_ref.shape[1]
+    span = query_ref.shape[2] // LAYER
     head_width = rows // LOCAL
     scale = 1.0 / math.sqrt(head_width)
     clear(grads, span)
     for head in range(LOCAL):
         at = block(head, head_width)
-        grad = grad_ref[at]
+        grad = query_ref[1, at]
         delta = stats_ref[LOCAL + head : LOCAL + head + 1]
         for j in range(BLOCKS):
             low, high = readers(j)
@@ -229,20 +227,20 @@
 
 
 def key_grad_kernel(
-    head, pair_ref, query_ref, grad_ref, low_ref, high_ref, stats_ref, stats_low, stats_high,
+    head, pair_ref, query_ref, low_ref, high_ref, stats_ref, stats_low, stats_high,
     dead_ref, *refs
 ):
     before, refs = refs[:head], refs[head:]
     out_ref, refs = refs[0], refs[1:]
-    span = query_ref.shape[1] // LAYER
-    head_width = query_ref.shape[0] // LOCAL
+    span = query_ref.shape[2] // LAYER
+    head_width = query_ref.shape[1] // LOCAL
     at = block(head, head_width)
 
     def window(low, own, high):
         return jnp.concatenate([low, own, high], 1)
 
-    query = window(low_ref[0, at], query_ref[at], high_ref[0, at])
-    grad = window(low_ref[1, at], grad_ref[at], high_ref[1, at])
+    query = window(low_ref[0, at], query_ref[0, at], high_ref[0, at])
+    grad = window(low_ref[1, at], query_ref[1, at], high_ref[1, at])
     row = slice(head, head + 1)
     log_sum = window(stats_low[row], stats_ref[row], stats_high[row])
     row = slice(LOCAL + head, LOCAL + head + 1)
@@ -273,11 +271,12 @@
 
 
 def key_output_kernel(*refs):
-    ins, (dk_ref, dv_ref, flipped) = refs[:LAYER], refs[LAYER:]
+    ins, (dk_ref, dv_ref, token_ref, flipped) = refs[:LAYER], refs[LAYER:]
     for peer, ref in enumerate(ins):
         flipped[:, place(peer, ref.shape[1])] = ref[...]
     dk_ref[...] = flipped[0].T
     dv_ref[...] = flipped[1].T
+    token_ref[...] = jnp.zeros_like(token_ref)
 
 
 def halves(bit, half):
@@ -290,10 +289,13 @@
     return lax.rem(lax.axis_index("station") // stride, 2)
 
 
-def weight_kernel(mixed_ref, all_ref, send_ref, keep_ref):
+def weight_kernel(mixed_ref, mine_ref, sib_ref, send_ref, keep_ref, right):
+    for n in range(2):
+        right[place(2 * n, mine_ref.shape[1])] = mine_ref[n]
+        right[place(2 * n + 1, mine_ref.shape[1])] = sib_ref[n]
     send, keep = halves(lax.rem(lax.axis_index("dp"), 2), send_ref.shape[0])
-    send_ref[...] = dot(mixed_ref[send], all_ref[...], NN).astype(bf16)
-    keep_ref[...] = dot(mixed_ref[keep], all_ref[...], NN)
+    send_ref[...] = dot(mixed_ref[send], right[...], NN).astype(bf16)
+    keep_ref[...] = dot(mixed_ref[keep], right[...], NN)
 
 
 def split_kernel(stride, part_ref, got_ref, send_ref, keep_ref):
@@ -351,63 +353,73 @@
         return x.reshape(span, width)
 
     q, k, v, g = flat(query_states), flat(key_states), flat(value_states), flat(grad_output)
+    flat_shape = shape_of(span, width)
+    part_shape = shape_of(2, rows, span)
     reach_shape = shape_of(2, rows, HOPS * span)
-    layer_shape = shape_of(rows, LAYER * span)
+    layer_shape = shape_of(2, rows, LAYER * span)
+
+    def gather(parts, after=()):
+        return call(
+            gather_kernel, [VMEM] * LAYER, [reach_shape, reach_shape, layer_shape], parts,
+            name="gather", after=after,
+        )
+
     mine, *parts = call(
-        pack_kernel, [HBM] * 3, [shape_of(3, rows, span)] * LAYER, (k, v, q),
-        [pltpu.VMEM((3, span, width), bf16), pltpu.VMEM((3, width, span), bf16), dma((3,))],
+        pack_kernel, [HBM] * 2, [part_shape] * LAYER, (k, v),
+        [pltpu.VMEM((2, span, width), bf16), pltpu.VMEM((2, width, span), bf16), dma((2,))],
         limit=58, name="pack",
     )
-    parts = in_layer(parts)
-    up, down, pair, query = call(
-        gather_kernel, [VMEM] * LAYER,
-        [reach_shape, reach_shape, shape_of(2, rows, LAYER * span), layer_shape],
-        (mine, *parts), name="gather",
-    )
-    g_later, up, down = lax.optimization_barrier((g, up, down))
+    up, down, pair = gather((mine, *in_layer(parts)))
+    mine, *parts, g_copy = call(
+        project_kernel, [VMEM] * 3, [part_shape] * LAYER + [flat_shape],
+        (q, g, out_weight), [pltpu.VMEM((2, width, span), bf16)], name="project",
+    )
+    up, g_copy, *parts = lax.optimization_barrier((up, g_copy, *parts))
     kv_low, kv_high = along(up, down)
-    g_parts = in_layer([g_later] * 3)
-    all_grad, grad, up, down, bias, dead = call(
-        functools.partial(project_kernel, stations),
-        [SMEM] * 2 + [VMEM] * (LAYER + 2),
+    up, down, query = gather((mine, *in_layer(parts)))
+    qg_low, qg_high = along(up, down)
+    bias, dead = call(
+        functools.partial(live_kernel, stations), [SMEM] * 2,
         [
-            shape_of(LAYER * span, width), layer_shape, reach_shape, reach_shape,
             shape_of(16, LAYER * span, dtype=f32), shape_of(8, SLOTS * span, dtype=f32),
         ],
-        (partner_ids, partner_count, g, *g_parts, out_weight, query),
-        limit=16, name="project",
-    )
-    qg_low, qg_high = along(up, down)
+        (partner_ids, partner_count), name="live",
+    )
+    (g_pair,) = call(
+        pair_kernel, [VMEM] * 2, [shape_of(2, span, width)], (g_copy, swap(g_copy, 2)), name="pair",
+        after=(kv_low, kv_high, query, bias),
+    )
+    g_pairs = g_pair, swap(g_pair, 1)
     stats_shape = shape_of(8, HOPS * span, dtype=f32)
     mixed, stats, up, down, probs, window = call(
-        forward_kernel, [VMEM] * 6,
+        forward_kernel, [VMEM] * 5,
         [
-            layer_shape, shape_of(8, LAYER * span, dtype=f32), stats_shape, stats_shape,
+            shape_of(rows, LAYER * span), shape_of(8, LAYER * span, dtype=f32),
+            stats_shape, stats_shape,
             shape_of(LOCAL, BLOCKS * span, LAYER * span), shape_of(2, rows, BLOCKS * span),
         ],
-        (pair, kv_low, kv_high, query, grad, bias),
+        (pair, kv_low, kv_high, query, bias),
         [pltpu.VMEM((BLOCKS * span, LAYER * span), f32)],
         limit=20, name="forward",
     )
     stats_low, stats_high = along(up, down)
 
     send, part = call(
-        weight_kernel, [VMEM] * 2,
+        weight_kernel, [VMEM] * 3,
         [shape_of(rows // 2, width), shape_of(rows // 2, width, dtype=f32)],
-        (mixed, all_grad), name="weight",
-    )
-
-    part_shape = shape_of(2, rows, span)
+        (mixed, *g_pairs), [pltpu.VMEM((LAYER * span, width), bf16)], name="weight",
+    )
+
     mine, *parts, query_token = call(
         query_grad_kernel, [VMEM] * 5, [part_shape] * LAYER + [TOKEN],
-        (window, probs, grad, stats, mixed),
+        (window, probs, query, stats, mixed),
         [pltpu.VMEM((BLOCKS * span, LAYER * span), bf16), pltpu.VMEM((rows, LAYER * span), bf16)],
         limit=20, name="query_grad",
     )
-    parts = in_layer(parts)
+    query_parts = in_layer(parts)
     layer_output, grad_query, output_token = call(
-        output_kernel, [VMEM] * (LAYER + 1), [shape_of(span, width)] * 2 + [TOKEN],
-        (mine, *parts, out_weight), [pltpu.VMEM((2, width, span), bf16)], name="output",
+        output_kernel, [VMEM] * (LAYER + 1), [flat_shape] * 2 + [TOKEN],
+        (mine, *query_parts, out_weight), [pltpu.VMEM((2, width, span), bf16)], name="output",
     )
 
     before, key_tokens = [], []
@@ -415,17 +427,18 @@
         last = head == LOCAL - 1
         out, *parts, token = call(
             functools.partial(key_grad_kernel, head),
-            [VMEM] * (9 + len(before)),
+            [VMEM] * (8 + len(before)),
             [shape_of(2, rows // LOCAL, LAYER * span)] + [part_shape] * (LAYER * last) + [TOKEN],
-            (pair, query, grad, qg_low, qg_high, stats, stats_low, stats_high, dead, *before),
+            (pair, query, qg_low, qg_high, stats, stats_low, stats_high, dead, *before),
             limit=20, name="key_grad",
         )
         before.append(out)
         key_tokens.append(token)
     mine, *parts = parts
-    grad_key, grad_value = call(
-        key_output_kernel, [VMEM] * LAYER, [shape_of(span, width)] * 2,
-        (mine, *in_layer(parts)), [pltpu.VMEM((2, width, span), bf16)], name="key_output",
+    key_parts = in_layer(parts)
+    grad_key, grad_value, key_output_token = call(
+        key_output_kernel, [VMEM] * LAYER, [flat_shape] * 2 + [TOKEN],
+        (mine, *key_parts), [pltpu.VMEM((2, width, span), bf16)], name="key_output",
     )
 
     scale = 1.0 / math.sqrt(span * windows * stations)
@@ -435,21 +448,21 @@
         send, part = call(
             functools.partial(split_kernel, LAYER), [VMEM] * 2,
             [shape_of(count, width), shape_of(count, width, dtype=f32)],
-            (part, got), name="split", after=(query_token, qg_low, qg_high),
+            (part, got), name="split", after=(query_token, qg_low, qg_high, stats_low, stats_high),
         )
 
         def add_round(part, got, after=()):
             out = [shape_of(count, width)]
             return call(round_kernel, [VMEM] * 2, out, (part, got), name="add", after=after)[0]
 
-        total = add_round(part, swap(send, LAYER), key_tokens[:1])
+        total = add_round(part, swap(send, LAYER), key_tokens[:1] + query_parts)
         stride = 2 * LAYER
         while stride < stations:
-            total = add_round(total, swap(total, stride), key_tokens[1:2])
+            total = add_round(total, swap(total, stride), key_tokens[1:])
             stride *= 2
         (total,) = call(
             functools.partial(join_kernel, LAYER, None), [VMEM] * 2, [shape_of(2 * count, width)],
-            (total, swap(total, LAYER)), name="join", after=key_tokens[2:],
+            (total, swap(total, LAYER)), name="join", after=key_parts,
         )
         first, second = [], []
         for w in range(2):
@@ -471,6 +484,11 @@
         )
     else:
         start = lax.axis_index("station") % LAYER * rows
+        all_grad = jnp.zeros((LAYER * span, width), bf16)
+        for peer in range(LAYER):
+            value = g_pairs[peer % 2][peer // 2]
+            spot = lax.axis_index("station") % LAYER ^ peer
+            all_grad = lax.dynamic_update_slice_in_dim(all_grad, value, spot * span, 0)
         mine = dot(mixed, all_grad, NN).astype(bf16)
         whole = lax.dynamic_update_slice_in_dim(jnp.zeros((width, width), bf16), mine, start, 0)
         whole = lax.psum_scatter(whole, "dp", scatter_dimension=0, tiled=True)

time: 87.2 us -> 76.6 us (0.88)
  waiting for transfers between devices: 33.4 us -> 25.2 us
  starting transfers between devices: 30.7 us -> 28.5 us
    ppermute x16 -> x18, waiting for transfers between devices: 25.7 us -> 16.6 us  [swap(): lax.ppermute(value, 'station', [(s ^ stride, s) for s in range(stations)])]
    ppermute x3, waiting for transfers between devices: 5.09 us -> 0.63 us  [along(): lax.ppermute(down, 'station', [(s, (s - LAYER) % stations) for s in range...]
    ppermute x1, waiting for transfers between devices: 0.01 us -> 3.7 us  [local(): lax.ppermute(total, axes, second)]
    ppermute x16 -> x18, starting transfers between devices: 16.2 us -> 13.5 us  [swap(): lax.ppermute(value, 'station', [(s ^ stride, s) for s in range(stations)])]
    ppermute x3, waiting for transfers between devices: 1.08 us -> 3.63 us  [along(): lax.ppermute(up, 'station', [(s, (s + LAYER) % stations) for s in range(s...]
    ppermute x1, waiting for transfers between devices: 1.49 us -> 0.01 us  [other_window(): return lax.ppermute(value, 'dp', [(0, 1), (1, 0)])]
    ppermute x1, starting transfers between devices: 0.06 us -> 1.29 us  [local(): lax.ppermute(total, axes, first)]
    pallas_call x17 -> x20, Pallas kernels: 18 us -> 18.3 us  [call(): pl.pallas_call(kernel, in_specs=ins, out_specs=[VMEM] * len(outs), out_sh...]
  transfers between devices with their start and end apart: 25 -> 27, of which waited for: 13 -> 12; matrix products, arithmetic and copies ran while one was open for 1% -> 0% of each run, Pallas kernels for 17% -> 20%
where the time goes in v6:
time: 76.6 us; the launch traced here: 76 us
  starting transfers between devices  28.5 us (37%)
  waiting for transfers between devices  25.2 us (33%)
  Pallas kernels  18.3 us (24%)
  local copies, waits for them, and re-layouts  3.22 us (4%)
  between operations  0.86 us (1%)
    pallas_call x20, Pallas kernels, call(): pl.pallas_call(kernel, in_specs=ins, out_specs=[VMEM] * len(outs), out_sh...  18.3 us
    ppermute x18, waiting for transfers between devices, swap(): lax.ppermute(value, 'station', [(s ^ stride, s) for s in range(stations)])  16.6 us
    ppermute x18, starting transfers between devices, swap(): lax.ppermute(value, 'station', [(s ^ stride, s) for s in range(stations)])  13.5 us
    ppermute x3, starting transfers between devices, along(): lax.ppermute(down, 'station', [(s, (s - LAYER) % stations) for s in range...  7.77 us
    ppermute x1, waiting for transfers between devices, local(): lax.ppermute(total, axes, second)  3.7 us
    ppermute x3, waiting for transfers between devices, along(): lax.ppermute(up, 'station', [(s, (s + LAYER) % stations) for s in range(s...  3.63 us
    unnamed x15, local copies, waits for them, and re-layouts  3.22 us
    ppermute x1, starting transfers between devices, local(): lax.ppermute(total, axes, second)  2.42 us
  transfers between devices with their start and end apart: 27, of which 12 were waited for; matrix products, arithmetic and copies ran while one was open for 0% of the time, Pallas kernels for 20%

profile of v6, /device:TPU:3, one launch (start us, length us, event | category | flops | bytes accessed | tf_op | source)
XLA Modules:
  0.0 76.0 jit_solution(16108729358611819375)
XLA Ops:
  0.7 1.9 %pack.1 = (bf16[2,192,128]{2,1,0:T(8,128)(2,1)}, bf16[2,192,128]{2,1,0:T(8,128)(2,1)}, bf16[2,192,128]{2,1,0:T(8,128)(2,1)}, bf16[2,192,128]{2,1,0:T(8,128)(2,1)}) custom-call(bf16[128,768]{1,0:T(8,128)(2,1)} %bitcast.10, bf16[128,768]{1,0:T(8,128)(2,1)} %bitcast.11), custom_call_target="tpu_custom_call" | custom-call | flops 1 | bytes 1 | tf_op jit(solution)/shard_map/pack/pallas_call | solution.py:50
  2.6 0.7 collective-permute-start
  3.3 1.7 %collective-permute-start.2 = (bf16[2,192,128]{2,1,0:T(8,128)(2,1)}, bf16[2,192,128]{2,1,0:T(8,128)(2,1)S(1)}, u32[]{:S(2)}, u32[]{:S(2)}) collective-permute-start(bf16[2,192,128]{2,1,0:T(8,128)(2,1)} %get-tuple-element.59), channel_id=1, source_target_pairs={{3,0},{2,1},{1,2},{0,3},{7,4},{6,5},{5,6},{4,7},{11,8},{10,9},{9,1... | collective-permute-start | bytes 294920 | tf_op jit(solution)/shard_map/ppermute | solution.py:339
  5.0 1.3 %copy-done = bf16[768,768]{1,0:T(8,128)(2,1)S(1)} copy-done((bf16[768,768]{1,0:T(8,128)(2,1)S(1)}, bf16[768,768]{1,0:T(8,128)(2,1)}, u32[]{:S(2)}) %copy-start) | copy-done | bytes 1179672
  6.3 0.9 %copy-done.2 = bf16[1,1,128,768]{3,2,1,0:T(8,128)(2,1)S(1)} copy-done((bf16[1,1,128,768]{3,2,1,0:T(8,128)(2,1)S(1)}, bf16[1,1,128,768]{3,2,1,0:T(8,128)(2,1)}, u32[]{:S(2)}) %copy-start.2) | copy-done | bytes 196632
  7.2 0.9 %copy-done.3 = bf16[1,1,128,768]{3,2,1,0:T(8,128)(2,1)S(1)} copy-done((bf16[1,1,128,768]{3,2,1,0:T(8,128)(2,1)S(1)}, bf16[1,1,128,768]{3,2,1,0:T(8,128)(2,1)}, u32[]{:S(2)}) %copy-start.3) | copy-done | bytes 196632
  8.2 0.5 project.1
  8.7 1.5 %collective-permute-done.2.refs_3_ = bf16[2,192,128]{2,1,0:T(8,128)(2,1)S(1)} collective-permute-done((bf16[2,192,128]{2,1,0:T(8,128)(2,1)}, bf16[2,192,128]{2,1,0:T(8,128)(2,1)S(1)}, u32[]{:S(2)}, u32[]{:S(2)}) %collective-permute-start.2) | collective-permute-done | bytes 98336 | tf_op jit(solution)/shard_map/ppermute | solution.py:339
  10.3 1.3 %collective-permute-start.3 = (bf16[2,192,384]{2,1,0:T(8,128)(2,1)S(1)}, bf16[2,192,384]{2,1,0:T(8,128)(2,1)S(1)}, u32[]{:S(2)}, u32[]{:S(2)}) collective-permute-start(bf16[2,192,384]{2,1,0:T(8,128)(2,1)S(1)} %get-tuple-element.66), channel_id=1, source_target_pairs={{0,4},{1,5},{2,6},{3,7},{4,8},{5,9},{6,10},{7,11},{8,12},{9,13},{1... | collective-permute-start | bytes 884744 | tf_op jit(solution)/shard_map/ppermute | solution.py:345
  11.7 2.1 %collective-permute-start.4 = (bf16[2,192,384]{2,1,0:T(8,128)(2,1)S(1)}, bf16[2,192,384]{2,1,0:T(8,128)(2,1)S(1)}, u32[]{:S(2)}, u32[]{:S(2)}) collective-permute-start(bf16[2,192,384]{2,1,0:T(8,128)(2,1)S(1)} %get-tuple-element.67), channel_id=1, source_target_pairs={{0,12},{1,13},{2,14},{3,15},{4,0},{5,1},{6,2},{7,3},{8,4},{9,5},{1... | collective-permute-start | bytes 884744 | tf_op jit(solution)/shard_map/ppermute | solution.py:346
  13.8 0.7 collective-permute-start.5
  14.6 1.3 %collective-permute-start.6 = (bf16[2,192,128]{2,1,0:T(8,128)(2,1)S(1)}, bf16[2,192,128]{2,1,0:T(8,128)(2,1)S(1)}, u32[]{:S(2)}, u32[]{:S(2)}) collective-permute-start(bf16[2,192,128]{2,1,0:T(8,128)(2,1)S(1)} %get-tuple-element.70), channel_id=1, source_target_pairs={{2,0},{3,1},{0,2},{1,3},{6,4},{7,5},{4,6},{5,7},{10,8},{11,9},{8,1... | collective-permute-start | bytes 294920 | tf_op jit(solution)/shard_map/ppermute | solution.py:339
  15.9 0.6 collective-permute-start.7
  16.6 1.4 %live.1 = (f32[16,512]{1,0:T(8,128)S(1)}, f32[8,896]{1,0:T(8,128)S(1)}) custom-call(s32[16,6]{1,0:T(8,128)S(1)} %copy.12.ids_ref, s32[16]{0:T(128)S(1)} %copy-done.5), custom_call_target="tpu_custom_call" | custom-call | flops 1 | bytes 1 | tf_op jit(solution)/shard_map/live/pallas_call | solution.py:50
  18.0 5.0 %collective-permute-done.6.refs_2_ = bf16[2,192,128]{2,1,0:T(8,128)(2,1)S(1)} collective-permute-done((bf16[2,192,128]{2,1,0:T(8,128)(2,1)S(1)}, bf16[2,192,128]{2,1,0:T(8,128)(2,1)S(1)}, u32[]{:S(2)}, u32[]{:S(2)}) %collective-permute-start.6) | collective-permute-done | bytes 98336 | tf_op jit(solution)/shard_map/ppermute | solution.py:339
  23.1 2.5 %collective-permute-done.7.refs_3_ = bf16[2,192,128]{2,1,0:T(8,128)(2,1)S(1)} collective-permute-done((bf16[2,192,128]{2,1,0:T(8,128)(2,1)S(1)}, bf16[2,192,128]{2,1,0:T(8,128)(2,1)S(1)}, u32[]{:S(2)}, u32[]{:S(2)}) %collective-permute-start.7) | collective-permute-done | bytes 98336 | tf_op jit(solution)/shard_map/ppermute | solution.py:339
  25.7 0.6 collective-permute-done.4.high_ref.refs_3_
  26.4 1.1 %collective-permute-start.19 = (bf16[2,128,768]{2,1,0:T(8,128)(2,1)S(1)}, bf16[2,128,768]{2,1,0:T(8,128)(2,1)S(1)}, u32[]{:S(2)}, u32[]{:S(2)}) collective-permute-start(bf16[2,128,768]{2,1,0:T(8,128)(2,1)S(1)} %pair.1.mine_ref), channel_id=1, source_target_pairs={{1,0},{0,1},{3,2},{2,3},{5,4},{4,5},{7,6},{6,7},{9,8},{8,9},{11,10... | collective-permute-start | bytes 1179656 | tf_op jit(solution)/shard_map/ppermute | solution.py:339
  27.5 0.8 %collective-permute-start.11 = (bf16[2,192,384]{2,1,0:T(8,128)(2,1)S(1)}, bf16[2,192,384]{2,1,0:T(8,128)(2,1)S(1)}, u32[]{:S(2)}, u32[]{:S(2)}) collective-permute-start(bf16[2,192,384]{2,1,0:T(8,128)(2,1)S(1)} %get-tuple-element.84), channel_id=1, source_target_pairs={{0,4},{1,5},{2,6},{3,7},{4,8},{5,9},{6,10},{7,11},{8,12},{9,13},{1... | collective-permute-start | bytes 884744 | tf_op jit(solution)/shard_map/ppermute | solution.py:345
  28.4 2.4 %collective-permute-start.12 = (bf16[2,192,384]{2,1,0:T(8,128)(2,1)S(1)}, bf16[2,192,384]{2,1,0:T(8,128)(2,1)S(1)}, u32[]{:S(2)}, u32[]{:S(2)}) collective-permute-start(bf16[2,192,384]{2,1,0:T(8,128)(2,1)S(1)} %get-tuple-element.85), channel_id=1, source_target_pairs={{0,12},{1,13},{2,14},{3,15},{4,0},{5,1},{6,2},{7,3},{8,4},{9,5},{1... | collective-permute-start | bytes 884744 | tf_op jit(solution)/shard_map/ppermute | solution.py:346
  30.8 3.2 %forward.1 = (bf16[192,512]{1,0:T(8,128)(2,1)S(1)}, f32[8,512]{1,0:T(8,128)S(1)}, f32[8,384]{1,0:T(8,128)S(1)}, f32[8,384]{1,0:T(8,128)S(1)}, bf16[3,1280,512]{2...) custom-call(bf16[2,192,512]{2,1,0:T(8,128)(2,1)S(1)} %get-tuple-element.60.pair_ref, ...), custom_call_target="tpu_custom_call" | custom-call | flops 1 | bytes 1 | tf_op jit(solution)/shard_map/forward/pallas_call | solution.py:50
  34.0 0.5 weight.1
  34.5 1.3 %collective-permute-start.20 = (bf16[96,768]{1,0:T(8,128)(2,1)S(1)}, bf16[96,768]{1,0:T(8,128)(2,1)S(1)}, u32[]{:S(2)}, u32[]{:S(2)}) collective-permute-start(bf16[96,768]{1,0:T(8,128)(2,1)S(1)} %get-tuple-element.99), channel_id=1, source_target_pairs={{0,16},{16,0},{1,17},{17,1},{2,18},{18,2},{3,19},{19,3},{4,20},{20... | collective-permute-start | bytes 442376 | tf_op jit(solution)/shard_map/ppermute | solution.py:350
  35.8 3.3 %collective-permute-start.14 = (f32[8,384]{1,0:T(8,128)S(1)}, f32[8,384]{1,0:T(8,128)S(1)}, u32[]{:S(2)}, u32[]{:S(2)}) collective-permute-start(f32[8,384]{1,0:T(8,128)S(1)} %get-tuple-element.87), channel_id=1, source_target_pairs={{0,12},{1,13},{2,14},{3,15},{4,0},{5,1},{6,2},{7,3},{8,4},{9,5},{1... | collective-permute-start | bytes 36872 | tf_op jit(solution)/shard_map/ppermute | solution.py:346
  39.0 1.6 %query_grad.1 = (bf16[2,192,128]{2,1,0:T(8,128)(2,1)S(1)}, bf16[2,192,128]{2,1,0:T(8,128)(2,1)S(1)}, bf16[2,192,128]{2,1,0:T(8,128)(2,1)S(1)}, bf16[2,192,128]{2,1,0:T(8,128)(2,1)S(1)}, f32[8,128]{1,0:T(8,128)S(1)}) custom-call(bf16[2,192,1280]{2,1,0:T(8,128)(2,1)S(1)} %get-tuple-element.74.window_ref, ...), custom_call_target="tpu_custom_call" | custom-call | flops 1 | bytes 1 | tf_op jit(solution)/shard_map/query_grad/pallas_call | solution.py:50
  40.6 3.6 %collective-permute-done.13.stats_low.refs_5_ = f32[8,384]{1,0:T(8,128)S(1)} collective-permute-done((f32[8,384]{1,0:T(8,128)S(1)}, f32[8,384]{1,0:T(8,128)S(1)}, u32[]{:S(2)}, u32[]{:S(2)}) %collective-permute-start.13) | collective-permute-done | bytes 12320 | tf_op jit(solution)/shard_map/ppermute | solution.py:345
  44.2 1.3 %collective-permute-start.8 = (bf16[2,192,128]{2,1,0:T(8,128)(2,1)S(1)}, bf16[2,192,128]{2,1,0:T(8,128)(2,1)S(1)}, u32[]{:S(2)}, u32[]{:S(2)}) collective-permute-start(bf16[2,192,128]{2,1,0:T(8,128)(2,1)S(1)} %get-tuple-element.79), channel_id=1, source_target_pairs={{1,0},{0,1},{3,2},{2,3},{5,4},{4,5},{7,6},{6,7},{9,8},{8,9},{11,10... | collective-permute-start | bytes 294920 | tf_op jit(solution)/shard_map/ppermute | solution.py:339
  45.8 1.4 %collective-permute-start.10 = (bf16[2,192,128]{2,1,0:T(8,128)(2,1)S(1)}, bf16[2,192,128]{2,1,0:T(8,128)(2,1)S(1)}, u32[]{:S(2)}, u32[]{:S(2)}) collective-permute-start(bf16[2,192,128]{2,1,0:T(8,128)(2,1)S(1)} %get-tuple-element.81), channel_id=1, source_target_pairs={{3,0},{2,1},{1,2},{0,3},{7,4},{6,5},{5,6},{4,7},{11,8},{10,9},{9,1... | collective-permute-start | bytes 294920 | tf_op jit(solution)/shard_map/ppermute | solution.py:339
  47.3 1.7 %key_grad.3 = (bf16[2,64,512]{2,1,0:T(8,128)(2,1)S(1)}, f32[8,128]{1,0:T(8,128)S(1)}) custom-call(bf16[2,192,512]{2,1,0:T(8,128)(2,1)S(1)} %get-tuple-element.60.pair_ref, bf16[2,192,512]{2,1,0:T(8,128)(2,1)S(1)} %get-tuple-element.72.query_ref.refs_4_, bf16[2,192,384]{2,1,0:T(8,128)(2,1)S(1)} %collective-permute-done.11.low_ref.refs_3_, ...), custom_call_target="tpu_custom_call" | custom-call | flops 1 | bytes 1 | tf_op jit(solution)/shard_map/key_grad/pallas_call | solution.py:50
  49.0 1.0 %collective-permute-done.9.refs_2_.refs_4_ = bf16[2,192,128]{2,1,0:T(8,128)(2,1)S(1)} collective-permute-done((bf16[2,192,128]{2,1,0:T(8,128)(2,1)S(1)}, bf16[2,192,128]{2,1,0:T(8,128)(2,1)S(1)}, u32[]{:S(2)}, u32[]{:S(2)}) %collective-permute-start.9) | collective-permute-done | bytes 98336 | tf_op jit(solution)/shard_map/ppermute | solution.py:339
  49.9 2.2 %collective-permute-done.10.refs_3_.refs_5_ = bf16[2,192,128]{2,1,0:T(8,128)(2,1)S(1)} collective-permute-done((bf16[2,192,128]{2,1,0:T(8,128)(2,1)S(1)}, bf16[2,192,128]{2,1,0:T(8,128)(2,1)S(1)}, u32[]{:S(2)}, u32[]{:S(2)}) %collective-permute-start.10) | collective-permute-done | bytes 98336 | tf_op jit(solution)/shard_map/ppermute | solution.py:339
  52.2 1.7 %key_grad.4 = (bf16[2,64,512]{2,1,0:T(8,128)(2,1)S(1)}, f32[8,128]{1,0:T(8,128)S(1)}) custom-call(bf16[2,192,512]{2,1,0:T(8,128)(2,1)S(1)} %get-tuple-element.60.pair_ref, bf16[2,192,512]{2,1,0:T(8,128)(2,1)S(1)} %get-tuple-element.72.query_ref.refs_4_, bf16[2,192,384]{2,1,0:T(8,128)(2,1)S(1)} %collective-permute-done.11.low_ref.refs_3_, ...), custom_call_target="tpu_custom_call" | custom-call | flops 1 | bytes 1 | tf_op jit(solution)/shard_map/key_grad/pallas_call | solution.py:50
  53.9 2.4 %key_grad.5 = (bf16[2,64,512]{2,1,0:T(8,128)(2,1)}, bf16[2,192,128]{2,1,0:T(8,128)(2,1)S(1)}, bf16[2,192,128]{2,1,0:T(8,128)(2,1)S(1)}, bf16[2,192,128]{2,1,0:T(...) custom-call(bf16[2,192,512]{2,1,0:T(8,128)(2,1)S(1)} %get-tuple-element.60.pair_ref, ...), custom_call_target="tpu_custom_call" | custom-call | flops 1 | bytes 1 | tf_op jit(solution)/shard_map/key_grad/pallas_call | solution.py:50
  56.3 0.3 collective-permute-start.15
  56.6 0.6 collective-permute-start.16
  57.2 1.3 %collective-permute-start.17 = (bf16[2,192,128]{2,1,0:T(8,128)(2,1)S(1)}, bf16[2,192,128]{2,1,0:T(8,128)(2,1)S(1)}, u32[]{:S(2)}, u32[]{:S(2)}) collective-permute-start(bf16[2,192,128]{2,1,0:T(8,128)(2,1)S(1)} %get-tuple-element.94), channel_id=1, source_target_pairs={{3,0},{2,1},{1,2},{0,3},{7,4},{6,5},{5,6},{4,7},{11,8},{10,9},{9,1... | collective-permute-start | bytes 294920 | tf_op jit(solution)/shard_map/ppermute | solution.py:339
  58.4 0.7 collective-permute-start.23
  59.2 1.6 %collective-permute-done.16.refs_2_.refs_3_ = bf16[2,192,128]{2,1,0:T(8,128)(2,1)S(1)} collective-permute-done((bf16[2,192,128]{2,1,0:T(8,128)(2,1)S(1)}, bf16[2,192,128]{2,1,0:T(8,128)(2,1)S(1)}, u32[]{:S(2)}, u32[]{:S(2)}) %collective-permute-start.16) | collective-permute-done | bytes 98336 | tf_op jit(solution)/shard_map/ppermute | solution.py:339
  60.8 2.4 %collective-permute-done.17.refs_3_.refs_4_ = bf16[2,192,128]{2,1,0:T(8,128)(2,1)S(1)} collective-permute-done((bf16[2,192,128]{2,1,0:T(8,128)(2,1)S(1)}, bf16[2,192,128]{2,1,0:T(8,128)(2,1)S(1)}, u32[]{:S(2)}, u32[]{:S(2)}) %collective-permute-start.17) | collective-permute-done | bytes 98336 | tf_op jit(solution)/shard_map/ppermute | solution.py:339
  63.2 1.3 %collective-permute-start.24 = (bf16[96,768]{1,0:T(8,128)(2,1)S(1)}, bf16[96,768]{1,0:T(8,128)(2,1)S(1)}, u32[]{:S(2)}, u32[]{:S(2)}) collective-permute-start(bf16[96,768]{1,0:T(8,128)(2,1)S(1)} %join.1.refs_0_), channel_id=1, source_target_pairs={{0,2},{1,3},{2,18},{3,19},{4,6},{5,7},{6,22},{7,23},{8,10},{9,11},... | collective-permute-start | bytes 442376 | tf_op jit(solution)/shard_map/ppermute | solution.py:478
  64.5 2.4 %collective-permute-start.25 = (bf16[96,768]{1,0:T(8,128)(2,1)S(1)}, bf16[96,768]{1,0:T(8,128)(2,1)S(1)}, u32[]{:S(2)}, u32[]{:S(2)}) collective-permute-start(bf16[96,768]{1,0:T(8,128)(2,1)S(1)} %join.1.refs_0_), channel_id=1, source_target_pairs={{2,16},{3,17},{6,20},{7,21},{10,24},{11,25},{14,28},{15,29},{16,2}... | collective-permute-start | bytes 442376 | tf_op jit(solution)/shard_map/ppermute | solution.py:478
  67.0 1.1 %output.1 = (bf16[128,768]{1,0:T(8,128)(2,1)}, bf16[128,768]{1,0:T(8,128)(2,1)}, f32[8,128]{1,0:T(8,128)S(1)}) custom-call(bf16[2,192,128]{2,1,0:T(8,128)(2,1)S(1)} %get-tuple-element.78.refs_0_, bf16[2,192,128]{2,1,0:T(8,128)(2,1)S(1)} %collective-permute-done.8.refs_1_.refs_3_, bf16[2,192,128]{2,1,0:T(8,128)(2,1)S(1)} %collective-permute-done.9.refs_2_.refs_4_, ...), custom_call_target="tpu_custom_call" | custom-call | flops 1 | bytes 1 | tf_op jit(solution)/shard_map/output/pallas_call | solution.py:50
  68.1 0.6 collective-permute-done.24.refs_1_
  68.7 3.7 %collective-permute-done.25.refs_2_ = bf16[96,768]{1,0:T(8,128)(2,1)S(1)} collective-permute-done((bf16[96,768]{1,0:T(8,128)(2,1)S(1)}, bf16[96,768]{1,0:T(8,128)(2,1)S(1)}, u32[]{:S(2)}, u32[]{:S(2)}) %collective-permute-start.25) | collective-permute-done | bytes 147488 | tf_op jit(solution)/shard_map/ppermute | solution.py:478
  72.4 1.2 %collective-permute-start.26 = (bf16[192,768]{1,0:T(8,128)(2,1)S(1)}, bf16[192,768]{1,0:T(8,128)(2,1)S(1)}, u32[]{:S(2)}, u32[]{:S(2)}) collective-permute-start(bf16[192,768]{1,0:T(8,128)(2,1)S(1)} %cross.1.mine_ref), channel_id=1, source_target_pairs={{1,0},{0,1},{3,2},{2,3},{5,4},{4,5},{7,6},{6,7},{9,8},{8,9},{11,10... | collective-permute-start | bytes 884744 | tf_op jit(solution)/shard_map/ppermute | solution.py:339
  73.7 0.9 %key_output.1 = (bf16[128,768]{1,0:T(8,128)(2,1)}, bf16[128,768]{1,0:T(8,128)(2,1)}, f32[8,128]{1,0:T(8,128)}) custom-call(bf16[2,192,128]{2,1,0:T(8,128)(2,1)S(1)} %get-tuple-element.91.refs_0_, bf16[2,192,128]{2,1,0:T(8,128)(2,1)S(1)} %collective-permute-done.15.refs_1_.refs_2_, bf16[2,192,128]{2,1,0:T(8,128)(2,1)S(1)} %collective-permute-done.16.refs_2_.refs_3_, ...), custom_call_target="tpu_custom_call" | custom-call | flops 1 | bytes 1 | tf_op jit(solution)/shard_map/key_output/pallas_call | solution.py:50
  74.6 0.3 collective-permute-done.26.got_ref
  74.9 1.1 %last.1 = f32[384,768]{1,0:T(8,128)} custom-call(bf16[192,768]{1,0:T(8,128)(2,1)S(1)} %cross.1.mine_ref, bf16[192,768]{1,0:T(8,128)(2,1)S(1)} %collective-permute-done.26.got_ref), custom_call_target="tpu_custom_call" | custom-call | flops 1 | bytes 1 | tf_op jit(solution)/shard_map/last/pallas_call | solution.py:50
  (41 shorter events, 1.2 us)
Async XLA Ops:
  0.6 15.9 %copy-start.6 = (s32[16,6]{0,1:T(8,128)S(1)}, s32[16,6]{0,1:T(8,128)}, u32[]{:S(2)}) copy-start(s32[16,6]{0,1:T(8,128)} %param.12) | copy-start | bytes 1156
  0.6 16.0 %copy-start.5 = (s32[16]{0:T(128)S(1)}, s32[16]{0:T(128)}, u32[]{:S(2)}) copy-start(s32[16]{0:T(128)} %count_ref.1) | copy-start | bytes 196
  2.6 6.1 %collective-permute-start = (bf16[2,192,128]{2,1,0:T(8,128)(2,1)}, bf16[2,192,128]{2,1,0:T(8,128)(2,1)S(1)}, u32[]{:S(2)}, u32[]{:S(2)}) collective-permute-start(bf16[2,192,128]{2,1,0:T(8,128)(2,1)} %get-tuple-element.57), channel_id=1, source_target_pairs={{1,0},{0,1},{3,2},{2,3},{5,4},{4,5},{7,6},{6,7},{9,8},{8,9},{11,10... | collective-permute-start | bytes 294920 | tf_op jit(solution)/shard_map/ppermute | solution.py:339
  3.3 5.4 %collective-permute-start.1 = (bf16[2,192,128]{2,1,0:T(8,128)(2,1)}, bf16[2,192,128]{2,1,0:T(8,128)(2,1)S(1)}, u32[]{:S(2)}, u32[]{:S(2)}) collective-permute-start(bf16[2,192,128]{2,1,0:T(8,128)(2,1)} %get-tuple-element.58), channel_id=1, source_target_pairs={{2,0},{3,1},{0,2},{1,3},{6,4},{7,5},{4,6},{5,7},{10,8},{11,9},{8,1... | collective-permute-start | bytes 294920 | tf_op jit(solution)/shard_map/ppermute | solution.py:339
  3.3 6.8 %collective-permute-start.2 = (bf16[2,192,128]{2,1,0:T(8,128)(2,1)}, bf16[2,192,128]{2,1,0:T(8,128)(2,1)S(1)}, u32[]{:S(2)}, u32[]{:S(2)}) collective-permute-start(bf16[2,192,128]{2,1,0:T(8,128)(2,1)} %get-tuple-element.59), channel_id=1, source_target_pairs={{3,0},{2,1},{1,2},{0,3},{7,4},{6,5},{5,6},{4,7},{11,8},{10,9},{9,1... | collective-permute-start | bytes 294920 | tf_op jit(solution)/shard_map/ppermute | solution.py:339
  5.0 1.3 %copy-start = (bf16[768,768]{1,0:T(8,128)(2,1)S(1)}, bf16[768,768]{1,0:T(8,128)(2,1)}, u32[]{:S(2)}) copy-start(bf16[768,768]{1,0:T(8,128)(2,1)} %refs_4_.1) | copy-start | bytes 3538948
  6.3 0.9 %copy-start.2 = (bf16[1,1,128,768]{3,2,1,0:T(8,128)(2,1)S(1)}, bf16[1,1,128,768]{3,2,1,0:T(8,128)(2,1)}, u32[]{:S(2)}) copy-start(bf16[1,1,128,768]{3,2,1,0:T(8,128)(2,1)} %param.7) | copy-start | bytes 589828
  7.2 0.9 %copy-start.3 = (bf16[1,1,128,768]{3,2,1,0:T(8,128)(2,1)S(1)}, bf16[1,1,128,768]{3,2,1,0:T(8,128)(2,1)}, u32[]{:S(2)}) copy-start(bf16[1,1,128,768]{3,2,1,0:T(8,128)(2,1)} %param.10) | copy-start | bytes 589828
  8.2 2.0 %copy-start.4 = (bf16[2,192,128]{2,1,0:T(8,128)(2,1)S(1)}, bf16[2,192,128]{2,1,0:T(8,128)(2,1)}, u32[]{:S(2)}) copy-start(bf16[2,192,128]{2,1,0:T(8,128)(2,1)} %get-tuple-element.56.refs_0_) | copy-start | bytes 294916
  10.3 15.4 %collective-permute-start.3 = (bf16[2,192,384]{2,1,0:T(8,128)(2,1)S(1)}, bf16[2,192,384]{2,1,0:T(8,128)(2,1)S(1)}, u32[]{:S(2)}, u32[]{:S(2)}) collective-permute-start(bf16[2,192,384]{2,1,0:T(8,128)(2,1)S(1)} %get-tuple-element.66), channel_id=1, source_target_pairs={{0,4},{1,5},{2,6},{3,7},{4,8},{5,9},{6,10},{7,11},{8,12},{9,13},{1... | collective-permute-start | bytes 884744 | tf_op jit(solution)/shard_map/ppermute | solution.py:345
  11.7 14.7 %collective-permute-start.4 = (bf16[2,192,384]{2,1,0:T(8,128)(2,1)S(1)}, bf16[2,192,384]{2,1,0:T(8,128)(2,1)S(1)}, u32[]{:S(2)}, u32[]{:S(2)}) collective-permute-start(bf16[2,192,384]{2,1,0:T(8,128)(2,1)S(1)} %get-tuple-element.67), channel_id=1, source_target_pairs={{0,12},{1,13},{2,14},{3,15},{4,0},{5,1},{6,2},{7,3},{8,4},{9,5},{1... | collective-permute-start | bytes 884744 | tf_op jit(solution)/shard_map/ppermute | solution.py:346
  13.8 2.1 %collective-permute-start.5 = (bf16[2,192,128]{2,1,0:T(8,128)(2,1)S(1)}, bf16[2,192,128]{2,1,0:T(8,128)(2,1)S(1)}, u32[]{:S(2)}, u32[]{:S(2)}) collective-permute-start(bf16[2,192,128]{2,1,0:T(8,128)(2,1)S(1)} %get-tuple-element.69), channel_id=1, source_target_pairs={{1,0},{0,1},{3,2},{2,3},{5,4},{4,5},{7,6},{6,7},{9,8},{8,9},{11,10... | collective-permute-start | bytes 294920 | tf_op jit(solution)/shard_map/ppermute | solution.py:339
  14.4 11.3 %collective-permute-start.18 = (bf16[128,768]{1,0:T(8,128)(2,1)S(1)}, bf16[128,768]{1,0:T(8,128)(2,1)S(1)}, u32[]{:S(2)}, u32[]{:S(2)}) collective-permute-start(bf16[128,768]{1,0:T(8,128)(2,1)S(1)} %get-tuple-element.97.refs_0_), channel_id=1, source_target_pairs={{2,0},{3,1},{0,2},{1,3},{6,4},{7,5},{4,6},{5,7},{10,8},{11,9},{8,1... | collective-permute-start | bytes 589832 | tf_op jit(solution)/shard_map/ppermute | solution.py:339
  14.6 8.5 %collective-permute-start.6 = (bf16[2,192,128]{2,1,0:T(8,128)(2,1)S(1)}, bf16[2,192,128]{2,1,0:T(8,128)(2,1)S(1)}, u32[]{:S(2)}, u32[]{:S(2)}) collective-permute-start(bf16[2,192,128]{2,1,0:T(8,128)(2,1)S(1)} %get-tuple-element.70), channel_id=1, source_target_pairs={{2,0},{3,1},{0,2},{1,3},{6,4},{7,5},{4,6},{5,7},{10,8},{11,9},{8,1... | collective-permute-start | bytes 294920 | tf_op jit(solution)/shard_map/ppermute | solution.py:339
  15.9 9.7 %collective-permute-start.7 = (bf16[2,192,128]{2,1,0:T(8,128)(2,1)S(1)}, bf16[2,192,128]{2,1,0:T(8,128)(2,1)S(1)}, u32[]{:S(2)}, u32[]{:S(2)}) collective-permute-start(bf16[2,192,128]{2,1,0:T(8,128)(2,1)S(1)} %get-tuple-element.71), channel_id=1, source_target_pairs={{3,0},{2,1},{1,2},{0,3},{7,4},{6,5},{5,6},{4,7},{11,8},{10,9},{9,1... | collective-permute-start | bytes 294920 | tf_op jit(solution)/shard_map/ppermute | solution.py:339
  26.4 7.6 %collective-permute-start.19 = (bf16[2,128,768]{2,1,0:T(8,128)(2,1)S(1)}, bf16[2,128,768]{2,1,0:T(8,128)(2,1)S(1)}, u32[]{:S(2)}, u32[]{:S(2)}) collective-permute-start(bf16[2,128,768]{2,1,0:T(8,128)(2,1)S(1)} %pair.1.mine_ref), channel_id=1, source_target_pairs={{1,0},{0,1},{3,2},{2,3},{5,4},{4,5},{7,6},{6,7},{9,8},{8,9},{11,10... | collective-permute-start | bytes 1179656 | tf_op jit(solution)/shard_map/ppermute | solution.py:339
  27.5 18.2 %collective-permute-start.11 = (bf16[2,192,384]{2,1,0:T(8,128)(2,1)S(1)}, bf16[2,192,384]{2,1,0:T(8,128)(2,1)S(1)}, u32[]{:S(2)}, u32[]{:S(2)}) collective-permute-start(bf16[2,192,384]{2,1,0:T(8,128)(2,1)S(1)} %get-tuple-element.84), channel_id=1, source_target_pairs={{0,4},{1,5},{2,6},{3,7},{4,8},{5,9},{6,10},{7,11},{8,12},{9,13},{1... | collective-permute-start | bytes 884744 | tf_op jit(solution)/shard_map/ppermute | solution.py:345
  28.4 18.8 %collective-permute-start.12 = (bf16[2,192,384]{2,1,0:T(8,128)(2,1)S(1)}, bf16[2,192,384]{2,1,0:T(8,128)(2,1)S(1)}, u32[]{:S(2)}, u32[]{:S(2)}) collective-permute-start(bf16[2,192,384]{2,1,0:T(8,128)(2,1)S(1)} %get-tuple-element.85), channel_id=1, source_target_pairs={{0,12},{1,13},{2,14},{3,15},{4,0},{5,1},{6,2},{7,3},{8,4},{9,5},{1... | collective-permute-start | bytes 884744 | tf_op jit(solution)/shard_map/ppermute | solution.py:346
  34.5 12.7 %collective-permute-start.20 = (bf16[96,768]{1,0:T(8,128)(2,1)S(1)}, bf16[96,768]{1,0:T(8,128)(2,1)S(1)}, u32[]{:S(2)}, u32[]{:S(2)}) collective-permute-start(bf16[96,768]{1,0:T(8,128)(2,1)S(1)} %get-tuple-element.99), channel_id=1, source_target_pairs={{0,16},{16,0},{1,17},{17,1},{2,18},{18,2},{3,19},{19,3},{4,20},{20... | collective-permute-start | bytes 442376 | tf_op jit(solution)/shard_map/ppermute | solution.py:350
  35.8 8.5 %collective-permute-start.13 = (f32[8,384]{1,0:T(8,128)S(1)}, f32[8,384]{1,0:T(8,128)S(1)}, u32[]{:S(2)}, u32[]{:S(2)}) collective-permute-start(f32[8,384]{1,0:T(8,128)S(1)} %get-tuple-element.86), channel_id=1, source_target_pairs={{0,4},{1,5},{2,6},{3,7},{4,8},{5,9},{6,10},{7,11},{8,12},{9,13},{1... | collective-permute-start | bytes 36872 | tf_op jit(solution)/shard_map/ppermute | solution.py:345
  35.8 9.7 %collective-permute-start.14 = (f32[8,384]{1,0:T(8,128)S(1)}, f32[8,384]{1,0:T(8,128)S(1)}, u32[]{:S(2)}, u32[]{:S(2)}) collective-permute-start(f32[8,384]{1,0:T(8,128)S(1)} %get-tuple-element.87), channel_id=1, source_target_pairs={{0,12},{1,13},{2,14},{3,15},{4,0},{5,1},{6,2},{7,3},{8,4},{9,5},{1... | collective-permute-start | bytes 36872 | tf_op jit(solution)/shard_map/ppermute | solution.py:346
  44.2 4.7 %collective-permute-start.8 = (bf16[2,192,128]{2,1,0:T(8,128)(2,1)S(1)}, bf16[2,192,128]{2,1,0:T(8,128)(2,1)S(1)}, u32[]{:S(2)}, u32[]{:S(2)}) collective-permute-start(bf16[2,192,128]{2,1,0:T(8,128)(2,1)S(1)} %get-tuple-element.79), channel_id=1, source_target_pairs={{1,0},{0,1},{3,2},{2,3},{5,4},{4,5},{7,6},{6,7},{9,8},{8,9},{11,10... | collective-permute-start | bytes 294920 | tf_op jit(solution)/shard_map/ppermute | solution.py:339
  45.5 4.4 %collective-permute-start.9 = (bf16[2,192,128]{2,1,0:T(8,128)(2,1)S(1)}, bf16[2,192,128]{2,1,0:T(8,128)(2,1)S(1)}, u32[]{:S(2)}, u32[]{:S(2)}) collective-permute-start(bf16[2,192,128]{2,1,0:T(8,128)(2,1)S(1)} %get-tuple-element.80), channel_id=1, source_target_pairs={{2,0},{3,1},{0,2},{1,3},{6,4},{7,5},{4,6},{5,7},{10,8},{11,9},{8,1... | collective-permute-start | bytes 294920 | tf_op jit(solution)/shard_map/ppermute | solution.py:339
  45.8 6.4 %collective-permute-start.10 = (bf16[2,192,128]{2,1,0:T(8,128)(2,1)S(1)}, bf16[2,192,128]{2,1,0:T(8,128)(2,1)S(1)}, u32[]{:S(2)}, u32[]{:S(2)}) collective-permute-start(bf16[2,192,128]{2,1,0:T(8,128)(2,1)S(1)} %get-tuple-element.81), channel_id=1, source_target_pairs={{3,0},{2,1},{1,2},{0,3},{7,4},{6,5},{5,6},{4,7},{11,8},{10,9},{9,1... | collective-permute-start | bytes 294920 | tf_op jit(solution)/shard_map/ppermute | solution.py:339
  47.2 5.0 %collective-permute-start.21 = (bf16[48,768]{1,0:T(8,128)(2,1)S(1)}, bf16[48,768]{1,0:T(8,128)(2,1)S(1)}, u32[]{:S(2)}, u32[]{:S(2)}) collective-permute-start(bf16[48,768]{1,0:T(8,128)(2,1)S(1)} %get-tuple-element.102), channel_id=1, source_target_pairs={{4,0},{5,1},{6,2},{7,3},{0,4},{1,5},{2,6},{3,7},{12,8},{13,9},{14,... | collective-permute-start | bytes 221192 | tf_op jit(solution)/shard_map/ppermute | solution.py:339
  52.2 6.3 %collective-permute-start.22 = (bf16[48,768]{1,0:T(8,128)(2,1)S(1)}, bf16[48,768]{1,0:T(8,128)(2,1)S(1)}, u32[]{:S(2)}, u32[]{:S(2)}) collective-permute-start(bf16[48,768]{1,0:T(8,128)(2,1)S(1)} %add.2.refs_0_), channel_id=1, source_target_pairs={{8,0},{9,1},{10,2},{11,3},{12,4},{13,5},{14,6},{15,7},{0,8},{1,9},... | collective-permute-start | bytes 221192 | tf_op jit(solution)/shard_map/ppermute | solution.py:339
  53.9 13.1 %copy-start.1 = (bf16[768,768]{1,0:T(8,128)(2,1)S(1)}, bf16[768,768]{1,0:T(8,128)(2,1)}, u32[]{:S(2)}) copy-start(bf16[768,768]{1,0:T(8,128)(2,1)} %refs_4_.1) | copy-start | bytes 3538948
  56.3 2.9 %collective-permute-start.15 = (bf16[2,192,128]{2,1,0:T(8,128)(2,1)S(1)}, bf16[2,192,128]{2,1,0:T(8,128)(2,1)S(1)}, u32[]{:S(2)}, u32[]{:S(2)}) collective-permute-start(bf16[2,192,128]{2,1,0:T(8,128)(2,1)S(1)} %get-tuple-element.92), channel_id=1, source_target_pairs={{1,0},{0,1},{3,2},{2,3},{5,4},{4,5},{7,6},{6,7},{9,8},{8,9},{11,10... | collective-permute-start | bytes 294920 | tf_op jit(solution)/shard_map/ppermute | solution.py:339
  56.6 4.2 %collective-permute-start.16 = (bf16[2,192,128]{2,1,0:T(8,128)(2,1)S(1)}, bf16[2,192,128]{2,1,0:T(8,128)(2,1)S(1)}, u32[]{:S(2)}, u32[]{:S(2)}) collective-permute-start(bf16[2,192,128]{2,1,0:T(8,128)(2,1)S(1)} %get-tuple-element.93), channel_id=1, source_target_pairs={{2,0},{3,1},{0,2},{1,3},{6,4},{7,5},{4,6},{5,7},{10,8},{11,9},{8,1... | collective-permute-start | bytes 294920 | tf_op jit(solution)/shard_map/ppermute | solution.py:339
  57.2 6.1 %collective-permute-start.17 = (bf16[2,192,128]{2,1,0:T(8,128)(2,1)S(1)}, bf16[2,192,128]{2,1,0:T(8,128)(2,1)S(1)}, u32[]{:S(2)}, u32[]{:S(2)}) collective-permute-start(bf16[2,192,128]{2,1,0:T(8,128)(2,1)S(1)} %get-tuple-element.94), channel_id=1, source_target_pairs={{3,0},{2,1},{1,2},{0,3},{7,4},{6,5},{5,6},{4,7},{11,8},{10,9},{9,1... | collective-permute-start | bytes 294920 | tf_op jit(solution)/shard_map/ppermute | solution.py:339
  58.4 4.8 %collective-permute-start.23 = (bf16[48,768]{1,0:T(8,128)(2,1)S(1)}, bf16[48,768]{1,0:T(8,128)(2,1)S(1)}, u32[]{:S(2)}, u32[]{:S(2)}) collective-permute-start(bf16[48,768]{1,0:T(8,128)(2,1)S(1)} %add.3.refs_0_), channel_id=1, source_target_pairs={{4,0},{5,1},{6,2},{7,3},{0,4},{1,5},{2,6},{3,7},{12,8},{13,9},{14,... | collective-permute-start | bytes 221192 | tf_op jit(solution)/shard_map/ppermute | solution.py:339
  63.2 5.4 %collective-permute-start.24 = (bf16[96,768]{1,0:T(8,128)(2,1)S(1)}, bf16[96,768]{1,0:T(8,128)(2,1)S(1)}, u32[]{:S(2)}, u32[]{:S(2)}) collective-permute-start(bf16[96,768]{1,0:T(8,128)(2,1)S(1)} %join.1.refs_0_), channel_id=1, source_target_pairs={{0,2},{1,3},{2,18},{3,19},{4,6},{5,7},{6,22},{7,23},{8,10},{9,11},... | collective-permute-start | bytes 442376 | tf_op jit(solution)/shard_map/ppermute | solution.py:478
  64.5 7.9 %collective-permute-start.25 = (bf16[96,768]{1,0:T(8,128)(2,1)S(1)}, bf16[96,768]{1,0:T(8,128)(2,1)S(1)}, u32[]{:S(2)}, u32[]{:S(2)}) collective-permute-start(bf16[96,768]{1,0:T(8,128)(2,1)S(1)} %join.1.refs_0_), channel_id=1, source_target_pairs={{2,16},{3,17},{6,20},{7,21},{10,24},{11,25},{14,28},{15,29},{16,2}... | collective-permute-start | bytes 442376 | tf_op jit(solution)/shard_map/ppermute | solution.py:478
  72.4 2.5 %collective-permute-start.26 = (bf16[192,768]{1,0:T(8,128)(2,1)S(1)}, bf16[192,768]{1,0:T(8,128)(2,1)S(1)}, u32[]{:S(2)}, u32[]{:S(2)}) collective-permute-start(bf16[192,768]{1,0:T(8,128)(2,1)S(1)} %cross.1.mine_ref), channel_id=1, source_target_pairs={{1,0},{0,1},{3,2},{2,3},{5,4},{4,5},{7,6},{6,7},{9,8},{8,9},{11,10... | collective-permute-start | bytes 884744 | tf_op jit(solution)/shard_map/ppermute | solution.py:339

commit v7 on v6

--- a/solution.py
+++ b/solution.py
@@ -102,6 +102,11 @@
     out_ref[1] = second_ref[...]
 
 
+def relay_kernel(sib_ref, across_ref, out_ref):
+    out_ref[0] = sib_ref[...]
+    out_ref[1] = across_ref[1]
+
+
 def gather_kernel(*refs):
     ins, (up_ref, down_ref, pair_ref) = refs[:LAYER], refs[LAYER:]
     span = ins[0].shape[2]
@@ -131,12 +136,13 @@
             slot = j - i
             if slot == HOPS:
                 bias_ref[j : j + 1, block(i, span)] = 0.0 * ones
-                dead_ref[i : i + 1, block(slot, span)] = 0.0 * ones
             else:
                 reads = jnp.where(listed(inner, outer), 0.0, neg_big)
                 bias_ref[j : j + 1, block(i, span)] = reads * ones
+            if not HOPS <= j < HOPS + LAYER:
                 read_by = jnp.where(listed(outer, inner), 0.0, -neg_big)
-                dead_ref[i : i + 1, block(slot, span)] = read_by * ones
+                spot = slot if j < HOPS else slot - LAYER
+                dead_ref[i : i + 1, block(spot, span)] = read_by * ones
 
 
 def clear(ref, span):
@@ -202,12 +208,15 @@
     stats_down[...] = stats_ref[:, :reach]
 
 
-def query_grad_kernel(window_ref, probs_ref, query_ref, stats_ref, mixed_ref, *refs):
-    outs, (token_ref, grads, flipped) = refs[:LAYER], refs[LAYER:]
+def query_grad_kernel(
+    window_ref, probs_ref, query_ref, stats_ref, mixed_ref, mine_ref, sib_ref, across_ref, own_ref,
+    token_ref, grads, flipped
+):
     rows = query_ref.shape[1]
     span = query_ref.shape[2] // LAYER
     head_width = rows // LOCAL
     scale = 1.0 / math.sqrt(head_width)
+    inside = slice(HOPS * span, (HOPS + LAYER) * span)
     clear(grads, span)
     for head in range(LOCAL):
         at = block(head, head_width)
@@ -220,49 +229,52 @@
             prob = probs_ref[head, block(j, span), cols].astype(f32)
             grads[block(j, span), cols] = (prob * (back - delta[:, cols])).astype(bf16)
         flipped[at] = (dot(window_ref[0, at], grads[...], NN) * scale).astype(bf16)
-    for peer, out in enumerate(outs):
+        own_ref[0, at] = dot(query_ref[0, at], grads[inside], NT)
+        own_ref[1, at] = dot(grad, probs_ref[head, inside], NT)
+    for peer, out in enumerate((mine_ref, sib_ref, across_ref.at[0], across_ref.at[1])):
         out[0] = mixed_ref[:, place(peer, span)]
         out[1] = flipped[:, place(peer, span)]
     token_ref[...] = jnp.zeros_like(token_ref)
 
 
 def key_grad_kernel(
-    head, pair_ref, query_ref, low_ref, high_ref, stats_ref, stats_low, stats_high,
-    dead_ref, *refs
+    pair_ref, low_ref, high_ref, stats_low, stats_high, dead_ref, own_ref, *refs
 ):
-    before, refs = refs[:head], refs[head:]
-    out_ref, refs = refs[0], refs[1:]
-    span = query_ref.shape[2] // LAYER
-    head_width = query_ref.shape[1] // LOCAL
-    at = block(head, head_width)
-
-    def window(low, own, high):
-        return jnp.concatenate([low, own, high], 1)
-
-    query = window(low_ref[0, at], query_ref[0, at], high_ref[0, at])
-    grad = window(low_ref[1, at], query_ref[1, at], high_ref[1, at])
-    row = slice(head, head + 1)
-    log_sum = window(stats_low[row], stats_ref[row], stats_high[row])
-    row = slice(LOCAL + head, LOCAL + head + 1)
-    delta = window(stats_low[row], stats_ref[row], stats_high[row])
-    for i in range(LAYER):
-        cols = slice(i * span, (i + SLOTS) * span)
-        own = block(i, span)
-        scores = dot(pair_ref[0, at, own], query[:, cols], TN)
-        prob = jnp.exp(scores - (log_sum[:, cols] + dead_ref[i : i + 1]))
-        back = dot(pair_ref[1, at, own], grad[:, cols], TN)
-        grads = (prob * (back - delta[:, cols])).astype(bf16)
-        out_ref[0, :, own] = dot(query[:, cols], grads, NT).astype(bf16)
-        out_ref[1, :, own] = dot(grad[:, cols], prob.astype(bf16), NT).astype(bf16)
-    if head == LOCAL - 1:
-        for peer, ref in enumerate(refs[:LAYER]):
-            for h, source in enumerate((*before, out_ref)):
-                ref[:, block(h, head_width)] = source[:, :, place(peer, span)]
-    refs[-1][...] = jnp.zeros_like(refs[-1])
-
-
-def output_kernel(*refs):
-    ins, (weight_ref, out_ref, dq_ref, token_ref, flipped) = refs[:LAYER], refs[LAYER:]
+    outs, (token_ref, flipped) = refs[:LAYER], refs[LAYER:]
+    rows = pair_ref.shape[1]
+    span = pair_ref.shape[2] // LAYER
+    head_width = rows // LOCAL
+    for head in range(LOCAL):
+        at = block(head, head_width)
+        log_row = slice(head, head + 1)
+        delta_row = slice(LOCAL + head, LOCAL + head + 1)
+        for i in range(LAYER):
+            own = block(i, span)
+
+            def outside(low, high):
+                sides = [low[:, i * span :]] if i < HOPS else []
+                return jnp.concatenate(sides + ([high[:, : i * span]] if i else []), 1)
+
+            query = outside(low_ref[0, at], high_ref[0, at])
+            grad = outside(low_ref[1, at], high_ref[1, at])
+            log_sum = outside(stats_low[log_row], stats_high[log_row]) + dead_ref[i : i + 1]
+            delta = outside(stats_low[delta_row], stats_high[delta_row])
+            prob = jnp.exp(dot(pair_ref[0, at, own], query, TN) - log_sum)
+            back = dot(pair_ref[1, at, own], grad, TN)
+            grads = (prob * (back - delta)).astype(bf16)
+            keys = own_ref[0, at, own] + dot(query, grads, NT)
+            values = own_ref[1, at, own] + dot(grad, prob.astype(bf16), NT)
+            flipped[0, at, own] = keys.astype(bf16)
+            flipped[1, at, own] = values.astype(bf16)
+    for peer, out in enumerate(outs):
+        out[...] = flipped[:, :, place(peer, span)]
+    token_ref[...] = jnp.zeros_like(token_ref)
+
+
+def output_kernel(
+    mine_ref, across_ref, sib_ref, weight_ref, out_ref, dq_ref, token_ref, flipped
+):
+    ins = mine_ref, sib_ref.at[0], across_ref.at[0], sib_ref.at[1]
     for peer, ref in enumerate(ins):
         flipped[:, place(peer, ref.shape[1])] = ref[...]
     out_ref[...] = dot(flipped[0], weight_ref[...], TN).astype(bf16)
@@ -364,32 +376,30 @@
             name="gather", after=after,
         )
 
+    g_across = swap(g, 2)
     mine, *parts = call(
         pack_kernel, [HBM] * 2, [part_shape] * LAYER, (k, v),
         [pltpu.VMEM((2, span, width), bf16), pltpu.VMEM((2, width, span), bf16), dma((2,))],
         limit=58, name="pack",
     )
-    up, down, pair = gather((mine, *in_layer(parts)))
+    up, down, pair = gather((mine, *in_layer(parts)), (g_across,))
     mine, *parts, g_copy = call(
         project_kernel, [VMEM] * 3, [part_shape] * LAYER + [flat_shape],
         (q, g, out_weight), [pltpu.VMEM((2, width, span), bf16)], name="project",
     )
-    up, g_copy, *parts = lax.optimization_barrier((up, g_copy, *parts))
+    up, *parts = lax.optimization_barrier((up, *parts))
     kv_low, kv_high = along(up, down)
-    up, down, query = gather((mine, *in_layer(parts)))
-    qg_low, qg_high = along(up, down)
+    (g_pair,) = call(
+        pair_kernel, [VMEM] * 2, [shape_of(2, span, width)], (g_copy, g_across), name="pair",
+    )
+    g_pairs = g_pair, swap(g_pair, 1)
     bias, dead = call(
         functools.partial(live_kernel, stations), [SMEM] * 2,
-        [
-            shape_of(16, LAYER * span, dtype=f32), shape_of(8, SLOTS * span, dtype=f32),
-        ],
+        [shape_of(16, LAYER * span, dtype=f32), shape_of(8, HOPS * span, dtype=f32)],
         (partner_ids, partner_count), name="live",
     )
-    (g_pair,) = call(
-        pair_kernel, [VMEM] * 2, [shape_of(2, span, width)], (g_copy, swap(g_copy, 2)), name="pair",
-        after=(kv_low, kv_high, query, bias),
-    )
-    g_pairs = g_pair, swap(g_pair, 1)
+    up, down, query = gather((mine, *in_layer(parts)), (bias, g_pairs[1]))
+    qg_low, qg_high = along(up, down)
     stats_shape = shape_of(8, HOPS * span, dtype=f32)
     mixed, stats, up, down, probs, window = call(
         forward_kernel, [VMEM] * 5,
@@ -410,31 +420,29 @@
         (mixed, *g_pairs), [pltpu.VMEM((LAYER * span, width), bf16)], name="weight",
     )
 
-    mine, *parts, query_token = call(
-        query_grad_kernel, [VMEM] * 5, [part_shape] * LAYER + [TOKEN],
+    mine, to_sib, to_across, own_grad, query_token = call(
+        query_grad_kernel, [VMEM] * 5,
+        [part_shape, part_shape, shape_of(2, 2, rows, span), shape_of(2, rows, LAYER * span, dtype=f32)]
+        + [TOKEN],
         (window, probs, query, stats, mixed),
         [pltpu.VMEM((BLOCKS * span, LAYER * span), bf16), pltpu.VMEM((rows, LAYER * span), bf16)],
-        limit=20, name="query_grad",
-    )
-    query_parts = in_layer(parts)
+        limit=20, name="query_grad", after=(send,),
+    )
+    across = swap(to_across, 2)
+    (relay,) = call(
+        relay_kernel, [VMEM] * 2, [shape_of(2, 2, rows, span)], (to_sib, across), name="relay"
+    )
+    relayed = swap(relay, 1)
     layer_output, grad_query, output_token = call(
-        output_kernel, [VMEM] * (LAYER + 1), [flat_shape] * 2 + [TOKEN],
-        (mine, *query_parts, out_weight), [pltpu.VMEM((2, width, span), bf16)], name="output",
-    )
-
-    before, key_tokens = [], []
-    for head in range(LOCAL):
-        last = head == LOCAL - 1
-        out, *parts, token = call(
-            functools.partial(key_grad_kernel, head),
-            [VMEM] * (8 + len(before)),
-            [shape_of(2, rows // LOCAL, LAYER * span)] + [part_shape] * (LAYER * last) + [TOKEN],
-            (pair, query, qg_low, qg_high, stats, stats_low, stats_high, dead, *before),
-            limit=20, name="key_grad",
-        )
-        before.append(out)
-        key_tokens.append(token)
-    mine, *parts = parts
+        output_kernel, [VMEM] * 4, [flat_shape] * 2 + [TOKEN],
+        (mine, across, relayed, out_weight), [pltpu.VMEM((2, width, span), bf16)], name="output",
+    )
+
+    mine, *parts, key_token = call(
+        key_grad_kernel, [VMEM] * 7, [part_shape] * LAYER + [TOKEN],
+        (pair, qg_low, qg_high, stats_low, stats_high, dead, own_grad),
+        [pltpu.VMEM((2, rows, LAYER * span), bf16)], limit=20, name="key_grad",
+    )
     key_parts = in_layer(parts)
     grad_key, grad_value, key_output_token = call(
         key_output_kernel, [VMEM] * LAYER, [flat_shape] * 2 + [TOKEN],
@@ -448,17 +456,17 @@
         send, part = call(
             functools.partial(split_kernel, LAYER), [VMEM] * 2,
             [shape_of(count, width), shape_of(count, width, dtype=f32)],
-            (part, got), name="split", after=(query_token, qg_low, qg_high, stats_low, stats_high),
+            (part, got), name="split", after=(query_token, qg_low, qg_high),
         )
 
         def add_round(part, got, after=()):
             out = [shape_of(count, width)]
             return call(round_kernel, [VMEM] * 2, out, (part, got), name="add", after=after)[0]
 
-        total = add_round(part, swap(send, LAYER), key_tokens[:1] + query_parts)
+        total = add_round(part, swap(send, LAYER), (stats_low, stats_high))
         stride = 2 * LAYER
         while stride < stations:
-            total = add_round(total, swap(total, stride), key_tokens[1:])
+            total = add_round(total, swap(total, stride), (key_token, across))
             stride *= 2
         (total,) = call(
             functools.partial(join_kernel, LAYER, None), [VMEM] * 2, [shape_of(2 * count, width)],
@@ -476,7 +484,7 @@
         (total,) = call(
             cross_kernel, [VMEM] * 3, [shape_of(4 * count, width)],
             (total, lax.ppermute(total, axes, first), lax.ppermute(total, axes, second)),
-            name="cross", after=(output_token,),
+            name="cross", after=(output_token, key_output_token),
         )
         (grad_weight,) = call(
             functools.partial(join_kernel, 1, scale), [VMEM] * 2,

time: 76.6 us -> 80.1 us (1.046)
  starting transfers between devices: 28.5 us -> 33.9 us
  waiting for transfers between devices: 25.2 us -> 23.2 us
  Pallas kernels: 18.3 us -> 16.7 us
  local copies, waits for them, and re-layouts: 3.22 us -> 4.11 us
    ppermute x18 -> x17, starting transfers between devices: 13.5 us -> 19.1 us  [swap(): lax.ppermute(value, 'station', [(s ^ stride, s) for s in range(stations)])]
    ppermute x3, waiting for transfers between devices: 0.63 us -> 6.22 us  [along(): lax.ppermute(down, 'station', [(s, (s - LAYER) % stations) for s in range...]
    ppermute x18 -> x17, waiting for transfers between devices: 16.6 us -> 13.6 us  [swap(): lax.ppermute(value, 'station', [(s ^ stride, s) for s in range(stations)])]
    ppermute x3, waiting for transfers between devices: 3.63 us -> 1.08 us  [along(): lax.ppermute(up, 'station', [(s, (s + LAYER) % stations) for s in range(s...]
    ppermute x1, waiting for transfers between devices: 3.7 us -> 1.97 us  [local(): lax.ppermute(total, axes, second)]
    pallas_call x20 -> x19, Pallas kernels: 18.3 us -> 16.7 us  [call(): pl.pallas_call(kernel, in_specs=ins, out_specs=[VMEM] * len(outs), out_sh...]
    ppermute x1, starting transfers between devices: 1.29 us -> 0.06 us  [local(): lax.ppermute(total, axes, first)]
    ppermute x1, starting transfers between devices: 2.42 us -> 3.4 us  [local(): lax.ppermute(total, axes, second)]
  transfers between devices with their start and end apart: 27 -> 26, of which waited for: 12 -> 12; matrix products, arithmetic and copies ran while one was open for 0% -> 0% of each run, Pallas kernels for 20% -> 20%
where the time goes in v7:
time: 80.1 us; the launch traced here: 78.8 us
  starting transfers between devices  33.9 us (42%)
  waiting for transfers between devices  23.2 us (29%)
  Pallas kernels  16.7 us (21%)
  local copies, waits for them, and re-layouts  4.11 us (5%)
  between operations  0.82 us (1%)
    ppermute x17, starting transfers between devices, swap(): lax.ppermute(value, 'station', [(s ^ stride, s) for s in range(stations)])  19.1 us
    pallas_call x19, Pallas kernels, call(): pl.pallas_call(kernel, in_specs=ins, out_specs=[VMEM] * len(outs), out_sh...  16.7 us
    ppermute x17, waiting for transfers between devices, swap(): lax.ppermute(value, 'station', [(s ^ stride, s) for s in range(stations)])  13.6 us
    ppermute x3, starting transfers between devices, along(): lax.ppermute(down, 'station', [(s, (s - LAYER) % stations) for s in range...  8.54 us
    ppermute x3, waiting for transfers between devices, along(): lax.ppermute(down, 'station', [(s, (s - LAYER) % stations) for s in range...  6.22 us
    unnamed x15, local copies, waits for them, and re-layouts  4.11 us
    ppermute x1, starting transfers between devices, local(): lax.ppermute(total, axes, second)  3.4 us
    ppermute x1, waiting for transfers between devices, local(): lax.ppermute(total, axes, second)  1.97 us
  transfers between devices with their start and end apart: 26, of which 12 were waited for; matrix products, arithmetic and copies ran while one was open for 0% of the time, Pallas kernels for 20%

profile of v7, /device:TPU:3, one launch (start us, length us, event | category | flops | bytes accessed | tf_op | source)
XLA Modules:
  0.0 78.8 jit_solution(16587345654059993861)
XLA Ops:
  0.7 1.3 %copy-done = bf16[768,768]{1,0:T(8,128)(2,1)S(1)} copy-done((bf16[768,768]{1,0:T(8,128)(2,1)S(1)}, bf16[768,768]{1,0:T(8,128)(2,1)}, u32[]{:S(2)}) %copy-start) | copy-done | bytes 1179672
  2.0 0.9 %copy-done.2 = bf16[1,1,128,768]{3,2,1,0:T(8,128)(2,1)S(1)} copy-done((bf16[1,1,128,768]{3,2,1,0:T(8,128)(2,1)S(1)}, bf16[1,1,128,768]{3,2,1,0:T(8,128)(2,1)}, u32[]{:S(2)}) %copy-start.2) | copy-done | bytes 196632
  2.9 0.9 %copy-done.3 = bf16[1,1,128,768]{3,2,1,0:T(8,128)(2,1)S(1)} copy-done((bf16[1,1,128,768]{3,2,1,0:T(8,128)(2,1)S(1)}, bf16[1,1,128,768]{3,2,1,0:T(8,128)(2,1)}, u32[]{:S(2)}) %copy-start.3) | copy-done | bytes 196632
  3.8 0.5 project.1
  4.4 2.3 %collective-permute-done.3.refs_4_.second_ref = bf16[128,768]{1,0:T(8,128)(2,1)S(1)} collective-permute-done((bf16[128,768]{1,0:T(8,128)(2,1)}, bf16[128,768]{1,0:T(8,128)(2,1)S(1)}, u32[]{:S(2)}, u32[]{:S(2)}) %collective-permute-start.3) | collective-permute-done | bytes 196640 | tf_op jit(solution)/shard_map/ppermute | solution.py:351
  6.7 1.6 %collective-permute-start.9 = (bf16[2,128,768]{2,1,0:T(8,128)(2,1)S(1)}, bf16[2,128,768]{2,1,0:T(8,128)(2,1)S(1)}, u32[]{:S(2)}, u32[]{:S(2)}) collective-permute-start(bf16[2,128,768]{2,1,0:T(8,128)(2,1)S(1)} %pair.1.mine_ref), channel_id=1, source_target_pairs={{1,0},{0,1},{3,2},{2,3},{5,4},{4,5},{7,6},{6,7},{9,8},{8,9},{11,10... | collective-permute-start | bytes 1179656 | tf_op jit(solution)/shard_map/ppermute | solution.py:351
  8.3 1.9 %pack.1 = (bf16[2,192,128]{2,1,0:T(8,128)(2,1)}, bf16[2,192,128]{2,1,0:T(8,128)(2,1)}, bf16[2,192,128]{2,1,0:T(8,128)(2,1)}, bf16[2,192,128]{2,1,0:T(8,128)(2,1)}) custom-call(bf16[128,768]{1,0:T(8,128)(2,1)} %bitcast.11, bf16[128,768]{1,0:T(8,128)(2,1)} %bitcast.12), custom_call_target="tpu_custom_call" | custom-call | flops 1 | bytes 1 | tf_op jit(solution)/shard_map/pack/pallas_call | solution.py:50
  10.4 2.1 %collective-permute-start.2 = (bf16[2,192,128]{2,1,0:T(8,128)(2,1)}, bf16[2,192,128]{2,1,0:T(8,128)(2,1)S(1)}, u32[]{:S(2)}, u32[]{:S(2)}) collective-permute-start(bf16[2,192,128]{2,1,0:T(8,128)(2,1)} %get-tuple-element.55), channel_id=1, source_target_pairs={{3,0},{2,1},{1,2},{0,3},{7,4},{6,5},{5,6},{4,7},{11,8},{10,9},{9,1... | collective-permute-start | bytes 294920 | tf_op jit(solution)/shard_map/ppermute | solution.py:351
  12.5 2.1 %collective-permute-done.1.refs_2_ = bf16[2,192,128]{2,1,0:T(8,128)(2,1)S(1)} collective-permute-done((bf16[2,192,128]{2,1,0:T(8,128)(2,1)}, bf16[2,192,128]{2,1,0:T(8,128)(2,1)S(1)}, u32[]{:S(2)}, u32[]{:S(2)}) %collective-permute-start.1) | collective-permute-done | bytes 98336 | tf_op jit(solution)/shard_map/ppermute | solution.py:351
  14.5 2.7 %collective-permute-done.2.refs_3_ = bf16[2,192,128]{2,1,0:T(8,128)(2,1)S(1)} collective-permute-done((bf16[2,192,128]{2,1,0:T(8,128)(2,1)}, bf16[2,192,128]{2,1,0:T(8,128)(2,1)S(1)}, u32[]{:S(2)}, u32[]{:S(2)}) %collective-permute-start.2) | collective-permute-done | bytes 98336 | tf_op jit(solution)/shard_map/ppermute | solution.py:351
  17.2 0.9 %copy-done.4 = bf16[2,192,128]{2,1,0:T(8,128)(2,1)S(1)} copy-done((bf16[2,192,128]{2,1,0:T(8,128)(2,1)S(1)}, bf16[2,192,128]{2,1,0:T(8,128)(2,1)}, u32[]{:S(2)}) %copy-start.4) | copy-done | bytes 98328
  18.1 0.1 gather.2
  18.3 1.3 %collective-permute-start.4 = (bf16[2,192,384]{2,1,0:T(8,128)(2,1)S(1)}, bf16[2,192,384]{2,1,0:T(8,128)(2,1)S(1)}, u32[]{:S(2)}, u32[]{:S(2)}) collective-permute-start(bf16[2,192,384]{2,1,0:T(8,128)(2,1)S(1)} %get-tuple-element.61), channel_id=1, source_target_pairs={{0,4},{1,5},{2,6},{3,7},{4,8},{5,9},{6,10},{7,11},{8,12},{9,13},{1... | collective-permute-start | bytes 884744 | tf_op jit(solution)/shard_map/ppermute | solution.py:357
  19.7 2.1 %collective-permute-start.5 = (bf16[2,192,384]{2,1,0:T(8,128)(2,1)S(1)}, bf16[2,192,384]{2,1,0:T(8,128)(2,1)S(1)}, u32[]{:S(2)}, u32[]{:S(2)}) collective-permute-start(bf16[2,192,384]{2,1,0:T(8,128)(2,1)S(1)} %get-tuple-element.62), channel_id=1, source_target_pairs={{0,12},{1,13},{2,14},{3,15},{4,0},{5,1},{6,2},{7,3},{8,4},{9,5},{1... | collective-permute-start | bytes 884744 | tf_op jit(solution)/shard_map/ppermute | solution.py:358
  21.8 0.5 collective-permute-start.7
  22.3 2.0 %collective-permute-start.8 = (bf16[2,192,128]{2,1,0:T(8,128)(2,1)S(1)}, bf16[2,192,128]{2,1,0:T(8,128)(2,1)S(1)}, u32[]{:S(2)}, u32[]{:S(2)}) collective-permute-start(bf16[2,192,128]{2,1,0:T(8,128)(2,1)S(1)} %get-tuple-element.66), channel_id=1, source_target_pairs={{3,0},{2,1},{1,2},{0,3},{7,4},{6,5},{5,6},{4,7},{11,8},{10,9},{9,1... | collective-permute-start | bytes 294920 | tf_op jit(solution)/shard_map/ppermute | solution.py:351
  24.3 0.1 copy.12.ids_ref
  24.4 1.2 %live.1 = (f32[16,512]{1,0:T(8,128)S(1)}, f32[8,384]{1,0:T(8,128)S(1)}) custom-call(s32[16,6]{1,0:T(8,128)S(1)} %copy.12.ids_ref, s32[16]{0:T(128)S(1)} %copy-done.5), custom_call_target="tpu_custom_call" | custom-call | flops 1 | bytes 1 | tf_op jit(solution)/shard_map/live/pallas_call | solution.py:50
  25.6 3.4 %collective-permute-done.8.refs_3_ = bf16[2,192,128]{2,1,0:T(8,128)(2,1)S(1)} collective-permute-done((bf16[2,192,128]{2,1,0:T(8,128)(2,1)S(1)}, bf16[2,192,128]{2,1,0:T(8,128)(2,1)S(1)}, u32[]{:S(2)}, u32[]{:S(2)}) %collective-permute-start.8) | collective-permute-done | bytes 98336 | tf_op jit(solution)/shard_map/ppermute | solution.py:351
  29.0 0.1 gather.3
  29.2 3.3 %collective-permute-start.13 = (bf16[2,192,384]{2,1,0:T(8,128)(2,1)S(1)}, bf16[2,192,384]{2,1,0:T(8,128)(2,1)S(1)}, u32[]{:S(2)}, u32[]{:S(2)}) collective-permute-start(bf16[2,192,384]{2,1,0:T(8,128)(2,1)S(1)} %get-tuple-element.81), channel_id=1, source_target_pairs={{0,12},{1,13},{2,14},{3,15},{4,0},{5,1},{6,2},{7,3},{8,4},{9,5},{1... | collective-permute-start | bytes 884744 | tf_op jit(solution)/shard_map/ppermute | solution.py:358
  32.5 1.9 %collective-permute-done.5.high_ref = bf16[2,192,384]{2,1,0:T(8,128)(2,1)S(1)} collective-permute-done((bf16[2,192,384]{2,1,0:T(8,128)(2,1)S(1)}, bf16[2,192,384]{2,1,0:T(8,128)(2,1)S(1)}, u32[]{:S(2)}, u32[]{:S(2)}) %collective-permute-start.5) | collective-permute-done | bytes 294944 | tf_op jit(solution)/shard_map/ppermute | solution.py:358
  34.4 3.3 %forward.1 = (bf16[192,512]{1,0:T(8,128)(2,1)S(1)}, f32[8,512]{1,0:T(8,128)S(1)}, f32[8,384]{1,0:T(8,128)S(1)}, f32[8,384]{1,0:T(8,128)S(1)}, bf16[3,1280,512]{2...) custom-call(bf16[2,192,512]{2,1,0:T(8,128)(2,1)S(1)} %get-tuple-element.56.pair_ref, ...), custom_call_target="tpu_custom_call" | custom-call | flops 1 | bytes 1 | tf_op jit(solution)/shard_map/forward/pallas_call | solution.py:50
  37.7 0.5 weight.1
  38.1 1.3 %collective-permute-start.19 = (bf16[96,768]{1,0:T(8,128)(2,1)S(1)}, bf16[96,768]{1,0:T(8,128)(2,1)S(1)}, u32[]{:S(2)}, u32[]{:S(2)}) collective-permute-start(bf16[96,768]{1,0:T(8,128)(2,1)S(1)} %get-tuple-element.74.refs_5_), channel_id=1, source_target_pairs={{0,16},{16,0},{1,17},{17,1},{2,18},{18,2},{3,19},{19,3},{4,20},{20... | collective-permute-start | bytes 442376 | tf_op jit(solution)/shard_map/ppermute | solution.py:362
  39.4 2.6 %query_grad.1 = (bf16[2,192,128]{2,1,0:T(8,128)(2,1)S(1)}, bf16[2,192,128]{2,1,0:T(8,128)(2,1)S(1)}, bf16[2,2,192,128]{3,2,1,0:T(8,128)(2,1)S(1)}, f32[2,192,512]{2,1,0:T(8,128)S(1)}, f32[8,128]{1,0:T(8,128)S(1)}) custom-call(bf16[2,192,1280]{2,1,0:T(8,128)(2,1)S(1)} %get-tuple-element.70.refs_0_, bf16[3,1280,512]{2,1,0:T(8,128)(2,1)S(1)} %get-tuple-element.71.refs_1_, ...), custom_call_target="tpu_custom_call" | custom-call | flops 1 | bytes 1 | tf_op jit(solution)/shard_map/query_grad/pallas_call | solution.py:50
  42.0 0.7 collective-permute-start.10
  42.7 4.3 %collective-permute-done.13.high_ref.refs_4_ = bf16[2,192,384]{2,1,0:T(8,128)(2,1)S(1)} collective-permute-done((bf16[2,192,384]{2,1,0:T(8,128)(2,1)S(1)}, bf16[2,192,384]{2,1,0:T(8,128)(2,1)S(1)}, u32[]{:S(2)}, u32[]{:S(2)}) %collective-permute-start.13) | collective-permute-done | bytes 294944 | tf_op jit(solution)/shard_map/ppermute | solution.py:358
  47.0 1.5 %collective-permute-start.20 = (bf16[48,768]{1,0:T(8,128)(2,1)S(1)}, bf16[48,768]{1,0:T(8,128)(2,1)S(1)}, u32[]{:S(2)}, u32[]{:S(2)}) collective-permute-start(bf16[48,768]{1,0:T(8,128)(2,1)S(1)} %get-tuple-element.95), channel_id=1, source_target_pairs={{4,0},{5,1},{6,2},{7,3},{0,4},{1,5},{2,6},{3,7},{12,8},{13,9},{14,... | collective-permute-start | bytes 221192 | tf_op jit(solution)/shard_map/ppermute | solution.py:351
  48.6 3.2 %collective-permute-start.15 = (f32[8,384]{1,0:T(8,128)S(1)}, f32[8,384]{1,0:T(8,128)S(1)}, u32[]{:S(2)}, u32[]{:S(2)}) collective-permute-start(f32[8,384]{1,0:T(8,128)S(1)} %get-tuple-element.83), channel_id=1, source_target_pairs={{0,12},{1,13},{2,14},{3,15},{4,0},{5,1},{6,2},{7,3},{8,4},{9,5},{1... | collective-permute-start | bytes 36872 | tf_op jit(solution)/shard_map/ppermute | solution.py:358
  51.8 1.1 %collective-permute-done.14.stats_low.refs_2_ = f32[8,384]{1,0:T(8,128)S(1)} collective-permute-done((f32[8,384]{1,0:T(8,128)S(1)}, f32[8,384]{1,0:T(8,128)S(1)}, u32[]{:S(2)}, u32[]{:S(2)}) %collective-permute-start.14) | collective-permute-done | bytes 12320 | tf_op jit(solution)/shard_map/ppermute | solution.py:357
  52.9 0.5 collective-permute-start.21
  53.4 3.2 %key_grad.1 = (bf16[2,192,128]{2,1,0:T(8,128)(2,1)S(1)}, bf16[2,192,128]{2,1,0:T(8,128)(2,1)S(1)}, bf16[2,192,128]{2,1,0:T(8,128)(2,1)S(1)}, bf16[2,192,128]{2,1,0:T(8,128)(2,1)S(1)}, f32[8,128]{1,0:T(8,128)S(1)}) custom-call(bf16[2,192,512]{2,1,0:T(8,128)(2,1)S(1)} %get-tuple-element.56.pair_ref, ...), custom_call_target="tpu_custom_call" | custom-call | flops 1 | bytes 1 | tf_op jit(solution)/shard_map/key_grad/pallas_call | solution.py:50
  56.6 2.3 %collective-permute-start.16 = (bf16[2,192,128]{2,1,0:T(8,128)(2,1)S(1)}, bf16[2,192,128]{2,1,0:T(8,128)(2,1)S(1)}, u32[]{:S(2)}, u32[]{:S(2)}) collective-permute-start(bf16[2,192,128]{2,1,0:T(8,128)(2,1)S(1)} %get-tuple-element.87), channel_id=1, source_target_pairs={{1,0},{0,1},{3,2},{2,3},{5,4},{4,5},{7,6},{6,7},{9,8},{8,9},{11,10... | collective-permute-start | bytes 294920 | tf_op jit(solution)/shard_map/ppermute | solution.py:351
  58.9 0.6 collective-permute-start.17
  59.4 1.1 %collective-permute-start.18 = (bf16[2,192,128]{2,1,0:T(8,128)(2,1)S(1)}, bf16[2,192,128]{2,1,0:T(8,128)(2,1)S(1)}, u32[]{:S(2)}, u32[]{:S(2)}) collective-permute-start(bf16[2,192,128]{2,1,0:T(8,128)(2,1)S(1)} %get-tuple-element.89), channel_id=1, source_target_pairs={{3,0},{2,1},{1,2},{0,3},{7,4},{6,5},{5,6},{4,7},{11,8},{10,9},{9,1... | collective-permute-start | bytes 294920 | tf_op jit(solution)/shard_map/ppermute | solution.py:351
  60.6 3.5 %collective-permute-start.22 = (bf16[48,768]{1,0:T(8,128)(2,1)S(1)}, bf16[48,768]{1,0:T(8,128)(2,1)S(1)}, u32[]{:S(2)}, u32[]{:S(2)}) collective-permute-start(bf16[48,768]{1,0:T(8,128)(2,1)S(1)} %add.3.refs_0_), channel_id=1, source_target_pairs={{4,0},{5,1},{6,2},{7,3},{0,4},{1,5},{2,6},{3,7},{12,8},{13,9},{14,... | collective-permute-start | bytes 221192 | tf_op jit(solution)/shard_map/ppermute | solution.py:351
  64.2 0.5 collective-permute-start.11
  64.7 1.1 %collective-permute-done.18.refs_3_.refs_4_ = bf16[2,192,128]{2,1,0:T(8,128)(2,1)S(1)} collective-permute-done((bf16[2,192,128]{2,1,0:T(8,128)(2,1)S(1)}, bf16[2,192,128]{2,1,0:T(8,128)(2,1)S(1)}, u32[]{:S(2)}, u32[]{:S(2)}) %collective-permute-start.18) | collective-permute-done | bytes 98336 | tf_op jit(solution)/shard_map/ppermute | solution.py:351
  65.8 0.8 %collective-permute-done.22.refs_1_ = bf16[48,768]{1,0:T(8,128)(2,1)S(1)} collective-permute-done((bf16[48,768]{1,0:T(8,128)(2,1)S(1)}, bf16[48,768]{1,0:T(8,128)(2,1)S(1)}, u32[]{:S(2)}, u32[]{:S(2)}) %collective-permute-start.22) | collective-permute-done | bytes 73760 | tf_op jit(solution)/shard_map/ppermute | solution.py:351
  66.6 3.4 %collective-permute-start.24 = (bf16[96,768]{1,0:T(8,128)(2,1)S(1)}, bf16[96,768]{1,0:T(8,128)(2,1)S(1)}, u32[]{:S(2)}, u32[]{:S(2)}) collective-permute-start(bf16[96,768]{1,0:T(8,128)(2,1)S(1)} %join.1.refs_0_), channel_id=1, source_target_pairs={{2,16},{3,17},{6,20},{7,21},{10,24},{11,25},{14,28},{15,29},{16,2}... | collective-permute-start | bytes 442376 | tf_op jit(solution)/shard_map/ppermute | solution.py:486
  70.1 0.9 %key_output.1 = (bf16[128,768]{1,0:T(8,128)(2,1)}, bf16[128,768]{1,0:T(8,128)(2,1)}, f32[8,128]{1,0:T(8,128)S(1)}) custom-call(bf16[2,192,128]{2,1,0:T(8,128)(2,1)S(1)} %get-tuple-element.86.refs_0_, bf16[2,192,128]{2,1,0:T(8,128)(2,1)S(1)} %collective-permute-done.16.refs_1_.refs_2_, bf16[2,192,128]{2,1,0:T(8,128)(2,1)S(1)} %collective-permute-done.17.refs_2_.refs_3_, ...), custom_call_target="tpu_custom_call" | custom-call | flops 1 | bytes 1 | tf_op jit(solution)/shard_map/key_output/pallas_call | solution.py:50
  71.0 1.1 %output.1 = (bf16[128,768]{1,0:T(8,128)(2,1)}, bf16[128,768]{1,0:T(8,128)(2,1)}, f32[8,128]{1,0:T(8,128)S(1)}) custom-call(bf16[2,192,128]{2,1,0:T(8,128)(2,1)S(1)} %get-tuple-element.75.mine_ref, bf16[2,2,192,128]{3,2,1,0:T(8,128)(2,1)S(1)} %collective-permute-done.10.across_ref.refs_3_, bf16[2,2,192,128]{3,2,1,0:T(8,128)(2,1)S(1)} %collective-permute-done.11.sib_ref, ...), custom_call_target="tpu_custom_call" | custom-call | flops 1 | bytes 1 | tf_op jit(solution)/shard_map/output/pallas_call | solution.py:50
  72.1 2.0 %collective-permute-done.24.refs_2_ = bf16[96,768]{1,0:T(8,128)(2,1)S(1)} collective-permute-done((bf16[96,768]{1,0:T(8,128)(2,1)S(1)}, bf16[96,768]{1,0:T(8,128)(2,1)S(1)}, u32[]{:S(2)}, u32[]{:S(2)}) %collective-permute-start.24) | collective-permute-done | bytes 147488 | tf_op jit(solution)/shard_map/ppermute | solution.py:486
  74.1 0.4 collective-permute-done.23.refs_1_
  74.5 2.0 %collective-permute-start.25 = (bf16[192,768]{1,0:T(8,128)(2,1)S(1)}, bf16[192,768]{1,0:T(8,128)(2,1)S(1)}, u32[]{:S(2)}, u32[]{:S(2)}) collective-permute-start(bf16[192,768]{1,0:T(8,128)(2,1)S(1)} %cross.1.mine_ref), channel_id=1, source_target_pairs={{1,0},{0,1},{3,2},{2,3},{5,4},{4,5},{7,6},{6,7},{9,8},{8,9},{11,10... | collective-permute-start | bytes 884744 | tf_op jit(solution)/shard_map/ppermute | solution.py:351
  76.5 1.2 %collective-permute-done.25.got_ref = bf16[192,768]{1,0:T(8,128)(2,1)S(1)} collective-permute-done((bf16[192,768]{1,0:T(8,128)(2,1)S(1)}, bf16[192,768]{1,0:T(8,128)(2,1)S(1)}, u32[]{:S(2)}, u32[]{:S(2)}) %collective-permute-start.25) | collective-permute-done | bytes 294944 | tf_op jit(solution)/shard_map/ppermute | solution.py:351
  77.7 1.1 %last.1 = f32[384,768]{1,0:T(8,128)} custom-call(bf16[192,768]{1,0:T(8,128)(2,1)S(1)} %cross.1.mine_ref, bf16[192,768]{1,0:T(8,128)(2,1)S(1)} %collective-permute-done.25.got_ref), custom_call_target="tpu_custom_call" | custom-call | flops 1 | bytes 1 | tf_op jit(solution)/shard_map/last/pallas_call | solution.py:50
  (38 shorter events, 0.7 us)
Async XLA Ops:
  0.6 6.0 %collective-permute-start.3 = (bf16[128,768]{1,0:T(8,128)(2,1)}, bf16[128,768]{1,0:T(8,128)(2,1)S(1)}, u32[]{:S(2)}, u32[]{:S(2)}) collective-permute-start(bf16[128,768]{1,0:T(8,128)(2,1)} %bitcast.9), channel_id=1, source_target_pairs={{2,0},{3,1},{0,2},{1,3},{6,4},{7,5},{4,6},{5,7},{10,8},{11,9},{8,1... | collective-permute-start | bytes 589832 | tf_op jit(solution)/shard_map/ppermute | solution.py:351
  0.7 1.3 %copy-start = (bf16[768,768]{1,0:T(8,128)(2,1)S(1)}, bf16[768,768]{1,0:T(8,128)(2,1)}, u32[]{:S(2)}) copy-start(bf16[768,768]{1,0:T(8,128)(2,1)} %weight_ref.3) | copy-start | bytes 3538948
  2.0 0.9 %copy-start.2 = (bf16[1,1,128,768]{3,2,1,0:T(8,128)(2,1)S(1)}, bf16[1,1,128,768]{3,2,1,0:T(8,128)(2,1)}, u32[]{:S(2)}) copy-start(bf16[1,1,128,768]{3,2,1,0:T(8,128)(2,1)} %param.7) | copy-start | bytes 589828
  2.9 0.9 %copy-start.3 = (bf16[1,1,128,768]{3,2,1,0:T(8,128)(2,1)S(1)}, bf16[1,1,128,768]{3,2,1,0:T(8,128)(2,1)}, u32[]{:S(2)}) copy-start(bf16[1,1,128,768]{3,2,1,0:T(8,128)(2,1)} %param.10) | copy-start | bytes 589828
  4.3 20.0 %copy-start.6 = (s32[16,6]{0,1:T(8,128)S(1)}, s32[16,6]{0,1:T(8,128)}, u32[]{:S(2)}) copy-start(s32[16,6]{0,1:T(8,128)} %param.12) | copy-start | bytes 1156
  4.4 20.0 %copy-start.5 = (s32[16]{0:T(128)S(1)}, s32[16]{0:T(128)}, u32[]{:S(2)}) copy-start(s32[16]{0:T(128)} %count_ref.1) | copy-start | bytes 196
  6.7 22.3 %collective-permute-start.9 = (bf16[2,128,768]{2,1,0:T(8,128)(2,1)S(1)}, bf16[2,128,768]{2,1,0:T(8,128)(2,1)S(1)}, u32[]{:S(2)}, u32[]{:S(2)}) collective-permute-start(bf16[2,128,768]{2,1,0:T(8,128)(2,1)S(1)} %pair.1.mine_ref), channel_id=1, source_target_pairs={{1,0},{0,1},{3,2},{2,3},{5,4},{4,5},{7,6},{6,7},{9,8},{8,9},{11,10... | collective-permute-start | bytes 1179656 | tf_op jit(solution)/shard_map/ppermute | solution.py:351
  10.2 2.2 %collective-permute-start = (bf16[2,192,128]{2,1,0:T(8,128)(2,1)}, bf16[2,192,128]{2,1,0:T(8,128)(2,1)S(1)}, u32[]{:S(2)}, u32[]{:S(2)}) collective-permute-start(bf16[2,192,128]{2,1,0:T(8,128)(2,1)} %get-tuple-element.53), channel_id=1, source_target_pairs={{1,0},{0,1},{3,2},{2,3},{5,4},{4,5},{7,6},{6,7},{9,8},{8,9},{11,10... | collective-permute-start | bytes 294920 | tf_op jit(solution)/shard_map/ppermute | solution.py:351
  10.3 4.2 %collective-permute-start.1 = (bf16[2,192,128]{2,1,0:T(8,128)(2,1)}, bf16[2,192,128]{2,1,0:T(8,128)(2,1)S(1)}, u32[]{:S(2)}, u32[]{:S(2)}) collective-permute-start(bf16[2,192,128]{2,1,0:T(8,128)(2,1)} %get-tuple-element.54), channel_id=1, source_target_pairs={{2,0},{3,1},{0,2},{1,3},{6,4},{7,5},{4,6},{5,7},{10,8},{11,9},{8,1... | collective-permute-start | bytes 294920 | tf_op jit(solution)/shard_map/ppermute | solution.py:351
  10.4 6.8 %collective-permute-start.2 = (bf16[2,192,128]{2,1,0:T(8,128)(2,1)}, bf16[2,192,128]{2,1,0:T(8,128)(2,1)S(1)}, u32[]{:S(2)}, u32[]{:S(2)}) collective-permute-start(bf16[2,192,128]{2,1,0:T(8,128)(2,1)} %get-tuple-element.55), channel_id=1, source_target_pairs={{3,0},{2,1},{1,2},{0,3},{7,4},{6,5},{5,6},{4,7},{11,8},{10,9},{9,1... | collective-permute-start | bytes 294920 | tf_op jit(solution)/shard_map/ppermute | solution.py:351
  17.2 0.9 %copy-start.4 = (bf16[2,192,128]{2,1,0:T(8,128)(2,1)S(1)}, bf16[2,192,128]{2,1,0:T(8,128)(2,1)}, u32[]{:S(2)}) copy-start(bf16[2,192,128]{2,1,0:T(8,128)(2,1)} %get-tuple-element.52.refs_0_) | copy-start | bytes 294916
  18.3 4.0 %collective-permute-start.6 = (bf16[2,192,128]{2,1,0:T(8,128)(2,1)S(1)}, bf16[2,192,128]{2,1,0:T(8,128)(2,1)S(1)}, u32[]{:S(2)}, u32[]{:S(2)}) collective-permute-start(bf16[2,192,128]{2,1,0:T(8,128)(2,1)S(1)} %get-tuple-element.64), channel_id=1, source_target_pairs={{1,0},{0,1},{3,2},{2,3},{5,4},{4,5},{7,6},{6,7},{9,8},{8,9},{11,10... | collective-permute-start | bytes 294920 | tf_op jit(solution)/shard_map/ppermute | solution.py:351
  18.3 14.1 %collective-permute-start.4 = (bf16[2,192,384]{2,1,0:T(8,128)(2,1)S(1)}, bf16[2,192,384]{2,1,0:T(8,128)(2,1)S(1)}, u32[]{:S(2)}, u32[]{:S(2)}) collective-permute-start(bf16[2,192,384]{2,1,0:T(8,128)(2,1)S(1)} %get-tuple-element.61), channel_id=1, source_target_pairs={{0,4},{1,5},{2,6},{3,7},{4,8},{5,9},{6,10},{7,11},{8,12},{9,13},{1... | collective-permute-start | bytes 884744 | tf_op jit(solution)/shard_map/ppermute | solution.py:357
  19.7 14.7 %collective-permute-start.5 = (bf16[2,192,384]{2,1,0:T(8,128)(2,1)S(1)}, bf16[2,192,384]{2,1,0:T(8,128)(2,1)S(1)}, u32[]{:S(2)}, u32[]{:S(2)}) collective-permute-start(bf16[2,192,384]{2,1,0:T(8,128)(2,1)S(1)} %get-tuple-element.62), channel_id=1, source_target_pairs={{0,12},{1,13},{2,14},{3,15},{4,0},{5,1},{6,2},{7,3},{8,4},{9,5},{1... | collective-permute-start | bytes 884744 | tf_op jit(solution)/shard_map/ppermute | solution.py:358
  21.8 3.8 %collective-permute-start.7 = (bf16[2,192,128]{2,1,0:T(8,128)(2,1)S(1)}, bf16[2,192,128]{2,1,0:T(8,128)(2,1)S(1)}, u32[]{:S(2)}, u32[]{:S(2)}) collective-permute-start(bf16[2,192,128]{2,1,0:T(8,128)(2,1)S(1)} %get-tuple-element.65), channel_id=1, source_target_pairs={{2,0},{3,1},{0,2},{1,3},{6,4},{7,5},{4,6},{5,7},{10,8},{11,9},{8,1... | collective-permute-start | bytes 294920 | tf_op jit(solution)/shard_map/ppermute | solution.py:351
  22.3 6.7 %collective-permute-start.8 = (bf16[2,192,128]{2,1,0:T(8,128)(2,1)S(1)}, bf16[2,192,128]{2,1,0:T(8,128)(2,1)S(1)}, u32[]{:S(2)}, u32[]{:S(2)}) collective-permute-start(bf16[2,192,128]{2,1,0:T(8,128)(2,1)S(1)} %get-tuple-element.66), channel_id=1, source_target_pairs={{3,0},{2,1},{1,2},{0,3},{7,4},{6,5},{5,6},{4,7},{11,8},{10,9},{9,1... | collective-permute-start | bytes 294920 | tf_op jit(solution)/shard_map/ppermute | solution.py:351
  29.1 13.5 %collective-permute-start.12 = (bf16[2,192,384]{2,1,0:T(8,128)(2,1)S(1)}, bf16[2,192,384]{2,1,0:T(8,128)(2,1)S(1)}, u32[]{:S(2)}, u32[]{:S(2)}) collective-permute-start(bf16[2,192,384]{2,1,0:T(8,128)(2,1)S(1)} %get-tuple-element.80), channel_id=1, source_target_pairs={{0,4},{1,5},{2,6},{3,7},{4,8},{5,9},{6,10},{7,11},{8,12},{9,13},{1... | collective-permute-start | bytes 884744 | tf_op jit(solution)/shard_map/ppermute | solution.py:357
  29.2 17.8 %collective-permute-start.13 = (bf16[2,192,384]{2,1,0:T(8,128)(2,1)S(1)}, bf16[2,192,384]{2,1,0:T(8,128)(2,1)S(1)}, u32[]{:S(2)}, u32[]{:S(2)}) collective-permute-start(bf16[2,192,384]{2,1,0:T(8,128)(2,1)S(1)} %get-tuple-element.81), channel_id=1, source_target_pairs={{0,12},{1,13},{2,14},{3,15},{4,0},{5,1},{6,2},{7,3},{8,4},{9,5},{1... | collective-permute-start | bytes 884744 | tf_op jit(solution)/shard_map/ppermute | solution.py:358
  38.1 4.5 %collective-permute-start.19 = (bf16[96,768]{1,0:T(8,128)(2,1)S(1)}, bf16[96,768]{1,0:T(8,128)(2,1)S(1)}, u32[]{:S(2)}, u32[]{:S(2)}) collective-permute-start(bf16[96,768]{1,0:T(8,128)(2,1)S(1)} %get-tuple-element.74.refs_5_), channel_id=1, source_target_pairs={{0,16},{16,0},{1,17},{17,1},{2,18},{18,2},{3,19},{19,3},{4,20},{20... | collective-permute-start | bytes 442376 | tf_op jit(solution)/shard_map/ppermute | solution.py:362
  42.0 18.6 %collective-permute-start.10 = (bf16[2,2,192,128]{3,2,1,0:T(8,128)(2,1)S(1)}, bf16[2,2,192,128]{3,2,1,0:T(8,128)(2,1)S(1)}, u32[]{:S(2)}, u32[]{:S(2)}) collective-permute-start(bf16[2,2,192,128]{3,2,1,0:T(8,128)(2,1)S(1)} %get-tuple-element.76), channel_id=1, source_target_pairs={{2,0},{3,1},{0,2},{1,3},{6,4},{7,5},{4,6},{5,7},{10,8},{11,9},{8,1... | collective-permute-start | bytes 589832 | tf_op jit(solution)/shard_map/ppermute | solution.py:351
  47.0 5.8 %collective-permute-start.20 = (bf16[48,768]{1,0:T(8,128)(2,1)S(1)}, bf16[48,768]{1,0:T(8,128)(2,1)S(1)}, u32[]{:S(2)}, u32[]{:S(2)}) collective-permute-start(bf16[48,768]{1,0:T(8,128)(2,1)S(1)} %get-tuple-element.95), channel_id=1, source_target_pairs={{4,0},{5,1},{6,2},{7,3},{0,4},{1,5},{2,6},{3,7},{12,8},{13,9},{14,... | collective-permute-start | bytes 221192 | tf_op jit(solution)/shard_map/ppermute | solution.py:351
  48.5 4.3 %collective-permute-start.14 = (f32[8,384]{1,0:T(8,128)S(1)}, f32[8,384]{1,0:T(8,128)S(1)}, u32[]{:S(2)}, u32[]{:S(2)}) collective-permute-start(f32[8,384]{1,0:T(8,128)S(1)} %get-tuple-element.82), channel_id=1, source_target_pairs={{0,4},{1,5},{2,6},{3,7},{4,8},{5,9},{6,10},{7,11},{8,12},{9,13},{1... | collective-permute-start | bytes 36872 | tf_op jit(solution)/shard_map/ppermute | solution.py:357
  48.6 4.3 %collective-permute-start.15 = (f32[8,384]{1,0:T(8,128)S(1)}, f32[8,384]{1,0:T(8,128)S(1)}, u32[]{:S(2)}, u32[]{:S(2)}) collective-permute-start(f32[8,384]{1,0:T(8,128)S(1)} %get-tuple-element.83), channel_id=1, source_target_pairs={{0,12},{1,13},{2,14},{3,15},{4,0},{5,1},{6,2},{7,3},{8,4},{9,5},{1... | collective-permute-start | bytes 36872 | tf_op jit(solution)/shard_map/ppermute | solution.py:358
  52.9 7.7 %collective-permute-start.21 = (bf16[48,768]{1,0:T(8,128)(2,1)S(1)}, bf16[48,768]{1,0:T(8,128)(2,1)S(1)}, u32[]{:S(2)}, u32[]{:S(2)}) collective-permute-start(bf16[48,768]{1,0:T(8,128)(2,1)S(1)} %add.2.refs_0_), channel_id=1, source_target_pairs={{8,0},{9,1},{10,2},{11,3},{12,4},{13,5},{14,6},{15,7},{0,8},{1,9},... | collective-permute-start | bytes 221192 | tf_op jit(solution)/shard_map/ppermute | solution.py:351
  56.6 14.4 %copy-start.1 = (bf16[768,768]{1,0:T(8,128)(2,1)S(1)}, bf16[768,768]{1,0:T(8,128)(2,1)}, u32[]{:S(2)}) copy-start(bf16[768,768]{1,0:T(8,128)(2,1)} %weight_ref.3) | copy-start | bytes 3538948
  56.6 8.1 %collective-permute-start.16 = (bf16[2,192,128]{2,1,0:T(8,128)(2,1)S(1)}, bf16[2,192,128]{2,1,0:T(8,128)(2,1)S(1)}, u32[]{:S(2)}, u32[]{:S(2)}) collective-permute-start(bf16[2,192,128]{2,1,0:T(8,128)(2,1)S(1)} %get-tuple-element.87), channel_id=1, source_target_pairs={{1,0},{0,1},{3,2},{2,3},{5,4},{4,5},{7,6},{6,7},{9,8},{8,9},{11,10... | collective-permute-start | bytes 294920 | tf_op jit(solution)/shard_map/ppermute | solution.py:351
  58.9 5.8 %collective-permute-start.17 = (bf16[2,192,128]{2,1,0:T(8,128)(2,1)S(1)}, bf16[2,192,128]{2,1,0:T(8,128)(2,1)S(1)}, u32[]{:S(2)}, u32[]{:S(2)}) collective-permute-start(bf16[2,192,128]{2,1,0:T(8,128)(2,1)S(1)} %get-tuple-element.88), channel_id=1, source_target_pairs={{2,0},{3,1},{0,2},{1,3},{6,4},{7,5},{4,6},{5,7},{10,8},{11,9},{8,1... | collective-permute-start | bytes 294920 | tf_op jit(solution)/shard_map/ppermute | solution.py:351
  59.4 6.4 %collective-permute-start.18 = (bf16[2,192,128]{2,1,0:T(8,128)(2,1)S(1)}, bf16[2,192,128]{2,1,0:T(8,128)(2,1)S(1)}, u32[]{:S(2)}, u32[]{:S(2)}) collective-permute-start(bf16[2,192,128]{2,1,0:T(8,128)(2,1)S(1)} %get-tuple-element.89), channel_id=1, source_target_pairs={{3,0},{2,1},{1,2},{0,3},{7,4},{6,5},{5,6},{4,7},{11,8},{10,9},{9,1... | collective-permute-start | bytes 294920 | tf_op jit(solution)/shard_map/ppermute | solution.py:351
  60.6 6.0 %collective-permute-start.22 = (bf16[48,768]{1,0:T(8,128)(2,1)S(1)}, bf16[48,768]{1,0:T(8,128)(2,1)S(1)}, u32[]{:S(2)}, u32[]{:S(2)}) collective-permute-start(bf16[48,768]{1,0:T(8,128)(2,1)S(1)} %add.3.refs_0_), channel_id=1, source_target_pairs={{4,0},{5,1},{6,2},{7,3},{0,4},{1,5},{2,6},{3,7},{12,8},{13,9},{14,... | collective-permute-start | bytes 221192 | tf_op jit(solution)/shard_map/ppermute | solution.py:351
  64.2 6.9 %collective-permute-start.11 = (bf16[2,2,192,128]{3,2,1,0:T(8,128)(2,1)S(1)}, bf16[2,2,192,128]{3,2,1,0:T(8,128)(2,1)S(1)}, u32[]{:S(2)}, u32[]{:S(2)}) collective-permute-start(bf16[2,2,192,128]{3,2,1,0:T(8,128)(2,1)S(1)} %relay.1), channel_id=1, source_target_pairs={{1,0},{0,1},{3,2},{2,3},{5,4},{4,5},{7,6},{6,7},{9,8},{8,9},{11,10... | collective-permute-start | bytes 589832 | tf_op jit(solution)/shard_map/ppermute | solution.py:351
  66.6 7.4 %collective-permute-start.24 = (bf16[96,768]{1,0:T(8,128)(2,1)S(1)}, bf16[96,768]{1,0:T(8,128)(2,1)S(1)}, u32[]{:S(2)}, u32[]{:S(2)}) collective-permute-start(bf16[96,768]{1,0:T(8,128)(2,1)S(1)} %join.1.refs_0_), channel_id=1, source_target_pairs={{2,16},{3,17},{6,20},{7,21},{10,24},{11,25},{14,28},{15,29},{16,2}... | collective-permute-start | bytes 442376 | tf_op jit(solution)/shard_map/ppermute | solution.py:486
  70.0 4.4 %collective-permute-start.23 = (bf16[96,768]{1,0:T(8,128)(2,1)S(1)}, bf16[96,768]{1,0:T(8,128)(2,1)S(1)}, u32[]{:S(2)}, u32[]{:S(2)}) collective-permute-start(bf16[96,768]{1,0:T(8,128)(2,1)S(1)} %join.1.refs_0_), channel_id=1, source_target_pairs={{0,2},{1,3},{2,18},{3,19},{4,6},{5,7},{6,22},{7,23},{8,10},{9,11},... | collective-permute-start | bytes 442376 | tf_op jit(solution)/shard_map/ppermute | solution.py:486
  74.5 3.2 %collective-permute-start.25 = (bf16[192,768]{1,0:T(8,128)(2,1)S(1)}, bf16[192,768]{1,0:T(8,128)(2,1)S(1)}, u32[]{:S(2)}, u32[]{:S(2)}) collective-permute-start(bf16[192,768]{1,0:T(8,128)(2,1)S(1)} %cross.1.mine_ref), channel_id=1, source_target_pairs={{1,0},{0,1},{3,2},{2,3},{5,4},{4,5},{7,6},{6,7},{9,8},{8,9},{11,10... | collective-permute-start | bytes 884744 | tf_op jit(solution)/shard_map/ppermute | solution.py:351

commit v8 on v7

--- a/solution.py
+++ b/solution.py
@@ -329,7 +329,7 @@
         out_ref[at] = value
 
 
-def cross_kernel(mine_ref, first_ref, second_ref, out_ref):
+def cross_kernel(mine_ref, second_ref, first_ref, out_ref):
     window = lax.rem(lax.axis_index("dp"), 2)
     other, here = halves(window, mine_ref.shape[0])
     at_home = bit_of(2) == window
@@ -382,15 +382,18 @@
         [pltpu.VMEM((2, span, width), bf16), pltpu.VMEM((2, width, span), bf16), dma((2,))],
         limit=58, name="pack",
     )
-    up, down, pair = gather((mine, *in_layer(parts)), (g_across,))
-    mine, *parts, g_copy = call(
+    q, *parts = lax.optimization_barrier((q, *parts))
+    parts = in_layer(parts)
+    up, down, pair = gather((mine, *parts), (g_across,))
+    mine, *query_parts, g_copy = call(
         project_kernel, [VMEM] * 3, [part_shape] * LAYER + [flat_shape],
         (q, g, out_weight), [pltpu.VMEM((2, width, span), bf16)], name="project",
     )
-    up, *parts = lax.optimization_barrier((up, *parts))
+    up, *query_parts = lax.optimization_barrier((up, *query_parts))
     kv_low, kv_high = along(up, down)
     (g_pair,) = call(
         pair_kernel, [VMEM] * 2, [shape_of(2, span, width)], (g_copy, g_across), name="pair",
+        after=parts,
     )
     g_pairs = g_pair, swap(g_pair, 1)
     bias, dead = call(
@@ -398,7 +401,7 @@
         [shape_of(16, LAYER * span, dtype=f32), shape_of(8, HOPS * span, dtype=f32)],
         (partner_ids, partner_count), name="live",
     )
-    up, down, query = gather((mine, *in_layer(parts)), (bias, g_pairs[1]))
+    up, down, query = gather((mine, *in_layer(query_parts)), (bias, g_pairs[1]))
     qg_low, qg_high = along(up, down)
     stats_shape = shape_of(8, HOPS * span, dtype=f32)
     mixed, stats, up, down, probs, window = call(
@@ -456,17 +459,17 @@
         send, part = call(
             functools.partial(split_kernel, LAYER), [VMEM] * 2,
             [shape_of(count, width), shape_of(count, width, dtype=f32)],
-            (part, got), name="split", after=(query_token, qg_low, qg_high),
+            (part, got), name="split", after=(query_token, qg_low, qg_high, stats_low, stats_high),
         )
 
         def add_round(part, got, after=()):
             out = [shape_of(count, width)]
             return call(round_kernel, [VMEM] * 2, out, (part, got), name="add", after=after)[0]
 
-        total = add_round(part, swap(send, LAYER), (stats_low, stats_high))
+        total = add_round(part, swap(send, LAYER), (key_token,))
         stride = 2 * LAYER
         while stride < stations:
-            total = add_round(total, swap(total, stride), (key_token, across))
+            total = add_round(total, swap(total, stride), (across,))
             stride *= 2
         (total,) = call(
             functools.partial(join_kernel, LAYER, None), [VMEM] * 2, [shape_of(2 * count, width)],
@@ -483,7 +486,7 @@
         axes = ("dp", "station")
         (total,) = call(
             cross_kernel, [VMEM] * 3, [shape_of(4 * count, width)],
-            (total, lax.ppermute(total, axes, first), lax.ppermute(total, axes, second)),
+            (total, lax.ppermute(total, axes, second), lax.ppermute(total, axes, first)),
             name="cross", after=(output_token, key_output_token),
         )
         (grad_weight,) = call(

time: 80.1 us -> 75.6 us (0.944)
  waiting for transfers between devices: 23.2 us -> 17.8 us
  starting transfers between devices: 33.9 us -> 35.8 us
  local copies, waits for them, and re-layouts: 4.11 us -> 3.23 us
    ppermute x17, waiting for transfers between devices: 13.6 us -> 9.18 us  [swap(): lax.ppermute(value, 'station', [(s ^ stride, s) for s in range(stations)])]
    ppermute x3, waiting for transfers between devices: 6.22 us -> 3.12 us  [along(): lax.ppermute(down, 'station', [(s, (s - LAYER) % stations) for s in range...]
    ppermute x3, waiting for transfers between devices: 1.08 us -> 3.68 us  [along(): lax.ppermute(up, 'station', [(s, (s + LAYER) % stations) for s in range(s...]
    ppermute x3, starting transfers between devices: 1.47 us -> 3.25 us  [along(): lax.ppermute(up, 'station', [(s, (s + LAYER) % stations) for s in range(s...]
    ppermute x3, starting transfers between devices: 8.54 us -> 7.24 us  [along(): lax.ppermute(down, 'station', [(s, (s - LAYER) % stations) for s in range...]
    ppermute x1, starting transfers between devices: 0.06 us -> 1.08 us  [local(): lax.ppermute(total, axes, first)]
    ppermute x17, starting transfers between devices: 19.1 us -> 20.1 us  [swap(): lax.ppermute(value, 'station', [(s ^ stride, s) for s in range(stations)])]
    unnamed x15, local copies, waits for them, and re-layouts: 4.11 us -> 3.23 us
  transfers between devices with their start and end apart: 26 -> 26, of which waited for: 12 -> 10; matrix products, arithmetic and copies ran while one was open for 0% -> 0% of each run, Pallas kernels for 20% -> 21%
where the time goes in v8:
time: 75.6 us; the launch traced here: 74.5 us
  starting transfers between devices  35.8 us (47%)
  waiting for transfers between devices  17.8 us (24%)
  Pallas kernels  16.7 us (22%)
  local copies, waits for them, and re-layouts  3.23 us (4%)
  between operations  0.83 us (1%)
    ppermute x17, starting transfers between devices, swap(): lax.ppermute(value, 'station', [(s ^ stride, s) for s in range(stations)])  20.1 us
    pallas_call x19, Pallas kernels, call(): pl.pallas_call(kernel, in_specs=ins, out_specs=[VMEM] * len(outs), out_sh...  16.7 us
    ppermute x17, waiting for transfers between devices, swap(): lax.ppermute(value, 'station', [(s ^ stride, s) for s in range(stations)])  9.18 us
    ppermute x3, starting transfers between devices, along(): lax.ppermute(down, 'station', [(s, (s - LAYER) % stations) for s in range...  7.24 us
    ppermute x3, waiting for transfers between devices, along(): lax.ppermute(up, 'station', [(s, (s + LAYER) % stations) for s in range(s...  3.68 us
    ppermute x3, starting transfers between devices, along(): lax.ppermute(up, 'station', [(s, (s + LAYER) % stations) for s in range(s...  3.25 us
    unnamed x15, local copies, waits for them, and re-layouts  3.23 us
    ppermute x3, waiting for transfers between devices, along(): lax.ppermute(down, 'station', [(s, (s - LAYER) % stations) for s in range...  3.12 us
  transfers between devices with their start and end apart: 26, of which 10 were waited for; matrix products, arithmetic and copies ran while one was open for 0% of the time, Pallas kernels for 21%

profile of v8, /device:TPU:3, one launch (start us, length us, event | category | flops | bytes accessed | tf_op | source)
XLA Modules:
  0.0 74.5 jit_solution(6833010925615026100)
XLA Ops:
  0.6 0.1 collective-permute-start.3
  0.7 1.9 %pack.1 = (bf16[2,192,128]{2,1,0:T(8,128)(2,1)}, bf16[2,192,128]{2,1,0:T(8,128)(2,1)}, bf16[2,192,128]{2,1,0:T(8,128)(2,1)}, bf16[2,192,128]{2,1,0:T(8,128)(2,1)}) custom-call(bf16[128,768]{1,0:T(8,128)(2,1)} %bitcast.11, bf16[128,768]{1,0:T(8,128)(2,1)} %bitcast.12), custom_call_target="tpu_custom_call" | custom-call | flops 1 | bytes 1 | tf_op jit(solution)/shard_map/pack/pallas_call | solution.py:50
  2.6 0.7 collective-permute-start
  3.4 1.7 %collective-permute-start.1 = (bf16[2,192,128]{2,1,0:T(8,128)(2,1)}, bf16[2,192,128]{2,1,0:T(8,128)(2,1)S(1)}, u32[]{:S(2)}, u32[]{:S(2)}) collective-permute-start(bf16[2,192,128]{2,1,0:T(8,128)(2,1)} %get-tuple-element.61), channel_id=1, source_target_pairs={{2,0},{3,1},{0,2},{1,3},{6,4},{7,5},{4,6},{5,7},{10,8},{11,9},{8,1... | collective-permute-start | bytes 294920 | tf_op jit(solution)/shard_map/ppermute | solution.py:351
  5.2 1.3 %copy-done = bf16[768,768]{1,0:T(8,128)(2,1)S(1)} copy-done((bf16[768,768]{1,0:T(8,128)(2,1)S(1)}, bf16[768,768]{1,0:T(8,128)(2,1)}, u32[]{:S(2)}) %copy-start) | copy-done | bytes 1179672
  6.4 0.9 %copy-done.2 = bf16[1,1,128,768]{3,2,1,0:T(8,128)(2,1)S(1)} copy-done((bf16[1,1,128,768]{3,2,1,0:T(8,128)(2,1)S(1)}, bf16[1,1,128,768]{3,2,1,0:T(8,128)(2,1)}, u32[]{:S(2)}) %copy-start.2) | copy-done | bytes 196632
  7.4 0.9 %copy-done.3 = bf16[1,1,128,768]{3,2,1,0:T(8,128)(2,1)S(1)} copy-done((bf16[1,1,128,768]{3,2,1,0:T(8,128)(2,1)S(1)}, bf16[1,1,128,768]{3,2,1,0:T(8,128)(2,1)}, u32[]{:S(2)}) %copy-start.3) | copy-done | bytes 196632
  8.3 0.5 project.1
  8.8 2.9 %collective-permute-done.2.refs_3_.refs_4_ = bf16[2,192,128]{2,1,0:T(8,128)(2,1)S(1)} collective-permute-done((bf16[2,192,128]{2,1,0:T(8,128)(2,1)}, bf16[2,192,128]{2,1,0:T(8,128)(2,1)S(1)}, u32[]{:S(2)}, u32[]{:S(2)}) %collective-permute-start.2) | collective-permute-done | bytes 98336 | tf_op jit(solution)/shard_map/ppermute | solution.py:351
  11.9 0.1 gather.2
  12.0 0.5 collective-permute-start.6
  12.6 1.3 %collective-permute-start.4 = (bf16[2,192,384]{2,1,0:T(8,128)(2,1)S(1)}, bf16[2,192,384]{2,1,0:T(8,128)(2,1)S(1)}, u32[]{:S(2)}, u32[]{:S(2)}) collective-permute-start(bf16[2,192,384]{2,1,0:T(8,128)(2,1)S(1)} %get-tuple-element.69), channel_id=1, source_target_pairs={{0,4},{1,5},{2,6},{3,7},{4,8},{5,9},{6,10},{7,11},{8,12},{9,13},{1... | collective-permute-start | bytes 884744 | tf_op jit(solution)/shard_map/ppermute | solution.py:357
  13.9 2.0 %collective-permute-start.5 = (bf16[2,192,384]{2,1,0:T(8,128)(2,1)S(1)}, bf16[2,192,384]{2,1,0:T(8,128)(2,1)S(1)}, u32[]{:S(2)}, u32[]{:S(2)}) collective-permute-start(bf16[2,192,384]{2,1,0:T(8,128)(2,1)S(1)} %get-tuple-element.70), channel_id=1, source_target_pairs={{0,12},{1,13},{2,14},{3,15},{4,0},{5,1},{6,2},{7,3},{8,4},{9,5},{1... | collective-permute-start | bytes 884744 | tf_op jit(solution)/shard_map/ppermute | solution.py:358
  15.9 0.3 collective-permute-start.7
  16.2 1.9 %collective-permute-start.8 = (bf16[2,192,128]{2,1,0:T(8,128)(2,1)S(1)}, bf16[2,192,128]{2,1,0:T(8,128)(2,1)S(1)}, u32[]{:S(2)}, u32[]{:S(2)}) collective-permute-start(bf16[2,192,128]{2,1,0:T(8,128)(2,1)S(1)} %get-tuple-element.74), channel_id=1, source_target_pairs={{3,0},{2,1},{1,2},{0,3},{7,4},{6,5},{5,6},{4,7},{11,8},{10,9},{9,1... | collective-permute-start | bytes 294920 | tf_op jit(solution)/shard_map/ppermute | solution.py:351
  18.1 0.1 copy.12.ids_ref
  18.2 1.2 %live.1 = (f32[16,512]{1,0:T(8,128)S(1)}, f32[8,384]{1,0:T(8,128)S(1)}) custom-call(s32[16,6]{1,0:T(8,128)S(1)} %copy.12.ids_ref, s32[16]{0:T(128)S(1)} %copy-done.5), custom_call_target="tpu_custom_call" | custom-call | flops 1 | bytes 1 | tf_op jit(solution)/shard_map/live/pallas_call | solution.py:50
  19.4 0.3 collective-permute-done.7.refs_2_
  19.7 3.1 %collective-permute-done.8.refs_3_ = bf16[2,192,128]{2,1,0:T(8,128)(2,1)S(1)} collective-permute-done((bf16[2,192,128]{2,1,0:T(8,128)(2,1)S(1)}, bf16[2,192,128]{2,1,0:T(8,128)(2,1)S(1)}, u32[]{:S(2)}, u32[]{:S(2)}) %collective-permute-start.8) | collective-permute-done | bytes 98336 | tf_op jit(solution)/shard_map/ppermute | solution.py:351
  22.8 0.1 gather.3
  23.0 3.3 %collective-permute-start.13 = (bf16[2,192,384]{2,1,0:T(8,128)(2,1)S(1)}, bf16[2,192,384]{2,1,0:T(8,128)(2,1)S(1)}, u32[]{:S(2)}, u32[]{:S(2)}) collective-permute-start(bf16[2,192,384]{2,1,0:T(8,128)(2,1)S(1)} %get-tuple-element.89), channel_id=1, source_target_pairs={{0,12},{1,13},{2,14},{3,15},{4,0},{5,1},{6,2},{7,3},{8,4},{9,5},{1... | collective-permute-start | bytes 884744 | tf_op jit(solution)/shard_map/ppermute | solution.py:358
  26.3 2.3 %collective-permute-done.5.high_ref = bf16[2,192,384]{2,1,0:T(8,128)(2,1)S(1)} collective-permute-done((bf16[2,192,384]{2,1,0:T(8,128)(2,1)S(1)}, bf16[2,192,384]{2,1,0:T(8,128)(2,1)S(1)}, u32[]{:S(2)}, u32[]{:S(2)}) %collective-permute-start.5) | collective-permute-done | bytes 294944 | tf_op jit(solution)/shard_map/ppermute | solution.py:358
  28.6 3.3 %forward.1 = (bf16[192,512]{1,0:T(8,128)(2,1)S(1)}, f32[8,512]{1,0:T(8,128)S(1)}, f32[8,384]{1,0:T(8,128)S(1)}, f32[8,384]{1,0:T(8,128)S(1)}, bf16[3,1280,512]{2...) custom-call(bf16[2,192,512]{2,1,0:T(8,128)(2,1)S(1)} %get-tuple-element.63.pair_ref, ...), custom_call_target="tpu_custom_call" | custom-call | flops 1 | bytes 1 | tf_op jit(solution)/shard_map/forward/pallas_call | solution.py:50
  31.9 0.5 weight.1
  32.4 1.3 %collective-permute-start.19 = (bf16[96,768]{1,0:T(8,128)(2,1)S(1)}, bf16[96,768]{1,0:T(8,128)(2,1)S(1)}, u32[]{:S(2)}, u32[]{:S(2)}) collective-permute-start(bf16[96,768]{1,0:T(8,128)(2,1)S(1)} %get-tuple-element.82.refs_5_), channel_id=1, source_target_pairs={{0,16},{16,0},{1,17},{17,1},{2,18},{18,2},{3,19},{19,3},{4,20},{20... | collective-permute-start | bytes 442376 | tf_op jit(solution)/shard_map/ppermute | solution.py:362
  33.7 2.6 %query_grad.1 = (bf16[2,192,128]{2,1,0:T(8,128)(2,1)S(1)}, bf16[2,192,128]{2,1,0:T(8,128)(2,1)S(1)}, bf16[2,2,192,128]{3,2,1,0:T(8,128)(2,1)S(1)}, f32[2,192,512]{2,1,0:T(8,128)S(1)}, f32[8,128]{1,0:T(8,128)S(1)}) custom-call(bf16[2,192,1280]{2,1,0:T(8,128)(2,1)S(1)} %get-tuple-element.78.refs_0_, bf16[3,1280,512]{2,1,0:T(8,128)(2,1)S(1)} %get-tuple-element.79.refs_1_, ...), custom_call_target="tpu_custom_call" | custom-call | flops 1 | bytes 1 | tf_op jit(solution)/shard_map/query_grad/pallas_call | solution.py:50
  36.2 0.3 collective-permute-start.10
  36.5 1.9 %collective-permute-start.14 = (f32[8,384]{1,0:T(8,128)S(1)}, f32[8,384]{1,0:T(8,128)S(1)}, u32[]{:S(2)}, u32[]{:S(2)}) collective-permute-start(f32[8,384]{1,0:T(8,128)S(1)} %get-tuple-element.90), channel_id=1, source_target_pairs={{0,4},{1,5},{2,6},{3,7},{4,8},{5,9},{6,10},{7,11},{8,12},{9,13},{1... | collective-permute-start | bytes 36872 | tf_op jit(solution)/shard_map/ppermute | solution.py:357
  38.4 3.7 %collective-permute-done.14.stats_low.refs_5_ = f32[8,384]{1,0:T(8,128)S(1)} collective-permute-done((f32[8,384]{1,0:T(8,128)S(1)}, f32[8,384]{1,0:T(8,128)S(1)}, u32[]{:S(2)}, u32[]{:S(2)}) %collective-permute-start.14) | collective-permute-done | bytes 12320 | tf_op jit(solution)/shard_map/ppermute | solution.py:357
  42.1 2.0 %collective-permute-start.15 = (f32[8,384]{1,0:T(8,128)S(1)}, f32[8,384]{1,0:T(8,128)S(1)}, u32[]{:S(2)}, u32[]{:S(2)}) collective-permute-start(f32[8,384]{1,0:T(8,128)S(1)} %get-tuple-element.91), channel_id=1, source_target_pairs={{0,12},{1,13},{2,14},{3,15},{4,0},{5,1},{6,2},{7,3},{8,4},{9,5},{1... | collective-permute-start | bytes 36872 | tf_op jit(solution)/shard_map/ppermute | solution.py:358
  44.1 0.8 %collective-permute-done.15.stats_high.refs_6_ = f32[8,384]{1,0:T(8,128)S(1)} collective-permute-done((f32[8,384]{1,0:T(8,128)S(1)}, f32[8,384]{1,0:T(8,128)S(1)}, u32[]{:S(2)}, u32[]{:S(2)}) %collective-permute-start.15) | collective-permute-done | bytes 12320 | tf_op jit(solution)/shard_map/ppermute | solution.py:358
  45.0 3.2 %key_grad.1 = (bf16[2,192,128]{2,1,0:T(8,128)(2,1)S(1)}, bf16[2,192,128]{2,1,0:T(8,128)(2,1)S(1)}, bf16[2,192,128]{2,1,0:T(8,128)(2,1)S(1)}, bf16[2,192,128]{2,1,0:T(8,128)(2,1)S(1)}, f32[8,128]{1,0:T(8,128)S(1)}) custom-call(bf16[2,192,512]{2,1,0:T(8,128)(2,1)S(1)} %get-tuple-element.63.pair_ref, ...), custom_call_target="tpu_custom_call" | custom-call | flops 1 | bytes 1 | tf_op jit(solution)/shard_map/key_grad/pallas_call | solution.py:50
  48.3 0.1 collective-permute-done.20.refs_1_
  48.4 3.8 %collective-permute-start.21 = (bf16[48,768]{1,0:T(8,128)(2,1)S(1)}, bf16[48,768]{1,0:T(8,128)(2,1)S(1)}, u32[]{:S(2)}, u32[]{:S(2)}) collective-permute-start(bf16[48,768]{1,0:T(8,128)(2,1)S(1)} %add.2.refs_0_), channel_id=1, source_target_pairs={{8,0},{9,1},{10,2},{11,3},{12,4},{13,5},{14,6},{15,7},{0,8},{1,9},... | collective-permute-start | bytes 221192 | tf_op jit(solution)/shard_map/ppermute | solution.py:351
  52.1 2.4 %collective-permute-start.16 = (bf16[2,192,128]{2,1,0:T(8,128)(2,1)S(1)}, bf16[2,192,128]{2,1,0:T(8,128)(2,1)S(1)}, u32[]{:S(2)}, u32[]{:S(2)}) collective-permute-start(bf16[2,192,128]{2,1,0:T(8,128)(2,1)S(1)} %get-tuple-element.95), channel_id=1, source_target_pairs={{1,0},{0,1},{3,2},{2,3},{5,4},{4,5},{7,6},{6,7},{9,8},{8,9},{11,10... | collective-permute-start | bytes 294920 | tf_op jit(solution)/shard_map/ppermute | solution.py:351
  54.5 0.9 %collective-permute-start.17 = (bf16[2,192,128]{2,1,0:T(8,128)(2,1)S(1)}, bf16[2,192,128]{2,1,0:T(8,128)(2,1)S(1)}, u32[]{:S(2)}, u32[]{:S(2)}) collective-permute-start(bf16[2,192,128]{2,1,0:T(8,128)(2,1)S(1)} %get-tuple-element.96), channel_id=1, source_target_pairs={{2,0},{3,1},{0,2},{1,3},{6,4},{7,5},{4,6},{5,7},{10,8},{11,9},{8,1... | collective-permute-start | bytes 294920 | tf_op jit(solution)/shard_map/ppermute | solution.py:351
  55.4 0.8 %collective-permute-start.18 = (bf16[2,192,128]{2,1,0:T(8,128)(2,1)S(1)}, bf16[2,192,128]{2,1,0:T(8,128)(2,1)S(1)}, u32[]{:S(2)}, u32[]{:S(2)}) collective-permute-start(bf16[2,192,128]{2,1,0:T(8,128)(2,1)S(1)} %get-tuple-element.97), channel_id=1, source_target_pairs={{3,0},{2,1},{1,2},{0,3},{7,4},{6,5},{5,6},{4,7},{11,8},{10,9},{9,1... | collective-permute-start | bytes 294920 | tf_op jit(solution)/shard_map/ppermute | solution.py:351
  56.2 0.9 %collective-permute-start.22 = (bf16[48,768]{1,0:T(8,128)(2,1)S(1)}, bf16[48,768]{1,0:T(8,128)(2,1)S(1)}, u32[]{:S(2)}, u32[]{:S(2)}) collective-permute-start(bf16[48,768]{1,0:T(8,128)(2,1)S(1)} %add.3.refs_0_), channel_id=1, source_target_pairs={{4,0},{5,1},{6,2},{7,3},{0,4},{1,5},{2,6},{3,7},{12,8},{13,9},{14,... | collective-permute-start | bytes 221192 | tf_op jit(solution)/shard_map/ppermute | solution.py:351
  57.2 2.5 %collective-permute-start.11 = (bf16[2,2,192,128]{3,2,1,0:T(8,128)(2,1)S(1)}, bf16[2,2,192,128]{3,2,1,0:T(8,128)(2,1)S(1)}, u32[]{:S(2)}, u32[]{:S(2)}) collective-permute-start(bf16[2,2,192,128]{3,2,1,0:T(8,128)(2,1)S(1)} %relay.1), channel_id=1, source_target_pairs={{1,0},{0,1},{3,2},{2,3},{5,4},{4,5},{7,6},{6,7},{9,8},{8,9},{11,10... | collective-permute-start | bytes 589832 | tf_op jit(solution)/shard_map/ppermute | solution.py:351
  59.6 1.5 %collective-permute-done.18.refs_3_.refs_4_ = bf16[2,192,128]{2,1,0:T(8,128)(2,1)S(1)} collective-permute-done((bf16[2,192,128]{2,1,0:T(8,128)(2,1)S(1)}, bf16[2,192,128]{2,1,0:T(8,128)(2,1)S(1)}, u32[]{:S(2)}, u32[]{:S(2)}) %collective-permute-start.18) | collective-permute-done | bytes 98336 | tf_op jit(solution)/shard_map/ppermute | solution.py:351
  61.2 1.1 %collective-permute-start.24 = (bf16[96,768]{1,0:T(8,128)(2,1)S(1)}, bf16[96,768]{1,0:T(8,128)(2,1)S(1)}, u32[]{:S(2)}, u32[]{:S(2)}) collective-permute-start(bf16[96,768]{1,0:T(8,128)(2,1)S(1)} %join.1.refs_0_), channel_id=1, source_target_pairs={{0,2},{1,3},{2,18},{3,19},{4,6},{5,7},{6,22},{7,23},{8,10},{9,11},... | collective-permute-start | bytes 442376 | tf_op jit(solution)/shard_map/ppermute | solution.py:489
  62.3 2.9 %collective-permute-start.23 = (bf16[96,768]{1,0:T(8,128)(2,1)S(1)}, bf16[96,768]{1,0:T(8,128)(2,1)S(1)}, u32[]{:S(2)}, u32[]{:S(2)}) collective-permute-start(bf16[96,768]{1,0:T(8,128)(2,1)S(1)} %join.1.refs_0_), channel_id=1, source_target_pairs={{2,16},{3,17},{6,20},{7,21},{10,24},{11,25},{14,28},{15,29},{16,2}... | collective-permute-start | bytes 442376 | tf_op jit(solution)/shard_map/ppermute | solution.py:489
  65.2 0.9 %key_output.1 = (bf16[128,768]{1,0:T(8,128)(2,1)}, bf16[128,768]{1,0:T(8,128)(2,1)}, f32[8,128]{1,0:T(8,128)S(1)}) custom-call(bf16[2,192,128]{2,1,0:T(8,128)(2,1)S(1)} %get-tuple-element.94.refs_0_, bf16[2,192,128]{2,1,0:T(8,128)(2,1)S(1)} %collective-permute-done.16.refs_1_.refs_2_, bf16[2,192,128]{2,1,0:T(8,128)(2,1)S(1)} %collective-permute-done.17.refs_2_.refs_3_, ...), custom_call_target="tpu_custom_call" | custom-call | flops 1 | bytes 1 | tf_op jit(solution)/shard_map/key_output/pallas_call | solution.py:50
  66.1 1.1 %output.1 = (bf16[128,768]{1,0:T(8,128)(2,1)}, bf16[128,768]{1,0:T(8,128)(2,1)}, f32[8,128]{1,0:T(8,128)S(1)}) custom-call(bf16[2,192,128]{2,1,0:T(8,128)(2,1)S(1)} %get-tuple-element.83.mine_ref, bf16[2,2,192,128]{3,2,1,0:T(8,128)(2,1)S(1)} %collective-permute-done.10.across_ref.refs_2_, bf16[2,2,192,128]{3,2,1,0:T(8,128)(2,1)S(1)} %collective-permute-done.11.sib_ref, ...), custom_call_target="tpu_custom_call" | custom-call | flops 1 | bytes 1 | tf_op jit(solution)/shard_map/output/pallas_call | solution.py:50
  67.2 1.9 %collective-permute-done.23.refs_1_ = bf16[96,768]{1,0:T(8,128)(2,1)S(1)} collective-permute-done((bf16[96,768]{1,0:T(8,128)(2,1)S(1)}, bf16[96,768]{1,0:T(8,128)(2,1)S(1)}, u32[]{:S(2)}, u32[]{:S(2)}) %collective-permute-start.23) | collective-permute-done | bytes 147488 | tf_op jit(solution)/shard_map/ppermute | solution.py:489
  69.1 3.1 %collective-permute-start.25 = (bf16[192,768]{1,0:T(8,128)(2,1)S(1)}, bf16[192,768]{1,0:T(8,128)(2,1)S(1)}, u32[]{:S(2)}, u32[]{:S(2)}) collective-permute-start(bf16[192,768]{1,0:T(8,128)(2,1)S(1)} %cross.1.mine_ref), channel_id=1, source_target_pairs={{1,0},{0,1},{3,2},{2,3},{5,4},{4,5},{7,6},{6,7},{9,8},{8,9},{11,10... | collective-permute-start | bytes 884744 | tf_op jit(solution)/shard_map/ppermute | solution.py:351
  72.2 1.2 %collective-permute-done.25.got_ref = bf16[192,768]{1,0:T(8,128)(2,1)S(1)} collective-permute-done((bf16[192,768]{1,0:T(8,128)(2,1)S(1)}, bf16[192,768]{1,0:T(8,128)(2,1)S(1)}, u32[]{:S(2)}, u32[]{:S(2)}) %collective-permute-start.25) | collective-permute-done | bytes 294944 | tf_op jit(solution)/shard_map/ppermute | solution.py:351
  73.4 1.1 %last.1 = f32[384,768]{1,0:T(8,128)} custom-call(bf16[192,768]{1,0:T(8,128)(2,1)S(1)} %cross.1.mine_ref, bf16[192,768]{1,0:T(8,128)(2,1)S(1)} %collective-permute-done.25.got_ref), custom_call_target="tpu_custom_call" | custom-call | flops 1 | bytes 1 | tf_op jit(solution)/shard_map/last/pallas_call | solution.py:50
  (38 shorter events, 0.5 us)
Async XLA Ops:
  0.6 11.1 %collective-permute-start.3 = (bf16[128,768]{1,0:T(8,128)(2,1)}, bf16[128,768]{1,0:T(8,128)(2,1)S(1)}, u32[]{:S(2)}, u32[]{:S(2)}) collective-permute-start(bf16[128,768]{1,0:T(8,128)(2,1)} %bitcast.9), channel_id=1, source_target_pairs={{2,0},{3,1},{0,2},{1,3},{6,4},{7,5},{4,6},{5,7},{10,8},{11,9},{8,1... | collective-permute-start | bytes 589832 | tf_op jit(solution)/shard_map/ppermute | solution.py:351
  2.6 6.2 %collective-permute-start = (bf16[2,192,128]{2,1,0:T(8,128)(2,1)}, bf16[2,192,128]{2,1,0:T(8,128)(2,1)S(1)}, u32[]{:S(2)}, u32[]{:S(2)}) collective-permute-start(bf16[2,192,128]{2,1,0:T(8,128)(2,1)} %get-tuple-element.60), channel_id=1, source_target_pairs={{1,0},{0,1},{3,2},{2,3},{5,4},{4,5},{7,6},{6,7},{9,8},{8,9},{11,10... | collective-permute-start | bytes 294920 | tf_op jit(solution)/shard_map/ppermute | solution.py:351
  3.4 5.5 %collective-permute-start.1 = (bf16[2,192,128]{2,1,0:T(8,128)(2,1)}, bf16[2,192,128]{2,1,0:T(8,128)(2,1)S(1)}, u32[]{:S(2)}, u32[]{:S(2)}) collective-permute-start(bf16[2,192,128]{2,1,0:T(8,128)(2,1)} %get-tuple-element.61), channel_id=1, source_target_pairs={{2,0},{3,1},{0,2},{1,3},{6,4},{7,5},{4,6},{5,7},{10,8},{11,9},{8,1... | collective-permute-start | bytes 294920 | tf_op jit(solution)/shard_map/ppermute | solution.py:351
  5.1 6.6 %collective-permute-start.2 = (bf16[2,192,128]{2,1,0:T(8,128)(2,1)}, bf16[2,192,128]{2,1,0:T(8,128)(2,1)S(1)}, u32[]{:S(2)}, u32[]{:S(2)}) collective-permute-start(bf16[2,192,128]{2,1,0:T(8,128)(2,1)} %get-tuple-element.62), channel_id=1, source_target_pairs={{3,0},{2,1},{1,2},{0,3},{7,4},{6,5},{5,6},{4,7},{11,8},{10,9},{9,1... | collective-permute-start | bytes 294920 | tf_op jit(solution)/shard_map/ppermute | solution.py:351
  5.2 1.3 %copy-start = (bf16[768,768]{1,0:T(8,128)(2,1)S(1)}, bf16[768,768]{1,0:T(8,128)(2,1)}, u32[]{:S(2)}) copy-start(bf16[768,768]{1,0:T(8,128)(2,1)} %weight_ref.3) | copy-start | bytes 3538948
  6.4 0.9 %copy-start.2 = (bf16[1,1,128,768]{3,2,1,0:T(8,128)(2,1)S(1)}, bf16[1,1,128,768]{3,2,1,0:T(8,128)(2,1)}, u32[]{:S(2)}) copy-start(bf16[1,1,128,768]{3,2,1,0:T(8,128)(2,1)} %param.7) | copy-start | bytes 589828
  7.4 0.9 %copy-start.3 = (bf16[1,1,128,768]{3,2,1,0:T(8,128)(2,1)S(1)}, bf16[1,1,128,768]{3,2,1,0:T(8,128)(2,1)}, u32[]{:S(2)}) copy-start(bf16[1,1,128,768]{3,2,1,0:T(8,128)(2,1)} %param.10) | copy-start | bytes 589828
  8.3 3.6 %copy-start.4 = (bf16[2,192,128]{2,1,0:T(8,128)(2,1)S(1)}, bf16[2,192,128]{2,1,0:T(8,128)(2,1)}, u32[]{:S(2)}) copy-start(bf16[2,192,128]{2,1,0:T(8,128)(2,1)} %get-tuple-element.56.refs_0_) | copy-start | bytes 294916
  8.8 9.3 %copy-start.6 = (s32[16,6]{0,1:T(8,128)S(1)}, s32[16,6]{0,1:T(8,128)}, u32[]{:S(2)}) copy-start(s32[16,6]{0,1:T(8,128)} %param.12) | copy-start | bytes 1156
  8.8 9.4 %copy-start.5 = (s32[16]{0:T(128)S(1)}, s32[16]{0:T(128)}, u32[]{:S(2)}) copy-start(s32[16]{0:T(128)} %count_ref.1) | copy-start | bytes 196
  11.8 11.0 %collective-permute-start.9 = (bf16[2,128,768]{2,1,0:T(8,128)(2,1)S(1)}, bf16[2,128,768]{2,1,0:T(8,128)(2,1)S(1)}, u32[]{:S(2)}, u32[]{:S(2)}) collective-permute-start(bf16[2,128,768]{2,1,0:T(8,128)(2,1)S(1)} %pair.1.mine_ref), channel_id=1, source_target_pairs={{1,0},{0,1},{3,2},{2,3},{5,4},{4,5},{7,6},{6,7},{9,8},{8,9},{11,10... | collective-permute-start | bytes 1179656 | tf_op jit(solution)/shard_map/ppermute | solution.py:351
  12.0 4.1 %collective-permute-start.6 = (bf16[2,192,128]{2,1,0:T(8,128)(2,1)S(1)}, bf16[2,192,128]{2,1,0:T(8,128)(2,1)S(1)}, u32[]{:S(2)}, u32[]{:S(2)}) collective-permute-start(bf16[2,192,128]{2,1,0:T(8,128)(2,1)S(1)} %get-tuple-element.72), channel_id=1, source_target_pairs={{1,0},{0,1},{3,2},{2,3},{5,4},{4,5},{7,6},{6,7},{9,8},{8,9},{11,10... | collective-permute-start | bytes 294920 | tf_op jit(solution)/shard_map/ppermute | solution.py:351
  12.6 13.7 %collective-permute-start.4 = (bf16[2,192,384]{2,1,0:T(8,128)(2,1)S(1)}, bf16[2,192,384]{2,1,0:T(8,128)(2,1)S(1)}, u32[]{:S(2)}, u32[]{:S(2)}) collective-permute-start(bf16[2,192,384]{2,1,0:T(8,128)(2,1)S(1)} %get-tuple-element.69), channel_id=1, source_target_pairs={{0,4},{1,5},{2,6},{3,7},{4,8},{5,9},{6,10},{7,11},{8,12},{9,13},{1... | collective-permute-start | bytes 884744 | tf_op jit(solution)/shard_map/ppermute | solution.py:357
  13.9 14.7 %collective-permute-start.5 = (bf16[2,192,384]{2,1,0:T(8,128)(2,1)S(1)}, bf16[2,192,384]{2,1,0:T(8,128)(2,1)S(1)}, u32[]{:S(2)}, u32[]{:S(2)}) collective-permute-start(bf16[2,192,384]{2,1,0:T(8,128)(2,1)S(1)} %get-tuple-element.70), channel_id=1, source_target_pairs={{0,12},{1,13},{2,14},{3,15},{4,0},{5,1},{6,2},{7,3},{8,4},{9,5},{1... | collective-permute-start | bytes 884744 | tf_op jit(solution)/shard_map/ppermute | solution.py:358
  15.9 3.8 %collective-permute-start.7 = (bf16[2,192,128]{2,1,0:T(8,128)(2,1)S(1)}, bf16[2,192,128]{2,1,0:T(8,128)(2,1)S(1)}, u32[]{:S(2)}, u32[]{:S(2)}) collective-permute-start(bf16[2,192,128]{2,1,0:T(8,128)(2,1)S(1)} %get-tuple-element.73), channel_id=1, source_target_pairs={{2,0},{3,1},{0,2},{1,3},{6,4},{7,5},{4,6},{5,7},{10,8},{11,9},{8,1... | collective-permute-start | bytes 294920 | tf_op jit(solution)/shard_map/ppermute | solution.py:351
  16.2 6.7 %collective-permute-start.8 = (bf16[2,192,128]{2,1,0:T(8,128)(2,1)S(1)}, bf16[2,192,128]{2,1,0:T(8,128)(2,1)S(1)}, u32[]{:S(2)}, u32[]{:S(2)}) collective-permute-start(bf16[2,192,128]{2,1,0:T(8,128)(2,1)S(1)} %get-tuple-element.74), channel_id=1, source_target_pairs={{3,0},{2,1},{1,2},{0,3},{7,4},{6,5},{5,6},{4,7},{11,8},{10,9},{9,1... | collective-permute-start | bytes 294920 | tf_op jit(solution)/shard_map/ppermute | solution.py:351
  23.0 21.9 %collective-permute-start.12 = (bf16[2,192,384]{2,1,0:T(8,128)(2,1)S(1)}, bf16[2,192,384]{2,1,0:T(8,128)(2,1)S(1)}, u32[]{:S(2)}, u32[]{:S(2)}) collective-permute-start(bf16[2,192,384]{2,1,0:T(8,128)(2,1)S(1)} %get-tuple-element.88), channel_id=1, source_target_pairs={{0,4},{1,5},{2,6},{3,7},{4,8},{5,9},{6,10},{7,11},{8,12},{9,13},{1... | collective-permute-start | bytes 884744 | tf_op jit(solution)/shard_map/ppermute | solution.py:357
  23.0 21.9 %collective-permute-start.13 = (bf16[2,192,384]{2,1,0:T(8,128)(2,1)S(1)}, bf16[2,192,384]{2,1,0:T(8,128)(2,1)S(1)}, u32[]{:S(2)}, u32[]{:S(2)}) collective-permute-start(bf16[2,192,384]{2,1,0:T(8,128)(2,1)S(1)} %get-tuple-element.89), channel_id=1, source_target_pairs={{0,12},{1,13},{2,14},{3,15},{4,0},{5,1},{6,2},{7,3},{8,4},{9,5},{1... | collective-permute-start | bytes 884744 | tf_op jit(solution)/shard_map/ppermute | solution.py:358
  32.4 12.5 %collective-permute-start.19 = (bf16[96,768]{1,0:T(8,128)(2,1)S(1)}, bf16[96,768]{1,0:T(8,128)(2,1)S(1)}, u32[]{:S(2)}, u32[]{:S(2)}) collective-permute-start(bf16[96,768]{1,0:T(8,128)(2,1)S(1)} %get-tuple-element.82.refs_5_), channel_id=1, source_target_pairs={{0,16},{16,0},{1,17},{17,1},{2,18},{18,2},{3,19},{19,3},{4,20},{20... | collective-permute-start | bytes 442376 | tf_op jit(solution)/shard_map/ppermute | solution.py:362
  36.2 20.0 %collective-permute-start.10 = (bf16[2,2,192,128]{3,2,1,0:T(8,128)(2,1)S(1)}, bf16[2,2,192,128]{3,2,1,0:T(8,128)(2,1)S(1)}, u32[]{:S(2)}, u32[]{:S(2)}) collective-permute-start(bf16[2,2,192,128]{3,2,1,0:T(8,128)(2,1)S(1)} %get-tuple-element.84), channel_id=1, source_target_pairs={{2,0},{3,1},{0,2},{1,3},{6,4},{7,5},{4,6},{5,7},{10,8},{11,9},{8,1... | collective-permute-start | bytes 589832 | tf_op jit(solution)/shard_map/ppermute | solution.py:351
  36.5 5.6 %collective-permute-start.14 = (f32[8,384]{1,0:T(8,128)S(1)}, f32[8,384]{1,0:T(8,128)S(1)}, u32[]{:S(2)}, u32[]{:S(2)}) collective-permute-start(f32[8,384]{1,0:T(8,128)S(1)} %get-tuple-element.90), channel_id=1, source_target_pairs={{0,4},{1,5},{2,6},{3,7},{4,8},{5,9},{6,10},{7,11},{8,12},{9,13},{1... | collective-permute-start | bytes 36872 | tf_op jit(solution)/shard_map/ppermute | solution.py:357
  42.1 2.8 %collective-permute-start.15 = (f32[8,384]{1,0:T(8,128)S(1)}, f32[8,384]{1,0:T(8,128)S(1)}, u32[]{:S(2)}, u32[]{:S(2)}) collective-permute-start(f32[8,384]{1,0:T(8,128)S(1)} %get-tuple-element.91), channel_id=1, source_target_pairs={{0,12},{1,13},{2,14},{3,15},{4,0},{5,1},{6,2},{7,3},{8,4},{9,5},{1... | collective-permute-start | bytes 36872 | tf_op jit(solution)/shard_map/ppermute | solution.py:358
  45.0 3.4 %collective-permute-start.20 = (bf16[48,768]{1,0:T(8,128)(2,1)S(1)}, bf16[48,768]{1,0:T(8,128)(2,1)S(1)}, u32[]{:S(2)}, u32[]{:S(2)}) collective-permute-start(bf16[48,768]{1,0:T(8,128)(2,1)S(1)} %get-tuple-element.103), channel_id=1, source_target_pairs={{4,0},{5,1},{6,2},{7,3},{0,4},{1,5},{2,6},{3,7},{12,8},{13,9},{14,... | collective-permute-start | bytes 221192 | tf_op jit(solution)/shard_map/ppermute | solution.py:351
  48.2 17.9 %copy-start.1 = (bf16[768,768]{1,0:T(8,128)(2,1)S(1)}, bf16[768,768]{1,0:T(8,128)(2,1)}, u32[]{:S(2)}) copy-start(bf16[768,768]{1,0:T(8,128)(2,1)} %weight_ref.3) | copy-start | bytes 3538948
  48.4 7.8 %collective-permute-start.21 = (bf16[48,768]{1,0:T(8,128)(2,1)S(1)}, bf16[48,768]{1,0:T(8,128)(2,1)S(1)}, u32[]{:S(2)}, u32[]{:S(2)}) collective-permute-start(bf16[48,768]{1,0:T(8,128)(2,1)S(1)} %add.2.refs_0_), channel_id=1, source_target_pairs={{8,0},{9,1},{10,2},{11,3},{12,4},{13,5},{14,6},{15,7},{0,8},{1,9},... | collective-permute-start | bytes 221192 | tf_op jit(solution)/shard_map/ppermute | solution.py:351
  52.1 7.5 %collective-permute-start.16 = (bf16[2,192,128]{2,1,0:T(8,128)(2,1)S(1)}, bf16[2,192,128]{2,1,0:T(8,128)(2,1)S(1)}, u32[]{:S(2)}, u32[]{:S(2)}) collective-permute-start(bf16[2,192,128]{2,1,0:T(8,128)(2,1)S(1)} %get-tuple-element.95), channel_id=1, source_target_pairs={{1,0},{0,1},{3,2},{2,3},{5,4},{4,5},{7,6},{6,7},{9,8},{8,9},{11,10... | collective-permute-start | bytes 294920 | tf_op jit(solution)/shard_map/ppermute | solution.py:351
  54.5 5.1 %collective-permute-start.17 = (bf16[2,192,128]{2,1,0:T(8,128)(2,1)S(1)}, bf16[2,192,128]{2,1,0:T(8,128)(2,1)S(1)}, u32[]{:S(2)}, u32[]{:S(2)}) collective-permute-start(bf16[2,192,128]{2,1,0:T(8,128)(2,1)S(1)} %get-tuple-element.96), channel_id=1, source_target_pairs={{2,0},{3,1},{0,2},{1,3},{6,4},{7,5},{4,6},{5,7},{10,8},{11,9},{8,1... | collective-permute-start | bytes 294920 | tf_op jit(solution)/shard_map/ppermute | solution.py:351
  55.4 5.8 %collective-permute-start.18 = (bf16[2,192,128]{2,1,0:T(8,128)(2,1)S(1)}, bf16[2,192,128]{2,1,0:T(8,128)(2,1)S(1)}, u32[]{:S(2)}, u32[]{:S(2)}) collective-permute-start(bf16[2,192,128]{2,1,0:T(8,128)(2,1)S(1)} %get-tuple-element.97), channel_id=1, source_target_pairs={{3,0},{2,1},{1,2},{0,3},{7,4},{6,5},{5,6},{4,7},{11,8},{10,9},{9,1... | collective-permute-start | bytes 294920 | tf_op jit(solution)/shard_map/ppermute | solution.py:351
  56.2 5.0 %collective-permute-start.22 = (bf16[48,768]{1,0:T(8,128)(2,1)S(1)}, bf16[48,768]{1,0:T(8,128)(2,1)S(1)}, u32[]{:S(2)}, u32[]{:S(2)}) collective-permute-start(bf16[48,768]{1,0:T(8,128)(2,1)S(1)} %add.3.refs_0_), channel_id=1, source_target_pairs={{4,0},{5,1},{6,2},{7,3},{0,4},{1,5},{2,6},{3,7},{12,8},{13,9},{14,... | collective-permute-start | bytes 221192 | tf_op jit(solution)/shard_map/ppermute | solution.py:351
  57.2 9.0 %collective-permute-start.11 = (bf16[2,2,192,128]{3,2,1,0:T(8,128)(2,1)S(1)}, bf16[2,2,192,128]{3,2,1,0:T(8,128)(2,1)S(1)}, u32[]{:S(2)}, u32[]{:S(2)}) collective-permute-start(bf16[2,2,192,128]{3,2,1,0:T(8,128)(2,1)S(1)} %relay.1), channel_id=1, source_target_pairs={{1,0},{0,1},{3,2},{2,3},{5,4},{4,5},{7,6},{6,7},{9,8},{8,9},{11,10... | collective-permute-start | bytes 589832 | tf_op jit(solution)/shard_map/ppermute | solution.py:351
  61.2 6.0 %collective-permute-start.24 = (bf16[96,768]{1,0:T(8,128)(2,1)S(1)}, bf16[96,768]{1,0:T(8,128)(2,1)S(1)}, u32[]{:S(2)}, u32[]{:S(2)}) collective-permute-start(bf16[96,768]{1,0:T(8,128)(2,1)S(1)} %join.1.refs_0_), channel_id=1, source_target_pairs={{0,2},{1,3},{2,18},{3,19},{4,6},{5,7},{6,22},{7,23},{8,10},{9,11},... | collective-permute-start | bytes 442376 | tf_op jit(solution)/shard_map/ppermute | solution.py:489
  62.3 6.8 %collective-permute-start.23 = (bf16[96,768]{1,0:T(8,128)(2,1)S(1)}, bf16[96,768]{1,0:T(8,128)(2,1)S(1)}, u32[]{:S(2)}, u32[]{:S(2)}) collective-permute-start(bf16[96,768]{1,0:T(8,128)(2,1)S(1)} %join.1.refs_0_), channel_id=1, source_target_pairs={{2,16},{3,17},{6,20},{7,21},{10,24},{11,25},{14,28},{15,29},{16,2}... | collective-permute-start | bytes 442376 | tf_op jit(solution)/shard_map/ppermute | solution.py:489
  69.1 4.3 %collective-permute-start.25 = (bf16[192,768]{1,0:T(8,128)(2,1)S(1)}, bf16[192,768]{1,0:T(8,128)(2,1)S(1)}, u32[]{:S(2)}, u32[]{:S(2)}) collective-permute-start(bf16[192,768]{1,0:T(8,128)(2,1)S(1)} %cross.1.mine_ref), channel_id=1, source_target_pairs={{1,0},{0,1},{3,2},{2,3},{5,4},{4,5},{7,6},{6,7},{9,8},{8,9},{11,10... | collective-permute-start | bytes 884744 | tf_op jit(solution)/shard_map/ppermute | solution.py:351

commit v9 on v8

--- a/solution.py
+++ b/solution.py
@@ -423,7 +423,7 @@
         (mixed, *g_pairs), [pltpu.VMEM((LAYER * span, width), bf16)], name="weight",
     )
 
-    mine, to_sib, to_across, own_grad, query_token = call(
+    own_return, to_sib, to_across, own_grad, query_token = call(
         query_grad_kernel, [VMEM] * 5,
         [part_shape, part_shape, shape_of(2, 2, rows, span), shape_of(2, rows, LAYER * span, dtype=f32)]
         + [TOKEN],
@@ -431,15 +431,16 @@
         [pltpu.VMEM((BLOCKS * span, LAYER * span), bf16), pltpu.VMEM((rows, LAYER * span), bf16)],
         limit=20, name="query_grad", after=(send,),
     )
-    across = swap(to_across, 2)
-    (relay,) = call(
-        relay_kernel, [VMEM] * 2, [shape_of(2, 2, rows, span)], (to_sib, across), name="relay"
-    )
-    relayed = swap(relay, 1)
-    layer_output, grad_query, output_token = call(
-        output_kernel, [VMEM] * 4, [flat_shape] * 2 + [TOKEN],
-        (mine, across, relayed, out_weight), [pltpu.VMEM((2, width, span), bf16)], name="output",
-    )
+    def first_return(across):
+        (relay,) = call(
+            relay_kernel, [VMEM] * 2, [shape_of(2, 2, rows, span)], (to_sib, across), name="relay"
+        )
+        relayed = swap(relay, 1)
+        layer_output, grad_query, output_token = call(
+            output_kernel, [VMEM] * 4, [flat_shape] * 2 + [TOKEN],
+            (own_return, across, relayed, out_weight), [pltpu.VMEM((2, width, span), bf16)], name="output",
+        )
+        return layer_output, grad_query, output_token
 
     mine, *parts, key_token = call(
         key_grad_kernel, [VMEM] * 7, [part_shape] * LAYER + [TOKEN],
@@ -461,6 +462,10 @@
             [shape_of(count, width), shape_of(count, width, dtype=f32)],
             (part, got), name="split", after=(query_token, qg_low, qg_high, stats_low, stats_high),
         )
+
+        send, to_across = lax.optimization_barrier((send, to_across))
+        across = swap(to_across, 2)
+        layer_output, grad_query, output_token = first_return(across)
 
         def add_round(part, got, after=()):
             out = [shape_of(count, width)]
@@ -494,6 +499,7 @@
             [shape_of(8 * count, width, dtype=f32)], (total, swap(total, 1)), name="last",
         )
     else:
+        layer_output, grad_query, _ = first_return(swap(to_across, 2))
         start = lax.axis_index("station") % LAYER * rows
         all_grad = jnp.zeros((LAYER * span, width), bf16)
         for peer in range(LAYER):

time: 75.6 us -> 71.1 us (0.940); the launches traced: 74.5 us -> 70.9 us
  waiting for transfers between devices: 17.8 us -> 15.9 us
  starting transfers between devices: 35.8 us -> 34.2 us
    ppermute x3, waiting for transfers between devices: 3.68 us -> 2.61 us  [along(): lax.ppermute(up, 'station', [(s, (s + LAYER) % stations) for s in range(s...]
    ppermute x17, starting transfers between devices: 20.1 us -> 19 us  [swap(): lax.ppermute(value, 'station', [(s ^ stride, s) for s in range(stations)])]
    ppermute x3, waiting for transfers between devices: 3.12 us -> 2.29 us  [along(): lax.ppermute(down, 'station', [(s, (s - LAYER) % stations) for s in range...]
  transfers between devices with their start and end apart: 26 -> 26, of which waited for: 10 -> 8; matrix products, arithmetic and copies ran while one was open for 0% -> 0% of each run, Pallas kernels for 21% -> 22%
where the time goes in v9:
time: 71.1 us; the launch traced here: 70.9 us
  starting transfers between devices  34.2 us (48%)
  Pallas kernels  16.7 us (23%)
  waiting for transfers between devices  15.9 us (22%)
  local copies, waits for them, and re-layouts  3.23 us (5%)
  between operations  0.84 us (1%)
    ppermute x17, starting transfers between devices, swap(): lax.ppermute(value, 'station', [(s ^ stride, s) for s in range(stations)])  19 us
    pallas_call x19, Pallas kernels, call(): pl.pallas_call(kernel, in_specs=ins, out_specs=[VMEM] * len(outs), out_sh...  16.7 us
    ppermute x17, waiting for transfers between devices, swap(): lax.ppermute(value, 'station', [(s ^ stride, s) for s in range(stations)])  9.43 us
    ppermute x3, starting transfers between devices, along(): lax.ppermute(down, 'station', [(s, (s - LAYER) % stations) for s in range...  6.87 us
    ppermute x1, starting transfers between devices, local(): lax.ppermute(total, axes, second)  3.27 us
    unnamed x15, local copies, waits for them, and re-layouts  3.23 us
    ppermute x3, starting transfers between devices, along(): lax.ppermute(up, 'station', [(s, (s + LAYER) % stations) for s in range(s...  3.02 us
    ppermute x3, waiting for transfers between devices, along(): lax.ppermute(up, 'station', [(s, (s + LAYER) % stations) for s in range(s...  2.61 us
  transfers between devices with their start and end apart: 26, of which 8 were waited for; matrix products, arithmetic and copies ran while one was open for 0% of the time, Pallas kernels for 22%

profile of v9, /device:TPU:3, one launch (start us, length us, event | category | flops | bytes accessed | tf_op | source)
XLA Modules:
  0.0 70.9 jit_solution(129810002331399834)
XLA Ops:
  0.6 0.1 collective-permute-start.3
  0.7 1.9 %pack.1 = (bf16[2,192,128]{2,1,0:T(8,128)(2,1)}, bf16[2,192,128]{2,1,0:T(8,128)(2,1)}, bf16[2,192,128]{2,1,0:T(8,128)(2,1)}, bf16[2,192,128]{2,1,0:T(8,128)(2,1)}) custom-call(bf16[128,768]{1,0:T(8,128)(2,1)} %bitcast.11, bf16[128,768]{1,0:T(8,128)(2,1)} %bitcast.12), custom_call_target="tpu_custom_call" | custom-call | flops 1 | bytes 1 | tf_op jit(solution)/shard_map/pack/pallas_call | solution.py:50
  2.6 0.7 %collective-permute-start = (bf16[2,192,128]{2,1,0:T(8,128)(2,1)}, bf16[2,192,128]{2,1,0:T(8,128)(2,1)S(1)}, u32[]{:S(2)}, u32[]{:S(2)}) collective-permute-start(bf16[2,192,128]{2,1,0:T(8,128)(2,1)} %get-tuple-element.62), channel_id=1, source_target_pairs={{1,0},{0,1},{3,2},{2,3},{5,4},{4,5},{7,6},{6,7},{9,8},{8,9},{11,10... | collective-permute-start | bytes 294920 | tf_op jit(solution)/shard_map/ppermute | solution.py:351
  3.4 1.7 %collective-permute-start.1 = (bf16[2,192,128]{2,1,0:T(8,128)(2,1)}, bf16[2,192,128]{2,1,0:T(8,128)(2,1)S(1)}, u32[]{:S(2)}, u32[]{:S(2)}) collective-permute-start(bf16[2,192,128]{2,1,0:T(8,128)(2,1)} %get-tuple-element.63), channel_id=1, source_target_pairs={{2,0},{3,1},{0,2},{1,3},{6,4},{7,5},{4,6},{5,7},{10,8},{11,9},{8,1... | collective-permute-start | bytes 294920 | tf_op jit(solution)/shard_map/ppermute | solution.py:351
  5.2 1.3 %copy-done = bf16[768,768]{1,0:T(8,128)(2,1)S(1)} copy-done((bf16[768,768]{1,0:T(8,128)(2,1)S(1)}, bf16[768,768]{1,0:T(8,128)(2,1)}, u32[]{:S(2)}) %copy-start) | copy-done | bytes 1179672
  6.4 0.9 %copy-done.2 = bf16[1,1,128,768]{3,2,1,0:T(8,128)(2,1)S(1)} copy-done((bf16[1,1,128,768]{3,2,1,0:T(8,128)(2,1)S(1)}, bf16[1,1,128,768]{3,2,1,0:T(8,128)(2,1)}, u32[]{:S(2)}) %copy-start.2) | copy-done | bytes 196632
  7.4 0.9 %copy-done.3 = bf16[1,1,128,768]{3,2,1,0:T(8,128)(2,1)S(1)} copy-done((bf16[1,1,128,768]{3,2,1,0:T(8,128)(2,1)S(1)}, bf16[1,1,128,768]{3,2,1,0:T(8,128)(2,1)}, u32[]{:S(2)}) %copy-start.3) | copy-done | bytes 196632
  8.3 0.5 project.1
  8.8 2.9 %collective-permute-done.2.refs_3_.refs_4_ = bf16[2,192,128]{2,1,0:T(8,128)(2,1)S(1)} collective-permute-done((bf16[2,192,128]{2,1,0:T(8,128)(2,1)}, bf16[2,192,128]{2,1,0:T(8,128)(2,1)S(1)}, u32[]{:S(2)}, u32[]{:S(2)}) %collective-permute-start.2) | collective-permute-done | bytes 98336 | tf_op jit(solution)/shard_map/ppermute | solution.py:351
  11.8 0.1 collective-permute-start.9
  11.9 0.1 gather.2
  12.0 0.5 collective-permute-start.6
  12.6 1.3 %collective-permute-start.4 = (bf16[2,192,384]{2,1,0:T(8,128)(2,1)S(1)}, bf16[2,192,384]{2,1,0:T(8,128)(2,1)S(1)}, u32[]{:S(2)}, u32[]{:S(2)}) collective-permute-start(bf16[2,192,384]{2,1,0:T(8,128)(2,1)S(1)} %get-tuple-element.71), channel_id=1, source_target_pairs={{0,4},{1,5},{2,6},{3,7},{4,8},{5,9},{6,10},{7,11},{8,12},{9,13},{1... | collective-permute-start | bytes 884744 | tf_op jit(solution)/shard_map/ppermute | solution.py:357
  13.9 2.0 %collective-permute-start.5 = (bf16[2,192,384]{2,1,0:T(8,128)(2,1)S(1)}, bf16[2,192,384]{2,1,0:T(8,128)(2,1)S(1)}, u32[]{:S(2)}, u32[]{:S(2)}) collective-permute-start(bf16[2,192,384]{2,1,0:T(8,128)(2,1)S(1)} %get-tuple-element.72), channel_id=1, source_target_pairs={{0,12},{1,13},{2,14},{3,15},{4,0},{5,1},{6,2},{7,3},{8,4},{9,5},{1... | collective-permute-start | bytes 884744 | tf_op jit(solution)/shard_map/ppermute | solution.py:358
  15.9 0.3 collective-permute-start.7
  16.2 1.9 %collective-permute-start.8 = (bf16[2,192,128]{2,1,0:T(8,128)(2,1)S(1)}, bf16[2,192,128]{2,1,0:T(8,128)(2,1)S(1)}, u32[]{:S(2)}, u32[]{:S(2)}) collective-permute-start(bf16[2,192,128]{2,1,0:T(8,128)(2,1)S(1)} %get-tuple-element.76), channel_id=1, source_target_pairs={{3,0},{2,1},{1,2},{0,3},{7,4},{6,5},{5,6},{4,7},{11,8},{10,9},{9,1... | collective-permute-start | bytes 294920 | tf_op jit(solution)/shard_map/ppermute | solution.py:351
  18.1 0.1 copy.12.ids_ref
  18.2 1.2 %live.1 = (f32[16,512]{1,0:T(8,128)S(1)}, f32[8,384]{1,0:T(8,128)S(1)}) custom-call(s32[16,6]{1,0:T(8,128)S(1)} %copy.12.ids_ref, s32[16]{0:T(128)S(1)} %copy-done.5), custom_call_target="tpu_custom_call" | custom-call | flops 1 | bytes 1 | tf_op jit(solution)/shard_map/live/pallas_call | solution.py:50
  19.4 0.3 collective-permute-done.7.refs_2_
  19.7 3.1 %collective-permute-done.8.refs_3_ = bf16[2,192,128]{2,1,0:T(8,128)(2,1)S(1)} collective-permute-done((bf16[2,192,128]{2,1,0:T(8,128)(2,1)S(1)}, bf16[2,192,128]{2,1,0:T(8,128)(2,1)S(1)}, u32[]{:S(2)}, u32[]{:S(2)}) %collective-permute-start.8) | collective-permute-done | bytes 98336 | tf_op jit(solution)/shard_map/ppermute | solution.py:351
  22.8 0.1 gather.3
  23.0 3.3 %collective-permute-start.12 = (bf16[2,192,384]{2,1,0:T(8,128)(2,1)S(1)}, bf16[2,192,384]{2,1,0:T(8,128)(2,1)S(1)}, u32[]{:S(2)}, u32[]{:S(2)}) collective-permute-start(bf16[2,192,384]{2,1,0:T(8,128)(2,1)S(1)} %get-tuple-element.89), channel_id=1, source_target_pairs={{0,12},{1,13},{2,14},{3,15},{4,0},{5,1},{6,2},{7,3},{8,4},{9,5},{1... | collective-permute-start | bytes 884744 | tf_op jit(solution)/shard_map/ppermute | solution.py:358
  26.3 2.3 %collective-permute-done.5.high_ref = bf16[2,192,384]{2,1,0:T(8,128)(2,1)S(1)} collective-permute-done((bf16[2,192,384]{2,1,0:T(8,128)(2,1)S(1)}, bf16[2,192,384]{2,1,0:T(8,128)(2,1)S(1)}, u32[]{:S(2)}, u32[]{:S(2)}) %collective-permute-start.5) | collective-permute-done | bytes 294944 | tf_op jit(solution)/shard_map/ppermute | solution.py:358
  28.6 3.3 %forward.1 = (bf16[192,512]{1,0:T(8,128)(2,1)S(1)}, f32[8,512]{1,0:T(8,128)S(1)}, f32[8,384]{1,0:T(8,128)S(1)}, f32[8,384]{1,0:T(8,128)S(1)}, bf16[3,1280,512]{2...) custom-call(bf16[2,192,512]{2,1,0:T(8,128)(2,1)S(1)} %get-tuple-element.65.pair_ref, ...), custom_call_target="tpu_custom_call" | custom-call | flops 1 | bytes 1 | tf_op jit(solution)/shard_map/forward/pallas_call | solution.py:50
  31.9 0.5 weight.1
  32.4 1.3 %collective-permute-start.10 = (bf16[96,768]{1,0:T(8,128)(2,1)S(1)}, bf16[96,768]{1,0:T(8,128)(2,1)S(1)}, u32[]{:S(2)}, u32[]{:S(2)}) collective-permute-start(bf16[96,768]{1,0:T(8,128)(2,1)S(1)} %get-tuple-element.84.refs_5_), channel_id=1, source_target_pairs={{0,16},{16,0},{1,17},{17,1},{2,18},{18,2},{3,19},{19,3},{4,20},{20... | collective-permute-start | bytes 442376 | tf_op jit(solution)/shard_map/ppermute | solution.py:362
  33.7 1.7 %collective-permute-start.13 = (f32[8,384]{1,0:T(8,128)S(1)}, f32[8,384]{1,0:T(8,128)S(1)}, u32[]{:S(2)}, u32[]{:S(2)}) collective-permute-start(f32[8,384]{1,0:T(8,128)S(1)} %get-tuple-element.90), channel_id=1, source_target_pairs={{0,4},{1,5},{2,6},{3,7},{4,8},{5,9},{6,10},{7,11},{8,12},{9,13},{1... | collective-permute-start | bytes 36872 | tf_op jit(solution)/shard_map/ppermute | solution.py:357
  35.3 1.6 %collective-permute-start.14 = (f32[8,384]{1,0:T(8,128)S(1)}, f32[8,384]{1,0:T(8,128)S(1)}, u32[]{:S(2)}, u32[]{:S(2)}) collective-permute-start(f32[8,384]{1,0:T(8,128)S(1)} %get-tuple-element.91), channel_id=1, source_target_pairs={{0,12},{1,13},{2,14},{3,15},{4,0},{5,1},{6,2},{7,3},{8,4},{9,5},{1... | collective-permute-start | bytes 36872 | tf_op jit(solution)/shard_map/ppermute | solution.py:358
  36.9 2.6 %query_grad.1 = (bf16[2,192,128]{2,1,0:T(8,128)(2,1)S(1)}, bf16[2,192,128]{2,1,0:T(8,128)(2,1)S(1)}, bf16[2,2,192,128]{3,2,1,0:T(8,128)(2,1)S(1)}, f32[2,192,512]{2,1,0:T(8,128)S(1)}, f32[8,128]{1,0:T(8,128)S(1)}) custom-call(bf16[2,192,1280]{2,1,0:T(8,128)(2,1)S(1)} %get-tuple-element.80.refs_0_, bf16[3,1280,512]{2,1,0:T(8,128)(2,1)S(1)} %get-tuple-element.81.refs_1_, ...), custom_call_target="tpu_custom_call" | custom-call | flops 1 | bytes 1 | tf_op jit(solution)/shard_map/query_grad/pallas_call | solution.py:50
  39.5 2.6 %collective-permute-done.13.refs_5_.stats_low = f32[8,384]{1,0:T(8,128)S(1)} collective-permute-done((f32[8,384]{1,0:T(8,128)S(1)}, f32[8,384]{1,0:T(8,128)S(1)}, u32[]{:S(2)}, u32[]{:S(2)}) %collective-permute-start.13) | collective-permute-done | bytes 12320 | tf_op jit(solution)/shard_map/ppermute | solution.py:357
  42.2 0.2 collective-permute-start.15
  42.4 1.0 %collective-permute-start.20 = (bf16[48,768]{1,0:T(8,128)(2,1)S(1)}, bf16[48,768]{1,0:T(8,128)(2,1)S(1)}, u32[]{:S(2)}, u32[]{:S(2)}) collective-permute-start(bf16[48,768]{1,0:T(8,128)(2,1)S(1)} %get-tuple-element.107), channel_id=1, source_target_pairs={{4,0},{5,1},{6,2},{7,3},{0,4},{1,5},{2,6},{3,7},{12,8},{13,9},{14,... | collective-permute-start | bytes 221192 | tf_op jit(solution)/shard_map/ppermute | solution.py:351
  43.4 3.2 %key_grad.1 = (bf16[2,192,128]{2,1,0:T(8,128)(2,1)S(1)}, bf16[2,192,128]{2,1,0:T(8,128)(2,1)S(1)}, bf16[2,192,128]{2,1,0:T(8,128)(2,1)S(1)}, bf16[2,192,128]{2,1,0:T(8,128)(2,1)S(1)}, f32[8,128]{1,0:T(8,128)S(1)}) custom-call(bf16[2,192,512]{2,1,0:T(8,128)(2,1)S(1)} %get-tuple-element.65.pair_ref, ...), custom_call_target="tpu_custom_call" | custom-call | flops 1 | bytes 1 | tf_op jit(solution)/shard_map/key_grad/pallas_call | solution.py:50
  46.6 1.6 %collective-permute-start.21 = (bf16[48,768]{1,0:T(8,128)(2,1)S(1)}, bf16[48,768]{1,0:T(8,128)(2,1)S(1)}, u32[]{:S(2)}, u32[]{:S(2)}) collective-permute-start(bf16[48,768]{1,0:T(8,128)(2,1)S(1)} %add.2.refs_0_), channel_id=1, source_target_pairs={{8,0},{9,1},{10,2},{11,3},{12,4},{13,5},{14,6},{15,7},{0,8},{1,9},... | collective-permute-start | bytes 221192 | tf_op jit(solution)/shard_map/ppermute | solution.py:351
  48.3 1.9 %collective-permute-start.17 = (bf16[2,192,128]{2,1,0:T(8,128)(2,1)S(1)}, bf16[2,192,128]{2,1,0:T(8,128)(2,1)S(1)}, u32[]{:S(2)}, u32[]{:S(2)}) collective-permute-start(bf16[2,192,128]{2,1,0:T(8,128)(2,1)S(1)} %get-tuple-element.101), channel_id=1, source_target_pairs={{1,0},{0,1},{3,2},{2,3},{5,4},{4,5},{7,6},{6,7},{9,8},{8,9},{11,10... | collective-permute-start | bytes 294920 | tf_op jit(solution)/shard_map/ppermute | solution.py:351
  50.1 0.9 %collective-permute-start.18 = (bf16[2,192,128]{2,1,0:T(8,128)(2,1)S(1)}, bf16[2,192,128]{2,1,0:T(8,128)(2,1)S(1)}, u32[]{:S(2)}, u32[]{:S(2)}) collective-permute-start(bf16[2,192,128]{2,1,0:T(8,128)(2,1)S(1)} %get-tuple-element.102), channel_id=1, source_target_pairs={{2,0},{3,1},{0,2},{1,3},{6,4},{7,5},{4,6},{5,7},{10,8},{11,9},{8,1... | collective-permute-start | bytes 294920 | tf_op jit(solution)/shard_map/ppermute | solution.py:351
  51.1 0.7 collective-permute-start.19
  51.8 0.9 %collective-permute-start.22 = (bf16[48,768]{1,0:T(8,128)(2,1)S(1)}, bf16[48,768]{1,0:T(8,128)(2,1)S(1)}, u32[]{:S(2)}, u32[]{:S(2)}) collective-permute-start(bf16[48,768]{1,0:T(8,128)(2,1)S(1)} %add.3.refs_0_), channel_id=1, source_target_pairs={{4,0},{5,1},{6,2},{7,3},{0,4},{1,5},{2,6},{3,7},{12,8},{13,9},{14,... | collective-permute-start | bytes 221192 | tf_op jit(solution)/shard_map/ppermute | solution.py:351
  52.7 2.1 %collective-permute-start.16 = (bf16[2,2,192,128]{3,2,1,0:T(8,128)(2,1)S(1)}, bf16[2,2,192,128]{3,2,1,0:T(8,128)(2,1)S(1)}, u32[]{:S(2)}, u32[]{:S(2)}) collective-permute-start(bf16[2,2,192,128]{3,2,1,0:T(8,128)(2,1)S(1)} %relay.1), channel_id=1, source_target_pairs={{1,0},{0,1},{3,2},{2,3},{5,4},{4,5},{7,6},{6,7},{9,8},{8,9},{11,10... | collective-permute-start | bytes 589832 | tf_op jit(solution)/shard_map/ppermute | solution.py:351
  54.9 1.9 %collective-permute-done.19.refs_3_.refs_4_ = bf16[2,192,128]{2,1,0:T(8,128)(2,1)S(1)} collective-permute-done((bf16[2,192,128]{2,1,0:T(8,128)(2,1)S(1)}, bf16[2,192,128]{2,1,0:T(8,128)(2,1)S(1)}, u32[]{:S(2)}, u32[]{:S(2)}) %collective-permute-start.19) | collective-permute-done | bytes 98336 | tf_op jit(solution)/shard_map/ppermute | solution.py:351
  56.8 0.8 %collective-permute-start.24 = (bf16[96,768]{1,0:T(8,128)(2,1)S(1)}, bf16[96,768]{1,0:T(8,128)(2,1)S(1)}, u32[]{:S(2)}, u32[]{:S(2)}) collective-permute-start(bf16[96,768]{1,0:T(8,128)(2,1)S(1)} %join.1.refs_0_), channel_id=1, source_target_pairs={{0,2},{1,3},{2,18},{3,19},{4,6},{5,7},{6,22},{7,23},{8,10},{9,11},... | collective-permute-start | bytes 442376 | tf_op jit(solution)/shard_map/ppermute | solution.py:494
  57.6 3.3 %collective-permute-start.23 = (bf16[96,768]{1,0:T(8,128)(2,1)S(1)}, bf16[96,768]{1,0:T(8,128)(2,1)S(1)}, u32[]{:S(2)}, u32[]{:S(2)}) collective-permute-start(bf16[96,768]{1,0:T(8,128)(2,1)S(1)} %join.1.refs_0_), channel_id=1, source_target_pairs={{2,16},{3,17},{6,20},{7,21},{10,24},{11,25},{14,28},{15,29},{16,2}... | collective-permute-start | bytes 442376 | tf_op jit(solution)/shard_map/ppermute | solution.py:494
  60.9 0.9 %key_output.1 = (bf16[128,768]{1,0:T(8,128)(2,1)}, bf16[128,768]{1,0:T(8,128)(2,1)}, f32[8,128]{1,0:T(8,128)S(1)}) custom-call(bf16[2,192,128]{2,1,0:T(8,128)(2,1)S(1)} %get-tuple-element.100.refs_0_, bf16[2,192,128]{2,1,0:T(8,128)(2,1)S(1)} %collective-permute-done.17.refs_1_.refs_2_, bf16[2,192,128]{2,1,0:T(8,128)(2,1)S(1)} %collective-permute-done.18.refs_2_.refs_3_, ...), custom_call_target="tpu_custom_call" | custom-call | flops 1 | bytes 1 | tf_op jit(solution)/shard_map/key_output/pallas_call | solution.py:50
  61.8 1.1 %output.1 = (bf16[128,768]{1,0:T(8,128)(2,1)}, bf16[128,768]{1,0:T(8,128)(2,1)}, f32[8,128]{1,0:T(8,128)S(1)}) custom-call(bf16[2,192,128]{2,1,0:T(8,128)(2,1)S(1)} %get-tuple-element.85.mine_ref, bf16[2,2,192,128]{3,2,1,0:T(8,128)(2,1)S(1)} %collective-permute-done.15.across_ref.refs_2_, bf16[2,2,192,128]{3,2,1,0:T(8,128)(2,1)S(1)} %collective-permute-done.16.sib_ref, ...), custom_call_target="tpu_custom_call" | custom-call | flops 1 | bytes 1 | tf_op jit(solution)/shard_map/output/pallas_call | solution.py:50
  62.9 1.5 %collective-permute-done.23.refs_1_ = bf16[96,768]{1,0:T(8,128)(2,1)S(1)} collective-permute-done((bf16[96,768]{1,0:T(8,128)(2,1)S(1)}, bf16[96,768]{1,0:T(8,128)(2,1)S(1)}, u32[]{:S(2)}, u32[]{:S(2)}) %collective-permute-start.23) | collective-permute-done | bytes 147488 | tf_op jit(solution)/shard_map/ppermute | solution.py:494
  64.4 4.2 %collective-permute-start.25 = (bf16[192,768]{1,0:T(8,128)(2,1)S(1)}, bf16[192,768]{1,0:T(8,128)(2,1)S(1)}, u32[]{:S(2)}, u32[]{:S(2)}) collective-permute-start(bf16[192,768]{1,0:T(8,128)(2,1)S(1)} %cross.1.mine_ref), channel_id=1, source_target_pairs={{1,0},{0,1},{3,2},{2,3},{5,4},{4,5},{7,6},{6,7},{9,8},{8,9},{11,10... | collective-permute-start | bytes 884744 | tf_op jit(solution)/shard_map/ppermute | solution.py:351
  68.6 1.2 %collective-permute-done.25.got_ref = bf16[192,768]{1,0:T(8,128)(2,1)S(1)} collective-permute-done((bf16[192,768]{1,0:T(8,128)(2,1)S(1)}, bf16[192,768]{1,0:T(8,128)(2,1)S(1)}, u32[]{:S(2)}, u32[]{:S(2)}) %collective-permute-start.25) | collective-permute-done | bytes 294944 | tf_op jit(solution)/shard_map/ppermute | solution.py:351
  69.8 1.1 %last.1 = f32[384,768]{1,0:T(8,128)} custom-call(bf16[192,768]{1,0:T(8,128)(2,1)S(1)} %cross.1.mine_ref, bf16[192,768]{1,0:T(8,128)(2,1)S(1)} %collective-permute-done.25.got_ref), custom_call_target="tpu_custom_call" | custom-call | flops 1 | bytes 1 | tf_op jit(solution)/shard_map/last/pallas_call | solution.py:50
  (38 shorter events, 0.4 us)
Async XLA Ops:
  0.6 11.1 %collective-permute-start.3 = (bf16[128,768]{1,0:T(8,128)(2,1)}, bf16[128,768]{1,0:T(8,128)(2,1)S(1)}, u32[]{:S(2)}, u32[]{:S(2)}) collective-permute-start(bf16[128,768]{1,0:T(8,128)(2,1)} %bitcast.9), channel_id=1, source_target_pairs={{2,0},{3,1},{0,2},{1,3},{6,4},{7,5},{4,6},{5,7},{10,8},{11,9},{8,1... | collective-permute-start | bytes 589832 | tf_op jit(solution)/shard_map/ppermute | solution.py:351
  2.6 6.2 %collective-permute-start = (bf16[2,192,128]{2,1,0:T(8,128)(2,1)}, bf16[2,192,128]{2,1,0:T(8,128)(2,1)S(1)}, u32[]{:S(2)}, u32[]{:S(2)}) collective-permute-start(bf16[2,192,128]{2,1,0:T(8,128)(2,1)} %get-tuple-element.62), channel_id=1, source_target_pairs={{1,0},{0,1},{3,2},{2,3},{5,4},{4,5},{7,6},{6,7},{9,8},{8,9},{11,10... | collective-permute-start | bytes 294920 | tf_op jit(solution)/shard_map/ppermute | solution.py:351
  3.4 5.5 %collective-permute-start.1 = (bf16[2,192,128]{2,1,0:T(8,128)(2,1)}, bf16[2,192,128]{2,1,0:T(8,128)(2,1)S(1)}, u32[]{:S(2)}, u32[]{:S(2)}) collective-permute-start(bf16[2,192,128]{2,1,0:T(8,128)(2,1)} %get-tuple-element.63), channel_id=1, source_target_pairs={{2,0},{3,1},{0,2},{1,3},{6,4},{7,5},{4,6},{5,7},{10,8},{11,9},{8,1... | collective-permute-start | bytes 294920 | tf_op jit(solution)/shard_map/ppermute | solution.py:351
  5.1 6.6 %collective-permute-start.2 = (bf16[2,192,128]{2,1,0:T(8,128)(2,1)}, bf16[2,192,128]{2,1,0:T(8,128)(2,1)S(1)}, u32[]{:S(2)}, u32[]{:S(2)}) collective-permute-start(bf16[2,192,128]{2,1,0:T(8,128)(2,1)} %get-tuple-element.64), channel_id=1, source_target_pairs={{3,0},{2,1},{1,2},{0,3},{7,4},{6,5},{5,6},{4,7},{11,8},{10,9},{9,1... | collective-permute-start | bytes 294920 | tf_op jit(solution)/shard_map/ppermute | solution.py:351
  5.2 1.3 %copy-start = (bf16[768,768]{1,0:T(8,128)(2,1)S(1)}, bf16[768,768]{1,0:T(8,128)(2,1)}, u32[]{:S(2)}) copy-start(bf16[768,768]{1,0:T(8,128)(2,1)} %weight_ref.3) | copy-start | bytes 3538948
  6.4 0.9 %copy-start.2 = (bf16[1,1,128,768]{3,2,1,0:T(8,128)(2,1)S(1)}, bf16[1,1,128,768]{3,2,1,0:T(8,128)(2,1)}, u32[]{:S(2)}) copy-start(bf16[1,1,128,768]{3,2,1,0:T(8,128)(2,1)} %param.7) | copy-start | bytes 589828
  7.4 0.9 %copy-start.3 = (bf16[1,1,128,768]{3,2,1,0:T(8,128)(2,1)S(1)}, bf16[1,1,128,768]{3,2,1,0:T(8,128)(2,1)}, u32[]{:S(2)}) copy-start(bf16[1,1,128,768]{3,2,1,0:T(8,128)(2,1)} %param.10) | copy-start | bytes 589828
  8.3 3.6 %copy-start.4 = (bf16[2,192,128]{2,1,0:T(8,128)(2,1)S(1)}, bf16[2,192,128]{2,1,0:T(8,128)(2,1)}, u32[]{:S(2)}) copy-start(bf16[2,192,128]{2,1,0:T(8,128)(2,1)} %get-tuple-element.58.refs_0_) | copy-start | bytes 294916
  8.8 9.3 %copy-start.6 = (s32[16,6]{0,1:T(8,128)S(1)}, s32[16,6]{0,1:T(8,128)}, u32[]{:S(2)}) copy-start(s32[16,6]{0,1:T(8,128)} %param.12) | copy-start | bytes 1156
  8.8 9.4 %copy-start.5 = (s32[16]{0:T(128)S(1)}, s32[16]{0:T(128)}, u32[]{:S(2)}) copy-start(s32[16]{0:T(128)} %count_ref.1) | copy-start | bytes 196
  11.8 11.0 %collective-permute-start.9 = (bf16[2,128,768]{2,1,0:T(8,128)(2,1)S(1)}, bf16[2,128,768]{2,1,0:T(8,128)(2,1)S(1)}, u32[]{:S(2)}, u32[]{:S(2)}) collective-permute-start(bf16[2,128,768]{2,1,0:T(8,128)(2,1)S(1)} %pair.1.mine_ref), channel_id=1, source_target_pairs={{1,0},{0,1},{3,2},{2,3},{5,4},{4,5},{7,6},{6,7},{9,8},{8,9},{11,10... | collective-permute-start | bytes 1179656 | tf_op jit(solution)/shard_map/ppermute | solution.py:351
  12.0 4.1 %collective-permute-start.6 = (bf16[2,192,128]{2,1,0:T(8,128)(2,1)S(1)}, bf16[2,192,128]{2,1,0:T(8,128)(2,1)S(1)}, u32[]{:S(2)}, u32[]{:S(2)}) collective-permute-start(bf16[2,192,128]{2,1,0:T(8,128)(2,1)S(1)} %get-tuple-element.74), channel_id=1, source_target_pairs={{1,0},{0,1},{3,2},{2,3},{5,4},{4,5},{7,6},{6,7},{9,8},{8,9},{11,10... | collective-permute-start | bytes 294920 | tf_op jit(solution)/shard_map/ppermute | solution.py:351
  12.6 13.7 %collective-permute-start.4 = (bf16[2,192,384]{2,1,0:T(8,128)(2,1)S(1)}, bf16[2,192,384]{2,1,0:T(8,128)(2,1)S(1)}, u32[]{:S(2)}, u32[]{:S(2)}) collective-permute-start(bf16[2,192,384]{2,1,0:T(8,128)(2,1)S(1)} %get-tuple-element.71), channel_id=1, source_target_pairs={{0,4},{1,5},{2,6},{3,7},{4,8},{5,9},{6,10},{7,11},{8,12},{9,13},{1... | collective-permute-start | bytes 884744 | tf_op jit(solution)/shard_map/ppermute | solution.py:357
  13.9 14.7 %collective-permute-start.5 = (bf16[2,192,384]{2,1,0:T(8,128)(2,1)S(1)}, bf16[2,192,384]{2,1,0:T(8,128)(2,1)S(1)}, u32[]{:S(2)}, u32[]{:S(2)}) collective-permute-start(bf16[2,192,384]{2,1,0:T(8,128)(2,1)S(1)} %get-tuple-element.72), channel_id=1, source_target_pairs={{0,12},{1,13},{2,14},{3,15},{4,0},{5,1},{6,2},{7,3},{8,4},{9,5},{1... | collective-permute-start | bytes 884744 | tf_op jit(solution)/shard_map/ppermute | solution.py:358
  15.9 3.8 %collective-permute-start.7 = (bf16[2,192,128]{2,1,0:T(8,128)(2,1)S(1)}, bf16[2,192,128]{2,1,0:T(8,128)(2,1)S(1)}, u32[]{:S(2)}, u32[]{:S(2)}) collective-permute-start(bf16[2,192,128]{2,1,0:T(8,128)(2,1)S(1)} %get-tuple-element.75), channel_id=1, source_target_pairs={{2,0},{3,1},{0,2},{1,3},{6,4},{7,5},{4,6},{5,7},{10,8},{11,9},{8,1... | collective-permute-start | bytes 294920 | tf_op jit(solution)/shard_map/ppermute | solution.py:351
  16.2 6.7 %collective-permute-start.8 = (bf16[2,192,128]{2,1,0:T(8,128)(2,1)S(1)}, bf16[2,192,128]{2,1,0:T(8,128)(2,1)S(1)}, u32[]{:S(2)}, u32[]{:S(2)}) collective-permute-start(bf16[2,192,128]{2,1,0:T(8,128)(2,1)S(1)} %get-tuple-element.76), channel_id=1, source_target_pairs={{3,0},{2,1},{1,2},{0,3},{7,4},{6,5},{5,6},{4,7},{11,8},{10,9},{9,1... | collective-permute-start | bytes 294920 | tf_op jit(solution)/shard_map/ppermute | solution.py:351
  23.0 19.1 %collective-permute-start.11 = (bf16[2,192,384]{2,1,0:T(8,128)(2,1)S(1)}, bf16[2,192,384]{2,1,0:T(8,128)(2,1)S(1)}, u32[]{:S(2)}, u32[]{:S(2)}) collective-permute-start(bf16[2,192,384]{2,1,0:T(8,128)(2,1)S(1)} %get-tuple-element.88), channel_id=1, source_target_pairs={{0,4},{1,5},{2,6},{3,7},{4,8},{5,9},{6,10},{7,11},{8,12},{9,13},{1... | collective-permute-start | bytes 884744 | tf_op jit(solution)/shard_map/ppermute | solution.py:357
  23.0 19.1 %collective-permute-start.12 = (bf16[2,192,384]{2,1,0:T(8,128)(2,1)S(1)}, bf16[2,192,384]{2,1,0:T(8,128)(2,1)S(1)}, u32[]{:S(2)}, u32[]{:S(2)}) collective-permute-start(bf16[2,192,384]{2,1,0:T(8,128)(2,1)S(1)} %get-tuple-element.89), channel_id=1, source_target_pairs={{0,12},{1,13},{2,14},{3,15},{4,0},{5,1},{6,2},{7,3},{8,4},{9,5},{1... | collective-permute-start | bytes 884744 | tf_op jit(solution)/shard_map/ppermute | solution.py:358
  32.4 9.7 %collective-permute-start.10 = (bf16[96,768]{1,0:T(8,128)(2,1)S(1)}, bf16[96,768]{1,0:T(8,128)(2,1)S(1)}, u32[]{:S(2)}, u32[]{:S(2)}) collective-permute-start(bf16[96,768]{1,0:T(8,128)(2,1)S(1)} %get-tuple-element.84.refs_5_), channel_id=1, source_target_pairs={{0,16},{16,0},{1,17},{17,1},{2,18},{18,2},{3,19},{19,3},{4,20},{20... | collective-permute-start | bytes 442376 | tf_op jit(solution)/shard_map/ppermute | solution.py:362
  33.7 8.4 %collective-permute-start.13 = (f32[8,384]{1,0:T(8,128)S(1)}, f32[8,384]{1,0:T(8,128)S(1)}, u32[]{:S(2)}, u32[]{:S(2)}) collective-permute-start(f32[8,384]{1,0:T(8,128)S(1)} %get-tuple-element.90), channel_id=1, source_target_pairs={{0,4},{1,5},{2,6},{3,7},{4,8},{5,9},{6,10},{7,11},{8,12},{9,13},{1... | collective-permute-start | bytes 36872 | tf_op jit(solution)/shard_map/ppermute | solution.py:357
  35.3 6.8 %collective-permute-start.14 = (f32[8,384]{1,0:T(8,128)S(1)}, f32[8,384]{1,0:T(8,128)S(1)}, u32[]{:S(2)}, u32[]{:S(2)}) collective-permute-start(f32[8,384]{1,0:T(8,128)S(1)} %get-tuple-element.91), channel_id=1, source_target_pairs={{0,12},{1,13},{2,14},{3,15},{4,0},{5,1},{6,2},{7,3},{8,4},{9,5},{1... | collective-permute-start | bytes 36872 | tf_op jit(solution)/shard_map/ppermute | solution.py:358
  42.2 9.6 %collective-permute-start.15 = (bf16[2,2,192,128]{3,2,1,0:T(8,128)(2,1)S(1)}, bf16[2,2,192,128]{3,2,1,0:T(8,128)(2,1)S(1)}, u32[]{:S(2)}, u32[]{:S(2)}) collective-permute-start(bf16[2,2,192,128]{3,2,1,0:T(8,128)(2,1)S(1)} %get-tuple-element.94), channel_id=1, source_target_pairs={{2,0},{3,1},{0,2},{1,3},{6,4},{7,5},{4,6},{5,7},{10,8},{11,9},{8,1... | collective-permute-start | bytes 589832 | tf_op jit(solution)/shard_map/ppermute | solution.py:351
  42.4 4.2 %collective-permute-start.20 = (bf16[48,768]{1,0:T(8,128)(2,1)S(1)}, bf16[48,768]{1,0:T(8,128)(2,1)S(1)}, u32[]{:S(2)}, u32[]{:S(2)}) collective-permute-start(bf16[48,768]{1,0:T(8,128)(2,1)S(1)} %get-tuple-element.107), channel_id=1, source_target_pairs={{4,0},{5,1},{6,2},{7,3},{0,4},{1,5},{2,6},{3,7},{12,8},{13,9},{14,... | collective-permute-start | bytes 221192 | tf_op jit(solution)/shard_map/ppermute | solution.py:351
  46.6 15.2 %copy-start.1 = (bf16[768,768]{1,0:T(8,128)(2,1)S(1)}, bf16[768,768]{1,0:T(8,128)(2,1)}, u32[]{:S(2)}) copy-start(bf16[768,768]{1,0:T(8,128)(2,1)} %weight_ref.3) | copy-start | bytes 3538948
  46.6 5.1 %collective-permute-start.21 = (bf16[48,768]{1,0:T(8,128)(2,1)S(1)}, bf16[48,768]{1,0:T(8,128)(2,1)S(1)}, u32[]{:S(2)}, u32[]{:S(2)}) collective-permute-start(bf16[48,768]{1,0:T(8,128)(2,1)S(1)} %add.2.refs_0_), channel_id=1, source_target_pairs={{8,0},{9,1},{10,2},{11,3},{12,4},{13,5},{14,6},{15,7},{0,8},{1,9},... | collective-permute-start | bytes 221192 | tf_op jit(solution)/shard_map/ppermute | solution.py:351
  48.3 6.6 %collective-permute-start.17 = (bf16[2,192,128]{2,1,0:T(8,128)(2,1)S(1)}, bf16[2,192,128]{2,1,0:T(8,128)(2,1)S(1)}, u32[]{:S(2)}, u32[]{:S(2)}) collective-permute-start(bf16[2,192,128]{2,1,0:T(8,128)(2,1)S(1)} %get-tuple-element.101), channel_id=1, source_target_pairs={{1,0},{0,1},{3,2},{2,3},{5,4},{4,5},{7,6},{6,7},{9,8},{8,9},{11,10... | collective-permute-start | bytes 294920 | tf_op jit(solution)/shard_map/ppermute | solution.py:351
  50.1 4.7 %collective-permute-start.18 = (bf16[2,192,128]{2,1,0:T(8,128)(2,1)S(1)}, bf16[2,192,128]{2,1,0:T(8,128)(2,1)S(1)}, u32[]{:S(2)}, u32[]{:S(2)}) collective-permute-start(bf16[2,192,128]{2,1,0:T(8,128)(2,1)S(1)} %get-tuple-element.102), channel_id=1, source_target_pairs={{2,0},{3,1},{0,2},{1,3},{6,4},{7,5},{4,6},{5,7},{10,8},{11,9},{8,1... | collective-permute-start | bytes 294920 | tf_op jit(solution)/shard_map/ppermute | solution.py:351
  51.1 5.7 %collective-permute-start.19 = (bf16[2,192,128]{2,1,0:T(8,128)(2,1)S(1)}, bf16[2,192,128]{2,1,0:T(8,128)(2,1)S(1)}, u32[]{:S(2)}, u32[]{:S(2)}) collective-permute-start(bf16[2,192,128]{2,1,0:T(8,128)(2,1)S(1)} %get-tuple-element.103), channel_id=1, source_target_pairs={{3,0},{2,1},{1,2},{0,3},{7,4},{6,5},{5,6},{4,7},{11,8},{10,9},{9,1... | collective-permute-start | bytes 294920 | tf_op jit(solution)/shard_map/ppermute | solution.py:351
  51.8 5.0 %collective-permute-start.22 = (bf16[48,768]{1,0:T(8,128)(2,1)S(1)}, bf16[48,768]{1,0:T(8,128)(2,1)S(1)}, u32[]{:S(2)}, u32[]{:S(2)}) collective-permute-start(bf16[48,768]{1,0:T(8,128)(2,1)S(1)} %add.3.refs_0_), channel_id=1, source_target_pairs={{4,0},{5,1},{6,2},{7,3},{0,4},{1,5},{2,6},{3,7},{12,8},{13,9},{14,... | collective-permute-start | bytes 221192 | tf_op jit(solution)/shard_map/ppermute | solution.py:351
  52.7 9.0 %collective-permute-start.16 = (bf16[2,2,192,128]{3,2,1,0:T(8,128)(2,1)S(1)}, bf16[2,2,192,128]{3,2,1,0:T(8,128)(2,1)S(1)}, u32[]{:S(2)}, u32[]{:S(2)}) collective-permute-start(bf16[2,2,192,128]{3,2,1,0:T(8,128)(2,1)S(1)} %relay.1), channel_id=1, source_target_pairs={{1,0},{0,1},{3,2},{2,3},{5,4},{4,5},{7,6},{6,7},{9,8},{8,9},{11,10... | collective-permute-start | bytes 589832 | tf_op jit(solution)/shard_map/ppermute | solution.py:351
  56.8 6.1 %collective-permute-start.24 = (bf16[96,768]{1,0:T(8,128)(2,1)S(1)}, bf16[96,768]{1,0:T(8,128)(2,1)S(1)}, u32[]{:S(2)}, u32[]{:S(2)}) collective-permute-start(bf16[96,768]{1,0:T(8,128)(2,1)S(1)} %join.1.refs_0_), channel_id=1, source_target_pairs={{0,2},{1,3},{2,18},{3,19},{4,6},{5,7},{6,22},{7,23},{8,10},{9,11},... | collective-permute-start | bytes 442376 | tf_op jit(solution)/shard_map/ppermute | solution.py:494
  57.6 6.8 %collective-permute-start.23 = (bf16[96,768]{1,0:T(8,128)(2,1)S(1)}, bf16[96,768]{1,0:T(8,128)(2,1)S(1)}, u32[]{:S(2)}, u32[]{:S(2)}) collective-permute-start(bf16[96,768]{1,0:T(8,128)(2,1)S(1)} %join.1.refs_0_), channel_id=1, source_target_pairs={{2,16},{3,17},{6,20},{7,21},{10,24},{11,25},{14,28},{15,29},{16,2}... | collective-permute-start | bytes 442376 | tf_op jit(solution)/shard_map/ppermute | solution.py:494
  64.4 5.4 %collective-permute-start.25 = (bf16[192,768]{1,0:T(8,128)(2,1)S(1)}, bf16[192,768]{1,0:T(8,128)(2,1)S(1)}, u32[]{:S(2)}, u32[]{:S(2)}) collective-permute-start(bf16[192,768]{1,0:T(8,128)(2,1)S(1)} %cross.1.mine_ref), channel_id=1, source_target_pairs={{1,0},{0,1},{3,2},{2,3},{5,4},{4,5},{7,6},{6,7},{9,8},{8,9},{11,10... | collective-permute-start | bytes 884744 | tf_op jit(solution)/shard_map/ppermute | solution.py:351

commit v10 on v9

--- a/solution.py
+++ b/solution.py
@@ -97,11 +97,6 @@
         out[...] = flipped[:, place(peer, rows)]
 
 
-def pair_kernel(first_ref, second_ref, out_ref):
-    out_ref[0] = first_ref[...]
-    out_ref[1] = second_ref[...]
-
-
 def relay_kernel(sib_ref, across_ref, out_ref):
     out_ref[0] = sib_ref[...]
     out_ref[1] = across_ref[1]
@@ -139,10 +134,9 @@
             else:
                 reads = jnp.where(listed(inner, outer), 0.0, neg_big)
                 bias_ref[j : j + 1, block(i, span)] = reads * ones
-            if not HOPS <= j < HOPS + LAYER:
+            if j < HOPS:
                 read_by = jnp.where(listed(outer, inner), 0.0, -neg_big)
-                spot = slot if j < HOPS else slot - LAYER
-                dead_ref[i : i + 1, block(spot, span)] = read_by * ones
+                dead_ref[i : i + 1, block(slot, span)] = read_by * ones
 
 
 def clear(ref, span):
@@ -155,7 +149,7 @@
 
 def forward_kernel(
     pair_ref, low_ref, high_ref, query_ref, bias_ref,
-    mixed_ref, stats_ref, stats_up, stats_down, probs_ref, window_ref,
+    mixed_ref, stats_ref, stats_up, probs_ref, window_ref,
     raw,
 ):
     rows = query_ref.shape[1]
@@ -205,12 +199,11 @@
         stats_ref[LOCAL + head : LOCAL + head + 1] = jnp.sum(product, 0, keepdims=True)
     stats_ref[2 * LOCAL :] = jnp.zeros((8 - 2 * LOCAL, LAYER * span), f32)
     stats_up[...] = stats_ref[:, span:]
-    stats_down[...] = stats_ref[:, :reach]
 
 
 def query_grad_kernel(
     window_ref, probs_ref, query_ref, stats_ref, mixed_ref, mine_ref, sib_ref, across_ref, own_ref,
-    token_ref, grads, flipped
+    down_k, down_v, token_ref, grads, flipped
 ):
     rows = query_ref.shape[1]
     span = query_ref.shape[2] // LAYER
@@ -231,39 +224,38 @@
         flipped[at] = (dot(window_ref[0, at], grads[...], NN) * scale).astype(bf16)
         own_ref[0, at] = dot(query_ref[0, at], grads[inside], NT)
         own_ref[1, at] = dot(grad, probs_ref[head, inside], NT)
+        below = slice(0, HOPS * span)
+        down_k[at] = dot(query_ref[0, at, below], grads[below, below], NT).astype(bf16)
+        down_v[at] = dot(grad[:, below], probs_ref[head, below, below], NT).astype(bf16)
     for peer, out in enumerate((mine_ref, sib_ref, across_ref.at[0], across_ref.at[1])):
         out[0] = mixed_ref[:, place(peer, span)]
         out[1] = flipped[:, place(peer, span)]
     token_ref[...] = jnp.zeros_like(token_ref)
 
 
-def key_grad_kernel(
-    pair_ref, low_ref, high_ref, stats_low, stats_high, dead_ref, own_ref, *refs
-):
+def key_grad_kernel(pair_ref, low_ref, stats_ref, dead_ref, own_ref, above_k, above_v, *refs):
     outs, (token_ref, flipped) = refs[:LAYER], refs[LAYER:]
     rows = pair_ref.shape[1]
     span = pair_ref.shape[2] // LAYER
     head_width = rows // LOCAL
     for head in range(LOCAL):
         at = block(head, head_width)
-        log_row = slice(head, head + 1)
-        delta_row = slice(LOCAL + head, LOCAL + head + 1)
         for i in range(LAYER):
             own = block(i, span)
-
-            def outside(low, high):
-                sides = [low[:, i * span :]] if i < HOPS else []
-                return jnp.concatenate(sides + ([high[:, : i * span]] if i else []), 1)
-
-            query = outside(low_ref[0, at], high_ref[0, at])
-            grad = outside(low_ref[1, at], high_ref[1, at])
-            log_sum = outside(stats_low[log_row], stats_high[log_row]) + dead_ref[i : i + 1]
-            delta = outside(stats_low[delta_row], stats_high[delta_row])
-            prob = jnp.exp(dot(pair_ref[0, at, own], query, TN) - log_sum)
-            back = dot(pair_ref[1, at, own], grad, TN)
-            grads = (prob * (back - delta)).astype(bf16)
-            keys = own_ref[0, at, own] + dot(query, grads, NT)
-            values = own_ref[1, at, own] + dot(grad, prob.astype(bf16), NT)
+            keys, values = own_ref[0, at, own], own_ref[1, at, own]
+            if i:
+                keys = keys + above_k[at, block(i - 1, span)].astype(f32)
+                values = values + above_v[at, block(i - 1, span)].astype(f32)
+            if i < HOPS:
+                below = slice(i * span, HOPS * span)
+                query, grad = low_ref[0, at, below], low_ref[1, at, below]
+                log_sum = stats_ref[head : head + 1, below] + dead_ref[i : i + 1, : (HOPS - i) * span]
+                delta = stats_ref[LOCAL + head : LOCAL + head + 1, below]
+                prob = jnp.exp(dot(pair_ref[0, at, own], query, TN) - log_sum)
+                back = dot(pair_ref[1, at, own], grad, TN)
+                grads = (prob * (back - delta)).astype(bf16)
+                keys = keys + dot(query, grads, NT)
+                values = values + dot(grad, prob.astype(bf16), NT)
             flipped[0, at, own] = keys.astype(bf16)
             flipped[1, at, own] = values.astype(bf16)
     for peer, out in enumerate(outs):
@@ -301,10 +293,10 @@
     return lax.rem(lax.axis_index("station") // stride, 2)
 
 
-def weight_kernel(mixed_ref, mine_ref, sib_ref, send_ref, keep_ref, right):
-    for n in range(2):
-        right[place(2 * n, mine_ref.shape[1])] = mine_ref[n]
-        right[place(2 * n + 1, mine_ref.shape[1])] = sib_ref[n]
+def weight_kernel(mixed_ref, *refs):
+    ins, (send_ref, keep_ref, right) = refs[:LAYER], refs[LAYER:]
+    for peer, ref in enumerate(ins):
+        right[place(peer, ref.shape[0])] = ref[...]
     send, keep = halves(lax.rem(lax.axis_index("dp"), 2), send_ref.shape[0])
     send_ref[...] = dot(mixed_ref[send], right[...], NN).astype(bf16)
     keep_ref[...] = dot(mixed_ref[keep], right[...], NN)
@@ -353,10 +345,13 @@
     def in_layer(values):
         return [swap(values[n], n + 1) for n in range(LAYER - 1)]
 
-    def along(up, down):
-        low = lax.ppermute(up, "station", [(s, (s + LAYER) % stations) for s in range(stations)])
-        high = lax.ppermute(down, "station", [(s, (s - LAYER) % stations) for s in range(stations)])
-        return low, high
+    def from_below(value):
+        pairs = [(s, (s + LAYER) % stations) for s in range(stations)]
+        return lax.ppermute(value, "station", pairs)
+
+    def from_above(value):
+        pairs = [(s, (s - LAYER) % stations) for s in range(stations)]
+        return lax.ppermute(value, "station", pairs)
 
     def other_window(value):
         return lax.ppermute(value, "dp", [(0, 1), (1, 0)])
@@ -376,7 +371,6 @@
             name="gather", after=after,
         )
 
-    g_across = swap(g, 2)
     mine, *parts = call(
         pack_kernel, [HBM] * 2, [part_shape] * LAYER, (k, v),
         [pltpu.VMEM((2, span, width), bf16), pltpu.VMEM((2, width, span), bf16), dma((2,))],
@@ -384,49 +378,48 @@
     )
     q, *parts = lax.optimization_barrier((q, *parts))
     parts = in_layer(parts)
-    up, down, pair = gather((mine, *parts), (g_across,))
+    up, down, pair = gather((mine, *parts))
     mine, *query_parts, g_copy = call(
         project_kernel, [VMEM] * 3, [part_shape] * LAYER + [flat_shape],
         (q, g, out_weight), [pltpu.VMEM((2, width, span), bf16)], name="project",
     )
-    up, *query_parts = lax.optimization_barrier((up, *query_parts))
-    kv_low, kv_high = along(up, down)
-    (g_pair,) = call(
-        pair_kernel, [VMEM] * 2, [shape_of(2, span, width)], (g_copy, g_across), name="pair",
-        after=parts,
-    )
-    g_pairs = g_pair, swap(g_pair, 1)
+    up, g_later, *query_parts = lax.optimization_barrier((up, g, *query_parts))
+    kv_low, kv_high = from_below(up), from_above(down)
+    g_across = swap(g_later, 2)
+    g_parts = g_copy, swap(g_later, 1), g_across, swap(g_across, 1)
     bias, dead = call(
         functools.partial(live_kernel, stations), [SMEM] * 2,
         [shape_of(16, LAYER * span, dtype=f32), shape_of(8, HOPS * span, dtype=f32)],
         (partner_ids, partner_count), name="live",
     )
-    up, down, query = gather((mine, *in_layer(query_parts)), (bias, g_pairs[1]))
-    qg_low, qg_high = along(up, down)
+    up, _, query = gather((mine, *in_layer(query_parts)), (bias,))
+    qg_low = from_below(up)
     stats_shape = shape_of(8, HOPS * span, dtype=f32)
-    mixed, stats, up, down, probs, window = call(
+    mixed, stats, up, probs, window = call(
         forward_kernel, [VMEM] * 5,
         [
             shape_of(rows, LAYER * span), shape_of(8, LAYER * span, dtype=f32),
-            stats_shape, stats_shape,
-            shape_of(LOCAL, BLOCKS * span, LAYER * span), shape_of(2, rows, BLOCKS * span),
+            stats_shape, shape_of(LOCAL, BLOCKS * span, LAYER * span), shape_of(2, rows, BLOCKS * span),
         ],
         (pair, kv_low, kv_high, query, bias),
         [pltpu.VMEM((BLOCKS * span, LAYER * span), f32)],
         limit=20, name="forward",
     )
-    stats_low, stats_high = along(up, down)
+    stats_low = from_below(up)
 
     send, part = call(
-        weight_kernel, [VMEM] * 3,
+        weight_kernel, [VMEM] * (LAYER + 1),
         [shape_of(rows // 2, width), shape_of(rows // 2, width, dtype=f32)],
-        (mixed, *g_pairs), [pltpu.VMEM((LAYER * span, width), bf16)], name="weight",
-    )
-
-    own_return, to_sib, to_across, own_grad, query_token = call(
+        (mixed, *g_parts), [pltpu.VMEM((LAYER * span, width), bf16)], name="weight",
+    )
+
+    own_return, to_sib, to_across, own_grad, down_k, down_v, query_token = call(
         query_grad_kernel, [VMEM] * 5,
-        [part_shape, part_shape, shape_of(2, 2, rows, span), shape_of(2, rows, LAYER * span, dtype=f32)]
-        + [TOKEN],
+        [
+            part_shape, part_shape, shape_of(2, 2, rows, span),
+            shape_of(2, rows, LAYER * span, dtype=f32),
+            shape_of(rows, HOPS * span), shape_of(rows, HOPS * span), TOKEN,
+        ],
         (window, probs, query, stats, mixed),
         [pltpu.VMEM((BLOCKS * span, LAYER * span), bf16), pltpu.VMEM((rows, LAYER * span), bf16)],
         limit=20, name="query_grad", after=(send,),
@@ -444,7 +437,7 @@
 
     mine, *parts, key_token = call(
         key_grad_kernel, [VMEM] * 7, [part_shape] * LAYER + [TOKEN],
-        (pair, qg_low, qg_high, stats_low, stats_high, dead, own_grad),
+        (pair, qg_low, stats_low, dead, own_grad, from_above(down_k), from_above(down_v)),
         [pltpu.VMEM((2, rows, LAYER * span), bf16)], limit=20, name="key_grad",
     )
     key_parts = in_layer(parts)
@@ -460,10 +453,9 @@
         send, part = call(
             functools.partial(split_kernel, LAYER), [VMEM] * 2,
             [shape_of(count, width), shape_of(count, width, dtype=f32)],
-            (part, got), name="split", after=(query_token, qg_low, qg_high, stats_low, stats_high),
-        )
-
-        send, to_across = lax.optimization_barrier((send, to_across))
+            (part, got), name="split", after=(query_token, qg_low, stats_low),
+        )
+
         across = swap(to_across, 2)
         layer_output, grad_query, output_token = first_return(across)
 
@@ -471,10 +463,10 @@
             out = [shape_of(count, width)]
             return call(round_kernel, [VMEM] * 2, out, (part, got), name="add", after=after)[0]
 
-        total = add_round(part, swap(send, LAYER), (key_token,))
+        total = add_round(part, swap(send, LAYER), ())
         stride = 2 * LAYER
         while stride < stations:
-            total = add_round(total, swap(total, stride), (across,))
+            total = add_round(total, swap(total, stride), (across, key_token))
             stride *= 2
         (total,) = call(
             functools.partial(join_kernel, LAYER, None), [VMEM] * 2, [shape_of(2 * count, width)],
@@ -503,7 +495,7 @@
         start = lax.axis_index("station") % LAYER * rows
         all_grad = jnp.zeros((LAYER * span, width), bf16)
         for peer in range(LAYER):
-            value = g_pairs[peer % 2][peer // 2]
+            value = g_parts[peer]
             spot = lax.axis_index("station") % LAYER ^ peer
             all_grad = lax.dynamic_update_slice_in_dim(all_grad, value, spot * span, 0)
         mine = dot(mixed, all_grad, NN).astype(bf16)

time: 71.1 us -> 73 us (1.027)
  waiting for transfers between devices: 15.9 us -> 18 us
  starting transfers between devices: 34.2 us -> 33.3 us
    ppermute x17 -> x18, waiting for transfers between devices: 9.43 us -> 11.2 us  [swap(): lax.ppermute(value, 'station', [(s ^ stride, s) for s in range(stations)])]
    ppermute x6, starting transfers between devices: 9.9 us -> 8.33 us  [the longest x3 4.46 us: from_below(): return lax.ppermute(value, 'station', pairs)]
    ppermute x17 -> x18, starting transfers between devices: 19 us -> 20.3 us  [swap(): lax.ppermute(value, 'station', [(s ^ stride, s) for s in range(stations)])]
    ppermute x1, waiting for transfers between devices: 1.51 us -> 2.27 us  [local(): lax.ppermute(total, axes, second)]
    pallas_call x19 -> x18, Pallas kernels: 16.7 us -> 16.8 us  [call(): pl.pallas_call(kernel, in_specs=ins, out_specs=[VMEM] * len(outs), out_sh...]
    unnamed x15 -> x17, local copies, waits for them, and re-layouts: 3.23 us -> 3.23 us
  transfers between devices with their start and end apart: 26 -> 27, of which waited for: 8 -> 9; matrix products, arithmetic and copies ran while one was open for 0% -> 0% of each run, Pallas kernels for 22% -> 19%
where the time goes in v10:
time: 73 us; the launch traced here: 72.1 us
  starting transfers between devices  33.3 us (46%)
  waiting for transfers between devices  18 us (25%)
  Pallas kernels  16.8 us (23%)
  local copies, waits for them, and re-layouts  3.23 us (4%)
  between operations  0.82 us (1%)
    ppermute x18, starting transfers between devices, swap(): lax.ppermute(value, 'station', [(s ^ stride, s) for s in range(stations)])  20.3 us
    pallas_call x18, Pallas kernels, call(): pl.pallas_call(kernel, in_specs=ins, out_specs=[VMEM] * len(outs), out_sh...  16.8 us
    ppermute x18, waiting for transfers between devices, swap(): lax.ppermute(value, 'station', [(s ^ stride, s) for s in range(stations)])  11.2 us
    ppermute x3, starting transfers between devices, from_below(): return lax.ppermute(value, 'station', pairs)  4.46 us
    ppermute x3, starting transfers between devices, from_above(): return lax.ppermute(value, 'station', pairs)  3.87 us
    ppermute x3, waiting for transfers between devices, from_above(): return lax.ppermute(value, 'station', pairs)  3.31 us
    unnamed x17, local copies, waits for them, and re-layouts  3.23 us
    ppermute x1, starting transfers between devices, local(): lax.ppermute(total, axes, second)  3.1 us
  transfers between devices with their start and end apart: 27, of which 9 were waited for; matrix products, arithmetic and copies ran while one was open for 0% of the time, Pallas kernels for 19%

profile of v10, /device:TPU:3, one launch (start us, length us, event | category | flops | bytes accessed | tf_op | source)
XLA Modules:
  0.0 72.1 jit_solution(13461390593098912347)
XLA Ops:
  0.7 2.0 %pack.1 = (bf16[2,192,128]{2,1,0:T(8,128)(2,1)}, bf16[2,192,128]{2,1,0:T(8,128)(2,1)}, bf16[2,192,128]{2,1,0:T(8,128)(2,1)}, bf16[2,192,128]{2,1,0:T(8,128)(2,1)}) custom-call(bf16[128,768]{1,0:T(8,128)(2,1)} %bitcast.12, bf16[128,768]{1,0:T(8,128)(2,1)} %bitcast.13), custom_call_target="tpu_custom_call" | custom-call | flops 1 | bytes 1 | tf_op jit(solution)/shard_map/pack/pallas_call | solution.py:50
  2.6 0.7 %collective-permute-start = (bf16[2,192,128]{2,1,0:T(8,128)(2,1)}, bf16[2,192,128]{2,1,0:T(8,128)(2,1)S(1)}, u32[]{:S(2)}, u32[]{:S(2)}) collective-permute-start(bf16[2,192,128]{2,1,0:T(8,128)(2,1)} %get-tuple-element.61), channel_id=1, source_target_pairs={{1,0},{0,1},{3,2},{2,3},{5,4},{4,5},{7,6},{6,7},{9,8},{8,9},{11,10... | collective-permute-start | bytes 294920 | tf_op jit(solution)/shard_map/ppermute | solution.py:343
  3.4 1.7 %collective-permute-start.2 = (bf16[2,192,128]{2,1,0:T(8,128)(2,1)}, bf16[2,192,128]{2,1,0:T(8,128)(2,1)S(1)}, u32[]{:S(2)}, u32[]{:S(2)}) collective-permute-start(bf16[2,192,128]{2,1,0:T(8,128)(2,1)} %get-tuple-element.63), channel_id=1, source_target_pairs={{3,0},{2,1},{1,2},{0,3},{7,4},{6,5},{5,6},{4,7},{11,8},{10,9},{9,1... | collective-permute-start | bytes 294920 | tf_op jit(solution)/shard_map/ppermute | solution.py:343
  5.1 1.3 %copy-done = bf16[768,768]{1,0:T(8,128)(2,1)S(1)} copy-done((bf16[768,768]{1,0:T(8,128)(2,1)S(1)}, bf16[768,768]{1,0:T(8,128)(2,1)}, u32[]{:S(2)}) %copy-start) | copy-done | bytes 1179672
  6.3 0.9 %copy-done.2 = bf16[1,1,128,768]{3,2,1,0:T(8,128)(2,1)S(1)} copy-done((bf16[1,1,128,768]{3,2,1,0:T(8,128)(2,1)S(1)}, bf16[1,1,128,768]{3,2,1,0:T(8,128)(2,1)}, u32[]{:S(2)}) %copy-start.2) | copy-done | bytes 196632
  7.3 0.9 %copy-done.3 = bf16[1,1,128,768]{3,2,1,0:T(8,128)(2,1)S(1)} copy-done((bf16[1,1,128,768]{3,2,1,0:T(8,128)(2,1)S(1)}, bf16[1,1,128,768]{3,2,1,0:T(8,128)(2,1)}, u32[]{:S(2)}) %copy-start.3) | copy-done | bytes 196632
  8.2 0.5 project.1
  8.7 1.5 %collective-permute-done.2.refs_3_ = bf16[2,192,128]{2,1,0:T(8,128)(2,1)S(1)} collective-permute-done((bf16[2,192,128]{2,1,0:T(8,128)(2,1)}, bf16[2,192,128]{2,1,0:T(8,128)(2,1)S(1)}, u32[]{:S(2)}, u32[]{:S(2)}) %collective-permute-start.2) | collective-permute-done | bytes 98336 | tf_op jit(solution)/shard_map/ppermute | solution.py:343
  10.2 0.1 gather.2
  10.5 0.7 collective-permute-start.5
  11.1 1.4 %collective-permute-start.3 = (bf16[2,192,384]{2,1,0:T(8,128)(2,1)S(1)}, bf16[2,192,384]{2,1,0:T(8,128)(2,1)S(1)}, u32[]{:S(2)}, u32[]{:S(2)}) collective-permute-start(bf16[2,192,384]{2,1,0:T(8,128)(2,1)S(1)} %get-tuple-element.70), channel_id=1, source_target_pairs={{0,4},{1,5},{2,6},{3,7},{4,8},{5,9},{6,10},{7,11},{8,12},{9,13},{1... | collective-permute-start | bytes 884744 | tf_op jit(solution)/shard_map/ppermute | solution.py:350
  12.5 2.0 %collective-permute-start.4 = (bf16[2,192,384]{2,1,0:T(8,128)(2,1)S(1)}, bf16[2,192,384]{2,1,0:T(8,128)(2,1)S(1)}, u32[]{:S(2)}, u32[]{:S(2)}) collective-permute-start(bf16[2,192,384]{2,1,0:T(8,128)(2,1)S(1)} %get-tuple-element.71), channel_id=1, source_target_pairs={{0,12},{1,13},{2,14},{3,15},{4,0},{5,1},{6,2},{7,3},{8,4},{9,5},{1... | collective-permute-start | bytes 884744 | tf_op jit(solution)/shard_map/ppermute | solution.py:354
  14.5 1.2 %collective-permute-start.6 = (bf16[2,192,128]{2,1,0:T(8,128)(2,1)S(1)}, bf16[2,192,128]{2,1,0:T(8,128)(2,1)S(1)}, u32[]{:S(2)}, u32[]{:S(2)}) collective-permute-start(bf16[2,192,128]{2,1,0:T(8,128)(2,1)S(1)} %get-tuple-element.74), channel_id=1, source_target_pairs={{2,0},{3,1},{0,2},{1,3},{6,4},{7,5},{4,6},{5,7},{10,8},{11,9},{8,1... | collective-permute-start | bytes 294920 | tf_op jit(solution)/shard_map/ppermute | solution.py:343
  15.8 0.9 %collective-permute-start.7 = (bf16[2,192,128]{2,1,0:T(8,128)(2,1)S(1)}, bf16[2,192,128]{2,1,0:T(8,128)(2,1)S(1)}, u32[]{:S(2)}, u32[]{:S(2)}) collective-permute-start(bf16[2,192,128]{2,1,0:T(8,128)(2,1)S(1)} %get-tuple-element.75), channel_id=1, source_target_pairs={{3,0},{2,1},{1,2},{0,3},{7,4},{6,5},{5,6},{4,7},{11,8},{10,9},{9,1... | collective-permute-start | bytes 294920 | tf_op jit(solution)/shard_map/ppermute | solution.py:343
  16.6 2.1 %collective-permute-done.6.refs_2_ = bf16[2,192,128]{2,1,0:T(8,128)(2,1)S(1)} collective-permute-done((bf16[2,192,128]{2,1,0:T(8,128)(2,1)S(1)}, bf16[2,192,128]{2,1,0:T(8,128)(2,1)S(1)}, u32[]{:S(2)}, u32[]{:S(2)}) %collective-permute-start.6) | collective-permute-done | bytes 98336 | tf_op jit(solution)/shard_map/ppermute | solution.py:343
  18.7 1.5 %collective-permute-start.8 = (bf16[128,768]{1,0:T(8,128)(2,1)S(1)}, bf16[128,768]{1,0:T(8,128)(2,1)S(1)}, u32[]{:S(2)}, u32[]{:S(2)}) collective-permute-start(bf16[128,768]{1,0:T(8,128)(2,1)S(1)} %bitcast.11), channel_id=1, source_target_pairs={{1,0},{0,1},{3,2},{2,3},{5,4},{4,5},{7,6},{6,7},{9,8},{8,9},{11,10... | collective-permute-start | bytes 589832 | tf_op jit(solution)/shard_map/ppermute | solution.py:343
  20.3 1.1 %live.1 = (f32[16,512]{1,0:T(8,128)S(1)}, f32[8,384]{1,0:T(8,128)S(1)}) custom-call(s32[16,6]{1,0:T(8,128)S(1)} %copy.12.ids_ref, s32[16]{0:T(128)S(1)} %copy-done.6), custom_call_target="tpu_custom_call" | custom-call | flops 1 | bytes 1 | tf_op jit(solution)/shard_map/live/pallas_call | solution.py:50
  21.5 0.1 collective-permute-done.7.refs_3_
  21.6 0.9 %gather.3 = (bf16[2,192,384]{2,1,0:T(8,128)(2,1)S(1)}, bf16[2,192,384]{2,1,0:T(8,128)(2,1)}, bf16[2,192,512]{2,1,0:T(8,128)(2,1)S(1)}) custom-call(bf16[2,192,128]{2,1,0:T(8,128)(2,1)S(1)} %get-tuple-element.72.refs_0_, bf16[2,192,128]{2,1,0:T(8,128)(2,1)S(1)} %collective-permute-done.5.refs_1_, bf16[2,192,128]{2,1,0:T(8,128)(2,1)S(1)} %collective-permute-done.6.refs_2_, ...), custom_call_target="tpu_custom_call" | custom-call | flops 1 | bytes 1 | tf_op jit(solution)/shard_map/gather/pallas_call | solution.py:50
  22.4 1.5 %collective-permute-start.13 = (bf16[2,192,384]{2,1,0:T(8,128)(2,1)S(1)}, bf16[2,192,384]{2,1,0:T(8,128)(2,1)S(1)}, u32[]{:S(2)}, u32[]{:S(2)}) collective-permute-start(bf16[2,192,384]{2,1,0:T(8,128)(2,1)S(1)} %get-tuple-element.90), channel_id=1, source_target_pairs={{0,4},{1,5},{2,6},{3,7},{4,8},{5,9},{6,10},{7,11},{8,12},{9,13},{1... | collective-permute-start | bytes 884744 | tf_op jit(solution)/shard_map/ppermute | solution.py:350
  23.9 3.3 %collective-permute-done.4.high_ref = bf16[2,192,384]{2,1,0:T(8,128)(2,1)S(1)} collective-permute-done((bf16[2,192,384]{2,1,0:T(8,128)(2,1)S(1)}, bf16[2,192,384]{2,1,0:T(8,128)(2,1)S(1)}, u32[]{:S(2)}, u32[]{:S(2)}) %collective-permute-start.4) | collective-permute-done | bytes 294944 | tf_op jit(solution)/shard_map/ppermute | solution.py:354
  27.2 3.3 %forward.1 = (bf16[192,512]{1,0:T(8,128)(2,1)S(1)}, f32[8,512]{1,0:T(8,128)S(1)}, f32[8,384]{1,0:T(8,128)S(1)}, bf16[3,1280,512]{2,1,0:T(8,128)(2,1)S(1)}, bf16[2,192,1280]{2,1,0:T(8,128)(2,1)S(1)}) custom-call(bf16[2,192,512]{2,1,0:T(8,128)(2,1)S(1)} %get-tuple-element.64.pair_ref, bf16[2,192,384]{2,1,0:T(8,128)(2,1)S(1)} %collective-permute-done.3.low_ref, ...), custom_call_target="tpu_custom_call" | custom-call | flops 1 | bytes 1 | tf_op jit(solution)/shard_map/forward/pallas_call | solution.py:50
  30.6 0.5 weight.1
  31.0 1.3 %collective-permute-start.20 = (bf16[96,768]{1,0:T(8,128)(2,1)S(1)}, bf16[96,768]{1,0:T(8,128)(2,1)S(1)}, u32[]{:S(2)}, u32[]{:S(2)}) collective-permute-start(bf16[96,768]{1,0:T(8,128)(2,1)S(1)} %get-tuple-element.84.refs_5_), channel_id=1, source_target_pairs={{0,16},{16,0},{1,17},{17,1},{2,18},{18,2},{3,19},{19,3},{4,20},{20... | collective-permute-start | bytes 442376 | tf_op jit(solution)/shard_map/ppermute | solution.py:357
  32.3 3.1 %query_grad.1 = (bf16[2,192,128]{2,1,0:T(8,128)(2,1)S(1)}, bf16[2,192,128]{2,1,0:T(8,128)(2,1)S(1)}, bf16[2,2,192,128]{3,2,1,0:T(8,128)(2,1)S(1)}, f32[2,192,512...) custom-call(bf16[2,192,1280]{2,1,0:T(8,128)(2,1)S(1)} %get-tuple-element.78.r, ...), custom_call_target="tpu_custom_call" | custom-call | flops 1 | bytes 1 | tf_op jit(solution)/shard_map/query_grad/pallas_call | solution.py:50
  35.5 1.3 %collective-permute-start.11 = (bf16[2,2,192,128]{3,2,1,0:T(8,128)(2,1)S(1)}, bf16[2,2,192,128]{3,2,1,0:T(8,128)(2,1)S(1)}, u32[]{:S(2)}, u32[]{:S(2)}) collective-permute-start(bf16[2,2,192,128]{3,2,1,0:T(8,128)(2,1)S(1)} %get-tuple-element.86), channel_id=1, source_target_pairs={{2,0},{3,1},{0,2},{1,3},{6,4},{7,5},{4,6},{5,7},{10,8},{11,9},{8,1... | collective-permute-start | bytes 589832 | tf_op jit(solution)/shard_map/ppermute | solution.py:343
  36.7 1.6 %collective-permute-start.14 = (f32[8,384]{1,0:T(8,128)S(1)}, f32[8,384]{1,0:T(8,128)S(1)}, u32[]{:S(2)}, u32[]{:S(2)}) collective-permute-start(f32[8,384]{1,0:T(8,128)S(1)} %get-tuple-element.91), channel_id=1, source_target_pairs={{0,4},{1,5},{2,6},{3,7},{4,8},{5,9},{6,10},{7,11},{8,12},{9,13},{1... | collective-permute-start | bytes 36872 | tf_op jit(solution)/shard_map/ppermute | solution.py:350
  38.3 1.7 %collective-permute-start.15 = (bf16[192,384]{1,0:T(8,128)(2,1)S(1)}, bf16[192,384]{1,0:T(8,128)(2,1)S(1)}, u32[]{:S(2)}, u32[]{:S(2)}) collective-permute-start(bf16[192,384]{1,0:T(8,128)(2,1)S(1)} %get-tuple-element.94), channel_id=1, source_target_pairs={{0,12},{1,13},{2,14},{3,15},{4,0},{5,1},{6,2},{7,3},{8,4},{9,5},{1... | collective-permute-start | bytes 442376 | tf_op jit(solution)/shard_map/ppermute | solution.py:354
  40.0 1.2 %collective-permute-done.14.stats_ref.refs_4_ = f32[8,384]{1,0:T(8,128)S(1)} collective-permute-done((f32[8,384]{1,0:T(8,128)S(1)}, f32[8,384]{1,0:T(8,128)S(1)}, u32[]{:S(2)}, u32[]{:S(2)}) %collective-permute-start.14) | collective-permute-done | bytes 12320 | tf_op jit(solution)/shard_map/ppermute | solution.py:350
  41.2 0.2 collective-permute-start.16
  41.4 1.3 %collective-permute-start.21 = (bf16[48,768]{1,0:T(8,128)(2,1)S(1)}, bf16[48,768]{1,0:T(8,128)(2,1)S(1)}, u32[]{:S(2)}, u32[]{:S(2)}) collective-permute-start(bf16[48,768]{1,0:T(8,128)(2,1)S(1)} %get-tuple-element.105), channel_id=1, source_target_pairs={{4,0},{5,1},{6,2},{7,3},{0,4},{1,5},{2,6},{3,7},{12,8},{13,9},{14,... | collective-permute-start | bytes 221192 | tf_op jit(solution)/shard_map/ppermute | solution.py:343
  42.7 3.9 %collective-permute-done.21.got_ref = bf16[48,768]{1,0:T(8,128)(2,1)S(1)} collective-permute-done((bf16[48,768]{1,0:T(8,128)(2,1)S(1)}, bf16[48,768]{1,0:T(8,128)(2,1)S(1)}, u32[]{:S(2)}, u32[]{:S(2)}) %collective-permute-start.21) | collective-permute-done | bytes 73760 | tf_op jit(solution)/shard_map/ppermute | solution.py:343
  46.7 3.7 %collective-permute-start.22 = (bf16[48,768]{1,0:T(8,128)(2,1)S(1)}, bf16[48,768]{1,0:T(8,128)(2,1)S(1)}, u32[]{:S(2)}, u32[]{:S(2)}) collective-permute-start(bf16[48,768]{1,0:T(8,128)(2,1)S(1)} %add.2.refs_0_), channel_id=1, source_target_pairs={{8,0},{9,1},{10,2},{11,3},{12,4},{13,5},{14,6},{15,7},{0,8},{1,9},... | collective-permute-start | bytes 221192 | tf_op jit(solution)/shard_map/ppermute | solution.py:343
  50.3 2.0 %key_grad.1 = (bf16[2,192,128]{2,1,0:T(8,128)(2,1)S(1)}, bf16[2,192,128]{2,1,0:T(8,128)(2,1)S(1)}, bf16[2,192,128]{2,1,0:T(8,128)(2,1)S(1)}, bf16[2,192,128]{2,1,0:T(8,128)(2,1)S(1)}, f32[8,128]{1,0:T(8,128)S(1)}) custom-call(bf16[2,192,512]{2,1,0:T(8,128)(2,1)S(1)} %get-tuple-element.64.pair_ref, ...), custom_call_target="tpu_custom_call" | custom-call | flops 1 | bytes 1 | tf_op jit(solution)/shard_map/key_grad/pallas_call | solution.py:50
  52.4 1.0 %collective-permute-start.17 = (bf16[2,192,128]{2,1,0:T(8,128)(2,1)S(1)}, bf16[2,192,128]{2,1,0:T(8,128)(2,1)S(1)}, u32[]{:S(2)}, u32[]{:S(2)}) collective-permute-start(bf16[2,192,128]{2,1,0:T(8,128)(2,1)S(1)} %get-tuple-element.97), channel_id=1, source_target_pairs={{1,0},{0,1},{3,2},{2,3},{5,4},{4,5},{7,6},{6,7},{9,8},{8,9},{11,10... | collective-permute-start | bytes 294920 | tf_op jit(solution)/shard_map/ppermute | solution.py:343
  53.4 0.3 collective-permute-start.18
  53.7 1.4 %collective-permute-start.19 = (bf16[2,192,128]{2,1,0:T(8,128)(2,1)S(1)}, bf16[2,192,128]{2,1,0:T(8,128)(2,1)S(1)}, u32[]{:S(2)}, u32[]{:S(2)}) collective-permute-start(bf16[2,192,128]{2,1,0:T(8,128)(2,1)S(1)} %get-tuple-element.99), channel_id=1, source_target_pairs={{3,0},{2,1},{1,2},{0,3},{7,4},{6,5},{5,6},{4,7},{11,8},{10,9},{9,1... | collective-permute-start | bytes 294920 | tf_op jit(solution)/shard_map/ppermute | solution.py:343
  55.1 2.3 %collective-permute-start.23 = (bf16[48,768]{1,0:T(8,128)(2,1)S(1)}, bf16[48,768]{1,0:T(8,128)(2,1)S(1)}, u32[]{:S(2)}, u32[]{:S(2)}) collective-permute-start(bf16[48,768]{1,0:T(8,128)(2,1)S(1)} %add.3.refs_0_), channel_id=1, source_target_pairs={{4,0},{5,1},{6,2},{7,3},{0,4},{1,5},{2,6},{3,7},{12,8},{13,9},{14,... | collective-permute-start | bytes 221192 | tf_op jit(solution)/shard_map/ppermute | solution.py:343
  57.4 0.5 collective-permute-start.12
  57.9 2.4 %collective-permute-done.19.refs_3_.refs_4_ = bf16[2,192,128]{2,1,0:T(8,128)(2,1)S(1)} collective-permute-done((bf16[2,192,128]{2,1,0:T(8,128)(2,1)S(1)}, bf16[2,192,128]{2,1,0:T(8,128)(2,1)S(1)}, u32[]{:S(2)}, u32[]{:S(2)}) %collective-permute-start.19) | collective-permute-done | bytes 98336 | tf_op jit(solution)/shard_map/ppermute | solution.py:343
  60.4 0.3 collective-permute-start.25
  60.6 3.1 %collective-permute-start.24 = (bf16[96,768]{1,0:T(8,128)(2,1)S(1)}, bf16[96,768]{1,0:T(8,128)(2,1)S(1)}, u32[]{:S(2)}, u32[]{:S(2)}) collective-permute-start(bf16[96,768]{1,0:T(8,128)(2,1)S(1)} %join.1.refs_0_), channel_id=1, source_target_pairs={{2,16},{3,17},{6,20},{7,21},{10,24},{11,25},{14,28},{15,29},{16,2}... | collective-permute-start | bytes 442376 | tf_op jit(solution)/shard_map/ppermute | solution.py:486
  63.8 0.9 %key_output.1 = (bf16[128,768]{1,0:T(8,128)(2,1)}, bf16[128,768]{1,0:T(8,128)(2,1)}, f32[8,128]{1,0:T(8,128)S(1)}) custom-call(bf16[2,192,128]{2,1,0:T(8,128)(2,1)S(1)} %get-tuple-element.96.refs_0_, bf16[2,192,128]{2,1,0:T(8,128)(2,1)S(1)} %collective-permute-done.17.refs_1_.refs_2_, bf16[2,192,128]{2,1,0:T(8,128)(2,1)S(1)} %collective-permute-done.18.refs_2_.refs_3_, ...), custom_call_target="tpu_custom_call" | custom-call | flops 1 | bytes 1 | tf_op jit(solution)/shard_map/key_output/pallas_call | solution.py:50
  64.6 1.1 %output.1 = (bf16[128,768]{1,0:T(8,128)(2,1)}, bf16[128,768]{1,0:T(8,128)(2,1)}, f32[8,128]{1,0:T(8,128)S(1)}) custom-call(bf16[2,192,128]{2,1,0:T(8,128)(2,1)S(1)} %get-tuple-element.85.mine_ref, bf16[2,2,192,128]{3,2,1,0:T(8,128)(2,1)S(1)} %collective-permute-done.11.across_ref.refs_2_, bf16[2,2,192,128]{3,2,1,0:T(8,128)(2,1)S(1)} %collective-permute-done.12.sib_ref, ...), custom_call_target="tpu_custom_call" | custom-call | flops 1 | bytes 1 | tf_op jit(solution)/shard_map/output/pallas_call | solution.py:50
  65.7 2.3 %collective-permute-done.24.refs_1_ = bf16[96,768]{1,0:T(8,128)(2,1)S(1)} collective-permute-done((bf16[96,768]{1,0:T(8,128)(2,1)S(1)}, bf16[96,768]{1,0:T(8,128)(2,1)S(1)}, u32[]{:S(2)}, u32[]{:S(2)}) %collective-permute-start.24) | collective-permute-done | bytes 147488 | tf_op jit(solution)/shard_map/ppermute | solution.py:486
  68.1 1.7 %collective-permute-start.26 = (bf16[192,768]{1,0:T(8,128)(2,1)S(1)}, bf16[192,768]{1,0:T(8,128)(2,1)S(1)}, u32[]{:S(2)}, u32[]{:S(2)}) collective-permute-start(bf16[192,768]{1,0:T(8,128)(2,1)S(1)} %cross.1.mine_ref), channel_id=1, source_target_pairs={{1,0},{0,1},{3,2},{2,3},{5,4},{4,5},{7,6},{6,7},{9,8},{8,9},{11,10... | collective-permute-start | bytes 884744 | tf_op jit(solution)/shard_map/ppermute | solution.py:343
  69.8 1.2 %collective-permute-done.26.got_ref = bf16[192,768]{1,0:T(8,128)(2,1)S(1)} collective-permute-done((bf16[192,768]{1,0:T(8,128)(2,1)S(1)}, bf16[192,768]{1,0:T(8,128)(2,1)S(1)}, u32[]{:S(2)}, u32[]{:S(2)}) %collective-permute-start.26) | collective-permute-done | bytes 294944 | tf_op jit(solution)/shard_map/ppermute | solution.py:343
  71.0 1.1 %last.1 = f32[384,768]{1,0:T(8,128)} custom-call(bf16[192,768]{1,0:T(8,128)(2,1)S(1)} %cross.1.mine_ref, bf16[192,768]{1,0:T(8,128)(2,1)S(1)} %collective-permute-done.26.got_ref), custom_call_target="tpu_custom_call" | custom-call | flops 1 | bytes 1 | tf_op jit(solution)/shard_map/last/pallas_call | solution.py:50
  (41 shorter events, 0.4 us)
Async XLA Ops:
  0.6 9.7 %copy-start.4 = (bf16[1,1,128,768]{3,2,1,0:T(8,128)(2,1)S(1)}, bf16[1,1,128,768]{3,2,1,0:T(8,128)(2,1)}, u32[]{:S(2)}) copy-start(bf16[1,1,128,768]{3,2,1,0:T(8,128)(2,1)} %param.10) | copy-start | bytes 589828
  0.6 19.6 %copy-start.7 = (s32[16,6]{0,1:T(8,128)S(1)}, s32[16,6]{0,1:T(8,128)}, u32[]{:S(2)}) copy-start(s32[16,6]{0,1:T(8,128)} %param.12) | copy-start | bytes 1156
  0.7 19.7 %copy-start.6 = (s32[16]{0:T(128)S(1)}, s32[16]{0:T(128)}, u32[]{:S(2)}) copy-start(s32[16]{0:T(128)} %count_ref.1) | copy-start | bytes 196
  2.6 6.1 %collective-permute-start = (bf16[2,192,128]{2,1,0:T(8,128)(2,1)}, bf16[2,192,128]{2,1,0:T(8,128)(2,1)S(1)}, u32[]{:S(2)}, u32[]{:S(2)}) collective-permute-start(bf16[2,192,128]{2,1,0:T(8,128)(2,1)} %get-tuple-element.61), channel_id=1, source_target_pairs={{1,0},{0,1},{3,2},{2,3},{5,4},{4,5},{7,6},{6,7},{9,8},{8,9},{11,10... | collective-permute-start | bytes 294920 | tf_op jit(solution)/shard_map/ppermute | solution.py:343
  3.4 5.4 %collective-permute-start.1 = (bf16[2,192,128]{2,1,0:T(8,128)(2,1)}, bf16[2,192,128]{2,1,0:T(8,128)(2,1)S(1)}, u32[]{:S(2)}, u32[]{:S(2)}) collective-permute-start(bf16[2,192,128]{2,1,0:T(8,128)(2,1)} %get-tuple-element.62), channel_id=1, source_target_pairs={{2,0},{3,1},{0,2},{1,3},{6,4},{7,5},{4,6},{5,7},{10,8},{11,9},{8,1... | collective-permute-start | bytes 294920 | tf_op jit(solution)/shard_map/ppermute | solution.py:343
  3.4 6.8 %collective-permute-start.2 = (bf16[2,192,128]{2,1,0:T(8,128)(2,1)}, bf16[2,192,128]{2,1,0:T(8,128)(2,1)S(1)}, u32[]{:S(2)}, u32[]{:S(2)}) collective-permute-start(bf16[2,192,128]{2,1,0:T(8,128)(2,1)} %get-tuple-element.63), channel_id=1, source_target_pairs={{3,0},{2,1},{1,2},{0,3},{7,4},{6,5},{5,6},{4,7},{11,8},{10,9},{9,1... | collective-permute-start | bytes 294920 | tf_op jit(solution)/shard_map/ppermute | solution.py:343
  5.1 1.3 %copy-start = (bf16[768,768]{1,0:T(8,128)(2,1)S(1)}, bf16[768,768]{1,0:T(8,128)(2,1)}, u32[]{:S(2)}) copy-start(bf16[768,768]{1,0:T(8,128)(2,1)} %weight_ref.3) | copy-start | bytes 3538948
  6.3 0.9 %copy-start.2 = (bf16[1,1,128,768]{3,2,1,0:T(8,128)(2,1)S(1)}, bf16[1,1,128,768]{3,2,1,0:T(8,128)(2,1)}, u32[]{:S(2)}) copy-start(bf16[1,1,128,768]{3,2,1,0:T(8,128)(2,1)} %param.7) | copy-start | bytes 589828
  7.3 0.9 %copy-start.3 = (bf16[1,1,128,768]{3,2,1,0:T(8,128)(2,1)S(1)}, bf16[1,1,128,768]{3,2,1,0:T(8,128)(2,1)}, u32[]{:S(2)}) copy-start(bf16[1,1,128,768]{3,2,1,0:T(8,128)(2,1)} %param.10) | copy-start | bytes 589828
  8.2 2.0 %copy-start.5 = (bf16[2,192,128]{2,1,0:T(8,128)(2,1)S(1)}, bf16[2,192,128]{2,1,0:T(8,128)(2,1)}, u32[]{:S(2)}) copy-start(bf16[2,192,128]{2,1,0:T(8,128)(2,1)} %get-tuple-element.57.refs_0_) | copy-start | bytes 294916
  10.4 9.8 %collective-permute-start.9 = (bf16[128,768]{1,0:T(8,128)(2,1)S(1)}, bf16[128,768]{1,0:T(8,128)(2,1)S(1)}, u32[]{:S(2)}, u32[]{:S(2)}) collective-permute-start(bf16[128,768]{1,0:T(8,128)(2,1)S(1)} %bitcast.10), channel_id=1, source_target_pairs={{2,0},{3,1},{0,2},{1,3},{6,4},{7,5},{4,6},{5,7},{10,8},{11,9},{8,1... | collective-permute-start | bytes 589832 | tf_op jit(solution)/shard_map/ppermute | solution.py:343
  10.5 5.3 %collective-permute-start.5 = (bf16[2,192,128]{2,1,0:T(8,128)(2,1)S(1)}, bf16[2,192,128]{2,1,0:T(8,128)(2,1)S(1)}, u32[]{:S(2)}, u32[]{:S(2)}) collective-permute-start(bf16[2,192,128]{2,1,0:T(8,128)(2,1)S(1)} %get-tuple-element.73), channel_id=1, source_target_pairs={{1,0},{0,1},{3,2},{2,3},{5,4},{4,5},{7,6},{6,7},{9,8},{8,9},{11,10... | collective-permute-start | bytes 294920 | tf_op jit(solution)/shard_map/ppermute | solution.py:343
  11.1 12.8 %collective-permute-start.3 = (bf16[2,192,384]{2,1,0:T(8,128)(2,1)S(1)}, bf16[2,192,384]{2,1,0:T(8,128)(2,1)S(1)}, u32[]{:S(2)}, u32[]{:S(2)}) collective-permute-start(bf16[2,192,384]{2,1,0:T(8,128)(2,1)S(1)} %get-tuple-element.70), channel_id=1, source_target_pairs={{0,4},{1,5},{2,6},{3,7},{4,8},{5,9},{6,10},{7,11},{8,12},{9,13},{1... | collective-permute-start | bytes 884744 | tf_op jit(solution)/shard_map/ppermute | solution.py:350
  12.5 14.7 %collective-permute-start.4 = (bf16[2,192,384]{2,1,0:T(8,128)(2,1)S(1)}, bf16[2,192,384]{2,1,0:T(8,128)(2,1)S(1)}, u32[]{:S(2)}, u32[]{:S(2)}) collective-permute-start(bf16[2,192,384]{2,1,0:T(8,128)(2,1)S(1)} %get-tuple-element.71), channel_id=1, source_target_pairs={{0,12},{1,13},{2,14},{3,15},{4,0},{5,1},{6,2},{7,3},{8,4},{9,5},{1... | collective-permute-start | bytes 884744 | tf_op jit(solution)/shard_map/ppermute | solution.py:354
  14.5 4.2 %collective-permute-start.6 = (bf16[2,192,128]{2,1,0:T(8,128)(2,1)S(1)}, bf16[2,192,128]{2,1,0:T(8,128)(2,1)S(1)}, u32[]{:S(2)}, u32[]{:S(2)}) collective-permute-start(bf16[2,192,128]{2,1,0:T(8,128)(2,1)S(1)} %get-tuple-element.74), channel_id=1, source_target_pairs={{2,0},{3,1},{0,2},{1,3},{6,4},{7,5},{4,6},{5,7},{10,8},{11,9},{8,1... | collective-permute-start | bytes 294920 | tf_op jit(solution)/shard_map/ppermute | solution.py:343
  15.8 5.8 %collective-permute-start.7 = (bf16[2,192,128]{2,1,0:T(8,128)(2,1)S(1)}, bf16[2,192,128]{2,1,0:T(8,128)(2,1)S(1)}, u32[]{:S(2)}, u32[]{:S(2)}) collective-permute-start(bf16[2,192,128]{2,1,0:T(8,128)(2,1)S(1)} %get-tuple-element.75), channel_id=1, source_target_pairs={{3,0},{2,1},{1,2},{0,3},{7,4},{6,5},{5,6},{4,7},{11,8},{10,9},{9,1... | collective-permute-start | bytes 294920 | tf_op jit(solution)/shard_map/ppermute | solution.py:343
  18.7 11.8 %collective-permute-start.8 = (bf16[128,768]{1,0:T(8,128)(2,1)S(1)}, bf16[128,768]{1,0:T(8,128)(2,1)S(1)}, u32[]{:S(2)}, u32[]{:S(2)}) collective-permute-start(bf16[128,768]{1,0:T(8,128)(2,1)S(1)} %bitcast.11), channel_id=1, source_target_pairs={{1,0},{0,1},{3,2},{2,3},{5,4},{4,5},{7,6},{6,7},{9,8},{8,9},{11,10... | collective-permute-start | bytes 589832 | tf_op jit(solution)/shard_map/ppermute | solution.py:343
  20.2 10.3 %collective-permute-start.10 = (bf16[128,768]{1,0:T(8,128)(2,1)S(1)}, bf16[128,768]{1,0:T(8,128)(2,1)S(1)}, u32[]{:S(2)}, u32[]{:S(2)}) collective-permute-start(bf16[128,768]{1,0:T(8,128)(2,1)S(1)} %collective-permute-done.9.refs_2_), channel_id=1, source_target_pairs={{1,0},{0,1},{3,2},{2,3},{5,4},{4,5},{7,6},{6,7},{9,8},{8,9},{11,10... | collective-permute-start | bytes 589832 | tf_op jit(solution)/shard_map/ppermute | solution.py:343
  22.4 18.9 %collective-permute-start.13 = (bf16[2,192,384]{2,1,0:T(8,128)(2,1)S(1)}, bf16[2,192,384]{2,1,0:T(8,128)(2,1)S(1)}, u32[]{:S(2)}, u32[]{:S(2)}) collective-permute-start(bf16[2,192,384]{2,1,0:T(8,128)(2,1)S(1)} %get-tuple-element.90), channel_id=1, source_target_pairs={{0,4},{1,5},{2,6},{3,7},{4,8},{5,9},{6,10},{7,11},{8,12},{9,13},{1... | collective-permute-start | bytes 884744 | tf_op jit(solution)/shard_map/ppermute | solution.py:350
  31.0 10.3 %collective-permute-start.20 = (bf16[96,768]{1,0:T(8,128)(2,1)S(1)}, bf16[96,768]{1,0:T(8,128)(2,1)S(1)}, u32[]{:S(2)}, u32[]{:S(2)}) collective-permute-start(bf16[96,768]{1,0:T(8,128)(2,1)S(1)} %get-tuple-element.84.refs_5_), channel_id=1, source_target_pairs={{0,16},{16,0},{1,17},{17,1},{2,18},{18,2},{3,19},{19,3},{4,20},{20... | collective-permute-start | bytes 442376 | tf_op jit(solution)/shard_map/ppermute | solution.py:357
  35.5 19.6 %collective-permute-start.11 = (bf16[2,2,192,128]{3,2,1,0:T(8,128)(2,1)S(1)}, bf16[2,2,192,128]{3,2,1,0:T(8,128)(2,1)S(1)}, u32[]{:S(2)}, u32[]{:S(2)}) collective-permute-start(bf16[2,2,192,128]{3,2,1,0:T(8,128)(2,1)S(1)} %get-tuple-element.86), channel_id=1, source_target_pairs={{2,0},{3,1},{0,2},{1,3},{6,4},{7,5},{4,6},{5,7},{10,8},{11,9},{8,1... | collective-permute-start | bytes 589832 | tf_op jit(solution)/shard_map/ppermute | solution.py:343
  36.7 4.5 %collective-permute-start.14 = (f32[8,384]{1,0:T(8,128)S(1)}, f32[8,384]{1,0:T(8,128)S(1)}, u32[]{:S(2)}, u32[]{:S(2)}) collective-permute-start(f32[8,384]{1,0:T(8,128)S(1)} %get-tuple-element.91), channel_id=1, source_target_pairs={{0,4},{1,5},{2,6},{3,7},{4,8},{5,9},{6,10},{7,11},{8,12},{9,13},{1... | collective-permute-start | bytes 36872 | tf_op jit(solution)/shard_map/ppermute | solution.py:350
  38.3 12.0 %collective-permute-start.15 = (bf16[192,384]{1,0:T(8,128)(2,1)S(1)}, bf16[192,384]{1,0:T(8,128)(2,1)S(1)}, u32[]{:S(2)}, u32[]{:S(2)}) collective-permute-start(bf16[192,384]{1,0:T(8,128)(2,1)S(1)} %get-tuple-element.94), channel_id=1, source_target_pairs={{0,12},{1,13},{2,14},{3,15},{4,0},{5,1},{6,2},{7,3},{8,4},{9,5},{1... | collective-permute-start | bytes 442376 | tf_op jit(solution)/shard_map/ppermute | solution.py:354
  41.2 9.2 %collective-permute-start.16 = (bf16[192,384]{1,0:T(8,128)(2,1)S(1)}, bf16[192,384]{1,0:T(8,128)(2,1)S(1)}, u32[]{:S(2)}, u32[]{:S(2)}) collective-permute-start(bf16[192,384]{1,0:T(8,128)(2,1)S(1)} %get-tuple-element.95), channel_id=1, source_target_pairs={{0,12},{1,13},{2,14},{3,15},{4,0},{5,1},{6,2},{7,3},{8,4},{9,5},{1... | collective-permute-start | bytes 442376 | tf_op jit(solution)/shard_map/ppermute | solution.py:354
  41.4 5.2 %collective-permute-start.21 = (bf16[48,768]{1,0:T(8,128)(2,1)S(1)}, bf16[48,768]{1,0:T(8,128)(2,1)S(1)}, u32[]{:S(2)}, u32[]{:S(2)}) collective-permute-start(bf16[48,768]{1,0:T(8,128)(2,1)S(1)} %get-tuple-element.105), channel_id=1, source_target_pairs={{4,0},{5,1},{6,2},{7,3},{0,4},{1,5},{2,6},{3,7},{12,8},{13,9},{14,... | collective-permute-start | bytes 221192 | tf_op jit(solution)/shard_map/ppermute | solution.py:343
  46.7 8.4 %collective-permute-start.22 = (bf16[48,768]{1,0:T(8,128)(2,1)S(1)}, bf16[48,768]{1,0:T(8,128)(2,1)S(1)}, u32[]{:S(2)}, u32[]{:S(2)}) collective-permute-start(bf16[48,768]{1,0:T(8,128)(2,1)S(1)} %add.2.refs_0_), channel_id=1, source_target_pairs={{8,0},{9,1},{10,2},{11,3},{12,4},{13,5},{14,6},{15,7},{0,8},{1,9},... | collective-permute-start | bytes 221192 | tf_op jit(solution)/shard_map/ppermute | solution.py:343
  52.4 12.3 %copy-start.1 = (bf16[768,768]{1,0:T(8,128)(2,1)S(1)}, bf16[768,768]{1,0:T(8,128)(2,1)}, u32[]{:S(2)}) copy-start(bf16[768,768]{1,0:T(8,128)(2,1)} %weight_ref.3) | copy-start | bytes 3538948
  52.4 5.5 %collective-permute-start.17 = (bf16[2,192,128]{2,1,0:T(8,128)(2,1)S(1)}, bf16[2,192,128]{2,1,0:T(8,128)(2,1)S(1)}, u32[]{:S(2)}, u32[]{:S(2)}) collective-permute-start(bf16[2,192,128]{2,1,0:T(8,128)(2,1)S(1)} %get-tuple-element.97), channel_id=1, source_target_pairs={{1,0},{0,1},{3,2},{2,3},{5,4},{4,5},{7,6},{6,7},{9,8},{8,9},{11,10... | collective-permute-start | bytes 294920 | tf_op jit(solution)/shard_map/ppermute | solution.py:343
  53.4 4.5 %collective-permute-start.18 = (bf16[2,192,128]{2,1,0:T(8,128)(2,1)S(1)}, bf16[2,192,128]{2,1,0:T(8,128)(2,1)S(1)}, u32[]{:S(2)}, u32[]{:S(2)}) collective-permute-start(bf16[2,192,128]{2,1,0:T(8,128)(2,1)S(1)} %get-tuple-element.98), channel_id=1, source_target_pairs={{2,0},{3,1},{0,2},{1,3},{6,4},{7,5},{4,6},{5,7},{10,8},{11,9},{8,1... | collective-permute-start | bytes 294920 | tf_op jit(solution)/shard_map/ppermute | solution.py:343
  53.7 6.7 %collective-permute-start.19 = (bf16[2,192,128]{2,1,0:T(8,128)(2,1)S(1)}, bf16[2,192,128]{2,1,0:T(8,128)(2,1)S(1)}, u32[]{:S(2)}, u32[]{:S(2)}) collective-permute-start(bf16[2,192,128]{2,1,0:T(8,128)(2,1)S(1)} %get-tuple-element.99), channel_id=1, source_target_pairs={{3,0},{2,1},{1,2},{0,3},{7,4},{6,5},{5,6},{4,7},{11,8},{10,9},{9,1... | collective-permute-start | bytes 294920 | tf_op jit(solution)/shard_map/ppermute | solution.py:343
  55.1 5.2 %collective-permute-start.23 = (bf16[48,768]{1,0:T(8,128)(2,1)S(1)}, bf16[48,768]{1,0:T(8,128)(2,1)S(1)}, u32[]{:S(2)}, u32[]{:S(2)}) collective-permute-start(bf16[48,768]{1,0:T(8,128)(2,1)S(1)} %add.3.refs_0_), channel_id=1, source_target_pairs={{4,0},{5,1},{6,2},{7,3},{0,4},{1,5},{2,6},{3,7},{12,8},{13,9},{14,... | collective-permute-start | bytes 221192 | tf_op jit(solution)/shard_map/ppermute | solution.py:343
  57.4 7.2 %collective-permute-start.12 = (bf16[2,2,192,128]{3,2,1,0:T(8,128)(2,1)S(1)}, bf16[2,2,192,128]{3,2,1,0:T(8,128)(2,1)S(1)}, u32[]{:S(2)}, u32[]{:S(2)}) collective-permute-start(bf16[2,2,192,128]{3,2,1,0:T(8,128)(2,1)S(1)} %relay.1), channel_id=1, source_target_pairs={{1,0},{0,1},{3,2},{2,3},{5,4},{4,5},{7,6},{6,7},{9,8},{8,9},{11,10... | collective-permute-start | bytes 589832 | tf_op jit(solution)/shard_map/ppermute | solution.py:343
  60.4 5.4 %collective-permute-start.25 = (bf16[96,768]{1,0:T(8,128)(2,1)S(1)}, bf16[96,768]{1,0:T(8,128)(2,1)S(1)}, u32[]{:S(2)}, u32[]{:S(2)}) collective-permute-start(bf16[96,768]{1,0:T(8,128)(2,1)S(1)} %join.1.refs_0_), channel_id=1, source_target_pairs={{0,2},{1,3},{2,18},{3,19},{4,6},{5,7},{6,22},{7,23},{8,10},{9,11},... | collective-permute-start | bytes 442376 | tf_op jit(solution)/shard_map/ppermute | solution.py:486
  60.6 7.4 %collective-permute-start.24 = (bf16[96,768]{1,0:T(8,128)(2,1)S(1)}, bf16[96,768]{1,0:T(8,128)(2,1)S(1)}, u32[]{:S(2)}, u32[]{:S(2)}) collective-permute-start(bf16[96,768]{1,0:T(8,128)(2,1)S(1)} %join.1.refs_0_), channel_id=1, source_target_pairs={{2,16},{3,17},{6,20},{7,21},{10,24},{11,25},{14,28},{15,29},{16,2}... | collective-permute-start | bytes 442376 | tf_op jit(solution)/shard_map/ppermute | solution.py:486
  68.1 3.0 %collective-permute-start.26 = (bf16[192,768]{1,0:T(8,128)(2,1)S(1)}, bf16[192,768]{1,0:T(8,128)(2,1)S(1)}, u32[]{:S(2)}, u32[]{:S(2)}) collective-permute-start(bf16[192,768]{1,0:T(8,128)(2,1)S(1)} %cross.1.mine_ref), channel_id=1, source_target_pairs={{1,0},{0,1},{3,2},{2,3},{5,4},{4,5},{7,6},{6,7},{9,8},{8,9},{11,10... | collective-permute-start | bytes 884744 | tf_op jit(solution)/shard_map/ppermute | solution.py:343

commit v11 on v10

--- a/solution.py
+++ b/solution.py
@@ -435,16 +435,18 @@
         )
         return layer_output, grad_query, output_token
 
-    mine, *parts, key_token = call(
-        key_grad_kernel, [VMEM] * 7, [part_shape] * LAYER + [TOKEN],
-        (pair, qg_low, stats_low, dead, own_grad, from_above(down_k), from_above(down_v)),
-        [pltpu.VMEM((2, rows, LAYER * span), bf16)], limit=20, name="key_grad",
-    )
-    key_parts = in_layer(parts)
-    grad_key, grad_value, key_output_token = call(
-        key_output_kernel, [VMEM] * LAYER, [flat_shape] * 2 + [TOKEN],
-        (mine, *key_parts), [pltpu.VMEM((2, width, span), bf16)], name="key_output",
-    )
+    def key_return(down_k, down_v):
+        mine, *parts, key_token = call(
+            key_grad_kernel, [VMEM] * 7, [part_shape] * LAYER + [TOKEN],
+            (pair, qg_low, stats_low, dead, own_grad, from_above(down_k), from_above(down_v)),
+            [pltpu.VMEM((2, rows, LAYER * span), bf16)], limit=20, name="key_grad",
+        )
+        key_parts = in_layer(parts)
+        grad_key, grad_value, key_output_token = call(
+            key_output_kernel, [VMEM] * LAYER, [flat_shape] * 2 + [TOKEN],
+            (mine, *key_parts), [pltpu.VMEM((2, width, span), bf16)], name="key_output",
+        )
+        return grad_key, grad_value, key_parts, key_token, key_output_token
 
     scale = 1.0 / math.sqrt(span * windows * stations)
     if windows == 2:
@@ -453,7 +455,7 @@
         send, part = call(
             functools.partial(split_kernel, LAYER), [VMEM] * 2,
             [shape_of(count, width), shape_of(count, width, dtype=f32)],
-            (part, got), name="split", after=(query_token, qg_low, stats_low),
+            (part, got), name="split", after=(query_token, qg_low),
         )
 
         across = swap(to_across, 2)
@@ -463,10 +465,12 @@
             out = [shape_of(count, width)]
             return call(round_kernel, [VMEM] * 2, out, (part, got), name="add", after=after)[0]
 
-        total = add_round(part, swap(send, LAYER), ())
+        total = add_round(part, swap(send, LAYER), (stats_low,))
+        total, down_k, down_v = lax.optimization_barrier((total, down_k, down_v))
+        grad_key, grad_value, key_parts, key_token, key_output_token = key_return(down_k, down_v)
         stride = 2 * LAYER
         while stride < stations:
-            total = add_round(total, swap(total, stride), (across, key_token))
+            total = add_round(total, swap(total, stride), (across,))
             stride *= 2
         (total,) = call(
             functools.partial(join_kernel, LAYER, None), [VMEM] * 2, [shape_of(2 * count, width)],
@@ -492,6 +496,7 @@
         )
     else:
         layer_output, grad_query, _ = first_return(swap(to_across, 2))
+        grad_key, grad_value, *_ = key_return(down_k, down_v)
         start = lax.axis_index("station") % LAYER * rows
         all_grad = jnp.zeros((LAYER * span, width), bf16)
         for peer in range(LAYER):

time: 73 us -> 76.2 us (1.044)
  waiting for transfers between devices: 18 us -> 22.3 us
  starting transfers between devices: 33.3 us -> 32.4 us
    ppermute x3, waiting for transfers between devices: 1.2 us -> 4.27 us  [from_below(): return lax.ppermute(value, 'station', pairs)]
    ppermute x3, waiting for transfers between devices: 3.31 us -> 6.27 us  [from_above(): return lax.ppermute(value, 'station', pairs)]
    ppermute x18, waiting for transfers between devices: 11.2 us -> 8.33 us  [swap(): lax.ppermute(value, 'station', [(s ^ stride, s) for s in range(stations)])]
    ppermute x18, starting transfers between devices: 20.3 us -> 22.5 us  [swap(): lax.ppermute(value, 'station', [(s ^ stride, s) for s in range(stations)])]
    ppermute x3, starting transfers between devices: 3.87 us -> 2.14 us  [from_above(): return lax.ppermute(value, 'station', pairs)]
    ppermute x3, starting transfers between devices: 4.46 us -> 2.94 us  [from_below(): return lax.ppermute(value, 'station', pairs)]
    ppermute x1, waiting for transfers between devices: 2.27 us -> 3.45 us  [local(): lax.ppermute(total, axes, second)]
    ppermute x1, starting transfers between devices: 0.29 us -> 1.32 us  [local(): lax.ppermute(total, axes, first)]
  transfers between devices with their start and end apart: 27 -> 27, of which waited for: 9 -> 11; matrix products, arithmetic and copies ran while one was open for 0% -> 0% of each run, Pallas kernels for 19% -> 18%
where the time goes in v11:
time: 76.2 us; the launch traced here: 76 us
  starting transfers between devices  32.4 us (43%)
  waiting for transfers between devices  22.3 us (29%)
  Pallas kernels  17.2 us (23%)
  local copies, waits for them, and re-layouts  3.23 us (4%)
  between operations  0.85 us (1%)
    ppermute x18, starting transfers between devices, swap(): lax.ppermute(value, 'station', [(s ^ stride, s) for s in range(stations)])  22.5 us
    pallas_call x18, Pallas kernels, call(): pl.pallas_call(kernel, in_specs=ins, out_specs=[VMEM] * len(outs), out_sh...  17.2 us
    ppermute x18, waiting for transfers between devices, swap(): lax.ppermute(value, 'station', [(s ^ stride, s) for s in range(stations)])  8.33 us
    ppermute x3, waiting for transfers between devices, from_above(): return lax.ppermute(value, 'station', pairs)  6.27 us
    ppermute x3, waiting for transfers between devices, from_below(): return lax.ppermute(value, 'station', pairs)  4.27 us
    ppermute x1, waiting for transfers between devices, local(): lax.ppermute(total, axes, second)  3.45 us
    unnamed x17, local copies, waits for them, and re-layouts  3.23 us
    ppermute x3, starting transfers between devices, from_below(): return lax.ppermute(value, 'station', pairs)  2.94 us
  transfers between devices with their start and end apart: 27, of which 11 were waited for; matrix products, arithmetic and copies ran while one was open for 0% of the time, Pallas kernels for 18%

profile of v11, /device:TPU:3, one launch (start us, length us, event | category | flops | bytes accessed | tf_op | source)
XLA Modules:
  0.0 76.0 jit_solution(16033680288396056175)
XLA Ops:
  0.7 2.0 %pack.1 = (bf16[2,192,128]{2,1,0:T(8,128)(2,1)}, bf16[2,192,128]{2,1,0:T(8,128)(2,1)}, bf16[2,192,128]{2,1,0:T(8,128)(2,1)}, bf16[2,192,128]{2,1,0:T(8,128)(2,1)}) custom-call(bf16[128,768]{1,0:T(8,128)(2,1)} %bitcast.12, bf16[128,768]{1,0:T(8,128)(2,1)} %bitcast.13), custom_call_target="tpu_custom_call" | custom-call | flops 1 | bytes 1 | tf_op jit(solution)/shard_map/pack/pallas_call | solution.py:50
  2.6 0.7 collective-permute-start
  3.4 1.7 %collective-permute-start.2 = (bf16[2,192,128]{2,1,0:T(8,128)(2,1)}, bf16[2,192,128]{2,1,0:T(8,128)(2,1)S(1)}, u32[]{:S(2)}, u32[]{:S(2)}) collective-permute-start(bf16[2,192,128]{2,1,0:T(8,128)(2,1)} %get-tuple-element.65), channel_id=1, source_target_pairs={{3,0},{2,1},{1,2},{0,3},{7,4},{6,5},{5,6},{4,7},{11,8},{10,9},{9,1... | collective-permute-start | bytes 294920 | tf_op jit(solution)/shard_map/ppermute | solution.py:343
  5.1 1.3 %copy-done = bf16[768,768]{1,0:T(8,128)(2,1)S(1)} copy-done((bf16[768,768]{1,0:T(8,128)(2,1)S(1)}, bf16[768,768]{1,0:T(8,128)(2,1)}, u32[]{:S(2)}) %copy-start) | copy-done | bytes 1179672
  6.3 0.9 %copy-done.2 = bf16[1,1,128,768]{3,2,1,0:T(8,128)(2,1)S(1)} copy-done((bf16[1,1,128,768]{3,2,1,0:T(8,128)(2,1)S(1)}, bf16[1,1,128,768]{3,2,1,0:T(8,128)(2,1)}, u32[]{:S(2)}) %copy-start.2) | copy-done | bytes 196632
  7.3 0.9 %copy-done.3 = bf16[1,1,128,768]{3,2,1,0:T(8,128)(2,1)S(1)} copy-done((bf16[1,1,128,768]{3,2,1,0:T(8,128)(2,1)S(1)}, bf16[1,1,128,768]{3,2,1,0:T(8,128)(2,1)}, u32[]{:S(2)}) %copy-start.3) | copy-done | bytes 196632
  8.2 0.5 project.1
  8.7 1.5 %collective-permute-done.2.refs_3_ = bf16[2,192,128]{2,1,0:T(8,128)(2,1)S(1)} collective-permute-done((bf16[2,192,128]{2,1,0:T(8,128)(2,1)}, bf16[2,192,128]{2,1,0:T(8,128)(2,1)S(1)}, u32[]{:S(2)}, u32[]{:S(2)}) %collective-permute-start.2) | collective-permute-done | bytes 98336 | tf_op jit(solution)/shard_map/ppermute | solution.py:343
  10.2 0.1 gather.2
  10.4 0.1 collective-permute-start.9
  10.5 0.7 collective-permute-start.5
  11.1 1.4 %collective-permute-start.3 = (bf16[2,192,384]{2,1,0:T(8,128)(2,1)S(1)}, bf16[2,192,384]{2,1,0:T(8,128)(2,1)S(1)}, u32[]{:S(2)}, u32[]{:S(2)}) collective-permute-start(bf16[2,192,384]{2,1,0:T(8,128)(2,1)S(1)} %get-tuple-element.72), channel_id=1, source_target_pairs={{0,4},{1,5},{2,6},{3,7},{4,8},{5,9},{6,10},{7,11},{8,12},{9,13},{1... | collective-permute-start | bytes 884744 | tf_op jit(solution)/shard_map/ppermute | solution.py:350
  12.5 2.0 %collective-permute-start.4 = (bf16[2,192,384]{2,1,0:T(8,128)(2,1)S(1)}, bf16[2,192,384]{2,1,0:T(8,128)(2,1)S(1)}, u32[]{:S(2)}, u32[]{:S(2)}) collective-permute-start(bf16[2,192,384]{2,1,0:T(8,128)(2,1)S(1)} %get-tuple-element.73), channel_id=1, source_target_pairs={{0,12},{1,13},{2,14},{3,15},{4,0},{5,1},{6,2},{7,3},{8,4},{9,5},{1... | collective-permute-start | bytes 884744 | tf_op jit(solution)/shard_map/ppermute | solution.py:354
  14.5 1.2 %collective-permute-start.6 = (bf16[2,192,128]{2,1,0:T(8,128)(2,1)S(1)}, bf16[2,192,128]{2,1,0:T(8,128)(2,1)S(1)}, u32[]{:S(2)}, u32[]{:S(2)}) collective-permute-start(bf16[2,192,128]{2,1,0:T(8,128)(2,1)S(1)} %get-tuple-element.76), channel_id=1, source_target_pairs={{2,0},{3,1},{0,2},{1,3},{6,4},{7,5},{4,6},{5,7},{10,8},{11,9},{8,1... | collective-permute-start | bytes 294920 | tf_op jit(solution)/shard_map/ppermute | solution.py:343
  15.8 0.9 %collective-permute-start.7 = (bf16[2,192,128]{2,1,0:T(8,128)(2,1)S(1)}, bf16[2,192,128]{2,1,0:T(8,128)(2,1)S(1)}, u32[]{:S(2)}, u32[]{:S(2)}) collective-permute-start(bf16[2,192,128]{2,1,0:T(8,128)(2,1)S(1)} %get-tuple-element.77), channel_id=1, source_target_pairs={{3,0},{2,1},{1,2},{0,3},{7,4},{6,5},{5,6},{4,7},{11,8},{10,9},{9,1... | collective-permute-start | bytes 294920 | tf_op jit(solution)/shard_map/ppermute | solution.py:343
  16.6 2.1 %collective-permute-done.6.refs_2_ = bf16[2,192,128]{2,1,0:T(8,128)(2,1)S(1)} collective-permute-done((bf16[2,192,128]{2,1,0:T(8,128)(2,1)S(1)}, bf16[2,192,128]{2,1,0:T(8,128)(2,1)S(1)}, u32[]{:S(2)}, u32[]{:S(2)}) %collective-permute-start.6) | collective-permute-done | bytes 98336 | tf_op jit(solution)/shard_map/ppermute | solution.py:343
  18.7 1.5 %collective-permute-start.8 = (bf16[128,768]{1,0:T(8,128)(2,1)S(1)}, bf16[128,768]{1,0:T(8,128)(2,1)S(1)}, u32[]{:S(2)}, u32[]{:S(2)}) collective-permute-start(bf16[128,768]{1,0:T(8,128)(2,1)S(1)} %bitcast.11), channel_id=1, source_target_pairs={{1,0},{0,1},{3,2},{2,3},{5,4},{4,5},{7,6},{6,7},{9,8},{8,9},{11,10... | collective-permute-start | bytes 589832 | tf_op jit(solution)/shard_map/ppermute | solution.py:343
  20.3 1.1 %live.1 = (f32[16,512]{1,0:T(8,128)S(1)}, f32[8,384]{1,0:T(8,128)S(1)}) custom-call(s32[16,6]{1,0:T(8,128)S(1)} %copy.12.ids_ref, s32[16]{0:T(128)S(1)} %copy-done.6), custom_call_target="tpu_custom_call" | custom-call | flops 1 | bytes 1 | tf_op jit(solution)/shard_map/live/pallas_call | solution.py:50
  21.5 0.1 collective-permute-done.7.refs_3_
  21.6 0.9 %gather.3 = (bf16[2,192,384]{2,1,0:T(8,128)(2,1)S(1)}, bf16[2,192,384]{2,1,0:T(8,128)(2,1)}, bf16[2,192,512]{2,1,0:T(8,128)(2,1)S(1)}) custom-call(bf16[2,192,128]{2,1,0:T(8,128)(2,1)S(1)} %get-tuple-element.74.refs_0_, bf16[2,192,128]{2,1,0:T(8,128)(2,1)S(1)} %collective-permute-done.5.refs_1_, bf16[2,192,128]{2,1,0:T(8,128)(2,1)S(1)} %collective-permute-done.6.refs_2_, ...), custom_call_target="tpu_custom_call" | custom-call | flops 1 | bytes 1 | tf_op jit(solution)/shard_map/gather/pallas_call | solution.py:50
  22.4 1.5 %collective-permute-start.13 = (bf16[2,192,384]{2,1,0:T(8,128)(2,1)S(1)}, bf16[2,192,384]{2,1,0:T(8,128)(2,1)S(1)}, u32[]{:S(2)}, u32[]{:S(2)}) collective-permute-start(bf16[2,192,384]{2,1,0:T(8,128)(2,1)S(1)} %get-tuple-element.92), channel_id=1, source_target_pairs={{0,4},{1,5},{2,6},{3,7},{4,8},{5,9},{6,10},{7,11},{8,12},{9,13},{1... | collective-permute-start | bytes 884744 | tf_op jit(solution)/shard_map/ppermute | solution.py:350
  23.9 3.3 %collective-permute-done.4.high_ref = bf16[2,192,384]{2,1,0:T(8,128)(2,1)S(1)} collective-permute-done((bf16[2,192,384]{2,1,0:T(8,128)(2,1)S(1)}, bf16[2,192,384]{2,1,0:T(8,128)(2,1)S(1)}, u32[]{:S(2)}, u32[]{:S(2)}) %collective-permute-start.4) | collective-permute-done | bytes 294944 | tf_op jit(solution)/shard_map/ppermute | solution.py:354
  27.2 3.3 %forward.1 = (bf16[192,512]{1,0:T(8,128)(2,1)S(1)}, f32[8,512]{1,0:T(8,128)S(1)}, f32[8,384]{1,0:T(8,128)S(1)}, bf16[3,1280,512]{2,1,0:T(8,128)(2,1)S(1)}, bf16[2,192,1280]{2,1,0:T(8,128)(2,1)S(1)}) custom-call(bf16[2,192,512]{2,1,0:T(8,128)(2,1)S(1)} %get-tuple-element.66.pair_ref, bf16[2,192,384]{2,1,0:T(8,128)(2,1)S(1)} %collective-permute-done.3.low_ref, ...), custom_call_target="tpu_custom_call" | custom-call | flops 1 | bytes 1 | tf_op jit(solution)/shard_map/forward/pallas_call | solution.py:50
  30.6 0.5 weight.1
  31.0 1.3 %collective-permute-start.15 = (bf16[96,768]{1,0:T(8,128)(2,1)S(1)}, bf16[96,768]{1,0:T(8,128)(2,1)S(1)}, u32[]{:S(2)}, u32[]{:S(2)}) collective-permute-start(bf16[96,768]{1,0:T(8,128)(2,1)S(1)} %get-tuple-element.86.refs_5_), channel_id=1, source_target_pairs={{0,16},{16,0},{1,17},{17,1},{2,18},{18,2},{3,19},{19,3},{4,20},{20... | collective-permute-start | bytes 442376 | tf_op jit(solution)/shard_map/ppermute | solution.py:357
  32.3 3.1 %query_grad.1 = (bf16[2,192,128]{2,1,0:T(8,128)(2,1)S(1)}, bf16[2,192,128]{2,1,0:T(8,128)(2,1)S(1)}, bf16[2,2,192,128]{3,2,1,0:T(8,128)(2,1)S(1)}, f32[2,192,512...) custom-call(bf16[2,192,1280]{2,1,0:T(8,128)(2,1)S(1)} %get-tuple-element.80.r, ...), custom_call_target="tpu_custom_call" | custom-call | flops 1 | bytes 1 | tf_op jit(solution)/shard_map/query_grad/pallas_call | solution.py:50
  35.5 2.1 %collective-permute-start.16 = (bf16[48,768]{1,0:T(8,128)(2,1)S(1)}, bf16[48,768]{1,0:T(8,128)(2,1)S(1)}, u32[]{:S(2)}, u32[]{:S(2)}) collective-permute-start(bf16[48,768]{1,0:T(8,128)(2,1)S(1)} %get-tuple-element.99), channel_id=1, source_target_pairs={{4,0},{5,1},{6,2},{7,3},{0,4},{1,5},{2,6},{3,7},{12,8},{13,9},{14,... | collective-permute-start | bytes 221192 | tf_op jit(solution)/shard_map/ppermute | solution.py:343
  37.7 1.2 %collective-permute-start.11 = (bf16[2,2,192,128]{3,2,1,0:T(8,128)(2,1)S(1)}, bf16[2,2,192,128]{3,2,1,0:T(8,128)(2,1)S(1)}, u32[]{:S(2)}, u32[]{:S(2)}) collective-permute-start(bf16[2,2,192,128]{3,2,1,0:T(8,128)(2,1)S(1)} %get-tuple-element.88), channel_id=1, source_target_pairs={{2,0},{3,1},{0,2},{1,3},{6,4},{7,5},{4,6},{5,7},{10,8},{11,9},{8,1... | collective-permute-start | bytes 589832 | tf_op jit(solution)/shard_map/ppermute | solution.py:343
  38.9 4.3 %collective-permute-done.14.refs_2_.stats_ref = f32[8,384]{1,0:T(8,128)S(1)} collective-permute-done((f32[8,384]{1,0:T(8,128)S(1)}, f32[8,384]{1,0:T(8,128)S(1)}, u32[]{:S(2)}, u32[]{:S(2)}) %collective-permute-start.14) | collective-permute-done | bytes 12320 | tf_op jit(solution)/shard_map/ppermute | solution.py:350
  43.4 2.6 %collective-permute-start.22 = (bf16[48,768]{1,0:T(8,128)(2,1)S(1)}, bf16[48,768]{1,0:T(8,128)(2,1)S(1)}, u32[]{:S(2)}, u32[]{:S(2)}) collective-permute-start(bf16[48,768]{1,0:T(8,128)(2,1)S(1)} %add.2.refs_0_), channel_id=1, source_target_pairs={{8,0},{9,1},{10,2},{11,3},{12,4},{13,5},{14,6},{15,7},{0,8},{1,9},... | collective-permute-start | bytes 221192 | tf_op jit(solution)/shard_map/ppermute | solution.py:343
  45.9 1.4 %collective-permute-done.17.above_k = bf16[192,384]{1,0:T(8,128)(2,1)S(1)} collective-permute-done((bf16[192,384]{1,0:T(8,128)(2,1)S(1)}, bf16[192,384]{1,0:T(8,128)(2,1)S(1)}, u32[]{:S(2)}, u32[]{:S(2)}) %collective-permute-start.17) | collective-permute-done | bytes 147488 | tf_op jit(solution)/shard_map/ppermute | solution.py:354
  47.3 1.6 %collective-permute-done.18.above_v = bf16[192,384]{1,0:T(8,128)(2,1)S(1)} collective-permute-done((bf16[192,384]{1,0:T(8,128)(2,1)S(1)}, bf16[192,384]{1,0:T(8,128)(2,1)S(1)}, u32[]{:S(2)}, u32[]{:S(2)}) %collective-permute-start.18) | collective-permute-done | bytes 147488 | tf_op jit(solution)/shard_map/ppermute | solution.py:354
  48.9 2.5 %key_grad.1 = (bf16[2,192,128]{2,1,0:T(8,128)(2,1)S(1)}, bf16[2,192,128]{2,1,0:T(8,128)(2,1)S(1)}, bf16[2,192,128]{2,1,0:T(8,128)(2,1)S(1)}, bf16[2,192,128]{2,1,0:T(8,128)(2,1)S(1)}, f32[8,128]{1,0:T(8,128)}) custom-call(bf16[2,192,512]{2,1,0:T(8,128)(2,1)S(1)} %get-tuple-element.66.pair_ref, ...), custom_call_target="tpu_custom_call" | custom-call | flops 1 | bytes 1 | tf_op jit(solution)/shard_map/key_grad/pallas_call | solution.py:50
  51.4 5.2 %collective-permute-start.19 = (bf16[2,192,128]{2,1,0:T(8,128)(2,1)S(1)}, bf16[2,192,128]{2,1,0:T(8,128)(2,1)S(1)}, u32[]{:S(2)}, u32[]{:S(2)}) collective-permute-start(bf16[2,192,128]{2,1,0:T(8,128)(2,1)S(1)} %get-tuple-element.105), channel_id=1, source_target_pairs={{1,0},{0,1},{3,2},{2,3},{5,4},{4,5},{7,6},{6,7},{9,8},{8,9},{11,10... | collective-permute-start | bytes 294920 | tf_op jit(solution)/shard_map/ppermute | solution.py:343
  56.5 0.3 collective-permute-start.20
  56.9 1.3 %collective-permute-start.21 = (bf16[2,192,128]{2,1,0:T(8,128)(2,1)S(1)}, bf16[2,192,128]{2,1,0:T(8,128)(2,1)S(1)}, u32[]{:S(2)}, u32[]{:S(2)}) collective-permute-start(bf16[2,192,128]{2,1,0:T(8,128)(2,1)S(1)} %get-tuple-element.107), channel_id=1, source_target_pairs={{3,0},{2,1},{1,2},{0,3},{7,4},{6,5},{5,6},{4,7},{11,8},{10,9},{9,1... | collective-permute-start | bytes 294920 | tf_op jit(solution)/shard_map/ppermute | solution.py:343
  58.2 1.0 %collective-permute-start.23 = (bf16[48,768]{1,0:T(8,128)(2,1)S(1)}, bf16[48,768]{1,0:T(8,128)(2,1)S(1)}, u32[]{:S(2)}, u32[]{:S(2)}) collective-permute-start(bf16[48,768]{1,0:T(8,128)(2,1)S(1)} %add.3.refs_0_), channel_id=1, source_target_pairs={{4,0},{5,1},{6,2},{7,3},{0,4},{1,5},{2,6},{3,7},{12,8},{13,9},{14,... | collective-permute-start | bytes 221192 | tf_op jit(solution)/shard_map/ppermute | solution.py:343
  59.2 0.6 collective-permute-start.12
  59.8 2.2 %collective-permute-done.23.refs_1_ = bf16[48,768]{1,0:T(8,128)(2,1)S(1)} collective-permute-done((bf16[48,768]{1,0:T(8,128)(2,1)S(1)}, bf16[48,768]{1,0:T(8,128)(2,1)S(1)}, u32[]{:S(2)}, u32[]{:S(2)}) %collective-permute-start.23) | collective-permute-done | bytes 73760 | tf_op jit(solution)/shard_map/ppermute | solution.py:343
  61.9 1.2 %collective-permute-done.21.refs_3_.refs_4_ = bf16[2,192,128]{2,1,0:T(8,128)(2,1)S(1)} collective-permute-done((bf16[2,192,128]{2,1,0:T(8,128)(2,1)S(1)}, bf16[2,192,128]{2,1,0:T(8,128)(2,1)S(1)}, u32[]{:S(2)}, u32[]{:S(2)}) %collective-permute-start.21) | collective-permute-done | bytes 98336 | tf_op jit(solution)/shard_map/ppermute | solution.py:343
  63.2 1.3 %collective-permute-start.25 = (bf16[96,768]{1,0:T(8,128)(2,1)S(1)}, bf16[96,768]{1,0:T(8,128)(2,1)S(1)}, u32[]{:S(2)}, u32[]{:S(2)}) collective-permute-start(bf16[96,768]{1,0:T(8,128)(2,1)S(1)} %join.1.refs_0_), channel_id=1, source_target_pairs={{0,2},{1,3},{2,18},{3,19},{4,6},{5,7},{6,22},{7,23},{8,10},{9,11},... | collective-permute-start | bytes 442376 | tf_op jit(solution)/shard_map/ppermute | solution.py:490
  64.5 2.1 %collective-permute-start.24 = (bf16[96,768]{1,0:T(8,128)(2,1)S(1)}, bf16[96,768]{1,0:T(8,128)(2,1)S(1)}, u32[]{:S(2)}, u32[]{:S(2)}) collective-permute-start(bf16[96,768]{1,0:T(8,128)(2,1)S(1)} %join.1.refs_0_), channel_id=1, source_target_pairs={{2,16},{3,17},{6,20},{7,21},{10,24},{11,25},{14,28},{15,29},{16,2}... | collective-permute-start | bytes 442376 | tf_op jit(solution)/shard_map/ppermute | solution.py:490
  66.7 1.1 %output.1 = (bf16[128,768]{1,0:T(8,128)(2,1)}, bf16[128,768]{1,0:T(8,128)(2,1)}, f32[8,128]{1,0:T(8,128)S(1)}) custom-call(bf16[2,192,128]{2,1,0:T(8,128)(2,1)S(1)} %get-tuple-element.87.mine_ref, bf16[2,2,192,128]{3,2,1,0:T(8,128)(2,1)S(1)} %collective-permute-done.11.across_ref.refs_2_, bf16[2,2,192,128]{3,2,1,0:T(8,128)(2,1)S(1)} %collective-permute-done.12.sib_ref, ...), custom_call_target="tpu_custom_call" | custom-call | flops 1 | bytes 1 | tf_op jit(solution)/shard_map/output/pallas_call | solution.py:50
  67.8 0.9 %key_output.1 = (bf16[128,768]{1,0:T(8,128)(2,1)}, bf16[128,768]{1,0:T(8,128)(2,1)}, f32[8,128]{1,0:T(8,128)S(1)}) custom-call(bf16[2,192,128]{2,1,0:T(8,128)(2,1)S(1)} %get-tuple-element.104.refs_0_, bf16[2,192,128]{2,1,0:T(8,128)(2,1)S(1)} %collective-permute-done.19.refs_1_.refs_2_, bf16[2,192,128]{2,1,0:T(8,128)(2,1)S(1)} %collective-permute-done.20.refs_2_.refs_3_, ...), custom_call_target="tpu_custom_call" | custom-call | flops 1 | bytes 1 | tf_op jit(solution)/shard_map/key_output/pallas_call | solution.py:50
  68.7 3.5 %collective-permute-done.24.refs_1_ = bf16[96,768]{1,0:T(8,128)(2,1)S(1)} collective-permute-done((bf16[96,768]{1,0:T(8,128)(2,1)S(1)}, bf16[96,768]{1,0:T(8,128)(2,1)S(1)}, u32[]{:S(2)}, u32[]{:S(2)}) %collective-permute-start.24) | collective-permute-done | bytes 147488 | tf_op jit(solution)/shard_map/ppermute | solution.py:490
  72.2 1.5 %collective-permute-start.26 = (bf16[192,768]{1,0:T(8,128)(2,1)S(1)}, bf16[192,768]{1,0:T(8,128)(2,1)S(1)}, u32[]{:S(2)}, u32[]{:S(2)}) collective-permute-start(bf16[192,768]{1,0:T(8,128)(2,1)S(1)} %cross.1.mine_ref), channel_id=1, source_target_pairs={{1,0},{0,1},{3,2},{2,3},{5,4},{4,5},{7,6},{6,7},{9,8},{8,9},{11,10... | collective-permute-start | bytes 884744 | tf_op jit(solution)/shard_map/ppermute | solution.py:343
  73.7 1.2 %collective-permute-done.26.got_ref = bf16[192,768]{1,0:T(8,128)(2,1)S(1)} collective-permute-done((bf16[192,768]{1,0:T(8,128)(2,1)S(1)}, bf16[192,768]{1,0:T(8,128)(2,1)S(1)}, u32[]{:S(2)}, u32[]{:S(2)}) %collective-permute-start.26) | collective-permute-done | bytes 294944 | tf_op jit(solution)/shard_map/ppermute | solution.py:343
  74.9 1.1 %last.1 = f32[384,768]{1,0:T(8,128)} custom-call(bf16[192,768]{1,0:T(8,128)(2,1)S(1)} %cross.1.mine_ref, bf16[192,768]{1,0:T(8,128)(2,1)S(1)} %collective-permute-done.26.got_ref), custom_call_target="tpu_custom_call" | custom-call | flops 1 | bytes 1 | tf_op jit(solution)/shard_map/last/pallas_call | solution.py:50
  (41 shorter events, 0.5 us)
Async XLA Ops:
  0.6 9.7 %copy-start.4 = (bf16[1,1,128,768]{3,2,1,0:T(8,128)(2,1)S(1)}, bf16[1,1,128,768]{3,2,1,0:T(8,128)(2,1)}, u32[]{:S(2)}) copy-start(bf16[1,1,128,768]{3,2,1,0:T(8,128)(2,1)} %param.10) | copy-start | bytes 589828
  0.6 19.6 %copy-start.7 = (s32[16,6]{0,1:T(8,128)S(1)}, s32[16,6]{0,1:T(8,128)}, u32[]{:S(2)}) copy-start(s32[16,6]{0,1:T(8,128)} %param.12) | copy-start | bytes 1156
  0.7 19.7 %copy-start.6 = (s32[16]{0:T(128)S(1)}, s32[16]{0:T(128)}, u32[]{:S(2)}) copy-start(s32[16]{0:T(128)} %count_ref.1) | copy-start | bytes 196
  2.6 6.1 %collective-permute-start = (bf16[2,192,128]{2,1,0:T(8,128)(2,1)}, bf16[2,192,128]{2,1,0:T(8,128)(2,1)S(1)}, u32[]{:S(2)}, u32[]{:S(2)}) collective-permute-start(bf16[2,192,128]{2,1,0:T(8,128)(2,1)} %get-tuple-element.63), channel_id=1, source_target_pairs={{1,0},{0,1},{3,2},{2,3},{5,4},{4,5},{7,6},{6,7},{9,8},{8,9},{11,10... | collective-permute-start | bytes 294920 | tf_op jit(solution)/shard_map/ppermute | solution.py:343
  3.4 5.4 %collective-permute-start.1 = (bf16[2,192,128]{2,1,0:T(8,128)(2,1)}, bf16[2,192,128]{2,1,0:T(8,128)(2,1)S(1)}, u32[]{:S(2)}, u32[]{:S(2)}) collective-permute-start(bf16[2,192,128]{2,1,0:T(8,128)(2,1)} %get-tuple-element.64), channel_id=1, source_target_pairs={{2,0},{3,1},{0,2},{1,3},{6,4},{7,5},{4,6},{5,7},{10,8},{11,9},{8,1... | collective-permute-start | bytes 294920 | tf_op jit(solution)/shard_map/ppermute | solution.py:343
  3.4 6.8 %collective-permute-start.2 = (bf16[2,192,128]{2,1,0:T(8,128)(2,1)}, bf16[2,192,128]{2,1,0:T(8,128)(2,1)S(1)}, u32[]{:S(2)}, u32[]{:S(2)}) collective-permute-start(bf16[2,192,128]{2,1,0:T(8,128)(2,1)} %get-tuple-element.65), channel_id=1, source_target_pairs={{3,0},{2,1},{1,2},{0,3},{7,4},{6,5},{5,6},{4,7},{11,8},{10,9},{9,1... | collective-permute-start | bytes 294920 | tf_op jit(solution)/shard_map/ppermute | solution.py:343
  5.1 1.3 %copy-start = (bf16[768,768]{1,0:T(8,128)(2,1)S(1)}, bf16[768,768]{1,0:T(8,128)(2,1)}, u32[]{:S(2)}) copy-start(bf16[768,768]{1,0:T(8,128)(2,1)} %weight_ref.3) | copy-start | bytes 3538948
  6.3 0.9 %copy-start.2 = (bf16[1,1,128,768]{3,2,1,0:T(8,128)(2,1)S(1)}, bf16[1,1,128,768]{3,2,1,0:T(8,128)(2,1)}, u32[]{:S(2)}) copy-start(bf16[1,1,128,768]{3,2,1,0:T(8,128)(2,1)} %param.7) | copy-start | bytes 589828
  7.3 0.9 %copy-start.3 = (bf16[1,1,128,768]{3,2,1,0:T(8,128)(2,1)S(1)}, bf16[1,1,128,768]{3,2,1,0:T(8,128)(2,1)}, u32[]{:S(2)}) copy-start(bf16[1,1,128,768]{3,2,1,0:T(8,128)(2,1)} %param.10) | copy-start | bytes 589828
  8.2 2.0 %copy-start.5 = (bf16[2,192,128]{2,1,0:T(8,128)(2,1)S(1)}, bf16[2,192,128]{2,1,0:T(8,128)(2,1)}, u32[]{:S(2)}) copy-start(bf16[2,192,128]{2,1,0:T(8,128)(2,1)} %get-tuple-element.59.refs_0_) | copy-start | bytes 294916
  10.4 9.8 %collective-permute-start.9 = (bf16[128,768]{1,0:T(8,128)(2,1)S(1)}, bf16[128,768]{1,0:T(8,128)(2,1)S(1)}, u32[]{:S(2)}, u32[]{:S(2)}) collective-permute-start(bf16[128,768]{1,0:T(8,128)(2,1)S(1)} %bitcast.10), channel_id=1, source_target_pairs={{2,0},{3,1},{0,2},{1,3},{6,4},{7,5},{4,6},{5,7},{10,8},{11,9},{8,1... | collective-permute-start | bytes 589832 | tf_op jit(solution)/shard_map/ppermute | solution.py:343
  10.5 5.3 %collective-permute-start.5 = (bf16[2,192,128]{2,1,0:T(8,128)(2,1)S(1)}, bf16[2,192,128]{2,1,0:T(8,128)(2,1)S(1)}, u32[]{:S(2)}, u32[]{:S(2)}) collective-permute-start(bf16[2,192,128]{2,1,0:T(8,128)(2,1)S(1)} %get-tuple-element.75), channel_id=1, source_target_pairs={{1,0},{0,1},{3,2},{2,3},{5,4},{4,5},{7,6},{6,7},{9,8},{8,9},{11,10... | collective-permute-start | bytes 294920 | tf_op jit(solution)/shard_map/ppermute | solution.py:343
  11.1 12.8 %collective-permute-start.3 = (bf16[2,192,384]{2,1,0:T(8,128)(2,1)S(1)}, bf16[2,192,384]{2,1,0:T(8,128)(2,1)S(1)}, u32[]{:S(2)}, u32[]{:S(2)}) collective-permute-start(bf16[2,192,384]{2,1,0:T(8,128)(2,1)S(1)} %get-tuple-element.72), channel_id=1, source_target_pairs={{0,4},{1,5},{2,6},{3,7},{4,8},{5,9},{6,10},{7,11},{8,12},{9,13},{1... | collective-permute-start | bytes 884744 | tf_op jit(solution)/shard_map/ppermute | solution.py:350
  12.5 14.7 %collective-permute-start.4 = (bf16[2,192,384]{2,1,0:T(8,128)(2,1)S(1)}, bf16[2,192,384]{2,1,0:T(8,128)(2,1)S(1)}, u32[]{:S(2)}, u32[]{:S(2)}) collective-permute-start(bf16[2,192,384]{2,1,0:T(8,128)(2,1)S(1)} %get-tuple-element.73), channel_id=1, source_target_pairs={{0,12},{1,13},{2,14},{3,15},{4,0},{5,1},{6,2},{7,3},{8,4},{9,5},{1... | collective-permute-start | bytes 884744 | tf_op jit(solution)/shard_map/ppermute | solution.py:354
  14.5 4.2 %collective-permute-start.6 = (bf16[2,192,128]{2,1,0:T(8,128)(2,1)S(1)}, bf16[2,192,128]{2,1,0:T(8,128)(2,1)S(1)}, u32[]{:S(2)}, u32[]{:S(2)}) collective-permute-start(bf16[2,192,128]{2,1,0:T(8,128)(2,1)S(1)} %get-tuple-element.76), channel_id=1, source_target_pairs={{2,0},{3,1},{0,2},{1,3},{6,4},{7,5},{4,6},{5,7},{10,8},{11,9},{8,1... | collective-permute-start | bytes 294920 | tf_op jit(solution)/shard_map/ppermute | solution.py:343
  15.8 5.8 %collective-permute-start.7 = (bf16[2,192,128]{2,1,0:T(8,128)(2,1)S(1)}, bf16[2,192,128]{2,1,0:T(8,128)(2,1)S(1)}, u32[]{:S(2)}, u32[]{:S(2)}) collective-permute-start(bf16[2,192,128]{2,1,0:T(8,128)(2,1)S(1)} %get-tuple-element.77), channel_id=1, source_target_pairs={{3,0},{2,1},{1,2},{0,3},{7,4},{6,5},{5,6},{4,7},{11,8},{10,9},{9,1... | collective-permute-start | bytes 294920 | tf_op jit(solution)/shard_map/ppermute | solution.py:343
  18.7 11.8 %collective-permute-start.8 = (bf16[128,768]{1,0:T(8,128)(2,1)S(1)}, bf16[128,768]{1,0:T(8,128)(2,1)S(1)}, u32[]{:S(2)}, u32[]{:S(2)}) collective-permute-start(bf16[128,768]{1,0:T(8,128)(2,1)S(1)} %bitcast.11), channel_id=1, source_target_pairs={{1,0},{0,1},{3,2},{2,3},{5,4},{4,5},{7,6},{6,7},{9,8},{8,9},{11,10... | collective-permute-start | bytes 589832 | tf_op jit(solution)/shard_map/ppermute | solution.py:343
  20.2 10.3 %collective-permute-start.10 = (bf16[128,768]{1,0:T(8,128)(2,1)S(1)}, bf16[128,768]{1,0:T(8,128)(2,1)S(1)}, u32[]{:S(2)}, u32[]{:S(2)}) collective-permute-start(bf16[128,768]{1,0:T(8,128)(2,1)S(1)} %collective-permute-done.9.refs_2_), channel_id=1, source_target_pairs={{1,0},{0,1},{3,2},{2,3},{5,4},{4,5},{7,6},{6,7},{9,8},{8,9},{11,10... | collective-permute-start | bytes 589832 | tf_op jit(solution)/shard_map/ppermute | solution.py:343
  22.4 13.0 %collective-permute-start.13 = (bf16[2,192,384]{2,1,0:T(8,128)(2,1)S(1)}, bf16[2,192,384]{2,1,0:T(8,128)(2,1)S(1)}, u32[]{:S(2)}, u32[]{:S(2)}) collective-permute-start(bf16[2,192,384]{2,1,0:T(8,128)(2,1)S(1)} %get-tuple-element.92), channel_id=1, source_target_pairs={{0,4},{1,5},{2,6},{3,7},{4,8},{5,9},{6,10},{7,11},{8,12},{9,13},{1... | collective-permute-start | bytes 884744 | tf_op jit(solution)/shard_map/ppermute | solution.py:350
  31.0 4.4 %collective-permute-start.15 = (bf16[96,768]{1,0:T(8,128)(2,1)S(1)}, bf16[96,768]{1,0:T(8,128)(2,1)S(1)}, u32[]{:S(2)}, u32[]{:S(2)}) collective-permute-start(bf16[96,768]{1,0:T(8,128)(2,1)S(1)} %get-tuple-element.86.refs_5_), channel_id=1, source_target_pairs={{0,16},{16,0},{1,17},{17,1},{2,18},{18,2},{3,19},{19,3},{4,20},{20... | collective-permute-start | bytes 442376 | tf_op jit(solution)/shard_map/ppermute | solution.py:357
  35.5 7.7 %collective-permute-start.16 = (bf16[48,768]{1,0:T(8,128)(2,1)S(1)}, bf16[48,768]{1,0:T(8,128)(2,1)S(1)}, u32[]{:S(2)}, u32[]{:S(2)}) collective-permute-start(bf16[48,768]{1,0:T(8,128)(2,1)S(1)} %get-tuple-element.99), channel_id=1, source_target_pairs={{4,0},{5,1},{6,2},{7,3},{0,4},{1,5},{2,6},{3,7},{12,8},{13,9},{14,... | collective-permute-start | bytes 221192 | tf_op jit(solution)/shard_map/ppermute | solution.py:343
  37.7 20.5 %collective-permute-start.11 = (bf16[2,2,192,128]{3,2,1,0:T(8,128)(2,1)S(1)}, bf16[2,2,192,128]{3,2,1,0:T(8,128)(2,1)S(1)}, u32[]{:S(2)}, u32[]{:S(2)}) collective-permute-start(bf16[2,2,192,128]{3,2,1,0:T(8,128)(2,1)S(1)} %get-tuple-element.88), channel_id=1, source_target_pairs={{2,0},{3,1},{0,2},{1,3},{6,4},{7,5},{4,6},{5,7},{10,8},{11,9},{8,1... | collective-permute-start | bytes 589832 | tf_op jit(solution)/shard_map/ppermute | solution.py:343
  38.9 4.3 %collective-permute-start.14 = (f32[8,384]{1,0:T(8,128)S(1)}, f32[8,384]{1,0:T(8,128)S(1)}, u32[]{:S(2)}, u32[]{:S(2)}) collective-permute-start(f32[8,384]{1,0:T(8,128)S(1)} %get-tuple-element.93), channel_id=1, source_target_pairs={{0,4},{1,5},{2,6},{3,7},{4,8},{5,9},{6,10},{7,11},{8,12},{9,13},{1... | collective-permute-start | bytes 36872 | tf_op jit(solution)/shard_map/ppermute | solution.py:350
  43.2 4.1 %collective-permute-start.17 = (bf16[192,384]{1,0:T(8,128)(2,1)S(1)}, bf16[192,384]{1,0:T(8,128)(2,1)S(1)}, u32[]{:S(2)}, u32[]{:S(2)}) collective-permute-start(bf16[192,384]{1,0:T(8,128)(2,1)S(1)} %get-tuple-element.102), channel_id=1, source_target_pairs={{0,12},{1,13},{2,14},{3,15},{4,0},{5,1},{6,2},{7,3},{8,4},{9,5},{1... | collective-permute-start | bytes 442376 | tf_op jit(solution)/shard_map/ppermute | solution.py:354
  43.3 5.6 %collective-permute-start.18 = (bf16[192,384]{1,0:T(8,128)(2,1)S(1)}, bf16[192,384]{1,0:T(8,128)(2,1)S(1)}, u32[]{:S(2)}, u32[]{:S(2)}) collective-permute-start(bf16[192,384]{1,0:T(8,128)(2,1)S(1)} %get-tuple-element.103), channel_id=1, source_target_pairs={{0,12},{1,13},{2,14},{3,15},{4,0},{5,1},{6,2},{7,3},{8,4},{9,5},{1... | collective-permute-start | bytes 442376 | tf_op jit(solution)/shard_map/ppermute | solution.py:354
  43.4 14.8 %collective-permute-start.22 = (bf16[48,768]{1,0:T(8,128)(2,1)S(1)}, bf16[48,768]{1,0:T(8,128)(2,1)S(1)}, u32[]{:S(2)}, u32[]{:S(2)}) collective-permute-start(bf16[48,768]{1,0:T(8,128)(2,1)S(1)} %add.2.refs_0_), channel_id=1, source_target_pairs={{8,0},{9,1},{10,2},{11,3},{12,4},{13,5},{14,6},{15,7},{0,8},{1,9},... | collective-permute-start | bytes 221192 | tf_op jit(solution)/shard_map/ppermute | solution.py:343
  51.4 15.3 %copy-start.1 = (bf16[768,768]{1,0:T(8,128)(2,1)S(1)}, bf16[768,768]{1,0:T(8,128)(2,1)}, u32[]{:S(2)}) copy-start(bf16[768,768]{1,0:T(8,128)(2,1)} %weight_ref.3) | copy-start | bytes 3538948
  51.4 10.5 %collective-permute-start.19 = (bf16[2,192,128]{2,1,0:T(8,128)(2,1)S(1)}, bf16[2,192,128]{2,1,0:T(8,128)(2,1)S(1)}, u32[]{:S(2)}, u32[]{:S(2)}) collective-permute-start(bf16[2,192,128]{2,1,0:T(8,128)(2,1)S(1)} %get-tuple-element.105), channel_id=1, source_target_pairs={{1,0},{0,1},{3,2},{2,3},{5,4},{4,5},{7,6},{6,7},{9,8},{8,9},{11,10... | collective-permute-start | bytes 294920 | tf_op jit(solution)/shard_map/ppermute | solution.py:343
  56.5 5.4 %collective-permute-start.20 = (bf16[2,192,128]{2,1,0:T(8,128)(2,1)S(1)}, bf16[2,192,128]{2,1,0:T(8,128)(2,1)S(1)}, u32[]{:S(2)}, u32[]{:S(2)}) collective-permute-start(bf16[2,192,128]{2,1,0:T(8,128)(2,1)S(1)} %get-tuple-element.106), channel_id=1, source_target_pairs={{2,0},{3,1},{0,2},{1,3},{6,4},{7,5},{4,6},{5,7},{10,8},{11,9},{8,1... | collective-permute-start | bytes 294920 | tf_op jit(solution)/shard_map/ppermute | solution.py:343
  56.9 6.3 %collective-permute-start.21 = (bf16[2,192,128]{2,1,0:T(8,128)(2,1)S(1)}, bf16[2,192,128]{2,1,0:T(8,128)(2,1)S(1)}, u32[]{:S(2)}, u32[]{:S(2)}) collective-permute-start(bf16[2,192,128]{2,1,0:T(8,128)(2,1)S(1)} %get-tuple-element.107), channel_id=1, source_target_pairs={{3,0},{2,1},{1,2},{0,3},{7,4},{6,5},{5,6},{4,7},{11,8},{10,9},{9,1... | collective-permute-start | bytes 294920 | tf_op jit(solution)/shard_map/ppermute | solution.py:343
  58.2 3.7 %collective-permute-start.23 = (bf16[48,768]{1,0:T(8,128)(2,1)S(1)}, bf16[48,768]{1,0:T(8,128)(2,1)S(1)}, u32[]{:S(2)}, u32[]{:S(2)}) collective-permute-start(bf16[48,768]{1,0:T(8,128)(2,1)S(1)} %add.3.refs_0_), channel_id=1, source_target_pairs={{4,0},{5,1},{6,2},{7,3},{0,4},{1,5},{2,6},{3,7},{12,8},{13,9},{14,... | collective-permute-start | bytes 221192 | tf_op jit(solution)/shard_map/ppermute | solution.py:343
  59.2 7.5 %collective-permute-start.12 = (bf16[2,2,192,128]{3,2,1,0:T(8,128)(2,1)S(1)}, bf16[2,2,192,128]{3,2,1,0:T(8,128)(2,1)S(1)}, u32[]{:S(2)}, u32[]{:S(2)}) collective-permute-start(bf16[2,2,192,128]{3,2,1,0:T(8,128)(2,1)S(1)} %relay.1), channel_id=1, source_target_pairs={{1,0},{0,1},{3,2},{2,3},{5,4},{4,5},{7,6},{6,7},{9,8},{8,9},{11,10... | collective-permute-start | bytes 589832 | tf_op jit(solution)/shard_map/ppermute | solution.py:343
  63.2 5.5 %collective-permute-start.25 = (bf16[96,768]{1,0:T(8,128)(2,1)S(1)}, bf16[96,768]{1,0:T(8,128)(2,1)S(1)}, u32[]{:S(2)}, u32[]{:S(2)}) collective-permute-start(bf16[96,768]{1,0:T(8,128)(2,1)S(1)} %join.1.refs_0_), channel_id=1, source_target_pairs={{0,2},{1,3},{2,18},{3,19},{4,6},{5,7},{6,22},{7,23},{8,10},{9,11},... | collective-permute-start | bytes 442376 | tf_op jit(solution)/shard_map/ppermute | solution.py:490
  64.5 7.6 %collective-permute-start.24 = (bf16[96,768]{1,0:T(8,128)(2,1)S(1)}, bf16[96,768]{1,0:T(8,128)(2,1)S(1)}, u32[]{:S(2)}, u32[]{:S(2)}) collective-permute-start(bf16[96,768]{1,0:T(8,128)(2,1)S(1)} %join.1.refs_0_), channel_id=1, source_target_pairs={{2,16},{3,17},{6,20},{7,21},{10,24},{11,25},{14,28},{15,29},{16,2}... | collective-permute-start | bytes 442376 | tf_op jit(solution)/shard_map/ppermute | solution.py:490
  72.2 2.7 %collective-permute-start.26 = (bf16[192,768]{1,0:T(8,128)(2,1)S(1)}, bf16[192,768]{1,0:T(8,128)(2,1)S(1)}, u32[]{:S(2)}, u32[]{:S(2)}) collective-permute-start(bf16[192,768]{1,0:T(8,128)(2,1)S(1)} %cross.1.mine_ref), channel_id=1, source_target_pairs={{1,0},{0,1},{3,2},{2,3},{5,4},{4,5},{7,6},{6,7},{9,8},{8,9},{11,10... | collective-permute-start | bytes 884744 | tf_op jit(solution)/shard_map/ppermute | solution.py:343

commit v12 on v8

--- a/solution.py
+++ b/solution.py
@@ -95,16 +95,6 @@
     flipped[1] = dot(weight_ref[...], g_ref[...], NT).astype(bf16)
     for peer, out in enumerate(outs):
         out[...] = flipped[:, place(peer, rows)]
-
-
-def pair_kernel(first_ref, second_ref, out_ref):
-    out_ref[0] = first_ref[...]
-    out_ref[1] = second_ref[...]
-
-
-def relay_kernel(sib_ref, across_ref, out_ref):
-    out_ref[0] = sib_ref[...]
-    out_ref[1] = across_ref[1]
 
 
 def gather_kernel(*refs):
@@ -209,8 +199,7 @@
 
 
 def query_grad_kernel(
-    window_ref, probs_ref, query_ref, stats_ref, mixed_ref, mine_ref, sib_ref, across_ref, own_ref,
-    token_ref, grads, flipped
+    window_ref, probs_ref, query_ref, stats_ref, dq_ref, own_ref, token_ref, grads
 ):
     rows = query_ref.shape[1]
     span = query_ref.shape[2] // LAYER
@@ -228,17 +217,14 @@
             back = dot(window_ref[1, at, block(j, span)], grad[:, cols], TN)
             prob = probs_ref[head, block(j, span), cols].astype(f32)
             grads[block(j, span), cols] = (prob * (back - delta[:, cols])).astype(bf16)
-        flipped[at] = (dot(window_ref[0, at], grads[...], NN) * scale).astype(bf16)
+        dq_ref[at] = (dot(window_ref[0, at], grads[...], NN) * scale).astype(bf16)
         own_ref[0, at] = dot(query_ref[0, at], grads[inside], NT)
         own_ref[1, at] = dot(grad, probs_ref[head, inside], NT)
-    for peer, out in enumerate((mine_ref, sib_ref, across_ref.at[0], across_ref.at[1])):
-        out[0] = mixed_ref[:, place(peer, span)]
-        out[1] = flipped[:, place(peer, span)]
     token_ref[...] = jnp.zeros_like(token_ref)
 
 
 def key_grad_kernel(
-    pair_ref, low_ref, high_ref, stats_low, stats_high, dead_ref, own_ref, *refs
+    pair_ref, low_ref, high_ref, stats_low, stats_high, dead_ref, own_ref, mixed_ref, dq_ref, *refs
 ):
     outs, (token_ref, flipped) = refs[:LAYER], refs[LAYER:]
     rows = pair_ref.shape[1]
@@ -267,27 +253,21 @@
             flipped[0, at, own] = keys.astype(bf16)
             flipped[1, at, own] = values.astype(bf16)
     for peer, out in enumerate(outs):
-        out[...] = flipped[:, :, place(peer, span)]
+        at = place(peer, span)
+        out[0] = mixed_ref[:, at]
+        out[1] = dq_ref[:, at]
+        out[2:] = flipped[:, :, at]
     token_ref[...] = jnp.zeros_like(token_ref)
 
 
-def output_kernel(
-    mine_ref, across_ref, sib_ref, weight_ref, out_ref, dq_ref, token_ref, flipped
-):
-    ins = mine_ref, sib_ref.at[0], across_ref.at[0], sib_ref.at[1]
+def output_kernel(*refs):
+    ins, refs = refs[:LAYER], refs[LAYER:]
+    weight_ref, out_ref, dq_ref, dk_ref, dv_ref, token_ref, flipped = refs
     for peer, ref in enumerate(ins):
         flipped[:, place(peer, ref.shape[1])] = ref[...]
     out_ref[...] = dot(flipped[0], weight_ref[...], TN).astype(bf16)
-    dq_ref[...] = flipped[1].T
-    token_ref[...] = jnp.zeros_like(token_ref)
-
-
-def key_output_kernel(*refs):
-    ins, (dk_ref, dv_ref, token_ref, flipped) = refs[:LAYER], refs[LAYER:]
-    for peer, ref in enumerate(ins):
-        flipped[:, place(peer, ref.shape[1])] = ref[...]
-    dk_ref[...] = flipped[0].T
-    dv_ref[...] = flipped[1].T
+    for n, ref in enumerate((dq_ref, dk_ref, dv_ref)):
+        ref[...] = flipped[n + 1].T
     token_ref[...] = jnp.zeros_like(token_ref)
 
 
@@ -301,10 +281,10 @@
     return lax.rem(lax.axis_index("station") // stride, 2)
 
 
-def weight_kernel(mixed_ref, mine_ref, sib_ref, send_ref, keep_ref, right):
-    for n in range(2):
-        right[place(2 * n, mine_ref.shape[1])] = mine_ref[n]
-        right[place(2 * n + 1, mine_ref.shape[1])] = sib_ref[n]
+def weight_kernel(mixed_ref, *refs):
+    ins, (send_ref, keep_ref, right) = refs[:LAYER], refs[LAYER:]
+    for peer, ref in enumerate(ins):
+        right[place(peer, ref.shape[0])] = ref[...]
     send, keep = halves(lax.rem(lax.axis_index("dp"), 2), send_ref.shape[0])
     send_ref[...] = dot(mixed_ref[send], right[...], NN).astype(bf16)
     keep_ref[...] = dot(mixed_ref[keep], right[...], NN)
@@ -329,7 +309,7 @@
         out_ref[at] = value
 
 
-def cross_kernel(mine_ref, second_ref, first_ref, out_ref):
+def cross_kernel(mine_ref, first_ref, second_ref, out_ref):
     window = lax.rem(lax.axis_index("dp"), 2)
     other, here = halves(window, mine_ref.shape[0])
     at_home = bit_of(2) == window
@@ -376,7 +356,6 @@
             name="gather", after=after,
         )
 
-    g_across = swap(g, 2)
     mine, *parts = call(
         pack_kernel, [HBM] * 2, [part_shape] * LAYER, (k, v),
         [pltpu.VMEM((2, span, width), bf16), pltpu.VMEM((2, width, span), bf16), dma((2,))],
@@ -384,24 +363,21 @@
     )
     q, *parts = lax.optimization_barrier((q, *parts))
     parts = in_layer(parts)
-    up, down, pair = gather((mine, *parts), (g_across,))
+    up, down, pair = gather((mine, *parts))
     mine, *query_parts, g_copy = call(
         project_kernel, [VMEM] * 3, [part_shape] * LAYER + [flat_shape],
         (q, g, out_weight), [pltpu.VMEM((2, width, span), bf16)], name="project",
     )
-    up, *query_parts = lax.optimization_barrier((up, *query_parts))
+    up, g_later, *query_parts = lax.optimization_barrier((up, g, *query_parts))
     kv_low, kv_high = along(up, down)
-    (g_pair,) = call(
-        pair_kernel, [VMEM] * 2, [shape_of(2, span, width)], (g_copy, g_across), name="pair",
-        after=parts,
-    )
-    g_pairs = g_pair, swap(g_pair, 1)
+    g_across = swap(g_later, 2)
+    g_parts = g_copy, swap(g_later, 1), g_across, swap(g_across, 1)
     bias, dead = call(
         functools.partial(live_kernel, stations), [SMEM] * 2,
         [shape_of(16, LAYER * span, dtype=f32), shape_of(8, HOPS * span, dtype=f32)],
         (partner_ids, partner_count), name="live",
     )
-    up, down, query = gather((mine, *in_layer(query_parts)), (bias, g_pairs[1]))
+    up, down, query = gather((mine, *in_layer(query_parts)), (bias,))
     qg_low, qg_high = along(up, down)
     stats_shape = shape_of(8, HOPS * span, dtype=f32)
     mixed, stats, up, down, probs, window = call(
@@ -418,38 +394,26 @@
     stats_low, stats_high = along(up, down)
 
     send, part = call(
-        weight_kernel, [VMEM] * 3,
+        weight_kernel, [VMEM] * (LAYER + 1),
         [shape_of(rows // 2, width), shape_of(rows // 2, width, dtype=f32)],
-        (mixed, *g_pairs), [pltpu.VMEM((LAYER * span, width), bf16)], name="weight",
-    )
-
-    mine, to_sib, to_across, own_grad, query_token = call(
-        query_grad_kernel, [VMEM] * 5,
-        [part_shape, part_shape, shape_of(2, 2, rows, span), shape_of(2, rows, LAYER * span, dtype=f32)]
-        + [TOKEN],
-        (window, probs, query, stats, mixed),
-        [pltpu.VMEM((BLOCKS * span, LAYER * span), bf16), pltpu.VMEM((rows, LAYER * span), bf16)],
+        (mixed, *g_parts), [pltpu.VMEM((LAYER * span, width), bf16)], name="weight",
+    )
+
+    dq, own_grad, query_token = call(
+        query_grad_kernel, [VMEM] * 4,
+        [shape_of(rows, LAYER * span), shape_of(2, rows, LAYER * span, dtype=f32), TOKEN],
+        (window, probs, query, stats), [pltpu.VMEM((BLOCKS * span, LAYER * span), bf16)],
         limit=20, name="query_grad", after=(send,),
     )
-    across = swap(to_across, 2)
-    (relay,) = call(
-        relay_kernel, [VMEM] * 2, [shape_of(2, 2, rows, span)], (to_sib, across), name="relay"
-    )
-    relayed = swap(relay, 1)
-    layer_output, grad_query, output_token = call(
-        output_kernel, [VMEM] * 4, [flat_shape] * 2 + [TOKEN],
-        (mine, across, relayed, out_weight), [pltpu.VMEM((2, width, span), bf16)], name="output",
-    )
-
     mine, *parts, key_token = call(
-        key_grad_kernel, [VMEM] * 7, [part_shape] * LAYER + [TOKEN],
-        (pair, qg_low, qg_high, stats_low, stats_high, dead, own_grad),
+        key_grad_kernel, [VMEM] * 9, [shape_of(4, rows, span)] * LAYER + [TOKEN],
+        (pair, qg_low, qg_high, stats_low, stats_high, dead, own_grad, mixed, dq),
         [pltpu.VMEM((2, rows, LAYER * span), bf16)], limit=20, name="key_grad",
     )
-    key_parts = in_layer(parts)
-    grad_key, grad_value, key_output_token = call(
-        key_output_kernel, [VMEM] * LAYER, [flat_shape] * 2 + [TOKEN],
-        (mine, *key_parts), [pltpu.VMEM((2, width, span), bf16)], name="key_output",
+    parts = in_layer(parts)
+    layer_output, grad_query, grad_key, grad_value, output_token = call(
+        output_kernel, [VMEM] * (LAYER + 1), [flat_shape] * 4 + [TOKEN],
+        (mine, *parts, out_weight), [pltpu.VMEM((4, width, span), bf16)], name="output",
     )
 
     scale = 1.0 / math.sqrt(span * windows * stations)
@@ -469,11 +433,11 @@
         total = add_round(part, swap(send, LAYER), (key_token,))
         stride = 2 * LAYER
         while stride < stations:
-            total = add_round(total, swap(total, stride), (across,))
+            total = add_round(total, swap(total, stride))
             stride *= 2
         (total,) = call(
             functools.partial(join_kernel, LAYER, None), [VMEM] * 2, [shape_of(2 * count, width)],
-            (total, swap(total, LAYER)), name="join", after=key_parts,
+            (total, swap(total, LAYER)), name="join", after=parts,
         )
         first, second = [], []
         for w in range(2):
@@ -486,8 +450,8 @@
         axes = ("dp", "station")
         (total,) = call(
             cross_kernel, [VMEM] * 3, [shape_of(4 * count, width)],
-            (total, lax.ppermute(total, axes, second), lax.ppermute(total, axes, first)),
-            name="cross", after=(output_token, key_output_token),
+            (total, lax.ppermute(total, axes, first), lax.ppermute(total, axes, second)),
+            name="cross", after=(output_token,),
         )
         (grad_weight,) = call(
             functools.partial(join_kernel, 1, scale), [VMEM] * 2,
@@ -497,7 +461,7 @@
         start = lax.axis_index("station") % LAYER * rows
         all_grad = jnp.zeros((LAYER * span, width), bf16)
         for peer in range(LAYER):
-            value = g_pairs[peer % 2][peer // 2]
+            value = g_parts[peer]
             spot = lax.axis_index("station") % LAYER ^ peer
             all_grad = lax.dynamic_update_slice_in_dim(all_grad, value, spot * span, 0)
         mine = dot(mixed, all_grad, NN).astype(bf16)

time: 75.6 us -> 71.2 us (0.942); the launches traced: 74.5 us -> 70.9 us
  starting transfers between devices: 35.8 us -> 33 us
  Pallas kernels: 16.7 us -> 15.7 us
    ppermute x17 -> x16, waiting for transfers between devices: 9.18 us -> 13 us  [swap(): lax.ppermute(value, 'station', [(s ^ stride, s) for s in range(stations)])]
    ppermute x3, waiting for transfers between devices: 3.12 us -> 0.79 us  [along(): lax.ppermute(down, 'station', [(s, (s - LAYER) % stations) for s in range...]
    ppermute x3, waiting for transfers between devices: 3.68 us -> 1.59 us  [along(): lax.ppermute(up, 'station', [(s, (s + LAYER) % stations) for s in range(s...]
    ppermute x17 -> x16, starting transfers between devices: 20.1 us -> 18.4 us  [swap(): lax.ppermute(value, 'station', [(s ^ stride, s) for s in range(stations)])]
    pallas_call x19 -> x16, Pallas kernels: 16.7 us -> 15.7 us  [call(): pl.pallas_call(kernel, in_specs=ins, out_specs=[VMEM] * len(outs), out_sh...]
    ppermute x1, waiting for transfers between devices: 1.86 us -> 2.7 us  [local(): lax.ppermute(total, axes, second)]
    unnamed x15 -> x17, local copies, waits for them, and re-layouts: 3.23 us -> 3.23 us
  transfers between devices with their start and end apart: 26 -> 25, of which waited for: 10 -> 10; matrix products, arithmetic and copies ran while one was open for 0% -> 0% of each run, Pallas kernels for 21% -> 17%
where the time goes in v12:
time: 71.2 us; the launch traced here: 70.9 us
  starting transfers between devices  33 us (46%)
  waiting for transfers between devices  18.1 us (25%)
  Pallas kernels  15.7 us (22%)
  local copies, waits for them, and re-layouts  3.23 us (5%)
  between operations  0.84 us (1%)
    ppermute x16, starting transfers between devices, swap(): lax.ppermute(value, 'station', [(s ^ stride, s) for s in range(stations)])  18.4 us
    pallas_call x16, Pallas kernels, call(): pl.pallas_call(kernel, in_specs=ins, out_specs=[VMEM] * len(outs), out_sh...  15.7 us
    ppermute x16, waiting for transfers between devices, swap(): lax.ppermute(value, 'station', [(s ^ stride, s) for s in range(stations)])  13 us
    ppermute x3, starting transfers between devices, along(): lax.ppermute(down, 'station', [(s, (s - LAYER) % stations) for s in range...  6.84 us
    unnamed x17, local copies, waits for them, and re-layouts  3.23 us
    ppermute x3, starting transfers between devices, along(): lax.ppermute(up, 'station', [(s, (s + LAYER) % stations) for s in range(s...  2.98 us
    ppermute x1, starting transfers between devices, local(): lax.ppermute(total, axes, second)  2.87 us
    ppermute x1, waiting for transfers between devices, local(): lax.ppermute(total, axes, second)  2.7 us
  transfers between devices with their start and end apart: 25, of which 10 were waited for; matrix products, arithmetic and copies ran while one was open for 0% of the time, Pallas kernels for 17%

profile of v12, /device:TPU:3, one launch (start us, length us, event | category | flops | bytes accessed | tf_op | source)
XLA Modules:
  0.0 70.9 jit_solution(9440864348272431529)
XLA Ops:
  0.7 2.0 %pack.1 = (bf16[2,192,128]{2,1,0:T(8,128)(2,1)}, bf16[2,192,128]{2,1,0:T(8,128)(2,1)}, bf16[2,192,128]{2,1,0:T(8,128)(2,1)}, bf16[2,192,128]{2,1,0:T(8,128)(2,1)}) custom-call(bf16[128,768]{1,0:T(8,128)(2,1)} %bitcast.12, bf16[128,768]{1,0:T(8,128)(2,1)} %bitcast.13), custom_call_target="tpu_custom_call" | custom-call | flops 1 | bytes 1 | tf_op jit(solution)/shard_map/pack/pallas_call | solution.py:50
  2.6 0.7 %collective-permute-start = (bf16[2,192,128]{2,1,0:T(8,128)(2,1)}, bf16[2,192,128]{2,1,0:T(8,128)(2,1)S(1)}, u32[]{:S(2)}, u32[]{:S(2)}) collective-permute-start(bf16[2,192,128]{2,1,0:T(8,128)(2,1)} %get-tuple-element.58), channel_id=1, source_target_pairs={{1,0},{0,1},{3,2},{2,3},{5,4},{4,5},{7,6},{6,7},{9,8},{8,9},{11,10... | collective-permute-start | bytes 294920 | tf_op jit(solution)/shard_map/ppermute | solution.py:331
  3.4 1.7 %collective-permute-start.2 = (bf16[2,192,128]{2,1,0:T(8,128)(2,1)}, bf16[2,192,128]{2,1,0:T(8,128)(2,1)S(1)}, u32[]{:S(2)}, u32[]{:S(2)}) collective-permute-start(bf16[2,192,128]{2,1,0:T(8,128)(2,1)} %get-tuple-element.60), channel_id=1, source_target_pairs={{3,0},{2,1},{1,2},{0,3},{7,4},{6,5},{5,6},{4,7},{11,8},{10,9},{9,1... | collective-permute-start | bytes 294920 | tf_op jit(solution)/shard_map/ppermute | solution.py:331
  5.1 1.3 %copy-done = bf16[768,768]{1,0:T(8,128)(2,1)S(1)} copy-done((bf16[768,768]{1,0:T(8,128)(2,1)S(1)}, bf16[768,768]{1,0:T(8,128)(2,1)}, u32[]{:S(2)}) %copy-start) | copy-done | bytes 1179672
  6.3 0.9 %copy-done.2 = bf16[1,1,128,768]{3,2,1,0:T(8,128)(2,1)S(1)} copy-done((bf16[1,1,128,768]{3,2,1,0:T(8,128)(2,1)S(1)}, bf16[1,1,128,768]{3,2,1,0:T(8,128)(2,1)}, u32[]{:S(2)}) %copy-start.2) | copy-done | bytes 196632
  7.3 0.9 %copy-done.3 = bf16[1,1,128,768]{3,2,1,0:T(8,128)(2,1)S(1)} copy-done((bf16[1,1,128,768]{3,2,1,0:T(8,128)(2,1)S(1)}, bf16[1,1,128,768]{3,2,1,0:T(8,128)(2,1)}, u32[]{:S(2)}) %copy-start.3) | copy-done | bytes 196632
  8.2 0.5 project.1
  8.7 1.5 %collective-permute-done.2.refs_3_ = bf16[2,192,128]{2,1,0:T(8,128)(2,1)S(1)} collective-permute-done((bf16[2,192,128]{2,1,0:T(8,128)(2,1)}, bf16[2,192,128]{2,1,0:T(8,128)(2,1)S(1)}, u32[]{:S(2)}, u32[]{:S(2)}) %collective-permute-start.2) | collective-permute-done | bytes 98336 | tf_op jit(solution)/shard_map/ppermute | solution.py:331
  10.2 0.1 gather.2
  10.4 1.3 %collective-permute-start.8 = (bf16[2,192,384]{2,1,0:T(8,128)(2,1)S(1)}, bf16[2,192,384]{2,1,0:T(8,128)(2,1)S(1)}, u32[]{:S(2)}, u32[]{:S(2)}) collective-permute-start(bf16[2,192,384]{2,1,0:T(8,128)(2,1)S(1)} %get-tuple-element.74), channel_id=1, source_target_pairs={{0,4},{1,5},{2,6},{3,7},{4,8},{5,9},{6,10},{7,11},{8,12},{9,13},{1... | collective-permute-start | bytes 884744 | tf_op jit(solution)/shard_map/ppermute | solution.py:337
  11.7 0.3 collective-permute-start.13
  12.0 0.8 %collective-permute-start.3 = (bf16[2,192,128]{2,1,0:T(8,128)(2,1)S(1)}, bf16[2,192,128]{2,1,0:T(8,128)(2,1)S(1)}, u32[]{:S(2)}, u32[]{:S(2)}) collective-permute-start(bf16[2,192,128]{2,1,0:T(8,128)(2,1)S(1)} %get-tuple-element.68), channel_id=1, source_target_pairs={{1,0},{0,1},{3,2},{2,3},{5,4},{4,5},{7,6},{6,7},{9,8},{8,9},{11,10... | collective-permute-start | bytes 294920 | tf_op jit(solution)/shard_map/ppermute | solution.py:331
  12.8 1.9 %collective-permute-start.9 = (bf16[2,192,384]{2,1,0:T(8,128)(2,1)S(1)}, bf16[2,192,384]{2,1,0:T(8,128)(2,1)S(1)}, u32[]{:S(2)}, u32[]{:S(2)}) collective-permute-start(bf16[2,192,384]{2,1,0:T(8,128)(2,1)S(1)} %get-tuple-element.75), channel_id=1, source_target_pairs={{0,12},{1,13},{2,14},{3,15},{4,0},{5,1},{6,2},{7,3},{8,4},{9,5},{1... | collective-permute-start | bytes 884744 | tf_op jit(solution)/shard_map/ppermute | solution.py:338
  14.7 1.3 %collective-permute-start.4 = (bf16[2,192,128]{2,1,0:T(8,128)(2,1)S(1)}, bf16[2,192,128]{2,1,0:T(8,128)(2,1)S(1)}, u32[]{:S(2)}, u32[]{:S(2)}) collective-permute-start(bf16[2,192,128]{2,1,0:T(8,128)(2,1)S(1)} %get-tuple-element.69), channel_id=1, source_target_pairs={{2,0},{3,1},{0,2},{1,3},{6,4},{7,5},{4,6},{5,7},{10,8},{11,9},{8,1... | collective-permute-start | bytes 294920 | tf_op jit(solution)/shard_map/ppermute | solution.py:331
  16.0 0.6 collective-permute-start.5
  16.6 3.2 %collective-permute-done.4.refs_2_ = bf16[2,192,128]{2,1,0:T(8,128)(2,1)S(1)} collective-permute-done((bf16[2,192,128]{2,1,0:T(8,128)(2,1)S(1)}, bf16[2,192,128]{2,1,0:T(8,128)(2,1)S(1)}, u32[]{:S(2)}, u32[]{:S(2)}) %collective-permute-start.4) | collective-permute-done | bytes 98336 | tf_op jit(solution)/shard_map/ppermute | solution.py:331
  19.8 2.3 %collective-permute-start.12 = (bf16[128,768]{1,0:T(8,128)(2,1)S(1)}, bf16[128,768]{1,0:T(8,128)(2,1)S(1)}, u32[]{:S(2)}, u32[]{:S(2)}) collective-permute-start(bf16[128,768]{1,0:T(8,128)(2,1)S(1)} %bitcast.11), channel_id=1, source_target_pairs={{1,0},{0,1},{3,2},{2,3},{5,4},{4,5},{7,6},{6,7},{9,8},{8,9},{11,10... | collective-permute-start | bytes 589832 | tf_op jit(solution)/shard_map/ppermute | solution.py:331
  22.1 0.1 copy.12.ids_ref
  22.2 1.2 %live.1 = (f32[16,512]{1,0:T(8,128)S(1)}, f32[8,384]{1,0:T(8,128)S(1)}) custom-call(s32[16,6]{1,0:T(8,128)S(1)} %copy.12.ids_ref, s32[16]{0:T(128)S(1)} %copy-done.6), custom_call_target="tpu_custom_call" | custom-call | flops 1 | bytes 1 | tf_op jit(solution)/shard_map/live/pallas_call | solution.py:50
  23.5 0.1 gather.3
  23.6 1.3 %collective-permute-start.6 = (bf16[2,192,384]{2,1,0:T(8,128)(2,1)S(1)}, bf16[2,192,384]{2,1,0:T(8,128)(2,1)S(1)}, u32[]{:S(2)}, u32[]{:S(2)}) collective-permute-start(bf16[2,192,384]{2,1,0:T(8,128)(2,1)S(1)} %get-tuple-element.72), channel_id=1, source_target_pairs={{0,4},{1,5},{2,6},{3,7},{4,8},{5,9},{6,10},{7,11},{8,12},{9,13},{1... | collective-permute-start | bytes 884744 | tf_op jit(solution)/shard_map/ppermute | solution.py:337
  25.0 2.0 %collective-permute-start.7 = (bf16[2,192,384]{2,1,0:T(8,128)(2,1)S(1)}, bf16[2,192,384]{2,1,0:T(8,128)(2,1)S(1)}, u32[]{:S(2)}, u32[]{:S(2)}) collective-permute-start(bf16[2,192,384]{2,1,0:T(8,128)(2,1)S(1)} %get-tuple-element.73), channel_id=1, source_target_pairs={{0,12},{1,13},{2,14},{3,15},{4,0},{5,1},{6,2},{7,3},{8,4},{9,5},{1... | collective-permute-start | bytes 884744 | tf_op jit(solution)/shard_map/ppermute | solution.py:338
  26.9 0.7 collective-permute-done.9.high_ref
  27.6 3.2 %forward.1 = (bf16[192,512]{1,0:T(8,128)(2,1)S(1)}, f32[8,512]{1,0:T(8,128)S(1)}, f32[8,384]{1,0:T(8,128)S(1)}, f32[8,384]{1,0:T(8,128)S(1)}, bf16[3,1280,512]{2...) custom-call(bf16[2,192,512]{2,1,0:T(8,128)(2,1)S(1)} %get-tuple-element.61.pair_ref, ...), custom_call_target="tpu_custom_call" | custom-call | flops 1 | bytes 1 | tf_op jit(solution)/shard_map/forward/pallas_call | solution.py:50
  30.8 0.5 weight.1
  31.3 1.3 %collective-permute-start.18 = (bf16[96,768]{1,0:T(8,128)(2,1)S(1)}, bf16[96,768]{1,0:T(8,128)(2,1)S(1)}, u32[]{:S(2)}, u32[]{:S(2)}) collective-permute-start(bf16[96,768]{1,0:T(8,128)(2,1)S(1)} %get-tuple-element.86.refs_4_), channel_id=1, source_target_pairs={{0,16},{16,0},{1,17},{17,1},{2,18},{18,2},{3,19},{19,3},{4,20},{20... | collective-permute-start | bytes 442376 | tf_op jit(solution)/shard_map/ppermute | solution.py:342
  32.6 0.3 collective-permute-start.10
  32.9 3.0 %collective-permute-start.11 = (f32[8,384]{1,0:T(8,128)S(1)}, f32[8,384]{1,0:T(8,128)S(1)}, u32[]{:S(2)}, u32[]{:S(2)}) collective-permute-start(f32[8,384]{1,0:T(8,128)S(1)} %get-tuple-element.78), channel_id=1, source_target_pairs={{0,12},{1,13},{2,14},{3,15},{4,0},{5,1},{6,2},{7,3},{8,4},{9,5},{1... | collective-permute-start | bytes 36872 | tf_op jit(solution)/shard_map/ppermute | solution.py:338
  35.8 2.4 %query_grad.1 = (bf16[192,512]{1,0:T(8,128)(2,1)S(1)}, f32[2,192,512]{2,1,0:T(8,128)S(1)}, f32[8,128]{1,0:T(8,128)S(1)}) custom-call(bf16[2,192,1280]{2,1,0:T(8,128)(2,1)S(1)} %get-tuple-element.80.refs_0_, bf16[3,1280,512]{2,1,0:T(8,128)(2,1)S(1)} %get-tuple-element.81.refs_1_, bf16[2,192,512]{2,1,0:T(8,128)(2,1)S(1)} %get-tuple-element.76.query_ref.refs_2_, ...), custom_call_target="tpu_custom_call" | custom-call | flops 1 | bytes 1 | tf_op jit(solution)/shard_map/query_grad/pallas_call | solution.py:50
  38.3 1.6 %collective-permute-done.10.stats_low.refs_5_ = f32[8,384]{1,0:T(8,128)S(1)} collective-permute-done((f32[8,384]{1,0:T(8,128)S(1)}, f32[8,384]{1,0:T(8,128)S(1)}, u32[]{:S(2)}, u32[]{:S(2)}) %collective-permute-start.10) | collective-permute-done | bytes 12320 | tf_op jit(solution)/shard_map/ppermute | solution.py:337
  39.9 0.1 collective-permute-done.11.stats_high.refs_6_
  40.0 0.1 split.1
  40.1 1.5 %collective-permute-start.19 = (bf16[48,768]{1,0:T(8,128)(2,1)S(1)}, bf16[48,768]{1,0:T(8,128)(2,1)S(1)}, u32[]{:S(2)}, u32[]{:S(2)}) collective-permute-start(bf16[48,768]{1,0:T(8,128)(2,1)S(1)} %get-tuple-element.100), channel_id=1, source_target_pairs={{4,0},{5,1},{6,2},{7,3},{0,4},{1,5},{2,6},{3,7},{12,8},{13,9},{14,... | collective-permute-start | bytes 221192 | tf_op jit(solution)/shard_map/ppermute | solution.py:331
  41.5 3.2 %key_grad.1 = (bf16[4,192,128]{2,1,0:T(8,128)(2,1)S(1)}, bf16[4,192,128]{2,1,0:T(8,128)(2,1)S(1)}, bf16[4,192,128]{2,1,0:T(8,128)(2,1)S(1)}, bf16[4,192,128]{2,1,0:T(8,128)(2,1)S(1)}, f32[8,128]{1,0:T(8,128)S(1)}) custom-call(bf16[2,192,512]{2,1,0:T(8,128)(2,1)S(1)} %get-tuple-element.61.pair_ref, ...), custom_call_target="tpu_custom_call" | custom-call | flops 1 | bytes 1 | tf_op jit(solution)/shard_map/key_grad/pallas_call | solution.py:50
  44.7 0.8 %collective-permute-start.15 = (bf16[4,192,128]{2,1,0:T(8,128)(2,1)S(1)}, bf16[4,192,128]{2,1,0:T(8,128)(2,1)S(1)}, u32[]{:S(2)}, u32[]{:S(2)}) collective-permute-start(bf16[4,192,128]{2,1,0:T(8,128)(2,1)S(1)} %get-tuple-element.90), channel_id=1, source_target_pairs={{1,0},{0,1},{3,2},{2,3},{5,4},{4,5},{7,6},{6,7},{9,8},{8,9},{11,10... | collective-permute-start | bytes 589832 | tf_op jit(solution)/shard_map/ppermute | solution.py:331
  45.6 1.7 %collective-permute-start.17 = (bf16[4,192,128]{2,1,0:T(8,128)(2,1)S(1)}, bf16[4,192,128]{2,1,0:T(8,128)(2,1)S(1)}, u32[]{:S(2)}, u32[]{:S(2)}) collective-permute-start(bf16[4,192,128]{2,1,0:T(8,128)(2,1)S(1)} %get-tuple-element.92), channel_id=1, source_target_pairs={{3,0},{2,1},{1,2},{0,3},{7,4},{6,5},{5,6},{4,7},{11,8},{10,9},{9,1... | collective-permute-start | bytes 589832 | tf_op jit(solution)/shard_map/ppermute | solution.py:331
  47.3 2.5 %collective-permute-start.20 = (bf16[48,768]{1,0:T(8,128)(2,1)S(1)}, bf16[48,768]{1,0:T(8,128)(2,1)S(1)}, u32[]{:S(2)}, u32[]{:S(2)}) collective-permute-start(bf16[48,768]{1,0:T(8,128)(2,1)S(1)} %add.2.part_ref), channel_id=1, source_target_pairs={{8,0},{9,1},{10,2},{11,3},{12,4},{13,5},{14,6},{15,7},{0,8},{1,9},... | collective-permute-start | bytes 221192 | tf_op jit(solution)/shard_map/ppermute | solution.py:331
  49.8 4.0 %collective-permute-done.20.got_ref = bf16[48,768]{1,0:T(8,128)(2,1)S(1)} collective-permute-done((bf16[48,768]{1,0:T(8,128)(2,1)S(1)}, bf16[48,768]{1,0:T(8,128)(2,1)S(1)}, u32[]{:S(2)}, u32[]{:S(2)}) %collective-permute-start.20) | collective-permute-done | bytes 73760 | tf_op jit(solution)/shard_map/ppermute | solution.py:331
  53.8 0.1 collective-permute-start.21
  53.9 2.5 %collective-permute-done.17.refs_3_.refs_4_ = bf16[4,192,128]{2,1,0:T(8,128)(2,1)S(1)} collective-permute-done((bf16[4,192,128]{2,1,0:T(8,128)(2,1)S(1)}, bf16[4,192,128]{2,1,0:T(8,128)(2,1)S(1)}, u32[]{:S(2)}, u32[]{:S(2)}) %collective-permute-start.17) | collective-permute-done | bytes 196640 | tf_op jit(solution)/shard_map/ppermute | solution.py:331
  56.4 0.7 collective-permute-done.21.refs_1_
  57.1 0.6 collective-permute-start.22
  57.8 2.9 %collective-permute-start.23 = (bf16[96,768]{1,0:T(8,128)(2,1)S(1)}, bf16[96,768]{1,0:T(8,128)(2,1)S(1)}, u32[]{:S(2)}, u32[]{:S(2)}) collective-permute-start(bf16[96,768]{1,0:T(8,128)(2,1)S(1)} %join.1.refs_0_), channel_id=1, source_target_pairs={{2,16},{3,17},{6,20},{7,21},{10,24},{11,25},{14,28},{15,29},{16,2}... | collective-permute-start | bytes 442376 | tf_op jit(solution)/shard_map/ppermute | solution.py:453
  60.6 1.2 %output.1 = (bf16[128,768]{1,0:T(8,128)(2,1)}, bf16[128,768]{1,0:T(8,128)(2,1)}, bf16[128,768]{1,0:T(8,128)(2,1)}, bf16[128,768]{1,0:T(8,128)(2,1)}, f32[8,128]{1,0:T(8,128)S(1)}) custom-call(bf16[4,192,128]{2,1,0:T(8,128)(2,1)S(1)} %get-tuple-element.89.refs_0_, bf16[4,192,128]{2,1,0:T(8,128)(2,1)S(1)} %collective-permute-done.15.refs_1_.refs_2_, ...), custom_call_target="tpu_custom_call" | custom-call | flops 1 | bytes 1 | tf_op jit(solution)/shard_map/output/pallas_call | solution.py:50
  61.8 2.7 %collective-permute-done.23.refs_2_ = bf16[96,768]{1,0:T(8,128)(2,1)S(1)} collective-permute-done((bf16[96,768]{1,0:T(8,128)(2,1)S(1)}, bf16[96,768]{1,0:T(8,128)(2,1)S(1)}, u32[]{:S(2)}, u32[]{:S(2)}) %collective-permute-start.23) | collective-permute-done | bytes 147488 | tf_op jit(solution)/shard_map/ppermute | solution.py:453
  64.6 4.0 %collective-permute-start.24 = (bf16[192,768]{1,0:T(8,128)(2,1)S(1)}, bf16[192,768]{1,0:T(8,128)(2,1)S(1)}, u32[]{:S(2)}, u32[]{:S(2)}) collective-permute-start(bf16[192,768]{1,0:T(8,128)(2,1)S(1)} %cross.1.mine_ref), channel_id=1, source_target_pairs={{1,0},{0,1},{3,2},{2,3},{5,4},{4,5},{7,6},{6,7},{9,8},{8,9},{11,10... | collective-permute-start | bytes 884744 | tf_op jit(solution)/shard_map/ppermute | solution.py:331
  68.6 1.2 %collective-permute-done.24.got_ref = bf16[192,768]{1,0:T(8,128)(2,1)S(1)} collective-permute-done((bf16[192,768]{1,0:T(8,128)(2,1)S(1)}, bf16[192,768]{1,0:T(8,128)(2,1)S(1)}, u32[]{:S(2)}, u32[]{:S(2)}) %collective-permute-start.24) | collective-permute-done | bytes 294944 | tf_op jit(solution)/shard_map/ppermute | solution.py:331
  69.8 1.1 %last.1 = f32[384,768]{1,0:T(8,128)} custom-call(bf16[192,768]{1,0:T(8,128)(2,1)S(1)} %cross.1.mine_ref, bf16[192,768]{1,0:T(8,128)(2,1)S(1)} %collective-permute-done.24.got_ref), custom_call_target="tpu_custom_call" | custom-call | flops 1 | bytes 1 | tf_op jit(solution)/shard_map/last/pallas_call | solution.py:50
  (35 shorter events, 0.2 us)
Async XLA Ops:
  0.6 11.1 %copy-start.4 = (bf16[1,1,128,768]{3,2,1,0:T(8,128)(2,1)S(1)}, bf16[1,1,128,768]{3,2,1,0:T(8,128)(2,1)}, u32[]{:S(2)}) copy-start(bf16[1,1,128,768]{3,2,1,0:T(8,128)(2,1)} %param.10) | copy-start | bytes 589828
  0.6 21.5 %copy-start.7 = (s32[16,6]{0,1:T(8,128)S(1)}, s32[16,6]{0,1:T(8,128)}, u32[]{:S(2)}) copy-start(s32[16,6]{0,1:T(8,128)} %param.12) | copy-start | bytes 1156
  0.7 21.6 %copy-start.6 = (s32[16]{0:T(128)S(1)}, s32[16]{0:T(128)}, u32[]{:S(2)}) copy-start(s32[16]{0:T(128)} %count_ref.1) | copy-start | bytes 196
  2.6 6.1 %collective-permute-start = (bf16[2,192,128]{2,1,0:T(8,128)(2,1)}, bf16[2,192,128]{2,1,0:T(8,128)(2,1)S(1)}, u32[]{:S(2)}, u32[]{:S(2)}) collective-permute-start(bf16[2,192,128]{2,1,0:T(8,128)(2,1)} %get-tuple-element.58), channel_id=1, source_target_pairs={{1,0},{0,1},{3,2},{2,3},{5,4},{4,5},{7,6},{6,7},{9,8},{8,9},{11,10... | collective-permute-start | bytes 294920 | tf_op jit(solution)/shard_map/ppermute | solution.py:331
  3.4 5.4 %collective-permute-start.1 = (bf16[2,192,128]{2,1,0:T(8,128)(2,1)}, bf16[2,192,128]{2,1,0:T(8,128)(2,1)S(1)}, u32[]{:S(2)}, u32[]{:S(2)}) collective-permute-start(bf16[2,192,128]{2,1,0:T(8,128)(2,1)} %get-tuple-element.59), channel_id=1, source_target_pairs={{2,0},{3,1},{0,2},{1,3},{6,4},{7,5},{4,6},{5,7},{10,8},{11,9},{8,1... | collective-permute-start | bytes 294920 | tf_op jit(solution)/shard_map/ppermute | solution.py:331
  3.4 6.8 %collective-permute-start.2 = (bf16[2,192,128]{2,1,0:T(8,128)(2,1)}, bf16[2,192,128]{2,1,0:T(8,128)(2,1)S(1)}, u32[]{:S(2)}, u32[]{:S(2)}) collective-permute-start(bf16[2,192,128]{2,1,0:T(8,128)(2,1)} %get-tuple-element.60), channel_id=1, source_target_pairs={{3,0},{2,1},{1,2},{0,3},{7,4},{6,5},{5,6},{4,7},{11,8},{10,9},{9,1... | collective-permute-start | bytes 294920 | tf_op jit(solution)/shard_map/ppermute | solution.py:331
  5.1 1.3 %copy-start = (bf16[768,768]{1,0:T(8,128)(2,1)S(1)}, bf16[768,768]{1,0:T(8,128)(2,1)}, u32[]{:S(2)}) copy-start(bf16[768,768]{1,0:T(8,128)(2,1)} %refs_4_.1) | copy-start | bytes 3538948
  6.3 0.9 %copy-start.2 = (bf16[1,1,128,768]{3,2,1,0:T(8,128)(2,1)S(1)}, bf16[1,1,128,768]{3,2,1,0:T(8,128)(2,1)}, u32[]{:S(2)}) copy-start(bf16[1,1,128,768]{3,2,1,0:T(8,128)(2,1)} %param.7) | copy-start | bytes 589828
  7.3 0.9 %copy-start.3 = (bf16[1,1,128,768]{3,2,1,0:T(8,128)(2,1)S(1)}, bf16[1,1,128,768]{3,2,1,0:T(8,128)(2,1)}, u32[]{:S(2)}) copy-start(bf16[1,1,128,768]{3,2,1,0:T(8,128)(2,1)} %param.10) | copy-start | bytes 589828
  8.2 2.0 %copy-start.5 = (bf16[2,192,128]{2,1,0:T(8,128)(2,1)S(1)}, bf16[2,192,128]{2,1,0:T(8,128)(2,1)}, u32[]{:S(2)}) copy-start(bf16[2,192,128]{2,1,0:T(8,128)(2,1)} %get-tuple-element.54.refs_0_) | copy-start | bytes 294916
  10.4 14.6 %collective-permute-start.8 = (bf16[2,192,384]{2,1,0:T(8,128)(2,1)S(1)}, bf16[2,192,384]{2,1,0:T(8,128)(2,1)S(1)}, u32[]{:S(2)}, u32[]{:S(2)}) collective-permute-start(bf16[2,192,384]{2,1,0:T(8,128)(2,1)S(1)} %get-tuple-element.74), channel_id=1, source_target_pairs={{0,4},{1,5},{2,6},{3,7},{4,8},{5,9},{6,10},{7,11},{8,12},{9,13},{1... | collective-permute-start | bytes 884744 | tf_op jit(solution)/shard_map/ppermute | solution.py:337
  11.7 10.4 %collective-permute-start.13 = (bf16[128,768]{1,0:T(8,128)(2,1)S(1)}, bf16[128,768]{1,0:T(8,128)(2,1)S(1)}, u32[]{:S(2)}, u32[]{:S(2)}) collective-permute-start(bf16[128,768]{1,0:T(8,128)(2,1)S(1)} %bitcast.10), channel_id=1, source_target_pairs={{2,0},{3,1},{0,2},{1,3},{6,4},{7,5},{4,6},{5,7},{10,8},{11,9},{8,1... | collective-permute-start | bytes 589832 | tf_op jit(solution)/shard_map/ppermute | solution.py:331
  12.0 4.0 %collective-permute-start.3 = (bf16[2,192,128]{2,1,0:T(8,128)(2,1)S(1)}, bf16[2,192,128]{2,1,0:T(8,128)(2,1)S(1)}, u32[]{:S(2)}, u32[]{:S(2)}) collective-permute-start(bf16[2,192,128]{2,1,0:T(8,128)(2,1)S(1)} %get-tuple-element.68), channel_id=1, source_target_pairs={{1,0},{0,1},{3,2},{2,3},{5,4},{4,5},{7,6},{6,7},{9,8},{8,9},{11,10... | collective-permute-start | bytes 294920 | tf_op jit(solution)/shard_map/ppermute | solution.py:331
  12.8 14.8 %collective-permute-start.9 = (bf16[2,192,384]{2,1,0:T(8,128)(2,1)S(1)}, bf16[2,192,384]{2,1,0:T(8,128)(2,1)S(1)}, u32[]{:S(2)}, u32[]{:S(2)}) collective-permute-start(bf16[2,192,384]{2,1,0:T(8,128)(2,1)S(1)} %get-tuple-element.75), channel_id=1, source_target_pairs={{0,12},{1,13},{2,14},{3,15},{4,0},{5,1},{6,2},{7,3},{8,4},{9,5},{1... | collective-permute-start | bytes 884744 | tf_op jit(solution)/shard_map/ppermute | solution.py:338
  14.7 5.1 %collective-permute-start.4 = (bf16[2,192,128]{2,1,0:T(8,128)(2,1)S(1)}, bf16[2,192,128]{2,1,0:T(8,128)(2,1)S(1)}, u32[]{:S(2)}, u32[]{:S(2)}) collective-permute-start(bf16[2,192,128]{2,1,0:T(8,128)(2,1)S(1)} %get-tuple-element.69), channel_id=1, source_target_pairs={{2,0},{3,1},{0,2},{1,3},{6,4},{7,5},{4,6},{5,7},{10,8},{11,9},{8,1... | collective-permute-start | bytes 294920 | tf_op jit(solution)/shard_map/ppermute | solution.py:331
  16.0 7.5 %collective-permute-start.5 = (bf16[2,192,128]{2,1,0:T(8,128)(2,1)S(1)}, bf16[2,192,128]{2,1,0:T(8,128)(2,1)S(1)}, u32[]{:S(2)}, u32[]{:S(2)}) collective-permute-start(bf16[2,192,128]{2,1,0:T(8,128)(2,1)S(1)} %get-tuple-element.70), channel_id=1, source_target_pairs={{3,0},{2,1},{1,2},{0,3},{7,4},{6,5},{5,6},{4,7},{11,8},{10,9},{9,1... | collective-permute-start | bytes 294920 | tf_op jit(solution)/shard_map/ppermute | solution.py:331
  19.8 11.0 %collective-permute-start.12 = (bf16[128,768]{1,0:T(8,128)(2,1)S(1)}, bf16[128,768]{1,0:T(8,128)(2,1)S(1)}, u32[]{:S(2)}, u32[]{:S(2)}) collective-permute-start(bf16[128,768]{1,0:T(8,128)(2,1)S(1)} %bitcast.11), channel_id=1, source_target_pairs={{1,0},{0,1},{3,2},{2,3},{5,4},{4,5},{7,6},{6,7},{9,8},{8,9},{11,10... | collective-permute-start | bytes 589832 | tf_op jit(solution)/shard_map/ppermute | solution.py:331
  22.1 8.7 %collective-permute-start.14 = (bf16[128,768]{1,0:T(8,128)(2,1)S(1)}, bf16[128,768]{1,0:T(8,128)(2,1)S(1)}, u32[]{:S(2)}, u32[]{:S(2)}) collective-permute-start(bf16[128,768]{1,0:T(8,128)(2,1)S(1)} %collective-permute-done.13.refs_2_), channel_id=1, source_target_pairs={{1,0},{0,1},{3,2},{2,3},{5,4},{4,5},{7,6},{6,7},{9,8},{8,9},{11,10... | collective-permute-start | bytes 589832 | tf_op jit(solution)/shard_map/ppermute | solution.py:331
  23.6 16.4 %collective-permute-start.6 = (bf16[2,192,384]{2,1,0:T(8,128)(2,1)S(1)}, bf16[2,192,384]{2,1,0:T(8,128)(2,1)S(1)}, u32[]{:S(2)}, u32[]{:S(2)}) collective-permute-start(bf16[2,192,384]{2,1,0:T(8,128)(2,1)S(1)} %get-tuple-element.72), channel_id=1, source_target_pairs={{0,4},{1,5},{2,6},{3,7},{4,8},{5,9},{6,10},{7,11},{8,12},{9,13},{1... | collective-permute-start | bytes 884744 | tf_op jit(solution)/shard_map/ppermute | solution.py:337
  25.0 15.0 %collective-permute-start.7 = (bf16[2,192,384]{2,1,0:T(8,128)(2,1)S(1)}, bf16[2,192,384]{2,1,0:T(8,128)(2,1)S(1)}, u32[]{:S(2)}, u32[]{:S(2)}) collective-permute-start(bf16[2,192,384]{2,1,0:T(8,128)(2,1)S(1)} %get-tuple-element.73), channel_id=1, source_target_pairs={{0,12},{1,13},{2,14},{3,15},{4,0},{5,1},{6,2},{7,3},{8,4},{9,5},{1... | collective-permute-start | bytes 884744 | tf_op jit(solution)/shard_map/ppermute | solution.py:338
  31.3 8.7 %collective-permute-start.18 = (bf16[96,768]{1,0:T(8,128)(2,1)S(1)}, bf16[96,768]{1,0:T(8,128)(2,1)S(1)}, u32[]{:S(2)}, u32[]{:S(2)}) collective-permute-start(bf16[96,768]{1,0:T(8,128)(2,1)S(1)} %get-tuple-element.86.refs_4_), channel_id=1, source_target_pairs={{0,16},{16,0},{1,17},{17,1},{2,18},{18,2},{3,19},{19,3},{4,20},{20... | collective-permute-start | bytes 442376 | tf_op jit(solution)/shard_map/ppermute | solution.py:342
  32.6 7.3 %collective-permute-start.10 = (f32[8,384]{1,0:T(8,128)S(1)}, f32[8,384]{1,0:T(8,128)S(1)}, u32[]{:S(2)}, u32[]{:S(2)}) collective-permute-start(f32[8,384]{1,0:T(8,128)S(1)} %get-tuple-element.77), channel_id=1, source_target_pairs={{0,4},{1,5},{2,6},{3,7},{4,8},{5,9},{6,10},{7,11},{8,12},{9,13},{1... | collective-permute-start | bytes 36872 | tf_op jit(solution)/shard_map/ppermute | solution.py:337
  32.9 7.1 %collective-permute-start.11 = (f32[8,384]{1,0:T(8,128)S(1)}, f32[8,384]{1,0:T(8,128)S(1)}, u32[]{:S(2)}, u32[]{:S(2)}) collective-permute-start(f32[8,384]{1,0:T(8,128)S(1)} %get-tuple-element.78), channel_id=1, source_target_pairs={{0,12},{1,13},{2,14},{3,15},{4,0},{5,1},{6,2},{7,3},{8,4},{9,5},{1... | collective-permute-start | bytes 36872 | tf_op jit(solution)/shard_map/ppermute | solution.py:338
  40.1 7.2 %collective-permute-start.19 = (bf16[48,768]{1,0:T(8,128)(2,1)S(1)}, bf16[48,768]{1,0:T(8,128)(2,1)S(1)}, u32[]{:S(2)}, u32[]{:S(2)}) collective-permute-start(bf16[48,768]{1,0:T(8,128)(2,1)S(1)} %get-tuple-element.100), channel_id=1, source_target_pairs={{4,0},{5,1},{6,2},{7,3},{0,4},{1,5},{2,6},{3,7},{12,8},{13,9},{14,... | collective-permute-start | bytes 221192 | tf_op jit(solution)/shard_map/ppermute | solution.py:331
  44.7 15.9 %copy-start.1 = (bf16[768,768]{1,0:T(8,128)(2,1)S(1)}, bf16[768,768]{1,0:T(8,128)(2,1)}, u32[]{:S(2)}) copy-start(bf16[768,768]{1,0:T(8,128)(2,1)} %refs_4_.1) | copy-start | bytes 3538948
  44.7 9.2 %collective-permute-start.15 = (bf16[4,192,128]{2,1,0:T(8,128)(2,1)S(1)}, bf16[4,192,128]{2,1,0:T(8,128)(2,1)S(1)}, u32[]{:S(2)}, u32[]{:S(2)}) collective-permute-start(bf16[4,192,128]{2,1,0:T(8,128)(2,1)S(1)} %get-tuple-element.90), channel_id=1, source_target_pairs={{1,0},{0,1},{3,2},{2,3},{5,4},{4,5},{7,6},{6,7},{9,8},{8,9},{11,10... | collective-permute-start | bytes 589832 | tf_op jit(solution)/shard_map/ppermute | solution.py:331
  45.6 8.3 %collective-permute-start.16 = (bf16[4,192,128]{2,1,0:T(8,128)(2,1)S(1)}, bf16[4,192,128]{2,1,0:T(8,128)(2,1)S(1)}, u32[]{:S(2)}, u32[]{:S(2)}) collective-permute-start(bf16[4,192,128]{2,1,0:T(8,128)(2,1)S(1)} %get-tuple-element.91), channel_id=1, source_target_pairs={{2,0},{3,1},{0,2},{1,3},{6,4},{7,5},{4,6},{5,7},{10,8},{11,9},{8,1... | collective-permute-start | bytes 589832 | tf_op jit(solution)/shard_map/ppermute | solution.py:331
  45.6 10.9 %collective-permute-start.17 = (bf16[4,192,128]{2,1,0:T(8,128)(2,1)S(1)}, bf16[4,192,128]{2,1,0:T(8,128)(2,1)S(1)}, u32[]{:S(2)}, u32[]{:S(2)}) collective-permute-start(bf16[4,192,128]{2,1,0:T(8,128)(2,1)S(1)} %get-tuple-element.92), channel_id=1, source_target_pairs={{3,0},{2,1},{1,2},{0,3},{7,4},{6,5},{5,6},{4,7},{11,8},{10,9},{9,1... | collective-permute-start | bytes 589832 | tf_op jit(solution)/shard_map/ppermute | solution.py:331
  47.3 6.5 %collective-permute-start.20 = (bf16[48,768]{1,0:T(8,128)(2,1)S(1)}, bf16[48,768]{1,0:T(8,128)(2,1)S(1)}, u32[]{:S(2)}, u32[]{:S(2)}) collective-permute-start(bf16[48,768]{1,0:T(8,128)(2,1)S(1)} %add.2.part_ref), channel_id=1, source_target_pairs={{8,0},{9,1},{10,2},{11,3},{12,4},{13,5},{14,6},{15,7},{0,8},{1,9},... | collective-permute-start | bytes 221192 | tf_op jit(solution)/shard_map/ppermute | solution.py:331
  53.8 3.3 %collective-permute-start.21 = (bf16[48,768]{1,0:T(8,128)(2,1)S(1)}, bf16[48,768]{1,0:T(8,128)(2,1)S(1)}, u32[]{:S(2)}, u32[]{:S(2)}) collective-permute-start(bf16[48,768]{1,0:T(8,128)(2,1)S(1)} %add.3.refs_0_), channel_id=1, source_target_pairs={{4,0},{5,1},{6,2},{7,3},{0,4},{1,5},{2,6},{3,7},{12,8},{13,9},{14,... | collective-permute-start | bytes 221192 | tf_op jit(solution)/shard_map/ppermute | solution.py:331
  57.1 4.7 %collective-permute-start.22 = (bf16[96,768]{1,0:T(8,128)(2,1)S(1)}, bf16[96,768]{1,0:T(8,128)(2,1)S(1)}, u32[]{:S(2)}, u32[]{:S(2)}) collective-permute-start(bf16[96,768]{1,0:T(8,128)(2,1)S(1)} %join.1.refs_0_), channel_id=1, source_target_pairs={{0,2},{1,3},{2,18},{3,19},{4,6},{5,7},{6,22},{7,23},{8,10},{9,11},... | collective-permute-start | bytes 442376 | tf_op jit(solution)/shard_map/ppermute | solution.py:453
  57.8 6.8 %collective-permute-start.23 = (bf16[96,768]{1,0:T(8,128)(2,1)S(1)}, bf16[96,768]{1,0:T(8,128)(2,1)S(1)}, u32[]{:S(2)}, u32[]{:S(2)}) collective-permute-start(bf16[96,768]{1,0:T(8,128)(2,1)S(1)} %join.1.refs_0_), channel_id=1, source_target_pairs={{2,16},{3,17},{6,20},{7,21},{10,24},{11,25},{14,28},{15,29},{16,2}... | collective-permute-start | bytes 442376 | tf_op jit(solution)/shard_map/ppermute | solution.py:453
  64.6 5.2 %collective-permute-start.24 = (bf16[192,768]{1,0:T(8,128)(2,1)S(1)}, bf16[192,768]{1,0:T(8,128)(2,1)S(1)}, u32[]{:S(2)}, u32[]{:S(2)}) collective-permute-start(bf16[192,768]{1,0:T(8,128)(2,1)S(1)} %cross.1.mine_ref), channel_id=1, source_target_pairs={{1,0},{0,1},{3,2},{2,3},{5,4},{4,5},{7,6},{6,7},{9,8},{8,9},{11,10... | collective-permute-start | bytes 884744 | tf_op jit(solution)/shard_map/ppermute | solution.py:331

commit v13 on v12

--- a/solution.py
+++ b/solution.py
@@ -423,7 +423,7 @@
         send, part = call(
             functools.partial(split_kernel, LAYER), [VMEM] * 2,
             [shape_of(count, width), shape_of(count, width, dtype=f32)],
-            (part, got), name="split", after=(query_token, qg_low, qg_high, stats_low, stats_high),
+            (part, got), name="split", after=(query_token,),
         )
 
         def add_round(part, got, after=()):

time: 71.2 us -> 73.3 us (1.029)
  waiting for transfers between devices: 18.1 us -> 19.3 us
  starting transfers between devices: 33 us -> 34.1 us
    ppermute x16, starting transfers between devices: 18.4 us -> 19.6 us  [swap(): lax.ppermute(value, 'station', [(s ^ stride, s) for s in range(stations)])]
    ppermute x1, waiting for transfers between devices: 2.7 us -> 3.47 us  [local(): lax.ppermute(total, axes, second)]
    ppermute x1, starting transfers between devices: 2.87 us -> 2.09 us  [local(): lax.ppermute(total, axes, second)]
  transfers between devices with their start and end apart: 25 -> 25, of which waited for: 10 -> 9; matrix products, arithmetic and copies ran while one was open for 0% -> 0% of each run, Pallas kernels for 17% -> 17%
where the time goes in v13:
time: 73.3 us; the launch traced here: 73.1 us
  starting transfers between devices  34.1 us (47%)
  waiting for transfers between devices  19.3 us (26%)
  Pallas kernels  15.7 us (21%)
  local copies, waits for them, and re-layouts  3.23 us (4%)
  between operations  0.82 us (1%)
    ppermute x16, starting transfers between devices, swap(): lax.ppermute(value, 'station', [(s ^ stride, s) for s in range(stations)])  19.6 us
    pallas_call x16, Pallas kernels, call(): pl.pallas_call(kernel, in_specs=ins, out_specs=[VMEM] * len(outs), out_sh...  15.7 us
    ppermute x16, waiting for transfers between devices, swap(): lax.ppermute(value, 'station', [(s ^ stride, s) for s in range(stations)])  13 us
    ppermute x3, starting transfers between devices, along(): lax.ppermute(down, 'station', [(s, (s - LAYER) % stations) for s in range...  6.63 us
    ppermute x1, waiting for transfers between devices, local(): lax.ppermute(total, axes, second)  3.47 us
    unnamed x17, local copies, waits for them, and re-layouts  3.23 us
    ppermute x3, starting transfers between devices, along(): lax.ppermute(up, 'station', [(s, (s + LAYER) % stations) for s in range(s...  3.19 us
    ppermute x1, starting transfers between devices, local(): lax.ppermute(total, axes, second)  2.09 us
  transfers between devices with their start and end apart: 25, of which 9 were waited for; matrix products, arithmetic and copies ran while one was open for 0% of the time, Pallas kernels for 17%

profile of v13, /device:TPU:3, one launch (start us, length us, event | category | flops | bytes accessed | tf_op | source)
XLA Modules:
  0.0 73.1 jit_solution(9324833877765866335)
XLA Ops:
  0.7 2.0 %pack.1 = (bf16[2,192,128]{2,1,0:T(8,128)(2,1)}, bf16[2,192,128]{2,1,0:T(8,128)(2,1)}, bf16[2,192,128]{2,1,0:T(8,128)(2,1)}, bf16[2,192,128]{2,1,0:T(8,128)(2,1)}) custom-call(bf16[128,768]{1,0:T(8,128)(2,1)} %bitcast.12, bf16[128,768]{1,0:T(8,128)(2,1)} %bitcast.13), custom_call_target="tpu_custom_call" | custom-call | flops 1 | bytes 1 | tf_op jit(solution)/shard_map/pack/pallas_call | solution.py:50
  2.6 0.7 %collective-permute-start = (bf16[2,192,128]{2,1,0:T(8,128)(2,1)}, bf16[2,192,128]{2,1,0:T(8,128)(2,1)S(1)}, u32[]{:S(2)}, u32[]{:S(2)}) collective-permute-start(bf16[2,192,128]{2,1,0:T(8,128)(2,1)} %get-tuple-element.58), channel_id=1, source_target_pairs={{1,0},{0,1},{3,2},{2,3},{5,4},{4,5},{7,6},{6,7},{9,8},{8,9},{11,10... | collective-permute-start | bytes 294920 | tf_op jit(solution)/shard_map/ppermute | solution.py:331
  3.4 1.7 %collective-permute-start.2 = (bf16[2,192,128]{2,1,0:T(8,128)(2,1)}, bf16[2,192,128]{2,1,0:T(8,128)(2,1)S(1)}, u32[]{:S(2)}, u32[]{:S(2)}) collective-permute-start(bf16[2,192,128]{2,1,0:T(8,128)(2,1)} %get-tuple-element.60), channel_id=1, source_target_pairs={{3,0},{2,1},{1,2},{0,3},{7,4},{6,5},{5,6},{4,7},{11,8},{10,9},{9,1... | collective-permute-start | bytes 294920 | tf_op jit(solution)/shard_map/ppermute | solution.py:331
  5.1 1.3 %copy-done = bf16[768,768]{1,0:T(8,128)(2,1)S(1)} copy-done((bf16[768,768]{1,0:T(8,128)(2,1)S(1)}, bf16[768,768]{1,0:T(8,128)(2,1)}, u32[]{:S(2)}) %copy-start) | copy-done | bytes 1179672
  6.3 0.9 %copy-done.2 = bf16[1,1,128,768]{3,2,1,0:T(8,128)(2,1)S(1)} copy-done((bf16[1,1,128,768]{3,2,1,0:T(8,128)(2,1)S(1)}, bf16[1,1,128,768]{3,2,1,0:T(8,128)(2,1)}, u32[]{:S(2)}) %copy-start.2) | copy-done | bytes 196632
  7.3 0.9 %copy-done.3 = bf16[1,1,128,768]{3,2,1,0:T(8,128)(2,1)S(1)} copy-done((bf16[1,1,128,768]{3,2,1,0:T(8,128)(2,1)S(1)}, bf16[1,1,128,768]{3,2,1,0:T(8,128)(2,1)}, u32[]{:S(2)}) %copy-start.3) | copy-done | bytes 196632
  8.2 0.5 project.1
  8.7 1.5 %collective-permute-done.2.refs_3_ = bf16[2,192,128]{2,1,0:T(8,128)(2,1)S(1)} collective-permute-done((bf16[2,192,128]{2,1,0:T(8,128)(2,1)}, bf16[2,192,128]{2,1,0:T(8,128)(2,1)S(1)}, u32[]{:S(2)}, u32[]{:S(2)}) %collective-permute-start.2) | collective-permute-done | bytes 98336 | tf_op jit(solution)/shard_map/ppermute | solution.py:331
  10.2 0.1 gather.2
  10.4 1.3 %collective-permute-start.8 = (bf16[2,192,384]{2,1,0:T(8,128)(2,1)S(1)}, bf16[2,192,384]{2,1,0:T(8,128)(2,1)S(1)}, u32[]{:S(2)}, u32[]{:S(2)}) collective-permute-start(bf16[2,192,384]{2,1,0:T(8,128)(2,1)S(1)} %get-tuple-element.74), channel_id=1, source_target_pairs={{0,4},{1,5},{2,6},{3,7},{4,8},{5,9},{6,10},{7,11},{8,12},{9,13},{1... | collective-permute-start | bytes 884744 | tf_op jit(solution)/shard_map/ppermute | solution.py:337
  11.7 0.3 collective-permute-start.13
  12.0 0.8 %collective-permute-start.3 = (bf16[2,192,128]{2,1,0:T(8,128)(2,1)S(1)}, bf16[2,192,128]{2,1,0:T(8,128)(2,1)S(1)}, u32[]{:S(2)}, u32[]{:S(2)}) collective-permute-start(bf16[2,192,128]{2,1,0:T(8,128)(2,1)S(1)} %get-tuple-element.68), channel_id=1, source_target_pairs={{1,0},{0,1},{3,2},{2,3},{5,4},{4,5},{7,6},{6,7},{9,8},{8,9},{11,10... | collective-permute-start | bytes 294920 | tf_op jit(solution)/shard_map/ppermute | solution.py:331
  12.8 1.9 %collective-permute-start.9 = (bf16[2,192,384]{2,1,0:T(8,128)(2,1)S(1)}, bf16[2,192,384]{2,1,0:T(8,128)(2,1)S(1)}, u32[]{:S(2)}, u32[]{:S(2)}) collective-permute-start(bf16[2,192,384]{2,1,0:T(8,128)(2,1)S(1)} %get-tuple-element.75), channel_id=1, source_target_pairs={{0,12},{1,13},{2,14},{3,15},{4,0},{5,1},{6,2},{7,3},{8,4},{9,5},{1... | collective-permute-start | bytes 884744 | tf_op jit(solution)/shard_map/ppermute | solution.py:338
  14.7 1.3 %collective-permute-start.4 = (bf16[2,192,128]{2,1,0:T(8,128)(2,1)S(1)}, bf16[2,192,128]{2,1,0:T(8,128)(2,1)S(1)}, u32[]{:S(2)}, u32[]{:S(2)}) collective-permute-start(bf16[2,192,128]{2,1,0:T(8,128)(2,1)S(1)} %get-tuple-element.69), channel_id=1, source_target_pairs={{2,0},{3,1},{0,2},{1,3},{6,4},{7,5},{4,6},{5,7},{10,8},{11,9},{8,1... | collective-permute-start | bytes 294920 | tf_op jit(solution)/shard_map/ppermute | solution.py:331
  16.0 0.6 collective-permute-start.5
  16.6 3.2 %collective-permute-done.4.refs_2_ = bf16[2,192,128]{2,1,0:T(8,128)(2,1)S(1)} collective-permute-done((bf16[2,192,128]{2,1,0:T(8,128)(2,1)S(1)}, bf16[2,192,128]{2,1,0:T(8,128)(2,1)S(1)}, u32[]{:S(2)}, u32[]{:S(2)}) %collective-permute-start.4) | collective-permute-done | bytes 98336 | tf_op jit(solution)/shard_map/ppermute | solution.py:331
  19.8 2.3 %collective-permute-start.12 = (bf16[128,768]{1,0:T(8,128)(2,1)S(1)}, bf16[128,768]{1,0:T(8,128)(2,1)S(1)}, u32[]{:S(2)}, u32[]{:S(2)}) collective-permute-start(bf16[128,768]{1,0:T(8,128)(2,1)S(1)} %bitcast.11), channel_id=1, source_target_pairs={{1,0},{0,1},{3,2},{2,3},{5,4},{4,5},{7,6},{6,7},{9,8},{8,9},{11,10... | collective-permute-start | bytes 589832 | tf_op jit(solution)/shard_map/ppermute | solution.py:331
  22.1 0.1 copy.12.ids_ref
  22.2 1.2 %live.1 = (f32[16,512]{1,0:T(8,128)S(1)}, f32[8,384]{1,0:T(8,128)S(1)}) custom-call(s32[16,6]{1,0:T(8,128)S(1)} %copy.12.ids_ref, s32[16]{0:T(128)S(1)} %copy-done.6), custom_call_target="tpu_custom_call" | custom-call | flops 1 | bytes 1 | tf_op jit(solution)/shard_map/live/pallas_call | solution.py:50
  23.5 0.1 gather.3
  23.6 1.3 %collective-permute-start.6 = (bf16[2,192,384]{2,1,0:T(8,128)(2,1)S(1)}, bf16[2,192,384]{2,1,0:T(8,128)(2,1)S(1)}, u32[]{:S(2)}, u32[]{:S(2)}) collective-permute-start(bf16[2,192,384]{2,1,0:T(8,128)(2,1)S(1)} %get-tuple-element.72), channel_id=1, source_target_pairs={{0,4},{1,5},{2,6},{3,7},{4,8},{5,9},{6,10},{7,11},{8,12},{9,13},{1... | collective-permute-start | bytes 884744 | tf_op jit(solution)/shard_map/ppermute | solution.py:337
  25.0 2.0 %collective-permute-start.7 = (bf16[2,192,384]{2,1,0:T(8,128)(2,1)S(1)}, bf16[2,192,384]{2,1,0:T(8,128)(2,1)S(1)}, u32[]{:S(2)}, u32[]{:S(2)}) collective-permute-start(bf16[2,192,384]{2,1,0:T(8,128)(2,1)S(1)} %get-tuple-element.73), channel_id=1, source_target_pairs={{0,12},{1,13},{2,14},{3,15},{4,0},{5,1},{6,2},{7,3},{8,4},{9,5},{1... | collective-permute-start | bytes 884744 | tf_op jit(solution)/shard_map/ppermute | solution.py:338
  26.9 0.7 collective-permute-done.9.high_ref
  27.6 3.2 %forward.1 = (bf16[192,512]{1,0:T(8,128)(2,1)S(1)}, f32[8,512]{1,0:T(8,128)S(1)}, f32[8,384]{1,0:T(8,128)S(1)}, f32[8,384]{1,0:T(8,128)S(1)}, bf16[3,1280,512]{2...) custom-call(bf16[2,192,512]{2,1,0:T(8,128)(2,1)S(1)} %get-tuple-element.61.pair_ref, ...), custom_call_target="tpu_custom_call" | custom-call | flops 1 | bytes 1 | tf_op jit(solution)/shard_map/forward/pallas_call | solution.py:50
  30.8 0.5 weight.1
  31.3 1.3 %collective-permute-start.18 = (bf16[96,768]{1,0:T(8,128)(2,1)S(1)}, bf16[96,768]{1,0:T(8,128)(2,1)S(1)}, u32[]{:S(2)}, u32[]{:S(2)}) collective-permute-start(bf16[96,768]{1,0:T(8,128)(2,1)S(1)} %get-tuple-element.86.refs_4_), channel_id=1, source_target_pairs={{0,16},{16,0},{1,17},{17,1},{2,18},{18,2},{3,19},{19,3},{4,20},{20... | collective-permute-start | bytes 442376 | tf_op jit(solution)/shard_map/ppermute | solution.py:342
  32.6 2.4 %query_grad.1 = (bf16[192,512]{1,0:T(8,128)(2,1)S(1)}, f32[2,192,512]{2,1,0:T(8,128)S(1)}, f32[8,128]{1,0:T(8,128)S(1)}) custom-call(bf16[2,192,1280]{2,1,0:T(8,128)(2,1)S(1)} %get-tuple-element.80.refs_0_, bf16[3,1280,512]{2,1,0:T(8,128)(2,1)S(1)} %get-tuple-element.81.refs_1_, bf16[2,192,512]{2,1,0:T(8,128)(2,1)S(1)} %get-tuple-element.76.query_ref.refs_2_, ...), custom_call_target="tpu_custom_call" | custom-call | flops 1 | bytes 1 | tf_op jit(solution)/shard_map/query_grad/pallas_call | solution.py:50
  35.0 0.6 collective-permute-done.18.refs_1_
  35.7 1.0 %collective-permute-start.19 = (bf16[48,768]{1,0:T(8,128)(2,1)S(1)}, bf16[48,768]{1,0:T(8,128)(2,1)S(1)}, u32[]{:S(2)}, u32[]{:S(2)}) collective-permute-start(bf16[48,768]{1,0:T(8,128)(2,1)S(1)} %get-tuple-element.100), channel_id=1, source_target_pairs={{4,0},{5,1},{6,2},{7,3},{0,4},{1,5},{2,6},{3,7},{12,8},{13,9},{14,... | collective-permute-start | bytes 221192 | tf_op jit(solution)/shard_map/ppermute | solution.py:331
  36.7 0.5 collective-permute-start.10
  37.2 2.8 %collective-permute-start.11 = (f32[8,384]{1,0:T(8,128)S(1)}, f32[8,384]{1,0:T(8,128)S(1)}, u32[]{:S(2)}, u32[]{:S(2)}) collective-permute-start(f32[8,384]{1,0:T(8,128)S(1)} %get-tuple-element.78), channel_id=1, source_target_pairs={{0,12},{1,13},{2,14},{3,15},{4,0},{5,1},{6,2},{7,3},{8,4},{9,5},{1... | collective-permute-start | bytes 36872 | tf_op jit(solution)/shard_map/ppermute | solution.py:338
  40.0 1.5 %collective-permute-done.10.stats_low = f32[8,384]{1,0:T(8,128)S(1)} collective-permute-done((f32[8,384]{1,0:T(8,128)S(1)}, f32[8,384]{1,0:T(8,128)S(1)}, u32[]{:S(2)}, u32[]{:S(2)}) %collective-permute-start.10) | collective-permute-done | bytes 12320 | tf_op jit(solution)/shard_map/ppermute | solution.py:337
  41.5 3.2 %key_grad.1 = (bf16[4,192,128]{2,1,0:T(8,128)(2,1)S(1)}, bf16[4,192,128]{2,1,0:T(8,128)(2,1)S(1)}, bf16[4,192,128]{2,1,0:T(8,128)(2,1)S(1)}, bf16[4,192,128]{2,1,0:T(8,128)(2,1)S(1)}, f32[8,128]{1,0:T(8,128)S(1)}) custom-call(bf16[2,192,512]{2,1,0:T(8,128)(2,1)S(1)} %get-tuple-element.61.pair_ref, bf16[2,192,384]{2,1,0:T(8,128)(2,1)S(1)} %collective-permute-done.6.low_ref, ...), custom_call_target="tpu_custom_call" | custom-call | flops 1 | bytes 1 | tf_op jit(solution)/shard_map/key_grad/pallas_call | solution.py:50
  44.6 0.0 copy-start.1
  44.7 3.1 %collective-permute-start.15 = (bf16[4,192,128]{2,1,0:T(8,128)(2,1)S(1)}, bf16[4,192,128]{2,1,0:T(8,128)(2,1)S(1)}, u32[]{:S(2)}, u32[]{:S(2)}) collective-permute-start(bf16[4,192,128]{2,1,0:T(8,128)(2,1)S(1)} %get-tuple-element.90), channel_id=1, source_target_pairs={{1,0},{0,1},{3,2},{2,3},{5,4},{4,5},{7,6},{6,7},{9,8},{8,9},{11,10... | collective-permute-start | bytes 589832 | tf_op jit(solution)/shard_map/ppermute | solution.py:331
  47.8 0.3 collective-permute-start.16
  48.0 1.4 %collective-permute-start.17 = (bf16[4,192,128]{2,1,0:T(8,128)(2,1)S(1)}, bf16[4,192,128]{2,1,0:T(8,128)(2,1)S(1)}, u32[]{:S(2)}, u32[]{:S(2)}) collective-permute-start(bf16[4,192,128]{2,1,0:T(8,128)(2,1)S(1)} %get-tuple-element.92), channel_id=1, source_target_pairs={{3,0},{2,1},{1,2},{0,3},{7,4},{6,5},{5,6},{4,7},{11,8},{10,9},{9,1... | collective-permute-start | bytes 589832 | tf_op jit(solution)/shard_map/ppermute | solution.py:331
  49.5 0.3 collective-permute-start.20
  49.8 4.4 %collective-permute-done.20.got_ref = bf16[48,768]{1,0:T(8,128)(2,1)S(1)} collective-permute-done((bf16[48,768]{1,0:T(8,128)(2,1)S(1)}, bf16[48,768]{1,0:T(8,128)(2,1)S(1)}, u32[]{:S(2)}, u32[]{:S(2)}) %collective-permute-start.20) | collective-permute-done | bytes 73760 | tf_op jit(solution)/shard_map/ppermute | solution.py:331
  54.2 1.6 %collective-permute-start.21 = (bf16[48,768]{1,0:T(8,128)(2,1)S(1)}, bf16[48,768]{1,0:T(8,128)(2,1)S(1)}, u32[]{:S(2)}, u32[]{:S(2)}) collective-permute-start(bf16[48,768]{1,0:T(8,128)(2,1)S(1)} %add.3.refs_0_), channel_id=1, source_target_pairs={{4,0},{5,1},{6,2},{7,3},{0,4},{1,5},{2,6},{3,7},{12,8},{13,9},{14,... | collective-permute-start | bytes 221192 | tf_op jit(solution)/shard_map/ppermute | solution.py:331
  55.9 2.8 %collective-permute-done.17.refs_3_.refs_4_ = bf16[4,192,128]{2,1,0:T(8,128)(2,1)S(1)} collective-permute-done((bf16[4,192,128]{2,1,0:T(8,128)(2,1)S(1)}, bf16[4,192,128]{2,1,0:T(8,128)(2,1)S(1)}, u32[]{:S(2)}, u32[]{:S(2)}) %collective-permute-start.17) | collective-permute-done | bytes 196640 | tf_op jit(solution)/shard_map/ppermute | solution.py:331
  58.7 1.3 %collective-permute-start.22 = (bf16[96,768]{1,0:T(8,128)(2,1)S(1)}, bf16[96,768]{1,0:T(8,128)(2,1)S(1)}, u32[]{:S(2)}, u32[]{:S(2)}) collective-permute-start(bf16[96,768]{1,0:T(8,128)(2,1)S(1)} %join.1.refs_0_), channel_id=1, source_target_pairs={{0,2},{1,3},{2,18},{3,19},{4,6},{5,7},{6,22},{7,23},{8,10},{9,11},... | collective-permute-start | bytes 442376 | tf_op jit(solution)/shard_map/ppermute | solution.py:453
  60.0 2.1 %collective-permute-start.23 = (bf16[96,768]{1,0:T(8,128)(2,1)S(1)}, bf16[96,768]{1,0:T(8,128)(2,1)S(1)}, u32[]{:S(2)}, u32[]{:S(2)}) collective-permute-start(bf16[96,768]{1,0:T(8,128)(2,1)S(1)} %join.1.refs_0_), channel_id=1, source_target_pairs={{2,16},{3,17},{6,20},{7,21},{10,24},{11,25},{14,28},{15,29},{16,2}... | collective-permute-start | bytes 442376 | tf_op jit(solution)/shard_map/ppermute | solution.py:453
  62.1 1.2 %output.1 = (bf16[128,768]{1,0:T(8,128)(2,1)}, bf16[128,768]{1,0:T(8,128)(2,1)}, bf16[128,768]{1,0:T(8,128)(2,1)}, bf16[128,768]{1,0:T(8,128)(2,1)}, f32[8,128]{1,0:T(8,128)S(1)}) custom-call(bf16[4,192,128]{2,1,0:T(8,128)(2,1)S(1)} %get-tuple-element.89.refs_0_, bf16[4,192,128]{2,1,0:T(8,128)(2,1)S(1)} %collective-permute-done.15.refs_1_.refs_2_, ...), custom_call_target="tpu_custom_call" | custom-call | flops 1 | bytes 1 | tf_op jit(solution)/shard_map/output/pallas_call | solution.py:50
  63.3 3.5 %collective-permute-done.23.refs_2_ = bf16[96,768]{1,0:T(8,128)(2,1)S(1)} collective-permute-done((bf16[96,768]{1,0:T(8,128)(2,1)S(1)}, bf16[96,768]{1,0:T(8,128)(2,1)S(1)}, u32[]{:S(2)}, u32[]{:S(2)}) %collective-permute-start.23) | collective-permute-done | bytes 147488 | tf_op jit(solution)/shard_map/ppermute | solution.py:453
  66.8 4.0 %collective-permute-start.24 = (bf16[192,768]{1,0:T(8,128)(2,1)S(1)}, bf16[192,768]{1,0:T(8,128)(2,1)S(1)}, u32[]{:S(2)}, u32[]{:S(2)}) collective-permute-start(bf16[192,768]{1,0:T(8,128)(2,1)S(1)} %cross.1.mine_ref), channel_id=1, source_target_pairs={{1,0},{0,1},{3,2},{2,3},{5,4},{4,5},{7,6},{6,7},{9,8},{8,9},{11,10... | collective-permute-start | bytes 884744 | tf_op jit(solution)/shard_map/ppermute | solution.py:331
  70.8 1.2 %collective-permute-done.24.got_ref = bf16[192,768]{1,0:T(8,128)(2,1)S(1)} collective-permute-done((bf16[192,768]{1,0:T(8,128)(2,1)S(1)}, bf16[192,768]{1,0:T(8,128)(2,1)S(1)}, u32[]{:S(2)}, u32[]{:S(2)}) %collective-permute-start.24) | collective-permute-done | bytes 294944 | tf_op jit(solution)/shard_map/ppermute | solution.py:331
  72.0 1.1 %last.1 = f32[384,768]{1,0:T(8,128)} custom-call(bf16[192,768]{1,0:T(8,128)(2,1)S(1)} %cross.1.mine_ref, bf16[192,768]{1,0:T(8,128)(2,1)S(1)} %collective-permute-done.24.got_ref), custom_call_target="tpu_custom_call" | custom-call | flops 1 | bytes 1 | tf_op jit(solution)/shard_map/last/pallas_call | solution.py:50
  (35 shorter events, 0.2 us)
Async XLA Ops:
  0.6 11.1 %copy-start.4 = (bf16[1,1,128,768]{3,2,1,0:T(8,128)(2,1)S(1)}, bf16[1,1,128,768]{3,2,1,0:T(8,128)(2,1)}, u32[]{:S(2)}) copy-start(bf16[1,1,128,768]{3,2,1,0:T(8,128)(2,1)} %param.10) | copy-start | bytes 589828
  0.6 21.5 %copy-start.7 = (s32[16,6]{0,1:T(8,128)S(1)}, s32[16,6]{0,1:T(8,128)}, u32[]{:S(2)}) copy-start(s32[16,6]{0,1:T(8,128)} %param.12) | copy-start | bytes 1156
  0.7 21.6 %copy-start.6 = (s32[16]{0:T(128)S(1)}, s32[16]{0:T(128)}, u32[]{:S(2)}) copy-start(s32[16]{0:T(128)} %count_ref.1) | copy-start | bytes 196
  2.6 6.1 %collective-permute-start = (bf16[2,192,128]{2,1,0:T(8,128)(2,1)}, bf16[2,192,128]{2,1,0:T(8,128)(2,1)S(1)}, u32[]{:S(2)}, u32[]{:S(2)}) collective-permute-start(bf16[2,192,128]{2,1,0:T(8,128)(2,1)} %get-tuple-element.58), channel_id=1, source_target_pairs={{1,0},{0,1},{3,2},{2,3},{5,4},{4,5},{7,6},{6,7},{9,8},{8,9},{11,10... | collective-permute-start | bytes 294920 | tf_op jit(solution)/shard_map/ppermute | solution.py:331
  3.4 5.4 %collective-permute-start.1 = (bf16[2,192,128]{2,1,0:T(8,128)(2,1)}, bf16[2,192,128]{2,1,0:T(8,128)(2,1)S(1)}, u32[]{:S(2)}, u32[]{:S(2)}) collective-permute-start(bf16[2,192,128]{2,1,0:T(8,128)(2,1)} %get-tuple-element.59), channel_id=1, source_target_pairs={{2,0},{3,1},{0,2},{1,3},{6,4},{7,5},{4,6},{5,7},{10,8},{11,9},{8,1... | collective-permute-start | bytes 294920 | tf_op jit(solution)/shard_map/ppermute | solution.py:331
  3.4 6.8 %collective-permute-start.2 = (bf16[2,192,128]{2,1,0:T(8,128)(2,1)}, bf16[2,192,128]{2,1,0:T(8,128)(2,1)S(1)}, u32[]{:S(2)}, u32[]{:S(2)}) collective-permute-start(bf16[2,192,128]{2,1,0:T(8,128)(2,1)} %get-tuple-element.60), channel_id=1, source_target_pairs={{3,0},{2,1},{1,2},{0,3},{7,4},{6,5},{5,6},{4,7},{11,8},{10,9},{9,1... | collective-permute-start | bytes 294920 | tf_op jit(solution)/shard_map/ppermute | solution.py:331
  5.1 1.3 %copy-start = (bf16[768,768]{1,0:T(8,128)(2,1)S(1)}, bf16[768,768]{1,0:T(8,128)(2,1)}, u32[]{:S(2)}) copy-start(bf16[768,768]{1,0:T(8,128)(2,1)} %refs_4_.1) | copy-start | bytes 3538948
  6.3 0.9 %copy-start.2 = (bf16[1,1,128,768]{3,2,1,0:T(8,128)(2,1)S(1)}, bf16[1,1,128,768]{3,2,1,0:T(8,128)(2,1)}, u32[]{:S(2)}) copy-start(bf16[1,1,128,768]{3,2,1,0:T(8,128)(2,1)} %param.7) | copy-start | bytes 589828
  7.3 0.9 %copy-start.3 = (bf16[1,1,128,768]{3,2,1,0:T(8,128)(2,1)S(1)}, bf16[1,1,128,768]{3,2,1,0:T(8,128)(2,1)}, u32[]{:S(2)}) copy-start(bf16[1,1,128,768]{3,2,1,0:T(8,128)(2,1)} %param.10) | copy-start | bytes 589828
  8.2 2.0 %copy-start.5 = (bf16[2,192,128]{2,1,0:T(8,128)(2,1)S(1)}, bf16[2,192,128]{2,1,0:T(8,128)(2,1)}, u32[]{:S(2)}) copy-start(bf16[2,192,128]{2,1,0:T(8,128)(2,1)} %get-tuple-element.54.refs_0_) | copy-start | bytes 294916
  10.4 14.6 %collective-permute-start.8 = (bf16[2,192,384]{2,1,0:T(8,128)(2,1)S(1)}, bf16[2,192,384]{2,1,0:T(8,128)(2,1)S(1)}, u32[]{:S(2)}, u32[]{:S(2)}) collective-permute-start(bf16[2,192,384]{2,1,0:T(8,128)(2,1)S(1)} %get-tuple-element.74), channel_id=1, source_target_pairs={{0,4},{1,5},{2,6},{3,7},{4,8},{5,9},{6,10},{7,11},{8,12},{9,13},{1... | collective-permute-start | bytes 884744 | tf_op jit(solution)/shard_map/ppermute | solution.py:337
  11.7 10.4 %collective-permute-start.13 = (bf16[128,768]{1,0:T(8,128)(2,1)S(1)}, bf16[128,768]{1,0:T(8,128)(2,1)S(1)}, u32[]{:S(2)}, u32[]{:S(2)}) collective-permute-start(bf16[128,768]{1,0:T(8,128)(2,1)S(1)} %bitcast.10), channel_id=1, source_target_pairs={{2,0},{3,1},{0,2},{1,3},{6,4},{7,5},{4,6},{5,7},{10,8},{11,9},{8,1... | collective-permute-start | bytes 589832 | tf_op jit(solution)/shard_map/ppermute | solution.py:331
  12.0 4.0 %collective-permute-start.3 = (bf16[2,192,128]{2,1,0:T(8,128)(2,1)S(1)}, bf16[2,192,128]{2,1,0:T(8,128)(2,1)S(1)}, u32[]{:S(2)}, u32[]{:S(2)}) collective-permute-start(bf16[2,192,128]{2,1,0:T(8,128)(2,1)S(1)} %get-tuple-element.68), channel_id=1, source_target_pairs={{1,0},{0,1},{3,2},{2,3},{5,4},{4,5},{7,6},{6,7},{9,8},{8,9},{11,10... | collective-permute-start | bytes 294920 | tf_op jit(solution)/shard_map/ppermute | solution.py:331
  12.8 14.8 %collective-permute-start.9 = (bf16[2,192,384]{2,1,0:T(8,128)(2,1)S(1)}, bf16[2,192,384]{2,1,0:T(8,128)(2,1)S(1)}, u32[]{:S(2)}, u32[]{:S(2)}) collective-permute-start(bf16[2,192,384]{2,1,0:T(8,128)(2,1)S(1)} %get-tuple-element.75), channel_id=1, source_target_pairs={{0,12},{1,13},{2,14},{3,15},{4,0},{5,1},{6,2},{7,3},{8,4},{9,5},{1... | collective-permute-start | bytes 884744 | tf_op jit(solution)/shard_map/ppermute | solution.py:338
  14.7 5.1 %collective-permute-start.4 = (bf16[2,192,128]{2,1,0:T(8,128)(2,1)S(1)}, bf16[2,192,128]{2,1,0:T(8,128)(2,1)S(1)}, u32[]{:S(2)}, u32[]{:S(2)}) collective-permute-start(bf16[2,192,128]{2,1,0:T(8,128)(2,1)S(1)} %get-tuple-element.69), channel_id=1, source_target_pairs={{2,0},{3,1},{0,2},{1,3},{6,4},{7,5},{4,6},{5,7},{10,8},{11,9},{8,1... | collective-permute-start | bytes 294920 | tf_op jit(solution)/shard_map/ppermute | solution.py:331
  16.0 7.5 %collective-permute-start.5 = (bf16[2,192,128]{2,1,0:T(8,128)(2,1)S(1)}, bf16[2,192,128]{2,1,0:T(8,128)(2,1)S(1)}, u32[]{:S(2)}, u32[]{:S(2)}) collective-permute-start(bf16[2,192,128]{2,1,0:T(8,128)(2,1)S(1)} %get-tuple-element.70), channel_id=1, source_target_pairs={{3,0},{2,1},{1,2},{0,3},{7,4},{6,5},{5,6},{4,7},{11,8},{10,9},{9,1... | collective-permute-start | bytes 294920 | tf_op jit(solution)/shard_map/ppermute | solution.py:331
  19.8 11.0 %collective-permute-start.12 = (bf16[128,768]{1,0:T(8,128)(2,1)S(1)}, bf16[128,768]{1,0:T(8,128)(2,1)S(1)}, u32[]{:S(2)}, u32[]{:S(2)}) collective-permute-start(bf16[128,768]{1,0:T(8,128)(2,1)S(1)} %bitcast.11), channel_id=1, source_target_pairs={{1,0},{0,1},{3,2},{2,3},{5,4},{4,5},{7,6},{6,7},{9,8},{8,9},{11,10... | collective-permute-start | bytes 589832 | tf_op jit(solution)/shard_map/ppermute | solution.py:331
  22.1 8.7 %collective-permute-start.14 = (bf16[128,768]{1,0:T(8,128)(2,1)S(1)}, bf16[128,768]{1,0:T(8,128)(2,1)S(1)}, u32[]{:S(2)}, u32[]{:S(2)}) collective-permute-start(bf16[128,768]{1,0:T(8,128)(2,1)S(1)} %collective-permute-done.13.refs_2_), channel_id=1, source_target_pairs={{1,0},{0,1},{3,2},{2,3},{5,4},{4,5},{7,6},{6,7},{9,8},{8,9},{11,10... | collective-permute-start | bytes 589832 | tf_op jit(solution)/shard_map/ppermute | solution.py:331
  23.6 17.8 %collective-permute-start.6 = (bf16[2,192,384]{2,1,0:T(8,128)(2,1)S(1)}, bf16[2,192,384]{2,1,0:T(8,128)(2,1)S(1)}, u32[]{:S(2)}, u32[]{:S(2)}) collective-permute-start(bf16[2,192,384]{2,1,0:T(8,128)(2,1)S(1)} %get-tuple-element.72), channel_id=1, source_target_pairs={{0,4},{1,5},{2,6},{3,7},{4,8},{5,9},{6,10},{7,11},{8,12},{9,13},{1... | collective-permute-start | bytes 884744 | tf_op jit(solution)/shard_map/ppermute | solution.py:337
  25.0 16.5 %collective-permute-start.7 = (bf16[2,192,384]{2,1,0:T(8,128)(2,1)S(1)}, bf16[2,192,384]{2,1,0:T(8,128)(2,1)S(1)}, u32[]{:S(2)}, u32[]{:S(2)}) collective-permute-start(bf16[2,192,384]{2,1,0:T(8,128)(2,1)S(1)} %get-tuple-element.73), channel_id=1, source_target_pairs={{0,12},{1,13},{2,14},{3,15},{4,0},{5,1},{6,2},{7,3},{8,4},{9,5},{1... | collective-permute-start | bytes 884744 | tf_op jit(solution)/shard_map/ppermute | solution.py:338
  31.3 4.4 %collective-permute-start.18 = (bf16[96,768]{1,0:T(8,128)(2,1)S(1)}, bf16[96,768]{1,0:T(8,128)(2,1)S(1)}, u32[]{:S(2)}, u32[]{:S(2)}) collective-permute-start(bf16[96,768]{1,0:T(8,128)(2,1)S(1)} %get-tuple-element.86.refs_4_), channel_id=1, source_target_pairs={{0,16},{16,0},{1,17},{17,1},{2,18},{18,2},{3,19},{19,3},{4,20},{20... | collective-permute-start | bytes 442376 | tf_op jit(solution)/shard_map/ppermute | solution.py:342
  35.7 13.8 %collective-permute-start.19 = (bf16[48,768]{1,0:T(8,128)(2,1)S(1)}, bf16[48,768]{1,0:T(8,128)(2,1)S(1)}, u32[]{:S(2)}, u32[]{:S(2)}) collective-permute-start(bf16[48,768]{1,0:T(8,128)(2,1)S(1)} %get-tuple-element.100), channel_id=1, source_target_pairs={{4,0},{5,1},{6,2},{7,3},{0,4},{1,5},{2,6},{3,7},{12,8},{13,9},{14,... | collective-permute-start | bytes 221192 | tf_op jit(solution)/shard_map/ppermute | solution.py:331
  36.7 4.7 %collective-permute-start.10 = (f32[8,384]{1,0:T(8,128)S(1)}, f32[8,384]{1,0:T(8,128)S(1)}, u32[]{:S(2)}, u32[]{:S(2)}) collective-permute-start(f32[8,384]{1,0:T(8,128)S(1)} %get-tuple-element.77), channel_id=1, source_target_pairs={{0,4},{1,5},{2,6},{3,7},{4,8},{5,9},{6,10},{7,11},{8,12},{9,13},{1... | collective-permute-start | bytes 36872 | tf_op jit(solution)/shard_map/ppermute | solution.py:337
  37.2 4.2 %collective-permute-start.11 = (f32[8,384]{1,0:T(8,128)S(1)}, f32[8,384]{1,0:T(8,128)S(1)}, u32[]{:S(2)}, u32[]{:S(2)}) collective-permute-start(f32[8,384]{1,0:T(8,128)S(1)} %get-tuple-element.78), channel_id=1, source_target_pairs={{0,12},{1,13},{2,14},{3,15},{4,0},{5,1},{6,2},{7,3},{8,4},{9,5},{1... | collective-permute-start | bytes 36872 | tf_op jit(solution)/shard_map/ppermute | solution.py:338
  44.6 17.4 %copy-start.1 = (bf16[768,768]{1,0:T(8,128)(2,1)S(1)}, bf16[768,768]{1,0:T(8,128)(2,1)}, u32[]{:S(2)}) copy-start(bf16[768,768]{1,0:T(8,128)(2,1)} %refs_4_.1) | copy-start | bytes 3538948
  44.7 11.2 %collective-permute-start.15 = (bf16[4,192,128]{2,1,0:T(8,128)(2,1)S(1)}, bf16[4,192,128]{2,1,0:T(8,128)(2,1)S(1)}, u32[]{:S(2)}, u32[]{:S(2)}) collective-permute-start(bf16[4,192,128]{2,1,0:T(8,128)(2,1)S(1)} %get-tuple-element.90), channel_id=1, source_target_pairs={{1,0},{0,1},{3,2},{2,3},{5,4},{4,5},{7,6},{6,7},{9,8},{8,9},{11,10... | collective-permute-start | bytes 589832 | tf_op jit(solution)/shard_map/ppermute | solution.py:331
  47.8 8.1 %collective-permute-start.16 = (bf16[4,192,128]{2,1,0:T(8,128)(2,1)S(1)}, bf16[4,192,128]{2,1,0:T(8,128)(2,1)S(1)}, u32[]{:S(2)}, u32[]{:S(2)}) collective-permute-start(bf16[4,192,128]{2,1,0:T(8,128)(2,1)S(1)} %get-tuple-element.91), channel_id=1, source_target_pairs={{2,0},{3,1},{0,2},{1,3},{6,4},{7,5},{4,6},{5,7},{10,8},{11,9},{8,1... | collective-permute-start | bytes 589832 | tf_op jit(solution)/shard_map/ppermute | solution.py:331
  48.0 10.6 %collective-permute-start.17 = (bf16[4,192,128]{2,1,0:T(8,128)(2,1)S(1)}, bf16[4,192,128]{2,1,0:T(8,128)(2,1)S(1)}, u32[]{:S(2)}, u32[]{:S(2)}) collective-permute-start(bf16[4,192,128]{2,1,0:T(8,128)(2,1)S(1)} %get-tuple-element.92), channel_id=1, source_target_pairs={{3,0},{2,1},{1,2},{0,3},{7,4},{6,5},{5,6},{4,7},{11,8},{10,9},{9,1... | collective-permute-start | bytes 589832 | tf_op jit(solution)/shard_map/ppermute | solution.py:331
  49.5 4.7 %collective-permute-start.20 = (bf16[48,768]{1,0:T(8,128)(2,1)S(1)}, bf16[48,768]{1,0:T(8,128)(2,1)S(1)}, u32[]{:S(2)}, u32[]{:S(2)}) collective-permute-start(bf16[48,768]{1,0:T(8,128)(2,1)S(1)} %add.2.part_ref), channel_id=1, source_target_pairs={{8,0},{9,1},{10,2},{11,3},{12,4},{13,5},{14,6},{15,7},{0,8},{1,9},... | collective-permute-start | bytes 221192 | tf_op jit(solution)/shard_map/ppermute | solution.py:331
  54.2 4.4 %collective-permute-start.21 = (bf16[48,768]{1,0:T(8,128)(2,1)S(1)}, bf16[48,768]{1,0:T(8,128)(2,1)S(1)}, u32[]{:S(2)}, u32[]{:S(2)}) collective-permute-start(bf16[48,768]{1,0:T(8,128)(2,1)S(1)} %add.3.refs_0_), channel_id=1, source_target_pairs={{4,0},{5,1},{6,2},{7,3},{0,4},{1,5},{2,6},{3,7},{12,8},{13,9},{14,... | collective-permute-start | bytes 221192 | tf_op jit(solution)/shard_map/ppermute | solution.py:331
  58.7 4.6 %collective-permute-start.22 = (bf16[96,768]{1,0:T(8,128)(2,1)S(1)}, bf16[96,768]{1,0:T(8,128)(2,1)S(1)}, u32[]{:S(2)}, u32[]{:S(2)}) collective-permute-start(bf16[96,768]{1,0:T(8,128)(2,1)S(1)} %join.1.refs_0_), channel_id=1, source_target_pairs={{0,2},{1,3},{2,18},{3,19},{4,6},{5,7},{6,22},{7,23},{8,10},{9,11},... | collective-permute-start | bytes 442376 | tf_op jit(solution)/shard_map/ppermute | solution.py:453
  60.0 6.8 %collective-permute-start.23 = (bf16[96,768]{1,0:T(8,128)(2,1)S(1)}, bf16[96,768]{1,0:T(8,128)(2,1)S(1)}, u32[]{:S(2)}, u32[]{:S(2)}) collective-permute-start(bf16[96,768]{1,0:T(8,128)(2,1)S(1)} %join.1.refs_0_), channel_id=1, source_target_pairs={{2,16},{3,17},{6,20},{7,21},{10,24},{11,25},{14,28},{15,29},{16,2}... | collective-permute-start | bytes 442376 | tf_op jit(solution)/shard_map/ppermute | solution.py:453
  66.8 5.2 %collective-permute-start.24 = (bf16[192,768]{1,0:T(8,128)(2,1)S(1)}, bf16[192,768]{1,0:T(8,128)(2,1)S(1)}, u32[]{:S(2)}, u32[]{:S(2)}) collective-permute-start(bf16[192,768]{1,0:T(8,128)(2,1)S(1)} %cross.1.mine_ref), channel_id=1, source_target_pairs={{1,0},{0,1},{3,2},{2,3},{5,4},{4,5},{7,6},{6,7},{9,8},{8,9},{11,10... | collective-permute-start | bytes 884744 | tf_op jit(solution)/shard_map/ppermute | solution.py:331

commit v14 on v9

--- a/solution.py
+++ b/solution.py
@@ -95,11 +95,6 @@
     flipped[1] = dot(weight_ref[...], g_ref[...], NT).astype(bf16)
     for peer, out in enumerate(outs):
         out[...] = flipped[:, place(peer, rows)]
-
-
-def pair_kernel(first_ref, second_ref, out_ref):
-    out_ref[0] = first_ref[...]
-    out_ref[1] = second_ref[...]
 
 
 def relay_kernel(sib_ref, across_ref, out_ref):
@@ -301,10 +296,10 @@
     return lax.rem(lax.axis_index("station") // stride, 2)
 
 
-def weight_kernel(mixed_ref, mine_ref, sib_ref, send_ref, keep_ref, right):
-    for n in range(2):
-        right[place(2 * n, mine_ref.shape[1])] = mine_ref[n]
-        right[place(2 * n + 1, mine_ref.shape[1])] = sib_ref[n]
+def weight_kernel(mixed_ref, *refs):
+    ins, (send_ref, keep_ref, right) = refs[:LAYER], refs[LAYER:]
+    for peer, ref in enumerate(ins):
+        right[place(peer, ref.shape[0])] = ref[...]
     send, keep = halves(lax.rem(lax.axis_index("dp"), 2), send_ref.shape[0])
     send_ref[...] = dot(mixed_ref[send], right[...], NN).astype(bf16)
     keep_ref[...] = dot(mixed_ref[keep], right[...], NN)
@@ -376,7 +371,6 @@
             name="gather", after=after,
         )
 
-    g_across = swap(g, 2)
     mine, *parts = call(
         pack_kernel, [HBM] * 2, [part_shape] * LAYER, (k, v),
         [pltpu.VMEM((2, span, width), bf16), pltpu.VMEM((2, width, span), bf16), dma((2,))],
@@ -384,24 +378,21 @@
     )
     q, *parts = lax.optimization_barrier((q, *parts))
     parts = in_layer(parts)
-    up, down, pair = gather((mine, *parts), (g_across,))
+    up, down, pair = gather((mine, *parts))
     mine, *query_parts, g_copy = call(
         project_kernel, [VMEM] * 3, [part_shape] * LAYER + [flat_shape],
         (q, g, out_weight), [pltpu.VMEM((2, width, span), bf16)], name="project",
     )
-    up, *query_parts = lax.optimization_barrier((up, *query_parts))
+    up, g_later, *query_parts = lax.optimization_barrier((up, g, *query_parts))
     kv_low, kv_high = along(up, down)
-    (g_pair,) = call(
-        pair_kernel, [VMEM] * 2, [shape_of(2, span, width)], (g_copy, g_across), name="pair",
-        after=parts,
-    )
-    g_pairs = g_pair, swap(g_pair, 1)
+    g_across = swap(g_later, 2)
+    g_parts = g_copy, swap(g_later, 1), g_across, swap(g_across, 1)
     bias, dead = call(
         functools.partial(live_kernel, stations), [SMEM] * 2,
         [shape_of(16, LAYER * span, dtype=f32), shape_of(8, HOPS * span, dtype=f32)],
         (partner_ids, partner_count), name="live",
     )
-    up, down, query = gather((mine, *in_layer(query_parts)), (bias, g_pairs[1]))
+    up, down, query = gather((mine, *in_layer(query_parts)), (bias,))
     qg_low, qg_high = along(up, down)
     stats_shape = shape_of(8, HOPS * span, dtype=f32)
     mixed, stats, up, down, probs, window = call(
@@ -415,14 +406,17 @@
         [pltpu.VMEM((BLOCKS * span, LAYER * span), f32)],
         limit=20, name="forward",
     )
+
+    send, part = call(
+        weight_kernel, [VMEM] * (LAYER + 1),
+        [shape_of(rows // 2, width), shape_of(rows // 2, width, dtype=f32)],
+        (mixed, *g_parts), [pltpu.VMEM((LAYER * span, width), bf16)], name="weight",
+    )
+
+    if windows == 2:
+        got = other_window(send)
+        up, down, got = lax.optimization_barrier((up, down, got))
     stats_low, stats_high = along(up, down)
-
-    send, part = call(
-        weight_kernel, [VMEM] * 3,
-        [shape_of(rows // 2, width), shape_of(rows // 2, width, dtype=f32)],
-        (mixed, *g_pairs), [pltpu.VMEM((LAYER * span, width), bf16)], name="weight",
-    )
-
     own_return, to_sib, to_across, own_grad, query_token = call(
         query_grad_kernel, [VMEM] * 5,
         [part_shape, part_shape, shape_of(2, 2, rows, span), shape_of(2, rows, LAYER * span, dtype=f32)]
@@ -456,25 +450,23 @@
     scale = 1.0 / math.sqrt(span * windows * stations)
     if windows == 2:
         count = rows // 4
-        got = other_window(send)
+        across = swap(to_across, 2)
         send, part = call(
             functools.partial(split_kernel, LAYER), [VMEM] * 2,
             [shape_of(count, width), shape_of(count, width, dtype=f32)],
             (part, got), name="split", after=(query_token, qg_low, qg_high, stats_low, stats_high),
         )
 
-        send, to_across = lax.optimization_barrier((send, to_across))
-        across = swap(to_across, 2)
         layer_output, grad_query, output_token = first_return(across)
 
         def add_round(part, got, after=()):
             out = [shape_of(count, width)]
             return call(round_kernel, [VMEM] * 2, out, (part, got), name="add", after=after)[0]
 
-        total = add_round(part, swap(send, LAYER), (key_token,))
+        total = add_round(part, swap(send, LAYER), (key_token, across))
         stride = 2 * LAYER
         while stride < stations:
-            total = add_round(total, swap(total, stride), (across,))
+            total = add_round(total, swap(total, stride))
             stride *= 2
         (total,) = call(
             functools.partial(join_kernel, LAYER, None), [VMEM] * 2, [shape_of(2 * count, width)],
@@ -503,7 +495,7 @@
         start = lax.axis_index("station") % LAYER * rows
         all_grad = jnp.zeros((LAYER * span, width), bf16)
         for peer in range(LAYER):
-            value = g_pairs[peer % 2][peer // 2]
+            value = g_parts[peer]
             spot = lax.axis_index("station") % LAYER ^ peer
             all_grad = lax.dynamic_update_slice_in_dim(all_grad, value, spot * span, 0)
         mine = dot(mixed, all_grad, NN).astype(bf16)

time: 71.1 us -> 72.1 us (1.014)
  starting transfers between devices: 34.2 us -> 37.3 us
  waiting for transfers between devices: 15.9 us -> 13.4 us
    ppermute x17 -> x18, starting transfers between devices: 19 us -> 22.3 us  [swap(): lax.ppermute(value, 'station', [(s ^ stride, s) for s in range(stations)])]
    ppermute x3, waiting for transfers between devices: 2.61 us -> 0.61 us  [along(): lax.ppermute(up, 'station', [(s, (s + LAYER) % stations) for s in range(s...]
    ppermute x1, waiting for transfers between devices: 1.51 us -> 3.01 us  [local(): lax.ppermute(total, axes, second)]
    ppermute x17 -> x18, waiting for transfers between devices: 9.43 us -> 8.24 us  [swap(): lax.ppermute(value, 'station', [(s ^ stride, s) for s in range(stations)])]
    ppermute x3, waiting for transfers between devices: 2.29 us -> 1.33 us  [along(): lax.ppermute(down, 'station', [(s, (s - LAYER) % stations) for s in range...]
    ppermute x3, starting transfers between devices: 6.87 us -> 6.14 us  [along(): lax.ppermute(down, 'station', [(s, (s - LAYER) % stations) for s in range...]
    pallas_call x19 -> x18, Pallas kernels: 16.7 us -> 16.7 us  [call(): pl.pallas_call(kernel, in_specs=ins, out_specs=[VMEM] * len(outs), out_sh...]
    unnamed x15 -> x17, local copies, waits for them, and re-layouts: 3.23 us -> 3.23 us
  transfers between devices with their start and end apart: 26 -> 27, of which waited for: 8 -> 10; matrix products, arithmetic and copies ran while one was open for 0% -> 0% of each run, Pallas kernels for 22% -> 19%
where the time goes in v14:
time: 72.1 us; the launch traced here: 71.5 us
  starting transfers between devices  37.3 us (52%)
  Pallas kernels  16.7 us (23%)
  waiting for transfers between devices  13.4 us (19%)
  local copies, waits for them, and re-layouts  3.23 us (4%)
  between operations  0.84 us (1%)
    ppermute x18, starting transfers between devices, swap(): lax.ppermute(value, 'station', [(s ^ stride, s) for s in range(stations)])  22.3 us
    pallas_call x18, Pallas kernels, call(): pl.pallas_call(kernel, in_specs=ins, out_specs=[VMEM] * len(outs), out_sh...  16.7 us
    ppermute x18, waiting for transfers between devices, swap(): lax.ppermute(value, 'station', [(s ^ stride, s) for s in range(stations)])  8.24 us
    ppermute x3, starting transfers between devices, along(): lax.ppermute(down, 'station', [(s, (s - LAYER) % stations) for s in range...  6.14 us
    ppermute x3, starting transfers between devices, along(): lax.ppermute(up, 'station', [(s, (s + LAYER) % stations) for s in range(s...  3.68 us
    unnamed x17, local copies, waits for them, and re-layouts  3.23 us
    ppermute x1, waiting for transfers between devices, local(): lax.ppermute(total, axes, second)  3.01 us
    ppermute x1, starting transfers between devices, local(): lax.ppermute(total, axes, second)  2.6 us
  transfers between devices with their start and end apart: 27, of which 10 were waited for; matrix products, arithmetic and copies ran while one was open for 0% of the time, Pallas kernels for 19%

profile of v14, /device:TPU:3, one launch (start us, length us, event | category | flops | bytes accessed | tf_op | source)
XLA Modules:
  0.0 71.5 jit_solution(5217553731545656979)
XLA Ops:
  0.7 2.0 %pack.1 = (bf16[2,192,128]{2,1,0:T(8,128)(2,1)}, bf16[2,192,128]{2,1,0:T(8,128)(2,1)}, bf16[2,192,128]{2,1,0:T(8,128)(2,1)}, bf16[2,192,128]{2,1,0:T(8,128)(2,1)}) custom-call(bf16[128,768]{1,0:T(8,128)(2,1)} %bitcast.12, bf16[128,768]{1,0:T(8,128)(2,1)} %bitcast.13), custom_call_target="tpu_custom_call" | custom-call | flops 1 | bytes 1 | tf_op jit(solution)/shard_map/pack/pallas_call | solution.py:50
  2.6 0.7 %collective-permute-start = (bf16[2,192,128]{2,1,0:T(8,128)(2,1)}, bf16[2,192,128]{2,1,0:T(8,128)(2,1)S(1)}, u32[]{:S(2)}, u32[]{:S(2)}) collective-permute-start(bf16[2,192,128]{2,1,0:T(8,128)(2,1)} %get-tuple-element.64), channel_id=1, source_target_pairs={{1,0},{0,1},{3,2},{2,3},{5,4},{4,5},{7,6},{6,7},{9,8},{8,9},{11,10... | collective-permute-start | bytes 294920 | tf_op jit(solution)/shard_map/ppermute | solution.py:346
  3.4 1.7 %collective-permute-start.2 = (bf16[2,192,128]{2,1,0:T(8,128)(2,1)}, bf16[2,192,128]{2,1,0:T(8,128)(2,1)S(1)}, u32[]{:S(2)}, u32[]{:S(2)}) collective-permute-start(bf16[2,192,128]{2,1,0:T(8,128)(2,1)} %get-tuple-element.66), channel_id=1, source_target_pairs={{3,0},{2,1},{1,2},{0,3},{7,4},{6,5},{5,6},{4,7},{11,8},{10,9},{9,1... | collective-permute-start | bytes 294920 | tf_op jit(solution)/shard_map/ppermute | solution.py:346
  5.1 1.3 %copy-done = bf16[768,768]{1,0:T(8,128)(2,1)S(1)} copy-done((bf16[768,768]{1,0:T(8,128)(2,1)S(1)}, bf16[768,768]{1,0:T(8,128)(2,1)}, u32[]{:S(2)}) %copy-start) | copy-done | bytes 1179672
  6.3 0.9 %copy-done.2 = bf16[1,1,128,768]{3,2,1,0:T(8,128)(2,1)S(1)} copy-done((bf16[1,1,128,768]{3,2,1,0:T(8,128)(2,1)S(1)}, bf16[1,1,128,768]{3,2,1,0:T(8,128)(2,1)}, u32[]{:S(2)}) %copy-start.2) | copy-done | bytes 196632
  7.3 0.9 %copy-done.3 = bf16[1,1,128,768]{3,2,1,0:T(8,128)(2,1)S(1)} copy-done((bf16[1,1,128,768]{3,2,1,0:T(8,128)(2,1)S(1)}, bf16[1,1,128,768]{3,2,1,0:T(8,128)(2,1)}, u32[]{:S(2)}) %copy-start.3) | copy-done | bytes 196632
  8.2 0.5 project.1
  8.7 1.5 %collective-permute-done.2.refs_3_ = bf16[2,192,128]{2,1,0:T(8,128)(2,1)S(1)} collective-permute-done((bf16[2,192,128]{2,1,0:T(8,128)(2,1)}, bf16[2,192,128]{2,1,0:T(8,128)(2,1)S(1)}, u32[]{:S(2)}, u32[]{:S(2)}) %collective-permute-start.2) | collective-permute-done | bytes 98336 | tf_op jit(solution)/shard_map/ppermute | solution.py:346
  10.4 1.3 %collective-permute-start.3 = (bf16[2,192,384]{2,1,0:T(8,128)(2,1)S(1)}, bf16[2,192,384]{2,1,0:T(8,128)(2,1)S(1)}, u32[]{:S(2)}, u32[]{:S(2)}) collective-permute-start(bf16[2,192,384]{2,1,0:T(8,128)(2,1)S(1)} %get-tuple-element.73), channel_id=1, source_target_pairs={{0,4},{1,5},{2,6},{3,7},{4,8},{5,9},{6,10},{7,11},{8,12},{9,13},{1... | collective-permute-start | bytes 884744 | tf_op jit(solution)/shard_map/ppermute | solution.py:352
  11.7 0.3 collective-permute-start.9
  12.0 0.8 %collective-permute-start.5 = (bf16[2,192,128]{2,1,0:T(8,128)(2,1)S(1)}, bf16[2,192,128]{2,1,0:T(8,128)(2,1)S(1)}, u32[]{:S(2)}, u32[]{:S(2)}) collective-permute-start(bf16[2,192,128]{2,1,0:T(8,128)(2,1)S(1)} %get-tuple-element.76), channel_id=1, source_target_pairs={{1,0},{0,1},{3,2},{2,3},{5,4},{4,5},{7,6},{6,7},{9,8},{8,9},{11,10... | collective-permute-start | bytes 294920 | tf_op jit(solution)/shard_map/ppermute | solution.py:346
  12.8 1.9 %collective-permute-start.4 = (bf16[2,192,384]{2,1,0:T(8,128)(2,1)S(1)}, bf16[2,192,384]{2,1,0:T(8,128)(2,1)S(1)}, u32[]{:S(2)}, u32[]{:S(2)}) collective-permute-start(bf16[2,192,384]{2,1,0:T(8,128)(2,1)S(1)} %get-tuple-element.74), channel_id=1, source_target_pairs={{0,12},{1,13},{2,14},{3,15},{4,0},{5,1},{6,2},{7,3},{8,4},{9,5},{1... | collective-permute-start | bytes 884744 | tf_op jit(solution)/shard_map/ppermute | solution.py:353
  14.7 1.3 %collective-permute-start.6 = (bf16[2,192,128]{2,1,0:T(8,128)(2,1)S(1)}, bf16[2,192,128]{2,1,0:T(8,128)(2,1)S(1)}, u32[]{:S(2)}, u32[]{:S(2)}) collective-permute-start(bf16[2,192,128]{2,1,0:T(8,128)(2,1)S(1)} %get-tuple-element.77), channel_id=1, source_target_pairs={{2,0},{3,1},{0,2},{1,3},{6,4},{7,5},{4,6},{5,7},{10,8},{11,9},{8,1... | collective-permute-start | bytes 294920 | tf_op jit(solution)/shard_map/ppermute | solution.py:346
  16.0 0.6 collective-permute-start.7
  16.6 3.2 %collective-permute-done.6.refs_2_ = bf16[2,192,128]{2,1,0:T(8,128)(2,1)S(1)} collective-permute-done((bf16[2,192,128]{2,1,0:T(8,128)(2,1)S(1)}, bf16[2,192,128]{2,1,0:T(8,128)(2,1)S(1)}, u32[]{:S(2)}, u32[]{:S(2)}) %collective-permute-start.6) | collective-permute-done | bytes 98336 | tf_op jit(solution)/shard_map/ppermute | solution.py:346
  19.8 2.3 %collective-permute-start.8 = (bf16[128,768]{1,0:T(8,128)(2,1)S(1)}, bf16[128,768]{1,0:T(8,128)(2,1)S(1)}, u32[]{:S(2)}, u32[]{:S(2)}) collective-permute-start(bf16[128,768]{1,0:T(8,128)(2,1)S(1)} %bitcast.11), channel_id=1, source_target_pairs={{1,0},{0,1},{3,2},{2,3},{5,4},{4,5},{7,6},{6,7},{9,8},{8,9},{11,10... | collective-permute-start | bytes 589832 | tf_op jit(solution)/shard_map/ppermute | solution.py:346
  22.2 1.2 %live.1 = (f32[16,512]{1,0:T(8,128)S(1)}, f32[8,384]{1,0:T(8,128)S(1)}) custom-call(s32[16,6]{1,0:T(8,128)S(1)} %copy.12.ids_ref, s32[16]{0:T(128)S(1)} %copy-done.6), custom_call_target="tpu_custom_call" | custom-call | flops 1 | bytes 1 | tf_op jit(solution)/shard_map/live/pallas_call | solution.py:50
  23.5 0.1 gather.3
  23.6 1.3 %collective-permute-start.13 = (bf16[2,192,384]{2,1,0:T(8,128)(2,1)S(1)}, bf16[2,192,384]{2,1,0:T(8,128)(2,1)S(1)}, u32[]{:S(2)}, u32[]{:S(2)}) collective-permute-start(bf16[2,192,384]{2,1,0:T(8,128)(2,1)S(1)} %get-tuple-element.93), channel_id=1, source_target_pairs={{0,4},{1,5},{2,6},{3,7},{4,8},{5,9},{6,10},{7,11},{8,12},{9,13},{1... | collective-permute-start | bytes 884744 | tf_op jit(solution)/shard_map/ppermute | solution.py:352
  25.0 2.0 %collective-permute-start.14 = (bf16[2,192,384]{2,1,0:T(8,128)(2,1)S(1)}, bf16[2,192,384]{2,1,0:T(8,128)(2,1)S(1)}, u32[]{:S(2)}, u32[]{:S(2)}) collective-permute-start(bf16[2,192,384]{2,1,0:T(8,128)(2,1)S(1)} %get-tuple-element.94), channel_id=1, source_target_pairs={{0,12},{1,13},{2,14},{3,15},{4,0},{5,1},{6,2},{7,3},{8,4},{9,5},{1... | collective-permute-start | bytes 884744 | tf_op jit(solution)/shard_map/ppermute | solution.py:353
  26.9 0.7 collective-permute-done.4.high_ref
  27.6 3.3 %forward.1 = (bf16[192,512]{1,0:T(8,128)(2,1)S(1)}, f32[8,512]{1,0:T(8,128)S(1)}, f32[8,384]{1,0:T(8,128)S(1)}, f32[8,384]{1,0:T(8,128)S(1)}, bf16[3,1280,512]{2...) custom-call(bf16[2,192,512]{2,1,0:T(8,128)(2,1)S(1)} %get-tuple-element.67.pair_ref, ...), custom_call_target="tpu_custom_call" | custom-call | flops 1 | bytes 1 | tf_op jit(solution)/shard_map/forward/pallas_call | solution.py:50
  30.9 0.5 weight.1
  31.4 1.3 %collective-permute-start.15 = (bf16[96,768]{1,0:T(8,128)(2,1)S(1)}, bf16[96,768]{1,0:T(8,128)(2,1)S(1)}, u32[]{:S(2)}, u32[]{:S(2)}) collective-permute-start(bf16[96,768]{1,0:T(8,128)(2,1)S(1)} %get-tuple-element.87.refs_5_), channel_id=1, source_target_pairs={{0,16},{16,0},{1,17},{17,1},{2,18},{18,2},{3,19},{19,3},{4,20},{20... | collective-permute-start | bytes 442376 | tf_op jit(solution)/shard_map/ppermute | solution.py:357
  32.7 2.6 %query_grad.1 = (bf16[2,192,128]{2,1,0:T(8,128)(2,1)S(1)}, bf16[2,192,128]{2,1,0:T(8,128)(2,1)S(1)}, bf16[2,2,192,128]{3,2,1,0:T(8,128)(2,1)S(1)}, f32[2,192,512]{2,1,0:T(8,128)S(1)}, f32[8,128]{1,0:T(8,128)S(1)}) custom-call(bf16[2,192,1280]{2,1,0:T(8,128)(2,1)S(1)} %get-tuple-element.81.refs_0_, bf16[3,1280,512]{2,1,0:T(8,128)(2,1)S(1)} %get-tuple-element.82.refs_1_, ...), custom_call_target="tpu_custom_call" | custom-call | flops 1 | bytes 1 | tf_op jit(solution)/shard_map/query_grad/pallas_call | solution.py:50
  35.2 0.3 collective-permute-start.11
  35.6 0.2 collective-permute-done.15.refs_1_
  35.7 1.0 %collective-permute-start.16 = (f32[8,384]{1,0:T(8,128)S(1)}, f32[8,384]{1,0:T(8,128)S(1)}, u32[]{:S(2)}, u32[]{:S(2)}) collective-permute-start(f32[8,384]{1,0:T(8,128)S(1)} %get-tuple-element.97), channel_id=1, source_target_pairs={{0,4},{1,5},{2,6},{3,7},{4,8},{5,9},{6,10},{7,11},{8,12},{9,13},{1... | collective-permute-start | bytes 36872 | tf_op jit(solution)/shard_map/ppermute | solution.py:352
  36.7 2.3 %collective-permute-start.17 = (f32[8,384]{1,0:T(8,128)S(1)}, f32[8,384]{1,0:T(8,128)S(1)}, u32[]{:S(2)}, u32[]{:S(2)}) collective-permute-start(f32[8,384]{1,0:T(8,128)S(1)} %get-tuple-element.98), channel_id=1, source_target_pairs={{0,12},{1,13},{2,14},{3,15},{4,0},{5,1},{6,2},{7,3},{8,4},{9,5},{1... | collective-permute-start | bytes 36872 | tf_op jit(solution)/shard_map/ppermute | solution.py:353
  39.0 0.7 collective-permute-done.14.high_ref.refs_4_
  39.7 0.6 collective-permute-done.16.stats_low.refs_5_
  40.3 1.2 %collective-permute-start.21 = (bf16[48,768]{1,0:T(8,128)(2,1)S(1)}, bf16[48,768]{1,0:T(8,128)(2,1)S(1)}, u32[]{:S(2)}, u32[]{:S(2)}) collective-permute-start(bf16[48,768]{1,0:T(8,128)(2,1)S(1)} %get-tuple-element.111), channel_id=1, source_target_pairs={{4,0},{5,1},{6,2},{7,3},{0,4},{1,5},{2,6},{3,7},{12,8},{13,9},{14,... | collective-permute-start | bytes 221192 | tf_op jit(solution)/shard_map/ppermute | solution.py:346
  41.5 3.2 %key_grad.1 = (bf16[2,192,128]{2,1,0:T(8,128)(2,1)S(1)}, bf16[2,192,128]{2,1,0:T(8,128)(2,1)S(1)}, bf16[2,192,128]{2,1,0:T(8,128)(2,1)S(1)}, bf16[2,192,128]{2,1,0:T(8,128)(2,1)S(1)}, f32[8,128]{1,0:T(8,128)S(1)}) custom-call(bf16[2,192,512]{2,1,0:T(8,128)(2,1)S(1)} %get-tuple-element.67.pair_ref, ...), custom_call_target="tpu_custom_call" | custom-call | flops 1 | bytes 1 | tf_op jit(solution)/shard_map/key_grad/pallas_call | solution.py:50
  44.7 2.4 %collective-permute-start.22 = (bf16[48,768]{1,0:T(8,128)(2,1)S(1)}, bf16[48,768]{1,0:T(8,128)(2,1)S(1)}, u32[]{:S(2)}, u32[]{:S(2)}) collective-permute-start(bf16[48,768]{1,0:T(8,128)(2,1)S(1)} %add.2.part_ref), channel_id=1, source_target_pairs={{8,0},{9,1},{10,2},{11,3},{12,4},{13,5},{14,6},{15,7},{0,8},{1,9},... | collective-permute-start | bytes 221192 | tf_op jit(solution)/shard_map/ppermute | solution.py:346
  47.2 4.9 %collective-permute-start.18 = (bf16[2,192,128]{2,1,0:T(8,128)(2,1)S(1)}, bf16[2,192,128]{2,1,0:T(8,128)(2,1)S(1)}, u32[]{:S(2)}, u32[]{:S(2)}) collective-permute-start(bf16[2,192,128]{2,1,0:T(8,128)(2,1)S(1)} %get-tuple-element.102), channel_id=1, source_target_pairs={{1,0},{0,1},{3,2},{2,3},{5,4},{4,5},{7,6},{6,7},{9,8},{8,9},{11,10... | collective-permute-start | bytes 294920 | tf_op jit(solution)/shard_map/ppermute | solution.py:346
  52.1 0.8 %collective-permute-start.19 = (bf16[2,192,128]{2,1,0:T(8,128)(2,1)S(1)}, bf16[2,192,128]{2,1,0:T(8,128)(2,1)S(1)}, u32[]{:S(2)}, u32[]{:S(2)}) collective-permute-start(bf16[2,192,128]{2,1,0:T(8,128)(2,1)S(1)} %get-tuple-element.103), channel_id=1, source_target_pairs={{2,0},{3,1},{0,2},{1,3},{6,4},{7,5},{4,6},{5,7},{10,8},{11,9},{8,1... | collective-permute-start | bytes 294920 | tf_op jit(solution)/shard_map/ppermute | solution.py:346
  52.8 0.9 %collective-permute-start.20 = (bf16[2,192,128]{2,1,0:T(8,128)(2,1)S(1)}, bf16[2,192,128]{2,1,0:T(8,128)(2,1)S(1)}, u32[]{:S(2)}, u32[]{:S(2)}) collective-permute-start(bf16[2,192,128]{2,1,0:T(8,128)(2,1)S(1)} %get-tuple-element.104), channel_id=1, source_target_pairs={{3,0},{2,1},{1,2},{0,3},{7,4},{6,5},{5,6},{4,7},{11,8},{10,9},{9,1... | collective-permute-start | bytes 294920 | tf_op jit(solution)/shard_map/ppermute | solution.py:346
  53.7 1.4 %collective-permute-start.23 = (bf16[48,768]{1,0:T(8,128)(2,1)S(1)}, bf16[48,768]{1,0:T(8,128)(2,1)S(1)}, u32[]{:S(2)}, u32[]{:S(2)}) collective-permute-start(bf16[48,768]{1,0:T(8,128)(2,1)S(1)} %add.3.refs_0_), channel_id=1, source_target_pairs={{4,0},{5,1},{6,2},{7,3},{0,4},{1,5},{2,6},{3,7},{12,8},{13,9},{14,... | collective-permute-start | bytes 221192 | tf_op jit(solution)/shard_map/ppermute | solution.py:346
  55.1 1.3 %collective-permute-start.12 = (bf16[2,2,192,128]{3,2,1,0:T(8,128)(2,1)S(1)}, bf16[2,2,192,128]{3,2,1,0:T(8,128)(2,1)S(1)}, u32[]{:S(2)}, u32[]{:S(2)}) collective-permute-start(bf16[2,2,192,128]{3,2,1,0:T(8,128)(2,1)S(1)} %relay.1), channel_id=1, source_target_pairs={{1,0},{0,1},{3,2},{2,3},{5,4},{4,5},{7,6},{6,7},{9,8},{8,9},{11,10... | collective-permute-start | bytes 589832 | tf_op jit(solution)/shard_map/ppermute | solution.py:346
  56.5 2.2 %collective-permute-done.20.refs_3_.refs_4_ = bf16[2,192,128]{2,1,0:T(8,128)(2,1)S(1)} collective-permute-done((bf16[2,192,128]{2,1,0:T(8,128)(2,1)S(1)}, bf16[2,192,128]{2,1,0:T(8,128)(2,1)S(1)}, u32[]{:S(2)}, u32[]{:S(2)}) %collective-permute-start.20) | collective-permute-done | bytes 98336 | tf_op jit(solution)/shard_map/ppermute | solution.py:346
  58.7 1.3 %collective-permute-start.25 = (bf16[96,768]{1,0:T(8,128)(2,1)S(1)}, bf16[96,768]{1,0:T(8,128)(2,1)S(1)}, u32[]{:S(2)}, u32[]{:S(2)}) collective-permute-start(bf16[96,768]{1,0:T(8,128)(2,1)S(1)} %join.1.refs_0_), channel_id=1, source_target_pairs={{0,2},{1,3},{2,18},{3,19},{4,6},{5,7},{6,22},{7,23},{8,10},{9,11},... | collective-permute-start | bytes 442376 | tf_op jit(solution)/shard_map/ppermute | solution.py:486
  60.0 2.6 %collective-permute-start.24 = (bf16[96,768]{1,0:T(8,128)(2,1)S(1)}, bf16[96,768]{1,0:T(8,128)(2,1)S(1)}, u32[]{:S(2)}, u32[]{:S(2)}) collective-permute-start(bf16[96,768]{1,0:T(8,128)(2,1)S(1)} %join.1.refs_0_), channel_id=1, source_target_pairs={{2,16},{3,17},{6,20},{7,21},{10,24},{11,25},{14,28},{15,29},{16,2}... | collective-permute-start | bytes 442376 | tf_op jit(solution)/shard_map/ppermute | solution.py:486
  62.6 0.9 %key_output.1 = (bf16[128,768]{1,0:T(8,128)(2,1)}, bf16[128,768]{1,0:T(8,128)(2,1)}, f32[8,128]{1,0:T(8,128)S(1)}) custom-call(bf16[2,192,128]{2,1,0:T(8,128)(2,1)S(1)} %get-tuple-element.101.refs_0_, bf16[2,192,128]{2,1,0:T(8,128)(2,1)S(1)} %collective-permute-done.18.refs_1_.refs_2_, bf16[2,192,128]{2,1,0:T(8,128)(2,1)S(1)} %collective-permute-done.19.refs_2_.refs_3_, ...), custom_call_target="tpu_custom_call" | custom-call | flops 1 | bytes 1 | tf_op jit(solution)/shard_map/key_output/pallas_call | solution.py:50
  63.5 1.1 %output.1 = (bf16[128,768]{1,0:T(8,128)(2,1)}, bf16[128,768]{1,0:T(8,128)(2,1)}, f32[8,128]{1,0:T(8,128)S(1)}) custom-call(bf16[2,192,128]{2,1,0:T(8,128)(2,1)S(1)} %get-tuple-element.88.mine_ref, bf16[2,2,192,128]{3,2,1,0:T(8,128)(2,1)S(1)} %collective-permute-done.11.across_ref.refs_3_, bf16[2,2,192,128]{3,2,1,0:T(8,128)(2,1)S(1)} %collective-permute-done.12.sib_ref, ...), custom_call_target="tpu_custom_call" | custom-call | flops 1 | bytes 1 | tf_op jit(solution)/shard_map/output/pallas_call | solution.py:50
  64.6 3.0 %collective-permute-done.24.refs_1_ = bf16[96,768]{1,0:T(8,128)(2,1)S(1)} collective-permute-done((bf16[96,768]{1,0:T(8,128)(2,1)S(1)}, bf16[96,768]{1,0:T(8,128)(2,1)S(1)}, u32[]{:S(2)}, u32[]{:S(2)}) %collective-permute-start.24) | collective-permute-done | bytes 147488 | tf_op jit(solution)/shard_map/ppermute | solution.py:486
  67.7 1.5 %collective-permute-start.26 = (bf16[192,768]{1,0:T(8,128)(2,1)S(1)}, bf16[192,768]{1,0:T(8,128)(2,1)S(1)}, u32[]{:S(2)}, u32[]{:S(2)}) collective-permute-start(bf16[192,768]{1,0:T(8,128)(2,1)S(1)} %cross.1.mine_ref), channel_id=1, source_target_pairs={{1,0},{0,1},{3,2},{2,3},{5,4},{4,5},{7,6},{6,7},{9,8},{8,9},{11,10... | collective-permute-start | bytes 884744 | tf_op jit(solution)/shard_map/ppermute | solution.py:346
  69.2 1.2 %collective-permute-done.26.got_ref = bf16[192,768]{1,0:T(8,128)(2,1)S(1)} collective-permute-done((bf16[192,768]{1,0:T(8,128)(2,1)S(1)}, bf16[192,768]{1,0:T(8,128)(2,1)S(1)}, u32[]{:S(2)}, u32[]{:S(2)}) %collective-permute-start.26) | collective-permute-done | bytes 294944 | tf_op jit(solution)/shard_map/ppermute | solution.py:346
  70.4 1.1 %last.1 = f32[384,768]{1,0:T(8,128)} custom-call(bf16[192,768]{1,0:T(8,128)(2,1)S(1)} %cross.1.mine_ref, bf16[192,768]{1,0:T(8,128)(2,1)S(1)} %collective-permute-done.26.got_ref), custom_call_target="tpu_custom_call" | custom-call | flops 1 | bytes 1 | tf_op jit(solution)/shard_map/last/pallas_call | solution.py:50
  (41 shorter events, 0.6 us)
Async XLA Ops:
  0.6 11.1 %copy-start.4 = (bf16[1,1,128,768]{3,2,1,0:T(8,128)(2,1)S(1)}, bf16[1,1,128,768]{3,2,1,0:T(8,128)(2,1)}, u32[]{:S(2)}) copy-start(bf16[1,1,128,768]{3,2,1,0:T(8,128)(2,1)} %param.10) | copy-start | bytes 589828
  0.6 21.5 %copy-start.7 = (s32[16,6]{0,1:T(8,128)S(1)}, s32[16,6]{0,1:T(8,128)}, u32[]{:S(2)}) copy-start(s32[16,6]{0,1:T(8,128)} %param.12) | copy-start | bytes 1156
  0.7 21.6 %copy-start.6 = (s32[16]{0:T(128)S(1)}, s32[16]{0:T(128)}, u32[]{:S(2)}) copy-start(s32[16]{0:T(128)} %count_ref.1) | copy-start | bytes 196
  2.6 6.1 %collective-permute-start = (bf16[2,192,128]{2,1,0:T(8,128)(2,1)}, bf16[2,192,128]{2,1,0:T(8,128)(2,1)S(1)}, u32[]{:S(2)}, u32[]{:S(2)}) collective-permute-start(bf16[2,192,128]{2,1,0:T(8,128)(2,1)} %get-tuple-element.64), channel_id=1, source_target_pairs={{1,0},{0,1},{3,2},{2,3},{5,4},{4,5},{7,6},{6,7},{9,8},{8,9},{11,10... | collective-permute-start | bytes 294920 | tf_op jit(solution)/shard_map/ppermute | solution.py:346
  3.4 5.4 %collective-permute-start.1 = (bf16[2,192,128]{2,1,0:T(8,128)(2,1)}, bf16[2,192,128]{2,1,0:T(8,128)(2,1)S(1)}, u32[]{:S(2)}, u32[]{:S(2)}) collective-permute-start(bf16[2,192,128]{2,1,0:T(8,128)(2,1)} %get-tuple-element.65), channel_id=1, source_target_pairs={{2,0},{3,1},{0,2},{1,3},{6,4},{7,5},{4,6},{5,7},{10,8},{11,9},{8,1... | collective-permute-start | bytes 294920 | tf_op jit(solution)/shard_map/ppermute | solution.py:346
  3.4 6.8 %collective-permute-start.2 = (bf16[2,192,128]{2,1,0:T(8,128)(2,1)}, bf16[2,192,128]{2,1,0:T(8,128)(2,1)S(1)}, u32[]{:S(2)}, u32[]{:S(2)}) collective-permute-start(bf16[2,192,128]{2,1,0:T(8,128)(2,1)} %get-tuple-element.66), channel_id=1, source_target_pairs={{3,0},{2,1},{1,2},{0,3},{7,4},{6,5},{5,6},{4,7},{11,8},{10,9},{9,1... | collective-permute-start | bytes 294920 | tf_op jit(solution)/shard_map/ppermute | solution.py:346
  5.1 1.3 %copy-start = (bf16[768,768]{1,0:T(8,128)(2,1)S(1)}, bf16[768,768]{1,0:T(8,128)(2,1)}, u32[]{:S(2)}) copy-start(bf16[768,768]{1,0:T(8,128)(2,1)} %weight_ref.3) | copy-start | bytes 3538948
  6.3 0.9 %copy-start.2 = (bf16[1,1,128,768]{3,2,1,0:T(8,128)(2,1)S(1)}, bf16[1,1,128,768]{3,2,1,0:T(8,128)(2,1)}, u32[]{:S(2)}) copy-start(bf16[1,1,128,768]{3,2,1,0:T(8,128)(2,1)} %param.7) | copy-start | bytes 589828
  7.3 0.9 %copy-start.3 = (bf16[1,1,128,768]{3,2,1,0:T(8,128)(2,1)S(1)}, bf16[1,1,128,768]{3,2,1,0:T(8,128)(2,1)}, u32[]{:S(2)}) copy-start(bf16[1,1,128,768]{3,2,1,0:T(8,128)(2,1)} %param.10) | copy-start | bytes 589828
  8.2 2.0 %copy-start.5 = (bf16[2,192,128]{2,1,0:T(8,128)(2,1)S(1)}, bf16[2,192,128]{2,1,0:T(8,128)(2,1)}, u32[]{:S(2)}) copy-start(bf16[2,192,128]{2,1,0:T(8,128)(2,1)} %get-tuple-element.60.refs_0_) | copy-start | bytes 294916
  10.4 14.6 %collective-permute-start.3 = (bf16[2,192,384]{2,1,0:T(8,128)(2,1)S(1)}, bf16[2,192,384]{2,1,0:T(8,128)(2,1)S(1)}, u32[]{:S(2)}, u32[]{:S(2)}) collective-permute-start(bf16[2,192,384]{2,1,0:T(8,128)(2,1)S(1)} %get-tuple-element.73), channel_id=1, source_target_pairs={{0,4},{1,5},{2,6},{3,7},{4,8},{5,9},{6,10},{7,11},{8,12},{9,13},{1... | collective-permute-start | bytes 884744 | tf_op jit(solution)/shard_map/ppermute | solution.py:352
  11.7 10.4 %collective-permute-start.9 = (bf16[128,768]{1,0:T(8,128)(2,1)S(1)}, bf16[128,768]{1,0:T(8,128)(2,1)S(1)}, u32[]{:S(2)}, u32[]{:S(2)}) collective-permute-start(bf16[128,768]{1,0:T(8,128)(2,1)S(1)} %bitcast.10), channel_id=1, source_target_pairs={{2,0},{3,1},{0,2},{1,3},{6,4},{7,5},{4,6},{5,7},{10,8},{11,9},{8,1... | collective-permute-start | bytes 589832 | tf_op jit(solution)/shard_map/ppermute | solution.py:346
  12.0 4.0 %collective-permute-start.5 = (bf16[2,192,128]{2,1,0:T(8,128)(2,1)S(1)}, bf16[2,192,128]{2,1,0:T(8,128)(2,1)S(1)}, u32[]{:S(2)}, u32[]{:S(2)}) collective-permute-start(bf16[2,192,128]{2,1,0:T(8,128)(2,1)S(1)} %get-tuple-element.76), channel_id=1, source_target_pairs={{1,0},{0,1},{3,2},{2,3},{5,4},{4,5},{7,6},{6,7},{9,8},{8,9},{11,10... | collective-permute-start | bytes 294920 | tf_op jit(solution)/shard_map/ppermute | solution.py:346
  12.8 14.8 %collective-permute-start.4 = (bf16[2,192,384]{2,1,0:T(8,128)(2,1)S(1)}, bf16[2,192,384]{2,1,0:T(8,128)(2,1)S(1)}, u32[]{:S(2)}, u32[]{:S(2)}) collective-permute-start(bf16[2,192,384]{2,1,0:T(8,128)(2,1)S(1)} %get-tuple-element.74), channel_id=1, source_target_pairs={{0,12},{1,13},{2,14},{3,15},{4,0},{5,1},{6,2},{7,3},{8,4},{9,5},{1... | collective-permute-start | bytes 884744 | tf_op jit(solution)/shard_map/ppermute | solution.py:353
  14.7 5.1 %collective-permute-start.6 = (bf16[2,192,128]{2,1,0:T(8,128)(2,1)S(1)}, bf16[2,192,128]{2,1,0:T(8,128)(2,1)S(1)}, u32[]{:S(2)}, u32[]{:S(2)}) collective-permute-start(bf16[2,192,128]{2,1,0:T(8,128)(2,1)S(1)} %get-tuple-element.77), channel_id=1, source_target_pairs={{2,0},{3,1},{0,2},{1,3},{6,4},{7,5},{4,6},{5,7},{10,8},{11,9},{8,1... | collective-permute-start | bytes 294920 | tf_op jit(solution)/shard_map/ppermute | solution.py:346
  16.0 7.5 %collective-permute-start.7 = (bf16[2,192,128]{2,1,0:T(8,128)(2,1)S(1)}, bf16[2,192,128]{2,1,0:T(8,128)(2,1)S(1)}, u32[]{:S(2)}, u32[]{:S(2)}) collective-permute-start(bf16[2,192,128]{2,1,0:T(8,128)(2,1)S(1)} %get-tuple-element.78), channel_id=1, source_target_pairs={{3,0},{2,1},{1,2},{0,3},{7,4},{6,5},{5,6},{4,7},{11,8},{10,9},{9,1... | collective-permute-start | bytes 294920 | tf_op jit(solution)/shard_map/ppermute | solution.py:346
  19.8 11.1 %collective-permute-start.8 = (bf16[128,768]{1,0:T(8,128)(2,1)S(1)}, bf16[128,768]{1,0:T(8,128)(2,1)S(1)}, u32[]{:S(2)}, u32[]{:S(2)}) collective-permute-start(bf16[128,768]{1,0:T(8,128)(2,1)S(1)} %bitcast.11), channel_id=1, source_target_pairs={{1,0},{0,1},{3,2},{2,3},{5,4},{4,5},{7,6},{6,7},{9,8},{8,9},{11,10... | collective-permute-start | bytes 589832 | tf_op jit(solution)/shard_map/ppermute | solution.py:346
  22.1 8.8 %collective-permute-start.10 = (bf16[128,768]{1,0:T(8,128)(2,1)S(1)}, bf16[128,768]{1,0:T(8,128)(2,1)S(1)}, u32[]{:S(2)}, u32[]{:S(2)}) collective-permute-start(bf16[128,768]{1,0:T(8,128)(2,1)S(1)} %collective-permute-done.9.refs_2_), channel_id=1, source_target_pairs={{1,0},{0,1},{3,2},{2,3},{5,4},{4,5},{7,6},{6,7},{9,8},{8,9},{11,10... | collective-permute-start | bytes 589832 | tf_op jit(solution)/shard_map/ppermute | solution.py:346
  23.6 15.4 %collective-permute-start.13 = (bf16[2,192,384]{2,1,0:T(8,128)(2,1)S(1)}, bf16[2,192,384]{2,1,0:T(8,128)(2,1)S(1)}, u32[]{:S(2)}, u32[]{:S(2)}) collective-permute-start(bf16[2,192,384]{2,1,0:T(8,128)(2,1)S(1)} %get-tuple-element.93), channel_id=1, source_target_pairs={{0,4},{1,5},{2,6},{3,7},{4,8},{5,9},{6,10},{7,11},{8,12},{9,13},{1... | collective-permute-start | bytes 884744 | tf_op jit(solution)/shard_map/ppermute | solution.py:352
  25.0 14.7 %collective-permute-start.14 = (bf16[2,192,384]{2,1,0:T(8,128)(2,1)S(1)}, bf16[2,192,384]{2,1,0:T(8,128)(2,1)S(1)}, u32[]{:S(2)}, u32[]{:S(2)}) collective-permute-start(bf16[2,192,384]{2,1,0:T(8,128)(2,1)S(1)} %get-tuple-element.94), channel_id=1, source_target_pairs={{0,12},{1,13},{2,14},{3,15},{4,0},{5,1},{6,2},{7,3},{8,4},{9,5},{1... | collective-permute-start | bytes 884744 | tf_op jit(solution)/shard_map/ppermute | solution.py:353
  31.4 4.4 %collective-permute-start.15 = (bf16[96,768]{1,0:T(8,128)(2,1)S(1)}, bf16[96,768]{1,0:T(8,128)(2,1)S(1)}, u32[]{:S(2)}, u32[]{:S(2)}) collective-permute-start(bf16[96,768]{1,0:T(8,128)(2,1)S(1)} %get-tuple-element.87.refs_5_), channel_id=1, source_target_pairs={{0,16},{16,0},{1,17},{17,1},{2,18},{18,2},{3,19},{19,3},{4,20},{20... | collective-permute-start | bytes 442376 | tf_op jit(solution)/shard_map/ppermute | solution.py:357
  35.2 9.5 %collective-permute-start.11 = (bf16[2,2,192,128]{3,2,1,0:T(8,128)(2,1)S(1)}, bf16[2,2,192,128]{3,2,1,0:T(8,128)(2,1)S(1)}, u32[]{:S(2)}, u32[]{:S(2)}) collective-permute-start(bf16[2,2,192,128]{3,2,1,0:T(8,128)(2,1)S(1)} %get-tuple-element.89), channel_id=1, source_target_pairs={{2,0},{3,1},{0,2},{1,3},{6,4},{7,5},{4,6},{5,7},{10,8},{11,9},{8,1... | collective-permute-start | bytes 589832 | tf_op jit(solution)/shard_map/ppermute | solution.py:346
  35.7 4.5 %collective-permute-start.16 = (f32[8,384]{1,0:T(8,128)S(1)}, f32[8,384]{1,0:T(8,128)S(1)}, u32[]{:S(2)}, u32[]{:S(2)}) collective-permute-start(f32[8,384]{1,0:T(8,128)S(1)} %get-tuple-element.97), channel_id=1, source_target_pairs={{0,4},{1,5},{2,6},{3,7},{4,8},{5,9},{6,10},{7,11},{8,12},{9,13},{1... | collective-permute-start | bytes 36872 | tf_op jit(solution)/shard_map/ppermute | solution.py:352
  36.7 3.6 %collective-permute-start.17 = (f32[8,384]{1,0:T(8,128)S(1)}, f32[8,384]{1,0:T(8,128)S(1)}, u32[]{:S(2)}, u32[]{:S(2)}) collective-permute-start(f32[8,384]{1,0:T(8,128)S(1)} %get-tuple-element.98), channel_id=1, source_target_pairs={{0,12},{1,13},{2,14},{3,15},{4,0},{5,1},{6,2},{7,3},{8,4},{9,5},{1... | collective-permute-start | bytes 36872 | tf_op jit(solution)/shard_map/ppermute | solution.py:353
  40.3 4.4 %collective-permute-start.21 = (bf16[48,768]{1,0:T(8,128)(2,1)S(1)}, bf16[48,768]{1,0:T(8,128)(2,1)S(1)}, u32[]{:S(2)}, u32[]{:S(2)}) collective-permute-start(bf16[48,768]{1,0:T(8,128)(2,1)S(1)} %get-tuple-element.111), channel_id=1, source_target_pairs={{4,0},{5,1},{6,2},{7,3},{0,4},{1,5},{2,6},{3,7},{12,8},{13,9},{14,... | collective-permute-start | bytes 221192 | tf_op jit(solution)/shard_map/ppermute | solution.py:346
  44.7 18.8 %copy-start.1 = (bf16[768,768]{1,0:T(8,128)(2,1)S(1)}, bf16[768,768]{1,0:T(8,128)(2,1)}, u32[]{:S(2)}) copy-start(bf16[768,768]{1,0:T(8,128)(2,1)} %weight_ref.3) | copy-start | bytes 3538948
  44.7 9.0 %collective-permute-start.22 = (bf16[48,768]{1,0:T(8,128)(2,1)S(1)}, bf16[48,768]{1,0:T(8,128)(2,1)S(1)}, u32[]{:S(2)}, u32[]{:S(2)}) collective-permute-start(bf16[48,768]{1,0:T(8,128)(2,1)S(1)} %add.2.part_ref), channel_id=1, source_target_pairs={{8,0},{9,1},{10,2},{11,3},{12,4},{13,5},{14,6},{15,7},{0,8},{1,9},... | collective-permute-start | bytes 221192 | tf_op jit(solution)/shard_map/ppermute | solution.py:346
  47.2 9.2 %collective-permute-start.18 = (bf16[2,192,128]{2,1,0:T(8,128)(2,1)S(1)}, bf16[2,192,128]{2,1,0:T(8,128)(2,1)S(1)}, u32[]{:S(2)}, u32[]{:S(2)}) collective-permute-start(bf16[2,192,128]{2,1,0:T(8,128)(2,1)S(1)} %get-tuple-element.102), channel_id=1, source_target_pairs={{1,0},{0,1},{3,2},{2,3},{5,4},{4,5},{7,6},{6,7},{9,8},{8,9},{11,10... | collective-permute-start | bytes 294920 | tf_op jit(solution)/shard_map/ppermute | solution.py:346
  52.1 4.4 %collective-permute-start.19 = (bf16[2,192,128]{2,1,0:T(8,128)(2,1)S(1)}, bf16[2,192,128]{2,1,0:T(8,128)(2,1)S(1)}, u32[]{:S(2)}, u32[]{:S(2)}) collective-permute-start(bf16[2,192,128]{2,1,0:T(8,128)(2,1)S(1)} %get-tuple-element.103), channel_id=1, source_target_pairs={{2,0},{3,1},{0,2},{1,3},{6,4},{7,5},{4,6},{5,7},{10,8},{11,9},{8,1... | collective-permute-start | bytes 294920 | tf_op jit(solution)/shard_map/ppermute | solution.py:346
  52.8 5.9 %collective-permute-start.20 = (bf16[2,192,128]{2,1,0:T(8,128)(2,1)S(1)}, bf16[2,192,128]{2,1,0:T(8,128)(2,1)S(1)}, u32[]{:S(2)}, u32[]{:S(2)}) collective-permute-start(bf16[2,192,128]{2,1,0:T(8,128)(2,1)S(1)} %get-tuple-element.104), channel_id=1, source_target_pairs={{3,0},{2,1},{1,2},{0,3},{7,4},{6,5},{5,6},{4,7},{11,8},{10,9},{9,1... | collective-permute-start | bytes 294920 | tf_op jit(solution)/shard_map/ppermute | solution.py:346
  53.7 5.0 %collective-permute-start.23 = (bf16[48,768]{1,0:T(8,128)(2,1)S(1)}, bf16[48,768]{1,0:T(8,128)(2,1)S(1)}, u32[]{:S(2)}, u32[]{:S(2)}) collective-permute-start(bf16[48,768]{1,0:T(8,128)(2,1)S(1)} %add.3.refs_0_), channel_id=1, source_target_pairs={{4,0},{5,1},{6,2},{7,3},{0,4},{1,5},{2,6},{3,7},{12,8},{13,9},{14,... | collective-permute-start | bytes 221192 | tf_op jit(solution)/shard_map/ppermute | solution.py:346
  55.1 8.4 %collective-permute-start.12 = (bf16[2,2,192,128]{3,2,1,0:T(8,128)(2,1)S(1)}, bf16[2,2,192,128]{3,2,1,0:T(8,128)(2,1)S(1)}, u32[]{:S(2)}, u32[]{:S(2)}) collective-permute-start(bf16[2,2,192,128]{3,2,1,0:T(8,128)(2,1)S(1)} %relay.1), channel_id=1, source_target_pairs={{1,0},{0,1},{3,2},{2,3},{5,4},{4,5},{7,6},{6,7},{9,8},{8,9},{11,10... | collective-permute-start | bytes 589832 | tf_op jit(solution)/shard_map/ppermute | solution.py:346
  58.7 5.9 %collective-permute-start.25 = (bf16[96,768]{1,0:T(8,128)(2,1)S(1)}, bf16[96,768]{1,0:T(8,128)(2,1)S(1)}, u32[]{:S(2)}, u32[]{:S(2)}) collective-permute-start(bf16[96,768]{1,0:T(8,128)(2,1)S(1)} %join.1.refs_0_), channel_id=1, source_target_pairs={{0,2},{1,3},{2,18},{3,19},{4,6},{5,7},{6,22},{7,23},{8,10},{9,11},... | collective-permute-start | bytes 442376 | tf_op jit(solution)/shard_map/ppermute | solution.py:486
  60.0 7.6 %collective-permute-start.24 = (bf16[96,768]{1,0:T(8,128)(2,1)S(1)}, bf16[96,768]{1,0:T(8,128)(2,1)S(1)}, u32[]{:S(2)}, u32[]{:S(2)}) collective-permute-start(bf16[96,768]{1,0:T(8,128)(2,1)S(1)} %join.1.refs_0_), channel_id=1, source_target_pairs={{2,16},{3,17},{6,20},{7,21},{10,24},{11,25},{14,28},{15,29},{16,2}... | collective-permute-start | bytes 442376 | tf_op jit(solution)/shard_map/ppermute | solution.py:486
  67.7 2.7 %collective-permute-start.26 = (bf16[192,768]{1,0:T(8,128)(2,1)S(1)}, bf16[192,768]{1,0:T(8,128)(2,1)S(1)}, u32[]{:S(2)}, u32[]{:S(2)}) collective-permute-start(bf16[192,768]{1,0:T(8,128)(2,1)S(1)} %cross.1.mine_ref), channel_id=1, source_target_pairs={{1,0},{0,1},{3,2},{2,3},{5,4},{4,5},{7,6},{6,7},{9,8},{8,9},{11,10... | collective-permute-start | bytes 884744 | tf_op jit(solution)/shard_map/ppermute | solution.py:346

commit v15 on v12

--- a/solution.py
+++ b/solution.py
@@ -226,32 +226,38 @@
 def key_grad_kernel(
     pair_ref, low_ref, high_ref, stats_low, stats_high, dead_ref, own_ref, mixed_ref, dq_ref, *refs
 ):
-    outs, (token_ref, flipped) = refs[:LAYER], refs[LAYER:]
+    outs, (token_ref, flipped, scores, backs, probs, grads) = refs[:LAYER], refs[LAYER:]
     rows = pair_ref.shape[1]
     span = pair_ref.shape[2] // LAYER
     head_width = rows // LOCAL
-    for head in range(LOCAL):
+    pairs = [(head, i) for head in range(LOCAL) for i in range(LAYER)]
+
+    def outside(low, high, i):
+        sides = [low[:, i * span :]] if i < HOPS else []
+        return jnp.concatenate(sides + ([high[:, : i * span]] if i else []), 1)
+
+    def both(part, head, i):
         at = block(head, head_width)
-        log_row = slice(head, head + 1)
-        delta_row = slice(LOCAL + head, LOCAL + head + 1)
-        for i in range(LAYER):
-            own = block(i, span)
-
-            def outside(low, high):
-                sides = [low[:, i * span :]] if i < HOPS else []
-                return jnp.concatenate(sides + ([high[:, : i * span]] if i else []), 1)
-
-            query = outside(low_ref[0, at], high_ref[0, at])
-            grad = outside(low_ref[1, at], high_ref[1, at])
-            log_sum = outside(stats_low[log_row], stats_high[log_row]) + dead_ref[i : i + 1]
-            delta = outside(stats_low[delta_row], stats_high[delta_row])
-            prob = jnp.exp(dot(pair_ref[0, at, own], query, TN) - log_sum)
-            back = dot(pair_ref[1, at, own], grad, TN)
-            grads = (prob * (back - delta)).astype(bf16)
-            keys = own_ref[0, at, own] + dot(query, grads, NT)
-            values = own_ref[1, at, own] + dot(grad, prob.astype(bf16), NT)
-            flipped[0, at, own] = keys.astype(bf16)
-            flipped[1, at, own] = values.astype(bf16)
+        return outside(low_ref[part, at], high_ref[part, at], i)
+
+    for n, (head, i) in enumerate(pairs):
+        at, own = block(head, head_width), block(i, span)
+        scores[n] = dot(pair_ref[0, at, own], both(0, head, i), TN)
+        backs[n] = dot(pair_ref[1, at, own], both(1, head, i), TN)
+    for n, (head, i) in enumerate(pairs):
+        row = slice(head, head + 1)
+        log_sum = outside(stats_low[row], stats_high[row], i) + dead_ref[i : i + 1]
+        row = slice(LOCAL + head, LOCAL + head + 1)
+        delta = outside(stats_low[row], stats_high[row], i)
+        prob = jnp.exp(scores[n] - log_sum)
+        probs[n] = prob.astype(bf16)
+        grads[n] = (prob * (backs[n] - delta)).astype(bf16)
+    for n, (head, i) in enumerate(pairs):
+        at, own = block(head, head_width), block(i, span)
+        keys = own_ref[0, at, own] + dot(both(0, head, i), grads[n], NT)
+        values = own_ref[1, at, own] + dot(both(1, head, i), probs[n], NT)
+        flipped[0, at, own] = keys.astype(bf16)
+        flipped[1, at, own] = values.astype(bf16)
     for peer, out in enumerate(outs):
         at = place(peer, span)
         out[0] = mixed_ref[:, at]
@@ -300,13 +306,20 @@
     out_ref[...] = (part_ref[...].astype(f32) + got_ref[...].astype(f32)).astype(bf16)
 
 
-def join_kernel(stride, scale, mine_ref, got_ref, out_ref):
+def join_kernel(stride, mine_ref, got_ref, out_ref):
     other, here = halves(bit_of(stride), mine_ref.shape[0])
-    for at, ref in ((here, mine_ref), (other, got_ref)):
-        value = ref[...]
-        if scale is not None:
-            value = value.astype(f32) * scale
-        out_ref[at] = value
+    out_ref[here] = mine_ref[...]
+    out_ref[other] = got_ref[...]
+
+
+def write_kernel(own, scale, value_ref, *refs):
+    out_ref, wide, sem = refs[-3:]
+    half = value_ref.shape[0]
+    other, here = halves(bit_of(1), half)
+    wide[...] = value_ref[...].astype(f32) * scale
+    copy = pltpu.make_async_copy(wide, out_ref.at[here if own else other], sem)
+    copy.start()
+    copy.wait()
 
 
 def cross_kernel(mine_ref, first_ref, second_ref, out_ref):
@@ -408,7 +421,14 @@
     mine, *parts, key_token = call(
         key_grad_kernel, [VMEM] * 9, [shape_of(4, rows, span)] * LAYER + [TOKEN],
         (pair, qg_low, qg_high, stats_low, stats_high, dead, own_grad, mixed, dq),
-        [pltpu.VMEM((2, rows, LAYER * span), bf16)], limit=20, name="key_grad",
+        [
+            pltpu.VMEM((2, rows, LAYER * span), bf16),
+            pltpu.VMEM((HEADS, span, HOPS * span), f32),
+            pltpu.VMEM((HEADS, span, HOPS * span), f32),
+            pltpu.VMEM((HEADS, span, HOPS * span), bf16),
+            pltpu.VMEM((HEADS, span, HOPS * span), bf16),
+        ],
+        limit=24, name="key_grad",
     )
     parts = in_layer(parts)
     layer_output, grad_query, grad_key, grad_value, output_token = call(
@@ -436,7 +456,7 @@
             total = add_round(total, swap(total, stride))
             stride *= 2
         (total,) = call(
-            functools.partial(join_kernel, LAYER, None), [VMEM] * 2, [shape_of(2 * count, width)],
+            functools.partial(join_kernel, LAYER), [VMEM] * 2, [shape_of(2 * count, width)],
             (total, swap(total, LAYER)), name="join", after=parts,
         )
         first, second = [], []
@@ -453,10 +473,20 @@
             (total, lax.ppermute(total, axes, first), lax.ppermute(total, axes, second)),
             name="cross", after=(output_token,),
         )
-        (grad_weight,) = call(
-            functools.partial(join_kernel, 1, scale), [VMEM] * 2,
-            [shape_of(8 * count, width, dtype=f32)], (total, swap(total, 1)), name="last",
-        )
+        grad_weight = ()
+        for own, value in ((True, total), (False, swap(total, 1))):
+            grad_weight = (pl.pallas_call(
+                functools.partial(write_kernel, own, scale),
+                in_specs=[VMEM] + [ANY] * len(grad_weight),
+                out_specs=ANY,
+                out_shape=shape_of(8 * count, width, dtype=f32),
+                scratch_shapes=[pltpu.VMEM((4 * count, width), f32), dma],
+                input_output_aliases={1: 0} if grad_weight else {},
+                compiler_params=pltpu.CompilerParams(vmem_limit_bytes=8 * MIB),
+                cost_estimate=pl.CostEstimate(flops=1, bytes_accessed=1, transcendentals=0),
+                name="write",
+            )(value, *grad_weight),)
+        (grad_weight,) = grad_weight
     else:
         start = lax.axis_index("station") % LAYER * rows
         all_grad = jnp.zeros((LAYER * span, width), bf16)

time: 71.2 us -> 69.6 us (0.978)
  waiting for transfers between devices: 18.1 us -> 17.2 us
    pallas_call x16 -> x15, Pallas kernels: 15.7 us -> 13.3 us  [call(): pl.pallas_call(kernel, in_specs=ins, out_specs=[VMEM] * len(outs), out_sh...]
    pallas_call x0 -> x2, Pallas kernels: none -> 1.72 us  [local(): pl.pallas_call(functools.partial(write_kernel, own, scale), in_specs=[VME...]
    ppermute x16, waiting for transfers between devices: 13 us -> 12.1 us  [swap(): lax.ppermute(value, 'station', [(s ^ stride, s) for s in range(stations)])]
where the time goes in v15:
time: 69.6 us; the launch traced here: 69.4 us
  starting transfers between devices  33.1 us (48%)
  waiting for transfers between devices  17.2 us (25%)
  Pallas kernels  15 us (22%)
  local copies, waits for them, and re-layouts  3.23 us (5%)
  between operations  0.85 us (1%)
    ppermute x16, starting transfers between devices, swap(): lax.ppermute(value, 'station', [(s ^ stride, s) for s in range(stations)])  18.4 us
    pallas_call x15, Pallas kernels, call(): pl.pallas_call(kernel, in_specs=ins, out_specs=[VMEM] * len(outs), out_sh...  13.3 us
    ppermute x16, waiting for transfers between devices, swap(): lax.ppermute(value, 'station', [(s ^ stride, s) for s in range(stations)])  12.1 us
    ppermute x3, starting transfers between devices, along(): lax.ppermute(down, 'station', [(s, (s - LAYER) % stations) for s in range...  6.84 us
    unnamed x17, local copies, waits for them, and re-layouts  3.23 us
    ppermute x3, starting transfers between devices, along(): lax.ppermute(up, 'station', [(s, (s + LAYER) % stations) for s in range(s...  2.98 us
    ppermute x1, starting transfers between devices, local(): lax.ppermute(total, axes, second)  2.86 us
    ppermute x1, waiting for transfers between devices, local(): lax.ppermute(total, axes, second)  2.71 us
  transfers between devices with their start and end apart: 25, of which 10 were waited for; matrix products, arithmetic and copies ran while one was open for 0% of the time, Pallas kernels for 17%

profile of v15, /device:TPU:3, one launch (start us, length us, event | category | flops | bytes accessed | tf_op | source)
XLA Modules:
  0.0 69.4 jit_solution(9560494715105101839)
XLA Ops:
  0.7 2.0 %pack.1 = (bf16[2,192,128]{2,1,0:T(8,128)(2,1)}, bf16[2,192,128]{2,1,0:T(8,128)(2,1)}, bf16[2,192,128]{2,1,0:T(8,128)(2,1)}, bf16[2,192,128]{2,1,0:T(8,128)(2,1)}) custom-call(bf16[128,768]{1,0:T(8,128)(2,1)} %bitcast.12, bf16[128,768]{1,0:T(8,128)(2,1)} %bitcast.13), custom_call_target="tpu_custom_call" | custom-call | flops 1 | bytes 1 | tf_op jit(solution)/shard_map/pack/pallas_call | solution.py:50
  2.6 0.7 %collective-permute-start = (bf16[2,192,128]{2,1,0:T(8,128)(2,1)}, bf16[2,192,128]{2,1,0:T(8,128)(2,1)S(1)}, u32[]{:S(2)}, u32[]{:S(2)}) collective-permute-start(bf16[2,192,128]{2,1,0:T(8,128)(2,1)} %get-tuple-element.58), channel_id=1, source_target_pairs={{1,0},{0,1},{3,2},{2,3},{5,4},{4,5},{7,6},{6,7},{9,8},{8,9},{11,10... | collective-permute-start | bytes 294920 | tf_op jit(solution)/shard_map/ppermute | solution.py:344
  3.4 1.7 %collective-permute-start.2 = (bf16[2,192,128]{2,1,0:T(8,128)(2,1)}, bf16[2,192,128]{2,1,0:T(8,128)(2,1)S(1)}, u32[]{:S(2)}, u32[]{:S(2)}) collective-permute-start(bf16[2,192,128]{2,1,0:T(8,128)(2,1)} %get-tuple-element.60), channel_id=1, source_target_pairs={{3,0},{2,1},{1,2},{0,3},{7,4},{6,5},{5,6},{4,7},{11,8},{10,9},{9,1... | collective-permute-start | bytes 294920 | tf_op jit(solution)/shard_map/ppermute | solution.py:344
  5.1 1.3 %copy-done = bf16[768,768]{1,0:T(8,128)(2,1)S(1)} copy-done((bf16[768,768]{1,0:T(8,128)(2,1)S(1)}, bf16[768,768]{1,0:T(8,128)(2,1)}, u32[]{:S(2)}) %copy-start) | copy-done | bytes 1179672
  6.3 0.9 %copy-done.2 = bf16[1,1,128,768]{3,2,1,0:T(8,128)(2,1)S(1)} copy-done((bf16[1,1,128,768]{3,2,1,0:T(8,128)(2,1)S(1)}, bf16[1,1,128,768]{3,2,1,0:T(8,128)(2,1)}, u32[]{:S(2)}) %copy-start.2) | copy-done | bytes 196632
  7.3 0.9 %copy-done.3 = bf16[1,1,128,768]{3,2,1,0:T(8,128)(2,1)S(1)} copy-done((bf16[1,1,128,768]{3,2,1,0:T(8,128)(2,1)S(1)}, bf16[1,1,128,768]{3,2,1,0:T(8,128)(2,1)}, u32[]{:S(2)}) %copy-start.3) | copy-done | bytes 196632
  8.2 0.5 project.1
  8.7 1.5 %collective-permute-done.2.refs_3_ = bf16[2,192,128]{2,1,0:T(8,128)(2,1)S(1)} collective-permute-done((bf16[2,192,128]{2,1,0:T(8,128)(2,1)}, bf16[2,192,128]{2,1,0:T(8,128)(2,1)S(1)}, u32[]{:S(2)}, u32[]{:S(2)}) %collective-permute-start.2) | collective-permute-done | bytes 98336 | tf_op jit(solution)/shard_map/ppermute | solution.py:344
  10.2 0.1 gather.2
  10.4 1.3 %collective-permute-start.8 = (bf16[2,192,384]{2,1,0:T(8,128)(2,1)S(1)}, bf16[2,192,384]{2,1,0:T(8,128)(2,1)S(1)}, u32[]{:S(2)}, u32[]{:S(2)}) collective-permute-start(bf16[2,192,384]{2,1,0:T(8,128)(2,1)S(1)} %get-tuple-element.74), channel_id=1, source_target_pairs={{0,4},{1,5},{2,6},{3,7},{4,8},{5,9},{6,10},{7,11},{8,12},{9,13},{1... | collective-permute-start | bytes 884744 | tf_op jit(solution)/shard_map/ppermute | solution.py:350
  11.7 0.3 collective-permute-start.13
  12.0 0.8 %collective-permute-start.3 = (bf16[2,192,128]{2,1,0:T(8,128)(2,1)S(1)}, bf16[2,192,128]{2,1,0:T(8,128)(2,1)S(1)}, u32[]{:S(2)}, u32[]{:S(2)}) collective-permute-start(bf16[2,192,128]{2,1,0:T(8,128)(2,1)S(1)} %get-tuple-element.68), channel_id=1, source_target_pairs={{1,0},{0,1},{3,2},{2,3},{5,4},{4,5},{7,6},{6,7},{9,8},{8,9},{11,10... | collective-permute-start | bytes 294920 | tf_op jit(solution)/shard_map/ppermute | solution.py:344
  12.8 1.9 %collective-permute-start.9 = (bf16[2,192,384]{2,1,0:T(8,128)(2,1)S(1)}, bf16[2,192,384]{2,1,0:T(8,128)(2,1)S(1)}, u32[]{:S(2)}, u32[]{:S(2)}) collective-permute-start(bf16[2,192,384]{2,1,0:T(8,128)(2,1)S(1)} %get-tuple-element.75), channel_id=1, source_target_pairs={{0,12},{1,13},{2,14},{3,15},{4,0},{5,1},{6,2},{7,3},{8,4},{9,5},{1... | collective-permute-start | bytes 884744 | tf_op jit(solution)/shard_map/ppermute | solution.py:351
  14.7 1.3 %collective-permute-start.4 = (bf16[2,192,128]{2,1,0:T(8,128)(2,1)S(1)}, bf16[2,192,128]{2,1,0:T(8,128)(2,1)S(1)}, u32[]{:S(2)}, u32[]{:S(2)}) collective-permute-start(bf16[2,192,128]{2,1,0:T(8,128)(2,1)S(1)} %get-tuple-element.69), channel_id=1, source_target_pairs={{2,0},{3,1},{0,2},{1,3},{6,4},{7,5},{4,6},{5,7},{10,8},{11,9},{8,1... | collective-permute-start | bytes 294920 | tf_op jit(solution)/shard_map/ppermute | solution.py:344
  16.0 0.6 collective-permute-start.5
  16.6 3.2 %collective-permute-done.4.refs_2_ = bf16[2,192,128]{2,1,0:T(8,128)(2,1)S(1)} collective-permute-done((bf16[2,192,128]{2,1,0:T(8,128)(2,1)S(1)}, bf16[2,192,128]{2,1,0:T(8,128)(2,1)S(1)}, u32[]{:S(2)}, u32[]{:S(2)}) %collective-permute-start.4) | collective-permute-done | bytes 98336 | tf_op jit(solution)/shard_map/ppermute | solution.py:344
  19.8 2.3 %collective-permute-start.12 = (bf16[128,768]{1,0:T(8,128)(2,1)S(1)}, bf16[128,768]{1,0:T(8,128)(2,1)S(1)}, u32[]{:S(2)}, u32[]{:S(2)}) collective-permute-start(bf16[128,768]{1,0:T(8,128)(2,1)S(1)} %bitcast.11), channel_id=1, source_target_pairs={{1,0},{0,1},{3,2},{2,3},{5,4},{4,5},{7,6},{6,7},{9,8},{8,9},{11,10... | collective-permute-start | bytes 589832 | tf_op jit(solution)/shard_map/ppermute | solution.py:344
  22.1 0.1 copy.13.ids_ref
  22.2 1.2 %live.1 = (f32[16,512]{1,0:T(8,128)S(1)}, f32[8,384]{1,0:T(8,128)S(1)}) custom-call(s32[16,6]{1,0:T(8,128)S(1)} %copy.13.ids_ref, s32[16]{0:T(128)S(1)} %copy-done.6), custom_call_target="tpu_custom_call" | custom-call | flops 1 | bytes 1 | tf_op jit(solution)/shard_map/live/pallas_call | solution.py:50
  23.5 0.1 gather.3
  23.6 1.3 %collective-permute-start.6 = (bf16[2,192,384]{2,1,0:T(8,128)(2,1)S(1)}, bf16[2,192,384]{2,1,0:T(8,128)(2,1)S(1)}, u32[]{:S(2)}, u32[]{:S(2)}) collective-permute-start(bf16[2,192,384]{2,1,0:T(8,128)(2,1)S(1)} %get-tuple-element.72), channel_id=1, source_target_pairs={{0,4},{1,5},{2,6},{3,7},{4,8},{5,9},{6,10},{7,11},{8,12},{9,13},{1... | collective-permute-start | bytes 884744 | tf_op jit(solution)/shard_map/ppermute | solution.py:350
  25.0 2.0 %collective-permute-start.7 = (bf16[2,192,384]{2,1,0:T(8,128)(2,1)S(1)}, bf16[2,192,384]{2,1,0:T(8,128)(2,1)S(1)}, u32[]{:S(2)}, u32[]{:S(2)}) collective-permute-start(bf16[2,192,384]{2,1,0:T(8,128)(2,1)S(1)} %get-tuple-element.73), channel_id=1, source_target_pairs={{0,12},{1,13},{2,14},{3,15},{4,0},{5,1},{6,2},{7,3},{8,4},{9,5},{1... | collective-permute-start | bytes 884744 | tf_op jit(solution)/shard_map/ppermute | solution.py:351
  26.9 0.7 collective-permute-done.9.high_ref
  27.6 3.2 %forward.1 = (bf16[192,512]{1,0:T(8,128)(2,1)S(1)}, f32[8,512]{1,0:T(8,128)S(1)}, f32[8,384]{1,0:T(8,128)S(1)}, f32[8,384]{1,0:T(8,128)S(1)}, bf16[3,1280,512]{2...) custom-call(bf16[2,192,512]{2,1,0:T(8,128)(2,1)S(1)} %get-tuple-element.61.pair_ref, ...), custom_call_target="tpu_custom_call" | custom-call | flops 1 | bytes 1 | tf_op jit(solution)/shard_map/forward/pallas_call | solution.py:50
  30.8 0.5 weight.1
  31.3 1.3 %collective-permute-start.18 = (bf16[96,768]{1,0:T(8,128)(2,1)S(1)}, bf16[96,768]{1,0:T(8,128)(2,1)S(1)}, u32[]{:S(2)}, u32[]{:S(2)}) collective-permute-start(bf16[96,768]{1,0:T(8,128)(2,1)S(1)} %get-tuple-element.86.refs_4_), channel_id=1, source_target_pairs={{0,16},{16,0},{1,17},{17,1},{2,18},{18,2},{3,19},{19,3},{4,20},{20... | collective-permute-start | bytes 442376 | tf_op jit(solution)/shard_map/ppermute | solution.py:355
  32.6 0.3 collective-permute-start.10
  32.9 3.0 %collective-permute-start.11 = (f32[8,384]{1,0:T(8,128)S(1)}, f32[8,384]{1,0:T(8,128)S(1)}, u32[]{:S(2)}, u32[]{:S(2)}) collective-permute-start(f32[8,384]{1,0:T(8,128)S(1)} %get-tuple-element.78), channel_id=1, source_target_pairs={{0,12},{1,13},{2,14},{3,15},{4,0},{5,1},{6,2},{7,3},{8,4},{9,5},{1... | collective-permute-start | bytes 36872 | tf_op jit(solution)/shard_map/ppermute | solution.py:351
  35.8 2.4 %query_grad.1 = (bf16[192,512]{1,0:T(8,128)(2,1)S(1)}, f32[2,192,512]{2,1,0:T(8,128)S(1)}, f32[8,128]{1,0:T(8,128)S(1)}) custom-call(bf16[2,192,1280]{2,1,0:T(8,128)(2,1)S(1)} %get-tuple-element.80.refs_0_, bf16[3,1280,512]{2,1,0:T(8,128)(2,1)S(1)} %get-tuple-element.81.refs_1_, bf16[2,192,512]{2,1,0:T(8,128)(2,1)S(1)} %get-tuple-element.76.query_ref.refs_2_, ...), custom_call_target="tpu_custom_call" | custom-call | flops 1 | bytes 1 | tf_op jit(solution)/shard_map/query_grad/pallas_call | solution.py:50
  38.3 1.6 %collective-permute-done.10.stats_low.refs_5_ = f32[8,384]{1,0:T(8,128)S(1)} collective-permute-done((f32[8,384]{1,0:T(8,128)S(1)}, f32[8,384]{1,0:T(8,128)S(1)}, u32[]{:S(2)}, u32[]{:S(2)}) %collective-permute-start.10) | collective-permute-done | bytes 12320 | tf_op jit(solution)/shard_map/ppermute | solution.py:350
  39.9 0.1 collective-permute-done.11.stats_high.refs_6_
  40.1 1.5 %collective-permute-start.19 = (bf16[48,768]{1,0:T(8,128)(2,1)S(1)}, bf16[48,768]{1,0:T(8,128)(2,1)S(1)}, u32[]{:S(2)}, u32[]{:S(2)}) collective-permute-start(bf16[48,768]{1,0:T(8,128)(2,1)S(1)} %get-tuple-element.100), channel_id=1, source_target_pairs={{4,0},{5,1},{6,2},{7,3},{0,4},{1,5},{2,6},{3,7},{12,8},{13,9},{14,... | collective-permute-start | bytes 221192 | tf_op jit(solution)/shard_map/ppermute | solution.py:344
  41.5 1.9 %key_grad.1 = (bf16[4,192,128]{2,1,0:T(8,128)(2,1)S(1)}, bf16[4,192,128]{2,1,0:T(8,128)(2,1)S(1)}, bf16[4,192,128]{2,1,0:T(8,128)(2,1)S(1)}, bf16[4,192,128]{2,1,0:T(8,128)(2,1)S(1)}, f32[8,128]{1,0:T(8,128)S(1)}) custom-call(bf16[2,192,512]{2,1,0:T(8,128)(2,1)S(1)} %get-tuple-element.61.pair_ref, ...), custom_call_target="tpu_custom_call" | custom-call | flops 1 | bytes 1 | tf_op jit(solution)/shard_map/key_grad/pallas_call | solution.py:50
  43.4 0.8 %collective-permute-start.15 = (bf16[4,192,128]{2,1,0:T(8,128)(2,1)S(1)}, bf16[4,192,128]{2,1,0:T(8,128)(2,1)S(1)}, u32[]{:S(2)}, u32[]{:S(2)}) collective-permute-start(bf16[4,192,128]{2,1,0:T(8,128)(2,1)S(1)} %get-tuple-element.90), channel_id=1, source_target_pairs={{1,0},{0,1},{3,2},{2,3},{5,4},{4,5},{7,6},{6,7},{9,8},{8,9},{11,10... | collective-permute-start | bytes 589832 | tf_op jit(solution)/shard_map/ppermute | solution.py:344
  44.3 1.7 %collective-permute-start.17 = (bf16[4,192,128]{2,1,0:T(8,128)(2,1)S(1)}, bf16[4,192,128]{2,1,0:T(8,128)(2,1)S(1)}, u32[]{:S(2)}, u32[]{:S(2)}) collective-permute-start(bf16[4,192,128]{2,1,0:T(8,128)(2,1)S(1)} %get-tuple-element.92), channel_id=1, source_target_pairs={{3,0},{2,1},{1,2},{0,3},{7,4},{6,5},{5,6},{4,7},{11,8},{10,9},{9,1... | collective-permute-start | bytes 589832 | tf_op jit(solution)/shard_map/ppermute | solution.py:344
  46.0 2.5 %collective-permute-start.20 = (bf16[48,768]{1,0:T(8,128)(2,1)S(1)}, bf16[48,768]{1,0:T(8,128)(2,1)S(1)}, u32[]{:S(2)}, u32[]{:S(2)}) collective-permute-start(bf16[48,768]{1,0:T(8,128)(2,1)S(1)} %add.2.part_ref), channel_id=1, source_target_pairs={{8,0},{9,1},{10,2},{11,3},{12,4},{13,5},{14,6},{15,7},{0,8},{1,9},... | collective-permute-start | bytes 221192 | tf_op jit(solution)/shard_map/ppermute | solution.py:344
  48.6 3.9 %collective-permute-done.20.got_ref = bf16[48,768]{1,0:T(8,128)(2,1)S(1)} collective-permute-done((bf16[48,768]{1,0:T(8,128)(2,1)S(1)}, bf16[48,768]{1,0:T(8,128)(2,1)S(1)}, u32[]{:S(2)}, u32[]{:S(2)}) %collective-permute-start.20) | collective-permute-done | bytes 73760 | tf_op jit(solution)/shard_map/ppermute | solution.py:344
  52.5 0.1 collective-permute-start.21
  52.6 2.5 %collective-permute-done.17.refs_3_.refs_4_ = bf16[4,192,128]{2,1,0:T(8,128)(2,1)S(1)} collective-permute-done((bf16[4,192,128]{2,1,0:T(8,128)(2,1)S(1)}, bf16[4,192,128]{2,1,0:T(8,128)(2,1)S(1)}, u32[]{:S(2)}, u32[]{:S(2)}) %collective-permute-start.17) | collective-permute-done | bytes 196640 | tf_op jit(solution)/shard_map/ppermute | solution.py:344
  55.1 0.6 collective-permute-done.21.refs_1_
  55.8 0.7 collective-permute-start.22
  56.5 2.9 %collective-permute-start.23 = (bf16[96,768]{1,0:T(8,128)(2,1)S(1)}, bf16[96,768]{1,0:T(8,128)(2,1)S(1)}, u32[]{:S(2)}, u32[]{:S(2)}) collective-permute-start(bf16[96,768]{1,0:T(8,128)(2,1)S(1)} %join.1.refs_0_), channel_id=1, source_target_pairs={{2,16},{3,17},{6,20},{7,21},{10,24},{11,25},{14,28},{15,29},{16,2}... | collective-permute-start | bytes 442376 | tf_op jit(solution)/shard_map/ppermute | solution.py:473
  59.3 1.2 %output.1 = (bf16[128,768]{1,0:T(8,128)(2,1)}, bf16[128,768]{1,0:T(8,128)(2,1)}, bf16[128,768]{1,0:T(8,128)(2,1)}, bf16[128,768]{1,0:T(8,128)(2,1)}, f32[8,128]{1,0:T(8,128)S(1)}) custom-call(bf16[4,192,128]{2,1,0:T(8,128)(2,1)S(1)} %get-tuple-element.89.refs_0_, bf16[4,192,128]{2,1,0:T(8,128)(2,1)S(1)} %collective-permute-done.15.refs_1_.refs_2_, ...), custom_call_target="tpu_custom_call" | custom-call | flops 1 | bytes 1 | tf_op jit(solution)/shard_map/output/pallas_call | solution.py:50
  60.5 2.7 %collective-permute-done.23.refs_2_ = bf16[96,768]{1,0:T(8,128)(2,1)S(1)} collective-permute-done((bf16[96,768]{1,0:T(8,128)(2,1)S(1)}, bf16[96,768]{1,0:T(8,128)(2,1)S(1)}, u32[]{:S(2)}, u32[]{:S(2)}) %collective-permute-start.23) | collective-permute-done | bytes 147488 | tf_op jit(solution)/shard_map/ppermute | solution.py:473
  63.3 4.0 %collective-permute-start.24 = (bf16[192,768]{1,0:T(8,128)(2,1)S(1)}, bf16[192,768]{1,0:T(8,128)(2,1)S(1)}, u32[]{:S(2)}, u32[]{:S(2)}) collective-permute-start(bf16[192,768]{1,0:T(8,128)(2,1)S(1)} %cross.1.value_ref), channel_id=1, source_target_pairs={{1,0},{0,1},{3,2},{2,3},{5,4},{4,5},{7,6},{6,7},{9,8},{8,9},{11,10... | collective-permute-start | bytes 884744 | tf_op jit(solution)/shard_map/ppermute | solution.py:344
  67.3 0.9 %write.2.refs_0_ = f32[384,768]{1,0:T(8,128)} custom-call(bf16[192,768]{1,0:T(8,128)(2,1)S(1)} %cross.1.value_ref), custom_call_target="tpu_custom_call" | custom-call | flops 1 | bytes 1 | tf_op jit(solution)/shard_map/write/pallas_call | solution.py:478
  68.2 0.3 collective-permute-done.24.value_ref
  68.5 0.9 %write.3 = f32[384,768]{1,0:T(8,128)} custom-call(bf16[192,768]{1,0:T(8,128)(2,1)S(1)} %collective-permute-done.24.value_ref, f32[384,768]{1,0:T(8,128)} %write.2.refs_0_), custom_call_target="tpu_custom_call", output_to_operand_aliasing={{}: (1, {})} | custom-call | flops 1 | bytes 1 | tf_op jit(solution)/shard_map/write/pallas_call | solution.py:478
  (36 shorter events, 0.2 us)
Async XLA Ops:
  0.6 11.1 %copy-start.4 = (bf16[1,1,128,768]{3,2,1,0:T(8,128)(2,1)S(1)}, bf16[1,1,128,768]{3,2,1,0:T(8,128)(2,1)}, u32[]{:S(2)}) copy-start(bf16[1,1,128,768]{3,2,1,0:T(8,128)(2,1)} %param.10) | copy-start | bytes 589828
  0.6 21.5 %copy-start.7 = (s32[16,6]{0,1:T(8,128)S(1)}, s32[16,6]{0,1:T(8,128)}, u32[]{:S(2)}) copy-start(s32[16,6]{0,1:T(8,128)} %param.12) | copy-start | bytes 1156
  0.7 21.6 %copy-start.6 = (s32[16]{0:T(128)S(1)}, s32[16]{0:T(128)}, u32[]{:S(2)}) copy-start(s32[16]{0:T(128)} %count_ref.1) | copy-start | bytes 196
  2.6 6.1 %collective-permute-start = (bf16[2,192,128]{2,1,0:T(8,128)(2,1)}, bf16[2,192,128]{2,1,0:T(8,128)(2,1)S(1)}, u32[]{:S(2)}, u32[]{:S(2)}) collective-permute-start(bf16[2,192,128]{2,1,0:T(8,128)(2,1)} %get-tuple-element.58), channel_id=1, source_target_pairs={{1,0},{0,1},{3,2},{2,3},{5,4},{4,5},{7,6},{6,7},{9,8},{8,9},{11,10... | collective-permute-start | bytes 294920 | tf_op jit(solution)/shard_map/ppermute | solution.py:344
  3.4 5.4 %collective-permute-start.1 = (bf16[2,192,128]{2,1,0:T(8,128)(2,1)}, bf16[2,192,128]{2,1,0:T(8,128)(2,1)S(1)}, u32[]{:S(2)}, u32[]{:S(2)}) collective-permute-start(bf16[2,192,128]{2,1,0:T(8,128)(2,1)} %get-tuple-element.59), channel_id=1, source_target_pairs={{2,0},{3,1},{0,2},{1,3},{6,4},{7,5},{4,6},{5,7},{10,8},{11,9},{8,1... | collective-permute-start | bytes 294920 | tf_op jit(solution)/shard_map/ppermute | solution.py:344
  3.4 6.8 %collective-permute-start.2 = (bf16[2,192,128]{2,1,0:T(8,128)(2,1)}, bf16[2,192,128]{2,1,0:T(8,128)(2,1)S(1)}, u32[]{:S(2)}, u32[]{:S(2)}) collective-permute-start(bf16[2,192,128]{2,1,0:T(8,128)(2,1)} %get-tuple-element.60), channel_id=1, source_target_pairs={{3,0},{2,1},{1,2},{0,3},{7,4},{6,5},{5,6},{4,7},{11,8},{10,9},{9,1... | collective-permute-start | bytes 294920 | tf_op jit(solution)/shard_map/ppermute | solution.py:344
  5.1 1.3 %copy-start = (bf16[768,768]{1,0:T(8,128)(2,1)S(1)}, bf16[768,768]{1,0:T(8,128)(2,1)}, u32[]{:S(2)}) copy-start(bf16[768,768]{1,0:T(8,128)(2,1)} %refs_4_.1) | copy-start | bytes 3538948
  6.3 0.9 %copy-start.2 = (bf16[1,1,128,768]{3,2,1,0:T(8,128)(2,1)S(1)}, bf16[1,1,128,768]{3,2,1,0:T(8,128)(2,1)}, u32[]{:S(2)}) copy-start(bf16[1,1,128,768]{3,2,1,0:T(8,128)(2,1)} %param.7) | copy-start | bytes 589828
  7.3 0.9 %copy-start.3 = (bf16[1,1,128,768]{3,2,1,0:T(8,128)(2,1)S(1)}, bf16[1,1,128,768]{3,2,1,0:T(8,128)(2,1)}, u32[]{:S(2)}) copy-start(bf16[1,1,128,768]{3,2,1,0:T(8,128)(2,1)} %param.10) | copy-start | bytes 589828
  8.2 2.0 %copy-start.5 = (bf16[2,192,128]{2,1,0:T(8,128)(2,1)S(1)}, bf16[2,192,128]{2,1,0:T(8,128)(2,1)}, u32[]{:S(2)}) copy-start(bf16[2,192,128]{2,1,0:T(8,128)(2,1)} %get-tuple-element.54.refs_0_) | copy-start | bytes 294916
  10.4 14.6 %collective-permute-start.8 = (bf16[2,192,384]{2,1,0:T(8,128)(2,1)S(1)}, bf16[2,192,384]{2,1,0:T(8,128)(2,1)S(1)}, u32[]{:S(2)}, u32[]{:S(2)}) collective-permute-start(bf16[2,192,384]{2,1,0:T(8,128)(2,1)S(1)} %get-tuple-element.74), channel_id=1, source_target_pairs={{0,4},{1,5},{2,6},{3,7},{4,8},{5,9},{6,10},{7,11},{8,12},{9,13},{1... | collective-permute-start | bytes 884744 | tf_op jit(solution)/shard_map/ppermute | solution.py:350
  11.7 10.4 %collective-permute-start.13 = (bf16[128,768]{1,0:T(8,128)(2,1)S(1)}, bf16[128,768]{1,0:T(8,128)(2,1)S(1)}, u32[]{:S(2)}, u32[]{:S(2)}) collective-permute-start(bf16[128,768]{1,0:T(8,128)(2,1)S(1)} %bitcast.10), channel_id=1, source_target_pairs={{2,0},{3,1},{0,2},{1,3},{6,4},{7,5},{4,6},{5,7},{10,8},{11,9},{8,1... | collective-permute-start | bytes 589832 | tf_op jit(solution)/shard_map/ppermute | solution.py:344
  12.0 4.0 %collective-permute-start.3 = (bf16[2,192,128]{2,1,0:T(8,128)(2,1)S(1)}, bf16[2,192,128]{2,1,0:T(8,128)(2,1)S(1)}, u32[]{:S(2)}, u32[]{:S(2)}) collective-permute-start(bf16[2,192,128]{2,1,0:T(8,128)(2,1)S(1)} %get-tuple-element.68), channel_id=1, source_target_pairs={{1,0},{0,1},{3,2},{2,3},{5,4},{4,5},{7,6},{6,7},{9,8},{8,9},{11,10... | collective-permute-start | bytes 294920 | tf_op jit(solution)/shard_map/ppermute | solution.py:344
  12.8 14.8 %collective-permute-start.9 = (bf16[2,192,384]{2,1,0:T(8,128)(2,1)S(1)}, bf16[2,192,384]{2,1,0:T(8,128)(2,1)S(1)}, u32[]{:S(2)}, u32[]{:S(2)}) collective-permute-start(bf16[2,192,384]{2,1,0:T(8,128)(2,1)S(1)} %get-tuple-element.75), channel_id=1, source_target_pairs={{0,12},{1,13},{2,14},{3,15},{4,0},{5,1},{6,2},{7,3},{8,4},{9,5},{1... | collective-permute-start | bytes 884744 | tf_op jit(solution)/shard_map/ppermute | solution.py:351
  14.7 5.1 %collective-permute-start.4 = (bf16[2,192,128]{2,1,0:T(8,128)(2,1)S(1)}, bf16[2,192,128]{2,1,0:T(8,128)(2,1)S(1)}, u32[]{:S(2)}, u32[]{:S(2)}) collective-permute-start(bf16[2,192,128]{2,1,0:T(8,128)(2,1)S(1)} %get-tuple-element.69), channel_id=1, source_target_pairs={{2,0},{3,1},{0,2},{1,3},{6,4},{7,5},{4,6},{5,7},{10,8},{11,9},{8,1... | collective-permute-start | bytes 294920 | tf_op jit(solution)/shard_map/ppermute | solution.py:344
  16.0 7.5 %collective-permute-start.5 = (bf16[2,192,128]{2,1,0:T(8,128)(2,1)S(1)}, bf16[2,192,128]{2,1,0:T(8,128)(2,1)S(1)}, u32[]{:S(2)}, u32[]{:S(2)}) collective-permute-start(bf16[2,192,128]{2,1,0:T(8,128)(2,1)S(1)} %get-tuple-element.70), channel_id=1, source_target_pairs={{3,0},{2,1},{1,2},{0,3},{7,4},{6,5},{5,6},{4,7},{11,8},{10,9},{9,1... | collective-permute-start | bytes 294920 | tf_op jit(solution)/shard_map/ppermute | solution.py:344
  19.8 11.0 %collective-permute-start.12 = (bf16[128,768]{1,0:T(8,128)(2,1)S(1)}, bf16[128,768]{1,0:T(8,128)(2,1)S(1)}, u32[]{:S(2)}, u32[]{:S(2)}) collective-permute-start(bf16[128,768]{1,0:T(8,128)(2,1)S(1)} %bitcast.11), channel_id=1, source_target_pairs={{1,0},{0,1},{3,2},{2,3},{5,4},{4,5},{7,6},{6,7},{9,8},{8,9},{11,10... | collective-permute-start | bytes 589832 | tf_op jit(solution)/shard_map/ppermute | solution.py:344
  22.1 8.7 %collective-permute-start.14 = (bf16[128,768]{1,0:T(8,128)(2,1)S(1)}, bf16[128,768]{1,0:T(8,128)(2,1)S(1)}, u32[]{:S(2)}, u32[]{:S(2)}) collective-permute-start(bf16[128,768]{1,0:T(8,128)(2,1)S(1)} %collective-permute-done.13.refs_2_), channel_id=1, source_target_pairs={{1,0},{0,1},{3,2},{2,3},{5,4},{4,5},{7,6},{6,7},{9,8},{8,9},{11,10... | collective-permute-start | bytes 589832 | tf_op jit(solution)/shard_map/ppermute | solution.py:344
  23.6 16.4 %collective-permute-start.6 = (bf16[2,192,384]{2,1,0:T(8,128)(2,1)S(1)}, bf16[2,192,384]{2,1,0:T(8,128)(2,1)S(1)}, u32[]{:S(2)}, u32[]{:S(2)}) collective-permute-start(bf16[2,192,384]{2,1,0:T(8,128)(2,1)S(1)} %get-tuple-element.72), channel_id=1, source_target_pairs={{0,4},{1,5},{2,6},{3,7},{4,8},{5,9},{6,10},{7,11},{8,12},{9,13},{1... | collective-permute-start | bytes 884744 | tf_op jit(solution)/shard_map/ppermute | solution.py:350
  25.0 15.0 %collective-permute-start.7 = (bf16[2,192,384]{2,1,0:T(8,128)(2,1)S(1)}, bf16[2,192,384]{2,1,0:T(8,128)(2,1)S(1)}, u32[]{:S(2)}, u32[]{:S(2)}) collective-permute-start(bf16[2,192,384]{2,1,0:T(8,128)(2,1)S(1)} %get-tuple-element.73), channel_id=1, source_target_pairs={{0,12},{1,13},{2,14},{3,15},{4,0},{5,1},{6,2},{7,3},{8,4},{9,5},{1... | collective-permute-start | bytes 884744 | tf_op jit(solution)/shard_map/ppermute | solution.py:351
  31.3 8.7 %collective-permute-start.18 = (bf16[96,768]{1,0:T(8,128)(2,1)S(1)}, bf16[96,768]{1,0:T(8,128)(2,1)S(1)}, u32[]{:S(2)}, u32[]{:S(2)}) collective-permute-start(bf16[96,768]{1,0:T(8,128)(2,1)S(1)} %get-tuple-element.86.refs_4_), channel_id=1, source_target_pairs={{0,16},{16,0},{1,17},{17,1},{2,18},{18,2},{3,19},{19,3},{4,20},{20... | collective-permute-start | bytes 442376 | tf_op jit(solution)/shard_map/ppermute | solution.py:355
  32.6 7.3 %collective-permute-start.10 = (f32[8,384]{1,0:T(8,128)S(1)}, f32[8,384]{1,0:T(8,128)S(1)}, u32[]{:S(2)}, u32[]{:S(2)}) collective-permute-start(f32[8,384]{1,0:T(8,128)S(1)} %get-tuple-element.77), channel_id=1, source_target_pairs={{0,4},{1,5},{2,6},{3,7},{4,8},{5,9},{6,10},{7,11},{8,12},{9,13},{1... | collective-permute-start | bytes 36872 | tf_op jit(solution)/shard_map/ppermute | solution.py:350
  32.9 7.1 %collective-permute-start.11 = (f32[8,384]{1,0:T(8,128)S(1)}, f32[8,384]{1,0:T(8,128)S(1)}, u32[]{:S(2)}, u32[]{:S(2)}) collective-permute-start(f32[8,384]{1,0:T(8,128)S(1)} %get-tuple-element.78), channel_id=1, source_target_pairs={{0,12},{1,13},{2,14},{3,15},{4,0},{5,1},{6,2},{7,3},{8,4},{9,5},{1... | collective-permute-start | bytes 36872 | tf_op jit(solution)/shard_map/ppermute | solution.py:351
  40.1 5.9 %collective-permute-start.19 = (bf16[48,768]{1,0:T(8,128)(2,1)S(1)}, bf16[48,768]{1,0:T(8,128)(2,1)S(1)}, u32[]{:S(2)}, u32[]{:S(2)}) collective-permute-start(bf16[48,768]{1,0:T(8,128)(2,1)S(1)} %get-tuple-element.100), channel_id=1, source_target_pairs={{4,0},{5,1},{6,2},{7,3},{0,4},{1,5},{2,6},{3,7},{12,8},{13,9},{14,... | collective-permute-start | bytes 221192 | tf_op jit(solution)/shard_map/ppermute | solution.py:344
  43.4 15.9 %copy-start.1 = (bf16[768,768]{1,0:T(8,128)(2,1)S(1)}, bf16[768,768]{1,0:T(8,128)(2,1)}, u32[]{:S(2)}) copy-start(bf16[768,768]{1,0:T(8,128)(2,1)} %refs_4_.1) | copy-start | bytes 3538948
  43.4 9.1 %collective-permute-start.15 = (bf16[4,192,128]{2,1,0:T(8,128)(2,1)S(1)}, bf16[4,192,128]{2,1,0:T(8,128)(2,1)S(1)}, u32[]{:S(2)}, u32[]{:S(2)}) collective-permute-start(bf16[4,192,128]{2,1,0:T(8,128)(2,1)S(1)} %get-tuple-element.90), channel_id=1, source_target_pairs={{1,0},{0,1},{3,2},{2,3},{5,4},{4,5},{7,6},{6,7},{9,8},{8,9},{11,10... | collective-permute-start | bytes 589832 | tf_op jit(solution)/shard_map/ppermute | solution.py:344
  44.3 8.3 %collective-permute-start.16 = (bf16[4,192,128]{2,1,0:T(8,128)(2,1)S(1)}, bf16[4,192,128]{2,1,0:T(8,128)(2,1)S(1)}, u32[]{:S(2)}, u32[]{:S(2)}) collective-permute-start(bf16[4,192,128]{2,1,0:T(8,128)(2,1)S(1)} %get-tuple-element.91), channel_id=1, source_target_pairs={{2,0},{3,1},{0,2},{1,3},{6,4},{7,5},{4,6},{5,7},{10,8},{11,9},{8,1... | collective-permute-start | bytes 589832 | tf_op jit(solution)/shard_map/ppermute | solution.py:344
  44.3 10.9 %collective-permute-start.17 = (bf16[4,192,128]{2,1,0:T(8,128)(2,1)S(1)}, bf16[4,192,128]{2,1,0:T(8,128)(2,1)S(1)}, u32[]{:S(2)}, u32[]{:S(2)}) collective-permute-start(bf16[4,192,128]{2,1,0:T(8,128)(2,1)S(1)} %get-tuple-element.92), channel_id=1, source_target_pairs={{3,0},{2,1},{1,2},{0,3},{7,4},{6,5},{5,6},{4,7},{11,8},{10,9},{9,1... | collective-permute-start | bytes 589832 | tf_op jit(solution)/shard_map/ppermute | solution.py:344
  46.0 6.4 %collective-permute-start.20 = (bf16[48,768]{1,0:T(8,128)(2,1)S(1)}, bf16[48,768]{1,0:T(8,128)(2,1)S(1)}, u32[]{:S(2)}, u32[]{:S(2)}) collective-permute-start(bf16[48,768]{1,0:T(8,128)(2,1)S(1)} %add.2.part_ref), channel_id=1, source_target_pairs={{8,0},{9,1},{10,2},{11,3},{12,4},{13,5},{14,6},{15,7},{0,8},{1,9},... | collective-permute-start | bytes 221192 | tf_op jit(solution)/shard_map/ppermute | solution.py:344
  52.5 3.3 %collective-permute-start.21 = (bf16[48,768]{1,0:T(8,128)(2,1)S(1)}, bf16[48,768]{1,0:T(8,128)(2,1)S(1)}, u32[]{:S(2)}, u32[]{:S(2)}) collective-permute-start(bf16[48,768]{1,0:T(8,128)(2,1)S(1)} %add.3.refs_0_), channel_id=1, source_target_pairs={{4,0},{5,1},{6,2},{7,3},{0,4},{1,5},{2,6},{3,7},{12,8},{13,9},{14,... | collective-permute-start | bytes 221192 | tf_op jit(solution)/shard_map/ppermute | solution.py:344
  55.8 4.8 %collective-permute-start.22 = (bf16[96,768]{1,0:T(8,128)(2,1)S(1)}, bf16[96,768]{1,0:T(8,128)(2,1)S(1)}, u32[]{:S(2)}, u32[]{:S(2)}) collective-permute-start(bf16[96,768]{1,0:T(8,128)(2,1)S(1)} %join.1.refs_0_), channel_id=1, source_target_pairs={{0,2},{1,3},{2,18},{3,19},{4,6},{5,7},{6,22},{7,23},{8,10},{9,11},... | collective-permute-start | bytes 442376 | tf_op jit(solution)/shard_map/ppermute | solution.py:473
  56.5 6.8 %collective-permute-start.23 = (bf16[96,768]{1,0:T(8,128)(2,1)S(1)}, bf16[96,768]{1,0:T(8,128)(2,1)S(1)}, u32[]{:S(2)}, u32[]{:S(2)}) collective-permute-start(bf16[96,768]{1,0:T(8,128)(2,1)S(1)} %join.1.refs_0_), channel_id=1, source_target_pairs={{2,16},{3,17},{6,20},{7,21},{10,24},{11,25},{14,28},{15,29},{16,2}... | collective-permute-start | bytes 442376 | tf_op jit(solution)/shard_map/ppermute | solution.py:473
  63.3 5.2 %collective-permute-start.24 = (bf16[192,768]{1,0:T(8,128)(2,1)S(1)}, bf16[192,768]{1,0:T(8,128)(2,1)S(1)}, u32[]{:S(2)}, u32[]{:S(2)}) collective-permute-start(bf16[192,768]{1,0:T(8,128)(2,1)S(1)} %cross.1.value_ref), channel_id=1, source_target_pairs={{1,0},{0,1},{3,2},{2,3},{5,4},{4,5},{7,6},{6,7},{9,8},{8,9},{11,10... | collective-permute-start | bytes 884744 | tf_op jit(solution)/shard_map/ppermute | solution.py:344

commit v16 on v15

--- a/solution.py
+++ b/solution.py
@@ -53,7 +53,7 @@
         out_specs=[VMEM] * len(outs),
         out_shape=outs,
         scratch_shapes=list(scratch),
-        compiler_params=pltpu.CompilerParams(vmem_limit_bytes=limit * MIB),
+        compiler_params=pltpu.CompilerParams(vmem_limit_bytes=int(limit * MIB)),
         cost_estimate=pl.CostEstimate(flops=1, bytes_accessed=1, transcendentals=0),
         name=name,
     )(*args)
@@ -194,8 +194,9 @@
         stats_ref[head : head + 1] = top + jnp.log(total)
         stats_ref[LOCAL + head : LOCAL + head + 1] = jnp.sum(product, 0, keepdims=True)
     stats_ref[2 * LOCAL :] = jnp.zeros((8 - 2 * LOCAL, LAYER * span), f32)
-    stats_up[...] = stats_ref[:, span:]
-    stats_down[...] = stats_ref[:, :reach]
+    for ref, at in ((stats_up, slice(span, None)), (stats_down, slice(0, reach))):
+        ref[...] = jnp.zeros_like(ref)
+        ref[:8] = stats_ref[:, at]
 
 
 def query_grad_kernel(
@@ -372,7 +373,7 @@
     mine, *parts = call(
         pack_kernel, [HBM] * 2, [part_shape] * LAYER, (k, v),
         [pltpu.VMEM((2, span, width), bf16), pltpu.VMEM((2, width, span), bf16), dma((2,))],
-        limit=58, name="pack",
+        limit=53.5, name="pack",
     )
     q, *parts = lax.optimization_barrier((q, *parts))
     parts = in_layer(parts)
@@ -392,7 +393,7 @@
     )
     up, down, query = gather((mine, *in_layer(query_parts)), (bias,))
     qg_low, qg_high = along(up, down)
-    stats_shape = shape_of(8, HOPS * span, dtype=f32)
+    stats_shape = shape_of(16, HOPS * span, dtype=f32)
     mixed, stats, up, down, probs, window = call(
         forward_kernel, [VMEM] * 5,
         [
@@ -443,7 +444,7 @@
         send, part = call(
             functools.partial(split_kernel, LAYER), [VMEM] * 2,
             [shape_of(count, width), shape_of(count, width, dtype=f32)],
-            (part, got), name="split", after=(query_token, qg_low, qg_high, stats_low, stats_high),
+            (part, got), name="split", after=(query_token,),
         )
 
         def add_round(part, got, after=()):

time: 69.6 us -> 68.5 us (0.984)
  starting transfers between devices: 33.1 us -> 29.7 us
  waiting for transfers between devices: 17.2 us -> 20.3 us
  Pallas kernels: 15 us -> 14.2 us
    ppermute x16, starting transfers between devices: 18.4 us -> 15.7 us  [swap(): lax.ppermute(value, 'station', [(s ^ stride, s) for s in range(stations)])]
    ppermute x16, waiting for transfers between devices: 12.1 us -> 13.9 us  [swap(): lax.ppermute(value, 'station', [(s ^ stride, s) for s in range(stations)])]
    ppermute x1, starting transfers between devices: 2.86 us -> 1.91 us  [local(): lax.ppermute(total, axes, second)]
    ppermute x1, waiting for transfers between devices: 2.71 us -> 3.65 us  [local(): lax.ppermute(total, axes, second)]
    pallas_call x15, Pallas kernels: 13.3 us -> 12.5 us  [call(): pl.pallas_call(kernel, in_specs=ins, out_specs=[VMEM] * len(outs), out_sh...]
    unnamed x17 -> x15, local copies, waits for them, and re-layouts: 3.23 us -> 3.23 us
where the time goes in v16:
time: 68.5 us; the launch traced here: 68.3 us
  starting transfers between devices  29.7 us (43%)
  waiting for transfers between devices  20.3 us (30%)
  Pallas kernels  14.2 us (21%)
  local copies, waits for them, and re-layouts  3.23 us (5%)
  between operations  0.86 us (1%)
    ppermute x16, starting transfers between devices, swap(): lax.ppermute(value, 'station', [(s ^ stride, s) for s in range(stations)])  15.7 us
    ppermute x16, waiting for transfers between devices, swap(): lax.ppermute(value, 'station', [(s ^ stride, s) for s in range(stations)])  13.9 us
    pallas_call x15, Pallas kernels, call(): pl.pallas_call(kernel, in_specs=ins, out_specs=[VMEM] * len(outs), out_sh...  12.5 us
    ppermute x3, starting transfers between devices, along(): lax.ppermute(down, 'station', [(s, (s - LAYER) % stations) for s in range...  6.84 us
    ppermute x1, waiting for transfers between devices, local(): lax.ppermute(total, axes, second)  3.65 us
    unnamed x15, local copies, waits for them, and re-layouts  3.23 us
    ppermute x3, starting transfers between devices, along(): lax.ppermute(up, 'station', [(s, (s + LAYER) % stations) for s in range(s...  2.98 us
    ppermute x1, starting transfers between devices, local(): lax.ppermute(total, axes, second)  1.91 us
  transfers between devices with their start and end apart: 25, of which 10 were waited for; matrix products, arithmetic and copies ran while one was open for 0% of the time, Pallas kernels for 17%

profile of v16, /device:TPU:3, one launch (start us, length us, event | category | flops | bytes accessed | tf_op | source)
XLA Modules:
  0.0 68.3 jit_solution(15604240734692932259)
XLA Ops:
  0.7 1.2 %pack.1 = (bf16[2,192,128]{2,1,0:T(8,128)(2,1)S(1)}, bf16[2,192,128]{2,1,0:T(8,128)(2,1)S(1)}, bf16[2,192,128]{2,1,0:T(8,128)(2,1)S(1)}, bf16[2,192,128]{2,1,0:T(8,128)(2,1)S(1)}) custom-call(bf16[128,768]{1,0:T(8,128)(2,1)} %bitcast.12, bf16[128,768]{1,0:T(8,128)(2,1)} %bitcast.13), custom_call_target="tpu_custom_call" | custom-call | flops 1 | bytes 1 | tf_op jit(solution)/shard_map/pack/pallas_call | solution.py:50
  1.9 0.7 %collective-permute-start = (bf16[2,192,128]{2,1,0:T(8,128)(2,1)S(1)}, bf16[2,192,128]{2,1,0:T(8,128)(2,1)S(1)}, u32[]{:S(2)}, u32[]{:S(2)}) collective-permute-start(bf16[2,192,128]{2,1,0:T(8,128)(2,1)S(1)} %get-tuple-element.58), channel_id=1, source_target_pairs={{1,0},{0,1},{3,2},{2,3},{5,4},{4,5},{7,6},{6,7},{9,8},{8,9},{11,10... | collective-permute-start | bytes 294920 | tf_op jit(solution)/shard_map/ppermute | solution.py:345
  2.6 1.7 %collective-permute-start.2 = (bf16[2,192,128]{2,1,0:T(8,128)(2,1)S(1)}, bf16[2,192,128]{2,1,0:T(8,128)(2,1)S(1)}, u32[]{:S(2)}, u32[]{:S(2)}) collective-permute-start(bf16[2,192,128]{2,1,0:T(8,128)(2,1)S(1)} %get-tuple-element.60), channel_id=1, source_target_pairs={{3,0},{2,1},{1,2},{0,3},{7,4},{6,5},{5,6},{4,7},{11,8},{10,9},{9,1... | collective-permute-start | bytes 294920 | tf_op jit(solution)/shard_map/ppermute | solution.py:345
  4.4 1.3 %copy-done = bf16[768,768]{1,0:T(8,128)(2,1)S(1)} copy-done((bf16[768,768]{1,0:T(8,128)(2,1)S(1)}, bf16[768,768]{1,0:T(8,128)(2,1)}, u32[]{:S(2)}) %copy-start) | copy-done | bytes 1179672
  5.6 0.9 %copy-done.2 = bf16[1,1,128,768]{3,2,1,0:T(8,128)(2,1)S(1)} copy-done((bf16[1,1,128,768]{3,2,1,0:T(8,128)(2,1)S(1)}, bf16[1,1,128,768]{3,2,1,0:T(8,128)(2,1)}, u32[]{:S(2)}) %copy-start.2) | copy-done | bytes 196632
  6.6 0.9 %copy-done.3 = bf16[1,1,128,768]{3,2,1,0:T(8,128)(2,1)S(1)} copy-done((bf16[1,1,128,768]{3,2,1,0:T(8,128)(2,1)S(1)}, bf16[1,1,128,768]{3,2,1,0:T(8,128)(2,1)}, u32[]{:S(2)}) %copy-start.3) | copy-done | bytes 196632
  7.5 0.5 project.1
  8.0 1.3 %collective-permute-done.2.refs_3_ = bf16[2,192,128]{2,1,0:T(8,128)(2,1)S(1)} collective-permute-done((bf16[2,192,128]{2,1,0:T(8,128)(2,1)S(1)}, bf16[2,192,128]{2,1,0:T(8,128)(2,1)S(1)}, u32[]{:S(2)}, u32[]{:S(2)}) %collective-permute-start.2) | collective-permute-done | bytes 98336 | tf_op jit(solution)/shard_map/ppermute | solution.py:345
  9.3 0.1 gather.2
  9.4 1.3 %collective-permute-start.8 = (bf16[2,192,384]{2,1,0:T(8,128)(2,1)S(1)}, bf16[2,192,384]{2,1,0:T(8,128)(2,1)S(1)}, u32[]{:S(2)}, u32[]{:S(2)}) collective-permute-start(bf16[2,192,384]{2,1,0:T(8,128)(2,1)S(1)} %get-tuple-element.74), channel_id=1, source_target_pairs={{0,4},{1,5},{2,6},{3,7},{4,8},{5,9},{6,10},{7,11},{8,12},{9,13},{1... | collective-permute-start | bytes 884744 | tf_op jit(solution)/shard_map/ppermute | solution.py:351
  10.8 0.3 collective-permute-start.13
  11.0 0.8 %collective-permute-start.3 = (bf16[2,192,128]{2,1,0:T(8,128)(2,1)S(1)}, bf16[2,192,128]{2,1,0:T(8,128)(2,1)S(1)}, u32[]{:S(2)}, u32[]{:S(2)}) collective-permute-start(bf16[2,192,128]{2,1,0:T(8,128)(2,1)S(1)} %get-tuple-element.68), channel_id=1, source_target_pairs={{1,0},{0,1},{3,2},{2,3},{5,4},{4,5},{7,6},{6,7},{9,8},{8,9},{11,10... | collective-permute-start | bytes 294920 | tf_op jit(solution)/shard_map/ppermute | solution.py:345
  11.8 1.9 %collective-permute-start.9 = (bf16[2,192,384]{2,1,0:T(8,128)(2,1)S(1)}, bf16[2,192,384]{2,1,0:T(8,128)(2,1)S(1)}, u32[]{:S(2)}, u32[]{:S(2)}) collective-permute-start(bf16[2,192,384]{2,1,0:T(8,128)(2,1)S(1)} %get-tuple-element.75), channel_id=1, source_target_pairs={{0,12},{1,13},{2,14},{3,15},{4,0},{5,1},{6,2},{7,3},{8,4},{9,5},{1... | collective-permute-start | bytes 884744 | tf_op jit(solution)/shard_map/ppermute | solution.py:352
  13.7 1.3 %collective-permute-start.4 = (bf16[2,192,128]{2,1,0:T(8,128)(2,1)S(1)}, bf16[2,192,128]{2,1,0:T(8,128)(2,1)S(1)}, u32[]{:S(2)}, u32[]{:S(2)}) collective-permute-start(bf16[2,192,128]{2,1,0:T(8,128)(2,1)S(1)} %get-tuple-element.69), channel_id=1, source_target_pairs={{2,0},{3,1},{0,2},{1,3},{6,4},{7,5},{4,6},{5,7},{10,8},{11,9},{8,1... | collective-permute-start | bytes 294920 | tf_op jit(solution)/shard_map/ppermute | solution.py:345
  15.0 0.6 collective-permute-start.5
  15.6 3.2 %collective-permute-done.4.refs_2_ = bf16[2,192,128]{2,1,0:T(8,128)(2,1)S(1)} collective-permute-done((bf16[2,192,128]{2,1,0:T(8,128)(2,1)S(1)}, bf16[2,192,128]{2,1,0:T(8,128)(2,1)S(1)}, u32[]{:S(2)}, u32[]{:S(2)}) %collective-permute-start.4) | collective-permute-done | bytes 98336 | tf_op jit(solution)/shard_map/ppermute | solution.py:345
  18.8 2.3 %collective-permute-start.12 = (bf16[128,768]{1,0:T(8,128)(2,1)S(1)}, bf16[128,768]{1,0:T(8,128)(2,1)S(1)}, u32[]{:S(2)}, u32[]{:S(2)}) collective-permute-start(bf16[128,768]{1,0:T(8,128)(2,1)S(1)} %bitcast.11), channel_id=1, source_target_pairs={{1,0},{0,1},{3,2},{2,3},{5,4},{4,5},{7,6},{6,7},{9,8},{8,9},{11,10... | collective-permute-start | bytes 589832 | tf_op jit(solution)/shard_map/ppermute | solution.py:345
  21.2 0.1 copy.13.ids_ref
  21.3 1.2 %live.1 = (f32[16,512]{1,0:T(8,128)S(1)}, f32[8,384]{1,0:T(8,128)S(1)}) custom-call(s32[16,6]{1,0:T(8,128)S(1)} %copy.13.ids_ref, s32[16]{0:T(128)S(1)} %copy-done.5), custom_call_target="tpu_custom_call" | custom-call | flops 1 | bytes 1 | tf_op jit(solution)/shard_map/live/pallas_call | solution.py:50
  22.5 0.1 gather.3
  22.7 1.3 %collective-permute-start.6 = (bf16[2,192,384]{2,1,0:T(8,128)(2,1)S(1)}, bf16[2,192,384]{2,1,0:T(8,128)(2,1)S(1)}, u32[]{:S(2)}, u32[]{:S(2)}) collective-permute-start(bf16[2,192,384]{2,1,0:T(8,128)(2,1)S(1)} %get-tuple-element.72), channel_id=1, source_target_pairs={{0,4},{1,5},{2,6},{3,7},{4,8},{5,9},{6,10},{7,11},{8,12},{9,13},{1... | collective-permute-start | bytes 884744 | tf_op jit(solution)/shard_map/ppermute | solution.py:351
  24.0 2.0 %collective-permute-start.7 = (bf16[2,192,384]{2,1,0:T(8,128)(2,1)S(1)}, bf16[2,192,384]{2,1,0:T(8,128)(2,1)S(1)}, u32[]{:S(2)}, u32[]{:S(2)}) collective-permute-start(bf16[2,192,384]{2,1,0:T(8,128)(2,1)S(1)} %get-tuple-element.73), channel_id=1, source_target_pairs={{0,12},{1,13},{2,14},{3,15},{4,0},{5,1},{6,2},{7,3},{8,4},{9,5},{1... | collective-permute-start | bytes 884744 | tf_op jit(solution)/shard_map/ppermute | solution.py:352
  26.0 0.7 collective-permute-done.9.high_ref
  26.6 3.2 %forward.1 = (bf16[192,512]{1,0:T(8,128)(2,1)S(1)}, f32[8,512]{1,0:T(8,128)S(1)}, f32[16,384]{1,0:T(8,128)S(1)}, f32[16,384]{1,0:T(8,128)S(1)}, bf16[3,1280,512]...) custom-call(bf16[2,192,512]{2,1,0:T(8,128)(2,1)S(1)} %get-tuple-element.61.pair_ref, ...), custom_call_target="tpu_custom_call" | custom-call | flops 1 | bytes 1 | tf_op jit(solution)/shard_map/forward/pallas_call | solution.py:50
  29.9 0.5 weight.1
  30.3 1.3 %collective-permute-start.18 = (bf16[96,768]{1,0:T(8,128)(2,1)S(1)}, bf16[96,768]{1,0:T(8,128)(2,1)S(1)}, u32[]{:S(2)}, u32[]{:S(2)}) collective-permute-start(bf16[96,768]{1,0:T(8,128)(2,1)S(1)} %get-tuple-element.86.refs_4_), channel_id=1, source_target_pairs={{0,16},{16,0},{1,17},{17,1},{2,18},{18,2},{3,19},{19,3},{4,20},{20... | collective-permute-start | bytes 442376 | tf_op jit(solution)/shard_map/ppermute | solution.py:356
  31.6 0.3 collective-permute-start.10
  31.9 3.0 %collective-permute-start.11 = (f32[16,384]{1,0:T(8,128)S(1)}, f32[16,384]{1,0:T(8,128)S(1)}, u32[]{:S(2)}, u32[]{:S(2)}) collective-permute-start(f32[16,384]{1,0:T(8,128)S(1)} %get-tuple-element.78), channel_id=1, source_target_pairs={{0,12},{1,13},{2,14},{3,15},{4,0},{5,1},{6,2},{7,3},{8,4},{9,5},{1... | collective-permute-start | bytes 73736 | tf_op jit(solution)/shard_map/ppermute | solution.py:352
  34.9 2.4 %query_grad.1 = (bf16[192,512]{1,0:T(8,128)(2,1)S(1)}, f32[2,192,512]{2,1,0:T(8,128)S(1)}, f32[8,128]{1,0:T(8,128)S(1)}) custom-call(bf16[2,192,1280]{2,1,0:T(8,128)(2,1)S(1)} %get-tuple-element.80.refs_0_, bf16[3,1280,512]{2,1,0:T(8,128)(2,1)S(1)} %get-tuple-element.81.refs_1_, bf16[2,192,512]{2,1,0:T(8,128)(2,1)S(1)} %get-tuple-element.76.query_ref.refs_2_, ...), custom_call_target="tpu_custom_call" | custom-call | flops 1 | bytes 1 | tf_op jit(solution)/shard_map/query_grad/pallas_call | solution.py:50
  37.4 0.1 collective-permute-start.19
  37.5 1.7 %collective-permute-done.10.stats_low = f32[16,384]{1,0:T(8,128)S(1)} collective-permute-done((f32[16,384]{1,0:T(8,128)S(1)}, f32[16,384]{1,0:T(8,128)S(1)}, u32[]{:S(2)}, u32[]{:S(2)}) %collective-permute-start.10) | collective-permute-done | bytes 24608 | tf_op jit(solution)/shard_map/ppermute | solution.py:351
  39.2 0.3 collective-permute-done.11.stats_high
  39.5 1.9 %key_grad.1 = (bf16[4,192,128]{2,1,0:T(8,128)(2,1)S(1)}, bf16[4,192,128]{2,1,0:T(8,128)(2,1)S(1)}, bf16[4,192,128]{2,1,0:T(8,128)(2,1)S(1)}, bf16[4,192,128]{2,1,0:T(8,128)(2,1)S(1)}, f32[8,128]{1,0:T(8,128)S(1)}) custom-call(bf16[2,192,512]{2,1,0:T(8,128)(2,1)S(1)} %get-tuple-element.61.pair_ref, bf16[2,192,384]{2,1,0:T(8,128)(2,1)S(1)} %collective-permute-done.6.low_ref, ...), custom_call_target="tpu_custom_call" | custom-call | flops 1 | bytes 1 | tf_op jit(solution)/shard_map/key_grad/pallas_call | solution.py:50
  41.4 2.3 %collective-permute-start.15 = (bf16[4,192,128]{2,1,0:T(8,128)(2,1)S(1)}, bf16[4,192,128]{2,1,0:T(8,128)(2,1)S(1)}, u32[]{:S(2)}, u32[]{:S(2)}) collective-permute-start(bf16[4,192,128]{2,1,0:T(8,128)(2,1)S(1)} %get-tuple-element.90), channel_id=1, source_target_pairs={{1,0},{0,1},{3,2},{2,3},{5,4},{4,5},{7,6},{6,7},{9,8},{8,9},{11,10... | collective-permute-start | bytes 589832 | tf_op jit(solution)/shard_map/ppermute | solution.py:345
  43.8 1.7 %collective-permute-start.17 = (bf16[4,192,128]{2,1,0:T(8,128)(2,1)S(1)}, bf16[4,192,128]{2,1,0:T(8,128)(2,1)S(1)}, u32[]{:S(2)}, u32[]{:S(2)}) collective-permute-start(bf16[4,192,128]{2,1,0:T(8,128)(2,1)S(1)} %get-tuple-element.92), channel_id=1, source_target_pairs={{3,0},{2,1},{1,2},{0,3},{7,4},{6,5},{5,6},{4,7},{11,8},{10,9},{9,1... | collective-permute-start | bytes 589832 | tf_op jit(solution)/shard_map/ppermute | solution.py:345
  45.5 0.7 %collective-permute-start.20 = (bf16[48,768]{1,0:T(8,128)(2,1)S(1)}, bf16[48,768]{1,0:T(8,128)(2,1)S(1)}, u32[]{:S(2)}, u32[]{:S(2)}) collective-permute-start(bf16[48,768]{1,0:T(8,128)(2,1)S(1)} %add.2.part_ref), channel_id=1, source_target_pairs={{8,0},{9,1},{10,2},{11,3},{12,4},{13,5},{14,6},{15,7},{0,8},{1,9},... | collective-permute-start | bytes 221192 | tf_op jit(solution)/shard_map/ppermute | solution.py:345
  46.2 5.9 %collective-permute-done.20.got_ref = bf16[48,768]{1,0:T(8,128)(2,1)S(1)} collective-permute-done((bf16[48,768]{1,0:T(8,128)(2,1)S(1)}, bf16[48,768]{1,0:T(8,128)(2,1)S(1)}, u32[]{:S(2)}, u32[]{:S(2)}) %collective-permute-start.20) | collective-permute-done | bytes 73760 | tf_op jit(solution)/shard_map/ppermute | solution.py:345
  52.1 0.1 collective-permute-start.21
  52.2 2.4 %collective-permute-done.17.refs_3_.refs_4_ = bf16[4,192,128]{2,1,0:T(8,128)(2,1)S(1)} collective-permute-done((bf16[4,192,128]{2,1,0:T(8,128)(2,1)S(1)}, bf16[4,192,128]{2,1,0:T(8,128)(2,1)S(1)}, u32[]{:S(2)}, u32[]{:S(2)}) %collective-permute-start.17) | collective-permute-done | bytes 196640 | tf_op jit(solution)/shard_map/ppermute | solution.py:345
  54.6 0.8 %collective-permute-done.21.refs_1_ = bf16[48,768]{1,0:T(8,128)(2,1)S(1)} collective-permute-done((bf16[48,768]{1,0:T(8,128)(2,1)S(1)}, bf16[48,768]{1,0:T(8,128)(2,1)S(1)}, u32[]{:S(2)}, u32[]{:S(2)}) %collective-permute-start.21) | collective-permute-done | bytes 73760 | tf_op jit(solution)/shard_map/ppermute | solution.py:345
  55.4 0.9 %collective-permute-start.22 = (bf16[96,768]{1,0:T(8,128)(2,1)S(1)}, bf16[96,768]{1,0:T(8,128)(2,1)S(1)}, u32[]{:S(2)}, u32[]{:S(2)}) collective-permute-start(bf16[96,768]{1,0:T(8,128)(2,1)S(1)} %join.1.refs_0_), channel_id=1, source_target_pairs={{0,2},{1,3},{2,18},{3,19},{4,6},{5,7},{6,22},{7,23},{8,10},{9,11},... | collective-permute-start | bytes 442376 | tf_op jit(solution)/shard_map/ppermute | solution.py:474
  56.3 1.9 %collective-permute-start.23 = (bf16[96,768]{1,0:T(8,128)(2,1)S(1)}, bf16[96,768]{1,0:T(8,128)(2,1)S(1)}, u32[]{:S(2)}, u32[]{:S(2)}) collective-permute-start(bf16[96,768]{1,0:T(8,128)(2,1)S(1)} %join.1.refs_0_), channel_id=1, source_target_pairs={{2,16},{3,17},{6,20},{7,21},{10,24},{11,25},{14,28},{15,29},{16,2}... | collective-permute-start | bytes 442376 | tf_op jit(solution)/shard_map/ppermute | solution.py:474
  58.2 1.2 %output.1 = (bf16[128,768]{1,0:T(8,128)(2,1)}, bf16[128,768]{1,0:T(8,128)(2,1)}, bf16[128,768]{1,0:T(8,128)(2,1)}, bf16[128,768]{1,0:T(8,128)(2,1)}, f32[8,128]{1,0:T(8,128)S(1)}) custom-call(bf16[4,192,128]{2,1,0:T(8,128)(2,1)S(1)} %get-tuple-element.89.refs_0_, bf16[4,192,128]{2,1,0:T(8,128)(2,1)S(1)} %collective-permute-done.15.refs_1_.refs_2_, ...), custom_call_target="tpu_custom_call" | custom-call | flops 1 | bytes 1 | tf_op jit(solution)/shard_map/output/pallas_call | solution.py:50
  59.4 3.7 %collective-permute-done.23.refs_2_ = bf16[96,768]{1,0:T(8,128)(2,1)S(1)} collective-permute-done((bf16[96,768]{1,0:T(8,128)(2,1)S(1)}, bf16[96,768]{1,0:T(8,128)(2,1)S(1)}, u32[]{:S(2)}, u32[]{:S(2)}) %collective-permute-start.23) | collective-permute-done | bytes 147488 | tf_op jit(solution)/shard_map/ppermute | solution.py:474
  63.1 3.1 %collective-permute-start.24 = (bf16[192,768]{1,0:T(8,128)(2,1)S(1)}, bf16[192,768]{1,0:T(8,128)(2,1)S(1)}, u32[]{:S(2)}, u32[]{:S(2)}) collective-permute-start(bf16[192,768]{1,0:T(8,128)(2,1)S(1)} %cross.1.value_ref), channel_id=1, source_target_pairs={{1,0},{0,1},{3,2},{2,3},{5,4},{4,5},{7,6},{6,7},{9,8},{8,9},{11,10... | collective-permute-start | bytes 884744 | tf_op jit(solution)/shard_map/ppermute | solution.py:345
  66.2 0.9 %write.2.refs_0_ = f32[384,768]{1,0:T(8,128)} custom-call(bf16[192,768]{1,0:T(8,128)(2,1)S(1)} %cross.1.value_ref), custom_call_target="tpu_custom_call" | custom-call | flops 1 | bytes 1 | tf_op jit(solution)/shard_map/write/pallas_call | solution.py:479
  67.1 0.3 collective-permute-done.24.value_ref
  67.4 0.9 %write.3 = f32[384,768]{1,0:T(8,128)} custom-call(bf16[192,768]{1,0:T(8,128)(2,1)S(1)} %collective-permute-done.24.value_ref, f32[384,768]{1,0:T(8,128)} %write.2.refs_0_), custom_call_target="tpu_custom_call", output_to_operand_aliasing={{}: (1, {})} | custom-call | flops 1 | bytes 1 | tf_op jit(solution)/shard_map/write/pallas_call | solution.py:479
  (34 shorter events, 0.2 us)
Async XLA Ops:
  0.6 10.2 %copy-start.4 = (bf16[1,1,128,768]{3,2,1,0:T(8,128)(2,1)S(1)}, bf16[1,1,128,768]{3,2,1,0:T(8,128)(2,1)}, u32[]{:S(2)}) copy-start(bf16[1,1,128,768]{3,2,1,0:T(8,128)(2,1)} %param.10) | copy-start | bytes 589828
  0.6 20.5 %copy-start.6 = (s32[16,6]{0,1:T(8,128)S(1)}, s32[16,6]{0,1:T(8,128)}, u32[]{:S(2)}) copy-start(s32[16,6]{0,1:T(8,128)} %param.12) | copy-start | bytes 1156
  0.7 20.6 %copy-start.5 = (s32[16]{0:T(128)S(1)}, s32[16]{0:T(128)}, u32[]{:S(2)}) copy-start(s32[16]{0:T(128)} %count_ref.1) | copy-start | bytes 196
  1.9 6.1 %collective-permute-start = (bf16[2,192,128]{2,1,0:T(8,128)(2,1)S(1)}, bf16[2,192,128]{2,1,0:T(8,128)(2,1)S(1)}, u32[]{:S(2)}, u32[]{:S(2)}) collective-permute-start(bf16[2,192,128]{2,1,0:T(8,128)(2,1)S(1)} %get-tuple-element.58), channel_id=1, source_target_pairs={{1,0},{0,1},{3,2},{2,3},{5,4},{4,5},{7,6},{6,7},{9,8},{8,9},{11,10... | collective-permute-start | bytes 294920 | tf_op jit(solution)/shard_map/ppermute | solution.py:345
  2.6 5.4 %collective-permute-start.1 = (bf16[2,192,128]{2,1,0:T(8,128)(2,1)S(1)}, bf16[2,192,128]{2,1,0:T(8,128)(2,1)S(1)}, u32[]{:S(2)}, u32[]{:S(2)}) collective-permute-start(bf16[2,192,128]{2,1,0:T(8,128)(2,1)S(1)} %get-tuple-element.59), channel_id=1, source_target_pairs={{2,0},{3,1},{0,2},{1,3},{6,4},{7,5},{4,6},{5,7},{10,8},{11,9},{8,1... | collective-permute-start | bytes 294920 | tf_op jit(solution)/shard_map/ppermute | solution.py:345
  2.6 6.6 %collective-permute-start.2 = (bf16[2,192,128]{2,1,0:T(8,128)(2,1)S(1)}, bf16[2,192,128]{2,1,0:T(8,128)(2,1)S(1)}, u32[]{:S(2)}, u32[]{:S(2)}) collective-permute-start(bf16[2,192,128]{2,1,0:T(8,128)(2,1)S(1)} %get-tuple-element.60), channel_id=1, source_target_pairs={{3,0},{2,1},{1,2},{0,3},{7,4},{6,5},{5,6},{4,7},{11,8},{10,9},{9,1... | collective-permute-start | bytes 294920 | tf_op jit(solution)/shard_map/ppermute | solution.py:345
  4.4 1.3 %copy-start = (bf16[768,768]{1,0:T(8,128)(2,1)S(1)}, bf16[768,768]{1,0:T(8,128)(2,1)}, u32[]{:S(2)}) copy-start(bf16[768,768]{1,0:T(8,128)(2,1)} %refs_4_.1) | copy-start | bytes 3538948
  5.6 0.9 %copy-start.2 = (bf16[1,1,128,768]{3,2,1,0:T(8,128)(2,1)S(1)}, bf16[1,1,128,768]{3,2,1,0:T(8,128)(2,1)}, u32[]{:S(2)}) copy-start(bf16[1,1,128,768]{3,2,1,0:T(8,128)(2,1)} %param.7) | copy-start | bytes 589828
  6.5 0.9 %copy-start.3 = (bf16[1,1,128,768]{3,2,1,0:T(8,128)(2,1)S(1)}, bf16[1,1,128,768]{3,2,1,0:T(8,128)(2,1)}, u32[]{:S(2)}) copy-start(bf16[1,1,128,768]{3,2,1,0:T(8,128)(2,1)} %param.10) | copy-start | bytes 589828
  9.4 14.6 %collective-permute-start.8 = (bf16[2,192,384]{2,1,0:T(8,128)(2,1)S(1)}, bf16[2,192,384]{2,1,0:T(8,128)(2,1)S(1)}, u32[]{:S(2)}, u32[]{:S(2)}) collective-permute-start(bf16[2,192,384]{2,1,0:T(8,128)(2,1)S(1)} %get-tuple-element.74), channel_id=1, source_target_pairs={{0,4},{1,5},{2,6},{3,7},{4,8},{5,9},{6,10},{7,11},{8,12},{9,13},{1... | collective-permute-start | bytes 884744 | tf_op jit(solution)/shard_map/ppermute | solution.py:351
  10.8 10.4 %collective-permute-start.13 = (bf16[128,768]{1,0:T(8,128)(2,1)S(1)}, bf16[128,768]{1,0:T(8,128)(2,1)S(1)}, u32[]{:S(2)}, u32[]{:S(2)}) collective-permute-start(bf16[128,768]{1,0:T(8,128)(2,1)S(1)} %bitcast.10), channel_id=1, source_target_pairs={{2,0},{3,1},{0,2},{1,3},{6,4},{7,5},{4,6},{5,7},{10,8},{11,9},{8,1... | collective-permute-start | bytes 589832 | tf_op jit(solution)/shard_map/ppermute | solution.py:345
  11.0 4.0 %collective-permute-start.3 = (bf16[2,192,128]{2,1,0:T(8,128)(2,1)S(1)}, bf16[2,192,128]{2,1,0:T(8,128)(2,1)S(1)}, u32[]{:S(2)}, u32[]{:S(2)}) collective-permute-start(bf16[2,192,128]{2,1,0:T(8,128)(2,1)S(1)} %get-tuple-element.68), channel_id=1, source_target_pairs={{1,0},{0,1},{3,2},{2,3},{5,4},{4,5},{7,6},{6,7},{9,8},{8,9},{11,10... | collective-permute-start | bytes 294920 | tf_op jit(solution)/shard_map/ppermute | solution.py:345
  11.8 14.8 %collective-permute-start.9 = (bf16[2,192,384]{2,1,0:T(8,128)(2,1)S(1)}, bf16[2,192,384]{2,1,0:T(8,128)(2,1)S(1)}, u32[]{:S(2)}, u32[]{:S(2)}) collective-permute-start(bf16[2,192,384]{2,1,0:T(8,128)(2,1)S(1)} %get-tuple-element.75), channel_id=1, source_target_pairs={{0,12},{1,13},{2,14},{3,15},{4,0},{5,1},{6,2},{7,3},{8,4},{9,5},{1... | collective-permute-start | bytes 884744 | tf_op jit(solution)/shard_map/ppermute | solution.py:352
  13.7 5.1 %collective-permute-start.4 = (bf16[2,192,128]{2,1,0:T(8,128)(2,1)S(1)}, bf16[2,192,128]{2,1,0:T(8,128)(2,1)S(1)}, u32[]{:S(2)}, u32[]{:S(2)}) collective-permute-start(bf16[2,192,128]{2,1,0:T(8,128)(2,1)S(1)} %get-tuple-element.69), channel_id=1, source_target_pairs={{2,0},{3,1},{0,2},{1,3},{6,4},{7,5},{4,6},{5,7},{10,8},{11,9},{8,1... | collective-permute-start | bytes 294920 | tf_op jit(solution)/shard_map/ppermute | solution.py:345
  15.0 7.5 %collective-permute-start.5 = (bf16[2,192,128]{2,1,0:T(8,128)(2,1)S(1)}, bf16[2,192,128]{2,1,0:T(8,128)(2,1)S(1)}, u32[]{:S(2)}, u32[]{:S(2)}) collective-permute-start(bf16[2,192,128]{2,1,0:T(8,128)(2,1)S(1)} %get-tuple-element.70), channel_id=1, source_target_pairs={{3,0},{2,1},{1,2},{0,3},{7,4},{6,5},{5,6},{4,7},{11,8},{10,9},{9,1... | collective-permute-start | bytes 294920 | tf_op jit(solution)/shard_map/ppermute | solution.py:345
  18.8 11.0 %collective-permute-start.12 = (bf16[128,768]{1,0:T(8,128)(2,1)S(1)}, bf16[128,768]{1,0:T(8,128)(2,1)S(1)}, u32[]{:S(2)}, u32[]{:S(2)}) collective-permute-start(bf16[128,768]{1,0:T(8,128)(2,1)S(1)} %bitcast.11), channel_id=1, source_target_pairs={{1,0},{0,1},{3,2},{2,3},{5,4},{4,5},{7,6},{6,7},{9,8},{8,9},{11,10... | collective-permute-start | bytes 589832 | tf_op jit(solution)/shard_map/ppermute | solution.py:345
  21.2 8.7 %collective-permute-start.14 = (bf16[128,768]{1,0:T(8,128)(2,1)S(1)}, bf16[128,768]{1,0:T(8,128)(2,1)S(1)}, u32[]{:S(2)}, u32[]{:S(2)}) collective-permute-start(bf16[128,768]{1,0:T(8,128)(2,1)S(1)} %collective-permute-done.13.refs_2_), channel_id=1, source_target_pairs={{1,0},{0,1},{3,2},{2,3},{5,4},{4,5},{7,6},{6,7},{9,8},{8,9},{11,10... | collective-permute-start | bytes 589832 | tf_op jit(solution)/shard_map/ppermute | solution.py:345
  22.7 16.9 %collective-permute-start.6 = (bf16[2,192,384]{2,1,0:T(8,128)(2,1)S(1)}, bf16[2,192,384]{2,1,0:T(8,128)(2,1)S(1)}, u32[]{:S(2)}, u32[]{:S(2)}) collective-permute-start(bf16[2,192,384]{2,1,0:T(8,128)(2,1)S(1)} %get-tuple-element.72), channel_id=1, source_target_pairs={{0,4},{1,5},{2,6},{3,7},{4,8},{5,9},{6,10},{7,11},{8,12},{9,13},{1... | collective-permute-start | bytes 884744 | tf_op jit(solution)/shard_map/ppermute | solution.py:351
  24.0 15.5 %collective-permute-start.7 = (bf16[2,192,384]{2,1,0:T(8,128)(2,1)S(1)}, bf16[2,192,384]{2,1,0:T(8,128)(2,1)S(1)}, u32[]{:S(2)}, u32[]{:S(2)}) collective-permute-start(bf16[2,192,384]{2,1,0:T(8,128)(2,1)S(1)} %get-tuple-element.73), channel_id=1, source_target_pairs={{0,12},{1,13},{2,14},{3,15},{4,0},{5,1},{6,2},{7,3},{8,4},{9,5},{1... | collective-permute-start | bytes 884744 | tf_op jit(solution)/shard_map/ppermute | solution.py:352
  30.3 7.0 %collective-permute-start.18 = (bf16[96,768]{1,0:T(8,128)(2,1)S(1)}, bf16[96,768]{1,0:T(8,128)(2,1)S(1)}, u32[]{:S(2)}, u32[]{:S(2)}) collective-permute-start(bf16[96,768]{1,0:T(8,128)(2,1)S(1)} %get-tuple-element.86.refs_4_), channel_id=1, source_target_pairs={{0,16},{16,0},{1,17},{17,1},{2,18},{18,2},{3,19},{19,3},{4,20},{20... | collective-permute-start | bytes 442376 | tf_op jit(solution)/shard_map/ppermute | solution.py:356
  31.6 7.6 %collective-permute-start.10 = (f32[16,384]{1,0:T(8,128)S(1)}, f32[16,384]{1,0:T(8,128)S(1)}, u32[]{:S(2)}, u32[]{:S(2)}) collective-permute-start(f32[16,384]{1,0:T(8,128)S(1)} %get-tuple-element.77), channel_id=1, source_target_pairs={{0,4},{1,5},{2,6},{3,7},{4,8},{5,9},{6,10},{7,11},{8,12},{9,13},{1... | collective-permute-start | bytes 73736 | tf_op jit(solution)/shard_map/ppermute | solution.py:351
  31.9 7.6 %collective-permute-start.11 = (f32[16,384]{1,0:T(8,128)S(1)}, f32[16,384]{1,0:T(8,128)S(1)}, u32[]{:S(2)}, u32[]{:S(2)}) collective-permute-start(f32[16,384]{1,0:T(8,128)S(1)} %get-tuple-element.78), channel_id=1, source_target_pairs={{0,12},{1,13},{2,14},{3,15},{4,0},{5,1},{6,2},{7,3},{8,4},{9,5},{1... | collective-permute-start | bytes 73736 | tf_op jit(solution)/shard_map/ppermute | solution.py:352
  37.4 8.1 %collective-permute-start.19 = (bf16[48,768]{1,0:T(8,128)(2,1)S(1)}, bf16[48,768]{1,0:T(8,128)(2,1)S(1)}, u32[]{:S(2)}, u32[]{:S(2)}) collective-permute-start(bf16[48,768]{1,0:T(8,128)(2,1)S(1)} %get-tuple-element.100), channel_id=1, source_target_pairs={{4,0},{5,1},{6,2},{7,3},{0,4},{1,5},{2,6},{3,7},{12,8},{13,9},{14,... | collective-permute-start | bytes 221192 | tf_op jit(solution)/shard_map/ppermute | solution.py:345
  41.4 16.8 %copy-start.1 = (bf16[768,768]{1,0:T(8,128)(2,1)S(1)}, bf16[768,768]{1,0:T(8,128)(2,1)}, u32[]{:S(2)}) copy-start(bf16[768,768]{1,0:T(8,128)(2,1)} %refs_4_.1) | copy-start | bytes 3538948
  41.4 10.8 %collective-permute-start.15 = (bf16[4,192,128]{2,1,0:T(8,128)(2,1)S(1)}, bf16[4,192,128]{2,1,0:T(8,128)(2,1)S(1)}, u32[]{:S(2)}, u32[]{:S(2)}) collective-permute-start(bf16[4,192,128]{2,1,0:T(8,128)(2,1)S(1)} %get-tuple-element.90), channel_id=1, source_target_pairs={{1,0},{0,1},{3,2},{2,3},{5,4},{4,5},{7,6},{6,7},{9,8},{8,9},{11,10... | collective-permute-start | bytes 589832 | tf_op jit(solution)/shard_map/ppermute | solution.py:345
  43.7 8.4 %collective-permute-start.16 = (bf16[4,192,128]{2,1,0:T(8,128)(2,1)S(1)}, bf16[4,192,128]{2,1,0:T(8,128)(2,1)S(1)}, u32[]{:S(2)}, u32[]{:S(2)}) collective-permute-start(bf16[4,192,128]{2,1,0:T(8,128)(2,1)S(1)} %get-tuple-element.91), channel_id=1, source_target_pairs={{2,0},{3,1},{0,2},{1,3},{6,4},{7,5},{4,6},{5,7},{10,8},{11,9},{8,1... | collective-permute-start | bytes 589832 | tf_op jit(solution)/shard_map/ppermute | solution.py:345
  43.8 10.9 %collective-permute-start.17 = (bf16[4,192,128]{2,1,0:T(8,128)(2,1)S(1)}, bf16[4,192,128]{2,1,0:T(8,128)(2,1)S(1)}, u32[]{:S(2)}, u32[]{:S(2)}) collective-permute-start(bf16[4,192,128]{2,1,0:T(8,128)(2,1)S(1)} %get-tuple-element.92), channel_id=1, source_target_pairs={{3,0},{2,1},{1,2},{0,3},{7,4},{6,5},{5,6},{4,7},{11,8},{10,9},{9,1... | collective-permute-start | bytes 589832 | tf_op jit(solution)/shard_map/ppermute | solution.py:345
  45.5 6.6 %collective-permute-start.20 = (bf16[48,768]{1,0:T(8,128)(2,1)S(1)}, bf16[48,768]{1,0:T(8,128)(2,1)S(1)}, u32[]{:S(2)}, u32[]{:S(2)}) collective-permute-start(bf16[48,768]{1,0:T(8,128)(2,1)S(1)} %add.2.part_ref), channel_id=1, source_target_pairs={{8,0},{9,1},{10,2},{11,3},{12,4},{13,5},{14,6},{15,7},{0,8},{1,9},... | collective-permute-start | bytes 221192 | tf_op jit(solution)/shard_map/ppermute | solution.py:345
  52.1 3.3 %collective-permute-start.21 = (bf16[48,768]{1,0:T(8,128)(2,1)S(1)}, bf16[48,768]{1,0:T(8,128)(2,1)S(1)}, u32[]{:S(2)}, u32[]{:S(2)}) collective-permute-start(bf16[48,768]{1,0:T(8,128)(2,1)S(1)} %add.3.refs_0_), channel_id=1, source_target_pairs={{4,0},{5,1},{6,2},{7,3},{0,4},{1,5},{2,6},{3,7},{12,8},{13,9},{14,... | collective-permute-start | bytes 221192 | tf_op jit(solution)/shard_map/ppermute | solution.py:345
  55.4 4.0 %collective-permute-start.22 = (bf16[96,768]{1,0:T(8,128)(2,1)S(1)}, bf16[96,768]{1,0:T(8,128)(2,1)S(1)}, u32[]{:S(2)}, u32[]{:S(2)}) collective-permute-start(bf16[96,768]{1,0:T(8,128)(2,1)S(1)} %join.1.refs_0_), channel_id=1, source_target_pairs={{0,2},{1,3},{2,18},{3,19},{4,6},{5,7},{6,22},{7,23},{8,10},{9,11},... | collective-permute-start | bytes 442376 | tf_op jit(solution)/shard_map/ppermute | solution.py:474
  56.3 6.8 %collective-permute-start.23 = (bf16[96,768]{1,0:T(8,128)(2,1)S(1)}, bf16[96,768]{1,0:T(8,128)(2,1)S(1)}, u32[]{:S(2)}, u32[]{:S(2)}) collective-permute-start(bf16[96,768]{1,0:T(8,128)(2,1)S(1)} %join.1.refs_0_), channel_id=1, source_target_pairs={{2,16},{3,17},{6,20},{7,21},{10,24},{11,25},{14,28},{15,29},{16,2}... | collective-permute-start | bytes 442376 | tf_op jit(solution)/shard_map/ppermute | solution.py:474
  63.1 4.3 %collective-permute-start.24 = (bf16[192,768]{1,0:T(8,128)(2,1)S(1)}, bf16[192,768]{1,0:T(8,128)(2,1)S(1)}, u32[]{:S(2)}, u32[]{:S(2)}) collective-permute-start(bf16[192,768]{1,0:T(8,128)(2,1)S(1)} %cross.1.value_ref), channel_id=1, source_target_pairs={{1,0},{0,1},{3,2},{2,3},{5,4},{4,5},{7,6},{6,7},{9,8},{8,9},{11,10... | collective-permute-start | bytes 884744 | tf_op jit(solution)/shard_map/ppermute | solution.py:345

commit v17 on v16

--- a/solution.py
+++ b/solution.py
@@ -297,20 +297,20 @@
     keep_ref[...] = dot(mixed_ref[keep], right[...], NN)
 
 
-def split_kernel(stride, part_ref, got_ref, send_ref, keep_ref):
-    send, keep = halves(bit_of(stride), send_ref.shape[0])
-    send_ref[...] = (part_ref[send] + got_ref[send].astype(f32)).astype(bf16)
-    keep_ref[...] = part_ref[keep] + got_ref[keep].astype(f32)
+def split_kernel(part_ref, got_ref, top_ref, bottom_ref):
+    half = top_ref.shape[0]
+    for out, at in ((top_ref, slice(0, half)), (bottom_ref, slice(half, 2 * half))):
+        out[...] = (part_ref[at] + got_ref[at].astype(f32)).astype(bf16)
+
+
+def meet_kernel(top_ref, bottom_ref, got_top, got_bottom, out_ref):
+    half = top_ref.shape[0]
+    for n, (mine, got) in enumerate(((top_ref, got_top), (bottom_ref, got_bottom))):
+        out_ref[n * half : (n + 1) * half] = (mine[...].astype(f32) + got[...].astype(f32)).astype(bf16)
 
 
 def round_kernel(part_ref, got_ref, out_ref):
     out_ref[...] = (part_ref[...].astype(f32) + got_ref[...].astype(f32)).astype(bf16)
-
-
-def join_kernel(stride, mine_ref, got_ref, out_ref):
-    other, here = halves(bit_of(stride), mine_ref.shape[0])
-    out_ref[here] = mine_ref[...]
-    out_ref[other] = got_ref[...]
 
 
 def write_kernel(own, scale, value_ref, *refs):
@@ -439,27 +439,23 @@
 
     scale = 1.0 / math.sqrt(span * windows * stations)
     if windows == 2:
-        count = rows // 4
+        count = rows // 2
         got = other_window(send)
-        send, part = call(
-            functools.partial(split_kernel, LAYER), [VMEM] * 2,
-            [shape_of(count, width), shape_of(count, width, dtype=f32)],
-            (part, got), name="split", after=(query_token,),
+        top, bottom = call(
+            split_kernel, [VMEM] * 2, [shape_of(count // 2, width)] * 2, (part, got), name="split",
+            after=(query_token,),
         )
-
-        def add_round(part, got, after=()):
-            out = [shape_of(count, width)]
-            return call(round_kernel, [VMEM] * 2, out, (part, got), name="add", after=after)[0]
-
-        total = add_round(part, swap(send, LAYER), (key_token,))
+        (total,) = call(
+            meet_kernel, [VMEM] * 4, [shape_of(count, width)],
+            (top, bottom, swap(top, LAYER), swap(bottom, LAYER)), name="meet", after=(key_token,),
+        )
         stride = 2 * LAYER
         while stride < stations:
-            total = add_round(total, swap(total, stride))
+            (total,) = call(
+                round_kernel, [VMEM] * 2, [shape_of(count, width)], (total, swap(total, stride)),
+                name="add", after=parts if 2 * stride >= stations else (),
+            )
             stride *= 2
-        (total,) = call(
-            functools.partial(join_kernel, LAYER), [VMEM] * 2, [shape_of(2 * count, width)],
-            (total, swap(total, LAYER)), name="join", after=parts,
-        )
         first, second = [], []
         for w in range(2):
             for s in range(stations):
@@ -470,7 +466,7 @@
                     second.append((w * stations + s, (1 - w) * stations + (s ^ 2)))
         axes = ("dp", "station")
         (total,) = call(
-            cross_kernel, [VMEM] * 3, [shape_of(4 * count, width)],
+            cross_kernel, [VMEM] * 3, [shape_of(2 * count, width)],
             (total, lax.ppermute(total, axes, first), lax.ppermute(total, axes, second)),
             name="cross", after=(output_token,),
         )
@@ -480,8 +476,8 @@
                 functools.partial(write_kernel, own, scale),
                 in_specs=[VMEM] + [ANY] * len(grad_weight),
                 out_specs=ANY,
-                out_shape=shape_of(8 * count, width, dtype=f32),
-                scratch_shapes=[pltpu.VMEM((4 * count, width), f32), dma],
+                out_shape=shape_of(4 * count, width, dtype=f32),
+                scratch_shapes=[pltpu.VMEM((2 * count, width), f32), dma],
                 input_output_aliases={1: 0} if grad_weight else {},
                 compiler_params=pltpu.CompilerParams(vmem_limit_bytes=8 * MIB),
                 cost_estimate=pl.CostEstimate(flops=1, bytes_accessed=1, transcendentals=0),

time: 68.5 us -> 67.9 us (level)
  waiting for transfers between devices: 20.3 us -> 19 us
    ppermute x1, starting transfers between devices: 1.91 us -> 3.03 us  [local(): lax.ppermute(total, axes, second)]
    ppermute x1, waiting for transfers between devices: 3.65 us -> 2.53 us  [local(): lax.ppermute(total, axes, second)]
    pallas_call x15 -> x14, Pallas kernels: 12.5 us -> 12.5 us  [call(): pl.pallas_call(kernel, in_specs=ins, out_specs=[VMEM] * len(outs), out_sh...]
  transfers between devices with their start and end apart: 25 -> 25, of which waited for: 10 -> 9; matrix products, arithmetic and copies ran while one was open for 0% -> 0% of each run, Pallas kernels for 17% -> 18%
where the time goes in v17:
time: 67.9 us; the launch traced here: 67.6 us
  starting transfers between devices  30.3 us (45%)
  waiting for transfers between devices  19 us (28%)
  Pallas kernels  14.3 us (21%)
  local copies, waits for them, and re-layouts  3.23 us (5%)
  between operations  0.83 us (1%)
    ppermute x16, starting transfers between devices, swap(): lax.ppermute(value, 'station', [(s ^ stride, s) for s in range(stations)])  15.5 us
    ppermute x16, waiting for transfers between devices, swap(): lax.ppermute(value, 'station', [(s ^ stride, s) for s in range(stations)])  13.8 us
    pallas_call x14, Pallas kernels, call(): pl.pallas_call(kernel, in_specs=ins, out_specs=[VMEM] * len(outs), out_sh...  12.5 us
    ppermute x3, starting transfers between devices, along(): lax.ppermute(down, 'station', [(s, (s - LAYER) % stations) for s in range...  6.84 us
    unnamed x15, local copies, waits for them, and re-layouts  3.23 us
    ppermute x1, starting transfers between devices, local(): lax.ppermute(total, axes, second)  3.03 us
    ppermute x3, starting transfers between devices, along(): lax.ppermute(up, 'station', [(s, (s + LAYER) % stations) for s in range(s...  2.98 us
    ppermute x1, waiting for transfers between devices, local(): lax.ppermute(total, axes, second)  2.53 us
  transfers between devices with their start and end apart: 25, of which 9 were waited for; matrix products, arithmetic and copies ran while one was open for 0% of the time, Pallas kernels for 18%

profile of v17, /device:TPU:3, one launch (start us, length us, event | category | flops | bytes accessed | tf_op | source)
XLA Modules:
  0.0 67.6 jit_solution(17825813556689408717)
XLA Ops:
  0.7 1.2 %pack.1 = (bf16[2,192,128]{2,1,0:T(8,128)(2,1)S(1)}, bf16[2,192,128]{2,1,0:T(8,128)(2,1)S(1)}, bf16[2,192,128]{2,1,0:T(8,128)(2,1)S(1)}, bf16[2,192,128]{2,1,0:T(8,128)(2,1)S(1)}) custom-call(bf16[128,768]{1,0:T(8,128)(2,1)} %bitcast.12, bf16[128,768]{1,0:T(8,128)(2,1)} %bitcast.13), custom_call_target="tpu_custom_call" | custom-call | flops 1 | bytes 1 | tf_op jit(solution)/shard_map/pack/pallas_call | solution.py:50
  1.9 0.7 %collective-permute-start = (bf16[2,192,128]{2,1,0:T(8,128)(2,1)S(1)}, bf16[2,192,128]{2,1,0:T(8,128)(2,1)S(1)}, u32[]{:S(2)}, u32[]{:S(2)}) collective-permute-start(bf16[2,192,128]{2,1,0:T(8,128)(2,1)S(1)} %get-tuple-element.58), channel_id=1, source_target_pairs={{1,0},{0,1},{3,2},{2,3},{5,4},{4,5},{7,6},{6,7},{9,8},{8,9},{11,10... | collective-permute-start | bytes 294920 | tf_op jit(solution)/shard_map/ppermute | solution.py:345
  2.6 1.7 %collective-permute-start.2 = (bf16[2,192,128]{2,1,0:T(8,128)(2,1)S(1)}, bf16[2,192,128]{2,1,0:T(8,128)(2,1)S(1)}, u32[]{:S(2)}, u32[]{:S(2)}) collective-permute-start(bf16[2,192,128]{2,1,0:T(8,128)(2,1)S(1)} %get-tuple-element.60), channel_id=1, source_target_pairs={{3,0},{2,1},{1,2},{0,3},{7,4},{6,5},{5,6},{4,7},{11,8},{10,9},{9,1... | collective-permute-start | bytes 294920 | tf_op jit(solution)/shard_map/ppermute | solution.py:345
  4.4 1.3 %copy-done = bf16[768,768]{1,0:T(8,128)(2,1)S(1)} copy-done((bf16[768,768]{1,0:T(8,128)(2,1)S(1)}, bf16[768,768]{1,0:T(8,128)(2,1)}, u32[]{:S(2)}) %copy-start) | copy-done | bytes 1179672
  5.6 0.9 %copy-done.2 = bf16[1,1,128,768]{3,2,1,0:T(8,128)(2,1)S(1)} copy-done((bf16[1,1,128,768]{3,2,1,0:T(8,128)(2,1)S(1)}, bf16[1,1,128,768]{3,2,1,0:T(8,128)(2,1)}, u32[]{:S(2)}) %copy-start.2) | copy-done | bytes 196632
  6.6 0.9 %copy-done.3 = bf16[1,1,128,768]{3,2,1,0:T(8,128)(2,1)S(1)} copy-done((bf16[1,1,128,768]{3,2,1,0:T(8,128)(2,1)S(1)}, bf16[1,1,128,768]{3,2,1,0:T(8,128)(2,1)}, u32[]{:S(2)}) %copy-start.3) | copy-done | bytes 196632
  7.5 0.5 project.1
  8.0 1.3 %collective-permute-done.2.refs_3_ = bf16[2,192,128]{2,1,0:T(8,128)(2,1)S(1)} collective-permute-done((bf16[2,192,128]{2,1,0:T(8,128)(2,1)S(1)}, bf16[2,192,128]{2,1,0:T(8,128)(2,1)S(1)}, u32[]{:S(2)}, u32[]{:S(2)}) %collective-permute-start.2) | collective-permute-done | bytes 98336 | tf_op jit(solution)/shard_map/ppermute | solution.py:345
  9.3 0.1 gather.2
  9.4 1.3 %collective-permute-start.8 = (bf16[2,192,384]{2,1,0:T(8,128)(2,1)S(1)}, bf16[2,192,384]{2,1,0:T(8,128)(2,1)S(1)}, u32[]{:S(2)}, u32[]{:S(2)}) collective-permute-start(bf16[2,192,384]{2,1,0:T(8,128)(2,1)S(1)} %get-tuple-element.74), channel_id=1, source_target_pairs={{0,4},{1,5},{2,6},{3,7},{4,8},{5,9},{6,10},{7,11},{8,12},{9,13},{1... | collective-permute-start | bytes 884744 | tf_op jit(solution)/shard_map/ppermute | solution.py:351
  10.8 0.3 collective-permute-start.13
  11.0 0.8 %collective-permute-start.3 = (bf16[2,192,128]{2,1,0:T(8,128)(2,1)S(1)}, bf16[2,192,128]{2,1,0:T(8,128)(2,1)S(1)}, u32[]{:S(2)}, u32[]{:S(2)}) collective-permute-start(bf16[2,192,128]{2,1,0:T(8,128)(2,1)S(1)} %get-tuple-element.68), channel_id=1, source_target_pairs={{1,0},{0,1},{3,2},{2,3},{5,4},{4,5},{7,6},{6,7},{9,8},{8,9},{11,10... | collective-permute-start | bytes 294920 | tf_op jit(solution)/shard_map/ppermute | solution.py:345
  11.8 1.9 %collective-permute-start.9 = (bf16[2,192,384]{2,1,0:T(8,128)(2,1)S(1)}, bf16[2,192,384]{2,1,0:T(8,128)(2,1)S(1)}, u32[]{:S(2)}, u32[]{:S(2)}) collective-permute-start(bf16[2,192,384]{2,1,0:T(8,128)(2,1)S(1)} %get-tuple-element.75), channel_id=1, source_target_pairs={{0,12},{1,13},{2,14},{3,15},{4,0},{5,1},{6,2},{7,3},{8,4},{9,5},{1... | collective-permute-start | bytes 884744 | tf_op jit(solution)/shard_map/ppermute | solution.py:352
  13.7 1.3 %collective-permute-start.4 = (bf16[2,192,128]{2,1,0:T(8,128)(2,1)S(1)}, bf16[2,192,128]{2,1,0:T(8,128)(2,1)S(1)}, u32[]{:S(2)}, u32[]{:S(2)}) collective-permute-start(bf16[2,192,128]{2,1,0:T(8,128)(2,1)S(1)} %get-tuple-element.69), channel_id=1, source_target_pairs={{2,0},{3,1},{0,2},{1,3},{6,4},{7,5},{4,6},{5,7},{10,8},{11,9},{8,1... | collective-permute-start | bytes 294920 | tf_op jit(solution)/shard_map/ppermute | solution.py:345
  15.0 0.6 collective-permute-start.5
  15.6 3.2 %collective-permute-done.4.refs_2_ = bf16[2,192,128]{2,1,0:T(8,128)(2,1)S(1)} collective-permute-done((bf16[2,192,128]{2,1,0:T(8,128)(2,1)S(1)}, bf16[2,192,128]{2,1,0:T(8,128)(2,1)S(1)}, u32[]{:S(2)}, u32[]{:S(2)}) %collective-permute-start.4) | collective-permute-done | bytes 98336 | tf_op jit(solution)/shard_map/ppermute | solution.py:345
  18.8 2.3 %collective-permute-start.12 = (bf16[128,768]{1,0:T(8,128)(2,1)S(1)}, bf16[128,768]{1,0:T(8,128)(2,1)S(1)}, u32[]{:S(2)}, u32[]{:S(2)}) collective-permute-start(bf16[128,768]{1,0:T(8,128)(2,1)S(1)} %bitcast.11), channel_id=1, source_target_pairs={{1,0},{0,1},{3,2},{2,3},{5,4},{4,5},{7,6},{6,7},{9,8},{8,9},{11,10... | collective-permute-start | bytes 589832 | tf_op jit(solution)/shard_map/ppermute | solution.py:345
  21.2 0.1 copy.13.ids_ref
  21.3 1.2 %live.1 = (f32[16,512]{1,0:T(8,128)S(1)}, f32[8,384]{1,0:T(8,128)S(1)}) custom-call(s32[16,6]{1,0:T(8,128)S(1)} %copy.13.ids_ref, s32[16]{0:T(128)S(1)} %copy-done.5), custom_call_target="tpu_custom_call" | custom-call | flops 1 | bytes 1 | tf_op jit(solution)/shard_map/live/pallas_call | solution.py:50
  22.5 0.1 gather.3
  22.7 1.3 %collective-permute-start.6 = (bf16[2,192,384]{2,1,0:T(8,128)(2,1)S(1)}, bf16[2,192,384]{2,1,0:T(8,128)(2,1)S(1)}, u32[]{:S(2)}, u32[]{:S(2)}) collective-permute-start(bf16[2,192,384]{2,1,0:T(8,128)(2,1)S(1)} %get-tuple-element.72), channel_id=1, source_target_pairs={{0,4},{1,5},{2,6},{3,7},{4,8},{5,9},{6,10},{7,11},{8,12},{9,13},{1... | collective-permute-start | bytes 884744 | tf_op jit(solution)/shard_map/ppermute | solution.py:351
  24.0 2.0 %collective-permute-start.7 = (bf16[2,192,384]{2,1,0:T(8,128)(2,1)S(1)}, bf16[2,192,384]{2,1,0:T(8,128)(2,1)S(1)}, u32[]{:S(2)}, u32[]{:S(2)}) collective-permute-start(bf16[2,192,384]{2,1,0:T(8,128)(2,1)S(1)} %get-tuple-element.73), channel_id=1, source_target_pairs={{0,12},{1,13},{2,14},{3,15},{4,0},{5,1},{6,2},{7,3},{8,4},{9,5},{1... | collective-permute-start | bytes 884744 | tf_op jit(solution)/shard_map/ppermute | solution.py:352
  26.0 0.7 collective-permute-done.9.high_ref
  26.6 3.2 %forward.1 = (bf16[192,512]{1,0:T(8,128)(2,1)S(1)}, f32[8,512]{1,0:T(8,128)S(1)}, f32[16,384]{1,0:T(8,128)S(1)}, f32[16,384]{1,0:T(8,128)S(1)}, bf16[3,1280,512]...) custom-call(bf16[2,192,512]{2,1,0:T(8,128)(2,1)S(1)} %get-tuple-element.61.pair_ref, ...), custom_call_target="tpu_custom_call" | custom-call | flops 1 | bytes 1 | tf_op jit(solution)/shard_map/forward/pallas_call | solution.py:50
  29.9 0.5 weight.1
  30.3 1.3 %collective-permute-start.18 = (bf16[96,768]{1,0:T(8,128)(2,1)S(1)}, bf16[96,768]{1,0:T(8,128)(2,1)S(1)}, u32[]{:S(2)}, u32[]{:S(2)}) collective-permute-start(bf16[96,768]{1,0:T(8,128)(2,1)S(1)} %get-tuple-element.86.refs_4_), channel_id=1, source_target_pairs={{0,16},{16,0},{1,17},{17,1},{2,18},{18,2},{3,19},{19,3},{4,20},{20... | collective-permute-start | bytes 442376 | tf_op jit(solution)/shard_map/ppermute | solution.py:356
  31.6 0.3 collective-permute-start.10
  31.9 3.0 %collective-permute-start.11 = (f32[16,384]{1,0:T(8,128)S(1)}, f32[16,384]{1,0:T(8,128)S(1)}, u32[]{:S(2)}, u32[]{:S(2)}) collective-permute-start(f32[16,384]{1,0:T(8,128)S(1)} %get-tuple-element.78), channel_id=1, source_target_pairs={{0,12},{1,13},{2,14},{3,15},{4,0},{5,1},{6,2},{7,3},{8,4},{9,5},{1... | collective-permute-start | bytes 73736 | tf_op jit(solution)/shard_map/ppermute | solution.py:352
  34.9 2.4 %query_grad.1 = (bf16[192,512]{1,0:T(8,128)(2,1)S(1)}, f32[2,192,512]{2,1,0:T(8,128)S(1)}, f32[8,128]{1,0:T(8,128)S(1)}) custom-call(bf16[2,192,1280]{2,1,0:T(8,128)(2,1)S(1)} %get-tuple-element.80.refs_0_, bf16[3,1280,512]{2,1,0:T(8,128)(2,1)S(1)} %get-tuple-element.81.refs_1_, bf16[2,192,512]{2,1,0:T(8,128)(2,1)S(1)} %get-tuple-element.76.query_ref.refs_2_, ...), custom_call_target="tpu_custom_call" | custom-call | flops 1 | bytes 1 | tf_op jit(solution)/shard_map/query_grad/pallas_call | solution.py:50
  37.4 0.1 collective-permute-start.19
  37.5 1.7 %collective-permute-done.10.stats_low = f32[16,384]{1,0:T(8,128)S(1)} collective-permute-done((f32[16,384]{1,0:T(8,128)S(1)}, f32[16,384]{1,0:T(8,128)S(1)}, u32[]{:S(2)}, u32[]{:S(2)}) %collective-permute-start.10) | collective-permute-done | bytes 24608 | tf_op jit(solution)/shard_map/ppermute | solution.py:351
  39.2 0.3 collective-permute-done.11.stats_high
  39.5 1.9 %key_grad.1 = (bf16[4,192,128]{2,1,0:T(8,128)(2,1)S(1)}, bf16[4,192,128]{2,1,0:T(8,128)(2,1)S(1)}, bf16[4,192,128]{2,1,0:T(8,128)(2,1)S(1)}, bf16[4,192,128]{2,1,0:T(8,128)(2,1)S(1)}, f32[8,128]{1,0:T(8,128)S(1)}) custom-call(bf16[2,192,512]{2,1,0:T(8,128)(2,1)S(1)} %get-tuple-element.61.pair_ref, bf16[2,192,384]{2,1,0:T(8,128)(2,1)S(1)} %collective-permute-done.6.low_ref, ...), custom_call_target="tpu_custom_call" | custom-call | flops 1 | bytes 1 | tf_op jit(solution)/shard_map/key_grad/pallas_call | solution.py:50
  41.4 3.0 %collective-permute-start.15 = (bf16[4,192,128]{2,1,0:T(8,128)(2,1)S(1)}, bf16[4,192,128]{2,1,0:T(8,128)(2,1)S(1)}, u32[]{:S(2)}, u32[]{:S(2)}) collective-permute-start(bf16[4,192,128]{2,1,0:T(8,128)(2,1)S(1)} %get-tuple-element.90), channel_id=1, source_target_pairs={{1,0},{0,1},{3,2},{2,3},{5,4},{4,5},{7,6},{6,7},{9,8},{8,9},{11,10... | collective-permute-start | bytes 589832 | tf_op jit(solution)/shard_map/ppermute | solution.py:345
  44.5 0.3 collective-permute-start.16
  44.7 1.4 %collective-permute-start.17 = (bf16[4,192,128]{2,1,0:T(8,128)(2,1)S(1)}, bf16[4,192,128]{2,1,0:T(8,128)(2,1)S(1)}, u32[]{:S(2)}, u32[]{:S(2)}) collective-permute-start(bf16[4,192,128]{2,1,0:T(8,128)(2,1)S(1)} %get-tuple-element.92), channel_id=1, source_target_pairs={{3,0},{2,1},{1,2},{0,3},{7,4},{6,5},{5,6},{4,7},{11,8},{10,9},{9,1... | collective-permute-start | bytes 589832 | tf_op jit(solution)/shard_map/ppermute | solution.py:345
  46.2 0.5 collective-permute-start.21
  46.7 4.2 %collective-permute-done.16.refs_2_.refs_3_ = bf16[4,192,128]{2,1,0:T(8,128)(2,1)S(1)} collective-permute-done((bf16[4,192,128]{2,1,0:T(8,128)(2,1)S(1)}, bf16[4,192,128]{2,1,0:T(8,128)(2,1)S(1)}, u32[]{:S(2)}, u32[]{:S(2)}) %collective-permute-start.16) | collective-permute-done | bytes 196640 | tf_op jit(solution)/shard_map/ppermute | solution.py:345
  50.9 4.7 %collective-permute-done.17.refs_3_.refs_4_ = bf16[4,192,128]{2,1,0:T(8,128)(2,1)S(1)} collective-permute-done((bf16[4,192,128]{2,1,0:T(8,128)(2,1)S(1)}, bf16[4,192,128]{2,1,0:T(8,128)(2,1)S(1)}, u32[]{:S(2)}, u32[]{:S(2)}) %collective-permute-start.17) | collective-permute-done | bytes 196640 | tf_op jit(solution)/shard_map/ppermute | solution.py:345
  55.6 0.0 collective-permute-done.21.refs_1_
  55.7 0.6 collective-permute-start.22
  56.2 3.0 %collective-permute-start.23 = (bf16[96,768]{1,0:T(8,128)(2,1)S(1)}, bf16[96,768]{1,0:T(8,128)(2,1)S(1)}, u32[]{:S(2)}, u32[]{:S(2)}) collective-permute-start(bf16[96,768]{1,0:T(8,128)(2,1)S(1)} %add.1.refs_0_), channel_id=1, source_target_pairs={{2,16},{3,17},{6,20},{7,21},{10,24},{11,25},{14,28},{15,29},{16,2}... | collective-permute-start | bytes 442376 | tf_op jit(solution)/shard_map/ppermute | solution.py:470
  59.3 1.2 %output.1 = (bf16[128,768]{1,0:T(8,128)(2,1)}, bf16[128,768]{1,0:T(8,128)(2,1)}, bf16[128,768]{1,0:T(8,128)(2,1)}, bf16[128,768]{1,0:T(8,128)(2,1)}, f32[8,128]{1,0:T(8,128)S(1)}) custom-call(bf16[4,192,128]{2,1,0:T(8,128)(2,1)S(1)} %get-tuple-element.89.refs_0_, bf16[4,192,128]{2,1,0:T(8,128)(2,1)S(1)} %collective-permute-done.15.refs_1_.refs_2_, ...), custom_call_target="tpu_custom_call" | custom-call | flops 1 | bytes 1 | tf_op jit(solution)/shard_map/output/pallas_call | solution.py:50
  60.5 2.5 %collective-permute-done.23.refs_2_ = bf16[96,768]{1,0:T(8,128)(2,1)S(1)} collective-permute-done((bf16[96,768]{1,0:T(8,128)(2,1)S(1)}, bf16[96,768]{1,0:T(8,128)(2,1)S(1)}, u32[]{:S(2)}, u32[]{:S(2)}) %collective-permute-start.23) | collective-permute-done | bytes 147488 | tf_op jit(solution)/shard_map/ppermute | solution.py:470
  63.1 2.5 %collective-permute-start.24 = (bf16[192,768]{1,0:T(8,128)(2,1)S(1)}, bf16[192,768]{1,0:T(8,128)(2,1)S(1)}, u32[]{:S(2)}, u32[]{:S(2)}) collective-permute-start(bf16[192,768]{1,0:T(8,128)(2,1)S(1)} %cross.1.value_ref), channel_id=1, source_target_pairs={{1,0},{0,1},{3,2},{2,3},{5,4},{4,5},{7,6},{6,7},{9,8},{8,9},{11,10... | collective-permute-start | bytes 884744 | tf_op jit(solution)/shard_map/ppermute | solution.py:345
  65.6 0.9 %write.2.refs_0_ = f32[384,768]{1,0:T(8,128)} custom-call(bf16[192,768]{1,0:T(8,128)(2,1)S(1)} %cross.1.value_ref), custom_call_target="tpu_custom_call" | custom-call | flops 1 | bytes 1 | tf_op jit(solution)/shard_map/write/pallas_call | solution.py:475
  66.4 0.3 collective-permute-done.24.value_ref
  66.8 0.9 %write.3 = f32[384,768]{1,0:T(8,128)} custom-call(bf16[192,768]{1,0:T(8,128)(2,1)S(1)} %collective-permute-done.24.value_ref, f32[384,768]{1,0:T(8,128)} %write.2.refs_0_), custom_call_target="tpu_custom_call", output_to_operand_aliasing={{}: (1, {})} | custom-call | flops 1 | bytes 1 | tf_op jit(solution)/shard_map/write/pallas_call | solution.py:475
  (33 shorter events, 0.2 us)
Async XLA Ops:
  0.6 10.2 %copy-start.4 = (bf16[1,1,128,768]{3,2,1,0:T(8,128)(2,1)S(1)}, bf16[1,1,128,768]{3,2,1,0:T(8,128)(2,1)}, u32[]{:S(2)}) copy-start(bf16[1,1,128,768]{3,2,1,0:T(8,128)(2,1)} %param.10) | copy-start | bytes 589828
  0.6 20.5 %copy-start.6 = (s32[16,6]{0,1:T(8,128)S(1)}, s32[16,6]{0,1:T(8,128)}, u32[]{:S(2)}) copy-start(s32[16,6]{0,1:T(8,128)} %param.12) | copy-start | bytes 1156
  0.7 20.6 %copy-start.5 = (s32[16]{0:T(128)S(1)}, s32[16]{0:T(128)}, u32[]{:S(2)}) copy-start(s32[16]{0:T(128)} %count_ref.1) | copy-start | bytes 196
  1.9 6.1 %collective-permute-start = (bf16[2,192,128]{2,1,0:T(8,128)(2,1)S(1)}, bf16[2,192,128]{2,1,0:T(8,128)(2,1)S(1)}, u32[]{:S(2)}, u32[]{:S(2)}) collective-permute-start(bf16[2,192,128]{2,1,0:T(8,128)(2,1)S(1)} %get-tuple-element.58), channel_id=1, source_target_pairs={{1,0},{0,1},{3,2},{2,3},{5,4},{4,5},{7,6},{6,7},{9,8},{8,9},{11,10... | collective-permute-start | bytes 294920 | tf_op jit(solution)/shard_map/ppermute | solution.py:345
  2.6 5.4 %collective-permute-start.1 = (bf16[2,192,128]{2,1,0:T(8,128)(2,1)S(1)}, bf16[2,192,128]{2,1,0:T(8,128)(2,1)S(1)}, u32[]{:S(2)}, u32[]{:S(2)}) collective-permute-start(bf16[2,192,128]{2,1,0:T(8,128)(2,1)S(1)} %get-tuple-element.59), channel_id=1, source_target_pairs={{2,0},{3,1},{0,2},{1,3},{6,4},{7,5},{4,6},{5,7},{10,8},{11,9},{8,1... | collective-permute-start | bytes 294920 | tf_op jit(solution)/shard_map/ppermute | solution.py:345
  2.6 6.6 %collective-permute-start.2 = (bf16[2,192,128]{2,1,0:T(8,128)(2,1)S(1)}, bf16[2,192,128]{2,1,0:T(8,128)(2,1)S(1)}, u32[]{:S(2)}, u32[]{:S(2)}) collective-permute-start(bf16[2,192,128]{2,1,0:T(8,128)(2,1)S(1)} %get-tuple-element.60), channel_id=1, source_target_pairs={{3,0},{2,1},{1,2},{0,3},{7,4},{6,5},{5,6},{4,7},{11,8},{10,9},{9,1... | collective-permute-start | bytes 294920 | tf_op jit(solution)/shard_map/ppermute | solution.py:345
  4.4 1.3 %copy-start = (bf16[768,768]{1,0:T(8,128)(2,1)S(1)}, bf16[768,768]{1,0:T(8,128)(2,1)}, u32[]{:S(2)}) copy-start(bf16[768,768]{1,0:T(8,128)(2,1)} %refs_4_.1) | copy-start | bytes 3538948
  5.6 0.9 %copy-start.2 = (bf16[1,1,128,768]{3,2,1,0:T(8,128)(2,1)S(1)}, bf16[1,1,128,768]{3,2,1,0:T(8,128)(2,1)}, u32[]{:S(2)}) copy-start(bf16[1,1,128,768]{3,2,1,0:T(8,128)(2,1)} %param.7) | copy-start | bytes 589828
  6.5 0.9 %copy-start.3 = (bf16[1,1,128,768]{3,2,1,0:T(8,128)(2,1)S(1)}, bf16[1,1,128,768]{3,2,1,0:T(8,128)(2,1)}, u32[]{:S(2)}) copy-start(bf16[1,1,128,768]{3,2,1,0:T(8,128)(2,1)} %param.10) | copy-start | bytes 589828
  9.4 14.6 %collective-permute-start.8 = (bf16[2,192,384]{2,1,0:T(8,128)(2,1)S(1)}, bf16[2,192,384]{2,1,0:T(8,128)(2,1)S(1)}, u32[]{:S(2)}, u32[]{:S(2)}) collective-permute-start(bf16[2,192,384]{2,1,0:T(8,128)(2,1)S(1)} %get-tuple-element.74), channel_id=1, source_target_pairs={{0,4},{1,5},{2,6},{3,7},{4,8},{5,9},{6,10},{7,11},{8,12},{9,13},{1... | collective-permute-start | bytes 884744 | tf_op jit(solution)/shard_map/ppermute | solution.py:351
  10.8 10.4 %collective-permute-start.13 = (bf16[128,768]{1,0:T(8,128)(2,1)S(1)}, bf16[128,768]{1,0:T(8,128)(2,1)S(1)}, u32[]{:S(2)}, u32[]{:S(2)}) collective-permute-start(bf16[128,768]{1,0:T(8,128)(2,1)S(1)} %bitcast.10), channel_id=1, source_target_pairs={{2,0},{3,1},{0,2},{1,3},{6,4},{7,5},{4,6},{5,7},{10,8},{11,9},{8,1... | collective-permute-start | bytes 589832 | tf_op jit(solution)/shard_map/ppermute | solution.py:345
  11.0 4.0 %collective-permute-start.3 = (bf16[2,192,128]{2,1,0:T(8,128)(2,1)S(1)}, bf16[2,192,128]{2,1,0:T(8,128)(2,1)S(1)}, u32[]{:S(2)}, u32[]{:S(2)}) collective-permute-start(bf16[2,192,128]{2,1,0:T(8,128)(2,1)S(1)} %get-tuple-element.68), channel_id=1, source_target_pairs={{1,0},{0,1},{3,2},{2,3},{5,4},{4,5},{7,6},{6,7},{9,8},{8,9},{11,10... | collective-permute-start | bytes 294920 | tf_op jit(solution)/shard_map/ppermute | solution.py:345
  11.8 14.8 %collective-permute-start.9 = (bf16[2,192,384]{2,1,0:T(8,128)(2,1)S(1)}, bf16[2,192,384]{2,1,0:T(8,128)(2,1)S(1)}, u32[]{:S(2)}, u32[]{:S(2)}) collective-permute-start(bf16[2,192,384]{2,1,0:T(8,128)(2,1)S(1)} %get-tuple-element.75), channel_id=1, source_target_pairs={{0,12},{1,13},{2,14},{3,15},{4,0},{5,1},{6,2},{7,3},{8,4},{9,5},{1... | collective-permute-start | bytes 884744 | tf_op jit(solution)/shard_map/ppermute | solution.py:352
  13.7 5.1 %collective-permute-start.4 = (bf16[2,192,128]{2,1,0:T(8,128)(2,1)S(1)}, bf16[2,192,128]{2,1,0:T(8,128)(2,1)S(1)}, u32[]{:S(2)}, u32[]{:S(2)}) collective-permute-start(bf16[2,192,128]{2,1,0:T(8,128)(2,1)S(1)} %get-tuple-element.69), channel_id=1, source_target_pairs={{2,0},{3,1},{0,2},{1,3},{6,4},{7,5},{4,6},{5,7},{10,8},{11,9},{8,1... | collective-permute-start | bytes 294920 | tf_op jit(solution)/shard_map/ppermute | solution.py:345
  15.0 7.5 %collective-permute-start.5 = (bf16[2,192,128]{2,1,0:T(8,128)(2,1)S(1)}, bf16[2,192,128]{2,1,0:T(8,128)(2,1)S(1)}, u32[]{:S(2)}, u32[]{:S(2)}) collective-permute-start(bf16[2,192,128]{2,1,0:T(8,128)(2,1)S(1)} %get-tuple-element.70), channel_id=1, source_target_pairs={{3,0},{2,1},{1,2},{0,3},{7,4},{6,5},{5,6},{4,7},{11,8},{10,9},{9,1... | collective-permute-start | bytes 294920 | tf_op jit(solution)/shard_map/ppermute | solution.py:345
  18.8 11.0 %collective-permute-start.12 = (bf16[128,768]{1,0:T(8,128)(2,1)S(1)}, bf16[128,768]{1,0:T(8,128)(2,1)S(1)}, u32[]{:S(2)}, u32[]{:S(2)}) collective-permute-start(bf16[128,768]{1,0:T(8,128)(2,1)S(1)} %bitcast.11), channel_id=1, source_target_pairs={{1,0},{0,1},{3,2},{2,3},{5,4},{4,5},{7,6},{6,7},{9,8},{8,9},{11,10... | collective-permute-start | bytes 589832 | tf_op jit(solution)/shard_map/ppermute | solution.py:345
  21.2 8.7 %collective-permute-start.14 = (bf16[128,768]{1,0:T(8,128)(2,1)S(1)}, bf16[128,768]{1,0:T(8,128)(2,1)S(1)}, u32[]{:S(2)}, u32[]{:S(2)}) collective-permute-start(bf16[128,768]{1,0:T(8,128)(2,1)S(1)} %collective-permute-done.13.refs_2_), channel_id=1, source_target_pairs={{1,0},{0,1},{3,2},{2,3},{5,4},{4,5},{7,6},{6,7},{9,8},{8,9},{11,10... | collective-permute-start | bytes 589832 | tf_op jit(solution)/shard_map/ppermute | solution.py:345
  22.7 16.9 %collective-permute-start.6 = (bf16[2,192,384]{2,1,0:T(8,128)(2,1)S(1)}, bf16[2,192,384]{2,1,0:T(8,128)(2,1)S(1)}, u32[]{:S(2)}, u32[]{:S(2)}) collective-permute-start(bf16[2,192,384]{2,1,0:T(8,128)(2,1)S(1)} %get-tuple-element.72), channel_id=1, source_target_pairs={{0,4},{1,5},{2,6},{3,7},{4,8},{5,9},{6,10},{7,11},{8,12},{9,13},{1... | collective-permute-start | bytes 884744 | tf_op jit(solution)/shard_map/ppermute | solution.py:351
  24.0 15.5 %collective-permute-start.7 = (bf16[2,192,384]{2,1,0:T(8,128)(2,1)S(1)}, bf16[2,192,384]{2,1,0:T(8,128)(2,1)S(1)}, u32[]{:S(2)}, u32[]{:S(2)}) collective-permute-start(bf16[2,192,384]{2,1,0:T(8,128)(2,1)S(1)} %get-tuple-element.73), channel_id=1, source_target_pairs={{0,12},{1,13},{2,14},{3,15},{4,0},{5,1},{6,2},{7,3},{8,4},{9,5},{1... | collective-permute-start | bytes 884744 | tf_op jit(solution)/shard_map/ppermute | solution.py:352
  30.3 7.0 %collective-permute-start.18 = (bf16[96,768]{1,0:T(8,128)(2,1)S(1)}, bf16[96,768]{1,0:T(8,128)(2,1)S(1)}, u32[]{:S(2)}, u32[]{:S(2)}) collective-permute-start(bf16[96,768]{1,0:T(8,128)(2,1)S(1)} %get-tuple-element.86.refs_4_), channel_id=1, source_target_pairs={{0,16},{16,0},{1,17},{17,1},{2,18},{18,2},{3,19},{19,3},{4,20},{20... | collective-permute-start | bytes 442376 | tf_op jit(solution)/shard_map/ppermute | solution.py:356
  31.6 7.6 %collective-permute-start.10 = (f32[16,384]{1,0:T(8,128)S(1)}, f32[16,384]{1,0:T(8,128)S(1)}, u32[]{:S(2)}, u32[]{:S(2)}) collective-permute-start(f32[16,384]{1,0:T(8,128)S(1)} %get-tuple-element.77), channel_id=1, source_target_pairs={{0,4},{1,5},{2,6},{3,7},{4,8},{5,9},{6,10},{7,11},{8,12},{9,13},{1... | collective-permute-start | bytes 73736 | tf_op jit(solution)/shard_map/ppermute | solution.py:351
  31.9 7.6 %collective-permute-start.11 = (f32[16,384]{1,0:T(8,128)S(1)}, f32[16,384]{1,0:T(8,128)S(1)}, u32[]{:S(2)}, u32[]{:S(2)}) collective-permute-start(f32[16,384]{1,0:T(8,128)S(1)} %get-tuple-element.78), channel_id=1, source_target_pairs={{0,12},{1,13},{2,14},{3,15},{4,0},{5,1},{6,2},{7,3},{8,4},{9,5},{1... | collective-permute-start | bytes 73736 | tf_op jit(solution)/shard_map/ppermute | solution.py:352
  37.4 8.8 %collective-permute-start.19 = (bf16[48,768]{1,0:T(8,128)(2,1)S(1)}, bf16[48,768]{1,0:T(8,128)(2,1)S(1)}, u32[]{:S(2)}, u32[]{:S(2)}) collective-permute-start(bf16[48,768]{1,0:T(8,128)(2,1)S(1)} %get-tuple-element.99.refs_0_), channel_id=1, source_target_pairs={{4,0},{5,1},{6,2},{7,3},{0,4},{1,5},{2,6},{3,7},{12,8},{13,9},{14,... | collective-permute-start | bytes 221192 | tf_op jit(solution)/shard_map/ppermute | solution.py:345
  39.2 7.0 %collective-permute-start.20 = (bf16[48,768]{1,0:T(8,128)(2,1)S(1)}, bf16[48,768]{1,0:T(8,128)(2,1)S(1)}, u32[]{:S(2)}, u32[]{:S(2)}) collective-permute-start(bf16[48,768]{1,0:T(8,128)(2,1)S(1)} %get-tuple-element.100.refs_1_), channel_id=1, source_target_pairs={{4,0},{5,1},{6,2},{7,3},{0,4},{1,5},{2,6},{3,7},{12,8},{13,9},{14,... | collective-permute-start | bytes 221192 | tf_op jit(solution)/shard_map/ppermute | solution.py:345
  41.4 17.9 %copy-start.1 = (bf16[768,768]{1,0:T(8,128)(2,1)S(1)}, bf16[768,768]{1,0:T(8,128)(2,1)}, u32[]{:S(2)}) copy-start(bf16[768,768]{1,0:T(8,128)(2,1)} %refs_4_.1) | copy-start | bytes 3538948
  41.4 5.3 %collective-permute-start.15 = (bf16[4,192,128]{2,1,0:T(8,128)(2,1)S(1)}, bf16[4,192,128]{2,1,0:T(8,128)(2,1)S(1)}, u32[]{:S(2)}, u32[]{:S(2)}) collective-permute-start(bf16[4,192,128]{2,1,0:T(8,128)(2,1)S(1)} %get-tuple-element.90), channel_id=1, source_target_pairs={{1,0},{0,1},{3,2},{2,3},{5,4},{4,5},{7,6},{6,7},{9,8},{8,9},{11,10... | collective-permute-start | bytes 589832 | tf_op jit(solution)/shard_map/ppermute | solution.py:345
  44.5 6.5 %collective-permute-start.16 = (bf16[4,192,128]{2,1,0:T(8,128)(2,1)S(1)}, bf16[4,192,128]{2,1,0:T(8,128)(2,1)S(1)}, u32[]{:S(2)}, u32[]{:S(2)}) collective-permute-start(bf16[4,192,128]{2,1,0:T(8,128)(2,1)S(1)} %get-tuple-element.91), channel_id=1, source_target_pairs={{2,0},{3,1},{0,2},{1,3},{6,4},{7,5},{4,6},{5,7},{10,8},{11,9},{8,1... | collective-permute-start | bytes 589832 | tf_op jit(solution)/shard_map/ppermute | solution.py:345
  44.7 10.9 %collective-permute-start.17 = (bf16[4,192,128]{2,1,0:T(8,128)(2,1)S(1)}, bf16[4,192,128]{2,1,0:T(8,128)(2,1)S(1)}, u32[]{:S(2)}, u32[]{:S(2)}) collective-permute-start(bf16[4,192,128]{2,1,0:T(8,128)(2,1)S(1)} %get-tuple-element.92), channel_id=1, source_target_pairs={{3,0},{2,1},{1,2},{0,3},{7,4},{6,5},{5,6},{4,7},{11,8},{10,9},{9,1... | collective-permute-start | bytes 589832 | tf_op jit(solution)/shard_map/ppermute | solution.py:345
  46.2 9.4 %collective-permute-start.21 = (bf16[96,768]{1,0:T(8,128)(2,1)S(1)}, bf16[96,768]{1,0:T(8,128)(2,1)S(1)}, u32[]{:S(2)}, u32[]{:S(2)}) collective-permute-start(bf16[96,768]{1,0:T(8,128)(2,1)S(1)} %meet.1.refs_0_), channel_id=1, source_target_pairs={{8,0},{9,1},{10,2},{11,3},{12,4},{13,5},{14,6},{15,7},{0,8},{1,9},... | collective-permute-start | bytes 442376 | tf_op jit(solution)/shard_map/ppermute | solution.py:345
  55.7 4.8 %collective-permute-start.22 = (bf16[96,768]{1,0:T(8,128)(2,1)S(1)}, bf16[96,768]{1,0:T(8,128)(2,1)S(1)}, u32[]{:S(2)}, u32[]{:S(2)}) collective-permute-start(bf16[96,768]{1,0:T(8,128)(2,1)S(1)} %add.1.refs_0_), channel_id=1, source_target_pairs={{0,2},{1,3},{2,18},{3,19},{4,6},{5,7},{6,22},{7,23},{8,10},{9,11},... | collective-permute-start | bytes 442376 | tf_op jit(solution)/shard_map/ppermute | solution.py:470
  56.2 6.8 %collective-permute-start.23 = (bf16[96,768]{1,0:T(8,128)(2,1)S(1)}, bf16[96,768]{1,0:T(8,128)(2,1)S(1)}, u32[]{:S(2)}, u32[]{:S(2)}) collective-permute-start(bf16[96,768]{1,0:T(8,128)(2,1)S(1)} %add.1.refs_0_), channel_id=1, source_target_pairs={{2,16},{3,17},{6,20},{7,21},{10,24},{11,25},{14,28},{15,29},{16,2}... | collective-permute-start | bytes 442376 | tf_op jit(solution)/shard_map/ppermute | solution.py:470
  63.1 3.7 %collective-permute-start.24 = (bf16[192,768]{1,0:T(8,128)(2,1)S(1)}, bf16[192,768]{1,0:T(8,128)(2,1)S(1)}, u32[]{:S(2)}, u32[]{:S(2)}) collective-permute-start(bf16[192,768]{1,0:T(8,128)(2,1)S(1)} %cross.1.value_ref), channel_id=1, source_target_pairs={{1,0},{0,1},{3,2},{2,3},{5,4},{4,5},{7,6},{6,7},{9,8},{8,9},{11,10... | collective-permute-start | bytes 884744 | tf_op jit(solution)/shard_map/ppermute | solution.py:345

commit v18 on v17

--- a/solution.py
+++ b/solution.py
@@ -453,7 +453,7 @@
         while stride < stations:
             (total,) = call(
                 round_kernel, [VMEM] * 2, [shape_of(count, width)], (total, swap(total, stride)),
-                name="add", after=parts if 2 * stride >= stations else (),
+                name="add", after=parts[:1] if 2 * stride >= stations else (),
             )
             stride *= 2
         first, second = [], []

time: 67.9 us -> 66.1 us (0.973)
  waiting for transfers between devices: 19 us -> 15 us
  starting transfers between devices: 30.3 us -> 32.6 us
    ppermute x16, waiting for transfers between devices: 13.8 us -> 10.4 us  [swap(): lax.ppermute(value, 'station', [(s ^ stride, s) for s in range(stations)])]
    ppermute x16, starting transfers between devices: 15.5 us -> 17.6 us  [swap(): lax.ppermute(value, 'station', [(s ^ stride, s) for s in range(stations)])]
    ppermute x1, waiting for transfers between devices: 2.53 us -> 1.78 us  [local(): lax.ppermute(total, axes, second)]
    ppermute x1, starting transfers between devices: 3.03 us -> 3.79 us  [local(): lax.ppermute(total, axes, second)]
  transfers between devices with their start and end apart: 25 -> 25, of which waited for: 9 -> 8; matrix products, arithmetic and copies ran while one was open for 0% -> 0% of each run, Pallas kernels for 18% -> 18%
where the time goes in v18:
time: 66.1 us; the launch traced here: 65.9 us
  starting transfers between devices  32.6 us (49%)
  waiting for transfers between devices  15 us (23%)
  Pallas kernels  14.3 us (22%)
  local copies, waits for them, and re-layouts  3.22 us (5%)
  between operations  0.85 us (1%)
    ppermute x16, starting transfers between devices, swap(): lax.ppermute(value, 'station', [(s ^ stride, s) for s in range(stations)])  17.6 us
    pallas_call x14, Pallas kernels, call(): pl.pallas_call(kernel, in_specs=ins, out_specs=[VMEM] * len(outs), out_sh...  12.5 us
    ppermute x16, waiting for transfers between devices, swap(): lax.ppermute(value, 'station', [(s ^ stride, s) for s in range(stations)])  10.4 us
    ppermute x3, starting transfers between devices, along(): lax.ppermute(down, 'station', [(s, (s - LAYER) % stations) for s in range...  6.84 us
    ppermute x1, starting transfers between devices, local(): lax.ppermute(total, axes, second)  3.79 us
    unnamed x15, local copies, waits for them, and re-layouts  3.22 us
    ppermute x3, starting transfers between devices, along(): lax.ppermute(up, 'station', [(s, (s + LAYER) % stations) for s in range(s...  2.98 us
    ppermute x1, waiting for transfers between devices, local(): lax.ppermute(total, axes, second)  1.78 us
  transfers between devices with their start and end apart: 25, of which 8 were waited for; matrix products, arithmetic and copies ran while one was open for 0% of the time, Pallas kernels for 18%

profile of v18, /device:TPU:3, one launch (start us, length us, event | category | flops | bytes accessed | tf_op | source)
XLA Modules:
  0.0 65.9 jit_solution(4901512817929920576)
XLA Ops:
  0.6 0.0 copy-start.4
  0.7 1.2 %pack.1 = (bf16[2,192,128]{2,1,0:T(8,128)(2,1)S(1)}, bf16[2,192,128]{2,1,0:T(8,128)(2,1)S(1)}, bf16[2,192,128]{2,1,0:T(8,128)(2,1)S(1)}, bf16[2,192,128]{2,1,0:T(8,128)(2,1)S(1)}) custom-call(bf16[128,768]{1,0:T(8,128)(2,1)} %bitcast.12, bf16[128,768]{1,0:T(8,128)(2,1)} %bitcast.13), custom_call_target="tpu_custom_call" | custom-call | flops 1 | bytes 1 | tf_op jit(solution)/shard_map/pack/pallas_call | solution.py:50
  1.9 0.7 %collective-permute-start = (bf16[2,192,128]{2,1,0:T(8,128)(2,1)S(1)}, bf16[2,192,128]{2,1,0:T(8,128)(2,1)S(1)}, u32[]{:S(2)}, u32[]{:S(2)}) collective-permute-start(bf16[2,192,128]{2,1,0:T(8,128)(2,1)S(1)} %get-tuple-element.58), channel_id=1, source_target_pairs={{1,0},{0,1},{3,2},{2,3},{5,4},{4,5},{7,6},{6,7},{9,8},{8,9},{11,10... | collective-permute-start | bytes 294920 | tf_op jit(solution)/shard_map/ppermute | solution.py:345
  2.6 1.7 %collective-permute-start.2 = (bf16[2,192,128]{2,1,0:T(8,128)(2,1)S(1)}, bf16[2,192,128]{2,1,0:T(8,128)(2,1)S(1)}, u32[]{:S(2)}, u32[]{:S(2)}) collective-permute-start(bf16[2,192,128]{2,1,0:T(8,128)(2,1)S(1)} %get-tuple-element.60), channel_id=1, source_target_pairs={{3,0},{2,1},{1,2},{0,3},{7,4},{6,5},{5,6},{4,7},{11,8},{10,9},{9,1... | collective-permute-start | bytes 294920 | tf_op jit(solution)/shard_map/ppermute | solution.py:345
  4.4 1.3 %copy-done = bf16[768,768]{1,0:T(8,128)(2,1)S(1)} copy-done((bf16[768,768]{1,0:T(8,128)(2,1)S(1)}, bf16[768,768]{1,0:T(8,128)(2,1)}, u32[]{:S(2)}) %copy-start) | copy-done | bytes 1179672
  5.6 0.9 %copy-done.2 = bf16[1,1,128,768]{3,2,1,0:T(8,128)(2,1)S(1)} copy-done((bf16[1,1,128,768]{3,2,1,0:T(8,128)(2,1)S(1)}, bf16[1,1,128,768]{3,2,1,0:T(8,128)(2,1)}, u32[]{:S(2)}) %copy-start.2) | copy-done | bytes 196632
  6.6 0.9 %copy-done.3 = bf16[1,1,128,768]{3,2,1,0:T(8,128)(2,1)S(1)} copy-done((bf16[1,1,128,768]{3,2,1,0:T(8,128)(2,1)S(1)}, bf16[1,1,128,768]{3,2,1,0:T(8,128)(2,1)}, u32[]{:S(2)}) %copy-start.3) | copy-done | bytes 196632
  7.5 0.5 project.1
  8.0 1.3 %collective-permute-done.2.refs_3_ = bf16[2,192,128]{2,1,0:T(8,128)(2,1)S(1)} collective-permute-done((bf16[2,192,128]{2,1,0:T(8,128)(2,1)S(1)}, bf16[2,192,128]{2,1,0:T(8,128)(2,1)S(1)}, u32[]{:S(2)}, u32[]{:S(2)}) %collective-permute-start.2) | collective-permute-done | bytes 98336 | tf_op jit(solution)/shard_map/ppermute | solution.py:345
  9.3 0.1 gather.2
  9.4 1.3 %collective-permute-start.8 = (bf16[2,192,384]{2,1,0:T(8,128)(2,1)S(1)}, bf16[2,192,384]{2,1,0:T(8,128)(2,1)S(1)}, u32[]{:S(2)}, u32[]{:S(2)}) collective-permute-start(bf16[2,192,384]{2,1,0:T(8,128)(2,1)S(1)} %get-tuple-element.74), channel_id=1, source_target_pairs={{0,4},{1,5},{2,6},{3,7},{4,8},{5,9},{6,10},{7,11},{8,12},{9,13},{1... | collective-permute-start | bytes 884744 | tf_op jit(solution)/shard_map/ppermute | solution.py:351
  10.8 0.3 collective-permute-start.13
  11.0 0.8 %collective-permute-start.3 = (bf16[2,192,128]{2,1,0:T(8,128)(2,1)S(1)}, bf16[2,192,128]{2,1,0:T(8,128)(2,1)S(1)}, u32[]{:S(2)}, u32[]{:S(2)}) collective-permute-start(bf16[2,192,128]{2,1,0:T(8,128)(2,1)S(1)} %get-tuple-element.68), channel_id=1, source_target_pairs={{1,0},{0,1},{3,2},{2,3},{5,4},{4,5},{7,6},{6,7},{9,8},{8,9},{11,10... | collective-permute-start | bytes 294920 | tf_op jit(solution)/shard_map/ppermute | solution.py:345
  11.8 1.9 %collective-permute-start.9 = (bf16[2,192,384]{2,1,0:T(8,128)(2,1)S(1)}, bf16[2,192,384]{2,1,0:T(8,128)(2,1)S(1)}, u32[]{:S(2)}, u32[]{:S(2)}) collective-permute-start(bf16[2,192,384]{2,1,0:T(8,128)(2,1)S(1)} %get-tuple-element.75), channel_id=1, source_target_pairs={{0,12},{1,13},{2,14},{3,15},{4,0},{5,1},{6,2},{7,3},{8,4},{9,5},{1... | collective-permute-start | bytes 884744 | tf_op jit(solution)/shard_map/ppermute | solution.py:352
  13.7 1.3 %collective-permute-start.4 = (bf16[2,192,128]{2,1,0:T(8,128)(2,1)S(1)}, bf16[2,192,128]{2,1,0:T(8,128)(2,1)S(1)}, u32[]{:S(2)}, u32[]{:S(2)}) collective-permute-start(bf16[2,192,128]{2,1,0:T(8,128)(2,1)S(1)} %get-tuple-element.69), channel_id=1, source_target_pairs={{2,0},{3,1},{0,2},{1,3},{6,4},{7,5},{4,6},{5,7},{10,8},{11,9},{8,1... | collective-permute-start | bytes 294920 | tf_op jit(solution)/shard_map/ppermute | solution.py:345
  15.0 0.6 collective-permute-start.5
  15.6 3.2 %collective-permute-done.4.refs_2_ = bf16[2,192,128]{2,1,0:T(8,128)(2,1)S(1)} collective-permute-done((bf16[2,192,128]{2,1,0:T(8,128)(2,1)S(1)}, bf16[2,192,128]{2,1,0:T(8,128)(2,1)S(1)}, u32[]{:S(2)}, u32[]{:S(2)}) %collective-permute-start.4) | collective-permute-done | bytes 98336 | tf_op jit(solution)/shard_map/ppermute | solution.py:345
  18.8 2.3 %collective-permute-start.12 = (bf16[128,768]{1,0:T(8,128)(2,1)S(1)}, bf16[128,768]{1,0:T(8,128)(2,1)S(1)}, u32[]{:S(2)}, u32[]{:S(2)}) collective-permute-start(bf16[128,768]{1,0:T(8,128)(2,1)S(1)} %bitcast.11), channel_id=1, source_target_pairs={{1,0},{0,1},{3,2},{2,3},{5,4},{4,5},{7,6},{6,7},{9,8},{8,9},{11,10... | collective-permute-start | bytes 589832 | tf_op jit(solution)/shard_map/ppermute | solution.py:345
  21.2 0.0 collective-permute-start.14
  21.2 0.1 copy.13.ids_ref
  21.3 1.2 %live.1 = (f32[16,512]{1,0:T(8,128)S(1)}, f32[8,384]{1,0:T(8,128)S(1)}) custom-call(s32[16,6]{1,0:T(8,128)S(1)} %copy.13.ids_ref, s32[16]{0:T(128)S(1)} %copy-done.5), custom_call_target="tpu_custom_call" | custom-call | flops 1 | bytes 1 | tf_op jit(solution)/shard_map/live/pallas_call | solution.py:50
  22.5 0.1 gather.3
  22.7 1.3 %collective-permute-start.6 = (bf16[2,192,384]{2,1,0:T(8,128)(2,1)S(1)}, bf16[2,192,384]{2,1,0:T(8,128)(2,1)S(1)}, u32[]{:S(2)}, u32[]{:S(2)}) collective-permute-start(bf16[2,192,384]{2,1,0:T(8,128)(2,1)S(1)} %get-tuple-element.72), channel_id=1, source_target_pairs={{0,4},{1,5},{2,6},{3,7},{4,8},{5,9},{6,10},{7,11},{8,12},{9,13},{1... | collective-permute-start | bytes 884744 | tf_op jit(solution)/shard_map/ppermute | solution.py:351
  24.0 2.0 %collective-permute-start.7 = (bf16[2,192,384]{2,1,0:T(8,128)(2,1)S(1)}, bf16[2,192,384]{2,1,0:T(8,128)(2,1)S(1)}, u32[]{:S(2)}, u32[]{:S(2)}) collective-permute-start(bf16[2,192,384]{2,1,0:T(8,128)(2,1)S(1)} %get-tuple-element.73), channel_id=1, source_target_pairs={{0,12},{1,13},{2,14},{3,15},{4,0},{5,1},{6,2},{7,3},{8,4},{9,5},{1... | collective-permute-start | bytes 884744 | tf_op jit(solution)/shard_map/ppermute | solution.py:352
  26.0 0.7 %collective-permute-done.9.high_ref = bf16[2,192,384]{2,1,0:T(8,128)(2,1)S(1)} collective-permute-done((bf16[2,192,384]{2,1,0:T(8,128)(2,1)S(1)}, bf16[2,192,384]{2,1,0:T(8,128)(2,1)S(1)}, u32[]{:S(2)}, u32[]{:S(2)}) %collective-permute-start.9) | collective-permute-done | bytes 294944 | tf_op jit(solution)/shard_map/ppermute | solution.py:352
  26.6 3.2 %forward.1 = (bf16[192,512]{1,0:T(8,128)(2,1)S(1)}, f32[8,512]{1,0:T(8,128)S(1)}, f32[16,384]{1,0:T(8,128)S(1)}, f32[16,384]{1,0:T(8,128)S(1)}, bf16[3,1280,512]...) custom-call(bf16[2,192,512]{2,1,0:T(8,128)(2,1)S(1)} %get-tuple-element.61.pair_ref, ...), custom_call_target="tpu_custom_call" | custom-call | flops 1 | bytes 1 | tf_op jit(solution)/shard_map/forward/pallas_call | solution.py:50
  29.9 0.5 weight.1
  30.3 1.3 %collective-permute-start.18 = (bf16[96,768]{1,0:T(8,128)(2,1)S(1)}, bf16[96,768]{1,0:T(8,128)(2,1)S(1)}, u32[]{:S(2)}, u32[]{:S(2)}) collective-permute-start(bf16[96,768]{1,0:T(8,128)(2,1)S(1)} %get-tuple-element.86.refs_4_), channel_id=1, source_target_pairs={{0,16},{16,0},{1,17},{17,1},{2,18},{18,2},{3,19},{19,3},{4,20},{20... | collective-permute-start | bytes 442376 | tf_op jit(solution)/shard_map/ppermute | solution.py:356
  31.6 0.3 collective-permute-start.10
  31.9 3.0 %collective-permute-start.11 = (f32[16,384]{1,0:T(8,128)S(1)}, f32[16,384]{1,0:T(8,128)S(1)}, u32[]{:S(2)}, u32[]{:S(2)}) collective-permute-start(f32[16,384]{1,0:T(8,128)S(1)} %get-tuple-element.78), channel_id=1, source_target_pairs={{0,12},{1,13},{2,14},{3,15},{4,0},{5,1},{6,2},{7,3},{8,4},{9,5},{1... | collective-permute-start | bytes 73736 | tf_op jit(solution)/shard_map/ppermute | solution.py:352
  34.9 2.4 %query_grad.1 = (bf16[192,512]{1,0:T(8,128)(2,1)S(1)}, f32[2,192,512]{2,1,0:T(8,128)S(1)}, f32[8,128]{1,0:T(8,128)S(1)}) custom-call(bf16[2,192,1280]{2,1,0:T(8,128)(2,1)S(1)} %get-tuple-element.80.refs_0_, bf16[3,1280,512]{2,1,0:T(8,128)(2,1)S(1)} %get-tuple-element.81.refs_1_, bf16[2,192,512]{2,1,0:T(8,128)(2,1)S(1)} %get-tuple-element.76.query_ref.refs_2_, ...), custom_call_target="tpu_custom_call" | custom-call | flops 1 | bytes 1 | tf_op jit(solution)/shard_map/query_grad/pallas_call | solution.py:50
  37.4 0.1 collective-permute-start.19
  37.5 1.7 %collective-permute-done.10.stats_low = f32[16,384]{1,0:T(8,128)S(1)} collective-permute-done((f32[16,384]{1,0:T(8,128)S(1)}, f32[16,384]{1,0:T(8,128)S(1)}, u32[]{:S(2)}, u32[]{:S(2)}) %collective-permute-start.10) | collective-permute-done | bytes 24608 | tf_op jit(solution)/shard_map/ppermute | solution.py:351
  39.2 0.3 collective-permute-done.11.stats_high
  39.5 1.9 %key_grad.1 = (bf16[4,192,128]{2,1,0:T(8,128)(2,1)S(1)}, bf16[4,192,128]{2,1,0:T(8,128)(2,1)S(1)}, bf16[4,192,128]{2,1,0:T(8,128)(2,1)S(1)}, bf16[4,192,128]{2,1,0:T(8,128)(2,1)S(1)}, f32[8,128]{1,0:T(8,128)S(1)}) custom-call(bf16[2,192,512]{2,1,0:T(8,128)(2,1)S(1)} %get-tuple-element.61.pair_ref, bf16[2,192,384]{2,1,0:T(8,128)(2,1)S(1)} %collective-permute-done.6.low_ref, ...), custom_call_target="tpu_custom_call" | custom-call | flops 1 | bytes 1 | tf_op jit(solution)/shard_map/key_grad/pallas_call | solution.py:50
  41.4 3.0 %collective-permute-start.15 = (bf16[4,192,128]{2,1,0:T(8,128)(2,1)S(1)}, bf16[4,192,128]{2,1,0:T(8,128)(2,1)S(1)}, u32[]{:S(2)}, u32[]{:S(2)}) collective-permute-start(bf16[4,192,128]{2,1,0:T(8,128)(2,1)S(1)} %get-tuple-element.90), channel_id=1, source_target_pairs={{1,0},{0,1},{3,2},{2,3},{5,4},{4,5},{7,6},{6,7},{9,8},{8,9},{11,10... | collective-permute-start | bytes 589832 | tf_op jit(solution)/shard_map/ppermute | solution.py:345
  44.5 0.5 collective-permute-start.21
  45.0 0.3 collective-permute-start.16
  45.2 2.7 %collective-permute-start.17 = (bf16[4,192,128]{2,1,0:T(8,128)(2,1)S(1)}, bf16[4,192,128]{2,1,0:T(8,128)(2,1)S(1)}, u32[]{:S(2)}, u32[]{:S(2)}) collective-permute-start(bf16[4,192,128]{2,1,0:T(8,128)(2,1)S(1)} %get-tuple-element.92), channel_id=1, source_target_pairs={{3,0},{2,1},{1,2},{0,3},{7,4},{6,5},{5,6},{4,7},{11,8},{10,9},{9,1... | collective-permute-start | bytes 589832 | tf_op jit(solution)/shard_map/ppermute | solution.py:345
  48.0 5.6 %collective-permute-done.21.refs_1_ = bf16[96,768]{1,0:T(8,128)(2,1)S(1)} collective-permute-done((bf16[96,768]{1,0:T(8,128)(2,1)S(1)}, bf16[96,768]{1,0:T(8,128)(2,1)S(1)}, u32[]{:S(2)}, u32[]{:S(2)}) %collective-permute-start.21) | collective-permute-done | bytes 147488 | tf_op jit(solution)/shard_map/ppermute | solution.py:345
  53.6 0.1 collective-permute-start.22
  53.7 3.8 %collective-permute-start.23 = (bf16[96,768]{1,0:T(8,128)(2,1)S(1)}, bf16[96,768]{1,0:T(8,128)(2,1)S(1)}, u32[]{:S(2)}, u32[]{:S(2)}) collective-permute-start(bf16[96,768]{1,0:T(8,128)(2,1)S(1)} %add.1.refs_0_), channel_id=1, source_target_pairs={{2,16},{3,17},{6,20},{7,21},{10,24},{11,25},{14,28},{15,29},{16,2}... | collective-permute-start | bytes 442376 | tf_op jit(solution)/shard_map/ppermute | solution.py:470
  57.5 1.2 %output.1 = (bf16[128,768]{1,0:T(8,128)(2,1)}, bf16[128,768]{1,0:T(8,128)(2,1)}, bf16[128,768]{1,0:T(8,128)(2,1)}, bf16[128,768]{1,0:T(8,128)(2,1)}, f32[8,128]{1,0:T(8,128)S(1)}) custom-call(bf16[4,192,128]{2,1,0:T(8,128)(2,1)S(1)} %get-tuple-element.89.refs_0_, bf16[4,192,128]{2,1,0:T(8,128)(2,1)S(1)} %collective-permute-done.15.refs_1_.refs_2_, ...), custom_call_target="tpu_custom_call" | custom-call | flops 1 | bytes 1 | tf_op jit(solution)/shard_map/output/pallas_call | solution.py:50
  58.7 1.8 %collective-permute-done.23.refs_2_ = bf16[96,768]{1,0:T(8,128)(2,1)S(1)} collective-permute-done((bf16[96,768]{1,0:T(8,128)(2,1)S(1)}, bf16[96,768]{1,0:T(8,128)(2,1)S(1)}, u32[]{:S(2)}, u32[]{:S(2)}) %collective-permute-start.23) | collective-permute-done | bytes 147488 | tf_op jit(solution)/shard_map/ppermute | solution.py:470
  60.5 3.3 %collective-permute-start.24 = (bf16[192,768]{1,0:T(8,128)(2,1)S(1)}, bf16[192,768]{1,0:T(8,128)(2,1)S(1)}, u32[]{:S(2)}, u32[]{:S(2)}) collective-permute-start(bf16[192,768]{1,0:T(8,128)(2,1)S(1)} %cross.1.value_ref), channel_id=1, source_target_pairs={{1,0},{0,1},{3,2},{2,3},{5,4},{4,5},{7,6},{6,7},{9,8},{8,9},{11,10... | collective-permute-start | bytes 884744 | tf_op jit(solution)/shard_map/ppermute | solution.py:345
  63.8 0.9 %write.2.refs_0_ = f32[384,768]{1,0:T(8,128)} custom-call(bf16[192,768]{1,0:T(8,128)(2,1)S(1)} %cross.1.value_ref), custom_call_target="tpu_custom_call" | custom-call | flops 1 | bytes 1 | tf_op jit(solution)/shard_map/write/pallas_call | solution.py:475
  64.7 0.3 collective-permute-done.24.value_ref
  65.1 0.9 %write.3 = f32[384,768]{1,0:T(8,128)} custom-call(bf16[192,768]{1,0:T(8,128)(2,1)S(1)} %collective-permute-done.24.value_ref, f32[384,768]{1,0:T(8,128)} %write.2.refs_0_), custom_call_target="tpu_custom_call", output_to_operand_aliasing={{}: (1, {})} | custom-call | flops 1 | bytes 1 | tf_op jit(solution)/shard_map/write/pallas_call | solution.py:475
  (33 shorter events, 0.2 us)
Async XLA Ops:
  0.6 10.2 %copy-start.4 = (bf16[1,1,128,768]{3,2,1,0:T(8,128)(2,1)S(1)}, bf16[1,1,128,768]{3,2,1,0:T(8,128)(2,1)}, u32[]{:S(2)}) copy-start(bf16[1,1,128,768]{3,2,1,0:T(8,128)(2,1)} %param.10) | copy-start | bytes 589828
  0.6 20.5 %copy-start.6 = (s32[16,6]{0,1:T(8,128)S(1)}, s32[16,6]{0,1:T(8,128)}, u32[]{:S(2)}) copy-start(s32[16,6]{0,1:T(8,128)} %param.12) | copy-start | bytes 1156
  0.7 20.6 %copy-start.5 = (s32[16]{0:T(128)S(1)}, s32[16]{0:T(128)}, u32[]{:S(2)}) copy-start(s32[16]{0:T(128)} %count_ref.1) | copy-start | bytes 196
  1.9 6.1 %collective-permute-start = (bf16[2,192,128]{2,1,0:T(8,128)(2,1)S(1)}, bf16[2,192,128]{2,1,0:T(8,128)(2,1)S(1)}, u32[]{:S(2)}, u32[]{:S(2)}) collective-permute-start(bf16[2,192,128]{2,1,0:T(8,128)(2,1)S(1)} %get-tuple-element.58), channel_id=1, source_target_pairs={{1,0},{0,1},{3,2},{2,3},{5,4},{4,5},{7,6},{6,7},{9,8},{8,9},{11,10... | collective-permute-start | bytes 294920 | tf_op jit(solution)/shard_map/ppermute | solution.py:345
  2.6 5.4 %collective-permute-start.1 = (bf16[2,192,128]{2,1,0:T(8,128)(2,1)S(1)}, bf16[2,192,128]{2,1,0:T(8,128)(2,1)S(1)}, u32[]{:S(2)}, u32[]{:S(2)}) collective-permute-start(bf16[2,192,128]{2,1,0:T(8,128)(2,1)S(1)} %get-tuple-element.59), channel_id=1, source_target_pairs={{2,0},{3,1},{0,2},{1,3},{6,4},{7,5},{4,6},{5,7},{10,8},{11,9},{8,1... | collective-permute-start | bytes 294920 | tf_op jit(solution)/shard_map/ppermute | solution.py:345
  2.6 6.6 %collective-permute-start.2 = (bf16[2,192,128]{2,1,0:T(8,128)(2,1)S(1)}, bf16[2,192,128]{2,1,0:T(8,128)(2,1)S(1)}, u32[]{:S(2)}, u32[]{:S(2)}) collective-permute-start(bf16[2,192,128]{2,1,0:T(8,128)(2,1)S(1)} %get-tuple-element.60), channel_id=1, source_target_pairs={{3,0},{2,1},{1,2},{0,3},{7,4},{6,5},{5,6},{4,7},{11,8},{10,9},{9,1... | collective-permute-start | bytes 294920 | tf_op jit(solution)/shard_map/ppermute | solution.py:345
  4.4 1.3 %copy-start = (bf16[768,768]{1,0:T(8,128)(2,1)S(1)}, bf16[768,768]{1,0:T(8,128)(2,1)}, u32[]{:S(2)}) copy-start(bf16[768,768]{1,0:T(8,128)(2,1)} %refs_4_.1) | copy-start | bytes 3538948
  5.6 0.9 %copy-start.2 = (bf16[1,1,128,768]{3,2,1,0:T(8,128)(2,1)S(1)}, bf16[1,1,128,768]{3,2,1,0:T(8,128)(2,1)}, u32[]{:S(2)}) copy-start(bf16[1,1,128,768]{3,2,1,0:T(8,128)(2,1)} %param.7) | copy-start | bytes 589828
  6.5 0.9 %copy-start.3 = (bf16[1,1,128,768]{3,2,1,0:T(8,128)(2,1)S(1)}, bf16[1,1,128,768]{3,2,1,0:T(8,128)(2,1)}, u32[]{:S(2)}) copy-start(bf16[1,1,128,768]{3,2,1,0:T(8,128)(2,1)} %param.10) | copy-start | bytes 589828
  9.4 14.6 %collective-permute-start.8 = (bf16[2,192,384]{2,1,0:T(8,128)(2,1)S(1)}, bf16[2,192,384]{2,1,0:T(8,128)(2,1)S(1)}, u32[]{:S(2)}, u32[]{:S(2)}) collective-permute-start(bf16[2,192,384]{2,1,0:T(8,128)(2,1)S(1)} %get-tuple-element.74), channel_id=1, source_target_pairs={{0,4},{1,5},{2,6},{3,7},{4,8},{5,9},{6,10},{7,11},{8,12},{9,13},{1... | collective-permute-start | bytes 884744 | tf_op jit(solution)/shard_map/ppermute | solution.py:351
  10.8 10.4 %collective-permute-start.13 = (bf16[128,768]{1,0:T(8,128)(2,1)S(1)}, bf16[128,768]{1,0:T(8,128)(2,1)S(1)}, u32[]{:S(2)}, u32[]{:S(2)}) collective-permute-start(bf16[128,768]{1,0:T(8,128)(2,1)S(1)} %bitcast.10), channel_id=1, source_target_pairs={{2,0},{3,1},{0,2},{1,3},{6,4},{7,5},{4,6},{5,7},{10,8},{11,9},{8,1... | collective-permute-start | bytes 589832 | tf_op jit(solution)/shard_map/ppermute | solution.py:345
  11.0 4.0 %collective-permute-start.3 = (bf16[2,192,128]{2,1,0:T(8,128)(2,1)S(1)}, bf16[2,192,128]{2,1,0:T(8,128)(2,1)S(1)}, u32[]{:S(2)}, u32[]{:S(2)}) collective-permute-start(bf16[2,192,128]{2,1,0:T(8,128)(2,1)S(1)} %get-tuple-element.68), channel_id=1, source_target_pairs={{1,0},{0,1},{3,2},{2,3},{5,4},{4,5},{7,6},{6,7},{9,8},{8,9},{11,10... | collective-permute-start | bytes 294920 | tf_op jit(solution)/shard_map/ppermute | solution.py:345
  11.8 14.8 %collective-permute-start.9 = (bf16[2,192,384]{2,1,0:T(8,128)(2,1)S(1)}, bf16[2,192,384]{2,1,0:T(8,128)(2,1)S(1)}, u32[]{:S(2)}, u32[]{:S(2)}) collective-permute-start(bf16[2,192,384]{2,1,0:T(8,128)(2,1)S(1)} %get-tuple-element.75), channel_id=1, source_target_pairs={{0,12},{1,13},{2,14},{3,15},{4,0},{5,1},{6,2},{7,3},{8,4},{9,5},{1... | collective-permute-start | bytes 884744 | tf_op jit(solution)/shard_map/ppermute | solution.py:352
  13.7 5.1 %collective-permute-start.4 = (bf16[2,192,128]{2,1,0:T(8,128)(2,1)S(1)}, bf16[2,192,128]{2,1,0:T(8,128)(2,1)S(1)}, u32[]{:S(2)}, u32[]{:S(2)}) collective-permute-start(bf16[2,192,128]{2,1,0:T(8,128)(2,1)S(1)} %get-tuple-element.69), channel_id=1, source_target_pairs={{2,0},{3,1},{0,2},{1,3},{6,4},{7,5},{4,6},{5,7},{10,8},{11,9},{8,1... | collective-permute-start | bytes 294920 | tf_op jit(solution)/shard_map/ppermute | solution.py:345
  15.0 7.5 %collective-permute-start.5 = (bf16[2,192,128]{2,1,0:T(8,128)(2,1)S(1)}, bf16[2,192,128]{2,1,0:T(8,128)(2,1)S(1)}, u32[]{:S(2)}, u32[]{:S(2)}) collective-permute-start(bf16[2,192,128]{2,1,0:T(8,128)(2,1)S(1)} %get-tuple-element.70), channel_id=1, source_target_pairs={{3,0},{2,1},{1,2},{0,3},{7,4},{6,5},{5,6},{4,7},{11,8},{10,9},{9,1... | collective-permute-start | bytes 294920 | tf_op jit(solution)/shard_map/ppermute | solution.py:345
  18.8 11.0 %collective-permute-start.12 = (bf16[128,768]{1,0:T(8,128)(2,1)S(1)}, bf16[128,768]{1,0:T(8,128)(2,1)S(1)}, u32[]{:S(2)}, u32[]{:S(2)}) collective-permute-start(bf16[128,768]{1,0:T(8,128)(2,1)S(1)} %bitcast.11), channel_id=1, source_target_pairs={{1,0},{0,1},{3,2},{2,3},{5,4},{4,5},{7,6},{6,7},{9,8},{8,9},{11,10... | collective-permute-start | bytes 589832 | tf_op jit(solution)/shard_map/ppermute | solution.py:345
  21.2 8.7 %collective-permute-start.14 = (bf16[128,768]{1,0:T(8,128)(2,1)S(1)}, bf16[128,768]{1,0:T(8,128)(2,1)S(1)}, u32[]{:S(2)}, u32[]{:S(2)}) collective-permute-start(bf16[128,768]{1,0:T(8,128)(2,1)S(1)} %collective-permute-done.13.refs_2_), channel_id=1, source_target_pairs={{1,0},{0,1},{3,2},{2,3},{5,4},{4,5},{7,6},{6,7},{9,8},{8,9},{11,10... | collective-permute-start | bytes 589832 | tf_op jit(solution)/shard_map/ppermute | solution.py:345
  22.7 16.9 %collective-permute-start.6 = (bf16[2,192,384]{2,1,0:T(8,128)(2,1)S(1)}, bf16[2,192,384]{2,1,0:T(8,128)(2,1)S(1)}, u32[]{:S(2)}, u32[]{:S(2)}) collective-permute-start(bf16[2,192,384]{2,1,0:T(8,128)(2,1)S(1)} %get-tuple-element.72), channel_id=1, source_target_pairs={{0,4},{1,5},{2,6},{3,7},{4,8},{5,9},{6,10},{7,11},{8,12},{9,13},{1... | collective-permute-start | bytes 884744 | tf_op jit(solution)/shard_map/ppermute | solution.py:351
  24.0 15.5 %collective-permute-start.7 = (bf16[2,192,384]{2,1,0:T(8,128)(2,1)S(1)}, bf16[2,192,384]{2,1,0:T(8,128)(2,1)S(1)}, u32[]{:S(2)}, u32[]{:S(2)}) collective-permute-start(bf16[2,192,384]{2,1,0:T(8,128)(2,1)S(1)} %get-tuple-element.73), channel_id=1, source_target_pairs={{0,12},{1,13},{2,14},{3,15},{4,0},{5,1},{6,2},{7,3},{8,4},{9,5},{1... | collective-permute-start | bytes 884744 | tf_op jit(solution)/shard_map/ppermute | solution.py:352
  30.3 7.0 %collective-permute-start.18 = (bf16[96,768]{1,0:T(8,128)(2,1)S(1)}, bf16[96,768]{1,0:T(8,128)(2,1)S(1)}, u32[]{:S(2)}, u32[]{:S(2)}) collective-permute-start(bf16[96,768]{1,0:T(8,128)(2,1)S(1)} %get-tuple-element.86.refs_4_), channel_id=1, source_target_pairs={{0,16},{16,0},{1,17},{17,1},{2,18},{18,2},{3,19},{19,3},{4,20},{20... | collective-permute-start | bytes 442376 | tf_op jit(solution)/shard_map/ppermute | solution.py:356
  31.6 7.6 %collective-permute-start.10 = (f32[16,384]{1,0:T(8,128)S(1)}, f32[16,384]{1,0:T(8,128)S(1)}, u32[]{:S(2)}, u32[]{:S(2)}) collective-permute-start(f32[16,384]{1,0:T(8,128)S(1)} %get-tuple-element.77), channel_id=1, source_target_pairs={{0,4},{1,5},{2,6},{3,7},{4,8},{5,9},{6,10},{7,11},{8,12},{9,13},{1... | collective-permute-start | bytes 73736 | tf_op jit(solution)/shard_map/ppermute | solution.py:351
  31.9 7.6 %collective-permute-start.11 = (f32[16,384]{1,0:T(8,128)S(1)}, f32[16,384]{1,0:T(8,128)S(1)}, u32[]{:S(2)}, u32[]{:S(2)}) collective-permute-start(f32[16,384]{1,0:T(8,128)S(1)} %get-tuple-element.78), channel_id=1, source_target_pairs={{0,12},{1,13},{2,14},{3,15},{4,0},{5,1},{6,2},{7,3},{8,4},{9,5},{1... | collective-permute-start | bytes 73736 | tf_op jit(solution)/shard_map/ppermute | solution.py:352
  37.4 7.1 %collective-permute-start.19 = (bf16[48,768]{1,0:T(8,128)(2,1)S(1)}, bf16[48,768]{1,0:T(8,128)(2,1)S(1)}, u32[]{:S(2)}, u32[]{:S(2)}) collective-permute-start(bf16[48,768]{1,0:T(8,128)(2,1)S(1)} %get-tuple-element.99.refs_0_), channel_id=1, source_target_pairs={{4,0},{5,1},{6,2},{7,3},{0,4},{1,5},{2,6},{3,7},{12,8},{13,9},{14,... | collective-permute-start | bytes 221192 | tf_op jit(solution)/shard_map/ppermute | solution.py:345
  39.2 5.3 %collective-permute-start.20 = (bf16[48,768]{1,0:T(8,128)(2,1)S(1)}, bf16[48,768]{1,0:T(8,128)(2,1)S(1)}, u32[]{:S(2)}, u32[]{:S(2)}) collective-permute-start(bf16[48,768]{1,0:T(8,128)(2,1)S(1)} %get-tuple-element.100.refs_1_), channel_id=1, source_target_pairs={{4,0},{5,1},{6,2},{7,3},{0,4},{1,5},{2,6},{3,7},{12,8},{13,9},{14,... | collective-permute-start | bytes 221192 | tf_op jit(solution)/shard_map/ppermute | solution.py:345
  39.5 18.0 %copy-start.1 = (bf16[768,768]{1,0:T(8,128)(2,1)S(1)}, bf16[768,768]{1,0:T(8,128)(2,1)}, u32[]{:S(2)}) copy-start(bf16[768,768]{1,0:T(8,128)(2,1)} %refs_4_.1) | copy-start | bytes 3538948
  41.4 6.5 %collective-permute-start.15 = (bf16[4,192,128]{2,1,0:T(8,128)(2,1)S(1)}, bf16[4,192,128]{2,1,0:T(8,128)(2,1)S(1)}, u32[]{:S(2)}, u32[]{:S(2)}) collective-permute-start(bf16[4,192,128]{2,1,0:T(8,128)(2,1)S(1)} %get-tuple-element.90), channel_id=1, source_target_pairs={{1,0},{0,1},{3,2},{2,3},{5,4},{4,5},{7,6},{6,7},{9,8},{8,9},{11,10... | collective-permute-start | bytes 589832 | tf_op jit(solution)/shard_map/ppermute | solution.py:345
  44.5 9.1 %collective-permute-start.21 = (bf16[96,768]{1,0:T(8,128)(2,1)S(1)}, bf16[96,768]{1,0:T(8,128)(2,1)S(1)}, u32[]{:S(2)}, u32[]{:S(2)}) collective-permute-start(bf16[96,768]{1,0:T(8,128)(2,1)S(1)} %meet.1.refs_0_), channel_id=1, source_target_pairs={{8,0},{9,1},{10,2},{11,3},{12,4},{13,5},{14,6},{15,7},{0,8},{1,9},... | collective-permute-start | bytes 442376 | tf_op jit(solution)/shard_map/ppermute | solution.py:345
  45.0 12.5 %collective-permute-start.16 = (bf16[4,192,128]{2,1,0:T(8,128)(2,1)S(1)}, bf16[4,192,128]{2,1,0:T(8,128)(2,1)S(1)}, u32[]{:S(2)}, u32[]{:S(2)}) collective-permute-start(bf16[4,192,128]{2,1,0:T(8,128)(2,1)S(1)} %get-tuple-element.91), channel_id=1, source_target_pairs={{2,0},{3,1},{0,2},{1,3},{6,4},{7,5},{4,6},{5,7},{10,8},{11,9},{8,1... | collective-permute-start | bytes 589832 | tf_op jit(solution)/shard_map/ppermute | solution.py:345
  45.2 12.2 %collective-permute-start.17 = (bf16[4,192,128]{2,1,0:T(8,128)(2,1)S(1)}, bf16[4,192,128]{2,1,0:T(8,128)(2,1)S(1)}, u32[]{:S(2)}, u32[]{:S(2)}) collective-permute-start(bf16[4,192,128]{2,1,0:T(8,128)(2,1)S(1)} %get-tuple-element.92), channel_id=1, source_target_pairs={{3,0},{2,1},{1,2},{0,3},{7,4},{6,5},{5,6},{4,7},{11,8},{10,9},{9,1... | collective-permute-start | bytes 589832 | tf_op jit(solution)/shard_map/ppermute | solution.py:345
  53.6 5.1 %collective-permute-start.22 = (bf16[96,768]{1,0:T(8,128)(2,1)S(1)}, bf16[96,768]{1,0:T(8,128)(2,1)S(1)}, u32[]{:S(2)}, u32[]{:S(2)}) collective-permute-start(bf16[96,768]{1,0:T(8,128)(2,1)S(1)} %add.1.refs_0_), channel_id=1, source_target_pairs={{0,2},{1,3},{2,18},{3,19},{4,6},{5,7},{6,22},{7,23},{8,10},{9,11},... | collective-permute-start | bytes 442376 | tf_op jit(solution)/shard_map/ppermute | solution.py:470
  53.7 6.8 %collective-permute-start.23 = (bf16[96,768]{1,0:T(8,128)(2,1)S(1)}, bf16[96,768]{1,0:T(8,128)(2,1)S(1)}, u32[]{:S(2)}, u32[]{:S(2)}) collective-permute-start(bf16[96,768]{1,0:T(8,128)(2,1)S(1)} %add.1.refs_0_), channel_id=1, source_target_pairs={{2,16},{3,17},{6,20},{7,21},{10,24},{11,25},{14,28},{15,29},{16,2}... | collective-permute-start | bytes 442376 | tf_op jit(solution)/shard_map/ppermute | solution.py:470
  60.5 4.5 %collective-permute-start.24 = (bf16[192,768]{1,0:T(8,128)(2,1)S(1)}, bf16[192,768]{1,0:T(8,128)(2,1)S(1)}, u32[]{:S(2)}, u32[]{:S(2)}) collective-permute-start(bf16[192,768]{1,0:T(8,128)(2,1)S(1)} %cross.1.value_ref), channel_id=1, source_target_pairs={{1,0},{0,1},{3,2},{2,3},{5,4},{4,5},{7,6},{6,7},{9,8},{8,9},{11,10... | collective-permute-start | bytes 884744 | tf_op jit(solution)/shard_map/ppermute | solution.py:345

commit v19 on v18

--- a/solution.py
+++ b/solution.py
@@ -405,7 +405,6 @@
         [pltpu.VMEM((BLOCKS * span, LAYER * span), f32)],
         limit=20, name="forward",
     )
-    stats_low, stats_high = along(up, down)
 
     send, part = call(
         weight_kernel, [VMEM] * (LAYER + 1),
@@ -419,6 +418,8 @@
         (window, probs, query, stats), [pltpu.VMEM((BLOCKS * span, LAYER * span), bf16)],
         limit=20, name="query_grad", after=(send,),
     )
+    up, down, query_token = lax.optimization_barrier((up, down, query_token))
+    stats_low, stats_high = along(up, down)
     mine, *parts, key_token = call(
         key_grad_kernel, [VMEM] * 9, [shape_of(4, rows, span)] * LAYER + [TOKEN],
         (pair, qg_low, qg_high, stats_low, stats_high, dead, own_grad, mixed, dq),

time: 66.1 us -> 66.1 us (level)
    ppermute x3, waiting for transfers between devices: 1.74 us -> 0.24 us  [along(): lax.ppermute(up, 'station', [(s, (s + LAYER) % stations) for s in range(s...]
    ppermute x1, starting transfers between devices: 3.79 us -> 2.61 us  [local(): lax.ppermute(total, axes, second)]
    ppermute x1, waiting for transfers between devices: 1.78 us -> 2.94 us  [local(): lax.ppermute(total, axes, second)]
    ppermute x1, starting transfers between devices: 0.06 us -> 0.78 us  [local(): lax.ppermute(total, axes, first)]
where the time goes in v19:
time: 66.1 us; the launch traced here: 65.9 us
  starting transfers between devices  32.6 us (49%)
  waiting for transfers between devices  15 us (23%)
  Pallas kernels  14.2 us (21%)
  local copies, waits for them, and re-layouts  3.22 us (5%)
  between operations  0.84 us (1%)
    ppermute x16, starting transfers between devices, swap(): lax.ppermute(value, 'station', [(s ^ stride, s) for s in range(stations)])  18 us
    pallas_call x14, Pallas kernels, call(): pl.pallas_call(kernel, in_specs=ins, out_specs=[VMEM] * len(outs), out_sh...  12.5 us
    ppermute x16, waiting for transfers between devices, swap(): lax.ppermute(value, 'station', [(s ^ stride, s) for s in range(stations)])  10.8 us
    ppermute x3, starting transfers between devices, along(): lax.ppermute(down, 'station', [(s, (s - LAYER) % stations) for s in range...  6.84 us
    unnamed x15, local copies, waits for them, and re-layouts  3.22 us
    ppermute x3, starting transfers between devices, along(): lax.ppermute(up, 'station', [(s, (s + LAYER) % stations) for s in range(s...  3.03 us
    ppermute x1, waiting for transfers between devices, local(): lax.ppermute(total, axes, second)  2.94 us
    ppermute x1, starting transfers between devices, local(): lax.ppermute(total, axes, second)  2.61 us
  transfers between devices with their start and end apart: 25, of which 8 were waited for; matrix products, arithmetic and copies ran while one was open for 0% of the time, Pallas kernels for 18%

profile of v19, /device:TPU:3, one launch (start us, length us, event | category | flops | bytes accessed | tf_op | source)
XLA Modules:
  0.0 65.9 jit_solution(8238540418211504307)
XLA Ops:
  0.6 0.0 copy-start.4
  0.7 1.2 %pack.1 = (bf16[2,192,128]{2,1,0:T(8,128)(2,1)S(1)}, bf16[2,192,128]{2,1,0:T(8,128)(2,1)S(1)}, bf16[2,192,128]{2,1,0:T(8,128)(2,1)S(1)}, bf16[2,192,128]{2,1,0:T(8,128)(2,1)S(1)}) custom-call(bf16[128,768]{1,0:T(8,128)(2,1)} %bitcast.12, bf16[128,768]{1,0:T(8,128)(2,1)} %bitcast.13), custom_call_target="tpu_custom_call" | custom-call | flops 1 | bytes 1 | tf_op jit(solution)/shard_map/pack/pallas_call | solution.py:50
  1.9 0.7 %collective-permute-start = (bf16[2,192,128]{2,1,0:T(8,128)(2,1)S(1)}, bf16[2,192,128]{2,1,0:T(8,128)(2,1)S(1)}, u32[]{:S(2)}, u32[]{:S(2)}) collective-permute-start(bf16[2,192,128]{2,1,0:T(8,128)(2,1)S(1)} %get-tuple-element.61), channel_id=1, source_target_pairs={{1,0},{0,1},{3,2},{2,3},{5,4},{4,5},{7,6},{6,7},{9,8},{8,9},{11,10... | collective-permute-start | bytes 294920 | tf_op jit(solution)/shard_map/ppermute | solution.py:345
  2.6 1.7 %collective-permute-start.2 = (bf16[2,192,128]{2,1,0:T(8,128)(2,1)S(1)}, bf16[2,192,128]{2,1,0:T(8,128)(2,1)S(1)}, u32[]{:S(2)}, u32[]{:S(2)}) collective-permute-start(bf16[2,192,128]{2,1,0:T(8,128)(2,1)S(1)} %get-tuple-element.63), channel_id=1, source_target_pairs={{3,0},{2,1},{1,2},{0,3},{7,4},{6,5},{5,6},{4,7},{11,8},{10,9},{9,1... | collective-permute-start | bytes 294920 | tf_op jit(solution)/shard_map/ppermute | solution.py:345
  4.4 1.3 %copy-done = bf16[768,768]{1,0:T(8,128)(2,1)S(1)} copy-done((bf16[768,768]{1,0:T(8,128)(2,1)S(1)}, bf16[768,768]{1,0:T(8,128)(2,1)}, u32[]{:S(2)}) %copy-start) | copy-done | bytes 1179672
  5.6 0.9 %copy-done.2 = bf16[1,1,128,768]{3,2,1,0:T(8,128)(2,1)S(1)} copy-done((bf16[1,1,128,768]{3,2,1,0:T(8,128)(2,1)S(1)}, bf16[1,1,128,768]{3,2,1,0:T(8,128)(2,1)}, u32[]{:S(2)}) %copy-start.2) | copy-done | bytes 196632
  6.6 0.9 %copy-done.3 = bf16[1,1,128,768]{3,2,1,0:T(8,128)(2,1)S(1)} copy-done((bf16[1,1,128,768]{3,2,1,0:T(8,128)(2,1)S(1)}, bf16[1,1,128,768]{3,2,1,0:T(8,128)(2,1)}, u32[]{:S(2)}) %copy-start.3) | copy-done | bytes 196632
  7.5 0.5 project.1
  8.0 1.3 %collective-permute-done.2.refs_3_ = bf16[2,192,128]{2,1,0:T(8,128)(2,1)S(1)} collective-permute-done((bf16[2,192,128]{2,1,0:T(8,128)(2,1)S(1)}, bf16[2,192,128]{2,1,0:T(8,128)(2,1)S(1)}, u32[]{:S(2)}, u32[]{:S(2)}) %collective-permute-start.2) | collective-permute-done | bytes 98336 | tf_op jit(solution)/shard_map/ppermute | solution.py:345
  9.3 0.1 gather.2
  9.4 1.3 %collective-permute-start.8 = (bf16[2,192,384]{2,1,0:T(8,128)(2,1)S(1)}, bf16[2,192,384]{2,1,0:T(8,128)(2,1)S(1)}, u32[]{:S(2)}, u32[]{:S(2)}) collective-permute-start(bf16[2,192,384]{2,1,0:T(8,128)(2,1)S(1)} %get-tuple-element.77), channel_id=1, source_target_pairs={{0,4},{1,5},{2,6},{3,7},{4,8},{5,9},{6,10},{7,11},{8,12},{9,13},{1... | collective-permute-start | bytes 884744 | tf_op jit(solution)/shard_map/ppermute | solution.py:351
  10.8 0.3 collective-permute-start.11
  11.0 0.8 %collective-permute-start.3 = (bf16[2,192,128]{2,1,0:T(8,128)(2,1)S(1)}, bf16[2,192,128]{2,1,0:T(8,128)(2,1)S(1)}, u32[]{:S(2)}, u32[]{:S(2)}) collective-permute-start(bf16[2,192,128]{2,1,0:T(8,128)(2,1)S(1)} %get-tuple-element.71), channel_id=1, source_target_pairs={{1,0},{0,1},{3,2},{2,3},{5,4},{4,5},{7,6},{6,7},{9,8},{8,9},{11,10... | collective-permute-start | bytes 294920 | tf_op jit(solution)/shard_map/ppermute | solution.py:345
  11.8 1.9 %collective-permute-start.9 = (bf16[2,192,384]{2,1,0:T(8,128)(2,1)S(1)}, bf16[2,192,384]{2,1,0:T(8,128)(2,1)S(1)}, u32[]{:S(2)}, u32[]{:S(2)}) collective-permute-start(bf16[2,192,384]{2,1,0:T(8,128)(2,1)S(1)} %get-tuple-element.78), channel_id=1, source_target_pairs={{0,12},{1,13},{2,14},{3,15},{4,0},{5,1},{6,2},{7,3},{8,4},{9,5},{1... | collective-permute-start | bytes 884744 | tf_op jit(solution)/shard_map/ppermute | solution.py:352
  13.7 1.3 %collective-permute-start.4 = (bf16[2,192,128]{2,1,0:T(8,128)(2,1)S(1)}, bf16[2,192,128]{2,1,0:T(8,128)(2,1)S(1)}, u32[]{:S(2)}, u32[]{:S(2)}) collective-permute-start(bf16[2,192,128]{2,1,0:T(8,128)(2,1)S(1)} %get-tuple-element.72), channel_id=1, source_target_pairs={{2,0},{3,1},{0,2},{1,3},{6,4},{7,5},{4,6},{5,7},{10,8},{11,9},{8,1... | collective-permute-start | bytes 294920 | tf_op jit(solution)/shard_map/ppermute | solution.py:345
  15.0 0.6 collective-permute-start.5
  15.6 3.2 %collective-permute-done.4.refs_2_ = bf16[2,192,128]{2,1,0:T(8,128)(2,1)S(1)} collective-permute-done((bf16[2,192,128]{2,1,0:T(8,128)(2,1)S(1)}, bf16[2,192,128]{2,1,0:T(8,128)(2,1)S(1)}, u32[]{:S(2)}, u32[]{:S(2)}) %collective-permute-start.4) | collective-permute-done | bytes 98336 | tf_op jit(solution)/shard_map/ppermute | solution.py:345
  18.8 2.3 %collective-permute-start.10 = (bf16[128,768]{1,0:T(8,128)(2,1)S(1)}, bf16[128,768]{1,0:T(8,128)(2,1)S(1)}, u32[]{:S(2)}, u32[]{:S(2)}) collective-permute-start(bf16[128,768]{1,0:T(8,128)(2,1)S(1)} %bitcast.11), channel_id=1, source_target_pairs={{1,0},{0,1},{3,2},{2,3},{5,4},{4,5},{7,6},{6,7},{9,8},{8,9},{11,10... | collective-permute-start | bytes 589832 | tf_op jit(solution)/shard_map/ppermute | solution.py:345
  21.2 0.0 collective-permute-start.12
  21.2 0.1 copy.13.ids_ref
  21.3 1.2 %live.1 = (f32[16,512]{1,0:T(8,128)S(1)}, f32[8,384]{1,0:T(8,128)S(1)}) custom-call(s32[16,6]{1,0:T(8,128)S(1)} %copy.13.ids_ref, s32[16]{0:T(128)S(1)} %copy-done.5), custom_call_target="tpu_custom_call" | custom-call | flops 1 | bytes 1 | tf_op jit(solution)/shard_map/live/pallas_call | solution.py:50
  22.5 0.1 gather.3
  22.7 1.3 %collective-permute-start.6 = (bf16[2,192,384]{2,1,0:T(8,128)(2,1)S(1)}, bf16[2,192,384]{2,1,0:T(8,128)(2,1)S(1)}, u32[]{:S(2)}, u32[]{:S(2)}) collective-permute-start(bf16[2,192,384]{2,1,0:T(8,128)(2,1)S(1)} %get-tuple-element.75), channel_id=1, source_target_pairs={{0,4},{1,5},{2,6},{3,7},{4,8},{5,9},{6,10},{7,11},{8,12},{9,13},{1... | collective-permute-start | bytes 884744 | tf_op jit(solution)/shard_map/ppermute | solution.py:351
  24.0 2.0 %collective-permute-start.7 = (bf16[2,192,384]{2,1,0:T(8,128)(2,1)S(1)}, bf16[2,192,384]{2,1,0:T(8,128)(2,1)S(1)}, u32[]{:S(2)}, u32[]{:S(2)}) collective-permute-start(bf16[2,192,384]{2,1,0:T(8,128)(2,1)S(1)} %get-tuple-element.76), channel_id=1, source_target_pairs={{0,12},{1,13},{2,14},{3,15},{4,0},{5,1},{6,2},{7,3},{8,4},{9,5},{1... | collective-permute-start | bytes 884744 | tf_op jit(solution)/shard_map/ppermute | solution.py:352
  26.0 0.7 %collective-permute-done.9.high_ref = bf16[2,192,384]{2,1,0:T(8,128)(2,1)S(1)} collective-permute-done((bf16[2,192,384]{2,1,0:T(8,128)(2,1)S(1)}, bf16[2,192,384]{2,1,0:T(8,128)(2,1)S(1)}, u32[]{:S(2)}, u32[]{:S(2)}) %collective-permute-start.9) | collective-permute-done | bytes 294944 | tf_op jit(solution)/shard_map/ppermute | solution.py:352
  26.6 3.2 %forward.1 = (bf16[192,512]{1,0:T(8,128)(2,1)S(1)}, f32[8,512]{1,0:T(8,128)S(1)}, f32[16,384]{1,0:T(8,128)S(1)}, f32[16,384]{1,0:T(8,128)S(1)}, bf16[3,1280,512]...) custom-call(bf16[2,192,512]{2,1,0:T(8,128)(2,1)S(1)} %get-tuple-element.64.pair_ref, ...), custom_call_target="tpu_custom_call" | custom-call | flops 1 | bytes 1 | tf_op jit(solution)/shard_map/forward/pallas_call | solution.py:50
  29.9 0.5 weight.1
  30.3 1.3 %collective-permute-start.18 = (bf16[96,768]{1,0:T(8,128)(2,1)S(1)}, bf16[96,768]{1,0:T(8,128)(2,1)S(1)}, u32[]{:S(2)}, u32[]{:S(2)}) collective-permute-start(bf16[96,768]{1,0:T(8,128)(2,1)S(1)} %get-tuple-element.88.refs_4_), channel_id=1, source_target_pairs={{0,16},{16,0},{1,17},{17,1},{2,18},{18,2},{3,19},{19,3},{4,20},{20... | collective-permute-start | bytes 442376 | tf_op jit(solution)/shard_map/ppermute | solution.py:356
  31.6 2.4 %query_grad.1 = (bf16[192,512]{1,0:T(8,128)(2,1)S(1)}, f32[2,192,512]{2,1,0:T(8,128)S(1)}, f32[8,128]{1,0:T(8,128)S(1)}) custom-call(bf16[2,192,1280]{2,1,0:T(8,128)(2,1)S(1)} %get-tuple-element.82.refs_0_, bf16[3,1280,512]{2,1,0:T(8,128)(2,1)S(1)} %get-tuple-element.83.refs_1_, bf16[2,192,512]{2,1,0:T(8,128)(2,1)S(1)} %get-tuple-element.79.query_ref.refs_2_, ...), custom_call_target="tpu_custom_call" | custom-call | flops 1 | bytes 1 | tf_op jit(solution)/shard_map/query_grad/pallas_call | solution.py:50
  34.1 0.3 collective-permute-start.13
  34.4 3.0 %collective-permute-start.14 = (f32[16,384]{1,0:T(8,128)S(1)}, f32[16,384]{1,0:T(8,128)S(1)}, u32[]{:S(2)}, u32[]{:S(2)}) collective-permute-start(f32[16,384]{1,0:T(8,128)S(1)} %get-tuple-element.91), channel_id=1, source_target_pairs={{0,12},{1,13},{2,14},{3,15},{4,0},{5,1},{6,2},{7,3},{8,4},{9,5},{1... | collective-permute-start | bytes 73736 | tf_op jit(solution)/shard_map/ppermute | solution.py:352
  37.4 0.1 collective-permute-start.19
  37.5 1.4 %collective-permute-start.20 = (bf16[48,768]{1,0:T(8,128)(2,1)S(1)}, bf16[48,768]{1,0:T(8,128)(2,1)S(1)}, u32[]{:S(2)}, u32[]{:S(2)}) collective-permute-start(bf16[48,768]{1,0:T(8,128)(2,1)S(1)} %get-tuple-element.106.refs_1_), channel_id=1, source_target_pairs={{4,0},{5,1},{6,2},{7,3},{0,4},{1,5},{2,6},{3,7},{12,8},{13,9},{14,... | collective-permute-start | bytes 221192 | tf_op jit(solution)/shard_map/ppermute | solution.py:345
  39.0 0.2 collective-permute-done.13.stats_low
  39.2 0.3 collective-permute-done.14.stats_high
  39.5 1.9 %key_grad.1 = (bf16[4,192,128]{2,1,0:T(8,128)(2,1)S(1)}, bf16[4,192,128]{2,1,0:T(8,128)(2,1)S(1)}, bf16[4,192,128]{2,1,0:T(8,128)(2,1)S(1)}, bf16[4,192,128]{2,1,0:T(8,128)(2,1)S(1)}, f32[8,128]{1,0:T(8,128)S(1)}) custom-call(bf16[2,192,512]{2,1,0:T(8,128)(2,1)S(1)} %get-tuple-element.64.pair_ref, bf16[2,192,384]{2,1,0:T(8,128)(2,1)S(1)} %collective-permute-done.6.low_ref, ...), custom_call_target="tpu_custom_call" | custom-call | flops 1 | bytes 1 | tf_op jit(solution)/shard_map/key_grad/pallas_call | solution.py:50
  41.4 3.1 %collective-permute-start.15 = (bf16[4,192,128]{2,1,0:T(8,128)(2,1)S(1)}, bf16[4,192,128]{2,1,0:T(8,128)(2,1)S(1)}, u32[]{:S(2)}, u32[]{:S(2)}) collective-permute-start(bf16[4,192,128]{2,1,0:T(8,128)(2,1)S(1)} %get-tuple-element.96), channel_id=1, source_target_pairs={{1,0},{0,1},{3,2},{2,3},{5,4},{4,5},{7,6},{6,7},{9,8},{8,9},{11,10... | collective-permute-start | bytes 589832 | tf_op jit(solution)/shard_map/ppermute | solution.py:345
  44.5 0.7 %collective-permute-start.21 = (bf16[96,768]{1,0:T(8,128)(2,1)S(1)}, bf16[96,768]{1,0:T(8,128)(2,1)S(1)}, u32[]{:S(2)}, u32[]{:S(2)}) collective-permute-start(bf16[96,768]{1,0:T(8,128)(2,1)S(1)} %meet.1.refs_0_), channel_id=1, source_target_pairs={{8,0},{9,1},{10,2},{11,3},{12,4},{13,5},{14,6},{15,7},{0,8},{1,9},... | collective-permute-start | bytes 442376 | tf_op jit(solution)/shard_map/ppermute | solution.py:345
  45.3 2.2 %collective-permute-start.17 = (bf16[4,192,128]{2,1,0:T(8,128)(2,1)S(1)}, bf16[4,192,128]{2,1,0:T(8,128)(2,1)S(1)}, u32[]{:S(2)}, u32[]{:S(2)}) collective-permute-start(bf16[4,192,128]{2,1,0:T(8,128)(2,1)S(1)} %get-tuple-element.98), channel_id=1, source_target_pairs={{3,0},{2,1},{1,2},{0,3},{7,4},{6,5},{5,6},{4,7},{11,8},{10,9},{9,1... | collective-permute-start | bytes 589832 | tf_op jit(solution)/shard_map/ppermute | solution.py:345
  47.5 6.0 %collective-permute-done.21.refs_1_ = bf16[96,768]{1,0:T(8,128)(2,1)S(1)} collective-permute-done((bf16[96,768]{1,0:T(8,128)(2,1)S(1)}, bf16[96,768]{1,0:T(8,128)(2,1)S(1)}, u32[]{:S(2)}, u32[]{:S(2)}) %collective-permute-start.21) | collective-permute-done | bytes 147488 | tf_op jit(solution)/shard_map/ppermute | solution.py:345
  53.5 0.8 %collective-permute-start.22 = (bf16[96,768]{1,0:T(8,128)(2,1)S(1)}, bf16[96,768]{1,0:T(8,128)(2,1)S(1)}, u32[]{:S(2)}, u32[]{:S(2)}) collective-permute-start(bf16[96,768]{1,0:T(8,128)(2,1)S(1)} %add.1.refs_0_), channel_id=1, source_target_pairs={{0,2},{1,3},{2,18},{3,19},{4,6},{5,7},{6,22},{7,23},{8,10},{9,11},... | collective-permute-start | bytes 442376 | tf_op jit(solution)/shard_map/ppermute | solution.py:471
  54.3 2.6 %collective-permute-start.23 = (bf16[96,768]{1,0:T(8,128)(2,1)S(1)}, bf16[96,768]{1,0:T(8,128)(2,1)S(1)}, u32[]{:S(2)}, u32[]{:S(2)}) collective-permute-start(bf16[96,768]{1,0:T(8,128)(2,1)S(1)} %add.1.refs_0_), channel_id=1, source_target_pairs={{2,16},{3,17},{6,20},{7,21},{10,24},{11,25},{14,28},{15,29},{16,2}... | collective-permute-start | bytes 442376 | tf_op jit(solution)/shard_map/ppermute | solution.py:471
  56.9 1.2 %output.1 = (bf16[128,768]{1,0:T(8,128)(2,1)}, bf16[128,768]{1,0:T(8,128)(2,1)}, bf16[128,768]{1,0:T(8,128)(2,1)}, bf16[128,768]{1,0:T(8,128)(2,1)}, f32[8,128]{1,0:T(8,128)S(1)}) custom-call(bf16[4,192,128]{2,1,0:T(8,128)(2,1)S(1)} %get-tuple-element.95.refs_0_, bf16[4,192,128]{2,1,0:T(8,128)(2,1)S(1)} %collective-permute-done.15.refs_1_.refs_2_, ...), custom_call_target="tpu_custom_call" | custom-call | flops 1 | bytes 1 | tf_op jit(solution)/shard_map/output/pallas_call | solution.py:50
  58.1 2.9 %collective-permute-done.23.refs_2_ = bf16[96,768]{1,0:T(8,128)(2,1)S(1)} collective-permute-done((bf16[96,768]{1,0:T(8,128)(2,1)S(1)}, bf16[96,768]{1,0:T(8,128)(2,1)S(1)}, u32[]{:S(2)}, u32[]{:S(2)}) %collective-permute-start.23) | collective-permute-done | bytes 147488 | tf_op jit(solution)/shard_map/ppermute | solution.py:471
  61.1 2.7 %collective-permute-start.24 = (bf16[192,768]{1,0:T(8,128)(2,1)S(1)}, bf16[192,768]{1,0:T(8,128)(2,1)S(1)}, u32[]{:S(2)}, u32[]{:S(2)}) collective-permute-start(bf16[192,768]{1,0:T(8,128)(2,1)S(1)} %cross.1.value_ref), channel_id=1, source_target_pairs={{1,0},{0,1},{3,2},{2,3},{5,4},{4,5},{7,6},{6,7},{9,8},{8,9},{11,10... | collective-permute-start | bytes 884744 | tf_op jit(solution)/shard_map/ppermute | solution.py:345
  63.8 0.9 %write.2.refs_0_ = f32[384,768]{1,0:T(8,128)} custom-call(bf16[192,768]{1,0:T(8,128)(2,1)S(1)} %cross.1.value_ref), custom_call_target="tpu_custom_call" | custom-call | flops 1 | bytes 1 | tf_op jit(solution)/shard_map/write/pallas_call | solution.py:476
  64.7 0.3 collective-permute-done.24.value_ref
  65.0 0.9 %write.3 = f32[384,768]{1,0:T(8,128)} custom-call(bf16[192,768]{1,0:T(8,128)(2,1)S(1)} %collective-permute-done.24.value_ref, f32[384,768]{1,0:T(8,128)} %write.2.refs_0_), custom_call_target="tpu_custom_call", output_to_operand_aliasing={{}: (1, {})} | custom-call | flops 1 | bytes 1 | tf_op jit(solution)/shard_map/write/pallas_call | solution.py:476
  (33 shorter events, 0.2 us)
Async XLA Ops:
  0.6 10.2 %copy-start.4 = (bf16[1,1,128,768]{3,2,1,0:T(8,128)(2,1)S(1)}, bf16[1,1,128,768]{3,2,1,0:T(8,128)(2,1)}, u32[]{:S(2)}) copy-start(bf16[1,1,128,768]{3,2,1,0:T(8,128)(2,1)} %param.10) | copy-start | bytes 589828
  0.6 20.5 %copy-start.6 = (s32[16,6]{0,1:T(8,128)S(1)}, s32[16,6]{0,1:T(8,128)}, u32[]{:S(2)}) copy-start(s32[16,6]{0,1:T(8,128)} %param.12) | copy-start | bytes 1156
  0.7 20.6 %copy-start.5 = (s32[16]{0:T(128)S(1)}, s32[16]{0:T(128)}, u32[]{:S(2)}) copy-start(s32[16]{0:T(128)} %count_ref.1) | copy-start | bytes 196
  1.9 6.1 %collective-permute-start = (bf16[2,192,128]{2,1,0:T(8,128)(2,1)S(1)}, bf16[2,192,128]{2,1,0:T(8,128)(2,1)S(1)}, u32[]{:S(2)}, u32[]{:S(2)}) collective-permute-start(bf16[2,192,128]{2,1,0:T(8,128)(2,1)S(1)} %get-tuple-element.61), channel_id=1, source_target_pairs={{1,0},{0,1},{3,2},{2,3},{5,4},{4,5},{7,6},{6,7},{9,8},{8,9},{11,10... | collective-permute-start | bytes 294920 | tf_op jit(solution)/shard_map/ppermute | solution.py:345
  2.6 5.4 %collective-permute-start.1 = (bf16[2,192,128]{2,1,0:T(8,128)(2,1)S(1)}, bf16[2,192,128]{2,1,0:T(8,128)(2,1)S(1)}, u32[]{:S(2)}, u32[]{:S(2)}) collective-permute-start(bf16[2,192,128]{2,1,0:T(8,128)(2,1)S(1)} %get-tuple-element.62), channel_id=1, source_target_pairs={{2,0},{3,1},{0,2},{1,3},{6,4},{7,5},{4,6},{5,7},{10,8},{11,9},{8,1... | collective-permute-start | bytes 294920 | tf_op jit(solution)/shard_map/ppermute | solution.py:345
  2.6 6.6 %collective-permute-start.2 = (bf16[2,192,128]{2,1,0:T(8,128)(2,1)S(1)}, bf16[2,192,128]{2,1,0:T(8,128)(2,1)S(1)}, u32[]{:S(2)}, u32[]{:S(2)}) collective-permute-start(bf16[2,192,128]{2,1,0:T(8,128)(2,1)S(1)} %get-tuple-element.63), channel_id=1, source_target_pairs={{3,0},{2,1},{1,2},{0,3},{7,4},{6,5},{5,6},{4,7},{11,8},{10,9},{9,1... | collective-permute-start | bytes 294920 | tf_op jit(solution)/shard_map/ppermute | solution.py:345
  4.4 1.3 %copy-start = (bf16[768,768]{1,0:T(8,128)(2,1)S(1)}, bf16[768,768]{1,0:T(8,128)(2,1)}, u32[]{:S(2)}) copy-start(bf16[768,768]{1,0:T(8,128)(2,1)} %refs_4_.1) | copy-start | bytes 3538948
  5.6 0.9 %copy-start.2 = (bf16[1,1,128,768]{3,2,1,0:T(8,128)(2,1)S(1)}, bf16[1,1,128,768]{3,2,1,0:T(8,128)(2,1)}, u32[]{:S(2)}) copy-start(bf16[1,1,128,768]{3,2,1,0:T(8,128)(2,1)} %param.7) | copy-start | bytes 589828
  6.5 0.9 %copy-start.3 = (bf16[1,1,128,768]{3,2,1,0:T(8,128)(2,1)S(1)}, bf16[1,1,128,768]{3,2,1,0:T(8,128)(2,1)}, u32[]{:S(2)}) copy-start(bf16[1,1,128,768]{3,2,1,0:T(8,128)(2,1)} %param.10) | copy-start | bytes 589828
  9.4 14.6 %collective-permute-start.8 = (bf16[2,192,384]{2,1,0:T(8,128)(2,1)S(1)}, bf16[2,192,384]{2,1,0:T(8,128)(2,1)S(1)}, u32[]{:S(2)}, u32[]{:S(2)}) collective-permute-start(bf16[2,192,384]{2,1,0:T(8,128)(2,1)S(1)} %get-tuple-element.77), channel_id=1, source_target_pairs={{0,4},{1,5},{2,6},{3,7},{4,8},{5,9},{6,10},{7,11},{8,12},{9,13},{1... | collective-permute-start | bytes 884744 | tf_op jit(solution)/shard_map/ppermute | solution.py:351
  10.8 10.4 %collective-permute-start.11 = (bf16[128,768]{1,0:T(8,128)(2,1)S(1)}, bf16[128,768]{1,0:T(8,128)(2,1)S(1)}, u32[]{:S(2)}, u32[]{:S(2)}) collective-permute-start(bf16[128,768]{1,0:T(8,128)(2,1)S(1)} %bitcast.10), channel_id=1, source_target_pairs={{2,0},{3,1},{0,2},{1,3},{6,4},{7,5},{4,6},{5,7},{10,8},{11,9},{8,1... | collective-permute-start | bytes 589832 | tf_op jit(solution)/shard_map/ppermute | solution.py:345
  11.0 4.0 %collective-permute-start.3 = (bf16[2,192,128]{2,1,0:T(8,128)(2,1)S(1)}, bf16[2,192,128]{2,1,0:T(8,128)(2,1)S(1)}, u32[]{:S(2)}, u32[]{:S(2)}) collective-permute-start(bf16[2,192,128]{2,1,0:T(8,128)(2,1)S(1)} %get-tuple-element.71), channel_id=1, source_target_pairs={{1,0},{0,1},{3,2},{2,3},{5,4},{4,5},{7,6},{6,7},{9,8},{8,9},{11,10... | collective-permute-start | bytes 294920 | tf_op jit(solution)/shard_map/ppermute | solution.py:345
  11.8 14.8 %collective-permute-start.9 = (bf16[2,192,384]{2,1,0:T(8,128)(2,1)S(1)}, bf16[2,192,384]{2,1,0:T(8,128)(2,1)S(1)}, u32[]{:S(2)}, u32[]{:S(2)}) collective-permute-start(bf16[2,192,384]{2,1,0:T(8,128)(2,1)S(1)} %get-tuple-element.78), channel_id=1, source_target_pairs={{0,12},{1,13},{2,14},{3,15},{4,0},{5,1},{6,2},{7,3},{8,4},{9,5},{1... | collective-permute-start | bytes 884744 | tf_op jit(solution)/shard_map/ppermute | solution.py:352
  13.7 5.1 %collective-permute-start.4 = (bf16[2,192,128]{2,1,0:T(8,128)(2,1)S(1)}, bf16[2,192,128]{2,1,0:T(8,128)(2,1)S(1)}, u32[]{:S(2)}, u32[]{:S(2)}) collective-permute-start(bf16[2,192,128]{2,1,0:T(8,128)(2,1)S(1)} %get-tuple-element.72), channel_id=1, source_target_pairs={{2,0},{3,1},{0,2},{1,3},{6,4},{7,5},{4,6},{5,7},{10,8},{11,9},{8,1... | collective-permute-start | bytes 294920 | tf_op jit(solution)/shard_map/ppermute | solution.py:345
  15.0 7.5 %collective-permute-start.5 = (bf16[2,192,128]{2,1,0:T(8,128)(2,1)S(1)}, bf16[2,192,128]{2,1,0:T(8,128)(2,1)S(1)}, u32[]{:S(2)}, u32[]{:S(2)}) collective-permute-start(bf16[2,192,128]{2,1,0:T(8,128)(2,1)S(1)} %get-tuple-element.73), channel_id=1, source_target_pairs={{3,0},{2,1},{1,2},{0,3},{7,4},{6,5},{5,6},{4,7},{11,8},{10,9},{9,1... | collective-permute-start | bytes 294920 | tf_op jit(solution)/shard_map/ppermute | solution.py:345
  18.8 11.0 %collective-permute-start.10 = (bf16[128,768]{1,0:T(8,128)(2,1)S(1)}, bf16[128,768]{1,0:T(8,128)(2,1)S(1)}, u32[]{:S(2)}, u32[]{:S(2)}) collective-permute-start(bf16[128,768]{1,0:T(8,128)(2,1)S(1)} %bitcast.11), channel_id=1, source_target_pairs={{1,0},{0,1},{3,2},{2,3},{5,4},{4,5},{7,6},{6,7},{9,8},{8,9},{11,10... | collective-permute-start | bytes 589832 | tf_op jit(solution)/shard_map/ppermute | solution.py:345
  21.2 8.7 %collective-permute-start.12 = (bf16[128,768]{1,0:T(8,128)(2,1)S(1)}, bf16[128,768]{1,0:T(8,128)(2,1)S(1)}, u32[]{:S(2)}, u32[]{:S(2)}) collective-permute-start(bf16[128,768]{1,0:T(8,128)(2,1)S(1)} %collective-permute-done.11.refs_2_), channel_id=1, source_target_pairs={{1,0},{0,1},{3,2},{2,3},{5,4},{4,5},{7,6},{6,7},{9,8},{8,9},{11,10... | collective-permute-start | bytes 589832 | tf_op jit(solution)/shard_map/ppermute | solution.py:345
  22.7 14.8 %collective-permute-start.6 = (bf16[2,192,384]{2,1,0:T(8,128)(2,1)S(1)}, bf16[2,192,384]{2,1,0:T(8,128)(2,1)S(1)}, u32[]{:S(2)}, u32[]{:S(2)}) collective-permute-start(bf16[2,192,384]{2,1,0:T(8,128)(2,1)S(1)} %get-tuple-element.75), channel_id=1, source_target_pairs={{0,4},{1,5},{2,6},{3,7},{4,8},{5,9},{6,10},{7,11},{8,12},{9,13},{1... | collective-permute-start | bytes 884744 | tf_op jit(solution)/shard_map/ppermute | solution.py:351
  24.0 14.9 %collective-permute-start.7 = (bf16[2,192,384]{2,1,0:T(8,128)(2,1)S(1)}, bf16[2,192,384]{2,1,0:T(8,128)(2,1)S(1)}, u32[]{:S(2)}, u32[]{:S(2)}) collective-permute-start(bf16[2,192,384]{2,1,0:T(8,128)(2,1)S(1)} %get-tuple-element.76), channel_id=1, source_target_pairs={{0,12},{1,13},{2,14},{3,15},{4,0},{5,1},{6,2},{7,3},{8,4},{9,5},{1... | collective-permute-start | bytes 884744 | tf_op jit(solution)/shard_map/ppermute | solution.py:352
  30.3 7.1 %collective-permute-start.18 = (bf16[96,768]{1,0:T(8,128)(2,1)S(1)}, bf16[96,768]{1,0:T(8,128)(2,1)S(1)}, u32[]{:S(2)}, u32[]{:S(2)}) collective-permute-start(bf16[96,768]{1,0:T(8,128)(2,1)S(1)} %get-tuple-element.88.refs_4_), channel_id=1, source_target_pairs={{0,16},{16,0},{1,17},{17,1},{2,18},{18,2},{3,19},{19,3},{4,20},{20... | collective-permute-start | bytes 442376 | tf_op jit(solution)/shard_map/ppermute | solution.py:356
  34.1 5.1 %collective-permute-start.13 = (f32[16,384]{1,0:T(8,128)S(1)}, f32[16,384]{1,0:T(8,128)S(1)}, u32[]{:S(2)}, u32[]{:S(2)}) collective-permute-start(f32[16,384]{1,0:T(8,128)S(1)} %get-tuple-element.90), channel_id=1, source_target_pairs={{0,4},{1,5},{2,6},{3,7},{4,8},{5,9},{6,10},{7,11},{8,12},{9,13},{1... | collective-permute-start | bytes 73736 | tf_op jit(solution)/shard_map/ppermute | solution.py:351
  34.4 5.1 %collective-permute-start.14 = (f32[16,384]{1,0:T(8,128)S(1)}, f32[16,384]{1,0:T(8,128)S(1)}, u32[]{:S(2)}, u32[]{:S(2)}) collective-permute-start(f32[16,384]{1,0:T(8,128)S(1)} %get-tuple-element.91), channel_id=1, source_target_pairs={{0,12},{1,13},{2,14},{3,15},{4,0},{5,1},{6,2},{7,3},{8,4},{9,5},{1... | collective-permute-start | bytes 73736 | tf_op jit(solution)/shard_map/ppermute | solution.py:352
  37.4 7.1 %collective-permute-start.19 = (bf16[48,768]{1,0:T(8,128)(2,1)S(1)}, bf16[48,768]{1,0:T(8,128)(2,1)S(1)}, u32[]{:S(2)}, u32[]{:S(2)}) collective-permute-start(bf16[48,768]{1,0:T(8,128)(2,1)S(1)} %get-tuple-element.105.refs_0_), channel_id=1, source_target_pairs={{4,0},{5,1},{6,2},{7,3},{0,4},{1,5},{2,6},{3,7},{12,8},{13,9},{14,... | collective-permute-start | bytes 221192 | tf_op jit(solution)/shard_map/ppermute | solution.py:345
  37.5 7.0 %collective-permute-start.20 = (bf16[48,768]{1,0:T(8,128)(2,1)S(1)}, bf16[48,768]{1,0:T(8,128)(2,1)S(1)}, u32[]{:S(2)}, u32[]{:S(2)}) collective-permute-start(bf16[48,768]{1,0:T(8,128)(2,1)S(1)} %get-tuple-element.106.refs_1_), channel_id=1, source_target_pairs={{4,0},{5,1},{6,2},{7,3},{0,4},{1,5},{2,6},{3,7},{12,8},{13,9},{14,... | collective-permute-start | bytes 221192 | tf_op jit(solution)/shard_map/ppermute | solution.py:345
  39.5 17.4 %copy-start.1 = (bf16[768,768]{1,0:T(8,128)(2,1)S(1)}, bf16[768,768]{1,0:T(8,128)(2,1)}, u32[]{:S(2)}) copy-start(bf16[768,768]{1,0:T(8,128)(2,1)} %refs_4_.1) | copy-start | bytes 3538948
  41.4 6.1 %collective-permute-start.15 = (bf16[4,192,128]{2,1,0:T(8,128)(2,1)S(1)}, bf16[4,192,128]{2,1,0:T(8,128)(2,1)S(1)}, u32[]{:S(2)}, u32[]{:S(2)}) collective-permute-start(bf16[4,192,128]{2,1,0:T(8,128)(2,1)S(1)} %get-tuple-element.96), channel_id=1, source_target_pairs={{1,0},{0,1},{3,2},{2,3},{5,4},{4,5},{7,6},{6,7},{9,8},{8,9},{11,10... | collective-permute-start | bytes 589832 | tf_op jit(solution)/shard_map/ppermute | solution.py:345
  44.5 8.9 %collective-permute-start.21 = (bf16[96,768]{1,0:T(8,128)(2,1)S(1)}, bf16[96,768]{1,0:T(8,128)(2,1)S(1)}, u32[]{:S(2)}, u32[]{:S(2)}) collective-permute-start(bf16[96,768]{1,0:T(8,128)(2,1)S(1)} %meet.1.refs_0_), channel_id=1, source_target_pairs={{8,0},{9,1},{10,2},{11,3},{12,4},{13,5},{14,6},{15,7},{0,8},{1,9},... | collective-permute-start | bytes 442376 | tf_op jit(solution)/shard_map/ppermute | solution.py:345
  45.3 11.6 %collective-permute-start.16 = (bf16[4,192,128]{2,1,0:T(8,128)(2,1)S(1)}, bf16[4,192,128]{2,1,0:T(8,128)(2,1)S(1)}, u32[]{:S(2)}, u32[]{:S(2)}) collective-permute-start(bf16[4,192,128]{2,1,0:T(8,128)(2,1)S(1)} %get-tuple-element.97), channel_id=1, source_target_pairs={{2,0},{3,1},{0,2},{1,3},{6,4},{7,5},{4,6},{5,7},{10,8},{11,9},{8,1... | collective-permute-start | bytes 589832 | tf_op jit(solution)/shard_map/ppermute | solution.py:345
  45.3 11.6 %collective-permute-start.17 = (bf16[4,192,128]{2,1,0:T(8,128)(2,1)S(1)}, bf16[4,192,128]{2,1,0:T(8,128)(2,1)S(1)}, u32[]{:S(2)}, u32[]{:S(2)}) collective-permute-start(bf16[4,192,128]{2,1,0:T(8,128)(2,1)S(1)} %get-tuple-element.98), channel_id=1, source_target_pairs={{3,0},{2,1},{1,2},{0,3},{7,4},{6,5},{5,6},{4,7},{11,8},{10,9},{9,1... | collective-permute-start | bytes 589832 | tf_op jit(solution)/shard_map/ppermute | solution.py:345
  53.5 4.6 %collective-permute-start.22 = (bf16[96,768]{1,0:T(8,128)(2,1)S(1)}, bf16[96,768]{1,0:T(8,128)(2,1)S(1)}, u32[]{:S(2)}, u32[]{:S(2)}) collective-permute-start(bf16[96,768]{1,0:T(8,128)(2,1)S(1)} %add.1.refs_0_), channel_id=1, source_target_pairs={{0,2},{1,3},{2,18},{3,19},{4,6},{5,7},{6,22},{7,23},{8,10},{9,11},... | collective-permute-start | bytes 442376 | tf_op jit(solution)/shard_map/ppermute | solution.py:471
  54.3 6.8 %collective-permute-start.23 = (bf16[96,768]{1,0:T(8,128)(2,1)S(1)}, bf16[96,768]{1,0:T(8,128)(2,1)S(1)}, u32[]{:S(2)}, u32[]{:S(2)}) collective-permute-start(bf16[96,768]{1,0:T(8,128)(2,1)S(1)} %add.1.refs_0_), channel_id=1, source_target_pairs={{2,16},{3,17},{6,20},{7,21},{10,24},{11,25},{14,28},{15,29},{16,2}... | collective-permute-start | bytes 442376 | tf_op jit(solution)/shard_map/ppermute | solution.py:471
  61.1 3.9 %collective-permute-start.24 = (bf16[192,768]{1,0:T(8,128)(2,1)S(1)}, bf16[192,768]{1,0:T(8,128)(2,1)S(1)}, u32[]{:S(2)}, u32[]{:S(2)}) collective-permute-start(bf16[192,768]{1,0:T(8,128)(2,1)S(1)} %cross.1.value_ref), channel_id=1, source_target_pairs={{1,0},{0,1},{3,2},{2,3},{5,4},{4,5},{7,6},{6,7},{9,8},{8,9},{11,10... | collective-permute-start | bytes 884744 | tf_op jit(solution)/shard_map/ppermute | solution.py:345

commit v20 on v19

--- a/solution.py
+++ b/solution.py
@@ -448,15 +448,15 @@
         )
         (total,) = call(
             meet_kernel, [VMEM] * 4, [shape_of(count, width)],
-            (top, bottom, swap(top, LAYER), swap(bottom, LAYER)), name="meet", after=(key_token,),
+            (top, bottom, swap(top, stations // 2), swap(bottom, stations // 2)), name="meet", after=(key_token,),
         )
-        stride = 2 * LAYER
-        while stride < stations:
+        stride = stations // 4
+        while stride >= LAYER:
             (total,) = call(
                 round_kernel, [VMEM] * 2, [shape_of(count, width)], (total, swap(total, stride)),
-                name="add", after=parts[:1] if 2 * stride >= stations else (),
+                name="add", after=parts[:1] if stride == LAYER else (),
             )
-            stride *= 2
+            stride //= 2
         first, second = [], []
         for w in range(2):
             for s in range(stations):

time: 66.1 us -> 65.2 us (0.986)
  waiting for transfers between devices: 15 us -> 10.9 us
  starting transfers between devices: 32.6 us -> 35.8 us
    ppermute x1, waiting for transfers between devices: 2.94 us -> 0.75 us  [local(): lax.ppermute(total, axes, second)]
    ppermute x1, starting transfers between devices: 0.78 us -> 2.95 us  [local(): lax.ppermute(total, axes, first)]
    ppermute x16, starting transfers between devices: 18 us -> 19.7 us  [swap(): lax.ppermute(value, 'station', [(s ^ stride, s) for s in range(stations)])]
    ppermute x16, waiting for transfers between devices: 10.8 us -> 9.48 us  [swap(): lax.ppermute(value, 'station', [(s ^ stride, s) for s in range(stations)])]
    ppermute x1, starting transfers between devices: 2.61 us -> 1.91 us  [local(): lax.ppermute(total, axes, second)]
where the time goes in v20:
time: 65.2 us; the launch traced here: 65 us
  starting transfers between devices  35.8 us (55%)
  Pallas kernels  14.2 us (22%)
  waiting for transfers between devices  10.9 us (17%)
  local copies, waits for them, and re-layouts  3.23 us (5%)
  between operations  0.84 us (1%)
    ppermute x16, starting transfers between devices, swap(): lax.ppermute(value, 'station', [(s ^ stride, s) for s in range(stations)])  19.7 us
    pallas_call x14, Pallas kernels, call(): pl.pallas_call(kernel, in_specs=ins, out_specs=[VMEM] * len(outs), out_sh...  12.5 us
    ppermute x16, waiting for transfers between devices, swap(): lax.ppermute(value, 'station', [(s ^ stride, s) for s in range(stations)])  9.48 us
    ppermute x3, starting transfers between devices, along(): lax.ppermute(down, 'station', [(s, (s - LAYER) % stations) for s in range...  6.84 us
    unnamed x15, local copies, waits for them, and re-layouts  3.23 us
    ppermute x3, starting transfers between devices, along(): lax.ppermute(up, 'station', [(s, (s + LAYER) % stations) for s in range(s...  3.03 us
    ppermute x1, starting transfers between devices, local(): lax.ppermute(total, axes, first)  2.95 us
    ppermute x1, starting transfers between devices, local(): lax.ppermute(total, axes, second)  1.91 us
  transfers between devices with their start and end apart: 25, of which 8 were waited for; matrix products, arithmetic and copies ran while one was open for 0% of the time, Pallas kernels for 18%

profile of v20, /device:TPU:3, one launch (start us, length us, event | category | flops | bytes accessed | tf_op | source)
XLA Modules:
  0.0 65.0 jit_solution(14232541554432940736)
XLA Ops:
  0.6 0.0 copy-start.4
  0.7 1.2 %pack.1 = (bf16[2,192,128]{2,1,0:T(8,128)(2,1)S(1)}, bf16[2,192,128]{2,1,0:T(8,128)(2,1)S(1)}, bf16[2,192,128]{2,1,0:T(8,128)(2,1)S(1)}, bf16[2,192,128]{2,1,0:T(8,128)(2,1)S(1)}) custom-call(bf16[128,768]{1,0:T(8,128)(2,1)} %bitcast.12, bf16[128,768]{1,0:T(8,128)(2,1)} %bitcast.13), custom_call_target="tpu_custom_call" | custom-call | flops 1 | bytes 1 | tf_op jit(solution)/shard_map/pack/pallas_call | solution.py:50
  1.9 0.7 %collective-permute-start = (bf16[2,192,128]{2,1,0:T(8,128)(2,1)S(1)}, bf16[2,192,128]{2,1,0:T(8,128)(2,1)S(1)}, u32[]{:S(2)}, u32[]{:S(2)}) collective-permute-start(bf16[2,192,128]{2,1,0:T(8,128)(2,1)S(1)} %get-tuple-element.61), channel_id=1, source_target_pairs={{1,0},{0,1},{3,2},{2,3},{5,4},{4,5},{7,6},{6,7},{9,8},{8,9},{11,10... | collective-permute-start | bytes 294920 | tf_op jit(solution)/shard_map/ppermute | solution.py:345
  2.6 1.7 %collective-permute-start.2 = (bf16[2,192,128]{2,1,0:T(8,128)(2,1)S(1)}, bf16[2,192,128]{2,1,0:T(8,128)(2,1)S(1)}, u32[]{:S(2)}, u32[]{:S(2)}) collective-permute-start(bf16[2,192,128]{2,1,0:T(8,128)(2,1)S(1)} %get-tuple-element.63), channel_id=1, source_target_pairs={{3,0},{2,1},{1,2},{0,3},{7,4},{6,5},{5,6},{4,7},{11,8},{10,9},{9,1... | collective-permute-start | bytes 294920 | tf_op jit(solution)/shard_map/ppermute | solution.py:345
  4.4 1.3 %copy-done = bf16[768,768]{1,0:T(8,128)(2,1)S(1)} copy-done((bf16[768,768]{1,0:T(8,128)(2,1)S(1)}, bf16[768,768]{1,0:T(8,128)(2,1)}, u32[]{:S(2)}) %copy-start) | copy-done | bytes 1179672
  5.6 0.9 %copy-done.2 = bf16[1,1,128,768]{3,2,1,0:T(8,128)(2,1)S(1)} copy-done((bf16[1,1,128,768]{3,2,1,0:T(8,128)(2,1)S(1)}, bf16[1,1,128,768]{3,2,1,0:T(8,128)(2,1)}, u32[]{:S(2)}) %copy-start.2) | copy-done | bytes 196632
  6.6 0.9 %copy-done.3 = bf16[1,1,128,768]{3,2,1,0:T(8,128)(2,1)S(1)} copy-done((bf16[1,1,128,768]{3,2,1,0:T(8,128)(2,1)S(1)}, bf16[1,1,128,768]{3,2,1,0:T(8,128)(2,1)}, u32[]{:S(2)}) %copy-start.3) | copy-done | bytes 196632
  7.5 0.5 project.1
  8.0 1.3 %collective-permute-done.2.refs_3_ = bf16[2,192,128]{2,1,0:T(8,128)(2,1)S(1)} collective-permute-done((bf16[2,192,128]{2,1,0:T(8,128)(2,1)S(1)}, bf16[2,192,128]{2,1,0:T(8,128)(2,1)S(1)}, u32[]{:S(2)}, u32[]{:S(2)}) %collective-permute-start.2) | collective-permute-done | bytes 98336 | tf_op jit(solution)/shard_map/ppermute | solution.py:345
  9.3 0.1 gather.2
  9.4 1.3 %collective-permute-start.8 = (bf16[2,192,384]{2,1,0:T(8,128)(2,1)S(1)}, bf16[2,192,384]{2,1,0:T(8,128)(2,1)S(1)}, u32[]{:S(2)}, u32[]{:S(2)}) collective-permute-start(bf16[2,192,384]{2,1,0:T(8,128)(2,1)S(1)} %get-tuple-element.77), channel_id=1, source_target_pairs={{0,4},{1,5},{2,6},{3,7},{4,8},{5,9},{6,10},{7,11},{8,12},{9,13},{1... | collective-permute-start | bytes 884744 | tf_op jit(solution)/shard_map/ppermute | solution.py:351
  10.8 0.3 collective-permute-start.11
  11.0 0.8 %collective-permute-start.3 = (bf16[2,192,128]{2,1,0:T(8,128)(2,1)S(1)}, bf16[2,192,128]{2,1,0:T(8,128)(2,1)S(1)}, u32[]{:S(2)}, u32[]{:S(2)}) collective-permute-start(bf16[2,192,128]{2,1,0:T(8,128)(2,1)S(1)} %get-tuple-element.71), channel_id=1, source_target_pairs={{1,0},{0,1},{3,2},{2,3},{5,4},{4,5},{7,6},{6,7},{9,8},{8,9},{11,10... | collective-permute-start | bytes 294920 | tf_op jit(solution)/shard_map/ppermute | solution.py:345
  11.8 1.9 %collective-permute-start.9 = (bf16[2,192,384]{2,1,0:T(8,128)(2,1)S(1)}, bf16[2,192,384]{2,1,0:T(8,128)(2,1)S(1)}, u32[]{:S(2)}, u32[]{:S(2)}) collective-permute-start(bf16[2,192,384]{2,1,0:T(8,128)(2,1)S(1)} %get-tuple-element.78), channel_id=1, source_target_pairs={{0,12},{1,13},{2,14},{3,15},{4,0},{5,1},{6,2},{7,3},{8,4},{9,5},{1... | collective-permute-start | bytes 884744 | tf_op jit(solution)/shard_map/ppermute | solution.py:352
  13.7 1.3 %collective-permute-start.4 = (bf16[2,192,128]{2,1,0:T(8,128)(2,1)S(1)}, bf16[2,192,128]{2,1,0:T(8,128)(2,1)S(1)}, u32[]{:S(2)}, u32[]{:S(2)}) collective-permute-start(bf16[2,192,128]{2,1,0:T(8,128)(2,1)S(1)} %get-tuple-element.72), channel_id=1, source_target_pairs={{2,0},{3,1},{0,2},{1,3},{6,4},{7,5},{4,6},{5,7},{10,8},{11,9},{8,1... | collective-permute-start | bytes 294920 | tf_op jit(solution)/shard_map/ppermute | solution.py:345
  15.0 0.6 collective-permute-start.5
  15.6 3.2 %collective-permute-done.4.refs_2_ = bf16[2,192,128]{2,1,0:T(8,128)(2,1)S(1)} collective-permute-done((bf16[2,192,128]{2,1,0:T(8,128)(2,1)S(1)}, bf16[2,192,128]{2,1,0:T(8,128)(2,1)S(1)}, u32[]{:S(2)}, u32[]{:S(2)}) %collective-permute-start.4) | collective-permute-done | bytes 98336 | tf_op jit(solution)/shard_map/ppermute | solution.py:345
  18.8 2.3 %collective-permute-start.10 = (bf16[128,768]{1,0:T(8,128)(2,1)S(1)}, bf16[128,768]{1,0:T(8,128)(2,1)S(1)}, u32[]{:S(2)}, u32[]{:S(2)}) collective-permute-start(bf16[128,768]{1,0:T(8,128)(2,1)S(1)} %bitcast.11), channel_id=1, source_target_pairs={{1,0},{0,1},{3,2},{2,3},{5,4},{4,5},{7,6},{6,7},{9,8},{8,9},{11,10... | collective-permute-start | bytes 589832 | tf_op jit(solution)/shard_map/ppermute | solution.py:345
  21.2 0.1 copy.13.ids_ref
  21.3 1.2 %live.1 = (f32[16,512]{1,0:T(8,128)S(1)}, f32[8,384]{1,0:T(8,128)S(1)}) custom-call(s32[16,6]{1,0:T(8,128)S(1)} %copy.13.ids_ref, s32[16]{0:T(128)S(1)} %copy-done.5), custom_call_target="tpu_custom_call" | custom-call | flops 1 | bytes 1 | tf_op jit(solution)/shard_map/live/pallas_call | solution.py:50
  22.5 0.1 gather.3
  22.7 1.3 %collective-permute-start.6 = (bf16[2,192,384]{2,1,0:T(8,128)(2,1)S(1)}, bf16[2,192,384]{2,1,0:T(8,128)(2,1)S(1)}, u32[]{:S(2)}, u32[]{:S(2)}) collective-permute-start(bf16[2,192,384]{2,1,0:T(8,128)(2,1)S(1)} %get-tuple-element.75), channel_id=1, source_target_pairs={{0,4},{1,5},{2,6},{3,7},{4,8},{5,9},{6,10},{7,11},{8,12},{9,13},{1... | collective-permute-start | bytes 884744 | tf_op jit(solution)/shard_map/ppermute | solution.py:351
  24.0 2.0 %collective-permute-start.7 = (bf16[2,192,384]{2,1,0:T(8,128)(2,1)S(1)}, bf16[2,192,384]{2,1,0:T(8,128)(2,1)S(1)}, u32[]{:S(2)}, u32[]{:S(2)}) collective-permute-start(bf16[2,192,384]{2,1,0:T(8,128)(2,1)S(1)} %get-tuple-element.76), channel_id=1, source_target_pairs={{0,12},{1,13},{2,14},{3,15},{4,0},{5,1},{6,2},{7,3},{8,4},{9,5},{1... | collective-permute-start | bytes 884744 | tf_op jit(solution)/shard_map/ppermute | solution.py:352
  26.0 0.7 %collective-permute-done.9.high_ref = bf16[2,192,384]{2,1,0:T(8,128)(2,1)S(1)} collective-permute-done((bf16[2,192,384]{2,1,0:T(8,128)(2,1)S(1)}, bf16[2,192,384]{2,1,0:T(8,128)(2,1)S(1)}, u32[]{:S(2)}, u32[]{:S(2)}) %collective-permute-start.9) | collective-permute-done | bytes 294944 | tf_op jit(solution)/shard_map/ppermute | solution.py:352
  26.6 3.2 %forward.1 = (bf16[192,512]{1,0:T(8,128)(2,1)S(1)}, f32[8,512]{1,0:T(8,128)S(1)}, f32[16,384]{1,0:T(8,128)S(1)}, f32[16,384]{1,0:T(8,128)S(1)}, bf16[3,1280,512]...) custom-call(bf16[2,192,512]{2,1,0:T(8,128)(2,1)S(1)} %get-tuple-element.64.pair_ref, ...), custom_call_target="tpu_custom_call" | custom-call | flops 1 | bytes 1 | tf_op jit(solution)/shard_map/forward/pallas_call | solution.py:50
  29.9 0.5 weight.1
  30.3 1.3 %collective-permute-start.18 = (bf16[96,768]{1,0:T(8,128)(2,1)S(1)}, bf16[96,768]{1,0:T(8,128)(2,1)S(1)}, u32[]{:S(2)}, u32[]{:S(2)}) collective-permute-start(bf16[96,768]{1,0:T(8,128)(2,1)S(1)} %get-tuple-element.88.refs_4_), channel_id=1, source_target_pairs={{0,16},{16,0},{1,17},{17,1},{2,18},{18,2},{3,19},{19,3},{4,20},{20... | collective-permute-start | bytes 442376 | tf_op jit(solution)/shard_map/ppermute | solution.py:356
  31.6 2.4 %query_grad.1 = (bf16[192,512]{1,0:T(8,128)(2,1)S(1)}, f32[2,192,512]{2,1,0:T(8,128)S(1)}, f32[8,128]{1,0:T(8,128)S(1)}) custom-call(bf16[2,192,1280]{2,1,0:T(8,128)(2,1)S(1)} %get-tuple-element.82.refs_0_, bf16[3,1280,512]{2,1,0:T(8,128)(2,1)S(1)} %get-tuple-element.83.refs_1_, bf16[2,192,512]{2,1,0:T(8,128)(2,1)S(1)} %get-tuple-element.79.query_ref.refs_2_, ...), custom_call_target="tpu_custom_call" | custom-call | flops 1 | bytes 1 | tf_op jit(solution)/shard_map/query_grad/pallas_call | solution.py:50
  34.1 0.3 collective-permute-start.13
  34.4 3.0 %collective-permute-start.14 = (f32[16,384]{1,0:T(8,128)S(1)}, f32[16,384]{1,0:T(8,128)S(1)}, u32[]{:S(2)}, u32[]{:S(2)}) collective-permute-start(f32[16,384]{1,0:T(8,128)S(1)} %get-tuple-element.91), channel_id=1, source_target_pairs={{0,12},{1,13},{2,14},{3,15},{4,0},{5,1},{6,2},{7,3},{8,4},{9,5},{1... | collective-permute-start | bytes 73736 | tf_op jit(solution)/shard_map/ppermute | solution.py:352
  37.4 0.1 collective-permute-start.19
  37.5 2.3 %collective-permute-start.20 = (bf16[48,768]{1,0:T(8,128)(2,1)S(1)}, bf16[48,768]{1,0:T(8,128)(2,1)S(1)}, u32[]{:S(2)}, u32[]{:S(2)}) collective-permute-start(bf16[48,768]{1,0:T(8,128)(2,1)S(1)} %get-tuple-element.106.refs_1_), channel_id=1, source_target_pairs={{8,0},{9,1},{10,2},{11,3},{12,4},{13,5},{14,6},{15,7},{0,8},{1,9},... | collective-permute-start | bytes 221192 | tf_op jit(solution)/shard_map/ppermute | solution.py:345
  39.9 0.0 copy-start.1
  39.9 1.9 %key_grad.1 = (bf16[4,192,128]{2,1,0:T(8,128)(2,1)S(1)}, bf16[4,192,128]{2,1,0:T(8,128)(2,1)S(1)}, bf16[4,192,128]{2,1,0:T(8,128)(2,1)S(1)}, bf16[4,192,128]{2,1,0:T(8,128)(2,1)S(1)}, f32[8,128]{1,0:T(8,128)S(1)}) custom-call(bf16[2,192,512]{2,1,0:T(8,128)(2,1)S(1)} %get-tuple-element.64.pair_ref, bf16[2,192,384]{2,1,0:T(8,128)(2,1)S(1)} %collective-permute-done.6.low_ref, ...), custom_call_target="tpu_custom_call" | custom-call | flops 1 | bytes 1 | tf_op jit(solution)/shard_map/key_grad/pallas_call | solution.py:50
  41.7 3.6 %collective-permute-start.15 = (bf16[4,192,128]{2,1,0:T(8,128)(2,1)S(1)}, bf16[4,192,128]{2,1,0:T(8,128)(2,1)S(1)}, u32[]{:S(2)}, u32[]{:S(2)}) collective-permute-start(bf16[4,192,128]{2,1,0:T(8,128)(2,1)S(1)} %get-tuple-element.96), channel_id=1, source_target_pairs={{1,0},{0,1},{3,2},{2,3},{5,4},{4,5},{7,6},{6,7},{9,8},{8,9},{11,10... | collective-permute-start | bytes 589832 | tf_op jit(solution)/shard_map/ppermute | solution.py:345
  45.4 0.5 collective-permute-done.20.refs_3_
  45.9 0.2 collective-permute-start.21
  46.1 3.3 %collective-permute-start.17 = (bf16[4,192,128]{2,1,0:T(8,128)(2,1)S(1)}, bf16[4,192,128]{2,1,0:T(8,128)(2,1)S(1)}, u32[]{:S(2)}, u32[]{:S(2)}) collective-permute-start(bf16[4,192,128]{2,1,0:T(8,128)(2,1)S(1)} %get-tuple-element.98), channel_id=1, source_target_pairs={{3,0},{2,1},{1,2},{0,3},{7,4},{6,5},{5,6},{4,7},{11,8},{10,9},{9,1... | collective-permute-start | bytes 589832 | tf_op jit(solution)/shard_map/ppermute | solution.py:345
  49.5 0.5 collective-permute-done.21.refs_1_
  50.0 3.0 %collective-permute-start.22 = (bf16[96,768]{1,0:T(8,128)(2,1)S(1)}, bf16[96,768]{1,0:T(8,128)(2,1)S(1)}, u32[]{:S(2)}, u32[]{:S(2)}) collective-permute-start(bf16[96,768]{1,0:T(8,128)(2,1)S(1)} %add.1.refs_0_), channel_id=1, source_target_pairs={{0,2},{1,3},{2,18},{3,19},{4,6},{5,7},{6,22},{7,23},{8,10},{9,11},... | collective-permute-start | bytes 442376 | tf_op jit(solution)/shard_map/ppermute | solution.py:471
  53.0 1.9 %collective-permute-start.23 = (bf16[96,768]{1,0:T(8,128)(2,1)S(1)}, bf16[96,768]{1,0:T(8,128)(2,1)S(1)}, u32[]{:S(2)}, u32[]{:S(2)}) collective-permute-start(bf16[96,768]{1,0:T(8,128)(2,1)S(1)} %add.1.refs_0_), channel_id=1, source_target_pairs={{2,16},{3,17},{6,20},{7,21},{10,24},{11,25},{14,28},{15,29},{16,2}... | collective-permute-start | bytes 442376 | tf_op jit(solution)/shard_map/ppermute | solution.py:471
  54.9 3.6 %collective-permute-done.17.refs_3_ = bf16[4,192,128]{2,1,0:T(8,128)(2,1)S(1)} collective-permute-done((bf16[4,192,128]{2,1,0:T(8,128)(2,1)S(1)}, bf16[4,192,128]{2,1,0:T(8,128)(2,1)S(1)}, u32[]{:S(2)}, u32[]{:S(2)}) %collective-permute-start.17) | collective-permute-done | bytes 196640 | tf_op jit(solution)/shard_map/ppermute | solution.py:345
  58.5 1.2 %output.1 = (bf16[128,768]{1,0:T(8,128)(2,1)}, bf16[128,768]{1,0:T(8,128)(2,1)}, bf16[128,768]{1,0:T(8,128)(2,1)}, bf16[128,768]{1,0:T(8,128)(2,1)}, f32[8,128]{1,0:T(8,128)S(1)}) custom-call(bf16[4,192,128]{2,1,0:T(8,128)(2,1)S(1)} %get-tuple-element.95.refs_0_, bf16[4,192,128]{2,1,0:T(8,128)(2,1)S(1)} %collective-permute-done.15.refs_1_.refs_2_, ...), custom_call_target="tpu_custom_call" | custom-call | flops 1 | bytes 1 | tf_op jit(solution)/shard_map/output/pallas_call | solution.py:50
  59.7 0.7 %collective-permute-done.23.refs_2_ = bf16[96,768]{1,0:T(8,128)(2,1)S(1)} collective-permute-done((bf16[96,768]{1,0:T(8,128)(2,1)S(1)}, bf16[96,768]{1,0:T(8,128)(2,1)S(1)}, u32[]{:S(2)}, u32[]{:S(2)}) %collective-permute-start.23) | collective-permute-done | bytes 147488 | tf_op jit(solution)/shard_map/ppermute | solution.py:471
  60.5 2.4 %collective-permute-start.24 = (bf16[192,768]{1,0:T(8,128)(2,1)S(1)}, bf16[192,768]{1,0:T(8,128)(2,1)S(1)}, u32[]{:S(2)}, u32[]{:S(2)}) collective-permute-start(bf16[192,768]{1,0:T(8,128)(2,1)S(1)} %cross.1.value_ref), channel_id=1, source_target_pairs={{1,0},{0,1},{3,2},{2,3},{5,4},{4,5},{7,6},{6,7},{9,8},{8,9},{11,10... | collective-permute-start | bytes 884744 | tf_op jit(solution)/shard_map/ppermute | solution.py:345
  62.9 0.9 %write.2.refs_0_ = f32[384,768]{1,0:T(8,128)} custom-call(bf16[192,768]{1,0:T(8,128)(2,1)S(1)} %cross.1.value_ref), custom_call_target="tpu_custom_call" | custom-call | flops 1 | bytes 1 | tf_op jit(solution)/shard_map/write/pallas_call | solution.py:476
  63.8 0.3 collective-permute-done.24.value_ref
  64.1 0.9 %write.3 = f32[384,768]{1,0:T(8,128)} custom-call(bf16[192,768]{1,0:T(8,128)(2,1)S(1)} %collective-permute-done.24.value_ref, f32[384,768]{1,0:T(8,128)} %write.2.refs_0_), custom_call_target="tpu_custom_call", output_to_operand_aliasing={{}: (1, {})} | custom-call | flops 1 | bytes 1 | tf_op jit(solution)/shard_map/write/pallas_call | solution.py:476
  (33 shorter events, 0.2 us)
Async XLA Ops:
  0.6 10.2 %copy-start.4 = (bf16[1,1,128,768]{3,2,1,0:T(8,128)(2,1)S(1)}, bf16[1,1,128,768]{3,2,1,0:T(8,128)(2,1)}, u32[]{:S(2)}) copy-start(bf16[1,1,128,768]{3,2,1,0:T(8,128)(2,1)} %param.10) | copy-start | bytes 589828
  0.6 20.5 %copy-start.6 = (s32[16,6]{0,1:T(8,128)S(1)}, s32[16,6]{0,1:T(8,128)}, u32[]{:S(2)}) copy-start(s32[16,6]{0,1:T(8,128)} %param.12) | copy-start | bytes 1156
  0.7 20.6 %copy-start.5 = (s32[16]{0:T(128)S(1)}, s32[16]{0:T(128)}, u32[]{:S(2)}) copy-start(s32[16]{0:T(128)} %count_ref.1) | copy-start | bytes 196
  1.9 6.1 %collective-permute-start = (bf16[2,192,128]{2,1,0:T(8,128)(2,1)S(1)}, bf16[2,192,128]{2,1,0:T(8,128)(2,1)S(1)}, u32[]{:S(2)}, u32[]{:S(2)}) collective-permute-start(bf16[2,192,128]{2,1,0:T(8,128)(2,1)S(1)} %get-tuple-element.61), channel_id=1, source_target_pairs={{1,0},{0,1},{3,2},{2,3},{5,4},{4,5},{7,6},{6,7},{9,8},{8,9},{11,10... | collective-permute-start | bytes 294920 | tf_op jit(solution)/shard_map/ppermute | solution.py:345
  2.6 5.4 %collective-permute-start.1 = (bf16[2,192,128]{2,1,0:T(8,128)(2,1)S(1)}, bf16[2,192,128]{2,1,0:T(8,128)(2,1)S(1)}, u32[]{:S(2)}, u32[]{:S(2)}) collective-permute-start(bf16[2,192,128]{2,1,0:T(8,128)(2,1)S(1)} %get-tuple-element.62), channel_id=1, source_target_pairs={{2,0},{3,1},{0,2},{1,3},{6,4},{7,5},{4,6},{5,7},{10,8},{11,9},{8,1... | collective-permute-start | bytes 294920 | tf_op jit(solution)/shard_map/ppermute | solution.py:345
  2.6 6.6 %collective-permute-start.2 = (bf16[2,192,128]{2,1,0:T(8,128)(2,1)S(1)}, bf16[2,192,128]{2,1,0:T(8,128)(2,1)S(1)}, u32[]{:S(2)}, u32[]{:S(2)}) collective-permute-start(bf16[2,192,128]{2,1,0:T(8,128)(2,1)S(1)} %get-tuple-element.63), channel_id=1, source_target_pairs={{3,0},{2,1},{1,2},{0,3},{7,4},{6,5},{5,6},{4,7},{11,8},{10,9},{9,1... | collective-permute-start | bytes 294920 | tf_op jit(solution)/shard_map/ppermute | solution.py:345
  4.4 1.3 %copy-start = (bf16[768,768]{1,0:T(8,128)(2,1)S(1)}, bf16[768,768]{1,0:T(8,128)(2,1)}, u32[]{:S(2)}) copy-start(bf16[768,768]{1,0:T(8,128)(2,1)} %refs_4_.1) | copy-start | bytes 3538948
  5.6 0.9 %copy-start.2 = (bf16[1,1,128,768]{3,2,1,0:T(8,128)(2,1)S(1)}, bf16[1,1,128,768]{3,2,1,0:T(8,128)(2,1)}, u32[]{:S(2)}) copy-start(bf16[1,1,128,768]{3,2,1,0:T(8,128)(2,1)} %param.7) | copy-start | bytes 589828
  6.5 0.9 %copy-start.3 = (bf16[1,1,128,768]{3,2,1,0:T(8,128)(2,1)S(1)}, bf16[1,1,128,768]{3,2,1,0:T(8,128)(2,1)}, u32[]{:S(2)}) copy-start(bf16[1,1,128,768]{3,2,1,0:T(8,128)(2,1)} %param.10) | copy-start | bytes 589828
  9.4 14.6 %collective-permute-start.8 = (bf16[2,192,384]{2,1,0:T(8,128)(2,1)S(1)}, bf16[2,192,384]{2,1,0:T(8,128)(2,1)S(1)}, u32[]{:S(2)}, u32[]{:S(2)}) collective-permute-start(bf16[2,192,384]{2,1,0:T(8,128)(2,1)S(1)} %get-tuple-element.77), channel_id=1, source_target_pairs={{0,4},{1,5},{2,6},{3,7},{4,8},{5,9},{6,10},{7,11},{8,12},{9,13},{1... | collective-permute-start | bytes 884744 | tf_op jit(solution)/shard_map/ppermute | solution.py:351
  10.8 10.4 %collective-permute-start.11 = (bf16[128,768]{1,0:T(8,128)(2,1)S(1)}, bf16[128,768]{1,0:T(8,128)(2,1)S(1)}, u32[]{:S(2)}, u32[]{:S(2)}) collective-permute-start(bf16[128,768]{1,0:T(8,128)(2,1)S(1)} %bitcast.10), channel_id=1, source_target_pairs={{2,0},{3,1},{0,2},{1,3},{6,4},{7,5},{4,6},{5,7},{10,8},{11,9},{8,1... | collective-permute-start | bytes 589832 | tf_op jit(solution)/shard_map/ppermute | solution.py:345
  11.0 4.0 %collective-permute-start.3 = (bf16[2,192,128]{2,1,0:T(8,128)(2,1)S(1)}, bf16[2,192,128]{2,1,0:T(8,128)(2,1)S(1)}, u32[]{:S(2)}, u32[]{:S(2)}) collective-permute-start(bf16[2,192,128]{2,1,0:T(8,128)(2,1)S(1)} %get-tuple-element.71), channel_id=1, source_target_pairs={{1,0},{0,1},{3,2},{2,3},{5,4},{4,5},{7,6},{6,7},{9,8},{8,9},{11,10... | collective-permute-start | bytes 294920 | tf_op jit(solution)/shard_map/ppermute | solution.py:345
  11.8 14.8 %collective-permute-start.9 = (bf16[2,192,384]{2,1,0:T(8,128)(2,1)S(1)}, bf16[2,192,384]{2,1,0:T(8,128)(2,1)S(1)}, u32[]{:S(2)}, u32[]{:S(2)}) collective-permute-start(bf16[2,192,384]{2,1,0:T(8,128)(2,1)S(1)} %get-tuple-element.78), channel_id=1, source_target_pairs={{0,12},{1,13},{2,14},{3,15},{4,0},{5,1},{6,2},{7,3},{8,4},{9,5},{1... | collective-permute-start | bytes 884744 | tf_op jit(solution)/shard_map/ppermute | solution.py:352
  13.7 5.1 %collective-permute-start.4 = (bf16[2,192,128]{2,1,0:T(8,128)(2,1)S(1)}, bf16[2,192,128]{2,1,0:T(8,128)(2,1)S(1)}, u32[]{:S(2)}, u32[]{:S(2)}) collective-permute-start(bf16[2,192,128]{2,1,0:T(8,128)(2,1)S(1)} %get-tuple-element.72), channel_id=1, source_target_pairs={{2,0},{3,1},{0,2},{1,3},{6,4},{7,5},{4,6},{5,7},{10,8},{11,9},{8,1... | collective-permute-start | bytes 294920 | tf_op jit(solution)/shard_map/ppermute | solution.py:345
  15.0 7.5 %collective-permute-start.5 = (bf16[2,192,128]{2,1,0:T(8,128)(2,1)S(1)}, bf16[2,192,128]{2,1,0:T(8,128)(2,1)S(1)}, u32[]{:S(2)}, u32[]{:S(2)}) collective-permute-start(bf16[2,192,128]{2,1,0:T(8,128)(2,1)S(1)} %get-tuple-element.73), channel_id=1, source_target_pairs={{3,0},{2,1},{1,2},{0,3},{7,4},{6,5},{5,6},{4,7},{11,8},{10,9},{9,1... | collective-permute-start | bytes 294920 | tf_op jit(solution)/shard_map/ppermute | solution.py:345
  18.8 11.0 %collective-permute-start.10 = (bf16[128,768]{1,0:T(8,128)(2,1)S(1)}, bf16[128,768]{1,0:T(8,128)(2,1)S(1)}, u32[]{:S(2)}, u32[]{:S(2)}) collective-permute-start(bf16[128,768]{1,0:T(8,128)(2,1)S(1)} %bitcast.11), channel_id=1, source_target_pairs={{1,0},{0,1},{3,2},{2,3},{5,4},{4,5},{7,6},{6,7},{9,8},{8,9},{11,10... | collective-permute-start | bytes 589832 | tf_op jit(solution)/shard_map/ppermute | solution.py:345
  21.2 8.7 %collective-permute-start.12 = (bf16[128,768]{1,0:T(8,128)(2,1)S(1)}, bf16[128,768]{1,0:T(8,128)(2,1)S(1)}, u32[]{:S(2)}, u32[]{:S(2)}) collective-permute-start(bf16[128,768]{1,0:T(8,128)(2,1)S(1)} %collective-permute-done.11.refs_2_), channel_id=1, source_target_pairs={{1,0},{0,1},{3,2},{2,3},{5,4},{4,5},{7,6},{6,7},{9,8},{8,9},{11,10... | collective-permute-start | bytes 589832 | tf_op jit(solution)/shard_map/ppermute | solution.py:345
  22.7 14.8 %collective-permute-start.6 = (bf16[2,192,384]{2,1,0:T(8,128)(2,1)S(1)}, bf16[2,192,384]{2,1,0:T(8,128)(2,1)S(1)}, u32[]{:S(2)}, u32[]{:S(2)}) collective-permute-start(bf16[2,192,384]{2,1,0:T(8,128)(2,1)S(1)} %get-tuple-element.75), channel_id=1, source_target_pairs={{0,4},{1,5},{2,6},{3,7},{4,8},{5,9},{6,10},{7,11},{8,12},{9,13},{1... | collective-permute-start | bytes 884744 | tf_op jit(solution)/shard_map/ppermute | solution.py:351
  24.0 15.8 %collective-permute-start.7 = (bf16[2,192,384]{2,1,0:T(8,128)(2,1)S(1)}, bf16[2,192,384]{2,1,0:T(8,128)(2,1)S(1)}, u32[]{:S(2)}, u32[]{:S(2)}) collective-permute-start(bf16[2,192,384]{2,1,0:T(8,128)(2,1)S(1)} %get-tuple-element.76), channel_id=1, source_target_pairs={{0,12},{1,13},{2,14},{3,15},{4,0},{5,1},{6,2},{7,3},{8,4},{9,5},{1... | collective-permute-start | bytes 884744 | tf_op jit(solution)/shard_map/ppermute | solution.py:352
  30.3 7.1 %collective-permute-start.18 = (bf16[96,768]{1,0:T(8,128)(2,1)S(1)}, bf16[96,768]{1,0:T(8,128)(2,1)S(1)}, u32[]{:S(2)}, u32[]{:S(2)}) collective-permute-start(bf16[96,768]{1,0:T(8,128)(2,1)S(1)} %get-tuple-element.88.refs_4_), channel_id=1, source_target_pairs={{0,16},{16,0},{1,17},{17,1},{2,18},{18,2},{3,19},{19,3},{4,20},{20... | collective-permute-start | bytes 442376 | tf_op jit(solution)/shard_map/ppermute | solution.py:356
  34.1 5.8 %collective-permute-start.13 = (f32[16,384]{1,0:T(8,128)S(1)}, f32[16,384]{1,0:T(8,128)S(1)}, u32[]{:S(2)}, u32[]{:S(2)}) collective-permute-start(f32[16,384]{1,0:T(8,128)S(1)} %get-tuple-element.90), channel_id=1, source_target_pairs={{0,4},{1,5},{2,6},{3,7},{4,8},{5,9},{6,10},{7,11},{8,12},{9,13},{1... | collective-permute-start | bytes 73736 | tf_op jit(solution)/shard_map/ppermute | solution.py:351
  34.4 5.5 %collective-permute-start.14 = (f32[16,384]{1,0:T(8,128)S(1)}, f32[16,384]{1,0:T(8,128)S(1)}, u32[]{:S(2)}, u32[]{:S(2)}) collective-permute-start(f32[16,384]{1,0:T(8,128)S(1)} %get-tuple-element.91), channel_id=1, source_target_pairs={{0,12},{1,13},{2,14},{3,15},{4,0},{5,1},{6,2},{7,3},{8,4},{9,5},{1... | collective-permute-start | bytes 73736 | tf_op jit(solution)/shard_map/ppermute | solution.py:352
  37.4 8.0 %collective-permute-start.19 = (bf16[48,768]{1,0:T(8,128)(2,1)S(1)}, bf16[48,768]{1,0:T(8,128)(2,1)S(1)}, u32[]{:S(2)}, u32[]{:S(2)}) collective-permute-start(bf16[48,768]{1,0:T(8,128)(2,1)S(1)} %get-tuple-element.105.refs_0_), channel_id=1, source_target_pairs={{8,0},{9,1},{10,2},{11,3},{12,4},{13,5},{14,6},{15,7},{0,8},{1,9},... | collective-permute-start | bytes 221192 | tf_op jit(solution)/shard_map/ppermute | solution.py:345
  37.5 8.4 %collective-permute-start.20 = (bf16[48,768]{1,0:T(8,128)(2,1)S(1)}, bf16[48,768]{1,0:T(8,128)(2,1)S(1)}, u32[]{:S(2)}, u32[]{:S(2)}) collective-permute-start(bf16[48,768]{1,0:T(8,128)(2,1)S(1)} %get-tuple-element.106.refs_1_), channel_id=1, source_target_pairs={{8,0},{9,1},{10,2},{11,3},{12,4},{13,5},{14,6},{15,7},{0,8},{1,9},... | collective-permute-start | bytes 221192 | tf_op jit(solution)/shard_map/ppermute | solution.py:345
  39.9 18.7 %copy-start.1 = (bf16[768,768]{1,0:T(8,128)(2,1)S(1)}, bf16[768,768]{1,0:T(8,128)(2,1)}, u32[]{:S(2)}) copy-start(bf16[768,768]{1,0:T(8,128)(2,1)} %refs_4_.1) | copy-start | bytes 3538948
  41.7 7.7 %collective-permute-start.15 = (bf16[4,192,128]{2,1,0:T(8,128)(2,1)S(1)}, bf16[4,192,128]{2,1,0:T(8,128)(2,1)S(1)}, u32[]{:S(2)}, u32[]{:S(2)}) collective-permute-start(bf16[4,192,128]{2,1,0:T(8,128)(2,1)S(1)} %get-tuple-element.96), channel_id=1, source_target_pairs={{1,0},{0,1},{3,2},{2,3},{5,4},{4,5},{7,6},{6,7},{9,8},{8,9},{11,10... | collective-permute-start | bytes 589832 | tf_op jit(solution)/shard_map/ppermute | solution.py:345
  45.9 4.1 %collective-permute-start.21 = (bf16[96,768]{1,0:T(8,128)(2,1)S(1)}, bf16[96,768]{1,0:T(8,128)(2,1)S(1)}, u32[]{:S(2)}, u32[]{:S(2)}) collective-permute-start(bf16[96,768]{1,0:T(8,128)(2,1)S(1)} %meet.1.refs_0_), channel_id=1, source_target_pairs={{4,0},{5,1},{6,2},{7,3},{0,4},{1,5},{2,6},{3,7},{12,8},{13,9},{14,... | collective-permute-start | bytes 442376 | tf_op jit(solution)/shard_map/ppermute | solution.py:345
  46.1 8.8 %collective-permute-start.16 = (bf16[4,192,128]{2,1,0:T(8,128)(2,1)S(1)}, bf16[4,192,128]{2,1,0:T(8,128)(2,1)S(1)}, u32[]{:S(2)}, u32[]{:S(2)}) collective-permute-start(bf16[4,192,128]{2,1,0:T(8,128)(2,1)S(1)} %get-tuple-element.97), channel_id=1, source_target_pairs={{2,0},{3,1},{0,2},{1,3},{6,4},{7,5},{4,6},{5,7},{10,8},{11,9},{8,1... | collective-permute-start | bytes 589832 | tf_op jit(solution)/shard_map/ppermute | solution.py:345
  46.1 12.4 %collective-permute-start.17 = (bf16[4,192,128]{2,1,0:T(8,128)(2,1)S(1)}, bf16[4,192,128]{2,1,0:T(8,128)(2,1)S(1)}, u32[]{:S(2)}, u32[]{:S(2)}) collective-permute-start(bf16[4,192,128]{2,1,0:T(8,128)(2,1)S(1)} %get-tuple-element.98), channel_id=1, source_target_pairs={{3,0},{2,1},{1,2},{0,3},{7,4},{6,5},{5,6},{4,7},{11,8},{10,9},{9,1... | collective-permute-start | bytes 589832 | tf_op jit(solution)/shard_map/ppermute | solution.py:345
  50.0 9.7 %collective-permute-start.22 = (bf16[96,768]{1,0:T(8,128)(2,1)S(1)}, bf16[96,768]{1,0:T(8,128)(2,1)S(1)}, u32[]{:S(2)}, u32[]{:S(2)}) collective-permute-start(bf16[96,768]{1,0:T(8,128)(2,1)S(1)} %add.1.refs_0_), channel_id=1, source_target_pairs={{0,2},{1,3},{2,18},{3,19},{4,6},{5,7},{6,22},{7,23},{8,10},{9,11},... | collective-permute-start | bytes 442376 | tf_op jit(solution)/shard_map/ppermute | solution.py:471
  53.0 7.5 %collective-permute-start.23 = (bf16[96,768]{1,0:T(8,128)(2,1)S(1)}, bf16[96,768]{1,0:T(8,128)(2,1)S(1)}, u32[]{:S(2)}, u32[]{:S(2)}) collective-permute-start(bf16[96,768]{1,0:T(8,128)(2,1)S(1)} %add.1.refs_0_), channel_id=1, source_target_pairs={{2,16},{3,17},{6,20},{7,21},{10,24},{11,25},{14,28},{15,29},{16,2}... | collective-permute-start | bytes 442376 | tf_op jit(solution)/shard_map/ppermute | solution.py:471
  60.5 3.6 %collective-permute-start.24 = (bf16[192,768]{1,0:T(8,128)(2,1)S(1)}, bf16[192,768]{1,0:T(8,128)(2,1)S(1)}, u32[]{:S(2)}, u32[]{:S(2)}) collective-permute-start(bf16[192,768]{1,0:T(8,128)(2,1)S(1)} %cross.1.value_ref), channel_id=1, source_target_pairs={{1,0},{0,1},{3,2},{2,3},{5,4},{4,5},{7,6},{6,7},{9,8},{8,9},{11,10... | collective-permute-start | bytes 884744 | tf_op jit(solution)/shard_map/ppermute | solution.py:345

commit v21 on v20

--- a/solution.py
+++ b/solution.py
@@ -469,7 +469,7 @@
         (total,) = call(
             cross_kernel, [VMEM] * 3, [shape_of(2 * count, width)],
             (total, lax.ppermute(total, axes, first), lax.ppermute(total, axes, second)),
-            name="cross", after=(output_token,),
+            name="cross", after=parts[1:],
         )
         grad_weight = ()
         for own, value in ((True, total), (False, swap(total, 1))):

time: 65.2 us -> 66.1 us (1.014)
  waiting for transfers between devices: 10.9 us -> 11.8 us
    ppermute x1, waiting for transfers between devices: 0.75 us -> 1.91 us  [local(): lax.ppermute(total, axes, second)]
  transfers between devices with their start and end apart: 25 -> 25, of which waited for: 8 -> 7; matrix products, arithmetic and copies ran while one was open for 0% -> 0% of each run, Pallas kernels for 18% -> 18%
where the time goes in v21:
time: 66.1 us; the launch traced here: 65.9 us
  starting transfers between devices  35.8 us (54%)
  Pallas kernels  14.3 us (22%)
  waiting for transfers between devices  11.8 us (18%)
  local copies, waits for them, and re-layouts  3.23 us (5%)
  between operations  0.85 us (1%)
    ppermute x16, starting transfers between devices, swap(): lax.ppermute(value, 'station', [(s ^ stride, s) for s in range(stations)])  19.7 us
    pallas_call x14, Pallas kernels, call(): pl.pallas_call(kernel, in_specs=ins, out_specs=[VMEM] * len(outs), out_sh...  12.5 us
    ppermute x16, waiting for transfers between devices, swap(): lax.ppermute(value, 'station', [(s ^ stride, s) for s in range(stations)])  9.16 us
    ppermute x3, starting transfers between devices, along(): lax.ppermute(down, 'station', [(s, (s - LAYER) % stations) for s in range...  6.84 us
    unnamed x15, local copies, waits for them, and re-layouts  3.23 us
    ppermute x3, starting transfers between devices, along(): lax.ppermute(up, 'station', [(s, (s + LAYER) % stations) for s in range(s...  3.03 us
    ppermute x1, starting transfers between devices, local(): lax.ppermute(total, axes, first)  2.95 us
    ppermute x1, waiting for transfers between devices, local(): lax.ppermute(total, axes, second)  1.91 us
  transfers between devices with their start and end apart: 25, of which 7 were waited for; matrix products, arithmetic and copies ran while one was open for 0% of the time, Pallas kernels for 18%

profile of v21, /device:TPU:3, one launch (start us, length us, event | category | flops | bytes accessed | tf_op | source)
XLA Modules:
  0.0 65.9 jit_solution(10124151374864140458)
XLA Ops:
  0.6 0.0 copy-start.4
  0.7 1.2 %pack.1 = (bf16[2,192,128]{2,1,0:T(8,128)(2,1)S(1)}, bf16[2,192,128]{2,1,0:T(8,128)(2,1)S(1)}, bf16[2,192,128]{2,1,0:T(8,128)(2,1)S(1)}, bf16[2,192,128]{2,1,0:T(8,128)(2,1)S(1)}) custom-call(bf16[128,768]{1,0:T(8,128)(2,1)} %bitcast.12, bf16[128,768]{1,0:T(8,128)(2,1)} %bitcast.13), custom_call_target="tpu_custom_call" | custom-call | flops 1 | bytes 1 | tf_op jit(solution)/shard_map/pack/pallas_call | solution.py:50
  1.9 0.7 %collective-permute-start = (bf16[2,192,128]{2,1,0:T(8,128)(2,1)S(1)}, bf16[2,192,128]{2,1,0:T(8,128)(2,1)S(1)}, u32[]{:S(2)}, u32[]{:S(2)}) collective-permute-start(bf16[2,192,128]{2,1,0:T(8,128)(2,1)S(1)} %get-tuple-element.60), channel_id=1, source_target_pairs={{1,0},{0,1},{3,2},{2,3},{5,4},{4,5},{7,6},{6,7},{9,8},{8,9},{11,10... | collective-permute-start | bytes 294920 | tf_op jit(solution)/shard_map/ppermute | solution.py:345
  2.6 1.7 %collective-permute-start.2 = (bf16[2,192,128]{2,1,0:T(8,128)(2,1)S(1)}, bf16[2,192,128]{2,1,0:T(8,128)(2,1)S(1)}, u32[]{:S(2)}, u32[]{:S(2)}) collective-permute-start(bf16[2,192,128]{2,1,0:T(8,128)(2,1)S(1)} %get-tuple-element.62), channel_id=1, source_target_pairs={{3,0},{2,1},{1,2},{0,3},{7,4},{6,5},{5,6},{4,7},{11,8},{10,9},{9,1... | collective-permute-start | bytes 294920 | tf_op jit(solution)/shard_map/ppermute | solution.py:345
  4.4 1.3 %copy-done = bf16[768,768]{1,0:T(8,128)(2,1)S(1)} copy-done((bf16[768,768]{1,0:T(8,128)(2,1)S(1)}, bf16[768,768]{1,0:T(8,128)(2,1)}, u32[]{:S(2)}) %copy-start) | copy-done | bytes 1179672
  5.6 0.9 %copy-done.2 = bf16[1,1,128,768]{3,2,1,0:T(8,128)(2,1)S(1)} copy-done((bf16[1,1,128,768]{3,2,1,0:T(8,128)(2,1)S(1)}, bf16[1,1,128,768]{3,2,1,0:T(8,128)(2,1)}, u32[]{:S(2)}) %copy-start.2) | copy-done | bytes 196632
  6.6 0.9 %copy-done.3 = bf16[1,1,128,768]{3,2,1,0:T(8,128)(2,1)S(1)} copy-done((bf16[1,1,128,768]{3,2,1,0:T(8,128)(2,1)S(1)}, bf16[1,1,128,768]{3,2,1,0:T(8,128)(2,1)}, u32[]{:S(2)}) %copy-start.3) | copy-done | bytes 196632
  7.5 0.5 project.1
  8.0 1.3 %collective-permute-done.2.refs_3_ = bf16[2,192,128]{2,1,0:T(8,128)(2,1)S(1)} collective-permute-done((bf16[2,192,128]{2,1,0:T(8,128)(2,1)S(1)}, bf16[2,192,128]{2,1,0:T(8,128)(2,1)S(1)}, u32[]{:S(2)}, u32[]{:S(2)}) %collective-permute-start.2) | collective-permute-done | bytes 98336 | tf_op jit(solution)/shard_map/ppermute | solution.py:345
  9.3 0.1 gather.2
  9.4 1.3 %collective-permute-start.8 = (bf16[2,192,384]{2,1,0:T(8,128)(2,1)S(1)}, bf16[2,192,384]{2,1,0:T(8,128)(2,1)S(1)}, u32[]{:S(2)}, u32[]{:S(2)}) collective-permute-start(bf16[2,192,384]{2,1,0:T(8,128)(2,1)S(1)} %get-tuple-element.76), channel_id=1, source_target_pairs={{0,4},{1,5},{2,6},{3,7},{4,8},{5,9},{6,10},{7,11},{8,12},{9,13},{1... | collective-permute-start | bytes 884744 | tf_op jit(solution)/shard_map/ppermute | solution.py:351
  10.8 0.3 collective-permute-start.11
  11.0 0.8 %collective-permute-start.3 = (bf16[2,192,128]{2,1,0:T(8,128)(2,1)S(1)}, bf16[2,192,128]{2,1,0:T(8,128)(2,1)S(1)}, u32[]{:S(2)}, u32[]{:S(2)}) collective-permute-start(bf16[2,192,128]{2,1,0:T(8,128)(2,1)S(1)} %get-tuple-element.70), channel_id=1, source_target_pairs={{1,0},{0,1},{3,2},{2,3},{5,4},{4,5},{7,6},{6,7},{9,8},{8,9},{11,10... | collective-permute-start | bytes 294920 | tf_op jit(solution)/shard_map/ppermute | solution.py:345
  11.8 1.9 %collective-permute-start.9 = (bf16[2,192,384]{2,1,0:T(8,128)(2,1)S(1)}, bf16[2,192,384]{2,1,0:T(8,128)(2,1)S(1)}, u32[]{:S(2)}, u32[]{:S(2)}) collective-permute-start(bf16[2,192,384]{2,1,0:T(8,128)(2,1)S(1)} %get-tuple-element.77), channel_id=1, source_target_pairs={{0,12},{1,13},{2,14},{3,15},{4,0},{5,1},{6,2},{7,3},{8,4},{9,5},{1... | collective-permute-start | bytes 884744 | tf_op jit(solution)/shard_map/ppermute | solution.py:352
  13.7 1.3 %collective-permute-start.4 = (bf16[2,192,128]{2,1,0:T(8,128)(2,1)S(1)}, bf16[2,192,128]{2,1,0:T(8,128)(2,1)S(1)}, u32[]{:S(2)}, u32[]{:S(2)}) collective-permute-start(bf16[2,192,128]{2,1,0:T(8,128)(2,1)S(1)} %get-tuple-element.71), channel_id=1, source_target_pairs={{2,0},{3,1},{0,2},{1,3},{6,4},{7,5},{4,6},{5,7},{10,8},{11,9},{8,1... | collective-permute-start | bytes 294920 | tf_op jit(solution)/shard_map/ppermute | solution.py:345
  15.0 0.6 collective-permute-start.5
  15.6 3.2 %collective-permute-done.4.refs_2_ = bf16[2,192,128]{2,1,0:T(8,128)(2,1)S(1)} collective-permute-done((bf16[2,192,128]{2,1,0:T(8,128)(2,1)S(1)}, bf16[2,192,128]{2,1,0:T(8,128)(2,1)S(1)}, u32[]{:S(2)}, u32[]{:S(2)}) %collective-permute-start.4) | collective-permute-done | bytes 98336 | tf_op jit(solution)/shard_map/ppermute | solution.py:345
  18.8 2.3 %collective-permute-start.10 = (bf16[128,768]{1,0:T(8,128)(2,1)S(1)}, bf16[128,768]{1,0:T(8,128)(2,1)S(1)}, u32[]{:S(2)}, u32[]{:S(2)}) collective-permute-start(bf16[128,768]{1,0:T(8,128)(2,1)S(1)} %bitcast.11), channel_id=1, source_target_pairs={{1,0},{0,1},{3,2},{2,3},{5,4},{4,5},{7,6},{6,7},{9,8},{8,9},{11,10... | collective-permute-start | bytes 589832 | tf_op jit(solution)/shard_map/ppermute | solution.py:345
  21.2 0.0 collective-permute-start.12
  21.2 0.1 copy.13.ids_ref
  21.3 1.2 %live.1 = (f32[16,512]{1,0:T(8,128)S(1)}, f32[8,384]{1,0:T(8,128)S(1)}) custom-call(s32[16,6]{1,0:T(8,128)S(1)} %copy.13.ids_ref, s32[16]{0:T(128)S(1)} %copy-done.5), custom_call_target="tpu_custom_call" | custom-call | flops 1 | bytes 1 | tf_op jit(solution)/shard_map/live/pallas_call | solution.py:50
  22.5 0.1 gather.3
  22.7 1.3 %collective-permute-start.6 = (bf16[2,192,384]{2,1,0:T(8,128)(2,1)S(1)}, bf16[2,192,384]{2,1,0:T(8,128)(2,1)S(1)}, u32[]{:S(2)}, u32[]{:S(2)}) collective-permute-start(bf16[2,192,384]{2,1,0:T(8,128)(2,1)S(1)} %get-tuple-element.74), channel_id=1, source_target_pairs={{0,4},{1,5},{2,6},{3,7},{4,8},{5,9},{6,10},{7,11},{8,12},{9,13},{1... | collective-permute-start | bytes 884744 | tf_op jit(solution)/shard_map/ppermute | solution.py:351
  24.0 2.0 %collective-permute-start.7 = (bf16[2,192,384]{2,1,0:T(8,128)(2,1)S(1)}, bf16[2,192,384]{2,1,0:T(8,128)(2,1)S(1)}, u32[]{:S(2)}, u32[]{:S(2)}) collective-permute-start(bf16[2,192,384]{2,1,0:T(8,128)(2,1)S(1)} %get-tuple-element.75), channel_id=1, source_target_pairs={{0,12},{1,13},{2,14},{3,15},{4,0},{5,1},{6,2},{7,3},{8,4},{9,5},{1... | collective-permute-start | bytes 884744 | tf_op jit(solution)/shard_map/ppermute | solution.py:352
  26.0 0.7 %collective-permute-done.9.high_ref = bf16[2,192,384]{2,1,0:T(8,128)(2,1)S(1)} collective-permute-done((bf16[2,192,384]{2,1,0:T(8,128)(2,1)S(1)}, bf16[2,192,384]{2,1,0:T(8,128)(2,1)S(1)}, u32[]{:S(2)}, u32[]{:S(2)}) %collective-permute-start.9) | collective-permute-done | bytes 294944 | tf_op jit(solution)/shard_map/ppermute | solution.py:352
  26.6 3.2 %forward.1 = (bf16[192,512]{1,0:T(8,128)(2,1)S(1)}, f32[8,512]{1,0:T(8,128)S(1)}, f32[16,384]{1,0:T(8,128)S(1)}, f32[16,384]{1,0:T(8,128)S(1)}, bf16[3,1280,512]...) custom-call(bf16[2,192,512]{2,1,0:T(8,128)(2,1)S(1)} %get-tuple-element.63.pair_ref, ...), custom_call_target="tpu_custom_call" | custom-call | flops 1 | bytes 1 | tf_op jit(solution)/shard_map/forward/pallas_call | solution.py:50
  29.9 0.5 weight.1
  30.3 1.3 %collective-permute-start.18 = (bf16[96,768]{1,0:T(8,128)(2,1)S(1)}, bf16[96,768]{1,0:T(8,128)(2,1)S(1)}, u32[]{:S(2)}, u32[]{:S(2)}) collective-permute-start(bf16[96,768]{1,0:T(8,128)(2,1)S(1)} %get-tuple-element.87.refs_4_), channel_id=1, source_target_pairs={{0,16},{16,0},{1,17},{17,1},{2,18},{18,2},{3,19},{19,3},{4,20},{20... | collective-permute-start | bytes 442376 | tf_op jit(solution)/shard_map/ppermute | solution.py:356
  31.6 2.4 %query_grad.1 = (bf16[192,512]{1,0:T(8,128)(2,1)S(1)}, f32[2,192,512]{2,1,0:T(8,128)S(1)}, f32[8,128]{1,0:T(8,128)S(1)}) custom-call(bf16[2,192,1280]{2,1,0:T(8,128)(2,1)S(1)} %get-tuple-element.81.refs_0_, bf16[3,1280,512]{2,1,0:T(8,128)(2,1)S(1)} %get-tuple-element.82.refs_1_, bf16[2,192,512]{2,1,0:T(8,128)(2,1)S(1)} %get-tuple-element.78.query_ref.refs_2_, ...), custom_call_target="tpu_custom_call" | custom-call | flops 1 | bytes 1 | tf_op jit(solution)/shard_map/query_grad/pallas_call | solution.py:50
  34.1 0.3 collective-permute-start.13
  34.4 3.0 %collective-permute-start.14 = (f32[16,384]{1,0:T(8,128)S(1)}, f32[16,384]{1,0:T(8,128)S(1)}, u32[]{:S(2)}, u32[]{:S(2)}) collective-permute-start(f32[16,384]{1,0:T(8,128)S(1)} %get-tuple-element.90), channel_id=1, source_target_pairs={{0,12},{1,13},{2,14},{3,15},{4,0},{5,1},{6,2},{7,3},{8,4},{9,5},{1... | collective-permute-start | bytes 73736 | tf_op jit(solution)/shard_map/ppermute | solution.py:352
  37.4 0.1 collective-permute-start.19
  37.5 2.3 %collective-permute-start.20 = (bf16[48,768]{1,0:T(8,128)(2,1)S(1)}, bf16[48,768]{1,0:T(8,128)(2,1)S(1)}, u32[]{:S(2)}, u32[]{:S(2)}) collective-permute-start(bf16[48,768]{1,0:T(8,128)(2,1)S(1)} %get-tuple-element.105.refs_1_), channel_id=1, source_target_pairs={{8,0},{9,1},{10,2},{11,3},{12,4},{13,5},{14,6},{15,7},{0,8},{1,9},... | collective-permute-start | bytes 221192 | tf_op jit(solution)/shard_map/ppermute | solution.py:345
  39.9 1.9 %key_grad.1 = (bf16[4,192,128]{2,1,0:T(8,128)(2,1)S(1)}, bf16[4,192,128]{2,1,0:T(8,128)(2,1)S(1)}, bf16[4,192,128]{2,1,0:T(8,128)(2,1)S(1)}, bf16[4,192,128]{2,1,0:T(8,128)(2,1)S(1)}, f32[8,128]{1,0:T(8,128)S(1)}) custom-call(bf16[2,192,512]{2,1,0:T(8,128)(2,1)S(1)} %get-tuple-element.63.pair_ref, bf16[2,192,384]{2,1,0:T(8,128)(2,1)S(1)} %collective-permute-done.6.low_ref, ...), custom_call_target="tpu_custom_call" | custom-call | flops 1 | bytes 1 | tf_op jit(solution)/shard_map/key_grad/pallas_call | solution.py:50
  41.7 0.0 copy-start.1
  41.7 3.6 %collective-permute-start.15 = (bf16[4,192,128]{2,1,0:T(8,128)(2,1)S(1)}, bf16[4,192,128]{2,1,0:T(8,128)(2,1)S(1)}, u32[]{:S(2)}, u32[]{:S(2)}) collective-permute-start(bf16[4,192,128]{2,1,0:T(8,128)(2,1)S(1)} %get-tuple-element.95), channel_id=1, source_target_pairs={{1,0},{0,1},{3,2},{2,3},{5,4},{4,5},{7,6},{6,7},{9,8},{8,9},{11,10... | collective-permute-start | bytes 589832 | tf_op jit(solution)/shard_map/ppermute | solution.py:345
  45.4 0.5 collective-permute-done.20.refs_3_
  45.9 0.2 collective-permute-start.21
  46.1 3.3 %collective-permute-start.17 = (bf16[4,192,128]{2,1,0:T(8,128)(2,1)S(1)}, bf16[4,192,128]{2,1,0:T(8,128)(2,1)S(1)}, u32[]{:S(2)}, u32[]{:S(2)}) collective-permute-start(bf16[4,192,128]{2,1,0:T(8,128)(2,1)S(1)} %get-tuple-element.97), channel_id=1, source_target_pairs={{3,0},{2,1},{1,2},{0,3},{7,4},{6,5},{5,6},{4,7},{11,8},{10,9},{9,1... | collective-permute-start | bytes 589832 | tf_op jit(solution)/shard_map/ppermute | solution.py:345
  49.5 0.5 collective-permute-done.21.refs_1_
  50.0 3.0 %collective-permute-start.22 = (bf16[96,768]{1,0:T(8,128)(2,1)S(1)}, bf16[96,768]{1,0:T(8,128)(2,1)S(1)}, u32[]{:S(2)}, u32[]{:S(2)}) collective-permute-start(bf16[96,768]{1,0:T(8,128)(2,1)S(1)} %add.1.refs_0_), channel_id=1, source_target_pairs={{0,2},{1,3},{2,18},{3,19},{4,6},{5,7},{6,22},{7,23},{8,10},{9,11},... | collective-permute-start | bytes 442376 | tf_op jit(solution)/shard_map/ppermute | solution.py:471
  53.0 1.9 %collective-permute-start.23 = (bf16[96,768]{1,0:T(8,128)(2,1)S(1)}, bf16[96,768]{1,0:T(8,128)(2,1)S(1)}, u32[]{:S(2)}, u32[]{:S(2)}) collective-permute-start(bf16[96,768]{1,0:T(8,128)(2,1)S(1)} %add.1.refs_0_), channel_id=1, source_target_pairs={{2,16},{3,17},{6,20},{7,21},{10,24},{11,25},{14,28},{15,29},{16,2}... | collective-permute-start | bytes 442376 | tf_op jit(solution)/shard_map/ppermute | solution.py:471
  54.9 3.6 %collective-permute-done.17.refs_3_.refs_4_ = bf16[4,192,128]{2,1,0:T(8,128)(2,1)S(1)} collective-permute-done((bf16[4,192,128]{2,1,0:T(8,128)(2,1)S(1)}, bf16[4,192,128]{2,1,0:T(8,128)(2,1)S(1)}, u32[]{:S(2)}, u32[]{:S(2)}) %collective-permute-start.17) | collective-permute-done | bytes 196640 | tf_op jit(solution)/shard_map/ppermute | solution.py:345
  58.5 1.9 %collective-permute-done.23.refs_2_ = bf16[96,768]{1,0:T(8,128)(2,1)S(1)} collective-permute-done((bf16[96,768]{1,0:T(8,128)(2,1)S(1)}, bf16[96,768]{1,0:T(8,128)(2,1)S(1)}, u32[]{:S(2)}, u32[]{:S(2)}) %collective-permute-start.23) | collective-permute-done | bytes 147488 | tf_op jit(solution)/shard_map/ppermute | solution.py:471
  60.5 2.4 %collective-permute-start.24 = (bf16[192,768]{1,0:T(8,128)(2,1)S(1)}, bf16[192,768]{1,0:T(8,128)(2,1)S(1)}, u32[]{:S(2)}, u32[]{:S(2)}) collective-permute-start(bf16[192,768]{1,0:T(8,128)(2,1)S(1)} %cross.1.value_ref), channel_id=1, source_target_pairs={{1,0},{0,1},{3,2},{2,3},{5,4},{4,5},{7,6},{6,7},{9,8},{8,9},{11,10... | collective-permute-start | bytes 884744 | tf_op jit(solution)/shard_map/ppermute | solution.py:345
  62.9 1.2 %output.1 = (bf16[128,768]{1,0:T(8,128)(2,1)}, bf16[128,768]{1,0:T(8,128)(2,1)}, bf16[128,768]{1,0:T(8,128)(2,1)}, bf16[128,768]{1,0:T(8,128)(2,1)}, f32[8,128]{1,0:T(8,128)}) custom-call(bf16[4,192,128]{2,1,0:T(8,128)(2,1)S(1)} %get-tuple-element.94.refs_0_, bf16[4,192,128]{2,1,0:T(8,128)(2,1)S(1)} %collective-permute-done.15.refs_1_.refs_2_, ...), custom_call_target="tpu_custom_call" | custom-call | flops 1 | bytes 1 | tf_op jit(solution)/shard_map/output/pallas_call | solution.py:50
  64.1 0.9 %write.2.refs_0_ = f32[384,768]{1,0:T(8,128)} custom-call(bf16[192,768]{1,0:T(8,128)(2,1)S(1)} %cross.1.value_ref), custom_call_target="tpu_custom_call" | custom-call | flops 1 | bytes 1 | tf_op jit(solution)/shard_map/write/pallas_call | solution.py:476
  65.0 0.9 %write.3 = f32[384,768]{1,0:T(8,128)} custom-call(bf16[192,768]{1,0:T(8,128)(2,1)S(1)} %collective-permute-done.24.value_ref, f32[384,768]{1,0:T(8,128)} %write.2.refs_0_), custom_call_target="tpu_custom_call", output_to_operand_aliasing={{}: (1, {})} | custom-call | flops 1 | bytes 1 | tf_op jit(solution)/shard_map/write/pallas_call | solution.py:476
  (33 shorter events, 0.2 us)
Async XLA Ops:
  0.6 10.2 %copy-start.4 = (bf16[1,1,128,768]{3,2,1,0:T(8,128)(2,1)S(1)}, bf16[1,1,128,768]{3,2,1,0:T(8,128)(2,1)}, u32[]{:S(2)}) copy-start(bf16[1,1,128,768]{3,2,1,0:T(8,128)(2,1)} %param.10) | copy-start | bytes 589828
  0.6 20.5 %copy-start.6 = (s32[16,6]{0,1:T(8,128)S(1)}, s32[16,6]{0,1:T(8,128)}, u32[]{:S(2)}) copy-start(s32[16,6]{0,1:T(8,128)} %param.12) | copy-start | bytes 1156
  0.7 20.6 %copy-start.5 = (s32[16]{0:T(128)S(1)}, s32[16]{0:T(128)}, u32[]{:S(2)}) copy-start(s32[16]{0:T(128)} %count_ref.1) | copy-start | bytes 196
  1.9 6.1 %collective-permute-start = (bf16[2,192,128]{2,1,0:T(8,128)(2,1)S(1)}, bf16[2,192,128]{2,1,0:T(8,128)(2,1)S(1)}, u32[]{:S(2)}, u32[]{:S(2)}) collective-permute-start(bf16[2,192,128]{2,1,0:T(8,128)(2,1)S(1)} %get-tuple-element.60), channel_id=1, source_target_pairs={{1,0},{0,1},{3,2},{2,3},{5,4},{4,5},{7,6},{6,7},{9,8},{8,9},{11,10... | collective-permute-start | bytes 294920 | tf_op jit(solution)/shard_map/ppermute | solution.py:345
  2.6 5.4 %collective-permute-start.1 = (bf16[2,192,128]{2,1,0:T(8,128)(2,1)S(1)}, bf16[2,192,128]{2,1,0:T(8,128)(2,1)S(1)}, u32[]{:S(2)}, u32[]{:S(2)}) collective-permute-start(bf16[2,192,128]{2,1,0:T(8,128)(2,1)S(1)} %get-tuple-element.61), channel_id=1, source_target_pairs={{2,0},{3,1},{0,2},{1,3},{6,4},{7,5},{4,6},{5,7},{10,8},{11,9},{8,1... | collective-permute-start | bytes 294920 | tf_op jit(solution)/shard_map/ppermute | solution.py:345
  2.6 6.6 %collective-permute-start.2 = (bf16[2,192,128]{2,1,0:T(8,128)(2,1)S(1)}, bf16[2,192,128]{2,1,0:T(8,128)(2,1)S(1)}, u32[]{:S(2)}, u32[]{:S(2)}) collective-permute-start(bf16[2,192,128]{2,1,0:T(8,128)(2,1)S(1)} %get-tuple-element.62), channel_id=1, source_target_pairs={{3,0},{2,1},{1,2},{0,3},{7,4},{6,5},{5,6},{4,7},{11,8},{10,9},{9,1... | collective-permute-start | bytes 294920 | tf_op jit(solution)/shard_map/ppermute | solution.py:345
  4.4 1.3 %copy-start = (bf16[768,768]{1,0:T(8,128)(2,1)S(1)}, bf16[768,768]{1,0:T(8,128)(2,1)}, u32[]{:S(2)}) copy-start(bf16[768,768]{1,0:T(8,128)(2,1)} %refs_4_.1) | copy-start | bytes 3538948
  5.6 0.9 %copy-start.2 = (bf16[1,1,128,768]{3,2,1,0:T(8,128)(2,1)S(1)}, bf16[1,1,128,768]{3,2,1,0:T(8,128)(2,1)}, u32[]{:S(2)}) copy-start(bf16[1,1,128,768]{3,2,1,0:T(8,128)(2,1)} %param.7) | copy-start | bytes 589828
  6.5 0.9 %copy-start.3 = (bf16[1,1,128,768]{3,2,1,0:T(8,128)(2,1)S(1)}, bf16[1,1,128,768]{3,2,1,0:T(8,128)(2,1)}, u32[]{:S(2)}) copy-start(bf16[1,1,128,768]{3,2,1,0:T(8,128)(2,1)} %param.10) | copy-start | bytes 589828
  9.4 14.6 %collective-permute-start.8 = (bf16[2,192,384]{2,1,0:T(8,128)(2,1)S(1)}, bf16[2,192,384]{2,1,0:T(8,128)(2,1)S(1)}, u32[]{:S(2)}, u32[]{:S(2)}) collective-permute-start(bf16[2,192,384]{2,1,0:T(8,128)(2,1)S(1)} %get-tuple-element.76), channel_id=1, source_target_pairs={{0,4},{1,5},{2,6},{3,7},{4,8},{5,9},{6,10},{7,11},{8,12},{9,13},{1... | collective-permute-start | bytes 884744 | tf_op jit(solution)/shard_map/ppermute | solution.py:351
  10.8 10.4 %collective-permute-start.11 = (bf16[128,768]{1,0:T(8,128)(2,1)S(1)}, bf16[128,768]{1,0:T(8,128)(2,1)S(1)}, u32[]{:S(2)}, u32[]{:S(2)}) collective-permute-start(bf16[128,768]{1,0:T(8,128)(2,1)S(1)} %bitcast.10), channel_id=1, source_target_pairs={{2,0},{3,1},{0,2},{1,3},{6,4},{7,5},{4,6},{5,7},{10,8},{11,9},{8,1... | collective-permute-start | bytes 589832 | tf_op jit(solution)/shard_map/ppermute | solution.py:345
  11.0 4.0 %collective-permute-start.3 = (bf16[2,192,128]{2,1,0:T(8,128)(2,1)S(1)}, bf16[2,192,128]{2,1,0:T(8,128)(2,1)S(1)}, u32[]{:S(2)}, u32[]{:S(2)}) collective-permute-start(bf16[2,192,128]{2,1,0:T(8,128)(2,1)S(1)} %get-tuple-element.70), channel_id=1, source_target_pairs={{1,0},{0,1},{3,2},{2,3},{5,4},{4,5},{7,6},{6,7},{9,8},{8,9},{11,10... | collective-permute-start | bytes 294920 | tf_op jit(solution)/shard_map/ppermute | solution.py:345
  11.8 14.8 %collective-permute-start.9 = (bf16[2,192,384]{2,1,0:T(8,128)(2,1)S(1)}, bf16[2,192,384]{2,1,0:T(8,128)(2,1)S(1)}, u32[]{:S(2)}, u32[]{:S(2)}) collective-permute-start(bf16[2,192,384]{2,1,0:T(8,128)(2,1)S(1)} %get-tuple-element.77), channel_id=1, source_target_pairs={{0,12},{1,13},{2,14},{3,15},{4,0},{5,1},{6,2},{7,3},{8,4},{9,5},{1... | collective-permute-start | bytes 884744 | tf_op jit(solution)/shard_map/ppermute | solution.py:352
  13.7 5.1 %collective-permute-start.4 = (bf16[2,192,128]{2,1,0:T(8,128)(2,1)S(1)}, bf16[2,192,128]{2,1,0:T(8,128)(2,1)S(1)}, u32[]{:S(2)}, u32[]{:S(2)}) collective-permute-start(bf16[2,192,128]{2,1,0:T(8,128)(2,1)S(1)} %get-tuple-element.71), channel_id=1, source_target_pairs={{2,0},{3,1},{0,2},{1,3},{6,4},{7,5},{4,6},{5,7},{10,8},{11,9},{8,1... | collective-permute-start | bytes 294920 | tf_op jit(solution)/shard_map/ppermute | solution.py:345
  15.0 7.5 %collective-permute-start.5 = (bf16[2,192,128]{2,1,0:T(8,128)(2,1)S(1)}, bf16[2,192,128]{2,1,0:T(8,128)(2,1)S(1)}, u32[]{:S(2)}, u32[]{:S(2)}) collective-permute-start(bf16[2,192,128]{2,1,0:T(8,128)(2,1)S(1)} %get-tuple-element.72), channel_id=1, source_target_pairs={{3,0},{2,1},{1,2},{0,3},{7,4},{6,5},{5,6},{4,7},{11,8},{10,9},{9,1... | collective-permute-start | bytes 294920 | tf_op jit(solution)/shard_map/ppermute | solution.py:345
  18.8 11.0 %collective-permute-start.10 = (bf16[128,768]{1,0:T(8,128)(2,1)S(1)}, bf16[128,768]{1,0:T(8,128)(2,1)S(1)}, u32[]{:S(2)}, u32[]{:S(2)}) collective-permute-start(bf16[128,768]{1,0:T(8,128)(2,1)S(1)} %bitcast.11), channel_id=1, source_target_pairs={{1,0},{0,1},{3,2},{2,3},{5,4},{4,5},{7,6},{6,7},{9,8},{8,9},{11,10... | collective-permute-start | bytes 589832 | tf_op jit(solution)/shard_map/ppermute | solution.py:345
  21.2 8.7 %collective-permute-start.12 = (bf16[128,768]{1,0:T(8,128)(2,1)S(1)}, bf16[128,768]{1,0:T(8,128)(2,1)S(1)}, u32[]{:S(2)}, u32[]{:S(2)}) collective-permute-start(bf16[128,768]{1,0:T(8,128)(2,1)S(1)} %collective-permute-done.11.refs_2_), channel_id=1, source_target_pairs={{1,0},{0,1},{3,2},{2,3},{5,4},{4,5},{7,6},{6,7},{9,8},{8,9},{11,10... | collective-permute-start | bytes 589832 | tf_op jit(solution)/shard_map/ppermute | solution.py:345
  22.7 14.8 %collective-permute-start.6 = (bf16[2,192,384]{2,1,0:T(8,128)(2,1)S(1)}, bf16[2,192,384]{2,1,0:T(8,128)(2,1)S(1)}, u32[]{:S(2)}, u32[]{:S(2)}) collective-permute-start(bf16[2,192,384]{2,1,0:T(8,128)(2,1)S(1)} %get-tuple-element.74), channel_id=1, source_target_pairs={{0,4},{1,5},{2,6},{3,7},{4,8},{5,9},{6,10},{7,11},{8,12},{9,13},{1... | collective-permute-start | bytes 884744 | tf_op jit(solution)/shard_map/ppermute | solution.py:351
  24.0 15.8 %collective-permute-start.7 = (bf16[2,192,384]{2,1,0:T(8,128)(2,1)S(1)}, bf16[2,192,384]{2,1,0:T(8,128)(2,1)S(1)}, u32[]{:S(2)}, u32[]{:S(2)}) collective-permute-start(bf16[2,192,384]{2,1,0:T(8,128)(2,1)S(1)} %get-tuple-element.75), channel_id=1, source_target_pairs={{0,12},{1,13},{2,14},{3,15},{4,0},{5,1},{6,2},{7,3},{8,4},{9,5},{1... | collective-permute-start | bytes 884744 | tf_op jit(solution)/shard_map/ppermute | solution.py:352
  30.3 7.1 %collective-permute-start.18 = (bf16[96,768]{1,0:T(8,128)(2,1)S(1)}, bf16[96,768]{1,0:T(8,128)(2,1)S(1)}, u32[]{:S(2)}, u32[]{:S(2)}) collective-permute-start(bf16[96,768]{1,0:T(8,128)(2,1)S(1)} %get-tuple-element.87.refs_4_), channel_id=1, source_target_pairs={{0,16},{16,0},{1,17},{17,1},{2,18},{18,2},{3,19},{19,3},{4,20},{20... | collective-permute-start | bytes 442376 | tf_op jit(solution)/shard_map/ppermute | solution.py:356
  34.1 5.8 %collective-permute-start.13 = (f32[16,384]{1,0:T(8,128)S(1)}, f32[16,384]{1,0:T(8,128)S(1)}, u32[]{:S(2)}, u32[]{:S(2)}) collective-permute-start(f32[16,384]{1,0:T(8,128)S(1)} %get-tuple-element.89), channel_id=1, source_target_pairs={{0,4},{1,5},{2,6},{3,7},{4,8},{5,9},{6,10},{7,11},{8,12},{9,13},{1... | collective-permute-start | bytes 73736 | tf_op jit(solution)/shard_map/ppermute | solution.py:351
  34.4 5.5 %collective-permute-start.14 = (f32[16,384]{1,0:T(8,128)S(1)}, f32[16,384]{1,0:T(8,128)S(1)}, u32[]{:S(2)}, u32[]{:S(2)}) collective-permute-start(f32[16,384]{1,0:T(8,128)S(1)} %get-tuple-element.90), channel_id=1, source_target_pairs={{0,12},{1,13},{2,14},{3,15},{4,0},{5,1},{6,2},{7,3},{8,4},{9,5},{1... | collective-permute-start | bytes 73736 | tf_op jit(solution)/shard_map/ppermute | solution.py:352
  37.4 8.0 %collective-permute-start.19 = (bf16[48,768]{1,0:T(8,128)(2,1)S(1)}, bf16[48,768]{1,0:T(8,128)(2,1)S(1)}, u32[]{:S(2)}, u32[]{:S(2)}) collective-permute-start(bf16[48,768]{1,0:T(8,128)(2,1)S(1)} %get-tuple-element.104.refs_0_), channel_id=1, source_target_pairs={{8,0},{9,1},{10,2},{11,3},{12,4},{13,5},{14,6},{15,7},{0,8},{1,9},... | collective-permute-start | bytes 221192 | tf_op jit(solution)/shard_map/ppermute | solution.py:345
  37.5 8.4 %collective-permute-start.20 = (bf16[48,768]{1,0:T(8,128)(2,1)S(1)}, bf16[48,768]{1,0:T(8,128)(2,1)S(1)}, u32[]{:S(2)}, u32[]{:S(2)}) collective-permute-start(bf16[48,768]{1,0:T(8,128)(2,1)S(1)} %get-tuple-element.105.refs_1_), channel_id=1, source_target_pairs={{8,0},{9,1},{10,2},{11,3},{12,4},{13,5},{14,6},{15,7},{0,8},{1,9},... | collective-permute-start | bytes 221192 | tf_op jit(solution)/shard_map/ppermute | solution.py:345
  41.7 21.2 %copy-start.1 = (bf16[768,768]{1,0:T(8,128)(2,1)S(1)}, bf16[768,768]{1,0:T(8,128)(2,1)}, u32[]{:S(2)}) copy-start(bf16[768,768]{1,0:T(8,128)(2,1)} %refs_4_.1) | copy-start | bytes 3538948
  41.7 7.7 %collective-permute-start.15 = (bf16[4,192,128]{2,1,0:T(8,128)(2,1)S(1)}, bf16[4,192,128]{2,1,0:T(8,128)(2,1)S(1)}, u32[]{:S(2)}, u32[]{:S(2)}) collective-permute-start(bf16[4,192,128]{2,1,0:T(8,128)(2,1)S(1)} %get-tuple-element.95), channel_id=1, source_target_pairs={{1,0},{0,1},{3,2},{2,3},{5,4},{4,5},{7,6},{6,7},{9,8},{8,9},{11,10... | collective-permute-start | bytes 589832 | tf_op jit(solution)/shard_map/ppermute | solution.py:345
  45.9 4.1 %collective-permute-start.21 = (bf16[96,768]{1,0:T(8,128)(2,1)S(1)}, bf16[96,768]{1,0:T(8,128)(2,1)S(1)}, u32[]{:S(2)}, u32[]{:S(2)}) collective-permute-start(bf16[96,768]{1,0:T(8,128)(2,1)S(1)} %meet.1.refs_0_), channel_id=1, source_target_pairs={{4,0},{5,1},{6,2},{7,3},{0,4},{1,5},{2,6},{3,7},{12,8},{13,9},{14,... | collective-permute-start | bytes 442376 | tf_op jit(solution)/shard_map/ppermute | solution.py:345
  46.1 8.8 %collective-permute-start.16 = (bf16[4,192,128]{2,1,0:T(8,128)(2,1)S(1)}, bf16[4,192,128]{2,1,0:T(8,128)(2,1)S(1)}, u32[]{:S(2)}, u32[]{:S(2)}) collective-permute-start(bf16[4,192,128]{2,1,0:T(8,128)(2,1)S(1)} %get-tuple-element.96), channel_id=1, source_target_pairs={{2,0},{3,1},{0,2},{1,3},{6,4},{7,5},{4,6},{5,7},{10,8},{11,9},{8,1... | collective-permute-start | bytes 589832 | tf_op jit(solution)/shard_map/ppermute | solution.py:345
  46.1 12.4 %collective-permute-start.17 = (bf16[4,192,128]{2,1,0:T(8,128)(2,1)S(1)}, bf16[4,192,128]{2,1,0:T(8,128)(2,1)S(1)}, u32[]{:S(2)}, u32[]{:S(2)}) collective-permute-start(bf16[4,192,128]{2,1,0:T(8,128)(2,1)S(1)} %get-tuple-element.97), channel_id=1, source_target_pairs={{3,0},{2,1},{1,2},{0,3},{7,4},{6,5},{5,6},{4,7},{11,8},{10,9},{9,1... | collective-permute-start | bytes 589832 | tf_op jit(solution)/shard_map/ppermute | solution.py:345
  50.0 8.5 %collective-permute-start.22 = (bf16[96,768]{1,0:T(8,128)(2,1)S(1)}, bf16[96,768]{1,0:T(8,128)(2,1)S(1)}, u32[]{:S(2)}, u32[]{:S(2)}) collective-permute-start(bf16[96,768]{1,0:T(8,128)(2,1)S(1)} %add.1.refs_0_), channel_id=1, source_target_pairs={{0,2},{1,3},{2,18},{3,19},{4,6},{5,7},{6,22},{7,23},{8,10},{9,11},... | collective-permute-start | bytes 442376 | tf_op jit(solution)/shard_map/ppermute | solution.py:471
  53.0 7.5 %collective-permute-start.23 = (bf16[96,768]{1,0:T(8,128)(2,1)S(1)}, bf16[96,768]{1,0:T(8,128)(2,1)S(1)}, u32[]{:S(2)}, u32[]{:S(2)}) collective-permute-start(bf16[96,768]{1,0:T(8,128)(2,1)S(1)} %add.1.refs_0_), channel_id=1, source_target_pairs={{2,16},{3,17},{6,20},{7,21},{10,24},{11,25},{14,28},{15,29},{16,2}... | collective-permute-start | bytes 442376 | tf_op jit(solution)/shard_map/ppermute | solution.py:471
  60.5 4.5 %collective-permute-start.24 = (bf16[192,768]{1,0:T(8,128)(2,1)S(1)}, bf16[192,768]{1,0:T(8,128)(2,1)S(1)}, u32[]{:S(2)}, u32[]{:S(2)}) collective-permute-start(bf16[192,768]{1,0:T(8,128)(2,1)S(1)} %cross.1.value_ref), channel_id=1, source_target_pairs={{1,0},{0,1},{3,2},{2,3},{5,4},{4,5},{7,6},{6,7},{9,8},{8,9},{11,10... | collective-permute-start | bytes 884744 | tf_op jit(solution)/shard_map/ppermute | solution.py:345
